TPU v7x, 32 devices: a whole 2x2x4 slice. The times are simulated.
32 devices in a mesh: groups: 2 (over x), dp: 16 (over z, y, core).
Axes of the slice: x: 2, y: 2, z: 4, core: 2. Of those that a mesh axis runs over, the one named last changes fastest.
Arguments:
- token_ids: int32 [64, 64], P(('groups', 'dp')), parts along dimension 0, may hold values from 0 to 3839, as said below
- lengths: int32 [64], P(('groups', 'dp')), parts along dimension 0, may hold values from 16 to 64
- word_table: bfloat16 [3840, 1024], P('dp'), may hold values from -6 to 6
- pos_table: bfloat16 [64, 1024], replicated, may hold values from -3 to 3
- emb_gain: float32 [1024], replicated, may hold values from 0.25 to 1.75
- emb_bias: float32 [1024], replicated, may hold values from -1.75 to 1.75
- w_qkv: bfloat16 [1024, 1536], replicated, may hold values from -0.1875 to 0.1875
- w_out: bfloat16 [512, 1024], replicated, may hold values from -0.25 to 0.25
- out_bias: float32 [1024], replicated, may hold values from -3 to 3
- norm_gain: float32 [1024], replicated, may hold values from 0.25 to 1.75
- norm_bias: float32 [1024], replicated, may hold values from -1.75 to 1.75
- stored_rows: bfloat16 [8128, 1024], P(('groups', 'dp')), parts along dimension 0, may hold values from -6 to 6
- row_owner: int32 [8192, 1], P(('groups', 'dp')), parts along dimension 0, may hold values from 0 to 15; in each aligned block of 256 rows (0 to 255, 256 to 511, ...) at most 48 rows name the same one
- row_slot: int32 [8192], P(('groups', 'dp')), parts along dimension 0, may hold values from 0 to 511
- centroids: float32 [16384, 1024], P(('groups', 'dp')), parts along dimension 0, may hold values from -6 to 6
Outputs:
- passage_embed: bfloat16 [64, 1024], P(('groups', 'dp')), parts along dimension 0
- new_centroids: float32 [16384, 1024], P(('groups', 'dp')), parts along dimension 0
There are 2 independent parts, one for each index of `groups`. A program takes and returns all parts, laid end to end along the dimension named above; an argument that names none is the same for every part. Nothing has to cross between parts.
Inputs may be any that keep to these rules, and one draw needn't show every extreme that they name: `token_ids`: token ids of device o's vocabulary rows are o * 240 to (o + 1) * 240 - 1. Among the 128 tokens of one index of dp, at most 24 have ids of one index's rows, and in every such block some index has exactly 24. `row_owner`: among the 256 rows of one index of dp, at most 48 name one index; some index is named 48 times.
All inputs are finite; a program needn't handle non-finite values.
Results may differ from a plain program's by a relative error of at most 0.0038.
Values may be sent and summed in bfloat16 or wider, within the bound.
No kernel may reach another device: no remote copies, remote signals or barrier semaphores. Data moves between devices by JAX's collectives and lax.ppermute only.
A program may use at most 64 MiB of HBM per device.

v0:
```python
import jax
import jax.numpy as jnp
from jax import lax
from jax.sharding import PartitionSpec as P

HEADS = 8
HD = 64


def layer_norm(values, gain, shift):
    center = values - jnp.mean(values, axis=-1, keepdims=True)
    spread = jnp.mean(center * center, axis=-1, keepdims=True)
    return center * lax.rsqrt(spread + 1e-12) * gain + shift


def encode(
    tok_rows, lengths, pos_table, emb_gain, emb_bias, w_qkv, w_out, out_bias, norm_gain, norm_bias
):
    passes, seq_len, width = tok_rows.shape
    summed = tok_rows.astype(jnp.float32) + pos_table.astype(jnp.float32)[None]
    embedded = layer_norm(summed, emb_gain, emb_bias).astype(jnp.bfloat16)
    flat = embedded.reshape(passes * seq_len, width)
    projected = jnp.dot(flat, w_qkv, preferred_element_type=jnp.float32).astype(jnp.bfloat16)
    projected = projected.reshape(passes, seq_len, 3, HEADS, HD)
    query = projected[:, :, 0]
    keyset = projected[:, :, 1]
    valueset = projected[:, :, 2]
    scores = jnp.einsum(
        "pqhd,pkhd->phqk", query, keyset, preferred_element_type=jnp.float32
    ) * HD ** (-0.5)
    valid = (jnp.arange(seq_len, dtype=jnp.int32)[None, :] < lengths[:, None]).astype(jnp.float32)
    weights = jnp.exp(scores) * valid[:, None, None, :]
    probs = (weights / jnp.sum(weights, axis=-1, keepdims=True)).astype(jnp.bfloat16)
    context = jnp.einsum(
        "phqk,pkhd->pqhd", probs, valueset, preferred_element_type=jnp.float32
    ).astype(jnp.bfloat16)
    context = context.reshape(passes * seq_len, HEADS * HD)
    attended = jnp.dot(context, w_out, preferred_element_type=jnp.float32) + out_bias
    hidden = layer_norm(flat.astype(jnp.float32) + attended, norm_gain, norm_bias).reshape(
        passes, seq_len, width
    )
    pooled = jnp.sum(hidden * valid[:, :, None], axis=1) / jnp.sum(valid, axis=1, keepdims=True)
    scaled = pooled * lax.rsqrt(jnp.mean(pooled * pooled, axis=-1, keepdims=True) + 1e-06)
    return scaled.astype(jnp.bfloat16)


def slot_rank(target):
    positions = jnp.arange(target.shape[0], dtype=jnp.int32)
    earlier = (target[:, None] == target[None, :]) & (positions[None, :] < positions[:, None])
    return jnp.sum(earlier.astype(jnp.int32), axis=1)


def slot_table(target, peer_count, capacity):
    slot = target * capacity + slot_rank(target)
    return slot[None, :] == jnp.arange(peer_count * capacity, dtype=jnp.int32)[:, None]


def place_ints(table, values, empty_value):
    filled = jnp.any(table, axis=1)
    picked = jnp.sum(jnp.where(table, values[None, :], 0), axis=1)
    return jnp.where(filled, picked, empty_value)


def pack_rows(row_block, target, places, peer_count, capacity):
    table = slot_table(target, peer_count, capacity)
    buffer = jnp.dot(
        table.astype(jnp.bfloat16), row_block, preferred_element_type=jnp.float32
    ).astype(jnp.bfloat16)
    place_buffer = place_ints(table, places, -1)
    return (
        buffer.reshape(peer_count, capacity, row_block.shape[1]),
        place_buffer.reshape(peer_count, capacity),
    )


def accumulate(row_block, places, centre_count):
    onehot = (jnp.arange(centre_count, dtype=jnp.int32)[:, None] == places[None, :]).astype(
        jnp.bfloat16
    )
    sums = jnp.dot(onehot, row_block, preferred_element_type=jnp.float32)
    counts = jnp.sum(onehot, axis=1, dtype=jnp.float32)
    return (sums, counts)


def shards(
    token_ids,
    lengths,
    word_table,
    pos_table,
    emb_gain,
    emb_bias,
    w_qkv,
    w_out,
    out_bias,
    norm_gain,
    norm_bias,
    stored_rows,
    row_owner,
    row_slot,
    centroids,
):
    peer_count = lax.axis_size("dp")
    width = word_table.shape[1]
    vocab_rows = word_table.shape[0]
    centre_count = centroids.shape[0]
    passes, seq_len = token_ids.shape
    token_list = token_ids.reshape(passes * seq_len)
    token_count = token_list.shape[0]
    row_count = row_slot.shape[0]
    owners_all = row_owner[:, 0]
    token_cap = max(2, 3 * token_count // peer_count)
    row_cap = max(2, 3 * row_count // peer_count)
    target = token_list // vocab_rows
    table = slot_table(target, peer_count, token_cap)
    requests = place_ints(table, token_list - target * vocab_rows, 0).reshape(peer_count, token_cap)
    found = word_table[lax.all_to_all(requests, "dp", split_axis=0, concat_axis=0, tiled=True)]
    fetched = lax.all_to_all(found, "dp", split_axis=0, concat_axis=0, tiled=True)
    picker = table.T.astype(jnp.bfloat16)
    tok_flat = jnp.dot(
        picker, fetched.reshape(peer_count * token_cap, width), preferred_element_type=jnp.float32
    )
    tok_rows = tok_flat.astype(jnp.bfloat16).reshape(passes, seq_len, width)
    passage_embed = encode(
        tok_rows,
        lengths,
        pos_table,
        emb_gain,
        emb_bias,
        w_qkv,
        w_out,
        out_bias,
        norm_gain,
        norm_bias,
    )
    all_rows = jnp.concatenate([stored_rows, passage_embed], axis=0)
    buffer, place_buffer = pack_rows(all_rows, owners_all, row_slot, peer_count, row_cap)
    got_rows, got_places = (
        lax.all_to_all(buffer, "dp", split_axis=0, concat_axis=0, tiled=True),
        lax.all_to_all(place_buffer, "dp", split_axis=0, concat_axis=0, tiled=True),
    )
    sums, counts = accumulate(
        got_rows.reshape(peer_count * row_cap, width),
        got_places.reshape(peer_count * row_cap),
        centre_count,
    )
    new_centroids = jnp.where(
        counts[:, None] > 0, sums / jnp.maximum(counts, 1.0)[:, None], centroids
    )
    return (passage_embed, new_centroids)


def solution(mesh):
    return jax.shard_map(
        shards,
        mesh=mesh,
        in_specs=(
            P(("groups", "dp"), None),
            P(("groups", "dp")),
            P("dp", None),
            P(),
            P(),
            P(),
            P(),
            P(),
            P(),
            P(),
            P(),
            P(("groups", "dp"), None),
            P(("groups", "dp"), None),
            P(("groups", "dp")),
            P(("groups", "dp"), None),
        ),
        out_specs=(P(("groups", "dp"), None), P(("groups", "dp"), None)),
        check_vma=False,
    )
```

profile of v0, /device:TPU:13, one launch (start us, length us, event | category | flops | bytes accessed | tf_op | source)
XLA Modules:
  0.0 112.9 jit_solution(10259179544346177041)
XLA Ops:
  0.6 0.0 copy-start
  0.6 0.9 reshape.274
  1.6 0.2 convert_reduce_fusion.2
  1.8 0.2 fusion.18
  1.9 0.1 select_reduce_fusion.1
  2.1 0.1 select_n.74
  2.2 10.2 %all_to_all.25 = s32[16,1,24]{2,1,0:T(1,128)S(1)} all-to-all(s32[16,1,24]{2,1,0:T(1,128)S(1)} %select_n.74), channel_id=1, replica_groups=mesh['groups'=2,'dp'=16] {'dp'}, dimensions={0} | all-to-all | bytes 3072 | tf_op jit(solution)/shard_map/all_to_all | solution.py:116
  12.3 0.1 reshape.283
  12.4 0.0 copy-start.9
  12.4 0.0 copy-start.16
  12.5 0.0 copy-start.18
  12.5 0.0 copy-start.3
  12.5 4.5 %gather_fusion = bf16[384,1024]{1,0:T(8,128)(2,1)} fusion(bf16[240,1024]{1,0:T(8,128)(2,1)} %param.17, s32[1024]{0:T(1024)S(1)} %pad_clamp_fusion), kind=kCustom, calls=%fused_computation | custom fusion | bytes 1574400 | tf_op jit(solution)/shard_map/gather | solution.py:116
  17.0 6.9 %all-to-all-start.1 = ((bf16[16,24,1024]{2,1,0:T(8,128)(2,1)}), bf16[16,24,1024]{2,1,0:T(8,128)(2,1)}, u32[]{:S(2)}, u32[]{:S(2)}) async-start(bf16[16,24,1024]{2,1,0:T(8,128)(2,1)} %bitcast.35), calls=%async_computation.1 | async-start | bytes 1572864 | tf_op jit(solution)/shard_map/all_to_all | solution.py:117
  23.9 0.0 copy-done.9
  23.9 0.2 convert_reduce_fusion.1
  24.1 0.0 copy-start.7
  24.1 0.2 fusion.9
  24.3 0.0 copy-done.16
  24.3 0.2 select_reduce_fusion
  24.5 0.7 select_n.78
  25.2 0.0 copy-done.18
  25.2 0.8 fusion.24
  25.9 0.6 compare_convert_fusion
  26.6 16.7 %all-to-all-done.1 = bf16[16,24,1024]{2,1,0:T(8,128)(2,1)} async-done(((bf16[16,24,1024]{2,1,0:T(8,128)(2,1)}), bf16[16,24,1024]{2,1,0:T(8,128)(2,1)}, u32[]{:S(2)}, u32[]{:S(2)}) %all-to-all-start.1) | async-done | bytes 786464 | tf_op jit(solution)/shard_map/all_to_all | solution.py:117
  43.3 4.9 %all-to-all-start.2 = ((s32[16,1,48]{2,1,0:T(1,128)}), s32[16,1,48]{2,1,0:T(1,128)S(1)}, u32[]{:S(2)}, u32[]{:S(2)}) async-start(s32[16,1,48]{2,1,0:T(1,128)} %select_n.78), calls=%async_computation.2 | async-start | bytes 16384 | tf_op jit(solution)/shard_map/all_to_all | solution.py:139
  48.2 0.0 copy-done.3
  48.2 1.6 %fusion.26 = (f32[128]{0:T(128)S(1)}, f32[128,1024]{1,0:T(8,128)S(1)}) fusion(f32[128,1024]{1,0:T(8,128)S(1)} %bitcast.36, bf16[384,1024]{1,0:T(8,128)(2,1)} %bitcast.2, s32[128]{0:T(128)S(1)} %multiply_add_fusion.2), kind=kOutput, calls=%fused_computation.70 | convolution fusion | flops 101236608 | bytes 1836032 | tf_op jit(solution)/shard_map/dot_general | solution.py:119
  49.8 0.0 copy-start.10
  49.8 0.2 multiply_reduce_fusion.2
  50.0 0.0 copy-done.7
  50.1 0.5 copy-done.1
  50.6 0.0 copy-done.10
  50.6 0.5 copy-done.13
  51.1 0.6 convolution_convert_fusion
  51.8 1.3 %reshape.276 = bf16[2,64,3,8,64]{4,3,2,1,0:T(8,128)(2,1)} reshape(bf16[128,1536]{1,0:T(8,128)(2,1)S(1)} %convolution_convert_fusion) | data formatting | bytes 786432 | tf_op jit(solution)/shard_map/reshape | solution.py:24
  53.1 2.0 %fusion.25 = (bf16[2,64,1,8,64]{4,3,2,1,0:T(8,128)(2,1)S(1)}, bf16[2,64,1,8,64]{4,3,2,1,0:T(8,128)(2,1)}, bf16[2,64,1,8,64]{4,3,2,1,0:T(8,128)(2,1)}) fusion(bf16[2,64,3,8,64]{4,3,2,1,0:T(8,128)(2,1)} %reshape.276), kind=kLoop, calls=%fused_computation.69 | loop fusion | bytes 786432 | tf_op jit(solution)/shard_map/slice | solution.py:27
  55.1 0.9 copy.32
  56.0 2.1 %fusion.4 = f32[2,8,64,64]{2,3,1,0:T(8,128)} fusion(bf16[2,64,1,8,64]{4,3,2,1,0:T(8,128)(2,1)} %get-tuple-element.7, bf16[2,64,1,8,64]{4,3,2,1,0:T(8,128)(2,1)} %get-tuple-element.8, f32[2,64]{1,0:T(2,128)S(1)} %copy-done.14), kind=kOutput, calls=%fused_computation.12 | convolution fusion | flops 8519680 | bytes 524800 | tf_op jit(solution)/shard_map/pqhd,pkhd->phqk/dot_general | solution.py:28
  58.1 2.3 %fusion.7 = bf16[2,64,8,64]{1,3,2,0:T(8,128)(2,1)} fusion(f32[2,8,64,64]{2,3,1,0:T(8,128)} %fusion.4, bf16[2,64,1,8,64]{1,4,3,0,2:T(8,128)(2,1)} %copy.32), kind=kOutput, calls=%fused_computation.17 | convolution fusion | flops 8586303 | bytes 524288 | tf_op jit(solution)/shard_map/phqk,pkhd->pqhd/dot_general | solution.py:34
  60.4 1.1 %copy.30 = bf16[2,64,8,64]{3,2,1,0:T(8,128)(2,1)S(1)} copy(bf16[2,64,8,64]{1,3,2,0:T(8,128)(2,1)} %fusion.7) | data formatting | bytes 262144 | tf_op jit(solution)/shard_map/convert_element_type | solution.py:36
  61.5 0.2 reshape.277
  61.7 0.0 copy-start.11
  61.7 0.0 copy-start.12
  61.7 0.0 copy-start.15
  61.8 0.0 copy-start.2
  61.8 1.9 %fusion.27 = (f32[128]{0:T(128)S(1)}, f32[128,1024]{1,0:T(8,128)S(1)}) fusion(f32[1024]{0:T(1024)} %param.23, bf16[128,512]{1,0:T(8,128)(2,1)S(1)} %reshape.277, bf16[512,1024]{1,0:T(8,128)(2,1)} %param.22, f32[1024]{0:T(1024)S(1)} %copy-done.4, f32[1024]{0:T(1024)S(1)} %copy-done.5, f32[128]{0:T(128)} %copy-done.13, f32[128,1024]{1,0:T(8,128)} %copy-done.1, ...), kind=kOutput, calls=%fused_computation.71 | convolution fusion | flops 135397248 | bytes 2242048 | tf_op jit(solution)/shard_map/dot_general | solution.py:38
  63.6 0.2 multiply_reduce_fusion.1
  63.9 0.2 multiply_reduce_fusion
  64.1 0.0 copy-done.17
  64.1 0.2 multiply_reduce_fusion.3
  64.3 0.1 multiply_convert_fusion
  64.4 0.0 copy-done.8
  64.4 0.0 copy-start.6
  64.4 1.7 %convolution_convert_fusion.1 = bf16[768,1024]{1,0:T(8,128)(2,1)} fusion(bf16[2,1024]{1,0:T(2,128)(2,1)S(1)} %multiply_convert_fusion, bf16[254,1024]{1,0:T(8,128)(2,1)S(1)} %copy-done.2, s32[256]{0:T(256)S(1)} %copy-done.8), kind=kOutput, calls=%fused_computation.3 | convolution fusion | flops 404684800 | bytes 2098176 | tf_op jit(solution)/shard_map/dot_general | solution.py:66
  66.2 0.0 all-to-all-done.2
  66.2 0.0 copy-done.6
  66.2 6.0 %all-to-all-start.3 = ((bf16[16,48,1024]{2,1,0:T(8,128)(2,1)}), bf16[16,48,1024]{2,1,0:T(8,128)(2,1)}, u32[]{:S(2)}, u32[]{:S(2)}) async-start(bf16[16,48,1024]{2,1,0:T(8,128)(2,1)} %bitcast.34), calls=%async_computation.3 | async-start | bytes 3145728 | tf_op jit(solution)/shard_map/all_to_all | solution.py:138
  72.2 0.5 broadcast.237
  72.7 0.6 reduce.5
  73.3 0.1 eq.80
  73.4 0.2 convert_reduce_fusion
  73.7 34.8 %all-to-all-done.3 = bf16[16,48,1024]{2,1,0:T(8,128)(2,1)} async-done(((bf16[16,48,1024]{2,1,0:T(8,128)(2,1)}), bf16[16,48,1024]{2,1,0:T(8,128)(2,1)}, u32[]{:S(2)}, u32[]{:S(2)}) %all-to-all-start.3) | async-done | bytes 1572896 | tf_op jit(solution)/shard_map/all_to_all | solution.py:138
  108.5 4.4 %divide_select_fusion = f32[512,1024]{1,0:T(8,128)} fusion(f32[512,1024]{1,0:T(8,128)} %param.29, bf16[768,1024]{1,0:T(8,128)(2,1)} %bitcast.11, f32[512]{0:T(512)S(1)} %broadcast_maximum_fusion, pred[512]{0:T(512)(128)(4,1)S(1)} %broadcast_compare_fusion, s32[768]{0:T(1024)S(1)} %eq.80), kind=kOutput, calls=%fused_computation.2 | convolution fusion | flops 806748160 | bytes 5772800 | tf_op jit(solution)/shard_map/dot_general | solution.py:80
  (30 shorter events, 0.2 us)
Async XLA Ops:
  0.6 50.5 %copy-start = (bf16[1024,1536]{1,0:T(8,128)(2,1)S(1)}, bf16[1024,1536]{1,0:T(8,128)(2,1)}, u32[]{:S(2)}) copy-start(bf16[1024,1536]{1,0:T(8,128)(2,1)} %param.21) | copy-start | bytes 9437188
  12.4 11.5 %copy-start.9 = (s32[256,1]{0,1:T(1,128)S(1)}, s32[256,1]{0,1:T(1,128)}, u32[]{:S(2)}) copy-start(s32[256,1]{0,1:T(1,128)} %param.27) | copy-start | bytes 3076
  12.4 11.8 %copy-start.16 = (s32[256]{0:T(256)S(1)}, s32[256]{0:T(256)}, u32[]{:S(2)}) copy-start(s32[256]{0:T(256)} %param.28) | copy-start | bytes 3076
  12.5 12.7 %copy-start.18 = (s32[2]{0:T(128)S(1)}, s32[2]{0:T(128)}, u32[]{:S(2)}) copy-start(s32[2]{0:T(128)} %param.16) | copy-start | bytes 28
  12.5 35.7 %copy-start.3 = (bf16[64,1024]{1,0:T(8,128)(2,1)S(1)}, bf16[64,1024]{1,0:T(8,128)(2,1)}, u32[]{:S(2)}) copy-start(bf16[64,1024]{1,0:T(8,128)(2,1)} %param.18) | copy-start | bytes 393220
  17.0 34.1 %copy-start.4 = (f32[1024]{0:T(1024)S(1)}, f32[1024]{0:T(1024)}, u32[]{:S(2)}) copy-start(f32[1024]{0:T(1024)} %param.20) | copy-start | bytes 12292
  17.0 34.1 %copy-start.5 = (f32[1024]{0:T(1024)S(1)}, f32[1024]{0:T(1024)}, u32[]{:S(2)}) copy-start(f32[1024]{0:T(1024)} %param.19) | copy-start | bytes 12292
  17.0 26.3 %all-to-all-start.1 = ((bf16[16,24,1024]{2,1,0:T(8,128)(2,1)}), bf16[16,24,1024]{2,1,0:T(8,128)(2,1)}, u32[]{:S(2)}, u32[]{:S(2)}) async-start(bf16[16,24,1024]{2,1,0:T(8,128)(2,1)} %bitcast.35), calls=%async_computation.1 | async-start | bytes 1572864 | tf_op jit(solution)/shard_map/all_to_all | solution.py:117
  24.1 25.9 %copy-start.7 = (s32[256]{0:T(256)}, s32[256]{0:T(256)S(1)}, u32[]{:S(2)}) copy-start(s32[256]{0:T(256)S(1)} %multiply_add_fusion.1) | copy-start | bytes 3076
  43.3 22.9 %all-to-all-start.2 = ((s32[16,1,48]{2,1,0:T(1,128)}), s32[16,1,48]{2,1,0:T(1,128)S(1)}, u32[]{:S(2)}, u32[]{:S(2)}) async-start(s32[16,1,48]{2,1,0:T(1,128)} %select_n.78), calls=%async_computation.2 | async-start | bytes 16384 | tf_op jit(solution)/shard_map/all_to_all | solution.py:139
  49.8 0.8 copy-start.1
  49.8 0.8 copy-start.10
  50.6 0.5 copy-start.13
  53.1 2.9 %copy-start.14 = (f32[2,64]{1,0:T(2,128)S(1)}, f32[2,64]{1,0:T(2,128)}, u32[]{:S(2)}) copy-start(f32[2,64]{1,0:T(2,128)} %compare_convert_fusion) | copy-start | bytes 1540
  61.7 2.2 %copy-start.11 = (f32[1024]{0:T(1024)S(1)}, f32[1024]{0:T(1024)}, u32[]{:S(2)}) copy-start(f32[1024]{0:T(1024)} %param.25) | copy-start | bytes 12292
  61.7 2.1 %copy-start.12 = (f32[1024]{0:T(1024)S(1)}, f32[1024]{0:T(1024)}, u32[]{:S(2)}) copy-start(f32[1024]{0:T(1024)} %param.24) | copy-start | bytes 12292
  61.7 2.1 %copy-start.15 = (f32[2,64]{1,0:T(2,128)S(1)}, f32[2,64]{1,0:T(2,128)}, u32[]{:S(2)}) copy-start(f32[2,64]{1,0:T(2,128)} %compare_convert_fusion) | copy-start | bytes 1540
  61.7 2.4 %copy-start.17 = (f32[2]{0:T(128)S(1)}, f32[2]{0:T(128)}, u32[]{:S(2)}) copy-start(f32[2]{0:T(128)} %fusion.24) | copy-start | bytes 28
  61.8 2.6 %copy-start.2 = (bf16[254,1024]{1,0:T(8,128)(2,1)S(1)}, bf16[254,1024]{1,0:T(8,128)(2,1)}, u32[]{:S(2)}) copy-start(bf16[254,1024]{1,0:T(8,128)(2,1)} %param.26) | copy-start | bytes 1560580
  61.8 2.6 %copy-start.8 = (s32[256]{0:T(256)S(1)}, s32[256]{0:T(256)}, u32[]{:S(2)}) copy-start(s32[256]{0:T(256)} %copy-done.7) | copy-start | bytes 3076
  64.4 1.7 %copy-start.6 = (bf16[2,1024]{1,0:T(2,128)(2,1)}, bf16[2,1024]{1,0:T(2,128)(2,1)S(1)}, u32[]{:S(2)}) copy-start(bf16[2,1024]{1,0:T(2,128)(2,1)S(1)} %multiply_convert_fusion) | copy-start | bytes 12292
  66.2 42.3 %all-to-all-start.3 = ((bf16[16,48,1024]{2,1,0:T(8,128)(2,1)}), bf16[16,48,1024]{2,1,0:T(8,128)(2,1)}, u32[]{:S(2)}, u32[]{:S(2)}) async-start(bf16[16,48,1024]{2,1,0:T(8,128)(2,1)} %bitcast.34), calls=%async_computation.3 | async-start | bytes 3145728 | tf_op jit(solution)/shard_map/all_to_all | solution.py:138
where the time goes:
time: 113 us
  waiting for transfers between devices  51.5 us (46%)
  starting transfers between devices  17.8 us (16%)
  matrix products  14.5 us (13%)
  local copies, waits for them, and re-layouts  13.7 us (12%)
  blocking collectives  10.2 us (9%)
  other arithmetic  4.23 us (4%)
    all_to_all x1, waiting for transfers between devices, shards(): lax.all_to_all(buffer, 'dp', split_axis=0, concat_axis=0, tiled=True)  34.8 us
    all_to_all x1, waiting for transfers between devices, shards(): lax.all_to_all(found, 'dp', split_axis=0, concat_axis=0, tiled=True)  16.7 us
    all_to_all x1, blocking collectives, shards(): lax.all_to_all(requests, 'dp', split_axis=0, concat_axis=0, tiled=True)  10.2 us
    all_to_all x1, starting transfers between devices, shards(): lax.all_to_all(found, 'dp', split_axis=0, concat_axis=0, tiled=True)  6.89 us
    all_to_all x1, starting transfers between devices, shards(): lax.all_to_all(buffer, 'dp', split_axis=0, concat_axis=0, tiled=True)  6.02 us
    all_to_all x1, starting transfers between devices, shards(): lax.all_to_all(place_buffer, 'dp', split_axis=0, concat_axis=0, tiled=True)  4.93 us
    gather x1, local copies, waits for them, and re-layouts, shards(): word_table[lax.all_to_all(requests, 'dp', split_axis=0, concat_axis=0, ti...  4.51 us
    dot_general x1, matrix products, accumulate(): sums = jnp.dot(onehot, row_block, preferred_element_type=jnp.float32)  4.39 us
  transfers between devices with their start and end apart: 3, of which 2 were waited for; matrix products, arithmetic and copies ran while one was open for 18% of the time, Pallas kernels for 0%

commit v1 on v0

--- a/solution.py
+++ b/solution.py
@@ -55,31 +55,15 @@
     return slot[None, :] == jnp.arange(peer_count * capacity, dtype=jnp.int32)[:, None]
 
 
-def place_ints(table, values, empty_value):
-    filled = jnp.any(table, axis=1)
-    picked = jnp.sum(jnp.where(table, values[None, :], 0), axis=1)
-    return jnp.where(filled, picked, empty_value)
-
-
-def pack_rows(row_block, target, places, peer_count, capacity):
-    table = slot_table(target, peer_count, capacity)
-    buffer = jnp.dot(
-        table.astype(jnp.bfloat16), row_block, preferred_element_type=jnp.float32
-    ).astype(jnp.bfloat16)
-    place_buffer = place_ints(table, places, -1)
-    return (
-        buffer.reshape(peer_count, capacity, row_block.shape[1]),
-        place_buffer.reshape(peer_count, capacity),
-    )
-
-
-def accumulate(row_block, places, centre_count):
-    onehot = (jnp.arange(centre_count, dtype=jnp.int32)[:, None] == places[None, :]).astype(
-        jnp.bfloat16
-    )
-    sums = jnp.dot(onehot, row_block, preferred_element_type=jnp.float32)
-    counts = jnp.sum(onehot, axis=1, dtype=jnp.float32)
-    return (sums, counts)
+def arrivals(mine, values, capacity):
+    count = mine.shape[1]
+    positions = jnp.arange(count, dtype=jnp.int32)
+    before = (positions[:, None] < positions[None, :]).astype(jnp.bfloat16)
+    rank = jnp.dot(mine.astype(jnp.bfloat16), before, preferred_element_type=jnp.float32)
+    rank = jnp.where(mine, rank.astype(jnp.int32), capacity)
+    places = jnp.arange(capacity, dtype=jnp.int32)
+    hit = rank[:, None, :] == places[None, :, None]
+    return jnp.sum(jnp.where(hit, values[:, None, :] + 1, 0), axis=2) - 1
 
 
 def shards(
@@ -100,6 +84,7 @@
     centroids,
 ):
     peer_count = lax.axis_size("dp")
+    me = lax.axis_index("dp")
     width = word_table.shape[1]
     vocab_rows = word_table.shape[0]
     centre_count = centroids.shape[0]
@@ -107,15 +92,38 @@
     token_list = token_ids.reshape(passes * seq_len)
     token_count = token_list.shape[0]
     row_count = row_slot.shape[0]
-    owners_all = row_owner[:, 0]
+    store_count = stored_rows.shape[0]
+    owners = row_owner[:, 0]
     token_cap = max(2, 3 * token_count // peer_count)
     row_cap = max(2, 3 * row_count // peer_count)
-    target = token_list // vocab_rows
-    table = slot_table(target, peer_count, token_cap)
-    requests = place_ints(table, token_list - target * vocab_rows, 0).reshape(peer_count, token_cap)
-    found = word_table[lax.all_to_all(requests, "dp", split_axis=0, concat_axis=0, tiled=True)]
-    fetched = lax.all_to_all(found, "dp", split_axis=0, concat_axis=0, tiled=True)
-    picker = table.T.astype(jnp.bfloat16)
+
+    plan = lax.all_gather(
+        jnp.concatenate([token_list, owners, row_slot]), "dp", axis=0, tiled=False
+    )
+    all_ids = plan[:, :token_count]
+    all_owners = plan[:, token_count : token_count + row_count]
+    all_slots = plan[:, token_count + row_count :]
+
+    row_table = slot_table(owners, peer_count, row_cap)
+    buffer = jnp.dot(
+        row_table[:, :store_count].astype(jnp.bfloat16),
+        stored_rows,
+        preferred_element_type=jnp.float32,
+    ).astype(jnp.bfloat16)
+    got_rows = lax.all_to_all(
+        buffer.reshape(peer_count, row_cap, width), "dp", split_axis=0, concat_axis=0, tiled=True
+    )
+
+    wanted = arrivals(all_ids // vocab_rows == me, all_ids - me * vocab_rows, token_cap)
+    wanted = wanted.reshape(peer_count * token_cap)
+    chosen = wanted[:, None] == jnp.arange(vocab_rows, dtype=jnp.int32)[None, :]
+    found = jnp.dot(
+        chosen.astype(jnp.bfloat16), word_table, preferred_element_type=jnp.float32
+    ).astype(jnp.bfloat16)
+    fetched = lax.all_to_all(
+        found.reshape(peer_count, token_cap, width), "dp", split_axis=0, concat_axis=0, tiled=True
+    )
+    picker = slot_table(token_list // vocab_rows, peer_count, token_cap).T.astype(jnp.bfloat16)
     tok_flat = jnp.dot(
         picker, fetched.reshape(peer_count * token_cap, width), preferred_element_type=jnp.float32
     )
@@ -132,17 +140,18 @@
         norm_gain,
         norm_bias,
     )
-    all_rows = jnp.concatenate([stored_rows, passage_embed], axis=0)
-    buffer, place_buffer = pack_rows(all_rows, owners_all, row_slot, peer_count, row_cap)
-    got_rows, got_places = (
-        lax.all_to_all(buffer, "dp", split_axis=0, concat_axis=0, tiled=True),
-        lax.all_to_all(place_buffer, "dp", split_axis=0, concat_axis=0, tiled=True),
+    all_embeds = lax.all_gather(passage_embed, "dp", axis=0, tiled=True)
+
+    centres = jnp.arange(centre_count, dtype=jnp.int32)[:, None]
+    places = arrivals(all_owners == me, all_slots, row_cap).reshape(peer_count * row_cap)
+    onehot = (centres == places[None, :]).astype(jnp.bfloat16)
+    counts = jnp.sum(onehot, axis=1, dtype=jnp.float32)
+    sums = jnp.dot(
+        onehot, got_rows.reshape(peer_count * row_cap, width), preferred_element_type=jnp.float32
     )
-    sums, counts = accumulate(
-        got_rows.reshape(peer_count * row_cap, width),
-        got_places.reshape(peer_count * row_cap),
-        centre_count,
-    )
+    late = jnp.where(all_owners[:, store_count:] == me, all_slots[:, store_count:], -1)
+    late_onehot = (centres == late.reshape(-1)[None, :]).astype(jnp.bfloat16)
+    sums = sums + jnp.dot(late_onehot, all_embeds, preferred_element_type=jnp.float32)
     new_centroids = jnp.where(
         counts[:, None] > 0, sums / jnp.maximum(counts, 1.0)[:, None], centroids
     )

time: 113 us -> 109 us (0.965)
  the two profiles are of different devices: /device:TPU:13 before, /device:TPU:9 now
where the time goes in v1:
time: 109 us; the launch traced here: 108 us
  blocking collectives  48.7 us (45%)
  matrix products  18 us (17%)
  waiting for transfers between devices  12.3 us (11%)
  starting transfers between devices  11.7 us (11%)
  local copies, waits for them, and re-layouts  8.6 us (8%)
  other arithmetic  7.66 us (7%)
    all_gather x1, blocking collectives, shards(): all_embeds = lax.all_gather(passage_embed, 'dp', axis=0, tiled=True)  29.3 us
    all_gather x1, blocking collectives, shards(): lax.all_gather(jnp.concatenate([token_list, owners, row_slot]), 'dp', axi...  19.4 us
    all_to_all x1, waiting for transfers between devices, shards(): lax.all_to_all(found.reshape(peer_count, token_cap, width), 'dp', split_a...  12.3 us
    all_to_all x1, starting transfers between devices, shards(): lax.all_to_all(found.reshape(peer_count, token_cap, width), 'dp', split_a...  7.11 us
    all_to_all x1, starting transfers between devices, shards(): lax.all_to_all(buffer.reshape(peer_count, row_cap, width), 'dp', split_ax...  4.61 us
    dot_general x1, matrix products, shards(): jnp.dot(row_table[:, :store_count].astype(jnp.bfloat16), stored_rows, pre...  2.76 us
    dot_general x1, matrix products, shards(): jnp.dot(onehot, got_rows.reshape(peer_count * row_cap, width), preferred_...  2.54 us
    dot_general x1, matrix products, shards(): jnp.dot(chosen.astype(jnp.bfloat16), word_table, preferred_element_type=j...  2.32 us
  transfers between devices with their start and end apart: 2, of which 1 were waited for; matrix products, arithmetic and copies ran while one was open for 22% of the time, Pallas kernels for 0%

profile of v1, /device:TPU:9, one launch (start us, length us, event | category | flops | bytes accessed | tf_op | source)
XLA Modules:
  0.0 108.0 jit_solution(6131567091016395509)
XLA Ops:
  0.6 0.0 copy-start
  0.6 0.0 copy-start.5
  0.7 0.0 copy-start.14
  0.7 0.9 reshape.207
  1.6 0.8 pad_add_fusion
  2.3 19.4 %all-gather.1 = s32[16,1,640]{2,1,0:T(1,128)S(1)} all-gather(s32[1,1,640]{2,1,0:T(1,128)S(1)} %reshape.216), channel_id=2, replica_groups=mesh['groups'=2,'dp'=16] {'dp'}, dimensions={0}, use_global_device_ids=true | all-gather | bytes 43520 | tf_op jit(solution)/shard_map/all_gather | solution.py:100
  21.8 0.1 fusion.9
  21.9 0.3 select_reduce_fusion.1
  22.3 0.1 sub.53
  22.4 2.3 %convolution_convert_fusion.2 = bf16[384,1024]{1,0:T(8,128)(2,1)} fusion(bf16[240,1024]{1,0:T(8,128)(2,1)} %param.17, s32[384]{0:T(512)S(1)} %sub.53), kind=kOutput, calls=%fused_computation.7 | convolution fusion | flops 189229056 | bytes 1279488 | tf_op jit(solution)/shard_map/dot_general | solution.py:120
  24.7 7.1 %all-to-all-start = ((bf16[16,24,1024]{2,1,0:T(8,128)(2,1)}), bf16[16,24,1024]{2,1,0:T(8,128)(2,1)}, u32[]{:S(2)}, u32[]{:S(2)}) async-start(bf16[16,24,1024]{2,1,0:T(8,128)(2,1)} %bitcast.41), calls=%async_computation | async-start | bytes 1572864 | tf_op jit(solution)/shard_map/all_to_all | solution.py:123
  31.8 0.0 copy-done.5
  31.8 0.2 convert_reduce_fusion.1
  32.0 0.2 fusion.8
  32.2 0.1 slice_select_fusion
  32.2 0.2 convert_reduce_fusion.2
  32.4 0.4 select_reduce_fusion
  32.8 0.1 sub.59
  32.9 0.2 convert_reduce_fusion
  33.1 0.7 eq.168
  33.8 0.0 copy-done.14
  33.8 0.8 fusion.36
  34.6 0.6 compare_convert_fusion
  35.2 0.6 broadcast_compare_fusion
  35.8 0.6 broadcast_maximum_fusion
  36.4 2.8 %convolution_convert_fusion.1 = bf16[768,1024]{1,0:T(8,128)(2,1)} fusion(bf16[254,1024]{1,0:T(8,128)(2,1)} %param.26, s32[254]{0:T(256)S(1)} %bitcast.51), kind=kOutput, calls=%fused_computation.2 | convolution fusion | flops 400488960 | bytes 2094072 | tf_op jit(solution)/shard_map/dot_general | solution.py:108
  39.2 12.3 %all-to-all-done = bf16[16,24,1024]{2,1,0:T(8,128)(2,1)} async-done(((bf16[16,24,1024]{2,1,0:T(8,128)(2,1)}), bf16[16,24,1024]{2,1,0:T(8,128)(2,1)}, u32[]{:S(2)}, u32[]{:S(2)}) %all-to-all-start) | async-done | bytes 786464 | tf_op jit(solution)/shard_map/all_to_all | solution.py:123
  51.5 4.6 %all-to-all-start.1 = ((bf16[16,48,1024]{2,1,0:T(8,128)(2,1)}), bf16[16,48,1024]{2,1,0:T(8,128)(2,1)}, u32[]{:S(2)}, u32[]{:S(2)}) async-start(bf16[16,48,1024]{2,1,0:T(8,128)(2,1)} %bitcast.40), calls=%async_computation.1 | async-start | bytes 3145728 | tf_op jit(solution)/shard_map/all_to_all | solution.py:113
  56.1 0.0 copy-done.2
  56.1 0.0 copy-start.3
  56.1 0.0 copy-start.4
  56.2 1.6 %fusion.38 = (f32[128]{0:T(128)S(1)}, f32[128,1024]{1,0:T(8,128)S(1)}) fusion(f32[128,1024]{1,0:T(8,128)S(1)} %bitcast.42, bf16[384,1024]{1,0:T(8,128)(2,1)} %bitcast.2, s32[128]{0:T(128)S(1)} %multiply_add_fusion.2), kind=kOutput, calls=%fused_computation.96 | convolution fusion | flops 101236608 | bytes 1836032 | tf_op jit(solution)/shard_map/dot_general | solution.py:127
  57.8 0.2 multiply_reduce_fusion.2
  58.0 0.6 copy-done.1
  58.6 0.5 copy-done.8
  59.1 0.0 copy-done
  59.1 0.0 copy-done.3
  59.1 0.0 copy-done.4
  59.1 0.6 convolution_convert_fusion
  59.7 1.3 %reshape.210 = bf16[2,64,3,8,64]{4,3,2,1,0:T(8,128)(2,1)} reshape(bf16[128,1536]{1,0:T(8,128)(2,1)S(1)} %convolution_convert_fusion) | data formatting | bytes 786432 | tf_op jit(solution)/shard_map/reshape | solution.py:24
  61.1 2.0 %fusion.37 = (bf16[2,64,1,8,64]{4,3,2,1,0:T(8,128)(2,1)S(1)}, bf16[2,64,1,8,64]{4,3,2,1,0:T(8,128)(2,1)}, bf16[2,64,1,8,64]{4,3,2,1,0:T(8,128)(2,1)}) fusion(bf16[2,64,3,8,64]{4,3,2,1,0:T(8,128)(2,1)} %reshape.210), kind=kLoop, calls=%fused_computation.95 | loop fusion | bytes 786432 | tf_op jit(solution)/shard_map/slice | solution.py:27
  63.1 0.9 copy.38
  64.0 0.0 copy-done.10
  64.0 2.1 %fusion.4 = f32[2,8,64,64]{2,3,1,0:T(8,128)} fusion(bf16[2,64,1,8,64]{4,3,2,1,0:T(8,128)(2,1)} %get-tuple-element.5, bf16[2,64,1,8,64]{4,3,2,1,0:T(8,128)(2,1)} %get-tuple-element.6, f32[2,64]{1,0:T(2,128)S(1)} %copy-done.10), kind=kOutput, calls=%fused_computation.12 | convolution fusion | flops 8519680 | bytes 524800 | tf_op jit(solution)/shard_map/pqhd,pkhd->phqk/dot_general | solution.py:28
  66.1 2.2 %fusion.7 = bf16[2,64,8,64]{1,3,2,0:T(8,128)(2,1)} fusion(f32[2,8,64,64]{2,3,1,0:T(8,128)} %fusion.4, bf16[2,64,1,8,64]{1,4,3,0,2:T(8,128)(2,1)} %copy.38), kind=kOutput, calls=%fused_computation.17 | convolution fusion | flops 8586303 | bytes 524288 | tf_op jit(solution)/shard_map/phqk,pkhd->pqhd/dot_general | solution.py:34
  68.4 1.1 %copy.35 = bf16[2,64,8,64]{3,2,1,0:T(8,128)(2,1)S(1)} copy(bf16[2,64,8,64]{1,3,2,0:T(8,128)(2,1)} %fusion.7) | data formatting | bytes 262144 | tf_op jit(solution)/shard_map/convert_element_type | solution.py:36
  69.5 0.2 reshape.211
  69.7 0.0 copy-start.6
  69.7 0.0 copy-start.7
  69.7 1.8 %fusion.39 = (f32[128]{0:T(128)S(1)}, f32[128,1024]{1,0:T(8,128)S(1)}) fusion(f32[1024]{0:T(1024)} %param.23, bf16[128,512]{1,0:T(8,128)(2,1)S(1)} %reshape.211, bf16[512,1024]{1,0:T(8,128)(2,1)} %param.22, f32[1024]{0:T(1024)S(1)} %copy-done.3, f32[1024]{0:T(1024)S(1)} %copy-done.4, f32[128]{0:T(128)} %copy-done.8, f32[128,1024]{1,0:T(8,128)} %copy-done.1, ...), kind=kOutput, calls=%fused_computation.97 | convolution fusion | flops 135397248 | bytes 2242048 | tf_op jit(solution)/shard_map/dot_general | solution.py:38
  71.5 0.2 multiply_reduce_fusion.1
  71.7 0.0 copy-done.6
  71.7 0.0 copy-done.7
  71.8 0.9 multiply_reduce_fusion
  72.6 0.9 multiply_reduce_fusion.3
  73.5 0.1 fusion.49
  73.6 29.3 %all-gather.2 = bf16[16,2,1024]{2,1,0:T(2,128)(2,1)S(1)} all-gather(bf16[1,2,1024]{2,1,0:T(2,128)(2,1)S(1)} %fusion.49), channel_id=1, replica_groups=mesh['groups'=2,'dp'=16] {'dp'}, dimensions={0}, use_global_device_ids=true | all-gather | bytes 69632 | tf_op jit(solution)/shard_map/all_gather | solution.py:143
  102.9 0.7 multiply_convert_fusion
  103.6 0.0 all-to-all-done.1
  103.6 0.0 copy-start.13
  103.6 2.5 %fusion = f32[512,1024]{1,0:T(8,128)S(1)} fusion(bf16[768,1024]{1,0:T(8,128)(2,1)} %bitcast.10, s32[768]{0:T(1024)S(1)} %sub.59), kind=kOutput, calls=%fused_computation.5 | convolution fusion | flops 805699584 | bytes 3673088 | tf_op jit(solution)/shard_map/dot_general | solution.py:149
  106.1 0.0 copy-done.9
  106.1 0.0 copy-done.11
  106.2 1.8 %divide_select_fusion = f32[512,1024]{1,0:T(8,128)} fusion(f32[512,1024]{1,0:T(8,128)S(1)} %copy-done.13, f32[512,1024]{1,0:T(8,128)S(1)} %fusion, bf16[32,1024]{1,0:T(8,128)(2,1)S(1)} %reshape.219, f32[512]{0:T(512)S(1)} %copy-done.9, pred[512]{0:T(512)(128)(4,1)S(1)} %copy-done.12, s32[32]{0:T(128)S(1)} %copy-done.11), kind=kOutput, calls=%fused_computation.1 | convolution fusion | flops 35143680 | bytes 6359680 | tf_op jit(solution)/shard_map/dot_general | solution.py:154
  (25 shorter events, 0.2 us)
Async XLA Ops:
  0.6 58.5 %copy-start = (bf16[1024,1536]{1,0:T(8,128)(2,1)S(1)}, bf16[1024,1536]{1,0:T(8,128)(2,1)}, u32[]{:S(2)}) copy-start(bf16[1024,1536]{1,0:T(8,128)(2,1)} %param.21) | copy-start | bytes 9437188
  0.6 31.2 %copy-start.5 = (s32[256,1]{0,1:T(1,128)S(1)}, s32[256,1]{0,1:T(1,128)}, u32[]{:S(2)}) copy-start(s32[256,1]{0,1:T(1,128)} %param.27) | copy-start | bytes 3076
  0.7 33.1 %copy-start.14 = (s32[2]{0:T(128)S(1)}, s32[2]{0:T(128)}, u32[]{:S(2)}) copy-start(s32[2]{0:T(128)} %param.16) | copy-start | bytes 28
  24.7 26.8 %all-to-all-start = ((bf16[16,24,1024]{2,1,0:T(8,128)(2,1)}), bf16[16,24,1024]{2,1,0:T(8,128)(2,1)}, u32[]{:S(2)}, u32[]{:S(2)}) async-start(bf16[16,24,1024]{2,1,0:T(8,128)(2,1)} %bitcast.41), calls=%async_computation | async-start | bytes 1572864 | tf_op jit(solution)/shard_map/all_to_all | solution.py:123
  39.2 17.0 %copy-start.2 = (bf16[64,1024]{1,0:T(8,128)(2,1)S(1)}, bf16[64,1024]{1,0:T(8,128)(2,1)}, u32[]{:S(2)}) copy-start(bf16[64,1024]{1,0:T(8,128)(2,1)} %param.18) | copy-start | bytes 393220
  51.5 52.1 %all-to-all-start.1 = ((bf16[16,48,1024]{2,1,0:T(8,128)(2,1)}), bf16[16,48,1024]{2,1,0:T(8,128)(2,1)}, u32[]{:S(2)}, u32[]{:S(2)}) async-start(bf16[16,48,1024]{2,1,0:T(8,128)(2,1)} %bitcast.40), calls=%async_computation.1 | async-start | bytes 3145728 | tf_op jit(solution)/shard_map/all_to_all | solution.py:113
  56.1 3.0 %copy-start.3 = (f32[1024]{0:T(1024)S(1)}, f32[1024]{0:T(1024)}, u32[]{:S(2)}) copy-start(f32[1024]{0:T(1024)} %param.20) | copy-start | bytes 12292
  56.1 3.0 %copy-start.4 = (f32[1024]{0:T(1024)S(1)}, f32[1024]{0:T(1024)}, u32[]{:S(2)}) copy-start(f32[1024]{0:T(1024)} %param.19) | copy-start | bytes 12292
  57.8 0.8 copy-start.1
  58.6 0.5 copy-start.8
  61.1 2.9 %copy-start.10 = (f32[2,64]{1,0:T(2,128)S(1)}, f32[2,64]{1,0:T(2,128)}, u32[]{:S(2)}) copy-start(f32[2,64]{1,0:T(2,128)} %compare_convert_fusion) | copy-start | bytes 1540
  69.7 2.0 %copy-start.6 = (f32[1024]{0:T(1024)S(1)}, f32[1024]{0:T(1024)}, u32[]{:S(2)}) copy-start(f32[1024]{0:T(1024)} %param.25) | copy-start | bytes 12292
  69.7 2.0 %copy-start.7 = (f32[1024]{0:T(1024)S(1)}, f32[1024]{0:T(1024)}, u32[]{:S(2)}) copy-start(f32[1024]{0:T(1024)} %param.24) | copy-start | bytes 12292
  103.6 2.6 %copy-start.9 = (f32[512]{0:T(512)S(1)}, f32[512]{0:T(512)}, u32[]{:S(2)}) copy-start(f32[512]{0:T(512)} %broadcast_maximum_fusion) | copy-start | bytes 6148
  103.6 2.6 %copy-start.11 = (s32[32]{0:T(128)S(1)}, s32[32]{0:T(128)}, u32[]{:S(2)}) copy-start(s32[32]{0:T(128)} %eq.168) | copy-start | bytes 388
  103.6 2.6 %copy-start.12 = (pred[512]{0:T(512)(128)(4,1)S(1)}, pred[512]{0:T(512)(128)(4,1)}, u32[]{:S(2)}) copy-start(pred[512]{0:T(512)(128)(4,1)} %broadcast_compare_fusion) | copy-start | bytes 1540
  103.6 2.6 %copy-start.13 = (f32[512,1024]{1,0:T(8,128)S(1)}, f32[512,1024]{1,0:T(8,128)}, u32[]{:S(2)}) copy-start(f32[512,1024]{1,0:T(8,128)} %param.29) | copy-start | bytes 6291460

commit v2 on v1

--- a/solution.py
+++ b/solution.py
@@ -55,15 +55,20 @@
     return slot[None, :] == jnp.arange(peer_count * capacity, dtype=jnp.int32)[:, None]
 
 
-def arrivals(mine, values, capacity):
-    count = mine.shape[1]
-    positions = jnp.arange(count, dtype=jnp.int32)
-    before = (positions[:, None] < positions[None, :]).astype(jnp.bfloat16)
-    rank = jnp.dot(mine.astype(jnp.bfloat16), before, preferred_element_type=jnp.float32)
-    rank = jnp.where(mine, rank.astype(jnp.int32), capacity)
-    places = jnp.arange(capacity, dtype=jnp.int32)
-    hit = rank[:, None, :] == places[None, :, None]
-    return jnp.sum(jnp.where(hit, values[:, None, :] + 1, 0), axis=2) - 1
+def place_ints(table, values, empty_value):
+    filled = jnp.any(table, axis=1)
+    picked = jnp.sum(jnp.where(table, values[None, :], 0), axis=1)
+    return jnp.where(filled, picked, empty_value)
+
+
+def swap_blocks(blocks, axis):
+    peers = blocks.shape[0]
+    me = lax.axis_index(axis)
+    got = [blocks[me]]
+    for step in range(1, peers):
+        moves = [(i, (i + step) % peers) for i in range(peers)]
+        got.append(lax.ppermute(blocks[(me + step) % peers], axis, moves))
+    return got
 
 
 def shards(
@@ -84,7 +89,6 @@
     centroids,
 ):
     peer_count = lax.axis_size("dp")
-    me = lax.axis_index("dp")
     width = word_table.shape[1]
     vocab_rows = word_table.shape[0]
     centre_count = centroids.shape[0]
@@ -97,25 +101,35 @@
     token_cap = max(2, 3 * token_count // peer_count)
     row_cap = max(2, 3 * row_count // peer_count)
 
-    plan = lax.all_gather(
-        jnp.concatenate([token_list, owners, row_slot]), "dp", axis=0, tiled=False
-    )
-    all_ids = plan[:, :token_count]
-    all_owners = plan[:, token_count : token_count + row_count]
-    all_slots = plan[:, token_count + row_count :]
-
+    target = token_list // vocab_rows
+    token_table = slot_table(target, peer_count, token_cap)
+    requests = place_ints(token_table, token_list - target * vocab_rows, -1)
     row_table = slot_table(owners, peer_count, row_cap)
+    places = place_ints(row_table, row_slot, -1)
+    late = jnp.where(
+        owners[None, store_count:] == jnp.arange(peer_count, dtype=jnp.int32)[:, None],
+        row_slot[None, store_count:],
+        -1,
+    )
+    plan = lax.all_to_all(
+        jnp.concatenate(
+            [requests.reshape(peer_count, token_cap), places.reshape(peer_count, row_cap), late],
+            axis=1,
+        ),
+        "dp",
+        split_axis=0,
+        concat_axis=0,
+        tiled=True,
+    )
+
     buffer = jnp.dot(
         row_table[:, :store_count].astype(jnp.bfloat16),
         stored_rows,
         preferred_element_type=jnp.float32,
     ).astype(jnp.bfloat16)
-    got_rows = lax.all_to_all(
-        buffer.reshape(peer_count, row_cap, width), "dp", split_axis=0, concat_axis=0, tiled=True
-    )
-
-    wanted = arrivals(all_ids // vocab_rows == me, all_ids - me * vocab_rows, token_cap)
-    wanted = wanted.reshape(peer_count * token_cap)
+    got_rows = swap_blocks(buffer.reshape(peer_count, row_cap, width), "dp")
+
+    wanted = plan[:, :token_cap].reshape(peer_count * token_cap)
     chosen = wanted[:, None] == jnp.arange(vocab_rows, dtype=jnp.int32)[None, :]
     found = jnp.dot(
         chosen.astype(jnp.bfloat16), word_table, preferred_element_type=jnp.float32
@@ -123,9 +137,10 @@
     fetched = lax.all_to_all(
         found.reshape(peer_count, token_cap, width), "dp", split_axis=0, concat_axis=0, tiled=True
     )
-    picker = slot_table(token_list // vocab_rows, peer_count, token_cap).T.astype(jnp.bfloat16)
     tok_flat = jnp.dot(
-        picker, fetched.reshape(peer_count * token_cap, width), preferred_element_type=jnp.float32
+        token_table.T.astype(jnp.bfloat16),
+        fetched.reshape(peer_count * token_cap, width),
+        preferred_element_type=jnp.float32,
     )
     tok_rows = tok_flat.astype(jnp.bfloat16).reshape(passes, seq_len, width)
     passage_embed = encode(
@@ -140,17 +155,22 @@
         norm_gain,
         norm_bias,
     )
-    all_embeds = lax.all_gather(passage_embed, "dp", axis=0, tiled=True)
+    all_embeds = lax.all_to_all(
+        jnp.broadcast_to(passage_embed[None], (peer_count, passes, width)),
+        "dp",
+        split_axis=0,
+        concat_axis=0,
+        tiled=True,
+    ).reshape(peer_count * passes, width)
 
     centres = jnp.arange(centre_count, dtype=jnp.int32)[:, None]
-    places = arrivals(all_owners == me, all_slots, row_cap).reshape(peer_count * row_cap)
-    onehot = (centres == places[None, :]).astype(jnp.bfloat16)
+    got_places = plan[:, token_cap : token_cap + row_cap]
+    onehot = (centres == got_places.reshape(peer_count * row_cap)[None, :]).astype(jnp.bfloat16)
     counts = jnp.sum(onehot, axis=1, dtype=jnp.float32)
-    sums = jnp.dot(
-        onehot, got_rows.reshape(peer_count * row_cap, width), preferred_element_type=jnp.float32
-    )
-    late = jnp.where(all_owners[:, store_count:] == me, all_slots[:, store_count:], -1)
-    late_onehot = (centres == late.reshape(-1)[None, :]).astype(jnp.bfloat16)
+    order = (lax.axis_index("dp") - jnp.arange(peer_count, dtype=jnp.int32)) % peer_count
+    onehot = (centres == got_places[order].reshape(peer_count * row_cap)[None, :]).astype(jnp.bfloat16)
+    sums = jnp.dot(onehot, jnp.concatenate(got_rows, axis=0), preferred_element_type=jnp.float32)
+    late_onehot = (centres == plan[:, token_cap + row_cap :].reshape(-1)[None, :]).astype(jnp.bfloat16)
     sums = sums + jnp.dot(late_onehot, all_embeds, preferred_element_type=jnp.float32)
     new_centroids = jnp.where(
         counts[:, None] > 0, sums / jnp.maximum(counts, 1.0)[:, None], centroids

time: 109 us -> 118 us (1.083)
  the two profiles are of different devices: /device:TPU:9 before, /device:TPU:0 now
where the time goes in v2:
time: 118 us; the launch traced here: 117 us
  starting transfers between devices  40.2 us (34%)
  local copies, waits for them, and re-layouts  28.9 us (24%)
  waiting for transfers between devices  23.5 us (20%)
  matrix products  16.7 us (14%)
  other arithmetic  6.44 us (5%)
  between operations  1.3 us (1%)
    ppermute x15, starting transfers between devices, swap_blocks(): got.append(lax.ppermute(blocks[(me + step) % peers], axis, moves))  26.6 us
    unnamed x62, local copies, waits for them, and re-layouts  18.3 us
    ppermute x15, waiting for transfers between devices, swap_blocks(): got.append(lax.ppermute(blocks[(me + step) % peers], axis, moves))  15.7 us
    all_to_all x1, starting transfers between devices, shards(): lax.all_to_all(jnp.concatenate([requests.reshape(peer_count, token_cap),...  5.78 us
    all_to_all x1, starting transfers between devices, shards(): lax.all_to_all(found.reshape(peer_count, token_cap, width), 'dp', split_a...  4.29 us
    dot_general x1, matrix products, shards(): jnp.dot(onehot, jnp.concatenate(got_rows, axis=0), preferred_element_type...  4.04 us
    all_to_all x1, waiting for transfers between devices, shards(): lax.all_to_all(jnp.concatenate([requests.reshape(peer_count, token_cap),...  4 us
    all_to_all x1, waiting for transfers between devices, shards(): lax.all_to_all(jnp.broadcast_to(passage_embed[None], (peer_count, passes,...  3.77 us
  transfers between devices with their start and end apart: 18, of which 4 were waited for; matrix products, arithmetic and copies ran while one was open for 34% of the time, Pallas kernels for 0%

profile of v2, /device:TPU:0, one launch (start us, length us, event | category | flops | bytes accessed | tf_op | source)
XLA Modules:
  0.0 117.1 jit_solution(7116009871699635679)
XLA Ops:
  0.8 1.0 convert_reduce_fusion.1
  1.8 0.7 multiply_add_fusion.1
  2.8 1.7 %convolution_convert_fusion.1 = bf16[768,1024]{1,0:T(8,128)(2,1)S(1)} fusion(bf16[254,1024]{1,0:T(8,128)(2,1)} %param.26, pred[768,256]{1,0:T(32,128)(4,1)S(1)} %get-tuple-element.24), kind=kOutput, calls=%fused_computation.3 | convolution fusion | flops 400293888 | bytes 2289664 | tf_op jit(solution)/shard_map/dot_general | solution.py:125
  4.6 1.1 copy-done.2
  5.7 1.1 dynamic-slice_bitcast_fusion
  6.8 0.5 collective-permute-start
  7.3 2.6 %collective-permute-start.1 = (bf16[48,1024]{1,0:T(8,128)(2,1)}, bf16[48,1024]{1,0:T(8,128)(2,1)}, u32[]{:S(2)}, u32[]{:S(2)}) collective-permute-start(bf16[48,1024]{1,0:T(8,128)(2,1)} %get-tuple-element.19), channel_id=1, source_target_pairs={{0,2},{1,3},{2,4},{3,5},{4,6},{5,7},{6,8},{7,9},{8,10},{9,11},{10,... | collective-permute-start | bytes 294920 | tf_op jit(solution)/shard_map/ppermute | solution.py:70
  9.8 2.4 %collective-permute-start.2 = (bf16[48,1024]{1,0:T(8,128)(2,1)}, bf16[48,1024]{1,0:T(8,128)(2,1)}, u32[]{:S(2)}, u32[]{:S(2)}) collective-permute-start(bf16[48,1024]{1,0:T(8,128)(2,1)} %get-tuple-element.18), channel_id=1, source_target_pairs={{0,3},{1,4},{2,5},{3,6},{4,7},{5,8},{6,9},{7,10},{8,11},{9,12},{10... | collective-permute-start | bytes 294920 | tf_op jit(solution)/shard_map/ppermute | solution.py:70
  12.3 1.6 %collective-permute-start.3 = (bf16[48,1024]{1,0:T(8,128)(2,1)}, bf16[48,1024]{1,0:T(8,128)(2,1)S(1)}, u32[]{:S(2)}, u32[]{:S(2)}) collective-permute-start(bf16[48,1024]{1,0:T(8,128)(2,1)} %get-tuple-element.17), channel_id=1, source_target_pairs={{0,4},{1,5},{2,6},{3,7},{4,8},{5,9},{6,10},{7,11},{8,12},{9,13},{1... | collective-permute-start | bytes 294920 | tf_op jit(solution)/shard_map/ppermute | solution.py:70
  15.1 0.7 pad_add_fusion
  15.8 5.8 %all-to-all-start = ((s32[16,1,74]{2,1,0:T(1,128)}), s32[16,1,74]{2,1,0:T(1,128)S(1)}, u32[]{:S(2)}, u32[]{:S(2)}) async-start(s32[16,1,74]{2,1,0:T(1,128)} %bitcast.2), calls=%async_computation | async-start | bytes 16384 | tf_op jit(solution)/shard_map/all_to_all | solution.py:114
  21.7 0.8 fusion.25
  22.4 1.5 %bitcast_dynamic-update-slice_fusion = bf16[768,1024]{1,0:T(8,128)(2,1)} fusion(bf16[16,48,1024]{2,1,0:T(8,128)(2,1)} %bitcast.73, s32[]{:T(128)S(6)} %select_n.195), kind=kLoop, calls=%fused_computation.45 | loop fusion | bytes 196612
  24.0 4.0 %all-to-all-done = s32[16,1,74]{2,1,0:T(1,128)S(1)} async-done(((s32[16,1,74]{2,1,0:T(1,128)}), s32[16,1,74]{2,1,0:T(1,128)S(1)}, u32[]{:S(2)}, u32[]{:S(2)}) %all-to-all-start) | async-done | bytes 4768 | tf_op jit(solution)/shard_map/all_to_all | solution.py:114
  28.5 0.6 broadcast_maximum_fusion
  29.0 2.3 %convolution_convert_fusion.2 = bf16[384,1024]{1,0:T(8,128)(2,1)} fusion(bf16[240,1024]{1,0:T(8,128)(2,1)} %param.17, s32[384]{0:T(512)S(1)} %eq.161), kind=kOutput, calls=%fused_computation.8 | convolution fusion | flops 189229056 | bytes 1279488 | tf_op jit(solution)/shard_map/dot_general | solution.py:134
  31.3 0.6 broadcast_compare_fusion
  32.0 4.3 %all-to-all-start.1 = ((bf16[16,24,1024]{2,1,0:T(8,128)(2,1)}), bf16[16,24,1024]{2,1,0:T(8,128)(2,1)}, u32[]{:S(2)}, u32[]{:S(2)}) async-start(bf16[16,24,1024]{2,1,0:T(8,128)(2,1)} %bitcast.74), calls=%async_computation.1 | async-start | bytes 1572864 | tf_op jit(solution)/shard_map/all_to_all | solution.py:137
  36.3 0.6 eq.174
  36.9 0.6 gather_fusion
  37.5 0.7 eq.170
  38.2 2.7 %collective-permute-start.5 = (bf16[48,1024]{1,0:T(8,128)(2,1)}, bf16[48,1024]{1,0:T(8,128)(2,1)S(1)}, u32[]{:S(2)}, u32[]{:S(2)}) collective-permute-start(bf16[48,1024]{1,0:T(8,128)(2,1)} %get-tuple-element.15), channel_id=1, source_target_pairs={{0,6},{1,7},{2,8},{3,9},{4,10},{5,11},{6,12},{7,13},{8,14},{9,15},... | collective-permute-start | bytes 294920 | tf_op jit(solution)/shard_map/ppermute | solution.py:70
  40.8 1.5 %constant_dynamic-update-slice_fusion.14 = bf16[768,1024]{1,0:T(8,128)(2,1)} fusion(bf16[768,1024]{1,0:T(8,128)(2,1)} %bitcast_dynamic-update-slice_fusion, bf16[48,1024]{1,0:T(8,128)(2,1)} %collective-permute-done), kind=kLoop, calls=%fused_computation.79 | loop fusion | bytes 196608
  42.4 1.9 %collective-permute-start.6 = (bf16[48,1024]{1,0:T(8,128)(2,1)}, bf16[48,1024]{1,0:T(8,128)(2,1)S(1)}, u32[]{:S(2)}, u32[]{:S(2)}) collective-permute-start(bf16[48,1024]{1,0:T(8,128)(2,1)} %get-tuple-element.14), channel_id=1, source_target_pairs={{0,7},{1,8},{2,9},{3,10},{4,11},{5,12},{6,13},{7,14},{8,15},{9,0},... | collective-permute-start | bytes 294920 | tf_op jit(solution)/shard_map/ppermute | solution.py:70
  44.2 1.5 %constant_dynamic-update-slice_fusion.13 = bf16[768,1024]{1,0:T(8,128)(2,1)} fusion(bf16[768,1024]{1,0:T(8,128)(2,1)} %constant_dynamic-update-slice_fusion.14, bf16[48,1024]{1,0:T(8,128)(2,1)} %collective-permute-done.1), kind=kLoop, calls=%fused_computation.78 | loop fusion | bytes 196608
  45.8 0.5 collective-permute-start.7
  46.3 1.5 %constant_dynamic-update-slice_fusion.12 = bf16[768,1024]{1,0:T(8,128)(2,1)} fusion(bf16[768,1024]{1,0:T(8,128)(2,1)} %constant_dynamic-update-slice_fusion.13, bf16[48,1024]{1,0:T(8,128)(2,1)} %collective-permute-done.2), kind=kLoop, calls=%fused_computation.77 | loop fusion | bytes 196608
  47.9 2.4 %collective-permute-start.8 = (bf16[48,1024]{1,0:T(8,128)(2,1)}, bf16[48,1024]{1,0:T(8,128)(2,1)S(1)}, u32[]{:S(2)}, u32[]{:S(2)}) collective-permute-start(bf16[48,1024]{1,0:T(8,128)(2,1)} %get-tuple-element.12), channel_id=1, source_target_pairs={{0,9},{1,10},{2,11},{3,12},{4,13},{5,14},{6,15},{7,0},{8,1},{9,2},... | collective-permute-start | bytes 294920 | tf_op jit(solution)/shard_map/ppermute | solution.py:70
  50.2 0.7 constant_dynamic-update-slice_fusion.11
  50.9 1.4 %collective-permute-start.9 = (bf16[48,1024]{1,0:T(8,128)(2,1)}, bf16[48,1024]{1,0:T(8,128)(2,1)S(1)}, u32[]{:S(2)}, u32[]{:S(2)}) collective-permute-start(bf16[48,1024]{1,0:T(8,128)(2,1)} %get-tuple-element.11), channel_id=1, source_target_pairs={{0,10},{1,11},{2,12},{3,13},{4,14},{5,15},{6,0},{7,1},{8,2},{9,3},... | collective-permute-start | bytes 294920 | tf_op jit(solution)/shard_map/ppermute | solution.py:70
  52.3 0.6 constant_dynamic-update-slice_fusion.10
  53.0 15.0 %collective-permute-done.5 = bf16[48,1024]{1,0:T(8,128)(2,1)S(1)} collective-permute-done((bf16[48,1024]{1,0:T(8,128)(2,1)}, bf16[48,1024]{1,0:T(8,128)(2,1)S(1)}, u32[]{:S(2)}, u32[]{:S(2)}) %collective-permute-start.5) | collective-permute-done | bytes 98336 | tf_op jit(solution)/shard_map/ppermute | solution.py:70
  68.0 0.6 constant_dynamic-update-slice_fusion.9
  68.7 0.6 collective-permute-done.6
  69.3 5.0 %collective-permute-start.11 = (bf16[48,1024]{1,0:T(8,128)(2,1)}, bf16[48,1024]{1,0:T(8,128)(2,1)S(1)}, u32[]{:S(2)}, u32[]{:S(2)}) collective-permute-start(bf16[48,1024]{1,0:T(8,128)(2,1)} %get-tuple-element.9), channel_id=1, source_target_pairs={{0,12},{1,13},{2,14},{3,15},{4,0},{5,1},{6,2},{7,3},{8,4},{9,5},{1... | collective-permute-start | bytes 294920 | tf_op jit(solution)/shard_map/ppermute | solution.py:70
  74.3 0.6 constant_dynamic-update-slice_fusion.8
  74.9 1.9 %collective-permute-start.12 = (bf16[48,1024]{1,0:T(8,128)(2,1)}, bf16[48,1024]{1,0:T(8,128)(2,1)S(1)}, u32[]{:S(2)}, u32[]{:S(2)}) collective-permute-start(bf16[48,1024]{1,0:T(8,128)(2,1)} %get-tuple-element.8), channel_id=1, source_target_pairs={{0,13},{1,14},{2,15},{3,0},{4,1},{5,2},{6,3},{7,4},{8,5},{9,6},{10... | collective-permute-start | bytes 294920 | tf_op jit(solution)/shard_map/ppermute | solution.py:70
  76.8 0.6 constant_dynamic-update-slice_fusion.7
  77.5 1.6 %collective-permute-start.13 = (bf16[48,1024]{1,0:T(8,128)(2,1)}, bf16[48,1024]{1,0:T(8,128)(2,1)}, u32[]{:S(2)}, u32[]{:S(2)}) collective-permute-start(bf16[48,1024]{1,0:T(8,128)(2,1)} %get-tuple-element.7), channel_id=1, source_target_pairs={{0,14},{1,15},{2,0},{3,1},{4,2},{5,3},{6,4},{7,5},{8,6},{9,7},{10,... | collective-permute-start | bytes 294920 | tf_op jit(solution)/shard_map/ppermute | solution.py:70
  79.1 0.6 constant_dynamic-update-slice_fusion.6
  79.7 2.1 %collective-permute-start.14 = (bf16[48,1024]{1,0:T(8,128)(2,1)}, bf16[48,1024]{1,0:T(8,128)(2,1)}, u32[]{:S(2)}, u32[]{:S(2)}) collective-permute-start(bf16[48,1024]{1,0:T(8,128)(2,1)} %get-tuple-element.6), channel_id=1, source_target_pairs={{0,15},{1,0},{2,1},{3,2},{4,3},{5,4},{6,5},{7,6},{8,7},{9,8},{10,9... | collective-permute-start | bytes 294920 | tf_op jit(solution)/shard_map/ppermute | solution.py:70
  81.8 0.6 constant_dynamic-update-slice_fusion.5
  82.4 0.6 constant_dynamic-update-slice_fusion.4
  83.1 0.6 constant_dynamic-update-slice_fusion.3
  83.7 0.7 constant_dynamic-update-slice_fusion.2
  84.4 1.6 %fusion.27 = (f32[128]{0:T(128)S(1)}, f32[128,1024]{1,0:T(8,128)S(1)}) fusion(f32[128,1024]{1,0:T(8,128)S(1)} %bitcast.75, bf16[384,1024]{1,0:T(8,128)(2,1)} %bitcast.5, s32[128]{0:T(128)S(1)} %multiply_add_fusion.2), kind=kOutput, calls=%fused_computation.112 | convolution fusion | flops 101236608 | bytes 1836032 | tf_op jit(solution)/shard_map/dot_general | solution.py:140
  86.2 0.6 copy-done.1
  86.8 0.6 copy-done.13
  87.4 0.6 convolution_convert_fusion
  88.0 1.3 %reshape.297 = bf16[2,64,3,8,64]{4,3,2,1,0:T(8,128)(2,1)} reshape(bf16[128,1536]{1,0:T(8,128)(2,1)S(1)} %convolution_convert_fusion) | data formatting | bytes 786432 | tf_op jit(solution)/shard_map/reshape | solution.py:24
  89.4 2.0 %fusion.26 = (bf16[2,64,1,8,64]{4,3,2,1,0:T(8,128)(2,1)S(1)}, bf16[2,64,1,8,64]{4,3,2,1,0:T(8,128)(2,1)}, bf16[2,64,1,8,64]{4,3,2,1,0:T(8,128)(2,1)}) fusion(bf16[2,64,3,8,64]{4,3,2,1,0:T(8,128)(2,1)} %reshape.297), kind=kLoop, calls=%fused_computation.111 | loop fusion | bytes 786432 | tf_op jit(solution)/shard_map/slice | solution.py:27
  91.3 0.9 copy.37
  92.2 2.1 %fusion.3 = f32[2,8,64,64]{2,3,1,0:T(8,128)} fusion(bf16[2,64,1,8,64]{4,3,2,1,0:T(8,128)(2,1)} %get-tuple-element.22, bf16[2,64,1,8,64]{4,3,2,1,0:T(8,128)(2,1)} %get-tuple-element.23, f32[2,64]{1,0:T(2,128)S(1)} %compare_convert_fusion), kind=kOutput, calls=%fused_computation.13 | convolution fusion | flops 8519680 | bytes 524800 | tf_op jit(solution)/shard_map/pqhd,pkhd->phqk/dot_general | solution.py:28
  94.3 2.2 %fusion.6 = bf16[2,64,8,64]{1,3,2,0:T(8,128)(2,1)} fusion(f32[2,8,64,64]{2,3,1,0:T(8,128)} %fusion.3, bf16[2,64,1,8,64]{1,4,3,0,2:T(8,128)(2,1)} %copy.37), kind=kOutput, calls=%fused_computation.18 | convolution fusion | flops 8586303 | bytes 524288 | tf_op jit(solution)/shard_map/phqk,pkhd->pqhd/dot_general | solution.py:34
  96.6 1.1 copy.35
  98.0 1.8 %fusion.28 = (f32[128]{0:T(128)S(1)}, f32[128,1024]{1,0:T(8,128)S(1)}) fusion(f32[1024]{0:T(1024)S(1)} %copy-done.9, bf16[128,512]{1,0:T(8,128)(2,1)S(1)} %reshape.298, bf16[512,1024]{1,0:T(8,128)(2,1)} %param.22, f32[1024]{0:T(1024)S(1)} %copy-done.4, f32[1024]{0:T(1024)S(1)} %copy-done.5, f32[128]{0:T(128)} %copy-done.13, f32[128,1024]{1,0:T(8,128)} %copy-done.1, ...), kind=kOutput, calls=%fused_computation.113 | convolution fusion | flops 135397248 | bytes 2242048 | tf_op jit(solution)/shard_map/dot_general | solution.py:38
  100.5 0.7 broadcast_in_dim.60
  101.2 3.5 %all-to-all-start.2 = ((bf16[16,2,1024]{2,1,0:T(2,128)(2,1)}), bf16[16,2,1024]{2,1,0:T(2,128)(2,1)S(1)}, u32[]{:S(2)}, u32[]{:S(2)}) async-start(bf16[16,2,1024]{2,1,0:T(2,128)(2,1)} %broadcast_in_dim.60), calls=%async_computation.2 | async-start | bytes 131072 | tf_op jit(solution)/shard_map/all_to_all | solution.py:158
  104.7 1.5 %constant_dynamic-update-slice_fusion.1 = bf16[768,1024]{1,0:T(8,128)(2,1)} fusion(bf16[768,1024]{1,0:T(8,128)(2,1)} %constant_dynamic-update-slice_fusion.2, bf16[48,1024]{1,0:T(8,128)(2,1)} %collective-permute-done.13), kind=kLoop, calls=%fused_computation.66 | loop fusion | bytes 196608
  106.3 1.5 %constant_dynamic-update-slice_fusion = bf16[768,1024]{1,0:T(8,128)(2,1)} fusion(bf16[768,1024]{1,0:T(8,128)(2,1)} %constant_dynamic-update-slice_fusion.1, bf16[48,1024]{1,0:T(8,128)(2,1)} %collective-permute-done.14), kind=kLoop, calls=%fused_computation.65 | loop fusion | bytes 196608 | tf_op jit(solution)/shard_map/concatenate | solution.py:172
  107.8 3.8 %all-to-all-done.2 = bf16[16,2,1024]{2,1,0:T(2,128)(2,1)S(1)} async-done(((bf16[16,2,1024]{2,1,0:T(2,128)(2,1)}), bf16[16,2,1024]{2,1,0:T(2,128)(2,1)S(1)}, u32[]{:S(2)}, u32[]{:S(2)}) %all-to-all-start.2) | async-done | bytes 65568 | tf_op jit(solution)/shard_map/all_to_all | solution.py:158
  111.6 0.4 fusion.14
  112.1 0.9 copy-done.8
  113.0 4.0 %divide_select_fusion = f32[512,1024]{1,0:T(8,128)} fusion(f32[512,1024]{1,0:T(8,128)} %param.29, f32[512,1024]{1,0:T(8,128)S(1)} %fusion.14, bf16[768,1024]{1,0:T(8,128)(2,1)S(1)} %copy-done.8, f32[512]{0:T(512)S(1)} %copy-done.15, pred[512]{0:T(512)(128)(4,1)S(1)} %copy-done.19, s32[768]{0:T(1024)S(1)} %copy-done.12), kind=kOutput, calls=%fused_computation.2 | convolution fusion | flops 807272448 | bytes 7869952 | tf_op jit(solution)/shard_map/dot_general | solution.py:172
  (94 shorter events, 3.4 us)
Async XLA Ops:
  0.6 86.8 %copy-start = (bf16[1024,1536]{1,0:T(8,128)(2,1)S(1)}, bf16[1024,1536]{1,0:T(8,128)(2,1)}, u32[]{:S(2)}) copy-start(bf16[1024,1536]{1,0:T(8,128)(2,1)} %param.21) | copy-start | bytes 9437188
  4.5 1.1 copy-start.2
  4.5 9.4 %copy-start.18 = (s32[256]{0:T(256)S(1)}, s32[256]{0:T(256)}, u32[]{:S(2)}) copy-start(s32[256]{0:T(256)} %param.28) | copy-start | bytes 3076
  4.6 9.7 %copy-start.7 = (s32[256,1]{0,1:T(1,128)S(1)}, s32[256,1]{0,1:T(1,128)}, u32[]{:S(2)}) copy-start(s32[256,1]{0,1:T(1,128)} %param.27) | copy-start | bytes 3076
  4.6 9.8 %copy-start.21 = (s32[2,64]{1,0:T(2,128)S(1)}, s32[2,64]{1,0:T(2,128)}, u32[]{:S(2)}) copy-start(s32[2,64]{1,0:T(2,128)} %param.15) | copy-start | bytes 1540
  4.6 17.0 %copy-start.22 = (s32[2]{0:T(128)S(1)}, s32[2]{0:T(128)}, u32[]{:S(2)}) copy-start(s32[2]{0:T(128)} %param.16) | copy-start | bytes 28
  6.8 31.3 %collective-permute-start = (bf16[48,1024]{1,0:T(8,128)(2,1)}, bf16[48,1024]{1,0:T(8,128)(2,1)}, u32[]{:S(2)}, u32[]{:S(2)}) collective-permute-start(bf16[48,1024]{1,0:T(8,128)(2,1)} %get-tuple-element.20), channel_id=1, source_target_pairs={{0,1},{1,2},{2,3},{3,4},{4,5},{5,6},{6,7},{7,8},{8,9},{9,10},{10,1... | collective-permute-start | bytes 294920 | tf_op jit(solution)/shard_map/ppermute | solution.py:70
  7.3 35.1 %collective-permute-start.1 = (bf16[48,1024]{1,0:T(8,128)(2,1)}, bf16[48,1024]{1,0:T(8,128)(2,1)}, u32[]{:S(2)}, u32[]{:S(2)}) collective-permute-start(bf16[48,1024]{1,0:T(8,128)(2,1)} %get-tuple-element.19), channel_id=1, source_target_pairs={{0,2},{1,3},{2,4},{3,5},{4,6},{5,7},{6,8},{7,9},{8,10},{9,11},{10,... | collective-permute-start | bytes 294920 | tf_op jit(solution)/shard_map/ppermute | solution.py:70
  9.8 36.0 %collective-permute-start.2 = (bf16[48,1024]{1,0:T(8,128)(2,1)}, bf16[48,1024]{1,0:T(8,128)(2,1)}, u32[]{:S(2)}, u32[]{:S(2)}) collective-permute-start(bf16[48,1024]{1,0:T(8,128)(2,1)} %get-tuple-element.18), channel_id=1, source_target_pairs={{0,3},{1,4},{2,5},{3,6},{4,7},{5,8},{6,9},{7,10},{8,11},{9,12},{10... | collective-permute-start | bytes 294920 | tf_op jit(solution)/shard_map/ppermute | solution.py:70
  12.3 35.6 %collective-permute-start.3 = (bf16[48,1024]{1,0:T(8,128)(2,1)}, bf16[48,1024]{1,0:T(8,128)(2,1)S(1)}, u32[]{:S(2)}, u32[]{:S(2)}) collective-permute-start(bf16[48,1024]{1,0:T(8,128)(2,1)} %get-tuple-element.17), channel_id=1, source_target_pairs={{0,4},{1,5},{2,6},{3,7},{4,8},{5,9},{6,10},{7,11},{8,12},{9,13},{1... | collective-permute-start | bytes 294920 | tf_op jit(solution)/shard_map/ppermute | solution.py:70
  13.8 37.1 %collective-permute-start.4 = (bf16[48,1024]{1,0:T(8,128)(2,1)}, bf16[48,1024]{1,0:T(8,128)(2,1)S(1)}, u32[]{:S(2)}, u32[]{:S(2)}) collective-permute-start(bf16[48,1024]{1,0:T(8,128)(2,1)} %get-tuple-element.16), channel_id=1, source_target_pairs={{0,5},{1,6},{2,7},{3,8},{4,9},{5,10},{6,11},{7,12},{8,13},{9,14},{... | collective-permute-start | bytes 294920 | tf_op jit(solution)/shard_map/ppermute | solution.py:70
  15.8 12.2 %all-to-all-start = ((s32[16,1,74]{2,1,0:T(1,128)}), s32[16,1,74]{2,1,0:T(1,128)S(1)}, u32[]{:S(2)}, u32[]{:S(2)}) async-start(s32[16,1,74]{2,1,0:T(1,128)} %bitcast.2), calls=%async_computation | async-start | bytes 16384 | tf_op jit(solution)/shard_map/all_to_all | solution.py:114
  21.7 70.6 %copy-start.16 = (f32[2,64]{1,0:T(2,128)}, f32[2,64]{1,0:T(2,128)S(1)}, u32[]{:S(2)}) copy-start(f32[2,64]{1,0:T(2,128)S(1)} %compare_convert_fusion) | copy-start | bytes 1540
  32.0 52.4 %all-to-all-start.1 = ((bf16[16,24,1024]{2,1,0:T(8,128)(2,1)}), bf16[16,24,1024]{2,1,0:T(8,128)(2,1)}, u32[]{:S(2)}, u32[]{:S(2)}) async-start(bf16[16,24,1024]{2,1,0:T(8,128)(2,1)} %bitcast.74), calls=%async_computation.1 | async-start | bytes 1572864 | tf_op jit(solution)/shard_map/all_to_all | solution.py:137
  36.3 48.1 %copy-start.3 = (bf16[64,1024]{1,0:T(8,128)(2,1)S(1)}, bf16[64,1024]{1,0:T(8,128)(2,1)}, u32[]{:S(2)}) copy-start(bf16[64,1024]{1,0:T(8,128)(2,1)} %param.18) | copy-start | bytes 393220
  38.2 29.9 %collective-permute-start.5 = (bf16[48,1024]{1,0:T(8,128)(2,1)}, bf16[48,1024]{1,0:T(8,128)(2,1)S(1)}, u32[]{:S(2)}, u32[]{:S(2)}) collective-permute-start(bf16[48,1024]{1,0:T(8,128)(2,1)} %get-tuple-element.15), channel_id=1, source_target_pairs={{0,6},{1,7},{2,8},{3,9},{4,10},{5,11},{6,12},{7,13},{8,14},{9,15},... | collective-permute-start | bytes 294920 | tf_op jit(solution)/shard_map/ppermute | solution.py:70
  42.4 26.9 %collective-permute-start.6 = (bf16[48,1024]{1,0:T(8,128)(2,1)}, bf16[48,1024]{1,0:T(8,128)(2,1)S(1)}, u32[]{:S(2)}, u32[]{:S(2)}) collective-permute-start(bf16[48,1024]{1,0:T(8,128)(2,1)} %get-tuple-element.14), channel_id=1, source_target_pairs={{0,7},{1,8},{2,9},{3,10},{4,11},{5,12},{6,13},{7,14},{8,15},{9,0},... | collective-permute-start | bytes 294920 | tf_op jit(solution)/shard_map/ppermute | solution.py:70
  45.8 29.1 %collective-permute-start.7 = (bf16[48,1024]{1,0:T(8,128)(2,1)}, bf16[48,1024]{1,0:T(8,128)(2,1)S(1)}, u32[]{:S(2)}, u32[]{:S(2)}) collective-permute-start(bf16[48,1024]{1,0:T(8,128)(2,1)} %get-tuple-element.13), channel_id=1, source_target_pairs={{0,8},{1,9},{2,10},{3,11},{4,12},{5,13},{6,14},{7,15},{8,0},{9,1},... | collective-permute-start | bytes 294920 | tf_op jit(solution)/shard_map/ppermute | solution.py:70
  47.9 29.6 %collective-permute-start.8 = (bf16[48,1024]{1,0:T(8,128)(2,1)}, bf16[48,1024]{1,0:T(8,128)(2,1)S(1)}, u32[]{:S(2)}, u32[]{:S(2)}) collective-permute-start(bf16[48,1024]{1,0:T(8,128)(2,1)} %get-tuple-element.12), channel_id=1, source_target_pairs={{0,9},{1,10},{2,11},{3,12},{4,13},{5,14},{6,15},{7,0},{8,1},{9,2},... | collective-permute-start | bytes 294920 | tf_op jit(solution)/shard_map/ppermute | solution.py:70
  50.9 28.8 %collective-permute-start.9 = (bf16[48,1024]{1,0:T(8,128)(2,1)}, bf16[48,1024]{1,0:T(8,128)(2,1)S(1)}, u32[]{:S(2)}, u32[]{:S(2)}) collective-permute-start(bf16[48,1024]{1,0:T(8,128)(2,1)} %get-tuple-element.11), channel_id=1, source_target_pairs={{0,10},{1,11},{2,12},{3,13},{4,14},{5,15},{6,0},{7,1},{8,2},{9,3},... | collective-permute-start | bytes 294920 | tf_op jit(solution)/shard_map/ppermute | solution.py:70
  68.0 14.4 %collective-permute-start.10 = (bf16[48,1024]{1,0:T(8,128)(2,1)}, bf16[48,1024]{1,0:T(8,128)(2,1)S(1)}, u32[]{:S(2)}, u32[]{:S(2)}) collective-permute-start(bf16[48,1024]{1,0:T(8,128)(2,1)} %get-tuple-element.10), channel_id=1, source_target_pairs={{0,11},{1,12},{2,13},{3,14},{4,15},{5,0},{6,1},{7,2},{8,3},{9,4},{... | collective-permute-start | bytes 294920 | tf_op jit(solution)/shard_map/ppermute | solution.py:70
  69.3 13.8 %collective-permute-start.11 = (bf16[48,1024]{1,0:T(8,128)(2,1)}, bf16[48,1024]{1,0:T(8,128)(2,1)S(1)}, u32[]{:S(2)}, u32[]{:S(2)}) collective-permute-start(bf16[48,1024]{1,0:T(8,128)(2,1)} %get-tuple-element.9), channel_id=1, source_target_pairs={{0,12},{1,13},{2,14},{3,15},{4,0},{5,1},{6,2},{7,3},{8,4},{9,5},{1... | collective-permute-start | bytes 294920 | tf_op jit(solution)/shard_map/ppermute | solution.py:70
  74.9 8.8 %collective-permute-start.12 = (bf16[48,1024]{1,0:T(8,128)(2,1)}, bf16[48,1024]{1,0:T(8,128)(2,1)S(1)}, u32[]{:S(2)}, u32[]{:S(2)}) collective-permute-start(bf16[48,1024]{1,0:T(8,128)(2,1)} %get-tuple-element.8), channel_id=1, source_target_pairs={{0,13},{1,14},{2,15},{3,0},{4,1},{5,2},{6,3},{7,4},{8,5},{9,6},{10... | collective-permute-start | bytes 294920 | tf_op jit(solution)/shard_map/ppermute | solution.py:70
  77.5 27.2 %collective-permute-start.13 = (bf16[48,1024]{1,0:T(8,128)(2,1)}, bf16[48,1024]{1,0:T(8,128)(2,1)}, u32[]{:S(2)}, u32[]{:S(2)}) collective-permute-start(bf16[48,1024]{1,0:T(8,128)(2,1)} %get-tuple-element.7), channel_id=1, source_target_pairs={{0,14},{1,15},{2,0},{3,1},{4,2},{5,3},{6,4},{7,5},{8,6},{9,7},{10,... | collective-permute-start | bytes 294920 | tf_op jit(solution)/shard_map/ppermute | solution.py:70
  79.7 26.6 %collective-permute-start.14 = (bf16[48,1024]{1,0:T(8,128)(2,1)}, bf16[48,1024]{1,0:T(8,128)(2,1)}, u32[]{:S(2)}, u32[]{:S(2)}) collective-permute-start(bf16[48,1024]{1,0:T(8,128)(2,1)} %get-tuple-element.6), channel_id=1, source_target_pairs={{0,15},{1,0},{2,1},{3,2},{4,3},{5,4},{6,5},{7,6},{8,7},{9,8},{10,9... | collective-permute-start | bytes 294920 | tf_op jit(solution)/shard_map/ppermute | solution.py:70
  83.7 3.7 %copy-start.4 = (f32[1024]{0:T(1024)S(1)}, f32[1024]{0:T(1024)}, u32[]{:S(2)}) copy-start(f32[1024]{0:T(1024)} %param.20) | copy-start | bytes 12292
  83.7 3.7 %copy-start.5 = (f32[1024]{0:T(1024)S(1)}, f32[1024]{0:T(1024)}, u32[]{:S(2)}) copy-start(f32[1024]{0:T(1024)} %param.19) | copy-start | bytes 12292
  86.0 0.8 copy-start.1
  86.8 0.6 copy-start.13
  94.3 3.6 %copy-start.9 = (f32[1024]{0:T(1024)S(1)}, f32[1024]{0:T(1024)}, u32[]{:S(2)}) copy-start(f32[1024]{0:T(1024)} %param.23) | copy-start | bytes 12292
  97.9 2.0 %copy-start.10 = (f32[1024]{0:T(1024)S(1)}, f32[1024]{0:T(1024)}, u32[]{:S(2)}) copy-start(f32[1024]{0:T(1024)} %param.25) | copy-start | bytes 12292
  97.9 2.0 %copy-start.11 = (f32[1024]{0:T(1024)S(1)}, f32[1024]{0:T(1024)}, u32[]{:S(2)}) copy-start(f32[1024]{0:T(1024)} %param.24) | copy-start | bytes 12292
  98.0 2.0 %copy-start.17 = (f32[2,64]{1,0:T(2,128)S(1)}, f32[2,64]{1,0:T(2,128)}, u32[]{:S(2)}) copy-start(f32[2,64]{1,0:T(2,128)} %copy-done.16) | copy-start | bytes 1540
  98.0 2.2 %copy-start.20 = (f32[2]{0:T(128)S(1)}, f32[2]{0:T(128)}, u32[]{:S(2)}) copy-start(f32[2]{0:T(128)} %fusion.25) | copy-start | bytes 28
  98.0 13.6 %copy-start.14 = (s32[32]{0:T(128)S(1)}, s32[32]{0:T(128)}, u32[]{:S(2)}) copy-start(s32[32]{0:T(128)} %eq.174) | copy-start | bytes 388
  100.2 11.8 %copy-start.12 = (s32[768]{0:T(1024)S(1)}, s32[768]{0:T(1024)}, u32[]{:S(2)}) copy-start(s32[768]{0:T(1024)} %eq.170) | copy-start | bytes 9220
  100.2 11.8 %copy-start.15 = (f32[512]{0:T(512)S(1)}, f32[512]{0:T(512)}, u32[]{:S(2)}) copy-start(f32[512]{0:T(512)} %broadcast_maximum_fusion) | copy-start | bytes 6148
  100.2 11.8 %copy-start.19 = (pred[512]{0:T(512)(128)(4,1)S(1)}, pred[512]{0:T(512)(128)(4,1)}, u32[]{:S(2)}) copy-start(pred[512]{0:T(512)(128)(4,1)} %broadcast_compare_fusion) | copy-start | bytes 1540
  100.5 16.5 %copy-start.6 = (bf16[2,1024]{1,0:T(2,128)(2,1)}, bf16[2,1024]{1,0:T(2,128)(2,1)S(1)}, u32[]{:S(2)}) copy-start(bf16[2,1024]{1,0:T(2,128)(2,1)S(1)} %multiply_convert_fusion) | copy-start | bytes 12292
  101.2 10.4 %all-to-all-start.2 = ((bf16[16,2,1024]{2,1,0:T(2,128)(2,1)}), bf16[16,2,1024]{2,1,0:T(2,128)(2,1)S(1)}, u32[]{:S(2)}, u32[]{:S(2)}) async-start(bf16[16,2,1024]{2,1,0:T(2,128)(2,1)} %broadcast_in_dim.60), calls=%async_computation.2 | async-start | bytes 131072 | tf_op jit(solution)/shard_map/all_to_all | solution.py:158
  111.6 1.4 %copy-start.8 = (bf16[768,1024]{1,0:T(8,128)(2,1)S(1)}, bf16[768,1024]{1,0:T(8,128)(2,1)}, u32[]{:S(2)}) copy-start(bf16[768,1024]{1,0:T(8,128)(2,1)} %constant_dynamic-update-slice_fusion) | copy-start | bytes 4718596

commit v3 on v2

v3 whole, which is shorter than its diff:
```python
import jax
import jax.numpy as jnp
from jax import lax
from jax.experimental import pallas as pl
from jax.experimental.pallas import tpu as pltpu
from jax.sharding import PartitionSpec as P

HEADS = 8
HD = 64


def normed(values, gain, shift):
    center = values - jnp.mean(values, axis=-1, keepdims=True)
    spread = jnp.mean(center * center, axis=-1, keepdims=True)
    return center * lax.rsqrt(spread + 1e-12) * gain + shift


def head_sums(weights, seq):
    rows, columns = weights.shape
    lane = lax.broadcasted_iota(jnp.int32, (rows, 2 * seq), 1)
    sums = []
    for start in range(0, columns, 2 * seq):
        pair = weights[:, start : start + 2 * seq]
        first = jnp.sum(jnp.where(lane < seq, pair, 0.0), axis=1, keepdims=True)
        second = jnp.sum(jnp.where(lane < seq, 0.0, pair), axis=1, keepdims=True)
        sums.append(jnp.where(lane < seq, first, second))
    return jnp.concatenate(sums, axis=1)


def encode_kernel(
    lengths, slots, fetched, pos, emb_gain, emb_bias, w_qkv, w_out, out_bias, norm_gain, norm_bias, out
):
    tokens, slot_count = slots.shape[0], fetched.shape[0]
    passes = out.shape[0]
    seq = tokens // passes
    inner = HEADS * HD
    spot = lax.broadcasted_iota(jnp.int32, (tokens, slot_count), 1)
    picker = jnp.where(slots[...] == spot, 1.0, 0.0).astype(jnp.bfloat16)
    tok = jnp.dot(picker, fetched[...], preferred_element_type=jnp.float32)
    where_at = pos[...].astype(jnp.float32)
    summed = tok + jnp.concatenate([where_at] * passes, axis=0)
    embedded = normed(summed, emb_gain[...], emb_bias[...]).astype(jnp.bfloat16)
    projected = jnp.dot(embedded, w_qkv[...], preferred_element_type=jnp.float32)
    projected = projected.astype(jnp.bfloat16)

    block_row = lax.broadcasted_iota(jnp.int32, (HEADS * seq, inner), 0) // seq
    block_col = lax.broadcasted_iota(jnp.int32, (HEADS * seq, inner), 1) // HD
    same = block_row == block_col
    lane = lax.broadcasted_iota(jnp.int32, (seq, HEADS * seq), 1) % seq
    contexts = []
    for p in range(passes):
        part = projected[p * seq : (p + 1) * seq]
        query, keys, vals = part[:, :inner], part[:, inner : 2 * inner], part[:, 2 * inner :]
        zero = jnp.zeros((), jnp.bfloat16)
        keys = jnp.where(same, jnp.concatenate([keys] * HEADS, axis=0), zero)
        vals = jnp.where(same, jnp.concatenate([vals] * HEADS, axis=0), zero)
        scores = lax.dot_general(
            query, keys, (((1,), (1,)), ((), ())), preferred_element_type=jnp.float32
        ) * HD ** (-0.5)
        weights = jnp.where(lane < lengths[p], jnp.exp(scores), 0.0)
        probs = (weights / head_sums(weights, seq)).astype(jnp.bfloat16)
        contexts.append(jnp.dot(probs, vals, preferred_element_type=jnp.float32))
    context = jnp.concatenate(contexts, axis=0).astype(jnp.bfloat16)
    attended = jnp.dot(context, w_out[...], preferred_element_type=jnp.float32) + out_bias[...]
    hidden = normed(embedded.astype(jnp.float32) + attended, norm_gain[...], norm_bias[...])
    row = lax.broadcasted_iota(jnp.int32, (seq, 1), 0)
    for p in range(passes):
        kept = jnp.where(row < lengths[p], hidden[p * seq : (p + 1) * seq], 0.0)
        pooled = jnp.sum(kept, axis=0, keepdims=True) / lengths[p].astype(jnp.float32)
        scale = lax.rsqrt(jnp.mean(pooled * pooled, axis=-1, keepdims=True) + 1e-06)
        out[p : p + 1, :] = (pooled * scale).astype(jnp.bfloat16)


def encode(
    slots, fetched, lengths, pos_table, emb_gain, emb_bias, w_qkv, w_out, out_bias, norm_gain, norm_bias
):
    width = fetched.shape[1]
    tokens = slots.shape[0]
    passes = lengths.shape[0]
    macs = tokens * width * (fetched.shape[0] + 4 * HEADS * HD)
    return pl.pallas_call(
        encode_kernel,
        out_shape=jax.ShapeDtypeStruct((passes, width), jnp.bfloat16),
        in_specs=[pl.BlockSpec(memory_space=pltpu.SMEM)]
        + [pl.BlockSpec(memory_space=pltpu.VMEM)] * 10,
        out_specs=pl.BlockSpec(memory_space=pltpu.VMEM),
        compiler_params=pltpu.CompilerParams(vmem_limit_bytes=32 * 1024 * 1024),
        cost_estimate=pl.CostEstimate(
            flops=2 * macs, bytes_accessed=6 * 1024 * 1024, transcendentals=0
        ),
        name="encode",
    )(
        lengths,
        slots[:, None],
        fetched,
        pos_table,
        emb_gain[None],
        emb_bias[None],
        w_qkv,
        w_out,
        out_bias[None],
        norm_gain[None],
        norm_bias[None],
    )


def slot_rank(target):
    positions = jnp.arange(target.shape[0], dtype=jnp.int32)
    earlier = (target[:, None] == target[None, :]) & (positions[None, :] < positions[:, None])
    return jnp.sum(earlier.astype(jnp.int32), axis=1)


def place_ints(slot, values, slot_count):
    table = slot[None, :] == jnp.arange(slot_count, dtype=jnp.int32)[:, None]
    return jnp.sum(jnp.where(table, values[None, :] + 1, 0), axis=1) - 1


def pack_rows(slot, rows, slot_count):
    table = slot[None, :] == jnp.arange(slot_count, dtype=jnp.int32)[:, None]
    packed = jnp.dot(table.astype(jnp.bfloat16), rows, preferred_element_type=jnp.float32)
    return packed.astype(jnp.bfloat16)


def gather_doubling(block, axis):
    peers = lax.axis_size(axis)
    reach = 1
    while reach < peers:
        moves = [(i, i ^ reach) for i in range(peers)]
        block = jnp.concatenate([block, lax.ppermute(block, axis, moves)], axis=0)
        reach *= 2
    return block


def update_kernel(places, late, rows, embeds, centroids, out):
    count = out.shape[0]
    first = pl.program_id(0) * count

    def onehot(where_to):
        centre = lax.broadcasted_iota(jnp.int32, (count, where_to.shape[1]), 0) + first
        return jnp.where(centre == where_to[...], 1.0, 0.0)

    early_hot, late_hot = onehot(places), onehot(late)
    sums = jnp.dot(
        early_hot.astype(jnp.bfloat16), rows[...], preferred_element_type=jnp.float32
    ) + jnp.dot(late_hot.astype(jnp.bfloat16), embeds[...], preferred_element_type=jnp.float32)
    counts = jnp.sum(early_hot, axis=1, keepdims=True)
    out[...] = jnp.where(counts > 0, sums / jnp.maximum(counts, 1.0), centroids[...])


def update(places, late, rows, embeds, centroids):
    centre_count, width = centroids.shape
    block = 128
    whole = lambda array: pl.BlockSpec(array.shape, lambda i: (0, 0))
    part = pl.BlockSpec((block, width), lambda i: (i, 0))
    return pl.pallas_call(
        update_kernel,
        grid=(centre_count // block,),
        out_shape=jax.ShapeDtypeStruct(centroids.shape, jnp.float32),
        in_specs=[whole(places), whole(late), whole(rows), whole(embeds), part],
        out_specs=part,
        compiler_params=pltpu.CompilerParams(vmem_limit_bytes=32 * 1024 * 1024),
        cost_estimate=pl.CostEstimate(
            flops=2 * centre_count * width * rows.shape[0],
            bytes_accessed=8 * centre_count * width,
            transcendentals=0,
        ),
        name="update",
    )(places, late, rows, embeds, centroids)


def shards(
    token_ids,
    lengths,
    word_table,
    pos_table,
    emb_gain,
    emb_bias,
    w_qkv,
    w_out,
    out_bias,
    norm_gain,
    norm_bias,
    stored_rows,
    row_owner,
    row_slot,
    centroids,
):
    peer_count = lax.axis_size("dp")
    half = peer_count // 2
    me = lax.axis_index("dp")
    base = me // half * half
    peers = jnp.arange(peer_count, dtype=jnp.int32)
    width = word_table.shape[1]
    vocab_rows = word_table.shape[0]
    passes, seq_len = token_ids.shape
    token_list = token_ids.reshape(passes * seq_len)
    token_count = token_list.shape[0]
    row_count = row_slot.shape[0]
    store_count = stored_rows.shape[0]
    owners = row_owner[:, 0]
    token_cap = max(2, 3 * token_count // peer_count)
    row_cap = max(2, 3 * row_count // peer_count)

    across = [(i, (i + half) % peer_count) for i in range(peer_count)]
    partner_owners = lax.ppermute(owners, "dp", across)
    partner_rows = lax.ppermute(stored_rows, "dp", across)

    target = token_list // vocab_rows
    token_slot = target * token_cap + slot_rank(target)
    requests = place_ints(token_slot, token_list - target * vocab_rows, peer_count * token_cap)
    row_rank = slot_rank(owners)
    places = place_ints(owners * row_cap + row_rank, row_slot, peer_count * row_cap)
    late = jnp.where(owners[None, store_count:] == peers[:, None], row_slot[None, store_count:], -1)
    plan = lax.all_to_all(
        jnp.concatenate(
            [requests.reshape(peer_count, token_cap), places.reshape(peer_count, row_cap), late],
            axis=1,
        ),
        "dp",
        split_axis=0,
        concat_axis=0,
        tiled=True,
    )
    wanted = plan[:, :token_cap].reshape(peer_count * token_cap)
    chosen = wanted[:, None] == jnp.arange(vocab_rows, dtype=jnp.int32)[None, :]
    found = jnp.dot(
        chosen.astype(jnp.bfloat16), word_table, preferred_element_type=jnp.float32
    ).astype(jnp.bfloat16)
    fetched = lax.all_to_all(
        found.reshape(peer_count, token_cap, width), "dp", split_axis=0, concat_axis=0, tiled=True
    ).reshape(peer_count * token_cap, width)

    def half_pack(row_block, row_owners, ranks):
        inside = (row_owners >= base) & (row_owners < base + half)
        slot = jnp.where(inside, (row_owners - base) * row_cap + ranks, -1)[:store_count]
        return pack_rows(slot, row_block, half * row_cap).reshape(half, row_cap, width)

    own_pack = half_pack(stored_rows, owners, row_rank)
    partner_pack = half_pack(partner_rows, partner_owners, slot_rank(partner_owners))
    groups = [list(range(half)), list(range(half, peer_count))]
    got_rows = lax.all_to_all(
        jnp.concatenate([own_pack, partner_pack], axis=1),
        "dp",
        split_axis=0,
        concat_axis=0,
        tiled=True,
        axis_index_groups=groups,
    ).reshape(peer_count * row_cap, width)
    got_places = plan[:, token_cap : token_cap + row_cap].reshape(2, half, row_cap)
    got_places = jnp.where(base == 0, got_places, got_places[::-1])
    got_places = got_places.transpose(1, 0, 2).reshape(1, peer_count * row_cap)

    passage_embed = encode(
        token_slot,
        fetched,
        lengths,
        pos_table,
        emb_gain,
        emb_bias,
        w_qkv,
        w_out,
        out_bias,
        norm_gain,
        norm_bias,
    )
    all_embeds = gather_doubling(passage_embed, "dp")
    late_places = plan[:, token_cap + row_cap :][me ^ peers].reshape(1, -1)
    new_centroids = update(got_places, late_places, got_rows, all_embeds, centroids)
    return (passage_embed, new_centroids)


def solution(mesh):
    return jax.shard_map(
        shards,
        mesh=mesh,
        in_specs=(
            P(("groups", "dp"), None),
            P(("groups", "dp")),
            P("dp", None),
            P(),
            P(),
            P(),
            P(),
            P(),
            P(),
            P(),
            P(),
            P(("groups", "dp"), None),
            P(("groups", "dp"), None),
            P(("groups", "dp")),
            P(("groups", "dp"), None),
        ),
        out_specs=(P(("groups", "dp"), None), P(("groups", "dp"), None)),
        check_vma=False,
    )
```

time: 118 us -> 110 us (0.932)
  waiting for transfers between devices: 23.5 us -> 55 us
  starting transfers between devices: 40.2 us -> 15 us
  local copies, waits for them, and re-layouts: 28.9 us -> 9.35 us
  matrix products: 16.7 us -> 2.06 us
  blocking collectives: 0 us -> 13.6 us
  Pallas kernels: 0 us -> 6.55 us
    ppermute x15 -> x6, waiting for transfers between devices: 15.7 us -> 55 us  [the longest x1 29.2 us: shards(): partner_owners = lax.ppermute(owners, 'dp', across)]
    ppermute x15 -> x6, starting transfers between devices: 26.6 us -> 7.62 us  [the longest x4 4.63 us: gather_doubling(): block = jnp.concatenate([block, lax.ppermute(block, axis, moves)], axis=0)]
    dot_general x8 -> x2, matrix products: 14.4 us -> 0.76 us  [pack_rows(): jnp.dot(table.astype(jnp.bfloat16), rows, preferred_element_type=jnp.floa...]
    unnamed x62 -> x28, local copies, waits for them, and re-layouts: 18.3 us -> 4.76 us
    all_to_all x0 -> x1, blocking collectives: none -> 13.6 us  [shards(): lax.all_to_all(jnp.concatenate([requests.reshape(peer_count, token_cap),...]
    all_to_all x2 -> x1, waiting for transfers between devices: 7.77 us -> 0.01 us  [shards(): lax.all_to_all(jnp.concatenate([own_pack, partner_pack], axis=1), 'dp', s...]
    pallas_call x0 -> x2, Pallas kernels: none -> 6.55 us  [the longest x1 3.64 us: encode(): pl.pallas_call(encode_kernel, out_shape=jax.ShapeDtypeStruct((passes, wid...]
    all_to_all x2 -> x1, starting transfers between devices: 9.28 us -> 3.73 us  [shards(): lax.all_to_all(jnp.concatenate([own_pack, partner_pack], axis=1), 'dp', s...]
  transfers between devices with their start and end apart: 18 -> 8, of which waited for: 4 -> 6; matrix products, arithmetic and copies ran while one was open for 34% -> 6% of each run, Pallas kernels for 0% -> 3%
where the time goes in v3:
time: 110 us; the launch traced here: 109 us
  waiting for transfers between devices  55 us (50%)
  starting transfers between devices  15 us (14%)
  blocking collectives  13.6 us (12%)
  local copies, waits for them, and re-layouts  9.35 us (8%)
  Pallas kernels  6.55 us (6%)
  other arithmetic  6.54 us (6%)
  matrix products  2.06 us (2%)
    ppermute x1, waiting for transfers between devices, shards(): partner_owners = lax.ppermute(owners, 'dp', across)  29.2 us
    ppermute x4, waiting for transfers between devices, gather_doubling(): block = jnp.concatenate([block, lax.ppermute(block, axis, moves)], axis=0)  15.3 us
    all_to_all x1, blocking collectives, shards(): lax.all_to_all(jnp.concatenate([requests.reshape(peer_count, token_cap),...  13.6 us
    ppermute x1, waiting for transfers between devices, shards(): partner_rows = lax.ppermute(stored_rows, 'dp', across)  10.6 us
    unnamed x28, local copies, waits for them, and re-layouts  4.76 us
    ppermute x4, starting transfers between devices, gather_doubling(): block = jnp.concatenate([block, lax.ppermute(block, axis, moves)], axis=0)  4.63 us
    all_to_all x1, starting transfers between devices, shards(): lax.all_to_all(jnp.concatenate([own_pack, partner_pack], axis=1), 'dp', s...  3.73 us
    pallas_call x1, Pallas kernels, encode(): pl.pallas_call(encode_kernel, out_shape=jax.ShapeDtypeStruct((passes, wid...  3.64 us
  transfers between devices with their start and end apart: 8, of which 6 were waited for; matrix products, arithmetic and copies ran while one was open for 6% of the time, Pallas kernels for 3%

profile of v3, /device:TPU:0, one launch (start us, length us, event | category | flops | bytes accessed | tf_op | source)
XLA Modules:
  0.0 109.0 jit_solution(16536811711672659320)
XLA Ops:
  0.6 0.0 copy-start
  0.6 0.0 copy-start.12
  0.7 0.0 copy-start.11
  0.7 0.8 slice.23
  1.5 0.7 broadcast_add_fusion.2
  2.2 0.7 slice_bitcast_fusion.1
  2.9 0.8 reshape.190
  3.7 0.2 convert_reduce_fusion.2
  3.9 0.1 select_reduce_fusion.1
  4.0 0.9 convert_reduce_fusion.1
  5.0 0.7 and_select_fusion.1
  5.7 0.2 select_reduce_fusion
  5.9 0.1 sub.45
  5.9 0.1 sub.43
  6.0 0.1 pad_add_fusion
  6.1 13.6 %all_to_all.22 = s32[16,1,74]{2,1,0:T(1,128)S(1)} all-to-all(s32[16,1,74]{2,1,0:T(1,128)S(1)} %bitcast.40), channel_id=1, replica_groups=mesh['groups'=2,'dp'=16] {'dp'}, dimensions={0} | all-to-all | bytes 9472 | tf_op jit(solution)/shard_map/all_to_all | solution.py:214
  19.7 0.1 eq.140
  19.8 0.0 copy-done
  19.8 1.3 %convolution_convert_fusion.2 = bf16[384,1024]{1,0:T(8,128)(2,1)} fusion(bf16[240,1024]{1,0:T(8,128)(2,1)S(1)} %copy-done, s32[384]{0:T(512)S(1)} %eq.140), kind=kOutput, calls=%fused_computation.4 | convolution fusion | flops 189229056 | bytes 1279488 | tf_op jit(solution)/shard_map/dot_general | solution.py:226
  21.1 3.6 %all-to-all-start.1 = ((bf16[16,24,1024]{2,1,0:T(8,128)(2,1)}), bf16[16,24,1024]{2,1,0:T(8,128)(2,1)S(1)}, u32[]{:S(2)}, u32[]{:S(2)}) async-start(bf16[16,24,1024]{2,1,0:T(8,128)(2,1)} %bitcast.5), calls=%async_computation.1 | async-start | bytes 1572864 | tf_op jit(solution)/shard_map/all_to_all | solution.py:229
  24.7 0.0 copy-done.12
  24.7 2.8 %collective-permute-start = (s32[256]{0:T(256)S(1)}, s32[256]{0:T(256)S(1)}, u32[]{:S(2)}, u32[]{:S(2)}) collective-permute-start(s32[256]{0:T(256)S(1)} %bitcast.43), channel_id=1, source_target_pairs={{0,8},{1,9},{2,10},{3,11},{4,12},{5,13},{6,14},{7,15},{8,0},{9,1},... | collective-permute-start | bytes 3080 | tf_op jit(solution)/shard_map/ppermute | solution.py:205
  27.5 0.2 collective-permute-start.1
  27.7 0.4 convolution_convert_fusion.1
  28.1 29.2 %collective-permute-done = s32[256]{0:T(256)S(1)} collective-permute-done((s32[256]{0:T(256)S(1)}, s32[256]{0:T(256)S(1)}, u32[]{:S(2)}, u32[]{:S(2)}) %collective-permute-start) | collective-permute-done | bytes 1056 | tf_op jit(solution)/shard_map/ppermute | solution.py:205
  57.3 0.2 convert_reduce_fusion
  57.5 10.6 %collective-permute-done.1 = bf16[254,1024]{1,0:T(8,128)(2,1)S(1)} collective-permute-done((bf16[254,1024]{1,0:T(8,128)(2,1)S(1)}, bf16[254,1024]{1,0:T(8,128)(2,1)S(1)}, u32[]{:S(2)}, u32[]{:S(2)}) %collective-permute-start.1) | collective-permute-done | bytes 520224 | tf_op jit(solution)/shard_map/ppermute | solution.py:206
  68.1 0.4 convolution_convert_fusion
  68.5 1.3 %pad_maximum_fusion = bf16[8,96,1024]{2,1,0:T(8,128)(2,1)} fusion(bf16[8,48,1024]{2,1,0:T(8,128)(2,1)S(1)} %bitcast.36, bf16[8,48,1024]{2,1,0:T(8,128)(2,1)S(1)} %bitcast.35), kind=kLoop, calls=%fused_computation.1 | loop fusion | flops 3145728 | bytes 3145728 | tf_op jit(solution)/shard_map/concatenate | solution.py:242
  69.7 0.0 copy-start.7
  69.8 0.0 copy-start.8
  69.8 0.0 copy-start.9
  69.8 0.0 copy-start.10
  69.8 0.0 all-to-all-done.1
  69.8 3.7 %all-to-all-start.2 = ((bf16[8,96,1024]{2,1,0:T(8,128)(2,1)}), bf16[8,96,1024]{2,1,0:T(8,128)(2,1)S(1)}, u32[]{:S(2)}, u32[]{:S(2)}) async-start(bf16[8,96,1024]{2,1,0:T(8,128)(2,1)} %pad_maximum_fusion), calls=%async_computation.2 | async-start | bytes 3145728 | tf_op jit(solution)/shard_map/all_to_all | solution.py:241
  73.5 0.0 copy-done.13
  73.6 0.2 and.59
  73.7 0.1 div.45
  73.9 0.1 copy.45
  74.1 0.0 copy-start.1
  74.1 1.9 %copy-done.1 = bf16[1024,1536]{1,0:T(8,128)(2,1)S(1)} copy-done((bf16[1024,1536]{1,0:T(8,128)(2,1)S(1)}, bf16[1024,1536]{1,0:T(8,128)(2,1)}, u32[]{:S(2)}) %copy-start.1) | copy-done | bytes 3145752
  76.0 1.2 %copy-done.3 = bf16[512,1024]{1,0:T(8,128)(2,1)S(1)} copy-done((bf16[512,1024]{1,0:T(8,128)(2,1)S(1)}, bf16[512,1024]{1,0:T(8,128)(2,1)}, u32[]{:S(2)}) %copy-start.3) | copy-done | bytes 1048600
  77.2 3.6 %encode.1 = bf16[2,1024]{1,0:T(2,128)(2,1)} custom-call(s32[2]{0:T(128)S(1)} %copy-done.10, s32[128,1]{1,0:T(8,128)S(1)} %fusion.6.slots, bf16[384,1024]{1,0:T(8,128)(2,1)S(1)} %bitcast.29, bf16[64,1024]{1,0:T(8,128)(2,1)S(1)} %copy-done.4, f32[1,1024]{1,0:T(1,128)S(1)} %bitcast.30, f32[1,1024]{1,0:T(1,128)S(1)} %bitcast.31, ...), custom_call_target="tpu_custom_call" | custom-call | flops 637534208 | bytes 6291456 | tf_op jit(solution)/shard_map/encode/pallas_call | solution.py:81
  80.8 0.4 collective-permute-start.2
  81.2 1.0 collective-permute-done.2
  82.3 0.7 pad_maximum_fusion.3
  83.0 1.9 %collective-permute-start.3 = (bf16[4,1024]{1,0:T(4,128)(2,1)S(1)}, bf16[4,1024]{1,0:T(4,128)(2,1)S(1)}, u32[]{:S(2)}, u32[]{:S(2)}) collective-permute-start(bf16[4,1024]{1,0:T(4,128)(2,1)S(1)} %pad_maximum_fusion.3), channel_id=1, source_target_pairs={{0,2},{1,3},{2,0},{3,1},{4,6},{5,7},{6,4},{7,5},{8,10},{9,11},{10,... | collective-permute-start | bytes 24584 | tf_op jit(solution)/shard_map/ppermute | solution.py:129
  84.9 8.8 %collective-permute-done.3 = bf16[4,1024]{1,0:T(4,128)(2,1)S(1)} collective-permute-done((bf16[4,1024]{1,0:T(4,128)(2,1)S(1)}, bf16[4,1024]{1,0:T(4,128)(2,1)S(1)}, u32[]{:S(2)}, u32[]{:S(2)}) %collective-permute-start.3) | collective-permute-done | bytes 8224 | tf_op jit(solution)/shard_map/ppermute | solution.py:129
  93.7 0.7 pad_maximum_fusion.2
  94.4 1.6 %collective-permute-start.4 = (bf16[8,1024]{1,0:T(8,128)(2,1)S(1)}, bf16[8,1024]{1,0:T(8,128)(2,1)S(1)}, u32[]{:S(2)}, u32[]{:S(2)}) collective-permute-start(bf16[8,1024]{1,0:T(8,128)(2,1)S(1)} %pad_maximum_fusion.2), channel_id=1, source_target_pairs={{0,4},{1,5},{2,6},{3,7},{4,0},{5,1},{6,2},{7,3},{8,12},{9,13},{10,... | collective-permute-start | bytes 49160 | tf_op jit(solution)/shard_map/ppermute | solution.py:129
  96.0 0.1 slice_bitcast_fusion
  96.1 2.1 %collective-permute-done.4 = bf16[8,1024]{1,0:T(8,128)(2,1)S(1)} collective-permute-done((bf16[8,1024]{1,0:T(8,128)(2,1)S(1)}, bf16[8,1024]{1,0:T(8,128)(2,1)S(1)}, u32[]{:S(2)}, u32[]{:S(2)}) %collective-permute-start.4) | collective-permute-done | bytes 16416 | tf_op jit(solution)/shard_map/ppermute | solution.py:129
  98.2 0.7 pad_maximum_fusion.1
  98.9 0.8 collective-permute-start.5
  99.7 0.1 slice.33
  99.8 0.6 gather_fusion
  100.3 0.1 reshape.195.late
  100.4 0.1 reshape.194.places
  100.5 3.3 %collective-permute-done.5 = bf16[16,1024]{1,0:T(8,128)(2,1)S(1)} collective-permute-done((bf16[16,1024]{1,0:T(8,128)(2,1)S(1)}, bf16[16,1024]{1,0:T(8,128)(2,1)S(1)}, u32[]{:S(2)}, u32[]{:S(2)}) %collective-permute-start.5) | collective-permute-done | bytes 32800 | tf_op jit(solution)/shard_map/ppermute | solution.py:129
  103.8 0.7 concatenate.26.embeds
  104.5 0.0 all-to-all-done.2
  104.5 0.0 copy-start.2
  104.5 1.6 %copy-done.2 = f32[512,1024]{1,0:T(8,128)S(1)} copy-done((f32[512,1024]{1,0:T(8,128)S(1)}, f32[512,1024]{1,0:T(8,128)}, u32[]{:S(2)}) %copy-start.2) | copy-done | bytes 2097176
  106.1 2.9 %update.1 = f32[512,1024]{1,0:T(8,128)} custom-call(s32[1,768]{1,0:T(1,128)S(1)} %reshape.194.places, s32[1,32]{1,0:T(1,128)S(1)} %reshape.195.late, bf16[768,1024]{1,0:T(8,128)(2,1)S(1)} %bitcast.28, bf16[32,1024]{1,0:T(8,128)(2,1)S(1)} %concatenate.26.embeds, f32[512,1024]{1,0:T(8,128)S(1)} %copy-done.2), custom_call_target="tpu_custom_call" | custom-call | flops 805306368 | bytes 4194304 | tf_op jit(solution)/shard_map/update/pallas_call | solution.py:155
  (27 shorter events, 0.2 us)
Async XLA Ops:
  0.6 19.2 %copy-start = (bf16[240,1024]{1,0:T(8,128)(2,1)S(1)}, bf16[240,1024]{1,0:T(8,128)(2,1)}, u32[]{:S(2)}) copy-start(bf16[240,1024]{1,0:T(8,128)(2,1)} %param.17) | copy-start | bytes 1474564
  0.6 24.1 %copy-start.12 = (s32[256,1]{0,1:T(1,128)S(1)}, s32[256,1]{0,1:T(1,128)}, u32[]{:S(2)}) copy-start(s32[256,1]{0,1:T(1,128)} %param.27) | copy-start | bytes 3076
  0.7 26.9 %copy-start.11 = (bf16[254,1024]{1,0:T(8,128)(2,1)S(1)}, bf16[254,1024]{1,0:T(8,128)(2,1)}, u32[]{:S(2)}) copy-start(bf16[254,1024]{1,0:T(8,128)(2,1)} %param.26) | copy-start | bytes 1560580
  21.1 48.7 %all-to-all-start.1 = ((bf16[16,24,1024]{2,1,0:T(8,128)(2,1)}), bf16[16,24,1024]{2,1,0:T(8,128)(2,1)S(1)}, u32[]{:S(2)}, u32[]{:S(2)}) async-start(bf16[16,24,1024]{2,1,0:T(8,128)(2,1)} %bitcast.5), calls=%async_computation.1 | async-start | bytes 1572864 | tf_op jit(solution)/shard_map/all_to_all | solution.py:229
  24.7 32.6 %collective-permute-start = (s32[256]{0:T(256)S(1)}, s32[256]{0:T(256)S(1)}, u32[]{:S(2)}, u32[]{:S(2)}) collective-permute-start(s32[256]{0:T(256)S(1)} %bitcast.43), channel_id=1, source_target_pairs={{0,8},{1,9},{2,10},{3,11},{4,12},{5,13},{6,14},{7,15},{8,0},{9,1},... | collective-permute-start | bytes 3080 | tf_op jit(solution)/shard_map/ppermute | solution.py:205
  27.5 40.5 %collective-permute-start.1 = (bf16[254,1024]{1,0:T(8,128)(2,1)S(1)}, bf16[254,1024]{1,0:T(8,128)(2,1)S(1)}, u32[]{:S(2)}, u32[]{:S(2)}) collective-permute-start(bf16[254,1024]{1,0:T(8,128)(2,1)S(1)} %copy-done.11), channel_id=1, source_target_pairs={{0,8},{1,9},{2,10},{3,11},{4,12},{5,13},{6,14},{7,15},{8,0},{9,1},... | collective-permute-start | bytes 1560584 | tf_op jit(solution)/shard_map/ppermute | solution.py:206
  69.7 3.8 %copy-start.13 = (s32[2,64]{1,0:T(2,128)S(1)}, s32[2,64]{1,0:T(2,128)}, u32[]{:S(2)}) copy-start(s32[2,64]{1,0:T(2,128)} %param.15) | copy-start | bytes 1540
  69.7 4.3 %copy-start.4 = (bf16[64,1024]{1,0:T(8,128)(2,1)S(1)}, bf16[64,1024]{1,0:T(8,128)(2,1)}, u32[]{:S(2)}) copy-start(bf16[64,1024]{1,0:T(8,128)(2,1)} %pos.1) | copy-start | bytes 393220
  69.7 4.3 %copy-start.5 = (f32[1024]{0:T(1024)S(1)}, f32[1024]{0:T(1024)}, u32[]{:S(2)}) copy-start(f32[1024]{0:T(1024)} %param.19) | copy-start | bytes 12292
  69.7 4.3 %copy-start.6 = (f32[1024]{0:T(1024)S(1)}, f32[1024]{0:T(1024)}, u32[]{:S(2)}) copy-start(f32[1024]{0:T(1024)} %param.20) | copy-start | bytes 12292
  69.7 4.3 %copy-start.7 = (f32[1024]{0:T(1024)S(1)}, f32[1024]{0:T(1024)}, u32[]{:S(2)}) copy-start(f32[1024]{0:T(1024)} %param.23) | copy-start | bytes 12292
  69.8 4.3 %copy-start.8 = (f32[1024]{0:T(1024)S(1)}, f32[1024]{0:T(1024)}, u32[]{:S(2)}) copy-start(f32[1024]{0:T(1024)} %param.24) | copy-start | bytes 12292
  69.8 4.3 %copy-start.9 = (f32[1024]{0:T(1024)S(1)}, f32[1024]{0:T(1024)}, u32[]{:S(2)}) copy-start(f32[1024]{0:T(1024)} %param.25) | copy-start | bytes 12292
  69.8 4.3 %copy-start.10 = (s32[2]{0:T(128)S(1)}, s32[2]{0:T(128)}, u32[]{:S(2)}) copy-start(s32[2]{0:T(128)} %lengths.1) | copy-start | bytes 28
  69.8 34.7 %all-to-all-start.2 = ((bf16[8,96,1024]{2,1,0:T(8,128)(2,1)}), bf16[8,96,1024]{2,1,0:T(8,128)(2,1)S(1)}, u32[]{:S(2)}, u32[]{:S(2)}) async-start(bf16[8,96,1024]{2,1,0:T(8,128)(2,1)} %pad_maximum_fusion), calls=%async_computation.2 | async-start | bytes 3145728 | tf_op jit(solution)/shard_map/all_to_all | solution.py:241
  74.1 1.9 %copy-start.1 = (bf16[1024,1536]{1,0:T(8,128)(2,1)S(1)}, bf16[1024,1536]{1,0:T(8,128)(2,1)}, u32[]{:S(2)}) copy-start(bf16[1024,1536]{1,0:T(8,128)(2,1)} %w_qkv.1) | copy-start | bytes 9437188
  76.0 1.2 %copy-start.3 = (bf16[512,1024]{1,0:T(8,128)(2,1)S(1)}, bf16[512,1024]{1,0:T(8,128)(2,1)}, u32[]{:S(2)}) copy-start(bf16[512,1024]{1,0:T(8,128)(2,1)} %w_out.1) | copy-start | bytes 3145732
  80.8 1.4 %collective-permute-start.2 = (bf16[2,1024]{1,0:T(2,128)(2,1)}, bf16[2,1024]{1,0:T(2,128)(2,1)S(1)}, u32[]{:S(2)}, u32[]{:S(2)}) collective-permute-start(bf16[2,1024]{1,0:T(2,128)(2,1)} %encode.1), channel_id=1, source_target_pairs={{0,1},{1,0},{2,3},{3,2},{4,5},{5,4},{6,7},{7,6},{8,9},{9,8},{10,11... | collective-permute-start | bytes 12296 | tf_op jit(solution)/shard_map/ppermute | solution.py:129
  83.0 10.7 %collective-permute-start.3 = (bf16[4,1024]{1,0:T(4,128)(2,1)S(1)}, bf16[4,1024]{1,0:T(4,128)(2,1)S(1)}, u32[]{:S(2)}, u32[]{:S(2)}) collective-permute-start(bf16[4,1024]{1,0:T(4,128)(2,1)S(1)} %pad_maximum_fusion.3), channel_id=1, source_target_pairs={{0,2},{1,3},{2,0},{3,1},{4,6},{5,7},{6,4},{7,5},{8,10},{9,11},{10,... | collective-permute-start | bytes 24584 | tf_op jit(solution)/shard_map/ppermute | solution.py:129
  94.4 3.8 %collective-permute-start.4 = (bf16[8,1024]{1,0:T(8,128)(2,1)S(1)}, bf16[8,1024]{1,0:T(8,128)(2,1)S(1)}, u32[]{:S(2)}, u32[]{:S(2)}) collective-permute-start(bf16[8,1024]{1,0:T(8,128)(2,1)S(1)} %pad_maximum_fusion.2), channel_id=1, source_target_pairs={{0,4},{1,5},{2,6},{3,7},{4,0},{5,1},{6,2},{7,3},{8,12},{9,13},{10,... | collective-permute-start | bytes 49160 | tf_op jit(solution)/shard_map/ppermute | solution.py:129
  98.9 4.9 %collective-permute-start.5 = (bf16[16,1024]{1,0:T(8,128)(2,1)S(1)}, bf16[16,1024]{1,0:T(8,128)(2,1)S(1)}, u32[]{:S(2)}, u32[]{:S(2)}) collective-permute-start(bf16[16,1024]{1,0:T(8,128)(2,1)S(1)} %pad_maximum_fusion.1), channel_id=1, source_target_pairs={{0,8},{1,9},{2,10},{3,11},{4,12},{5,13},{6,14},{7,15},{8,0},{9,1},... | collective-permute-start | bytes 98312 | tf_op jit(solution)/shard_map/ppermute | solution.py:129
  104.5 1.6 %copy-start.2 = (f32[512,1024]{1,0:T(8,128)S(1)}, f32[512,1024]{1,0:T(8,128)}, u32[]{:S(2)}) copy-start(f32[512,1024]{1,0:T(8,128)} %centroids.1) | copy-start | bytes 6291460

commit v4 on v3

--- a/solution.py
+++ b/solution.py
@@ -1,3 +1,5 @@
+import functools
+
 import jax
 import jax.numpy as jnp
 from jax import lax
@@ -115,28 +117,50 @@
     return jnp.sum(jnp.where(table, values[None, :] + 1, 0), axis=1) - 1
 
 
-def pack_rows(slot, rows, slot_count):
-    table = slot[None, :] == jnp.arange(slot_count, dtype=jnp.int32)[:, None]
-    packed = jnp.dot(table.astype(jnp.bfloat16), rows, preferred_element_type=jnp.float32)
-    return packed.astype(jnp.bfloat16)
-
-
-def gather_doubling(block, axis):
-    peers = lax.axis_size(axis)
-    reach = 1
-    while reach < peers:
-        moves = [(i, i ^ reach) for i in range(peers)]
-        block = jnp.concatenate([block, lax.ppermute(block, axis, moves)], axis=0)
-        reach *= 2
-    return block
-
-
-def update_kernel(places, late, rows, embeds, centroids, out):
+def pack_kernel(row_cap, own_slot, partner_slot, own_rows, partner_rows, *outs):
+    slot_count = len(outs) * row_cap
+    for source, (slot, rows) in enumerate(((own_slot, own_rows), (partner_slot, partner_rows))):
+        spot = lax.broadcasted_iota(jnp.int32, (slot_count, rows.shape[0]), 0)
+        table = jnp.where(slot[:, : rows.shape[0]] == spot, 1.0, 0.0).astype(jnp.bfloat16)
+        packed = jnp.dot(table, rows[...], preferred_element_type=jnp.float32)
+        packed = packed.astype(jnp.bfloat16)
+        for step, out in enumerate(outs):
+            out[source * row_cap : (source + 1) * row_cap, :] = packed[
+                step * row_cap : (step + 1) * row_cap
+            ]
+
+
+def pack_rows(own_slot, partner_slot, own_rows, partner_rows, steps, row_cap):
+    width = own_rows.shape[1]
+    return pl.pallas_call(
+        functools.partial(pack_kernel, row_cap),
+        out_shape=[jax.ShapeDtypeStruct((2 * row_cap, width), jnp.bfloat16)] * steps,
+        in_specs=[pl.BlockSpec(memory_space=pltpu.VMEM)] * 4,
+        out_specs=[pl.BlockSpec(memory_space=pltpu.VMEM)] * steps,
+        compiler_params=pltpu.CompilerParams(vmem_limit_bytes=32 * 1024 * 1024),
+        cost_estimate=pl.CostEstimate(
+            flops=4 * steps * row_cap * width * own_rows.shape[0],
+            bytes_accessed=4 * width * (own_rows.shape[0] + steps * row_cap),
+            transcendentals=0,
+        ),
+        name="pack",
+    )(own_slot[None], partner_slot[None], own_rows, partner_rows)
+
+
+def update_kernel(places, late, embeds, centroids, *rest):
+    pieces, out, rows = rest[:-2], rest[-2], rest[-1]
     count = out.shape[0]
-    first = pl.program_id(0) * count
+    step = pl.program_id(0)
+
+    @pl.when(step == 0)
+    def _():
+        at = 0
+        for piece in pieces:
+            rows[at : at + piece.shape[0], :] = piece[...]
+            at += piece.shape[0]
 
     def onehot(where_to):
-        centre = lax.broadcasted_iota(jnp.int32, (count, where_to.shape[1]), 0) + first
+        centre = lax.broadcasted_iota(jnp.int32, (count, where_to.shape[1]), 0) + step * count
         return jnp.where(centre == where_to[...], 1.0, 0.0)
 
     early_hot, late_hot = onehot(places), onehot(late)
@@ -147,25 +171,28 @@
     out[...] = jnp.where(counts > 0, sums / jnp.maximum(counts, 1.0), centroids[...])
 
 
-def update(places, late, rows, embeds, centroids):
+def update(places, late, embeds, centroids, pieces):
     centre_count, width = centroids.shape
     block = 128
     whole = lambda array: pl.BlockSpec(array.shape, lambda i: (0, 0))
     part = pl.BlockSpec((block, width), lambda i: (i, 0))
+    row_total = sum(piece.shape[0] for piece in pieces)
     return pl.pallas_call(
         update_kernel,
         grid=(centre_count // block,),
         out_shape=jax.ShapeDtypeStruct(centroids.shape, jnp.float32),
-        in_specs=[whole(places), whole(late), whole(rows), whole(embeds), part],
+        in_specs=[whole(places), whole(late), whole(embeds), part]
+        + [whole(piece) for piece in pieces],
         out_specs=part,
+        scratch_shapes=[pltpu.VMEM((row_total, width), jnp.bfloat16)],
         compiler_params=pltpu.CompilerParams(vmem_limit_bytes=32 * 1024 * 1024),
         cost_estimate=pl.CostEstimate(
-            flops=2 * centre_count * width * rows.shape[0],
+            flops=2 * centre_count * width * row_total,
             bytes_accessed=8 * centre_count * width,
             transcendentals=0,
         ),
         name="update",
-    )(places, late, rows, embeds, centroids)
+    )(places, late, embeds, centroids, *pieces)
 
 
 def shards(
@@ -202,13 +229,20 @@
     row_cap = max(2, 3 * row_count // peer_count)
 
     across = [(i, (i + half) % peer_count) for i in range(peer_count)]
-    partner_owners = lax.ppermute(owners, "dp", across)
     partner_rows = lax.ppermute(stored_rows, "dp", across)
+    row_rank = slot_rank(owners)
+
+    def half_slot(holder):
+        first = holder // half * half
+        inside = (owners >= first) & (owners < first + half)
+        return jnp.where(inside, (owners - holder + half) % half * row_cap + row_rank, -1)
+
+    own_slot = half_slot(me)
+    partner_slot = lax.ppermute(half_slot((me + half) % peer_count), "dp", across)
 
     target = token_list // vocab_rows
     token_slot = target * token_cap + slot_rank(target)
     requests = place_ints(token_slot, token_list - target * vocab_rows, peer_count * token_cap)
-    row_rank = slot_rank(owners)
     places = place_ints(owners * row_cap + row_rank, row_slot, peer_count * row_cap)
     late = jnp.where(owners[None, store_count:] == peers[:, None], row_slot[None, store_count:], -1)
     plan = lax.all_to_all(
@@ -221,6 +255,7 @@
         concat_axis=0,
         tiled=True,
     )
+    plan, partner_rows = lax.optimization_barrier((plan, partner_rows))
     wanted = plan[:, :token_cap].reshape(peer_count * token_cap)
     chosen = wanted[:, None] == jnp.arange(vocab_rows, dtype=jnp.int32)[None, :]
     found = jnp.dot(
@@ -230,25 +265,15 @@
         found.reshape(peer_count, token_cap, width), "dp", split_axis=0, concat_axis=0, tiled=True
     ).reshape(peer_count * token_cap, width)
 
-    def half_pack(row_block, row_owners, ranks):
-        inside = (row_owners >= base) & (row_owners < base + half)
-        slot = jnp.where(inside, (row_owners - base) * row_cap + ranks, -1)[:store_count]
-        return pack_rows(slot, row_block, half * row_cap).reshape(half, row_cap, width)
-
-    own_pack = half_pack(stored_rows, owners, row_rank)
-    partner_pack = half_pack(partner_rows, partner_owners, slot_rank(partner_owners))
-    groups = [list(range(half)), list(range(half, peer_count))]
-    got_rows = lax.all_to_all(
-        jnp.concatenate([own_pack, partner_pack], axis=1),
-        "dp",
-        split_axis=0,
-        concat_axis=0,
-        tiled=True,
-        axis_index_groups=groups,
-    ).reshape(peer_count * row_cap, width)
-    got_places = plan[:, token_cap : token_cap + row_cap].reshape(2, half, row_cap)
-    got_places = jnp.where(base == 0, got_places, got_places[::-1])
-    got_places = got_places.transpose(1, 0, 2).reshape(1, peer_count * row_cap)
+    blocks = pack_rows(own_slot, partner_slot, stored_rows, partner_rows, half, row_cap)
+    got_rows = [blocks[0]]
+    for step in range(1, half):
+        moves = [(i, i // half * half + (i + step) % half) for i in range(peer_count)]
+        got_rows.append(lax.ppermute(blocks[step], "dp", moves))
+    sources = base + (me - jnp.arange(half, dtype=jnp.int32)) % half
+    sources = jnp.stack([sources, (sources + half) % peer_count], axis=1).reshape(peer_count)
+    got_places = plan[:, token_cap : token_cap + row_cap][sources].reshape(1, peer_count * row_cap)
+    late_places = plan[:, token_cap + row_cap :].reshape(1, -1)
 
     passage_embed = encode(
         token_slot,
@@ -263,9 +288,14 @@
         norm_gain,
         norm_bias,
     )
-    all_embeds = gather_doubling(passage_embed, "dp")
-    late_places = plan[:, token_cap + row_cap :][me ^ peers].reshape(1, -1)
-    new_centroids = update(got_places, late_places, got_rows, all_embeds, centroids)
+    all_embeds = lax.all_to_all(
+        jnp.broadcast_to(passage_embed[None], (peer_count, passes, width)),
+        "dp",
+        split_axis=0,
+        concat_axis=0,
+        tiled=True,
+    ).reshape(peer_count * passes, width)
+    new_centroids = update(got_places, late_places, all_embeds, centroids, got_rows)
     return (passage_embed, new_centroids)
 
 

time: 110 us -> 91.7 us (0.83)
  waiting for transfers between devices: 55 us -> 23.4 us
  starting transfers between devices: 15 us -> 23.3 us
  blocking collectives: 13.6 us -> 19.8 us
  other arithmetic: 6.54 us -> 2.36 us
  Pallas kernels: 6.55 us -> 9.45 us
    ppermute x5 -> x8, waiting for transfers between devices: 44.5 us -> 20.4 us  [the longest x1 17.4 us: shards(): lax.ppermute(half_slot((me + half) % peer_count), 'dp', across)]
    ppermute x1, waiting for transfers between devices: 10.6 us -> 0.01 us  [shards(): partner_rows = lax.ppermute(stored_rows, 'dp', across)]
    all_to_all x1, blocking collectives: 13.6 us -> 19.8 us  [shards(): lax.all_to_all(jnp.concatenate([requests.reshape(peer_count, token_cap),...]
    ppermute x1, starting transfers between devices: 0.18 us -> 4.1 us  [shards(): partner_rows = lax.ppermute(stored_rows, 'dp', across)]
    concatenate x4 -> x0, other arithmetic: 3.38 us -> none  [the longest x3 2.12 us: gather_doubling(): block = jnp.concatenate([block, lax.ppermute(block, axis, moves)], axis=0)]
    all_to_all x1, waiting for transfers between devices: 0.01 us -> 3.07 us  [shards(): lax.all_to_all(jnp.broadcast_to(passage_embed[None], (peer_count, passes,...]
    ppermute x5 -> x8, starting transfers between devices: 7.44 us -> 10.2 us  [the longest x7 7.41 us: shards(): got_rows.append(lax.ppermute(blocks[step], 'dp', moves))]
    pallas_call x0 -> x1, Pallas kernels: none -> 1.47 us  [pack_rows(): pl.pallas_call(functools.partial(pack_kernel, row_cap), out_shape=[jax.Sh...]
  transfers between devices with their start and end apart: 8 -> 11, of which waited for: 6 -> 4; matrix products, arithmetic and copies ran while one was open for 6% -> 8% of each run, Pallas kernels for 3% -> 6%
where the time goes in v4:
time: 91.7 us; the launch traced here: 90.9 us
  waiting for transfers between devices  23.4 us (26%)
  starting transfers between devices  23.3 us (25%)
  blocking collectives  19.8 us (22%)
  local copies, waits for them, and re-layouts  10.3 us (11%)
  Pallas kernels  9.45 us (10%)
  other arithmetic  2.36 us (3%)
  matrix products  1.29 us (1%)
  between operations  0.97 us (1%)
    all_to_all x1, blocking collectives, shards(): lax.all_to_all(jnp.concatenate([requests.reshape(peer_count, token_cap),...  19.8 us
    ppermute x1, waiting for transfers between devices, shards(): lax.ppermute(half_slot((me + half) % peer_count), 'dp', across)  17.4 us
    ppermute x7, starting transfers between devices, shards(): got_rows.append(lax.ppermute(blocks[step], 'dp', moves))  7.41 us
    unnamed x36, local copies, waits for them, and re-layouts  5.02 us
    all_to_all x1, starting transfers between devices, shards(): lax.all_to_all(found.reshape(peer_count, token_cap, width), 'dp', split_a...  4.96 us
    pallas_call x1, Pallas kernels, update(): pl.pallas_call(update_kernel, grid=(centre_count // block,), out_shape=ja...  4.3 us
    ppermute x1, starting transfers between devices, shards(): partner_rows = lax.ppermute(stored_rows, 'dp', across)  4.1 us
    all_to_all x1, starting transfers between devices, shards(): lax.all_to_all(jnp.broadcast_to(passage_embed[None], (peer_count, passes,...  4 us
  transfers between devices with their start and end apart: 11, of which 4 were waited for; matrix products, arithmetic and copies ran while one was open for 8% of the time, Pallas kernels for 6%

profile of v4, /device:TPU:0, one launch (start us, length us, event | category | flops | bytes accessed | tf_op | source)
XLA Modules:
  0.0 90.9 jit_solution(14006507676770513860)
XLA Ops:
  0.6 0.0 copy-start
  0.7 0.0 copy-start.17
  0.7 0.0 copy-start.16
  0.7 4.1 %collective-permute-start = (bf16[254,1024]{1,0:T(8,128)(2,1)}, bf16[254,1024]{1,0:T(8,128)(2,1)S(1)}, u32[]{:S(2)}, u32[]{:S(2)}) collective-permute-start(bf16[254,1024]{1,0:T(8,128)(2,1)} %own_rows.1), channel_id=1, source_target_pairs={{0,8},{1,9},{2,10},{3,11},{4,12},{5,13},{6,14},{7,15},{8,0},{9,1},... | collective-permute-start | bytes 1560584 | tf_op jit(solution)/shard_map/ppermute | solution.py:232
  4.8 0.7 slice.17
  5.5 0.8 reshape.362
  6.3 0.2 convert_reduce_fusion.1
  6.5 0.9 %convert_reduce_fusion = s32[256]{0:T(256)S(1)} fusion(s32[256]{0:T(256)} %bitcast.34), kind=kLoop, calls=%fused_computation.5 | loop fusion | flops 327424 | bytes 2048 | tf_op jit(solution)/shard_map/reduce_sum | solution.py:112
  7.4 0.1 select_reduce_fusion.1
  7.6 0.7 and_select_fusion.2
  8.3 0.2 select_reduce_fusion
  8.5 0.1 sub.78
  8.6 0.1 sub.76
  8.7 0.7 slice_bitcast_fusion
  9.4 0.1 pad_add_fusion
  9.5 19.8 %all_to_all.22 = s32[16,1,74]{2,1,0:T(1,128)S(1)} all-to-all(s32[16,1,74]{2,1,0:T(1,128)S(1)} %bitcast.33), channel_id=1, replica_groups=mesh['groups'=2,'dp'=16] {'dp'}, dimensions={0} | all-to-all | bytes 9472 | tf_op jit(solution)/shard_map/all_to_all | solution.py:248
  29.3 0.0 collective-permute-done.partner_rows
  29.3 0.1 eq.106
  29.4 0.0 copy-start.7
  29.4 0.0 copy-start.8
  29.4 0.0 copy-start.9
  29.4 0.0 copy-start.10
  29.4 0.0 copy-start.11
  29.4 0.0 copy-start.12
  29.4 1.3 %convolution_convert_fusion = bf16[384,1024]{1,0:T(8,128)(2,1)} fusion(bf16[240,1024]{1,0:T(8,128)(2,1)S(1)} %copy-done, s32[384]{0:T(512)S(1)} %eq.106), kind=kOutput, calls=%fused_computation.1 | convolution fusion | flops 189229056 | bytes 1279488 | tf_op jit(solution)/shard_map/dot_general | solution.py:261
  30.7 5.0 %all-to-all-start.1 = ((bf16[16,24,1024]{2,1,0:T(8,128)(2,1)}), bf16[16,24,1024]{2,1,0:T(8,128)(2,1)S(1)}, u32[]{:S(2)}, u32[]{:S(2)}) async-start(bf16[16,24,1024]{2,1,0:T(8,128)(2,1)} %bitcast.5), calls=%async_computation.1 | async-start | bytes 1572864 | tf_op jit(solution)/shard_map/all_to_all | solution.py:264
  35.7 2.8 %collective-permute-start.1 = (s32[256]{0:T(256)S(1)}, s32[256]{0:T(256)S(1)}, u32[]{:S(2)}, u32[]{:S(2)}) collective-permute-start(s32[256]{0:T(256)S(1)} %get-tuple-element.26), channel_id=1, source_target_pairs={{0,8},{1,9},{2,10},{3,11},{4,12},{5,13},{6,14},{7,15},{8,0},{9,1},... | collective-permute-start | bytes 3080 | tf_op jit(solution)/shard_map/ppermute | solution.py:241
  38.6 0.1 copy.40
  38.7 0.1 reshape.365
  38.8 0.2 and.146
  39.0 0.1 div.56
  39.1 0.1 copy.39
  39.2 17.4 %collective-permute-done.1 = s32[256]{0:T(256)S(1)} collective-permute-done((s32[256]{0:T(256)S(1)}, s32[256]{0:T(256)S(1)}, u32[]{:S(2)}, u32[]{:S(2)}) %collective-permute-start.1) | collective-permute-done | bytes 1056 | tf_op jit(solution)/shard_map/ppermute | solution.py:241
  56.7 1.5 %pack.1 = (bf16[96,1024]{1,0:T(8,128)(2,1)S(1)}, bf16[96,1024]{1,0:T(8,128)(2,1)}, bf16[96,1024]{1,0:T(8,128)(2,1)}, bf16[96,1024]{1,0:T(8,128)(2,1)}, bf16[96,1...) custom-call(s32[1,256]{1,0:T(1,128)S(1)} %bitcast_select_fusion.own_slo, ...), custom_call_target="tpu_custom_call" | custom-call | flops 399507456 | bytes 2613248 | tf_op jit(solution)/shard_map/pack/pallas_call | solution.py:135
  58.1 0.0 collective-permute-start.2
  58.2 1.5 %collective-permute-start.3 = (bf16[96,1024]{1,0:T(8,128)(2,1)}, bf16[96,1024]{1,0:T(8,128)(2,1)}, u32[]{:S(2)}, u32[]{:S(2)}) collective-permute-start(bf16[96,1024]{1,0:T(8,128)(2,1)} %get-tuple-element.16), channel_id=1, source_target_pairs={{0,2},{1,3},{2,4},{3,5},{4,6},{5,7},{6,0},{7,1},{8,10},{9,11},{10,... | collective-permute-start | bytes 589832 | tf_op jit(solution)/shard_map/ppermute | solution.py:272
  59.7 0.1 collective-permute-start.4
  59.8 2.8 %collective-permute-start.5 = (bf16[96,1024]{1,0:T(8,128)(2,1)}, bf16[96,1024]{1,0:T(8,128)(2,1)}, u32[]{:S(2)}, u32[]{:S(2)}) collective-permute-start(bf16[96,1024]{1,0:T(8,128)(2,1)} %get-tuple-element.18), channel_id=1, source_target_pairs={{0,4},{1,5},{2,6},{3,7},{4,0},{5,1},{6,2},{7,3},{8,12},{9,13},{10,... | collective-permute-start | bytes 589832 | tf_op jit(solution)/shard_map/ppermute | solution.py:272
  62.6 0.1 collective-permute-start.6
  62.7 0.0 all-to-all-done.1
  62.8 0.0 copy-start.1
  62.8 1.9 %copy-done.1 = bf16[1024,1536]{1,0:T(8,128)(2,1)S(1)} copy-done((bf16[1024,1536]{1,0:T(8,128)(2,1)S(1)}, bf16[1024,1536]{1,0:T(8,128)(2,1)}, u32[]{:S(2)}) %copy-start.1) | copy-done | bytes 3145752
  64.7 1.2 %copy-done.3 = bf16[512,1024]{1,0:T(8,128)(2,1)S(1)} copy-done((bf16[512,1024]{1,0:T(8,128)(2,1)S(1)}, bf16[512,1024]{1,0:T(8,128)(2,1)}, u32[]{:S(2)}) %copy-start.3) | copy-done | bytes 1048600
  65.9 0.9 copy-done.6
  66.8 3.7 %encode.1 = bf16[2,1024]{1,0:T(2,128)(2,1)} custom-call(s32[2]{0:T(128)S(1)} %copy-done.12, s32[128,1]{1,0:T(8,128)S(1)} %fusion.3.slots, bf16[384,1024]{1,0:T(8,128)(2,1)S(1)} %bitcast.23, bf16[64,1024]{1,0:T(8,128)(2,1)S(1)} %copy-done.6, f32[1,1024]{1,0:T(1,128)S(1)} %bitcast.24, f32[1,1024]{1,0:T(1,128)S(1)} %bitcast.25, ...), custom_call_target="tpu_custom_call" | custom-call | flops 637534208 | bytes 6291456 | tf_op jit(solution)/shard_map/encode/pallas_call | solution.py:83
  70.5 1.4 %broadcast_in_dim.97 = bf16[16,2,1024]{2,1,0:T(2,128)(2,1)} broadcast(bf16[2,1024]{1,0:T(2,128)(2,1)} %encode.1), dimensions={1,2} | broadcast | bytes 69632 | tf_op jit(solution)/shard_map/broadcast_in_dim | solution.py:292
  71.8 4.0 %all-to-all-start.2 = ((bf16[16,2,1024]{2,1,0:T(2,128)(2,1)}), bf16[16,2,1024]{2,1,0:T(2,128)(2,1)S(1)}, u32[]{:S(2)}, u32[]{:S(2)}) async-start(bf16[16,2,1024]{2,1,0:T(2,128)(2,1)} %broadcast_in_dim.97), calls=%async_computation.2 | async-start | bytes 131072 | tf_op jit(solution)/shard_map/all_to_all | solution.py:291
  75.8 0.0 collective-permute-done.2.rest_1_
  75.8 2.9 %collective-permute-start.7 = (bf16[96,1024]{1,0:T(8,128)(2,1)}, bf16[96,1024]{1,0:T(8,128)(2,1)S(1)}, u32[]{:S(2)}, u32[]{:S(2)}) collective-permute-start(bf16[96,1024]{1,0:T(8,128)(2,1)} %copy-done.15), channel_id=1, source_target_pairs={{0,6},{1,7},{2,0},{3,1},{4,2},{5,3},{6,4},{7,5},{8,14},{9,15},{10,... | collective-permute-start | bytes 589832 | tf_op jit(solution)/shard_map/ppermute | solution.py:272
  78.7 0.0 collective-permute-done.3.rest_2_
  78.7 0.0 collective-permute-start.8
  78.8 0.1 slice.20
  78.8 0.1 slice.19
  78.9 0.1 reshape.367.late
  79.0 0.6 gather_fusion
  79.6 0.1 reshape.366.places
  79.7 3.1 %all-to-all-done.2 = bf16[16,2,1024]{2,1,0:T(2,128)(2,1)S(1)} async-done(((bf16[16,2,1024]{2,1,0:T(2,128)(2,1)}), bf16[16,2,1024]{2,1,0:T(2,128)(2,1)S(1)}, u32[]{:S(2)}, u32[]{:S(2)}) %all-to-all-start.2) | async-done | bytes 65568 | tf_op jit(solution)/shard_map/all_to_all | solution.py:291
  82.8 0.0 collective-permute-done.4.rest_3_
  82.8 0.0 collective-permute-done.5.rest_4_
  82.8 0.0 collective-permute-done.6.rest_5_
  82.8 1.6 %collective-permute-done.7.rest_6_ = bf16[96,1024]{1,0:T(8,128)(2,1)S(1)} collective-permute-done((bf16[96,1024]{1,0:T(8,128)(2,1)}, bf16[96,1024]{1,0:T(8,128)(2,1)S(1)}, u32[]{:S(2)}, u32[]{:S(2)}) %collective-permute-start.7) | collective-permute-done | bytes 196640 | tf_op jit(solution)/shard_map/ppermute | solution.py:272
  84.4 1.3 %collective-permute-done.8.rest_7_ = bf16[96,1024]{1,0:T(8,128)(2,1)S(1)} collective-permute-done((bf16[96,1024]{1,0:T(8,128)(2,1)}, bf16[96,1024]{1,0:T(8,128)(2,1)S(1)}, u32[]{:S(2)}, u32[]{:S(2)}) %collective-permute-start.8) | collective-permute-done | bytes 196640 | tf_op jit(solution)/shard_map/ppermute | solution.py:272
  85.7 0.9 %copy-done.5 = bf16[96,1024]{1,0:T(8,128)(2,1)S(1)} copy-done((bf16[96,1024]{1,0:T(8,128)(2,1)S(1)}, bf16[96,1024]{1,0:T(8,128)(2,1)}, u32[]{:S(2)}) %copy-start.5) | copy-done | bytes 196632
  86.6 4.3 %update.1 = f32[512,1024]{1,0:T(8,128)} custom-call(s32[1,768]{1,0:T(1,128)S(1)} %reshape.366.places, s32[1,32]{1,0:T(1,128)S(1)} %reshape.367.late, bf16[32,1024]{1,0:T(8,128)(2,1)S(1)} %reshape.368.embeds, f32[512,1024]{1,0:T(8,128)S(1)} %copy-done.2, bf16[96,1024]{1,0:T(8,128)(2,1)S(1)} %copy-done.5, bf16[96,1024]{1,0:T(8,128)(2,1)} %collective-permute-done.2.rest_1_, ...), custom_call_target="tpu_custom_call" | custom-call | flops 805306368 | bytes 4194304 | tf_op jit(solution)/shard_map/update/pallas_call | solution.py:180
  (36 shorter events, 0.2 us)
Async XLA Ops:
  0.6 28.7 %copy-start = (bf16[240,1024]{1,0:T(8,128)(2,1)S(1)}, bf16[240,1024]{1,0:T(8,128)(2,1)}, u32[]{:S(2)}) copy-start(bf16[240,1024]{1,0:T(8,128)(2,1)} %param.17) | copy-start | bytes 1474564
  0.6 56.0 %copy-start.13 = (bf16[254,1024]{1,0:T(8,128)(2,1)S(1)}, bf16[254,1024]{1,0:T(8,128)(2,1)}, u32[]{:S(2)}) copy-start(bf16[254,1024]{1,0:T(8,128)(2,1)} %own_rows.1) | copy-start | bytes 1560580
  0.7 37.9 %copy-start.17 = (s32[2,64]{1,0:T(2,128)S(1)}, s32[2,64]{1,0:T(2,128)}, u32[]{:S(2)}) copy-start(s32[2,64]{1,0:T(2,128)} %param.15) | copy-start | bytes 1540
  0.7 37.9 %copy-start.16 = (s32[256,1]{0,1:T(1,128)S(1)}, s32[256,1]{0,1:T(1,128)}, u32[]{:S(2)}) copy-start(s32[256,1]{0,1:T(1,128)} %param.27) | copy-start | bytes 3076
  0.7 28.6 %collective-permute-start = (bf16[254,1024]{1,0:T(8,128)(2,1)}, bf16[254,1024]{1,0:T(8,128)(2,1)S(1)}, u32[]{:S(2)}, u32[]{:S(2)}) collective-permute-start(bf16[254,1024]{1,0:T(8,128)(2,1)} %own_rows.1), channel_id=1, source_target_pairs={{0,8},{1,9},{2,10},{3,11},{4,12},{5,13},{6,14},{7,15},{8,0},{9,1},... | collective-permute-start | bytes 1560584 | tf_op jit(solution)/shard_map/ppermute | solution.py:232
  29.4 33.3 %copy-start.7 = (f32[1024]{0:T(1024)S(1)}, f32[1024]{0:T(1024)}, u32[]{:S(2)}) copy-start(f32[1024]{0:T(1024)} %param.19) | copy-start | bytes 12292
  29.4 33.3 %copy-start.8 = (f32[1024]{0:T(1024)S(1)}, f32[1024]{0:T(1024)}, u32[]{:S(2)}) copy-start(f32[1024]{0:T(1024)} %param.20) | copy-start | bytes 12292
  29.4 33.3 %copy-start.9 = (f32[1024]{0:T(1024)S(1)}, f32[1024]{0:T(1024)}, u32[]{:S(2)}) copy-start(f32[1024]{0:T(1024)} %param.23) | copy-start | bytes 12292
  29.4 33.3 %copy-start.10 = (f32[1024]{0:T(1024)S(1)}, f32[1024]{0:T(1024)}, u32[]{:S(2)}) copy-start(f32[1024]{0:T(1024)} %param.24) | copy-start | bytes 12292
  29.4 33.3 %copy-start.11 = (f32[1024]{0:T(1024)S(1)}, f32[1024]{0:T(1024)}, u32[]{:S(2)}) copy-start(f32[1024]{0:T(1024)} %param.25) | copy-start | bytes 12292
  29.4 33.3 %copy-start.12 = (s32[2]{0:T(128)S(1)}, s32[2]{0:T(128)}, u32[]{:S(2)}) copy-start(s32[2]{0:T(128)} %lengths.1) | copy-start | bytes 28
  30.7 32.0 %all-to-all-start.1 = ((bf16[16,24,1024]{2,1,0:T(8,128)(2,1)}), bf16[16,24,1024]{2,1,0:T(8,128)(2,1)S(1)}, u32[]{:S(2)}, u32[]{:S(2)}) async-start(bf16[16,24,1024]{2,1,0:T(8,128)(2,1)} %bitcast.5), calls=%async_computation.1 | async-start | bytes 1572864 | tf_op jit(solution)/shard_map/all_to_all | solution.py:264
  35.7 21.0 %collective-permute-start.1 = (s32[256]{0:T(256)S(1)}, s32[256]{0:T(256)S(1)}, u32[]{:S(2)}, u32[]{:S(2)}) collective-permute-start(s32[256]{0:T(256)S(1)} %get-tuple-element.26), channel_id=1, source_target_pairs={{0,8},{1,9},{2,10},{3,11},{4,12},{5,13},{6,14},{7,15},{8,0},{9,1},... | collective-permute-start | bytes 3080 | tf_op jit(solution)/shard_map/ppermute | solution.py:241
  58.1 4.5 %copy-start.4 = (bf16[96,1024]{1,0:T(8,128)(2,1)}, bf16[96,1024]{1,0:T(8,128)(2,1)S(1)}, u32[]{:S(2)}) copy-start(bf16[96,1024]{1,0:T(8,128)(2,1)S(1)} %get-tuple-element.14.rest_0_) | copy-start | bytes 589828
  58.1 4.5 %copy-start.14 = (bf16[96,1024]{1,0:T(8,128)(2,1)}, bf16[96,1024]{1,0:T(8,128)(2,1)S(1)}, u32[]{:S(2)}) copy-start(bf16[96,1024]{1,0:T(8,128)(2,1)S(1)} %get-tuple-element.21) | copy-start | bytes 589828
  58.1 4.5 %copy-start.15 = (bf16[96,1024]{1,0:T(8,128)(2,1)}, bf16[96,1024]{1,0:T(8,128)(2,1)S(1)}, u32[]{:S(2)}) copy-start(bf16[96,1024]{1,0:T(8,128)(2,1)S(1)} %get-tuple-element.20) | copy-start | bytes 589828
  58.1 17.7 %collective-permute-start.2 = (bf16[96,1024]{1,0:T(8,128)(2,1)}, bf16[96,1024]{1,0:T(8,128)(2,1)}, u32[]{:S(2)}, u32[]{:S(2)}) collective-permute-start(bf16[96,1024]{1,0:T(8,128)(2,1)} %get-tuple-element.15), channel_id=1, source_target_pairs={{0,1},{1,2},{2,3},{3,4},{4,5},{5,6},{6,7},{7,0},{8,9},{9,10},{10,1... | collective-permute-start | bytes 589832 | tf_op jit(solution)/shard_map/ppermute | solution.py:272
  58.2 20.5 %collective-permute-start.3 = (bf16[96,1024]{1,0:T(8,128)(2,1)}, bf16[96,1024]{1,0:T(8,128)(2,1)}, u32[]{:S(2)}, u32[]{:S(2)}) collective-permute-start(bf16[96,1024]{1,0:T(8,128)(2,1)} %get-tuple-element.16), channel_id=1, source_target_pairs={{0,2},{1,3},{2,4},{3,5},{4,6},{5,7},{6,0},{7,1},{8,10},{9,11},{10,... | collective-permute-start | bytes 589832 | tf_op jit(solution)/shard_map/ppermute | solution.py:272
  59.7 23.0 %collective-permute-start.4 = (bf16[96,1024]{1,0:T(8,128)(2,1)}, bf16[96,1024]{1,0:T(8,128)(2,1)}, u32[]{:S(2)}, u32[]{:S(2)}) collective-permute-start(bf16[96,1024]{1,0:T(8,128)(2,1)} %get-tuple-element.17), channel_id=1, source_target_pairs={{0,3},{1,4},{2,5},{3,6},{4,7},{5,0},{6,1},{7,2},{8,11},{9,12},{10,... | collective-permute-start | bytes 589832 | tf_op jit(solution)/shard_map/ppermute | solution.py:272
  59.8 23.0 %collective-permute-start.5 = (bf16[96,1024]{1,0:T(8,128)(2,1)}, bf16[96,1024]{1,0:T(8,128)(2,1)}, u32[]{:S(2)}, u32[]{:S(2)}) collective-permute-start(bf16[96,1024]{1,0:T(8,128)(2,1)} %get-tuple-element.18), channel_id=1, source_target_pairs={{0,4},{1,5},{2,6},{3,7},{4,0},{5,1},{6,2},{7,3},{8,12},{9,13},{10,... | collective-permute-start | bytes 589832 | tf_op jit(solution)/shard_map/ppermute | solution.py:272
  62.6 20.1 %collective-permute-start.6 = (bf16[96,1024]{1,0:T(8,128)(2,1)}, bf16[96,1024]{1,0:T(8,128)(2,1)}, u32[]{:S(2)}, u32[]{:S(2)}) collective-permute-start(bf16[96,1024]{1,0:T(8,128)(2,1)} %get-tuple-element.19), channel_id=1, source_target_pairs={{0,5},{1,6},{2,7},{3,0},{4,1},{5,2},{6,3},{7,4},{8,13},{9,14},{10,... | collective-permute-start | bytes 589832 | tf_op jit(solution)/shard_map/ppermute | solution.py:272
  62.8 1.9 %copy-start.1 = (bf16[1024,1536]{1,0:T(8,128)(2,1)S(1)}, bf16[1024,1536]{1,0:T(8,128)(2,1)}, u32[]{:S(2)}) copy-start(bf16[1024,1536]{1,0:T(8,128)(2,1)} %w_qkv.1) | copy-start | bytes 9437188
  64.7 1.2 %copy-start.3 = (bf16[512,1024]{1,0:T(8,128)(2,1)S(1)}, bf16[512,1024]{1,0:T(8,128)(2,1)}, u32[]{:S(2)}) copy-start(bf16[512,1024]{1,0:T(8,128)(2,1)} %w_out.1) | copy-start | bytes 3145732
  65.9 0.9 copy-start.6
  66.8 18.9 %copy-start.2 = (f32[512,1024]{1,0:T(8,128)S(1)}, f32[512,1024]{1,0:T(8,128)}, u32[]{:S(2)}) copy-start(f32[512,1024]{1,0:T(8,128)} %centroids.1) | copy-start | bytes 6291460
  71.8 10.9 %all-to-all-start.2 = ((bf16[16,2,1024]{2,1,0:T(2,128)(2,1)}), bf16[16,2,1024]{2,1,0:T(2,128)(2,1)S(1)}, u32[]{:S(2)}, u32[]{:S(2)}) async-start(bf16[16,2,1024]{2,1,0:T(2,128)(2,1)} %broadcast_in_dim.97), calls=%async_computation.2 | async-start | bytes 131072 | tf_op jit(solution)/shard_map/all_to_all | solution.py:291
  75.8 8.5 %collective-permute-start.7 = (bf16[96,1024]{1,0:T(8,128)(2,1)}, bf16[96,1024]{1,0:T(8,128)(2,1)S(1)}, u32[]{:S(2)}, u32[]{:S(2)}) collective-permute-start(bf16[96,1024]{1,0:T(8,128)(2,1)} %copy-done.15), channel_id=1, source_target_pairs={{0,6},{1,7},{2,0},{3,1},{4,2},{5,3},{6,4},{7,5},{8,14},{9,15},{10,... | collective-permute-start | bytes 589832 | tf_op jit(solution)/shard_map/ppermute | solution.py:272
  78.7 7.0 %collective-permute-start.8 = (bf16[96,1024]{1,0:T(8,128)(2,1)}, bf16[96,1024]{1,0:T(8,128)(2,1)S(1)}, u32[]{:S(2)}, u32[]{:S(2)}) collective-permute-start(bf16[96,1024]{1,0:T(8,128)(2,1)} %copy-done.14), channel_id=1, source_target_pairs={{0,7},{1,0},{2,1},{3,2},{4,3},{5,4},{6,5},{7,6},{8,15},{9,8},{10,9... | collective-permute-start | bytes 589832 | tf_op jit(solution)/shard_map/ppermute | solution.py:272
  85.7 0.9 %copy-start.5 = (bf16[96,1024]{1,0:T(8,128)(2,1)S(1)}, bf16[96,1024]{1,0:T(8,128)(2,1)}, u32[]{:S(2)}) copy-start(bf16[96,1024]{1,0:T(8,128)(2,1)} %copy-done.4) | copy-start | bytes 589828

commit v5 on v4

--- a/solution.py
+++ b/solution.py
@@ -30,8 +30,27 @@
 
 
 def encode_kernel(
-    lengths, slots, fetched, pos, emb_gain, emb_bias, w_qkv, w_out, out_bias, norm_gain, norm_bias, out
+    lengths,
+    slots,
+    fetched,
+    pos,
+    emb_gain,
+    emb_bias,
+    w_qkv_far,
+    w_out_far,
+    out_bias,
+    norm_gain,
+    norm_bias,
+    out,
+    spread,
+    w_qkv,
+    w_out,
+    arrived,
 ):
+    qkv_copy = pltpu.make_async_copy(w_qkv_far, w_qkv, arrived.at[0])
+    out_copy = pltpu.make_async_copy(w_out_far, w_out, arrived.at[1])
+    qkv_copy.start()
+    out_copy.start()
     tokens, slot_count = slots.shape[0], fetched.shape[0]
     passes = out.shape[0]
     seq = tokens // passes
@@ -42,6 +61,7 @@
     where_at = pos[...].astype(jnp.float32)
     summed = tok + jnp.concatenate([where_at] * passes, axis=0)
     embedded = normed(summed, emb_gain[...], emb_bias[...]).astype(jnp.bfloat16)
+    qkv_copy.wait()
     projected = jnp.dot(embedded, w_qkv[...], preferred_element_type=jnp.float32)
     projected = projected.astype(jnp.bfloat16)
 
@@ -63,6 +83,7 @@
         probs = (weights / head_sums(weights, seq)).astype(jnp.bfloat16)
         contexts.append(jnp.dot(probs, vals, preferred_element_type=jnp.float32))
     context = jnp.concatenate(contexts, axis=0).astype(jnp.bfloat16)
+    out_copy.wait()
     attended = jnp.dot(context, w_out[...], preferred_element_type=jnp.float32) + out_bias[...]
     hidden = normed(embedded.astype(jnp.float32) + attended, norm_gain[...], norm_bias[...])
     row = lax.broadcasted_iota(jnp.int32, (seq, 1), 0)
@@ -71,10 +92,11 @@
         pooled = jnp.sum(kept, axis=0, keepdims=True) / lengths[p].astype(jnp.float32)
         scale = lax.rsqrt(jnp.mean(pooled * pooled, axis=-1, keepdims=True) + 1e-06)
         out[p : p + 1, :] = (pooled * scale).astype(jnp.bfloat16)
+    spread[...] = jnp.broadcast_to(out[...][None], spread.shape)
 
 
 def encode(
-    slots, fetched, lengths, pos_table, emb_gain, emb_bias, w_qkv, w_out, out_bias, norm_gain, norm_bias
+    peers, slots, fetched, lengths, pos_table, emb_gain, emb_bias, w_qkv, w_out, out_bias, norm_gain, norm_bias
 ):
     width = fetched.shape[1]
     tokens = slots.shape[0]
@@ -82,10 +104,20 @@
     macs = tokens * width * (fetched.shape[0] + 4 * HEADS * HD)
     return pl.pallas_call(
         encode_kernel,
-        out_shape=jax.ShapeDtypeStruct((passes, width), jnp.bfloat16),
+        out_shape=[
+            jax.ShapeDtypeStruct((passes, width), jnp.bfloat16),
+            jax.ShapeDtypeStruct((peers, passes, width), jnp.bfloat16),
+        ],
         in_specs=[pl.BlockSpec(memory_space=pltpu.SMEM)]
-        + [pl.BlockSpec(memory_space=pltpu.VMEM)] * 10,
-        out_specs=pl.BlockSpec(memory_space=pltpu.VMEM),
+        + [pl.BlockSpec(memory_space=pltpu.VMEM)] * 5
+        + [pl.BlockSpec(memory_space=pltpu.HBM)] * 2
+        + [pl.BlockSpec(memory_space=pltpu.VMEM)] * 3,
+        out_specs=[pl.BlockSpec(memory_space=pltpu.VMEM)] * 2,
+        scratch_shapes=[
+            pltpu.VMEM(w_qkv.shape, w_qkv.dtype),
+            pltpu.VMEM(w_out.shape, w_out.dtype),
+            pltpu.SemaphoreType.DMA((2,)),
+        ],
         compiler_params=pltpu.CompilerParams(vmem_limit_bytes=32 * 1024 * 1024),
         cost_estimate=pl.CostEstimate(
             flops=2 * macs, bytes_accessed=6 * 1024 * 1024, transcendentals=0
@@ -93,7 +125,7 @@
         name="encode",
     )(
         lengths,
-        slots[:, None],
+        slots,
         fetched,
         pos_table,
         emb_gain[None],
@@ -106,15 +138,72 @@
     )
 
 
-def slot_rank(target):
-    positions = jnp.arange(target.shape[0], dtype=jnp.int32)
-    earlier = (target[:, None] == target[None, :]) & (positions[None, :] < positions[:, None])
-    return jnp.sum(earlier.astype(jnp.int32), axis=1)
-
-
-def place_ints(slot, values, slot_count):
-    table = slot[None, :] == jnp.arange(slot_count, dtype=jnp.int32)[:, None]
-    return jnp.sum(jnp.where(table, values[None, :] + 1, 0), axis=1) - 1
+def route_kernel(
+    sizes, token_ids, owners, row_slot, plan, token_slot, own_slot, partner_slot
+):
+    peers, vocab_rows, token_cap, row_cap, pooled = sizes
+    half = peers // 2
+    me = lax.axis_index("dp")
+    ids = jnp.concatenate([token_ids[p : p + 1, :] for p in range(token_ids.shape[0])], axis=1)
+    tokens, rows = ids.shape[1], owners.shape[1]
+    count = tokens + rows
+    edge = (lax.broadcasted_iota(jnp.int32, (peers, tokens), 0) + 1) * vocab_rows
+    holder = jnp.sum(jnp.where(ids >= edge, 1, 0), axis=0, keepdims=True)
+    values = jnp.concatenate([ids - holder * vocab_rows, row_slot[...]], axis=1)
+
+    kind = jnp.concatenate([holder, owners[...] + peers], axis=1)
+    at = lax.broadcasted_iota(jnp.int32, (count, count), 0)
+    by = lax.broadcasted_iota(jnp.int32, (count, count), 1)
+    across = jnp.broadcast_to(kind, (count, count))
+    down = jnp.sum(jnp.where(at == by, across, 0), axis=1, keepdims=True)
+    same = down == across
+    rank_row = jnp.sum(jnp.where(same & (at < by), 1, 0), axis=0, keepdims=True)
+    rank_col = jnp.sum(jnp.where(same & (by < at), 1, 0), axis=1, keepdims=True)
+
+    goal = jnp.concatenate([holder, owners[...]], axis=1)
+    peer = lax.broadcasted_iota(jnp.int32, (peers, count), 0)
+    left = jnp.where(peer == goal, values + 1, 0).astype(jnp.float32)
+    columns = plan.shape[1]
+    column = lax.broadcasted_iota(jnp.int32, (count, columns), 1)
+    entry = lax.broadcasted_iota(jnp.int32, (count, 1), 0)
+    first = jnp.where(entry < tokens, rank_col, rank_col + token_cap)
+    second = entry - (count - pooled) + token_cap + row_cap
+    second = jnp.where(entry < count - pooled, -1, second)
+    right = jnp.where((column == first) | (column == second), 1.0, 0.0)
+    filled = jnp.dot(
+        left, right, preferred_element_type=jnp.float32, precision=lax.Precision.HIGHEST
+    )
+    plan[...] = filled.astype(jnp.int32) - 1
+    token_slot[...] = down[:tokens] * token_cap + rank_col[:tokens]
+
+    def half_slot(device):
+        first = jnp.where(device < half, 0, half)
+        inside = (owners[...] >= first) & (owners[...] < first + half)
+        step = owners[...] - device
+        step = jnp.where(step < 0, step + half, step)
+        return jnp.where(inside, step * row_cap + rank_row[:, tokens:], -1)
+
+    own_slot[...] = half_slot(me)
+    partner_slot[...] = half_slot(jnp.where(me < half, me + half, me - half))
+
+
+def route(token_ids, owners, row_slot, sizes):
+    peers, _, token_cap, row_cap, pooled = sizes
+    passes, seq_len = token_ids.shape
+    rows = owners.shape[1]
+    ints = lambda *shape: jax.ShapeDtypeStruct(shape, jnp.int32)
+    return pl.pallas_call(
+        functools.partial(route_kernel, sizes),
+        out_shape=[
+            ints(peers, token_cap + row_cap + pooled),
+            ints(passes * seq_len, 1),
+            ints(1, rows),
+            ints(1, rows),
+        ],
+        in_specs=[pl.BlockSpec(memory_space=pltpu.VMEM)] * 3,
+        out_specs=[pl.BlockSpec(memory_space=pltpu.VMEM)] * 4,
+        name="route",
+    )(token_ids, owners, row_slot)
 
 
 def pack_kernel(row_cap, own_slot, partner_slot, own_rows, partner_rows, *outs):
@@ -144,55 +233,79 @@
             transcendentals=0,
         ),
         name="pack",
-    )(own_slot[None], partner_slot[None], own_rows, partner_rows)
-
-
-def update_kernel(places, late, embeds, centroids, *rest):
-    pieces, out, rows = rest[:-2], rest[-2], rest[-1]
+    )(own_slot, partner_slot, own_rows, partner_rows)
+
+
+def onehot(where_to, count):
+    centre = lax.broadcasted_iota(jnp.int32, (count, where_to.shape[1]), 0)
+    centre += pl.program_id(0) * count
+    return jnp.where(centre == where_to[...], 1.0, 0.0)
+
+
+def early_kernel(places, centroids, *rest):
+    pieces, (out, share, rows) = rest[:-3], rest[-3:]
     count = out.shape[0]
-    step = pl.program_id(0)
-
-    @pl.when(step == 0)
+
+    @pl.when(pl.program_id(0) == 0)
     def _():
         at = 0
         for piece in pieces:
             rows[at : at + piece.shape[0], :] = piece[...]
             at += piece.shape[0]
 
-    def onehot(where_to):
-        centre = lax.broadcasted_iota(jnp.int32, (count, where_to.shape[1]), 0) + step * count
-        return jnp.where(centre == where_to[...], 1.0, 0.0)
-
-    early_hot, late_hot = onehot(places), onehot(late)
-    sums = jnp.dot(
-        early_hot.astype(jnp.bfloat16), rows[...], preferred_element_type=jnp.float32
-    ) + jnp.dot(late_hot.astype(jnp.bfloat16), embeds[...], preferred_element_type=jnp.float32)
-    counts = jnp.sum(early_hot, axis=1, keepdims=True)
-    out[...] = jnp.where(counts > 0, sums / jnp.maximum(counts, 1.0), centroids[...])
+    hot = onehot(places, count)
+    sums = jnp.dot(hot.astype(jnp.bfloat16), rows[...], preferred_element_type=jnp.float32)
+    counts = jnp.sum(hot, axis=1, keepdims=True)
+    scale = 1.0 / jnp.maximum(counts, 1.0)
+    out[...] = jnp.where(counts > 0, sums * scale, centroids[...])
+    share[...] = jnp.broadcast_to(scale, share.shape)
+
+
+def late_kernel(late, embeds, early, share, out):
+    hot = onehot(late, out.shape[0]).astype(jnp.bfloat16)
+    sums = jnp.dot(hot, embeds[...], preferred_element_type=jnp.float32)
+    out[...] = early[...] + sums * share[:, :1]
 
 
 def update(places, late, embeds, centroids, pieces):
     centre_count, width = centroids.shape
     block = 128
+    grid = (centre_count // block,)
     whole = lambda array: pl.BlockSpec(array.shape, lambda i: (0, 0))
     part = pl.BlockSpec((block, width), lambda i: (i, 0))
+    thin = pl.BlockSpec((block, 128), lambda i: (i, 0))
     row_total = sum(piece.shape[0] for piece in pieces)
-    return pl.pallas_call(
-        update_kernel,
-        grid=(centre_count // block,),
-        out_shape=jax.ShapeDtypeStruct(centroids.shape, jnp.float32),
-        in_specs=[whole(places), whole(late), whole(embeds), part]
-        + [whole(piece) for piece in pieces],
-        out_specs=part,
+    full = jax.ShapeDtypeStruct(centroids.shape, jnp.float32)
+    params = pltpu.CompilerParams(vmem_limit_bytes=32 * 1024 * 1024)
+    early, share = pl.pallas_call(
+        early_kernel,
+        grid=grid,
+        out_shape=[full, jax.ShapeDtypeStruct((centre_count, 128), jnp.float32)],
+        in_specs=[whole(places), part] + [whole(piece) for piece in pieces],
+        out_specs=[part, thin],
         scratch_shapes=[pltpu.VMEM((row_total, width), jnp.bfloat16)],
-        compiler_params=pltpu.CompilerParams(vmem_limit_bytes=32 * 1024 * 1024),
+        compiler_params=params,
         cost_estimate=pl.CostEstimate(
             flops=2 * centre_count * width * row_total,
             bytes_accessed=8 * centre_count * width,
             transcendentals=0,
         ),
-        name="update",
-    )(places, late, embeds, centroids, *pieces)
+        name="early",
+    )(places, centroids, *pieces)
+    return pl.pallas_call(
+        late_kernel,
+        grid=grid,
+        out_shape=full,
+        in_specs=[whole(late), whole(embeds), part, thin],
+        out_specs=part,
+        compiler_params=params,
+        cost_estimate=pl.CostEstimate(
+            flops=2 * centre_count * width * late.shape[1],
+            bytes_accessed=8 * centre_count * width,
+            transcendentals=0,
+        ),
+        name="late",
+    )(late, embeds, early, share)
 
 
 def shards(
@@ -216,51 +329,30 @@
     half = peer_count // 2
     me = lax.axis_index("dp")
     base = me // half * half
-    peers = jnp.arange(peer_count, dtype=jnp.int32)
     width = word_table.shape[1]
     vocab_rows = word_table.shape[0]
     passes, seq_len = token_ids.shape
-    token_list = token_ids.reshape(passes * seq_len)
-    token_count = token_list.shape[0]
+    token_count = passes * seq_len
     row_count = row_slot.shape[0]
     store_count = stored_rows.shape[0]
-    owners = row_owner[:, 0]
     token_cap = max(2, 3 * token_count // peer_count)
     row_cap = max(2, 3 * row_count // peer_count)
 
     across = [(i, (i + half) % peer_count) for i in range(peer_count)]
     partner_rows = lax.ppermute(stored_rows, "dp", across)
-    row_rank = slot_rank(owners)
-
-    def half_slot(holder):
-        first = holder // half * half
-        inside = (owners >= first) & (owners < first + half)
-        return jnp.where(inside, (owners - holder + half) % half * row_cap + row_rank, -1)
-
-    own_slot = half_slot(me)
-    partner_slot = lax.ppermute(half_slot((me + half) % peer_count), "dp", across)
-
-    target = token_list // vocab_rows
-    token_slot = target * token_cap + slot_rank(target)
-    requests = place_ints(token_slot, token_list - target * vocab_rows, peer_count * token_cap)
-    places = place_ints(owners * row_cap + row_rank, row_slot, peer_count * row_cap)
-    late = jnp.where(owners[None, store_count:] == peers[:, None], row_slot[None, store_count:], -1)
-    plan = lax.all_to_all(
-        jnp.concatenate(
-            [requests.reshape(peer_count, token_cap), places.reshape(peer_count, row_cap), late],
-            axis=1,
-        ),
-        "dp",
-        split_axis=0,
-        concat_axis=0,
-        tiled=True,
+    sizes = (peer_count, vocab_rows, token_cap, row_cap, row_count - store_count)
+    plan, token_slot, own_slot, partner_slot = route(
+        token_ids, row_owner.reshape(1, row_count), row_slot[None], sizes
     )
-    plan, partner_rows = lax.optimization_barrier((plan, partner_rows))
+    partner_slot = lax.ppermute(partner_slot, "dp", across)
+    plan = lax.all_to_all(plan, "dp", split_axis=0, concat_axis=0, tiled=True)
+    plan, partner_slot = lax.optimization_barrier((plan, partner_slot))
     wanted = plan[:, :token_cap].reshape(peer_count * token_cap)
     chosen = wanted[:, None] == jnp.arange(vocab_rows, dtype=jnp.int32)[None, :]
     found = jnp.dot(
         chosen.astype(jnp.bfloat16), word_table, preferred_element_type=jnp.float32
     ).astype(jnp.bfloat16)
+    found, partner_rows = lax.optimization_barrier((found, partner_rows))
     fetched = lax.all_to_all(
         found.reshape(peer_count, token_cap, width), "dp", split_axis=0, concat_axis=0, tiled=True
     ).reshape(peer_count * token_cap, width)
@@ -275,7 +367,8 @@
     got_places = plan[:, token_cap : token_cap + row_cap][sources].reshape(1, peer_count * row_cap)
     late_places = plan[:, token_cap + row_cap :].reshape(1, -1)
 
-    passage_embed = encode(
+    passage_embed, spread = encode(
+        peer_count,
         token_slot,
         fetched,
         lengths,
@@ -289,11 +382,7 @@
         norm_bias,
     )
     all_embeds = lax.all_to_all(
-        jnp.broadcast_to(passage_embed[None], (peer_count, passes, width)),
-        "dp",
-        split_axis=0,
-        concat_axis=0,
-        tiled=True,
+        spread, "dp", split_axis=0, concat_axis=0, tiled=True
     ).reshape(peer_count * passes, width)
     new_centroids = update(got_places, late_places, all_embeds, centroids, got_rows)
     return (passage_embed, new_centroids)

time: 91.7 us -> 88.5 us (0.965)
  blocking collectives: 19.8 us -> 0 us
  starting transfers between devices: 23.3 us -> 30.2 us
  local copies, waits for them, and re-layouts: 10.3 us -> 16.1 us
  waiting for transfers between devices: 23.4 us -> 27.1 us
  Pallas kernels: 9.45 us -> 12.2 us
  other arithmetic: 2.36 us -> 0.04 us
    all_to_all x1 -> x0, blocking collectives: 19.8 us -> none  [shards(): lax.all_to_all(jnp.concatenate([requests.reshape(peer_count, token_cap),...]
    unnamed x36 -> x56, local copies, waits for them, and re-layouts: 5.02 us -> 14.1 us
    ppermute x7, waiting for transfers between devices: 2.91 us -> 11.3 us  [shards(): got_rows.append(lax.ppermute(blocks[step], 'dp', moves))]
    all_to_all x1 -> x2, starting transfers between devices: 4 us -> 10.5 us  [the longest x1 6.46 us: shards(): lax.all_to_all(spread, 'dp', split_axis=0, concat_axis=0, tiled=True)]
    pallas_call x2 -> x4, Pallas kernels: 7.98 us -> 10.9 us  [the longest x1 4.1 us: encode(): pl.pallas_call(encode_kernel, out_shape=[jax.ShapeDtypeStruct((passes, wi...]
    ppermute x1, waiting for transfers between devices: 17.4 us -> 14.9 us  [shards(): partner_slot = lax.ppermute(partner_slot, 'dp', across)]
    all_to_all x1 -> x2, waiting for transfers between devices: 3.07 us -> 0.89 us  [the longest x1 0.89 us: shards(): plan = lax.all_to_all(plan, 'dp', split_axis=0, concat_axis=0, tiled=True)]
    reduce_sum x4 -> x0, other arithmetic: 1.43 us -> none  [the longest x2 1.1 us: slot_rank(): return jnp.sum(earlier.astype(jnp.int32), axis=1)]
  transfers between devices with their start and end apart: 11 -> 12, of which waited for: 4 -> 4; matrix products, arithmetic and copies ran while one was open for 8% -> 3% of each run, Pallas kernels for 6% -> 11%
where the time goes in v5:
time: 88.5 us; the launch traced here: 87.8 us
  starting transfers between devices  30.2 us (34%)
  waiting for transfers between devices  27.1 us (31%)
  local copies, waits for them, and re-layouts  16.1 us (18%)
  Pallas kernels  12.2 us (14%)
  matrix products  1.29 us (1%)
  between operations  0.94 us (1%)
    ppermute x1, waiting for transfers between devices, shards(): partner_slot = lax.ppermute(partner_slot, 'dp', across)  14.9 us
    unnamed x56, local copies, waits for them, and re-layouts  14.1 us
    ppermute x7, waiting for transfers between devices, shards(): got_rows.append(lax.ppermute(blocks[step], 'dp', moves))  11.3 us
    ppermute x7, starting transfers between devices, shards(): got_rows.append(lax.ppermute(blocks[step], 'dp', moves))  7.82 us
    all_to_all x1, starting transfers between devices, shards(): lax.all_to_all(spread, 'dp', split_axis=0, concat_axis=0, tiled=True)  6.46 us
    all_to_all x1, starting transfers between devices, shards(): lax.all_to_all(found.reshape(peer_count, token_cap, width), 'dp', split_a...  4.98 us
    ppermute x1, starting transfers between devices, shards(): partner_rows = lax.ppermute(stored_rows, 'dp', across)  4.1 us
    pallas_call x1, Pallas kernels, encode(): pl.pallas_call(encode_kernel, out_shape=[jax.ShapeDtypeStruct((passes, wi...  4.1 us
  transfers between devices with their start and end apart: 12, of which 4 were waited for; matrix products, arithmetic and copies ran while one was open for 3% of the time, Pallas kernels for 11%

profile of v5, /device:TPU:0, one launch (start us, length us, event | category | flops | bytes accessed | tf_op | source)
XLA Modules:
  0.0 87.8 jit_solution(934555366410390389)
XLA Ops:
  0.6 0.0 copy-start
  0.7 4.1 %collective-permute-start.1 = (bf16[254,1024]{1,0:T(8,128)(2,1)}, bf16[254,1024]{1,0:T(8,128)(2,1)S(1)}, u32[]{:S(2)}, u32[]{:S(2)}) collective-permute-start(bf16[254,1024]{1,0:T(8,128)(2,1)} %own_rows.1), channel_id=1, source_target_pairs={{0,8},{1,9},{2,10},{3,11},{4,12},{5,13},{6,14},{7,15},{8,0},{9,1},... | collective-permute-start | bytes 1560584 | tf_op jit(solution)/shard_map/ppermute | solution.py:342
  4.8 1.8 %route.1 = (s32[16,74]{1,0:T(8,128)}, s32[128,1]{1,0:T(8,128)}, s32[1,256]{1,0:T(1,128)}, s32[1,256]{1,0:T(1,128)}) custom-call(s32[2,64]{1,0:T(2,128)} %token_ids.1, s32[1,256]{1,0:T(1,128)} %bitcast.28, s32[1,256]{1,0:T(1,128)} %bitcast.29), custom_call_target="tpu_custom_call" | custom-call | tf_op jit(solution)/shard_map/route/pallas_call | solution.py:195
  6.6 4.0 %all-to-all-start = ((s32[16,1,74]{2,1,0:T(1,128)}), s32[16,1,74]{2,1,0:T(1,128)S(1)}, u32[]{:S(2)}, u32[]{:S(2)}) async-start(s32[16,1,74]{2,1,0:T(1,128)} %bitcast.27), calls=%async_computation | async-start | bytes 16384 | tf_op jit(solution)/shard_map/all_to_all | solution.py:348
  10.7 2.8 %collective-permute-start = (s32[1,256]{1,0:T(1,128)}, s32[1,256]{1,0:T(1,128)S(1)}, u32[]{:S(2)}, u32[]{:S(2)}) collective-permute-start(s32[1,256]{1,0:T(1,128)} %get-tuple-element.24), channel_id=1, source_target_pairs={{0,8},{1,9},{2,10},{3,11},{4,12},{5,13},{6,14},{7,15},{8,0},{9,1},... | collective-permute-start | bytes 3080 | tf_op jit(solution)/shard_map/ppermute | solution.py:347
  13.5 14.9 %collective-permute-done.partner_slot = s32[1,256]{1,0:T(1,128)S(1)} collective-permute-done((s32[1,256]{1,0:T(1,128)}, s32[1,256]{1,0:T(1,128)S(1)}, u32[]{:S(2)}, u32[]{:S(2)}) %collective-permute-start) | collective-permute-done | bytes 1056 | tf_op jit(solution)/shard_map/ppermute | solution.py:347
  28.4 0.9 %all-to-all-done = s32[16,1,74]{2,1,0:T(1,128)S(1)} async-done(((s32[16,1,74]{2,1,0:T(1,128)}), s32[16,1,74]{2,1,0:T(1,128)S(1)}, u32[]{:S(2)}, u32[]{:S(2)}) %all-to-all-start) | async-done | bytes 4768 | tf_op jit(solution)/shard_map/all_to_all | solution.py:348
  29.3 0.1 eq.18
  29.4 0.0 copy-start.3
  29.4 0.0 copy-start.13
  29.4 0.0 copy-start.14
  29.4 0.0 copy-start.15
  29.4 0.0 copy-start.16
  29.4 0.0 copy-start.17
  29.4 0.0 copy-start.18
  29.5 1.3 %convolution_convert_fusion = bf16[384,1024]{1,0:T(8,128)(2,1)} fusion(bf16[240,1024]{1,0:T(8,128)(2,1)S(1)} %copy-done, s32[384]{0:T(512)S(1)} %eq.18), kind=kOutput, calls=%fused_computation.1 | convolution fusion | flops 189229056 | bytes 1279488 | tf_op jit(solution)/shard_map/dot_general | solution.py:352
  30.7 0.0 collective-permute-done.1.partner_rows
  30.8 5.0 %all-to-all-start.1 = ((bf16[16,24,1024]{2,1,0:T(8,128)(2,1)}), bf16[16,24,1024]{2,1,0:T(8,128)(2,1)S(1)}, u32[]{:S(2)}, u32[]{:S(2)}) async-start(bf16[16,24,1024]{2,1,0:T(8,128)(2,1)} %bitcast.23), calls=%async_computation.1 | async-start | bytes 1572864 | tf_op jit(solution)/shard_map/all_to_all | solution.py:356
  35.8 1.0 %copy-done.21 = bf16[254,1024]{1,0:T(8,128)(2,1)S(1)} copy-done((bf16[254,1024]{1,0:T(8,128)(2,1)S(1)}, bf16[254,1024]{1,0:T(8,128)(2,1)}, u32[]{:S(2)}) %copy-start.21) | copy-done | bytes 520216
  36.8 1.3 %pack.1 = (bf16[96,1024]{1,0:T(8,128)(2,1)S(1)}, bf16[96,1024]{1,0:T(8,128)(2,1)}, bf16[96,1024]{1,0:T(8,128)(2,1)}, bf16[96,1024]{1,0:T(8,128)(2,1)S(1)}, bf16[...) custom-call(s32[1,256]{1,0:T(1,128)S(1)} %copy-done.27, ...), custom_call_target="tpu_custom_call" | custom-call | flops 399507456 | bytes 2613248 | tf_op jit(solution)/shard_map/pack/pallas_call | solution.py:224
  38.1 0.7 copy-done.22
  38.8 0.7 copy-done.25
  39.5 0.7 copy-done.26
  40.1 0.4 collective-permute-start.2
  40.5 0.3 copy-done.23
  40.8 0.1 copy-done.24
  40.9 1.9 %collective-permute-start.3 = (bf16[96,1024]{1,0:T(8,128)(2,1)}, bf16[96,1024]{1,0:T(8,128)(2,1)S(1)}, u32[]{:S(2)}, u32[]{:S(2)}) collective-permute-start(bf16[96,1024]{1,0:T(8,128)(2,1)} %get-tuple-element.34), channel_id=1, source_target_pairs={{0,2},{1,3},{2,4},{3,5},{4,6},{5,7},{6,0},{7,1},{8,10},{9,11},{10,... | collective-permute-start | bytes 589832 | tf_op jit(solution)/shard_map/ppermute | solution.py:364
  42.8 0.1 copy.18
  42.9 0.1 reshape.141
  43.0 1.6 %collective-permute-start.4 = (bf16[96,1024]{1,0:T(8,128)(2,1)}, bf16[96,1024]{1,0:T(8,128)(2,1)S(1)}, u32[]{:S(2)}, u32[]{:S(2)}) collective-permute-start(bf16[96,1024]{1,0:T(8,128)(2,1)} %copy-done.26), channel_id=1, source_target_pairs={{0,3},{1,4},{2,5},{3,6},{4,7},{5,0},{6,1},{7,2},{8,11},{9,12},{10,... | collective-permute-start | bytes 589832 | tf_op jit(solution)/shard_map/ppermute | solution.py:364
  44.6 0.6 collective-permute-start.5
  45.2 0.7 collective-permute-start.6
  45.9 10.3 %collective-permute-done.2.rest_1_ = bf16[96,1024]{1,0:T(8,128)(2,1)S(1)} collective-permute-done((bf16[96,1024]{1,0:T(8,128)(2,1)}, bf16[96,1024]{1,0:T(8,128)(2,1)S(1)}, u32[]{:S(2)}, u32[]{:S(2)}) %collective-permute-start.2) | collective-permute-done | bytes 196640 | tf_op jit(solution)/shard_map/ppermute | solution.py:364
  56.2 0.0 collective-permute-start.7
  56.2 1.0 %collective-permute-done.3.rest_2_ = bf16[96,1024]{1,0:T(8,128)(2,1)S(1)} collective-permute-done((bf16[96,1024]{1,0:T(8,128)(2,1)}, bf16[96,1024]{1,0:T(8,128)(2,1)S(1)}, u32[]{:S(2)}, u32[]{:S(2)}) %collective-permute-start.3) | collective-permute-done | bytes 196640 | tf_op jit(solution)/shard_map/ppermute | solution.py:364
  57.2 2.6 %collective-permute-start.8 = (bf16[96,1024]{1,0:T(8,128)(2,1)}, bf16[96,1024]{1,0:T(8,128)(2,1)}, u32[]{:S(2)}, u32[]{:S(2)}) collective-permute-start(bf16[96,1024]{1,0:T(8,128)(2,1)} %copy-done.22), channel_id=1, source_target_pairs={{0,7},{1,0},{2,1},{3,2},{4,3},{5,4},{6,5},{7,6},{8,15},{9,8},{10,9... | collective-permute-start | bytes 589832 | tf_op jit(solution)/shard_map/ppermute | solution.py:364
  59.8 0.0 all-to-all-done.1
  59.9 0.0 copy-start.1
  59.9 1.9 %copy-done.1 = bf16[1024,1536]{1,0:T(8,128)(2,1)S(1)} copy-done((bf16[1024,1536]{1,0:T(8,128)(2,1)S(1)}, bf16[1024,1536]{1,0:T(8,128)(2,1)}, u32[]{:S(2)}) %copy-start.1) | copy-done | bytes 3145752
  61.7 0.9 %copy-done.10 = bf16[64,1024]{1,0:T(8,128)(2,1)S(1)} copy-done((bf16[64,1024]{1,0:T(8,128)(2,1)S(1)}, bf16[64,1024]{1,0:T(8,128)(2,1)}, u32[]{:S(2)}) %copy-start.10) | copy-done | bytes 131096
  62.7 0.8 copy-done.11
  63.5 4.1 %encode.1 = (bf16[2,1024]{1,0:T(2,128)(2,1)}, bf16[16,2,1024]{2,1,0:T(2,128)(2,1)S(1)}) custom-call(s32[2]{0:T(128)S(1)} %copy-done.18, s32[128,1]{1,0:T(8,128)S(1)} %copy-done.11, bf16[384,1024]{1,0:T(8,128)(2,1)S(1)} %bitcast.17, bf16[64,1024]{1,0:T(8,128)(2,1)S(1)} %copy-done.10, f32[1,1024]{1,0:T(1,128)S(1)} %bitcast.18, f32[1,1024]{1,0:T(1,128)S(1)} %bitcast.19, ...), custom_call_target="tpu_custom_call" | custom-call | flops 637534208 | bytes 6291456 | tf_op jit(solution)/shard_map/encode/pallas_call | solution.py:105
  67.6 0.6 copy-done.12
  68.2 6.5 %all-to-all-start.2 = ((bf16[16,2,1024]{2,1,0:T(2,128)(2,1)}), bf16[16,2,1024]{2,1,0:T(2,128)(2,1)}, u32[]{:S(2)}, u32[]{:S(2)}) async-start(bf16[16,2,1024]{2,1,0:T(2,128)(2,1)} %copy-done.12), calls=%async_computation.2 | async-start | bytes 131072 | tf_op jit(solution)/shard_map/all_to_all | solution.py:384
  74.7 0.1 slice.11
  74.8 0.1 slice.10
  74.8 0.6 gather_fusion
  75.4 0.1 reshape.142.places
  75.5 0.1 reshape.139.late
  75.6 0.0 collective-permute-done.4.rest_3_
  75.6 0.0 copy-start.4
  75.6 0.7 copy-done.4
  76.3 0.0 collective-permute-done.5.rest_4_
  76.3 0.7 copy-done.6
  76.9 0.7 copy-done.8
  77.6 0.0 collective-permute-done.7.rest_6_
  77.6 0.0 collective-permute-done.8.rest_7_
  77.6 1.6 %copy-done.2 = f32[512,1024]{1,0:T(8,128)S(1)} copy-done((f32[512,1024]{1,0:T(8,128)S(1)}, f32[512,1024]{1,0:T(8,128)}, u32[]{:S(2)}) %copy-start.2) | copy-done | bytes 2097176
  79.2 0.9 %copy-done.5 = bf16[96,1024]{1,0:T(8,128)(2,1)S(1)} copy-done((bf16[96,1024]{1,0:T(8,128)(2,1)S(1)}, bf16[96,1024]{1,0:T(8,128)(2,1)}, u32[]{:S(2)}) %copy-start.5) | copy-done | bytes 196632
  80.1 0.9 %copy-done.7 = bf16[96,1024]{1,0:T(8,128)(2,1)S(1)} copy-done((bf16[96,1024]{1,0:T(8,128)(2,1)S(1)}, bf16[96,1024]{1,0:T(8,128)(2,1)}, u32[]{:S(2)}) %copy-start.7) | copy-done | bytes 196632
  81.1 0.9 %copy-done.9 = bf16[96,1024]{1,0:T(8,128)(2,1)S(1)} copy-done((bf16[96,1024]{1,0:T(8,128)(2,1)S(1)}, bf16[96,1024]{1,0:T(8,128)(2,1)}, u32[]{:S(2)}) %copy-start.9) | copy-done | bytes 196632
  82.0 2.7 %early.1 = (f32[512,1024]{1,0:T(8,128)S(1)}, f32[512,128]{1,0:T(8,128)S(1)}) custom-call(s32[1,768]{1,0:T(1,128)S(1)} %reshape.142.places, f32[512,1024]{1,0:T(8,128)S(1)} %copy-done.2, bf16[96,1024]{1,0:T(8,128)(2,1)S(1)} %get-tuple-element.32.rest_0_, bf16[96,1024]{1,0:T(8,128)(2,1)S(1)} %collective-permute-done.2.rest_1_, ...), custom_call_target="tpu_custom_call" | custom-call | flops 805306368 | bytes 4194304 | tf_op jit(solution)/shard_map/early/pallas_call | solution.py:280
  84.8 0.9 reshape.140.embeds
  85.6 2.2 %late.1 = f32[512,1024]{1,0:T(8,128)} custom-call(s32[1,32]{1,0:T(1,128)S(1)} %reshape.139.late, bf16[32,1024]{1,0:T(8,128)(2,1)S(1)} %reshape.140.embeds, f32[512,1024]{1,0:T(8,128)S(1)} %get-tuple-element.40.early, f32[512,128]{1,0:T(8,128)S(1)} %get-tuple-element.41.share), custom_call_target="tpu_custom_call" | custom-call | flops 33554432 | bytes 4194304 | tf_op jit(solution)/shard_map/late/pallas_call | solution.py:295
  (35 shorter events, 0.1 us)
Async XLA Ops:
  0.6 28.7 %copy-start = (bf16[240,1024]{1,0:T(8,128)(2,1)S(1)}, bf16[240,1024]{1,0:T(8,128)(2,1)}, u32[]{:S(2)}) copy-start(bf16[240,1024]{1,0:T(8,128)(2,1)} %param.17) | copy-start | bytes 1474564
  0.6 35.1 %copy-start.19 = (bf16[254,1024]{1,0:T(8,128)(2,1)S(1)}, bf16[254,1024]{1,0:T(8,128)(2,1)}, u32[]{:S(2)}) copy-start(bf16[254,1024]{1,0:T(8,128)(2,1)} %own_rows.1) | copy-start | bytes 1560580
  0.7 30.1 %collective-permute-start.1 = (bf16[254,1024]{1,0:T(8,128)(2,1)}, bf16[254,1024]{1,0:T(8,128)(2,1)S(1)}, u32[]{:S(2)}, u32[]{:S(2)}) collective-permute-start(bf16[254,1024]{1,0:T(8,128)(2,1)} %own_rows.1), channel_id=1, source_target_pairs={{0,8},{1,9},{2,10},{3,11},{4,12},{5,13},{6,14},{7,15},{8,0},{9,1},... | collective-permute-start | bytes 1560584 | tf_op jit(solution)/shard_map/ppermute | solution.py:342
  6.6 29.2 %copy-start.27 = (s32[1,256]{1,0:T(1,128)S(1)}, s32[1,256]{1,0:T(1,128)}, u32[]{:S(2)}) copy-start(s32[1,256]{1,0:T(1,128)} %get-tuple-element.29.own_slot) | copy-start | bytes 3076
  6.6 22.7 %all-to-all-start = ((s32[16,1,74]{2,1,0:T(1,128)}), s32[16,1,74]{2,1,0:T(1,128)S(1)}, u32[]{:S(2)}, u32[]{:S(2)}) async-start(s32[16,1,74]{2,1,0:T(1,128)} %bitcast.27), calls=%async_computation | async-start | bytes 16384 | tf_op jit(solution)/shard_map/all_to_all | solution.py:348
  10.7 17.7 %collective-permute-start = (s32[1,256]{1,0:T(1,128)}, s32[1,256]{1,0:T(1,128)S(1)}, u32[]{:S(2)}, u32[]{:S(2)}) collective-permute-start(s32[1,256]{1,0:T(1,128)} %get-tuple-element.24), channel_id=1, source_target_pairs={{0,8},{1,9},{2,10},{3,11},{4,12},{5,13},{6,14},{7,15},{8,0},{9,1},... | collective-permute-start | bytes 3080 | tf_op jit(solution)/shard_map/ppermute | solution.py:347
  29.4 30.4 %copy-start.3 = (bf16[512,1024]{1,0:T(8,128)(2,1)S(1)}, bf16[512,1024]{1,0:T(8,128)(2,1)}, u32[]{:S(2)}) copy-start(bf16[512,1024]{1,0:T(8,128)(2,1)} %w_out_far.1) | copy-start | bytes 3145732
  29.4 30.4 %copy-start.13 = (f32[1024]{0:T(1024)S(1)}, f32[1024]{0:T(1024)}, u32[]{:S(2)}) copy-start(f32[1024]{0:T(1024)} %param.19) | copy-start | bytes 12292
  29.4 30.4 %copy-start.14 = (f32[1024]{0:T(1024)S(1)}, f32[1024]{0:T(1024)}, u32[]{:S(2)}) copy-start(f32[1024]{0:T(1024)} %param.20) | copy-start | bytes 12292
  29.4 30.4 %copy-start.15 = (f32[1024]{0:T(1024)S(1)}, f32[1024]{0:T(1024)}, u32[]{:S(2)}) copy-start(f32[1024]{0:T(1024)} %param.23) | copy-start | bytes 12292
  29.4 30.4 %copy-start.16 = (f32[1024]{0:T(1024)S(1)}, f32[1024]{0:T(1024)}, u32[]{:S(2)}) copy-start(f32[1024]{0:T(1024)} %param.24) | copy-start | bytes 12292
  29.4 30.4 %copy-start.17 = (f32[1024]{0:T(1024)S(1)}, f32[1024]{0:T(1024)}, u32[]{:S(2)}) copy-start(f32[1024]{0:T(1024)} %param.25) | copy-start | bytes 12292
  29.4 30.4 %copy-start.18 = (s32[2]{0:T(128)S(1)}, s32[2]{0:T(128)}, u32[]{:S(2)}) copy-start(s32[2]{0:T(128)} %lengths.1) | copy-start | bytes 28
  30.8 5.0 %copy-start.20 = (bf16[254,1024]{1,0:T(8,128)(2,1)}, bf16[254,1024]{1,0:T(8,128)(2,1)S(1)}, u32[]{:S(2)}) copy-start(bf16[254,1024]{1,0:T(8,128)(2,1)S(1)} %collective-permute-done.1.partner_rows) | copy-start | bytes 1560580
  30.8 29.0 %all-to-all-start.1 = ((bf16[16,24,1024]{2,1,0:T(8,128)(2,1)}), bf16[16,24,1024]{2,1,0:T(8,128)(2,1)S(1)}, u32[]{:S(2)}, u32[]{:S(2)}) async-start(bf16[16,24,1024]{2,1,0:T(8,128)(2,1)} %bitcast.23), calls=%async_computation.1 | async-start | bytes 1572864 | tf_op jit(solution)/shard_map/all_to_all | solution.py:356
  35.8 1.0 %copy-start.21 = (bf16[254,1024]{1,0:T(8,128)(2,1)S(1)}, bf16[254,1024]{1,0:T(8,128)(2,1)}, u32[]{:S(2)}) copy-start(bf16[254,1024]{1,0:T(8,128)(2,1)} %copy-done.20) | copy-start | bytes 1560580
  38.1 0.7 copy-start.22
  38.8 0.7 copy-start.25
  39.5 0.7 copy-start.26
  40.1 0.7 copy-start.23
  40.1 0.7 copy-start.24
  40.1 16.1 %collective-permute-start.2 = (bf16[96,1024]{1,0:T(8,128)(2,1)}, bf16[96,1024]{1,0:T(8,128)(2,1)S(1)}, u32[]{:S(2)}, u32[]{:S(2)}) collective-permute-start(bf16[96,1024]{1,0:T(8,128)(2,1)} %get-tuple-element.33), channel_id=1, source_target_pairs={{0,1},{1,2},{2,3},{3,4},{4,5},{5,6},{6,7},{7,0},{8,9},{9,10},{10,1... | collective-permute-start | bytes 589832 | tf_op jit(solution)/shard_map/ppermute | solution.py:364
  40.9 16.3 %collective-permute-start.3 = (bf16[96,1024]{1,0:T(8,128)(2,1)}, bf16[96,1024]{1,0:T(8,128)(2,1)S(1)}, u32[]{:S(2)}, u32[]{:S(2)}) collective-permute-start(bf16[96,1024]{1,0:T(8,128)(2,1)} %get-tuple-element.34), channel_id=1, source_target_pairs={{0,2},{1,3},{2,4},{3,5},{4,6},{5,7},{6,0},{7,1},{8,10},{9,11},{10,... | collective-permute-start | bytes 589832 | tf_op jit(solution)/shard_map/ppermute | solution.py:364
  43.0 32.6 %collective-permute-start.4 = (bf16[96,1024]{1,0:T(8,128)(2,1)}, bf16[96,1024]{1,0:T(8,128)(2,1)S(1)}, u32[]{:S(2)}, u32[]{:S(2)}) collective-permute-start(bf16[96,1024]{1,0:T(8,128)(2,1)} %copy-done.26), channel_id=1, source_target_pairs={{0,3},{1,4},{2,5},{3,6},{4,7},{5,0},{6,1},{7,2},{8,11},{9,12},{10,... | collective-permute-start | bytes 589832 | tf_op jit(solution)/shard_map/ppermute | solution.py:364
  44.6 31.7 %collective-permute-start.5 = (bf16[96,1024]{1,0:T(8,128)(2,1)}, bf16[96,1024]{1,0:T(8,128)(2,1)S(1)}, u32[]{:S(2)}, u32[]{:S(2)}) collective-permute-start(bf16[96,1024]{1,0:T(8,128)(2,1)} %copy-done.25), channel_id=1, source_target_pairs={{0,4},{1,5},{2,6},{3,7},{4,0},{5,1},{6,2},{7,3},{8,12},{9,13},{10,... | collective-permute-start | bytes 589832 | tf_op jit(solution)/shard_map/ppermute | solution.py:364
  45.2 31.8 %collective-permute-start.6 = (bf16[96,1024]{1,0:T(8,128)(2,1)}, bf16[96,1024]{1,0:T(8,128)(2,1)S(1)}, u32[]{:S(2)}, u32[]{:S(2)}) collective-permute-start(bf16[96,1024]{1,0:T(8,128)(2,1)} %copy-done.24), channel_id=1, source_target_pairs={{0,5},{1,6},{2,7},{3,0},{4,1},{5,2},{6,3},{7,4},{8,13},{9,14},{10,... | collective-permute-start | bytes 589832 | tf_op jit(solution)/shard_map/ppermute | solution.py:364
  56.2 21.4 %collective-permute-start.7 = (bf16[96,1024]{1,0:T(8,128)(2,1)}, bf16[96,1024]{1,0:T(8,128)(2,1)}, u32[]{:S(2)}, u32[]{:S(2)}) collective-permute-start(bf16[96,1024]{1,0:T(8,128)(2,1)} %copy-done.23), channel_id=1, source_target_pairs={{0,6},{1,7},{2,0},{3,1},{4,2},{5,3},{6,4},{7,5},{8,14},{9,15},{10,... | collective-permute-start | bytes 589832 | tf_op jit(solution)/shard_map/ppermute | solution.py:364
  57.2 20.4 %collective-permute-start.8 = (bf16[96,1024]{1,0:T(8,128)(2,1)}, bf16[96,1024]{1,0:T(8,128)(2,1)}, u32[]{:S(2)}, u32[]{:S(2)}) collective-permute-start(bf16[96,1024]{1,0:T(8,128)(2,1)} %copy-done.22), channel_id=1, source_target_pairs={{0,7},{1,0},{2,1},{3,2},{4,3},{5,4},{6,5},{7,6},{8,15},{9,8},{10,9... | collective-permute-start | bytes 589832 | tf_op jit(solution)/shard_map/ppermute | solution.py:364
  59.9 1.9 %copy-start.1 = (bf16[1024,1536]{1,0:T(8,128)(2,1)S(1)}, bf16[1024,1536]{1,0:T(8,128)(2,1)}, u32[]{:S(2)}) copy-start(bf16[1024,1536]{1,0:T(8,128)(2,1)} %w_qkv_far.1) | copy-start | bytes 9437188
  61.7 0.9 %copy-start.10 = (bf16[64,1024]{1,0:T(8,128)(2,1)S(1)}, bf16[64,1024]{1,0:T(8,128)(2,1)}, u32[]{:S(2)}) copy-start(bf16[64,1024]{1,0:T(8,128)(2,1)} %pos.1) | copy-start | bytes 393220
  62.6 0.8 copy-start.11
  67.6 0.6 copy-start.12
  68.2 16.5 %all-to-all-start.2 = ((bf16[16,2,1024]{2,1,0:T(2,128)(2,1)}), bf16[16,2,1024]{2,1,0:T(2,128)(2,1)}, u32[]{:S(2)}, u32[]{:S(2)}) async-start(bf16[16,2,1024]{2,1,0:T(2,128)(2,1)} %copy-done.12), calls=%async_computation.2 | async-start | bytes 131072 | tf_op jit(solution)/shard_map/all_to_all | solution.py:384
  75.6 0.7 copy-start.4
  76.3 0.7 copy-start.6
  76.9 0.7 copy-start.8
  77.6 1.6 %copy-start.2 = (f32[512,1024]{1,0:T(8,128)S(1)}, f32[512,1024]{1,0:T(8,128)}, u32[]{:S(2)}) copy-start(f32[512,1024]{1,0:T(8,128)} %centroids.1) | copy-start | bytes 6291460
  79.2 0.9 %copy-start.5 = (bf16[96,1024]{1,0:T(8,128)(2,1)S(1)}, bf16[96,1024]{1,0:T(8,128)(2,1)}, u32[]{:S(2)}) copy-start(bf16[96,1024]{1,0:T(8,128)(2,1)} %copy-done.4) | copy-start | bytes 589828
  80.1 0.9 %copy-start.7 = (bf16[96,1024]{1,0:T(8,128)(2,1)S(1)}, bf16[96,1024]{1,0:T(8,128)(2,1)}, u32[]{:S(2)}) copy-start(bf16[96,1024]{1,0:T(8,128)(2,1)} %copy-done.6) | copy-start | bytes 589828
  81.1 0.9 %copy-start.9 = (bf16[96,1024]{1,0:T(8,128)(2,1)S(1)}, bf16[96,1024]{1,0:T(8,128)(2,1)}, u32[]{:S(2)}) copy-start(bf16[96,1024]{1,0:T(8,128)(2,1)} %copy-done.8) | copy-start | bytes 589828

commit v6 on v5

--- a/solution.py
+++ b/solution.py
@@ -118,7 +118,7 @@
             pltpu.VMEM(w_out.shape, w_out.dtype),
             pltpu.SemaphoreType.DMA((2,)),
         ],
-        compiler_params=pltpu.CompilerParams(vmem_limit_bytes=32 * 1024 * 1024),
+        compiler_params=pltpu.CompilerParams(vmem_limit_bytes=60 * 1024 * 1024),
         cost_estimate=pl.CostEstimate(
             flops=2 * macs, bytes_accessed=6 * 1024 * 1024, transcendentals=0
         ),
@@ -138,12 +138,14 @@
     )
 
 
+def rank_bits(count):
+    return max(1, (count - 1).bit_length())
+
+
 def route_kernel(
-    sizes, token_ids, owners, row_slot, plan, token_slot, own_slot, partner_slot
+    sizes, token_ids, owners, row_slot, plan, token_slot, code
 ):
     peers, vocab_rows, token_cap, row_cap, pooled = sizes
-    half = peers // 2
-    me = lax.axis_index("dp")
     ids = jnp.concatenate([token_ids[p : p + 1, :] for p in range(token_ids.shape[0])], axis=1)
     tokens, rows = ids.shape[1], owners.shape[1]
     count = tokens + rows
@@ -160,10 +162,11 @@
     rank_row = jnp.sum(jnp.where(same & (at < by), 1, 0), axis=0, keepdims=True)
     rank_col = jnp.sum(jnp.where(same & (by < at), 1, 0), axis=1, keepdims=True)
 
+    code[...] = owners[...] * 2 ** rank_bits(rows) + rank_row[:, tokens:]
     goal = jnp.concatenate([holder, owners[...]], axis=1)
     peer = lax.broadcasted_iota(jnp.int32, (peers, count), 0)
     left = jnp.where(peer == goal, values + 1, 0).astype(jnp.float32)
-    columns = plan.shape[1]
+    columns = token_cap + row_cap + pooled
     column = lax.broadcasted_iota(jnp.int32, (count, columns), 1)
     entry = lax.broadcasted_iota(jnp.int32, (count, 1), 0)
     first = jnp.where(entry < tokens, rank_col, rank_col + token_cap)
@@ -173,18 +176,9 @@
     filled = jnp.dot(
         left, right, preferred_element_type=jnp.float32, precision=lax.Precision.HIGHEST
     )
-    plan[...] = filled.astype(jnp.int32) - 1
+    plan[:, :rows] = jnp.broadcast_to(code[...], (peers, rows))
+    plan[:, rows:] = filled.astype(jnp.int32) - 1
     token_slot[...] = down[:tokens] * token_cap + rank_col[:tokens]
-
-    def half_slot(device):
-        first = jnp.where(device < half, 0, half)
-        inside = (owners[...] >= first) & (owners[...] < first + half)
-        step = owners[...] - device
-        step = jnp.where(step < 0, step + half, step)
-        return jnp.where(inside, step * row_cap + rank_row[:, tokens:], -1)
-
-    own_slot[...] = half_slot(me)
-    partner_slot[...] = half_slot(jnp.where(me < half, me + half, me - half))
 
 
 def route(token_ids, owners, row_slot, sizes):
@@ -195,22 +189,31 @@
     return pl.pallas_call(
         functools.partial(route_kernel, sizes),
         out_shape=[
-            ints(peers, token_cap + row_cap + pooled),
+            ints(peers, rows + token_cap + row_cap + pooled),
             ints(passes * seq_len, 1),
-            ints(1, rows),
             ints(1, rows),
         ],
         in_specs=[pl.BlockSpec(memory_space=pltpu.VMEM)] * 3,
-        out_specs=[pl.BlockSpec(memory_space=pltpu.VMEM)] * 4,
+        out_specs=[pl.BlockSpec(memory_space=pltpu.VMEM)] * 3,
         name="route",
     )(token_ids, owners, row_slot)
 
 
-def pack_kernel(row_cap, own_slot, partner_slot, own_rows, partner_rows, *outs):
+def pack_kernel(half, row_cap, count, picks, codes_a, codes_b, rows_a, rows_b, *outs):
+    me = lax.axis_index("dp")
     slot_count = len(outs) * row_cap
-    for source, (slot, rows) in enumerate(((own_slot, own_rows), (partner_slot, partner_rows))):
+    for source, (codes, rows) in enumerate(((codes_a, rows_a), (codes_b, rows_b))):
+        if picks is None:
+            code = codes[...]
+        else:
+            code = codes[pl.ds(me ^ picks[source], 1), :count]
+        bits = rank_bits(count)
+        owner, rank = code >> bits, code & (2**bits - 1)
+        fits = ((owner ^ me) & (1 | half)) == 0
+        chip = ((owner ^ me) & (half - 1)) >> 1
+        slot = jnp.where(fits, chip * row_cap + rank, -1)[:, : rows.shape[0]]
         spot = lax.broadcasted_iota(jnp.int32, (slot_count, rows.shape[0]), 0)
-        table = jnp.where(slot[:, : rows.shape[0]] == spot, 1.0, 0.0).astype(jnp.bfloat16)
+        table = jnp.where(slot == spot, 1.0, 0.0).astype(jnp.bfloat16)
         packed = jnp.dot(table, rows[...], preferred_element_type=jnp.float32)
         packed = packed.astype(jnp.bfloat16)
         for step, out in enumerate(outs):
@@ -219,21 +222,22 @@
             ]
 
 
-def pack_rows(own_slot, partner_slot, own_rows, partner_rows, steps, row_cap):
-    width = own_rows.shape[1]
+def pack_rows(codes_a, codes_b, rows_a, rows_b, half, row_cap, count, picks=None):
+    width = rows_a.shape[1]
+    steps = half // 2
     return pl.pallas_call(
-        functools.partial(pack_kernel, row_cap),
+        functools.partial(pack_kernel, half, row_cap, count, picks),
         out_shape=[jax.ShapeDtypeStruct((2 * row_cap, width), jnp.bfloat16)] * steps,
         in_specs=[pl.BlockSpec(memory_space=pltpu.VMEM)] * 4,
         out_specs=[pl.BlockSpec(memory_space=pltpu.VMEM)] * steps,
-        compiler_params=pltpu.CompilerParams(vmem_limit_bytes=32 * 1024 * 1024),
+        compiler_params=pltpu.CompilerParams(vmem_limit_bytes=60 * 1024 * 1024),
         cost_estimate=pl.CostEstimate(
-            flops=4 * steps * row_cap * width * own_rows.shape[0],
-            bytes_accessed=4 * width * (own_rows.shape[0] + steps * row_cap),
+            flops=4 * steps * row_cap * width * rows_a.shape[0],
+            bytes_accessed=4 * width * (rows_a.shape[0] + steps * row_cap),
             transcendentals=0,
         ),
         name="pack",
-    )(own_slot, partner_slot, own_rows, partner_rows)
+    )(codes_a, codes_b, rows_a, rows_b)
 
 
 def onehot(where_to, count):
@@ -261,7 +265,14 @@
     share[...] = jnp.broadcast_to(scale, share.shape)
 
 
-def late_kernel(late, embeds, early, share, out):
+def late_kernel(late, spread, early, share, out, embeds):
+    passes = spread.shape[1]
+
+    @pl.when(pl.program_id(0) == 0)
+    def _():
+        for peer in range(spread.shape[0]):
+            embeds[peer * passes : (peer + 1) * passes, :] = spread[peer]
+
     hot = onehot(late, out.shape[0]).astype(jnp.bfloat16)
     sums = jnp.dot(hot, embeds[...], preferred_element_type=jnp.float32)
     out[...] = early[...] + sums * share[:, :1]
@@ -276,7 +287,7 @@
     thin = pl.BlockSpec((block, 128), lambda i: (i, 0))
     row_total = sum(piece.shape[0] for piece in pieces)
     full = jax.ShapeDtypeStruct(centroids.shape, jnp.float32)
-    params = pltpu.CompilerParams(vmem_limit_bytes=32 * 1024 * 1024)
+    params = pltpu.CompilerParams(vmem_limit_bytes=60 * 1024 * 1024)
     early, share = pl.pallas_call(
         early_kernel,
         grid=grid,
@@ -296,8 +307,9 @@
         late_kernel,
         grid=grid,
         out_shape=full,
-        in_specs=[whole(late), whole(embeds), part, thin],
+        in_specs=[whole(late), pl.BlockSpec(embeds.shape, lambda i: (0, 0, 0)), part, thin],
         out_specs=part,
+        scratch_shapes=[pltpu.VMEM((late.shape[1], width), jnp.bfloat16)],
         compiler_params=params,
         cost_estimate=pl.CostEstimate(
             flops=2 * centre_count * width * late.shape[1],
@@ -327,8 +339,6 @@
 ):
     peer_count = lax.axis_size("dp")
     half = peer_count // 2
-    me = lax.axis_index("dp")
-    base = me // half * half
     width = word_table.shape[1]
     vocab_rows = word_table.shape[0]
     passes, seq_len = token_ids.shape
@@ -338,32 +348,40 @@
     token_cap = max(2, 3 * token_count // peer_count)
     row_cap = max(2, 3 * row_count // peer_count)
 
-    across = [(i, (i + half) % peer_count) for i in range(peer_count)]
+    across = [(i, i ^ half) for i in range(peer_count)]
+    beside = [(i, i ^ 1) for i in range(peer_count)]
+
+    def hand_on(blocks):
+        got = [blocks[0]]
+        for step in range(1, len(blocks)):
+            moves = [(i, i ^ (2 * step)) for i in range(peer_count)]
+            got.append(lax.ppermute(blocks[step], "dp", moves))
+        return got
+
     partner_rows = lax.ppermute(stored_rows, "dp", across)
+    sibling_rows = lax.ppermute(stored_rows, "dp", beside)
     sizes = (peer_count, vocab_rows, token_cap, row_cap, row_count - store_count)
-    plan, token_slot, own_slot, partner_slot = route(
-        token_ids, row_owner.reshape(1, row_count), row_slot[None], sizes
-    )
-    partner_slot = lax.ppermute(partner_slot, "dp", across)
+    plan, token_slot, code = route(token_ids, row_owner.reshape(1, row_count), row_slot[None], sizes)
+    sibling_code = lax.ppermute(code, "dp", beside)
     plan = lax.all_to_all(plan, "dp", split_axis=0, concat_axis=0, tiled=True)
-    plan, partner_slot = lax.optimization_barrier((plan, partner_slot))
+    blocks = pack_rows(code, sibling_code, stored_rows, sibling_rows, half, row_cap, row_count)
+    own_half = hand_on(blocks)
+    codes, plan = plan[:, :row_count], plan[:, row_count:]
     wanted = plan[:, :token_cap].reshape(peer_count * token_cap)
     chosen = wanted[:, None] == jnp.arange(vocab_rows, dtype=jnp.int32)[None, :]
     found = jnp.dot(
         chosen.astype(jnp.bfloat16), word_table, preferred_element_type=jnp.float32
     ).astype(jnp.bfloat16)
-    found, partner_rows = lax.optimization_barrier((found, partner_rows))
+    found, partner_rows, own_half = lax.optimization_barrier((found, partner_rows, own_half))
     fetched = lax.all_to_all(
         found.reshape(peer_count, token_cap, width), "dp", split_axis=0, concat_axis=0, tiled=True
     ).reshape(peer_count * token_cap, width)
 
-    blocks = pack_rows(own_slot, partner_slot, stored_rows, partner_rows, half, row_cap)
-    got_rows = [blocks[0]]
-    for step in range(1, half):
-        moves = [(i, i // half * half + (i + step) % half) for i in range(peer_count)]
-        got_rows.append(lax.ppermute(blocks[step], "dp", moves))
-    sources = base + (me - jnp.arange(half, dtype=jnp.int32)) % half
-    sources = jnp.stack([sources, (sources + half) % peer_count], axis=1).reshape(peer_count)
+    far_rows = lax.ppermute(partner_rows, "dp", beside)
+    picks = (half, half ^ 1)
+    blocks = pack_rows(codes, codes, partner_rows, far_rows, half, row_cap, row_count, picks)
+    other_half = hand_on(blocks)
+    sources = lax.axis_index("dp") ^ jnp.arange(peer_count, dtype=jnp.int32)
     got_places = plan[:, token_cap : token_cap + row_cap][sources].reshape(1, peer_count * row_cap)
     late_places = plan[:, token_cap + row_cap :].reshape(1, -1)
 
@@ -383,8 +401,10 @@
     )
     all_embeds = lax.all_to_all(
         spread, "dp", split_axis=0, concat_axis=0, tiled=True
-    ).reshape(peer_count * passes, width)
-    new_centroids = update(got_places, late_places, all_embeds, centroids, got_rows)
+    )
+    new_centroids = update(
+        got_places, late_places, all_embeds, centroids, own_half + other_half
+    )
     return (passage_embed, new_centroids)
 
 

time: 88.5 us -> 96 us (1.085)
  waiting for transfers between devices: 27.1 us -> 36.9 us
  Pallas kernels: 12.2 us -> 21.8 us
  local copies, waits for them, and re-layouts: 16.1 us -> 8.55 us
  starting transfers between devices: 30.2 us -> 26 us
    ppermute x8 -> x9, waiting for transfers between devices: 26.2 us -> 8.71 us  [the longest x6 7.74 us: hand_on(): got.append(lax.ppermute(blocks[step], 'dp', moves))]
    all_to_all x1, waiting for transfers between devices: 0.89 us -> 17.8 us  [shards(): plan = lax.all_to_all(plan, 'dp', split_axis=0, concat_axis=0, tiled=True)]
    all_to_all x1, waiting for transfers between devices: 0.01 us -> 10.4 us  [shards(): lax.all_to_all(found.reshape(peer_count, token_cap, width), 'dp', split_a...]
    unnamed x56 -> x27, local copies, waits for them, and re-layouts: 14.1 us -> 4.44 us
    pallas_call x1 -> x2, Pallas kernels: 1.28 us -> 4.94 us  [pack_rows(): pl.pallas_call(functools.partial(pack_kernel, half, row_cap, count, picks...]
    ppermute x8 -> x9, starting transfers between devices: 10.7 us -> 8.31 us  [the longest x6 6.98 us: hand_on(): got.append(lax.ppermute(blocks[step], 'dp', moves))]
    pallas_call x1, Pallas kernels: 2.74 us -> 5.05 us  [update(): pl.pallas_call(early_kernel, grid=grid, out_shape=[full, jax.ShapeDtypeSt...]
    pallas_call x1, Pallas kernels: 2.22 us -> 4.16 us  [update(): pl.pallas_call(late_kernel, grid=grid, out_shape=full, in_specs=[whole(la...]
  transfers between devices with their start and end apart: 12 -> 13, of which waited for: 4 -> 6; matrix products, arithmetic and copies ran while one was open for 3% -> 6% of each run, Pallas kernels for 11% -> 19%
where the time goes in v6:
time: 96 us; the launch traced here: 95.4 us
  waiting for transfers between devices  36.9 us (38%)
  starting transfers between devices  26 us (27%)
  Pallas kernels  21.8 us (23%)
  local copies, waits for them, and re-layouts  8.55 us (9%)
  matrix products  1.29 us (1%)
    all_to_all x1, waiting for transfers between devices, shards(): plan = lax.all_to_all(plan, 'dp', split_axis=0, concat_axis=0, tiled=True)  17.8 us
    all_to_all x1, waiting for transfers between devices, shards(): lax.all_to_all(found.reshape(peer_count, token_cap, width), 'dp', split_a...  10.4 us
    ppermute x6, waiting for transfers between devices, hand_on(): got.append(lax.ppermute(blocks[step], 'dp', moves))  7.74 us
    ppermute x6, starting transfers between devices, hand_on(): got.append(lax.ppermute(blocks[step], 'dp', moves))  6.98 us
    pallas_call x1, Pallas kernels, encode(): pl.pallas_call(encode_kernel, out_shape=[jax.ShapeDtypeStruct((passes, wi...  5.83 us
    all_to_all x1, starting transfers between devices, shards(): lax.all_to_all(spread, 'dp', split_axis=0, concat_axis=0, tiled=True)  5.19 us
    pallas_call x1, Pallas kernels, update(): pl.pallas_call(early_kernel, grid=grid, out_shape=[full, jax.ShapeDtypeSt...  5.05 us
    pallas_call x2, Pallas kernels, pack_rows(): pl.pallas_call(functools.partial(pack_kernel, half, row_cap, count, picks...  4.94 us
  transfers between devices with their start and end apart: 13, of which 6 were waited for; matrix products, arithmetic and copies ran while one was open for 6% of the time, Pallas kernels for 19%

profile of v6, /device:TPU:0, one launch (start us, length us, event | category | flops | bytes accessed | tf_op | source)
XLA Modules:
  0.0 95.4 jit_solution(10740693385583339174)
XLA Ops:
  0.6 0.0 copy-start
  0.6 0.5 collective-permute-start.2
  1.2 3.7 %collective-permute-start = (bf16[254,1024]{1,0:T(8,128)(2,1)}, bf16[254,1024]{1,0:T(8,128)(2,1)S(1)}, u32[]{:S(2)}, u32[]{:S(2)}) collective-permute-start(bf16[254,1024]{1,0:T(8,128)(2,1)} %rows_a.1), channel_id=1, source_target_pairs={{0,8},{1,9},{2,10},{3,11},{4,12},{5,13},{6,14},{7,15},{8,0},{9,1},... | collective-permute-start | bytes 1560584 | tf_op jit(solution)/shard_map/ppermute | solution.py:361
  4.8 1.8 %route.1 = (s32[16,330]{1,0:T(8,128)}, s32[128,1]{1,0:T(8,128)}, s32[1,256]{1,0:T(1,128)}) custom-call(s32[2,64]{1,0:T(2,128)} %token_ids.1, s32[1,256]{1,0:T(1,128)} %bitcast.27, s32[1,256]{1,0:T(1,128)} %bitcast.28), custom_call_target="tpu_custom_call" | custom-call | tf_op jit(solution)/shard_map/route/pallas_call | solution.py:189
  6.7 1.4 %copy.17 = s32[16,1,330]{2,1,0:T(1,128)} copy(s32[16,1,330]{2,0,1:T(8,128)} %bitcast.21) | data formatting | bytes 42240 | tf_op jit(solution)/shard_map/all_to_all | solution.py:366
  8.0 3.9 %all-to-all-start = ((s32[16,1,330]{2,1,0:T(1,128)}), s32[16,1,330]{2,1,0:T(1,128)S(1)}, u32[]{:S(2)}, u32[]{:S(2)}) async-start(s32[16,1,330]{2,1,0:T(1,128)} %copy.17), calls=%async_computation | async-start | bytes 49152 | tf_op jit(solution)/shard_map/all_to_all | solution.py:366
  12.0 0.4 collective-permute-start.1
  12.4 17.8 %all-to-all-done = s32[16,1,330]{2,1,0:T(1,128)S(1)} async-done(((s32[16,1,330]{2,1,0:T(1,128)}), s32[16,1,330]{2,1,0:T(1,128)S(1)}, u32[]{:S(2)}, u32[]{:S(2)}) %all-to-all-start) | async-done | bytes 21152 | tf_op jit(solution)/shard_map/all_to_all | solution.py:366
  30.2 0.1 eq.15
  30.3 0.0 collective-permute-done.1.codes_b
  30.3 0.0 copy-start.12
  30.3 0.0 collective-permute-done.2.rows_b
  30.4 0.6 copy-done.12
  30.9 0.8 copy-done.3
  31.7 2.5 %pack.2 = (bf16[96,1024]{1,0:T(8,128)(2,1)}, bf16[96,1024]{1,0:T(8,128)(2,1)}, bf16[96,1024]{1,0:T(8,128)(2,1)}, bf16[96,1024]{1,0:T(8,128)(2,1)}) custom-call(s32[1,256]{1,0:T(1,128)} %get-tuple-element.25.codes_a, s32[1,256]{1,0:T(1,128)} %copy-done.12, bf16[254,1024]{1,0:T(8,128)(2,1)} %rows_a.1, bf16[254,1024]{1,0:T(8,128)(2,1)} %copy-done.3), custom_call_target="tpu_custom_call" | custom-call | flops 199753728 | bytes 1826816 | tf_op jit(solution)/shard_map/pack/pallas_call | solution.py:228
  34.2 0.6 collective-permute-start.3
  34.7 0.8 collective-permute-start.4
  35.5 2.1 %collective-permute-start.5 = (bf16[96,1024]{1,0:T(8,128)(2,1)}, bf16[96,1024]{1,0:T(8,128)(2,1)S(1)}, u32[]{:S(2)}, u32[]{:S(2)}) collective-permute-start(bf16[96,1024]{1,0:T(8,128)(2,1)} %get-tuple-element.29), channel_id=1, source_target_pairs={{0,6},{1,7},{2,4},{3,5},{4,2},{5,3},{6,0},{7,1},{8,14},{9,15},{10,... | collective-permute-start | bytes 589832 | tf_op jit(solution)/shard_map/ppermute | solution.py:358
  37.7 0.0 copy-done
  37.7 1.3 %convolution_convert_fusion = bf16[384,1024]{1,0:T(8,128)(2,1)} fusion(bf16[240,1024]{1,0:T(8,128)(2,1)S(1)} %copy-done, s32[384]{0:T(512)S(1)} %eq.15), kind=kOutput, calls=%fused_computation.1 | convolution fusion | flops 189229056 | bytes 1279488 | tf_op jit(solution)/shard_map/dot_general | solution.py:372
  39.0 0.0 collective-permute-done.rows_a
  39.0 0.0 copy-start.2
  39.0 2.3 %collective-permute-done.3.rest_1_ = bf16[96,1024]{1,0:T(8,128)(2,1)S(1)} collective-permute-done((bf16[96,1024]{1,0:T(8,128)(2,1)}, bf16[96,1024]{1,0:T(8,128)(2,1)S(1)}, u32[]{:S(2)}, u32[]{:S(2)}) %collective-permute-start.3) | collective-permute-done | bytes 196640 | tf_op jit(solution)/shard_map/ppermute | solution.py:358
  41.3 0.0 copy-start.6
  41.3 1.4 %collective-permute-done.4.rest_2_ = bf16[96,1024]{1,0:T(8,128)(2,1)S(1)} collective-permute-done((bf16[96,1024]{1,0:T(8,128)(2,1)}, bf16[96,1024]{1,0:T(8,128)(2,1)S(1)}, u32[]{:S(2)}, u32[]{:S(2)}) %collective-permute-start.4) | collective-permute-done | bytes 196640 | tf_op jit(solution)/shard_map/ppermute | solution.py:358
  42.7 0.0 copy-start.7
  42.8 3.9 %collective-permute-done.5.rest_3_ = bf16[96,1024]{1,0:T(8,128)(2,1)S(1)} collective-permute-done((bf16[96,1024]{1,0:T(8,128)(2,1)}, bf16[96,1024]{1,0:T(8,128)(2,1)S(1)}, u32[]{:S(2)}, u32[]{:S(2)}) %collective-permute-start.5) | collective-permute-done | bytes 196640 | tf_op jit(solution)/shard_map/ppermute | solution.py:358
  46.7 0.0 copy-start.8
  46.7 4.9 %all-to-all-start.1 = ((bf16[16,24,1024]{2,1,0:T(8,128)(2,1)}), bf16[16,24,1024]{2,1,0:T(8,128)(2,1)S(1)}, u32[]{:S(2)}, u32[]{:S(2)}) async-start(bf16[16,24,1024]{2,1,0:T(8,128)(2,1)} %bitcast.3), calls=%async_computation.1 | async-start | bytes 1572864 | tf_op jit(solution)/shard_map/all_to_all | solution.py:376
  51.6 0.4 collective-permute-start.6
  52.0 0.6 slice.25.codes_a.codes_b
  52.6 1.0 %collective-permute-done.6.rows_b = bf16[254,1024]{1,0:T(8,128)(2,1)S(1)} collective-permute-done((bf16[254,1024]{1,0:T(8,128)(2,1)S(1)}, bf16[254,1024]{1,0:T(8,128)(2,1)S(1)}, u32[]{:S(2)}, u32[]{:S(2)}) %collective-permute-start.6) | collective-permute-done | bytes 520224 | tf_op jit(solution)/shard_map/ppermute | solution.py:380
  53.6 0.0 copy-done.2
  53.6 0.0 copy-start.4
  53.6 0.8 copy-done.4
  54.4 2.5 %pack.3 = (bf16[96,1024]{1,0:T(8,128)(2,1)}, bf16[96,1024]{1,0:T(8,128)(2,1)}, bf16[96,1024]{1,0:T(8,128)(2,1)}, bf16[96,1024]{1,0:T(8,128)(2,1)}) custom-call(s32[16,256]{1,0:T(8,128)} %slice.25.codes_a.codes_b, s32[16,256]{1,0:T(8,128)} %slice.25.codes_a.codes_b, bf16[254,1024]{1,0:T(8,128)(2,1)} %copy-done.2, bf16[254,1024]{1,0:T(8,128)(2,1)} %copy-done.4), custom_call_target="tpu_custom_call" | custom-call | flops 199753728 | bytes 1826816 | tf_op jit(solution)/shard_map/pack/pallas_call | solution.py:228
  56.9 1.9 %collective-permute-start.7 = (bf16[96,1024]{1,0:T(8,128)(2,1)}, bf16[96,1024]{1,0:T(8,128)(2,1)S(1)}, u32[]{:S(2)}, u32[]{:S(2)}) collective-permute-start(bf16[96,1024]{1,0:T(8,128)(2,1)} %get-tuple-element.39), channel_id=1, source_target_pairs={{0,2},{1,3},{2,0},{3,1},{4,6},{5,7},{6,4},{7,5},{8,10},{9,11},{10,... | collective-permute-start | bytes 589832 | tf_op jit(solution)/shard_map/ppermute | solution.py:358
  58.7 1.5 %collective-permute-start.8 = (bf16[96,1024]{1,0:T(8,128)(2,1)}, bf16[96,1024]{1,0:T(8,128)(2,1)S(1)}, u32[]{:S(2)}, u32[]{:S(2)}) collective-permute-start(bf16[96,1024]{1,0:T(8,128)(2,1)} %get-tuple-element.40), channel_id=1, source_target_pairs={{0,4},{1,5},{2,6},{3,7},{4,0},{5,1},{6,2},{7,3},{8,12},{9,13},{10,... | collective-permute-start | bytes 589832 | tf_op jit(solution)/shard_map/ppermute | solution.py:358
  60.2 0.2 collective-permute-start.9
  60.4 10.4 %all-to-all-done.1 = bf16[16,24,1024]{2,1,0:T(8,128)(2,1)S(1)} async-done(((bf16[16,24,1024]{2,1,0:T(8,128)(2,1)}), bf16[16,24,1024]{2,1,0:T(8,128)(2,1)S(1)}, u32[]{:S(2)}, u32[]{:S(2)}) %all-to-all-start.1) | async-done | bytes 786464 | tf_op jit(solution)/shard_map/all_to_all | solution.py:376
  70.7 0.9 copy-done.1
  71.6 5.8 %encode.1 = (bf16[2,1024]{1,0:T(2,128)(2,1)}, bf16[16,2,1024]{2,1,0:T(2,128)(2,1)}) custom-call(s32[2]{0:T(128)} %lengths.1, s32[128,1]{1,0:T(8,128)} %get-tuple-element.23.slots, bf16[384,1024]{1,0:T(8,128)(2,1)} %bitcast.16, bf16[64,1024]{1,0:T(8,128)(2,1)} %pos.1, f32[1,1024]{1,0:T(1,128)} %bitcast.22, f32[1,1024]{1,0:T(1,128)} %bitcast.23, ...), custom_call_target="tpu_custom_call" | custom-call | flops 637534208 | bytes 6291456 | tf_op jit(solution)/shard_map/encode/pallas_call | solution.py:105
  77.5 0.0 copy-done.6
  77.5 0.0 copy-done.7
  77.5 0.0 copy-done.8
  77.5 5.2 %all-to-all-start.2 = ((bf16[16,2,1024]{2,1,0:T(2,128)(2,1)}), bf16[16,2,1024]{2,1,0:T(2,128)(2,1)S(1)}, u32[]{:S(2)}, u32[]{:S(2)}) async-start(bf16[16,2,1024]{2,1,0:T(2,128)(2,1)} %get-tuple-element.32), calls=%async_computation.2 | async-start | bytes 131072 | tf_op jit(solution)/shard_map/all_to_all | solution.py:402
  82.7 0.1 slice.24
  82.8 0.1 slice.23
  82.9 0.6 gather_fusion
  83.4 0.7 reshape.42.places
  84.1 0.7 reshape.41.late
  84.8 0.0 collective-permute-done.7.rest_5_
  84.8 0.0 collective-permute-done.8.rest_6_
  84.8 0.0 copy-start.10
  84.8 0.0 collective-permute-done.9.rest_7_
  84.8 0.0 copy-start.11
  84.8 0.6 copy-done.9
  85.4 0.1 copy-done.10
  85.5 0.1 copy-done.11
  85.6 5.0 %early.1 = (f32[512,1024]{1,0:T(8,128)}, f32[512,128]{1,0:T(8,128)}) custom-call(s32[1,768]{1,0:T(1,128)} %reshape.42.places, f32[512,1024]{1,0:T(8,128)} %centroids.1, bf16[96,1024]{1,0:T(8,128)(2,1)} %get-tuple-element.33.rest_0_, bf16[96,1024]{1,0:T(8,128)(2,1)} %copy-done.6, bf16[96,1024]{1,0:T(8,128)(2,1)} %copy-done.7, bf16[96,1024]{1,0:T(8,128)(2,1)} %copy-done.8, ...), custom_call_target="tpu_custom_call" | custom-call | flops 805306368 | bytes 4194304 | tf_op jit(solution)/shard_map/early/pallas_call | solution.py:291
  90.6 0.0 all-to-all-done.2.spread
  90.6 0.0 copy-start.5
  90.6 0.6 copy-done.5
  91.2 4.2 %late.1 = f32[512,1024]{1,0:T(8,128)} custom-call(s32[1,32]{1,0:T(1,128)} %reshape.41.late, bf16[16,2,1024]{2,1,0:T(2,128)(2,1)} %copy-done.5, f32[512,1024]{1,0:T(8,128)} %get-tuple-element.42.early, f32[512,128]{1,0:T(8,128)} %get-tuple-element.43.share), custom_call_target="tpu_custom_call" | custom-call | flops 33554432 | bytes 4194304 | tf_op jit(solution)/shard_map/late/pallas_call | solution.py:306
  (7 shorter events, 0.0 us)
Async XLA Ops:
  0.6 37.0 %copy-start = (bf16[240,1024]{1,0:T(8,128)(2,1)S(1)}, bf16[240,1024]{1,0:T(8,128)(2,1)}, u32[]{:S(2)}) copy-start(bf16[240,1024]{1,0:T(8,128)(2,1)} %param.17) | copy-start | bytes 1474564
  0.6 29.7 %collective-permute-start.2 = (bf16[254,1024]{1,0:T(8,128)(2,1)}, bf16[254,1024]{1,0:T(8,128)(2,1)S(1)}, u32[]{:S(2)}, u32[]{:S(2)}) collective-permute-start(bf16[254,1024]{1,0:T(8,128)(2,1)} %rows_a.1), channel_id=1, source_target_pairs={{0,1},{1,0},{2,3},{3,2},{4,5},{5,4},{6,7},{7,6},{8,9},{9,8},{10,11... | collective-permute-start | bytes 1560584 | tf_op jit(solution)/shard_map/ppermute | solution.py:362
  1.2 37.8 %collective-permute-start = (bf16[254,1024]{1,0:T(8,128)(2,1)}, bf16[254,1024]{1,0:T(8,128)(2,1)S(1)}, u32[]{:S(2)}, u32[]{:S(2)}) collective-permute-start(bf16[254,1024]{1,0:T(8,128)(2,1)} %rows_a.1), channel_id=1, source_target_pairs={{0,8},{1,9},{2,10},{3,11},{4,12},{5,13},{6,14},{7,15},{8,0},{9,1},... | collective-permute-start | bytes 1560584 | tf_op jit(solution)/shard_map/ppermute | solution.py:361
  8.0 22.2 %all-to-all-start = ((s32[16,1,330]{2,1,0:T(1,128)}), s32[16,1,330]{2,1,0:T(1,128)S(1)}, u32[]{:S(2)}, u32[]{:S(2)}) async-start(s32[16,1,330]{2,1,0:T(1,128)} %copy.17), calls=%async_computation | async-start | bytes 49152 | tf_op jit(solution)/shard_map/all_to_all | solution.py:366
  12.0 18.4 %collective-permute-start.1 = (s32[1,256]{1,0:T(1,128)}, s32[1,256]{1,0:T(1,128)S(1)}, u32[]{:S(2)}, u32[]{:S(2)}) collective-permute-start(s32[1,256]{1,0:T(1,128)} %get-tuple-element.25.codes_a), channel_id=1, source_target_pairs={{0,1},{1,0},{2,3},{3,2},{4,5},{5,4},{6,7},{7,6},{8,9},{9,8},{10,11... | collective-permute-start | bytes 3080 | tf_op jit(solution)/shard_map/ppermute | solution.py:365
  30.3 0.6 copy-start.12
  30.9 0.8 copy-start.3
  34.2 7.1 %collective-permute-start.3 = (bf16[96,1024]{1,0:T(8,128)(2,1)}, bf16[96,1024]{1,0:T(8,128)(2,1)S(1)}, u32[]{:S(2)}, u32[]{:S(2)}) collective-permute-start(bf16[96,1024]{1,0:T(8,128)(2,1)} %get-tuple-element.27), channel_id=1, source_target_pairs={{0,2},{1,3},{2,0},{3,1},{4,6},{5,7},{6,4},{7,5},{8,10},{9,11},{10,... | collective-permute-start | bytes 589832 | tf_op jit(solution)/shard_map/ppermute | solution.py:358
  34.7 8.0 %collective-permute-start.4 = (bf16[96,1024]{1,0:T(8,128)(2,1)}, bf16[96,1024]{1,0:T(8,128)(2,1)S(1)}, u32[]{:S(2)}, u32[]{:S(2)}) collective-permute-start(bf16[96,1024]{1,0:T(8,128)(2,1)} %get-tuple-element.28), channel_id=1, source_target_pairs={{0,4},{1,5},{2,6},{3,7},{4,0},{5,1},{6,2},{7,3},{8,12},{9,13},{10,... | collective-permute-start | bytes 589832 | tf_op jit(solution)/shard_map/ppermute | solution.py:358
  35.5 11.2 %collective-permute-start.5 = (bf16[96,1024]{1,0:T(8,128)(2,1)}, bf16[96,1024]{1,0:T(8,128)(2,1)S(1)}, u32[]{:S(2)}, u32[]{:S(2)}) collective-permute-start(bf16[96,1024]{1,0:T(8,128)(2,1)} %get-tuple-element.29), channel_id=1, source_target_pairs={{0,6},{1,7},{2,4},{3,5},{4,2},{5,3},{6,0},{7,1},{8,14},{9,15},{10,... | collective-permute-start | bytes 589832 | tf_op jit(solution)/shard_map/ppermute | solution.py:358
  39.0 14.6 %copy-start.2 = (bf16[254,1024]{1,0:T(8,128)(2,1)}, bf16[254,1024]{1,0:T(8,128)(2,1)S(1)}, u32[]{:S(2)}) copy-start(bf16[254,1024]{1,0:T(8,128)(2,1)S(1)} %collective-permute-done.rows_a) | copy-start | bytes 1560580
  41.3 36.2 %copy-start.6 = (bf16[96,1024]{1,0:T(8,128)(2,1)}, bf16[96,1024]{1,0:T(8,128)(2,1)S(1)}, u32[]{:S(2)}) copy-start(bf16[96,1024]{1,0:T(8,128)(2,1)S(1)} %collective-permute-done.3.rest_1_) | copy-start | bytes 589828
  42.7 34.7 %copy-start.7 = (bf16[96,1024]{1,0:T(8,128)(2,1)}, bf16[96,1024]{1,0:T(8,128)(2,1)S(1)}, u32[]{:S(2)}) copy-start(bf16[96,1024]{1,0:T(8,128)(2,1)S(1)} %collective-permute-done.4.rest_2_) | copy-start | bytes 589828
  46.7 30.8 %copy-start.8 = (bf16[96,1024]{1,0:T(8,128)(2,1)}, bf16[96,1024]{1,0:T(8,128)(2,1)S(1)}, u32[]{:S(2)}) copy-start(bf16[96,1024]{1,0:T(8,128)(2,1)S(1)} %collective-permute-done.5.rest_3_) | copy-start | bytes 589828
  46.7 24.0 %all-to-all-start.1 = ((bf16[16,24,1024]{2,1,0:T(8,128)(2,1)}), bf16[16,24,1024]{2,1,0:T(8,128)(2,1)S(1)}, u32[]{:S(2)}, u32[]{:S(2)}) async-start(bf16[16,24,1024]{2,1,0:T(8,128)(2,1)} %bitcast.3), calls=%async_computation.1 | async-start | bytes 1572864 | tf_op jit(solution)/shard_map/all_to_all | solution.py:376
  51.6 2.0 %collective-permute-start.6 = (bf16[254,1024]{1,0:T(8,128)(2,1)S(1)}, bf16[254,1024]{1,0:T(8,128)(2,1)S(1)}, u32[]{:S(2)}, u32[]{:S(2)}) collective-permute-start(bf16[254,1024]{1,0:T(8,128)(2,1)S(1)} %collective-permute-done.rows_a), channel_id=1, source_target_pairs={{0,1},{1,0},{2,3},{3,2},{4,5},{5,4},{6,7},{7,6},{8,9},{9,8},{10,11... | collective-permute-start | bytes 1560584 | tf_op jit(solution)/shard_map/ppermute | solution.py:380
  53.6 0.8 copy-start.4
  56.9 27.9 %collective-permute-start.7 = (bf16[96,1024]{1,0:T(8,128)(2,1)}, bf16[96,1024]{1,0:T(8,128)(2,1)S(1)}, u32[]{:S(2)}, u32[]{:S(2)}) collective-permute-start(bf16[96,1024]{1,0:T(8,128)(2,1)} %get-tuple-element.39), channel_id=1, source_target_pairs={{0,2},{1,3},{2,0},{3,1},{4,6},{5,7},{6,4},{7,5},{8,10},{9,11},{10,... | collective-permute-start | bytes 589832 | tf_op jit(solution)/shard_map/ppermute | solution.py:358
  58.7 26.0 %collective-permute-start.8 = (bf16[96,1024]{1,0:T(8,128)(2,1)}, bf16[96,1024]{1,0:T(8,128)(2,1)S(1)}, u32[]{:S(2)}, u32[]{:S(2)}) collective-permute-start(bf16[96,1024]{1,0:T(8,128)(2,1)} %get-tuple-element.40), channel_id=1, source_target_pairs={{0,4},{1,5},{2,6},{3,7},{4,0},{5,1},{6,2},{7,3},{8,12},{9,13},{10,... | collective-permute-start | bytes 589832 | tf_op jit(solution)/shard_map/ppermute | solution.py:358
  60.2 24.6 %collective-permute-start.9 = (bf16[96,1024]{1,0:T(8,128)(2,1)}, bf16[96,1024]{1,0:T(8,128)(2,1)S(1)}, u32[]{:S(2)}, u32[]{:S(2)}) collective-permute-start(bf16[96,1024]{1,0:T(8,128)(2,1)} %get-tuple-element.41), channel_id=1, source_target_pairs={{0,6},{1,7},{2,4},{3,5},{4,2},{5,3},{6,0},{7,1},{8,14},{9,15},{10,... | collective-permute-start | bytes 589832 | tf_op jit(solution)/shard_map/ppermute | solution.py:358
  70.7 0.9 copy-start.1
  77.5 13.1 %all-to-all-start.2 = ((bf16[16,2,1024]{2,1,0:T(2,128)(2,1)}), bf16[16,2,1024]{2,1,0:T(2,128)(2,1)S(1)}, u32[]{:S(2)}, u32[]{:S(2)}) async-start(bf16[16,2,1024]{2,1,0:T(2,128)(2,1)} %get-tuple-element.32), calls=%async_computation.2 | async-start | bytes 131072 | tf_op jit(solution)/shard_map/all_to_all | solution.py:402
  84.8 0.7 copy-start.9
  84.8 0.7 copy-start.10
  84.8 0.8 copy-start.11
  90.6 0.6 copy-start.5

commit v7 on v6

--- a/solution.py
+++ b/solution.py
@@ -32,38 +32,55 @@
 def encode_kernel(
     lengths,
     slots,
-    fetched,
-    pos,
     emb_gain,
     emb_bias,
-    w_qkv_far,
-    w_out_far,
     out_bias,
     norm_gain,
     norm_bias,
+    fetched_far,
+    pos_far,
+    w_qkv_far,
+    w_out_far,
     out,
     spread,
+    fetched,
+    pos,
     w_qkv,
     w_out,
     arrived,
 ):
-    qkv_copy = pltpu.make_async_copy(w_qkv_far, w_qkv, arrived.at[0])
-    out_copy = pltpu.make_async_copy(w_out_far, w_out, arrived.at[1])
-    qkv_copy.start()
-    out_copy.start()
+    inner = HEADS * HD
+    copies = [
+        pltpu.make_async_copy(fetched_far, fetched, arrived.at[0]),
+        pltpu.make_async_copy(pos_far, pos, arrived.at[1]),
+        pltpu.make_async_copy(w_out_far, w_out, arrived.at[2]),
+    ]
+    for third in range(3):
+        columns = pl.ds(third * inner, inner)
+        copies.append(
+            pltpu.make_async_copy(
+                w_qkv_far.at[:, columns], w_qkv.at[:, columns], arrived.at[3 + third]
+            )
+        )
+    for at in (0, 1, 3, 4, 5, 2):
+        copies[at].start()
     tokens, slot_count = slots.shape[0], fetched.shape[0]
     passes = out.shape[0]
     seq = tokens // passes
-    inner = HEADS * HD
     spot = lax.broadcasted_iota(jnp.int32, (tokens, slot_count), 1)
     picker = jnp.where(slots[...] == spot, 1.0, 0.0).astype(jnp.bfloat16)
+    copies[0].wait()
+    copies[1].wait()
     tok = jnp.dot(picker, fetched[...], preferred_element_type=jnp.float32)
     where_at = pos[...].astype(jnp.float32)
     summed = tok + jnp.concatenate([where_at] * passes, axis=0)
     embedded = normed(summed, emb_gain[...], emb_bias[...]).astype(jnp.bfloat16)
-    qkv_copy.wait()
-    projected = jnp.dot(embedded, w_qkv[...], preferred_element_type=jnp.float32)
-    projected = projected.astype(jnp.bfloat16)
+    parts = []
+    for third in range(3):
+        copies[3 + third].wait()
+        weights = w_qkv[:, third * inner : (third + 1) * inner]
+        part = jnp.dot(embedded, weights, preferred_element_type=jnp.float32)
+        parts.append(part.astype(jnp.bfloat16))
 
     block_row = lax.broadcasted_iota(jnp.int32, (HEADS * seq, inner), 0) // seq
     block_col = lax.broadcasted_iota(jnp.int32, (HEADS * seq, inner), 1) // HD
@@ -71,8 +88,7 @@
     lane = lax.broadcasted_iota(jnp.int32, (seq, HEADS * seq), 1) % seq
     contexts = []
     for p in range(passes):
-        part = projected[p * seq : (p + 1) * seq]
-        query, keys, vals = part[:, :inner], part[:, inner : 2 * inner], part[:, 2 * inner :]
+        query, keys, vals = (part[p * seq : (p + 1) * seq] for part in parts)
         zero = jnp.zeros((), jnp.bfloat16)
         keys = jnp.where(same, jnp.concatenate([keys] * HEADS, axis=0), zero)
         vals = jnp.where(same, jnp.concatenate([vals] * HEADS, axis=0), zero)
@@ -83,7 +99,7 @@
         probs = (weights / head_sums(weights, seq)).astype(jnp.bfloat16)
         contexts.append(jnp.dot(probs, vals, preferred_element_type=jnp.float32))
     context = jnp.concatenate(contexts, axis=0).astype(jnp.bfloat16)
-    out_copy.wait()
+    copies[2].wait()
     attended = jnp.dot(context, w_out[...], preferred_element_type=jnp.float32) + out_bias[...]
     hidden = normed(embedded.astype(jnp.float32) + attended, norm_gain[...], norm_bias[...])
     row = lax.broadcasted_iota(jnp.int32, (seq, 1), 0)
@@ -109,14 +125,15 @@
             jax.ShapeDtypeStruct((peers, passes, width), jnp.bfloat16),
         ],
         in_specs=[pl.BlockSpec(memory_space=pltpu.SMEM)]
-        + [pl.BlockSpec(memory_space=pltpu.VMEM)] * 5
-        + [pl.BlockSpec(memory_space=pltpu.HBM)] * 2
-        + [pl.BlockSpec(memory_space=pltpu.VMEM)] * 3,
+        + [pl.BlockSpec(memory_space=pltpu.VMEM)] * 6
+        + [pl.BlockSpec(memory_space=pltpu.HBM)] * 4,
         out_specs=[pl.BlockSpec(memory_space=pltpu.VMEM)] * 2,
         scratch_shapes=[
+            pltpu.VMEM(fetched.shape, fetched.dtype),
+            pltpu.VMEM(pos_table.shape, pos_table.dtype),
             pltpu.VMEM(w_qkv.shape, w_qkv.dtype),
             pltpu.VMEM(w_out.shape, w_out.dtype),
-            pltpu.SemaphoreType.DMA((2,)),
+            pltpu.SemaphoreType.DMA((6,)),
         ],
         compiler_params=pltpu.CompilerParams(vmem_limit_bytes=60 * 1024 * 1024),
         cost_estimate=pl.CostEstimate(
@@ -126,16 +143,20 @@
     )(
         lengths,
         slots,
-        fetched,
-        pos_table,
         emb_gain[None],
         emb_bias[None],
-        w_qkv,
-        w_out,
         out_bias[None],
         norm_gain[None],
         norm_bias[None],
+        fetched,
+        pos_table,
+        w_qkv,
+        w_out,
     )
+
+
+def padded(rows):
+    return -(-rows // 16) * 16
 
 
 def rank_bits(count):
@@ -176,8 +197,10 @@
     filled = jnp.dot(
         left, right, preferred_element_type=jnp.float32, precision=lax.Precision.HIGHEST
     )
-    plan[:, :rows] = jnp.broadcast_to(code[...], (peers, rows))
-    plan[:, rows:] = filled.astype(jnp.int32) - 1
+    filled = filled.astype(jnp.int32) - 1
+    for p in range(peers):
+        plan[p, :, :rows] = code[...]
+        plan[p, :, rows:] = filled[p : p + 1]
     token_slot[...] = down[:tokens] * token_cap + rank_col[:tokens]
 
 
@@ -189,7 +212,7 @@
     return pl.pallas_call(
         functools.partial(route_kernel, sizes),
         out_shape=[
-            ints(peers, rows + token_cap + row_cap + pooled),
+            ints(peers, 1, rows + token_cap + row_cap + pooled),
             ints(passes * seq_len, 1),
             ints(1, rows),
         ],
@@ -206,7 +229,7 @@
         if picks is None:
             code = codes[...]
         else:
-            code = codes[pl.ds(me ^ picks[source], 1), :count]
+            code = codes[me ^ picks[source], :, :count]
         bits = rank_bits(count)
         owner, rank = code >> bits, code & (2**bits - 1)
         fits = ((owner ^ me) & (1 | half)) == 0
@@ -217,6 +240,8 @@
         packed = jnp.dot(table, rows[...], preferred_element_type=jnp.float32)
         packed = packed.astype(jnp.bfloat16)
         for step, out in enumerate(outs):
+            if source == 0 and out.shape[0] > 2 * row_cap:
+                out[...] = jnp.zeros(out.shape, out.dtype)
             out[source * row_cap : (source + 1) * row_cap, :] = packed[
                 step * row_cap : (step + 1) * row_cap
             ]
@@ -227,7 +252,7 @@
     steps = half // 2
     return pl.pallas_call(
         functools.partial(pack_kernel, half, row_cap, count, picks),
-        out_shape=[jax.ShapeDtypeStruct((2 * row_cap, width), jnp.bfloat16)] * steps,
+        out_shape=[jax.ShapeDtypeStruct((padded(2 * row_cap), width), jnp.bfloat16)] * steps,
         in_specs=[pl.BlockSpec(memory_space=pltpu.VMEM)] * 4,
         out_specs=[pl.BlockSpec(memory_space=pltpu.VMEM)] * steps,
         compiler_params=pltpu.CompilerParams(vmem_limit_bytes=60 * 1024 * 1024),
@@ -240,62 +265,110 @@
     )(codes_a, codes_b, rows_a, rows_b)
 
 
-def onehot(where_to, count):
-    centre = lax.broadcasted_iota(jnp.int32, (count, where_to.shape[1]), 0)
-    centre += pl.program_id(0) * count
-    return jnp.where(centre == where_to[...], 1.0, 0.0)
-
-
-def early_kernel(places, centroids, *rest):
-    pieces, (out, share, rows) = rest[:-3], rest[-3:]
-    count = out.shape[0]
-
-    @pl.when(pl.program_id(0) == 0)
-    def _():
-        at = 0
-        for piece in pieces:
-            rows[at : at + piece.shape[0], :] = piece[...]
-            at += piece.shape[0]
-
-    hot = onehot(places, count)
-    sums = jnp.dot(hot.astype(jnp.bfloat16), rows[...], preferred_element_type=jnp.float32)
-    counts = jnp.sum(hot, axis=1, keepdims=True)
-    scale = 1.0 / jnp.maximum(counts, 1.0)
-    out[...] = jnp.where(counts > 0, sums * scale, centroids[...])
-    share[...] = jnp.broadcast_to(scale, share.shape)
-
-
-def late_kernel(late, spread, early, share, out, embeds):
-    passes = spread.shape[1]
-
-    @pl.when(pl.program_id(0) == 0)
-    def _():
-        for peer in range(spread.shape[0]):
-            embeds[peer * passes : (peer + 1) * passes, :] = spread[peer]
-
-    hot = onehot(late, out.shape[0]).astype(jnp.bfloat16)
-    sums = jnp.dot(hot, embeds[...], preferred_element_type=jnp.float32)
-    out[...] = early[...] + sums * share[:, :1]
-
-
-def update(places, late, embeds, centroids, pieces):
+def onehot(where_to, first, count):
+    centre = lax.broadcasted_iota(jnp.int32, (count, where_to.shape[1]), 0) + first
+    return jnp.where(centre == where_to, 1.0, 0.0)
+
+
+BLOCK = 128
+
+
+def early_kernel(places, centroids_far, *rest):
+    pieces, (out_far, share, rows, centroids, out, arrived, left) = rest[:-7], rest[-7:]
+    size = pieces[0].shape[0]
+    count = centroids.shape[0]
+    copies = []
+    for at, piece in enumerate(pieces):
+        copies.append(
+            pltpu.make_async_copy(piece, rows.at[pl.ds(at * size, size)], arrived.at[at])
+        )
+    copies.append(pltpu.make_async_copy(centroids_far, centroids, arrived.at[len(pieces)]))
+    for copy in copies:
+        copy.start()
+    for copy in copies:
+        copy.wait()
+    sends = []
+    for step in range(count // BLOCK):
+        block = pl.ds(step * BLOCK, BLOCK)
+        hot = onehot(places[...], step * BLOCK, BLOCK)
+        counts = jnp.sum(hot, axis=1, keepdims=True)
+        scale = jnp.where(counts > 0, 1.0 / jnp.maximum(counts, 1.0), 0.0)
+        sums = jnp.dot(
+            hot[:, : rows.shape[0]].astype(jnp.bfloat16),
+            rows[...],
+            preferred_element_type=jnp.float32,
+        )
+        out[block, :] = jnp.where(counts > 0, sums * scale, centroids[block, :])
+        share[block, :] = jnp.broadcast_to(scale, (BLOCK, share.shape[1]))
+        sends.append(pltpu.make_async_copy(out.at[block], out_far.at[block], left.at[step]))
+        sends[-1].start()
+    for send in sends:
+        send.wait()
+
+
+def late_kernel(places, late, spread, share, early_far, *rest):
+    pieces, (out_far, rows, early, out, arrived, left) = rest[:-6], rest[-6:]
+    size, passes = pieces[0].shape[0], spread.shape[1]
+    count = early.shape[0]
+    steps = count // BLOCK
+    loads = []
+    for at, piece in enumerate(pieces):
+        loads.append(
+            pltpu.make_async_copy(piece, rows.at[pl.ds(at * size, size)], arrived.at[at])
+        )
+    starts = []
+    for step in range(steps):
+        block = pl.ds(step * BLOCK, BLOCK)
+        starts.append(
+            pltpu.make_async_copy(
+                early_far.at[block], early.at[block], arrived.at[len(pieces) + step]
+            )
+        )
+    for copy in loads + starts:
+        copy.start()
+    top = len(pieces) * size
+    for peer in range(spread.shape[0]):
+        rows[top + peer * passes : top + (peer + 1) * passes, :] = spread[peer]
+    for copy in loads:
+        copy.wait()
+    where_to = jnp.concatenate([places[...], late[...]], axis=1)
+    sends = []
+    for step in range(steps):
+        block = pl.ds(step * BLOCK, BLOCK)
+        hot = onehot(where_to, step * BLOCK, BLOCK).astype(jnp.bfloat16)
+        sums = jnp.dot(hot, rows[...], preferred_element_type=jnp.float32)
+        starts[step].wait()
+        out[block, :] = early[block, :] + sums * share[block, :1]
+        sends.append(pltpu.make_async_copy(out.at[block], out_far.at[block], left.at[step]))
+        sends[-1].start()
+    for send in sends:
+        send.wait()
+
+
+def early_update(places, centroids, pieces):
     centre_count, width = centroids.shape
-    block = 128
-    grid = (centre_count // block,)
-    whole = lambda array: pl.BlockSpec(array.shape, lambda i: (0, 0))
-    part = pl.BlockSpec((block, width), lambda i: (i, 0))
-    thin = pl.BlockSpec((block, 128), lambda i: (i, 0))
     row_total = sum(piece.shape[0] for piece in pieces)
-    full = jax.ShapeDtypeStruct(centroids.shape, jnp.float32)
-    params = pltpu.CompilerParams(vmem_limit_bytes=60 * 1024 * 1024)
-    early, share = pl.pallas_call(
+    wide = pltpu.VMEM(centroids.shape, jnp.float32)
+    return pl.pallas_call(
         early_kernel,
-        grid=grid,
-        out_shape=[full, jax.ShapeDtypeStruct((centre_count, 128), jnp.float32)],
-        in_specs=[whole(places), part] + [whole(piece) for piece in pieces],
-        out_specs=[part, thin],
-        scratch_shapes=[pltpu.VMEM((row_total, width), jnp.bfloat16)],
-        compiler_params=params,
+        out_shape=[
+            jax.ShapeDtypeStruct(centroids.shape, jnp.float32),
+            jax.ShapeDtypeStruct((centre_count, 128), jnp.float32),
+        ],
+        in_specs=[pl.BlockSpec(memory_space=pltpu.VMEM)]
+        + [pl.BlockSpec(memory_space=pltpu.HBM)] * (1 + len(pieces)),
+        out_specs=[
+            pl.BlockSpec(memory_space=pltpu.HBM),
+            pl.BlockSpec(memory_space=pltpu.VMEM),
+        ],
+        scratch_shapes=[
+            pltpu.VMEM((row_total, width), jnp.bfloat16),
+            wide,
+            wide,
+            pltpu.SemaphoreType.DMA((len(pieces) + 1,)),
+            pltpu.SemaphoreType.DMA((centre_count // BLOCK,)),
+        ],
+        compiler_params=pltpu.CompilerParams(vmem_limit_bytes=60 * 1024 * 1024),
         cost_estimate=pl.CostEstimate(
             flops=2 * centre_count * width * row_total,
             bytes_accessed=8 * centre_count * width,
@@ -303,21 +376,34 @@
         ),
         name="early",
     )(places, centroids, *pieces)
+
+
+def late_update(places, late, spread, share, early, pieces):
+    centre_count, width = early.shape
+    row_total = places.shape[1] + late.shape[1]
+    wide = pltpu.VMEM(early.shape, jnp.float32)
+    steps = centre_count // BLOCK
     return pl.pallas_call(
         late_kernel,
-        grid=grid,
-        out_shape=full,
-        in_specs=[whole(late), pl.BlockSpec(embeds.shape, lambda i: (0, 0, 0)), part, thin],
-        out_specs=part,
-        scratch_shapes=[pltpu.VMEM((late.shape[1], width), jnp.bfloat16)],
-        compiler_params=params,
+        out_shape=jax.ShapeDtypeStruct(early.shape, jnp.float32),
+        in_specs=[pl.BlockSpec(memory_space=pltpu.VMEM)] * 4
+        + [pl.BlockSpec(memory_space=pltpu.HBM)] * (1 + len(pieces)),
+        out_specs=pl.BlockSpec(memory_space=pltpu.HBM),
+        scratch_shapes=[
+            pltpu.VMEM((row_total, width), jnp.bfloat16),
+            wide,
+            wide,
+            pltpu.SemaphoreType.DMA((len(pieces) + steps,)),
+            pltpu.SemaphoreType.DMA((steps,)),
+        ],
+        compiler_params=pltpu.CompilerParams(vmem_limit_bytes=60 * 1024 * 1024),
         cost_estimate=pl.CostEstimate(
-            flops=2 * centre_count * width * late.shape[1],
+            flops=2 * centre_count * width * row_total,
             bytes_accessed=8 * centre_count * width,
             transcendentals=0,
         ),
         name="late",
-    )(late, embeds, early, share)
+    )(places, late, spread, share, early, *pieces)
 
 
 def shards(
@@ -363,10 +449,11 @@
     sizes = (peer_count, vocab_rows, token_cap, row_cap, row_count - store_count)
     plan, token_slot, code = route(token_ids, row_owner.reshape(1, row_count), row_slot[None], sizes)
     sibling_code = lax.ppermute(code, "dp", beside)
-    plan = lax.all_to_all(plan, "dp", split_axis=0, concat_axis=0, tiled=True)
     blocks = pack_rows(code, sibling_code, stored_rows, sibling_rows, half, row_cap, row_count)
+    plan, *blocks = lax.optimization_barrier((plan, *blocks))
     own_half = hand_on(blocks)
-    codes, plan = plan[:, :row_count], plan[:, row_count:]
+    codes = lax.all_to_all(plan, "dp", split_axis=0, concat_axis=0, tiled=True)
+    plan = codes[:, 0, row_count:]
     wanted = plan[:, :token_cap].reshape(peer_count * token_cap)
     chosen = wanted[:, None] == jnp.arange(vocab_rows, dtype=jnp.int32)[None, :]
     found = jnp.dot(
@@ -382,7 +469,11 @@
     blocks = pack_rows(codes, codes, partner_rows, far_rows, half, row_cap, row_count, picks)
     other_half = hand_on(blocks)
     sources = lax.axis_index("dp") ^ jnp.arange(peer_count, dtype=jnp.int32)
-    got_places = plan[:, token_cap : token_cap + row_cap][sources].reshape(1, peer_count * row_cap)
+    got_places = plan[:, token_cap : token_cap + row_cap][sources].reshape(half, 2 * row_cap)
+    spare = padded(2 * row_cap) - 2 * row_cap
+    got_places = jnp.pad(got_places, ((0, 0), (0, spare)), constant_values=-1).reshape(1, -1)
+    means, share = early_update(got_places, centroids, own_half)
+    fetched, means, share = lax.optimization_barrier((fetched, means, share))
     late_places = plan[:, token_cap + row_cap :].reshape(1, -1)
 
     passage_embed, spread = encode(
@@ -402,9 +493,8 @@
     all_embeds = lax.all_to_all(
         spread, "dp", split_axis=0, concat_axis=0, tiled=True
     )
-    new_centroids = update(
-        got_places, late_places, all_embeds, centroids, own_half + other_half
-    )
+    other_places = got_places[:, got_places.shape[1] // 2 :]
+    new_centroids = late_update(other_places, late_places, all_embeds, share, means, other_half)
     return (passage_embed, new_centroids)
 
 

time: 96 us -> 87 us (0.906)
  waiting for transfers between devices: 36.9 us -> 30.1 us
  local copies, waits for them, and re-layouts: 8.55 us -> 6.41 us
    all_to_all x1, waiting for transfers between devices: 17.8 us -> 11 us  [shards(): codes = lax.all_to_all(plan, 'dp', split_axis=0, concat_axis=0, tiled=True)]
    all_to_all x1, waiting for transfers between devices: 0.01 us -> 5.54 us  [shards(): lax.all_to_all(spread, 'dp', split_axis=0, concat_axis=0, tiled=True)]
    all_to_all x1, waiting for transfers between devices: 10.4 us -> 5.26 us  [shards(): lax.all_to_all(found.reshape(peer_count, token_cap, width), 'dp', split_a...]
    all_to_all x1 -> x0, local copies, waits for them, and re-layouts: 1.37 us -> none  [shards(): plan = lax.all_to_all(plan, 'dp', split_axis=0, concat_axis=0, tiled=True)]
    ppermute x1, waiting for transfers between devices: 0.01 us -> 1.19 us  [shards(): sibling_code = lax.ppermute(code, 'dp', beside)]
    unnamed x27 -> x30, local copies, waits for them, and re-layouts: 4.44 us -> 3.69 us
  transfers between devices with their start and end apart: 13 -> 13, of which waited for: 6 -> 7; matrix products, arithmetic and copies ran while one was open for 6% -> 5% of each run, Pallas kernels for 19% -> 20%
where the time goes in v7:
time: 87 us; the launch traced here: 86.4 us
  waiting for transfers between devices  30.1 us (35%)
  starting transfers between devices  25.8 us (30%)
  Pallas kernels  22 us (25%)
  local copies, waits for them, and re-layouts  6.41 us (7%)
  matrix products  1.29 us (1%)
    all_to_all x1, waiting for transfers between devices, shards(): codes = lax.all_to_all(plan, 'dp', split_axis=0, concat_axis=0, tiled=True)  11 us
    ppermute x6, starting transfers between devices, hand_on(): got.append(lax.ppermute(blocks[step], 'dp', moves))  7.04 us
    ppermute x6, waiting for transfers between devices, hand_on(): got.append(lax.ppermute(blocks[step], 'dp', moves))  6.92 us
    pallas_call x1, Pallas kernels, encode(): pl.pallas_call(encode_kernel, out_shape=[jax.ShapeDtypeStruct((passes, wi...  5.67 us
    all_to_all x1, waiting for transfers between devices, shards(): lax.all_to_all(spread, 'dp', split_axis=0, concat_axis=0, tiled=True)  5.54 us
    all_to_all x1, waiting for transfers between devices, shards(): lax.all_to_all(found.reshape(peer_count, token_cap, width), 'dp', split_a...  5.26 us
    all_to_all x1, starting transfers between devices, shards(): lax.all_to_all(spread, 'dp', split_axis=0, concat_axis=0, tiled=True)  5.2 us
    pallas_call x1, Pallas kernels, early_update(): pl.pallas_call(early_kernel, out_shape=[jax.ShapeDtypeStruct(centroids.sh...  5.11 us
  transfers between devices with their start and end apart: 13, of which 7 were waited for; matrix products, arithmetic and copies ran while one was open for 5% of the time, Pallas kernels for 20%

profile of v7, /device:TPU:0, one launch (start us, length us, event | category | flops | bytes accessed | tf_op | source)
XLA Modules:
  0.0 86.4 jit_solution(18372162444937876087)
XLA Ops:
  0.6 0.0 copy-start
  0.6 0.5 collective-permute-start.1
  1.2 3.7 %collective-permute-start.2 = (bf16[254,1024]{1,0:T(8,128)(2,1)}, bf16[254,1024]{1,0:T(8,128)(2,1)S(1)}, u32[]{:S(2)}, u32[]{:S(2)}) collective-permute-start(bf16[254,1024]{1,0:T(8,128)(2,1)} %rows_a.1), channel_id=1, source_target_pairs={{0,8},{1,9},{2,10},{3,11},{4,12},{5,13},{6,14},{7,15},{8,0},{9,1},... | collective-permute-start | bytes 1560584 | tf_op jit(solution)/shard_map/ppermute | solution.py:447
  4.8 1.8 %route.1 = (s32[16,1,330]{2,1,0:T(1,128)}, s32[128,1]{1,0:T(8,128)}, s32[1,256]{1,0:T(1,128)}) custom-call(s32[2,64]{1,0:T(2,128)} %token_ids.1, s32[1,256]{1,0:T(1,128)} %bitcast.23, s32[1,256]{1,0:T(1,128)} %bitcast.24), custom_call_target="tpu_custom_call" | custom-call | tf_op jit(solution)/shard_map/route/pallas_call | solution.py:212
  6.7 0.2 collective-permute-start
  6.8 1.2 %collective-permute-done.codes_b = s32[1,256]{1,0:T(1,128)S(1)} collective-permute-done((s32[1,256]{1,0:T(1,128)}, s32[1,256]{1,0:T(1,128)S(1)}, u32[]{:S(2)}, u32[]{:S(2)}) %collective-permute-start) | collective-permute-done | bytes 1056 | tf_op jit(solution)/shard_map/ppermute | solution.py:451
  8.0 0.0 copy-start.14
  8.0 0.0 collective-permute-done.1.rows_b
  8.0 0.6 copy-done.14
  8.6 0.0 copy-start.4
  8.6 0.8 copy-done.4
  9.4 2.4 %pack.2 = (bf16[96,1024]{1,0:T(8,128)(2,1)}, bf16[96,1024]{1,0:T(8,128)(2,1)}, bf16[96,1024]{1,0:T(8,128)(2,1)}, bf16[96,1024]{1,0:T(8,128)(2,1)}) custom-call(s32[1,256]{1,0:T(1,128)} %get-tuple-element.33.codes_a, s32[1,256]{1,0:T(1,128)} %copy-done.14, bf16[254,1024]{1,0:T(8,128)(2,1)} %rows_a.1, bf16[254,1024]{1,0:T(8,128)(2,1)} %copy-done.4), custom_call_target="tpu_custom_call" | custom-call | flops 199753728 | bytes 1826816 | tf_op jit(solution)/shard_map/pack/pallas_call | solution.py:253
  11.8 3.9 %all-to-all-start = ((s32[16,1,330]{2,1,0:T(1,128)}), s32[16,1,330]{2,1,0:T(1,128)S(1)}, u32[]{:S(2)}, u32[]{:S(2)}) async-start(s32[16,1,330]{2,1,0:T(1,128)} %get-tuple-element.38), calls=%async_computation | async-start | bytes 49152 | tf_op jit(solution)/shard_map/all_to_all | solution.py:455
  15.8 1.9 %collective-permute-start.3 = (bf16[96,1024]{1,0:T(8,128)(2,1)}, bf16[96,1024]{1,0:T(8,128)(2,1)S(1)}, u32[]{:S(2)}, u32[]{:S(2)}) collective-permute-start(bf16[96,1024]{1,0:T(8,128)(2,1)} %get-tuple-element.40), channel_id=1, source_target_pairs={{0,2},{1,3},{2,0},{3,1},{4,6},{5,7},{6,4},{7,5},{8,10},{9,11},{10,... | collective-permute-start | bytes 589832 | tf_op jit(solution)/shard_map/ppermute | solution.py:444
  17.7 1.5 %collective-permute-start.4 = (bf16[96,1024]{1,0:T(8,128)(2,1)}, bf16[96,1024]{1,0:T(8,128)(2,1)S(1)}, u32[]{:S(2)}, u32[]{:S(2)}) collective-permute-start(bf16[96,1024]{1,0:T(8,128)(2,1)} %get-tuple-element.41), channel_id=1, source_target_pairs={{0,4},{1,5},{2,6},{3,7},{4,0},{5,1},{6,2},{7,3},{8,12},{9,13},{10,... | collective-permute-start | bytes 589832 | tf_op jit(solution)/shard_map/ppermute | solution.py:444
  19.2 0.2 collective-permute-start.5
  19.3 11.0 %all-to-all-done.codes_a.codes_b = s32[16,1,330]{2,1,0:T(1,128)S(1)} async-done(((s32[16,1,330]{2,1,0:T(1,128)}), s32[16,1,330]{2,1,0:T(1,128)S(1)}, u32[]{:S(2)}, u32[]{:S(2)}) %all-to-all-start) | async-done | bytes 21152 | tf_op jit(solution)/shard_map/all_to_all | solution.py:455
  30.3 0.0 copy-start.5
  30.3 0.1 eq.15
  30.4 0.0 copy-done
  30.4 1.3 %convolution_convert_fusion = bf16[384,1024]{1,0:T(8,128)(2,1)} fusion(bf16[240,1024]{1,0:T(8,128)(2,1)S(1)} %copy-done, s32[384]{0:T(512)S(1)} %eq.15), kind=kOutput, calls=%fused_computation.1 | convolution fusion | flops 189229056 | bytes 1279488 | tf_op jit(solution)/shard_map/dot_general | solution.py:459
  31.7 0.0 collective-permute-done.2.rows_a
  31.7 0.0 copy-start.2
  31.7 0.0 collective-permute-done.3.rest_1_
  31.7 0.0 copy-start.10
  31.7 1.7 %collective-permute-done.4.rest_2_ = bf16[96,1024]{1,0:T(8,128)(2,1)S(1)} collective-permute-done((bf16[96,1024]{1,0:T(8,128)(2,1)}, bf16[96,1024]{1,0:T(8,128)(2,1)S(1)}, u32[]{:S(2)}, u32[]{:S(2)}) %collective-permute-start.4) | collective-permute-done | bytes 196640 | tf_op jit(solution)/shard_map/ppermute | solution.py:444
  33.4 0.0 copy-start.11
  33.4 5.2 %collective-permute-done.5.rest_3_ = bf16[96,1024]{1,0:T(8,128)(2,1)S(1)} collective-permute-done((bf16[96,1024]{1,0:T(8,128)(2,1)}, bf16[96,1024]{1,0:T(8,128)(2,1)S(1)}, u32[]{:S(2)}, u32[]{:S(2)}) %collective-permute-start.5) | collective-permute-done | bytes 196640 | tf_op jit(solution)/shard_map/ppermute | solution.py:444
  38.6 4.9 %all-to-all-start.1 = ((bf16[16,24,1024]{2,1,0:T(8,128)(2,1)}), bf16[16,24,1024]{2,1,0:T(8,128)(2,1)S(1)}, u32[]{:S(2)}, u32[]{:S(2)}) async-start(bf16[16,24,1024]{2,1,0:T(8,128)(2,1)} %bitcast.8), calls=%async_computation.1 | async-start | bytes 1572864 | tf_op jit(solution)/shard_map/all_to_all | solution.py:463
  43.5 0.4 collective-permute-start.6
  43.9 0.1 slice.24
  44.0 0.6 gather_fusion
  44.6 0.7 reshape.41.places
  45.3 0.2 collective-permute-done.6.rows_b
  45.5 0.0 copy-done.5
  45.5 0.0 copy-done.2
  45.5 0.8 copy-done.3
  46.3 2.5 %pack.3 = (bf16[96,1024]{1,0:T(8,128)(2,1)}, bf16[96,1024]{1,0:T(8,128)(2,1)}, bf16[96,1024]{1,0:T(8,128)(2,1)}, bf16[96,1024]{1,0:T(8,128)(2,1)}) custom-call(s32[16,1,330]{2,1,0:T(1,128)} %copy-done.5, s32[16,1,330]{2,1,0:T(1,128)} %copy-done.5, bf16[254,1024]{1,0:T(8,128)(2,1)} %copy-done.2, bf16[254,1024]{1,0:T(8,128)(2,1)} %copy-done.3), custom_call_target="tpu_custom_call" | custom-call | flops 199753728 | bytes 1826816 | tf_op jit(solution)/shard_map/pack/pallas_call | solution.py:253
  48.8 1.9 %collective-permute-start.7 = (bf16[96,1024]{1,0:T(8,128)(2,1)}, bf16[96,1024]{1,0:T(8,128)(2,1)S(1)}, u32[]{:S(2)}, u32[]{:S(2)}) collective-permute-start(bf16[96,1024]{1,0:T(8,128)(2,1)} %get-tuple-element.57), channel_id=1, source_target_pairs={{0,2},{1,3},{2,0},{3,1},{4,6},{5,7},{6,4},{7,5},{8,10},{9,11},{10,... | collective-permute-start | bytes 589832 | tf_op jit(solution)/shard_map/ppermute | solution.py:444
  50.6 1.5 %collective-permute-start.8 = (bf16[96,1024]{1,0:T(8,128)(2,1)}, bf16[96,1024]{1,0:T(8,128)(2,1)S(1)}, u32[]{:S(2)}, u32[]{:S(2)}) collective-permute-start(bf16[96,1024]{1,0:T(8,128)(2,1)} %get-tuple-element.58), channel_id=1, source_target_pairs={{0,4},{1,5},{2,6},{3,7},{4,0},{5,1},{6,2},{7,3},{8,12},{9,13},{10,... | collective-permute-start | bytes 589832 | tf_op jit(solution)/shard_map/ppermute | solution.py:444
  52.1 0.2 collective-permute-start.9
  52.3 0.0 copy-done.10
  52.3 0.0 copy-done.11
  52.3 0.0 copy-done.12
  52.3 5.1 %early.1 = (f32[512,1024]{1,0:T(8,128)}, f32[512,128]{1,0:T(8,128)}) custom-call(s32[1,768]{1,0:T(1,128)} %reshape.41.places, f32[512,1024]{1,0:T(8,128)} %centroids_far.1, bf16[96,1024]{1,0:T(8,128)(2,1)} %get-tuple-element.44.rest_0_, bf16[96,1024]{1,0:T(8,128)(2,1)} %copy-done.10, bf16[96,1024]{1,0:T(8,128)(2,1)} %copy-done.11, bf16[96,1024]{1,0:T(8,128)(2,1)} %copy-done.12), custom_call_target="tpu_custom_call" | custom-call | flops 402653184 | bytes 4194304 | tf_op jit(solution)/shard_map/early/pallas_call | solution.py:352
  57.4 5.3 %all-to-all-done.1 = bf16[16,24,1024]{2,1,0:T(8,128)(2,1)S(1)} async-done(((bf16[16,24,1024]{2,1,0:T(8,128)(2,1)}), bf16[16,24,1024]{2,1,0:T(8,128)(2,1)S(1)}, u32[]{:S(2)}, u32[]{:S(2)}) %all-to-all-start.1) | async-done | bytes 786464 | tf_op jit(solution)/shard_map/all_to_all | solution.py:463
  62.7 0.9 %copy-done.1 = bf16[16,24,1024]{2,1,0:T(8,128)(2,1)} copy-done((bf16[16,24,1024]{2,1,0:T(8,128)(2,1)}, bf16[16,24,1024]{2,1,0:T(8,128)(2,1)S(1)}, u32[]{:S(2)}) %copy-start.1) | copy-done | bytes 786456
  63.5 5.7 %encode.1 = (bf16[2,1024]{1,0:T(2,128)(2,1)}, bf16[16,2,1024]{2,1,0:T(2,128)(2,1)}) custom-call(s32[2]{0:T(128)} %lengths.1, s32[128,1]{1,0:T(8,128)} %get-tuple-element.31.slots, f32[1,1024]{1,0:T(1,128)} %bitcast.18, f32[1,1024]{1,0:T(1,128)} %bitcast.19, f32[1,1024]{1,0:T(1,128)} %bitcast.20, f32[1,1024]{1,0:T(1,128)} %bitcast.21, f32[1,1024]{1,0:T(1,128)} %bitcast.22, ...), custom_call_target="tpu_custom_call" | custom-call | flops 637534208 | bytes 6291456 | tf_op jit(solution)/shard_map/encode/pallas_call | solution.py:121
  69.2 5.2 %all-to-all-start.2 = ((bf16[16,2,1024]{2,1,0:T(2,128)(2,1)}), bf16[16,2,1024]{2,1,0:T(2,128)(2,1)S(1)}, u32[]{:S(2)}, u32[]{:S(2)}) async-start(bf16[16,2,1024]{2,1,0:T(2,128)(2,1)} %get-tuple-element.52), calls=%async_computation.2 | async-start | bytes 131072 | tf_op jit(solution)/shard_map/all_to_all | solution.py:493
  74.4 0.1 slice.26
  74.5 0.0 copy-done.13
  74.5 0.6 slice.25.places
  75.1 0.7 reshape.42.late
  75.8 0.0 collective-permute-done.7.rest_1_
  75.8 0.0 collective-permute-done.8.rest_2_
  75.8 0.0 copy-start.8
  75.8 0.0 collective-permute-done.9.rest_3_
  75.8 0.0 copy-start.9
  75.8 5.5 %all-to-all-done.2.spread = bf16[16,2,1024]{2,1,0:T(2,128)(2,1)S(1)} async-done(((bf16[16,2,1024]{2,1,0:T(2,128)(2,1)}), bf16[16,2,1024]{2,1,0:T(2,128)(2,1)S(1)}, u32[]{:S(2)}, u32[]{:S(2)}) %all-to-all-start.2) | async-done | bytes 65568 | tf_op jit(solution)/shard_map/all_to_all | solution.py:493
  81.3 0.0 copy-done.7
  81.3 0.0 copy-done.8
  81.3 0.0 copy-done.9
  81.3 0.6 copy-done.6
  81.9 4.5 %late.1 = f32[512,1024]{1,0:T(8,128)} custom-call(s32[1,384]{1,0:T(1,128)} %slice.25.places, s32[1,32]{1,0:T(1,128)} %reshape.42.late, bf16[16,2,1024]{2,1,0:T(2,128)(2,1)} %copy-done.6, f32[512,128]{1,0:T(8,128)} %get-tuple-element.53.share, f32[512,1024]{1,0:T(8,128)} %get-tuple-element.54.early_far, bf16[96,1024]{1,0:T(8,128)(2,1)} %get-tuple-element.56.rest_0_, ...), custom_call_target="tpu_custom_call" | custom-call | flops 436207616 | bytes 4194304 | tf_op jit(solution)/shard_map/late/pallas_call | solution.py:386
  (9 shorter events, 0.0 us)
Async XLA Ops:
  0.6 29.8 %copy-start = (bf16[240,1024]{1,0:T(8,128)(2,1)S(1)}, bf16[240,1024]{1,0:T(8,128)(2,1)}, u32[]{:S(2)}) copy-start(bf16[240,1024]{1,0:T(8,128)(2,1)} %param.17) | copy-start | bytes 1474564
  0.6 7.4 %collective-permute-start.1 = (bf16[254,1024]{1,0:T(8,128)(2,1)}, bf16[254,1024]{1,0:T(8,128)(2,1)S(1)}, u32[]{:S(2)}, u32[]{:S(2)}) collective-permute-start(bf16[254,1024]{1,0:T(8,128)(2,1)} %rows_a.1), channel_id=1, source_target_pairs={{0,1},{1,0},{2,3},{3,2},{4,5},{5,4},{6,7},{7,6},{8,9},{9,8},{10,11... | collective-permute-start | bytes 1560584 | tf_op jit(solution)/shard_map/ppermute | solution.py:448
  1.2 30.5 %collective-permute-start.2 = (bf16[254,1024]{1,0:T(8,128)(2,1)}, bf16[254,1024]{1,0:T(8,128)(2,1)S(1)}, u32[]{:S(2)}, u32[]{:S(2)}) collective-permute-start(bf16[254,1024]{1,0:T(8,128)(2,1)} %rows_a.1), channel_id=1, source_target_pairs={{0,8},{1,9},{2,10},{3,11},{4,12},{5,13},{6,14},{7,15},{8,0},{9,1},... | collective-permute-start | bytes 1560584 | tf_op jit(solution)/shard_map/ppermute | solution.py:447
  6.7 1.4 %collective-permute-start = (s32[1,256]{1,0:T(1,128)}, s32[1,256]{1,0:T(1,128)S(1)}, u32[]{:S(2)}, u32[]{:S(2)}) collective-permute-start(s32[1,256]{1,0:T(1,128)} %get-tuple-element.33.codes_a), channel_id=1, source_target_pairs={{0,1},{1,0},{2,3},{3,2},{4,5},{5,4},{6,7},{7,6},{8,9},{9,8},{10,11... | collective-permute-start | bytes 3080 | tf_op jit(solution)/shard_map/ppermute | solution.py:451
  8.0 0.6 copy-start.14
  8.6 0.8 copy-start.4
  11.8 18.5 %all-to-all-start = ((s32[16,1,330]{2,1,0:T(1,128)}), s32[16,1,330]{2,1,0:T(1,128)S(1)}, u32[]{:S(2)}, u32[]{:S(2)}) async-start(s32[16,1,330]{2,1,0:T(1,128)} %get-tuple-element.38), calls=%async_computation | async-start | bytes 49152 | tf_op jit(solution)/shard_map/all_to_all | solution.py:455
  15.8 15.9 %collective-permute-start.3 = (bf16[96,1024]{1,0:T(8,128)(2,1)}, bf16[96,1024]{1,0:T(8,128)(2,1)S(1)}, u32[]{:S(2)}, u32[]{:S(2)}) collective-permute-start(bf16[96,1024]{1,0:T(8,128)(2,1)} %get-tuple-element.40), channel_id=1, source_target_pairs={{0,2},{1,3},{2,0},{3,1},{4,6},{5,7},{6,4},{7,5},{8,10},{9,11},{10,... | collective-permute-start | bytes 589832 | tf_op jit(solution)/shard_map/ppermute | solution.py:444
  17.7 15.8 %collective-permute-start.4 = (bf16[96,1024]{1,0:T(8,128)(2,1)}, bf16[96,1024]{1,0:T(8,128)(2,1)S(1)}, u32[]{:S(2)}, u32[]{:S(2)}) collective-permute-start(bf16[96,1024]{1,0:T(8,128)(2,1)} %get-tuple-element.41), channel_id=1, source_target_pairs={{0,4},{1,5},{2,6},{3,7},{4,0},{5,1},{6,2},{7,3},{8,12},{9,13},{10,... | collective-permute-start | bytes 589832 | tf_op jit(solution)/shard_map/ppermute | solution.py:444
  19.2 19.5 %collective-permute-start.5 = (bf16[96,1024]{1,0:T(8,128)(2,1)}, bf16[96,1024]{1,0:T(8,128)(2,1)S(1)}, u32[]{:S(2)}, u32[]{:S(2)}) collective-permute-start(bf16[96,1024]{1,0:T(8,128)(2,1)} %get-tuple-element.42), channel_id=1, source_target_pairs={{0,6},{1,7},{2,4},{3,5},{4,2},{5,3},{6,0},{7,1},{8,14},{9,15},{10,... | collective-permute-start | bytes 589832 | tf_op jit(solution)/shard_map/ppermute | solution.py:444
  30.3 15.2 %copy-start.5 = (s32[16,1,330]{2,1,0:T(1,128)}, s32[16,1,330]{2,1,0:T(1,128)S(1)}, u32[]{:S(2)}) copy-start(s32[16,1,330]{2,1,0:T(1,128)S(1)} %all-to-all-done.codes_a.codes_b) | copy-start | bytes 63364
  31.7 13.8 %copy-start.2 = (bf16[254,1024]{1,0:T(8,128)(2,1)}, bf16[254,1024]{1,0:T(8,128)(2,1)S(1)}, u32[]{:S(2)}) copy-start(bf16[254,1024]{1,0:T(8,128)(2,1)S(1)} %collective-permute-done.2.rows_a) | copy-start | bytes 1560580
  31.7 20.6 %copy-start.10 = (bf16[96,1024]{1,0:T(8,128)(2,1)}, bf16[96,1024]{1,0:T(8,128)(2,1)S(1)}, u32[]{:S(2)}) copy-start(bf16[96,1024]{1,0:T(8,128)(2,1)S(1)} %collective-permute-done.3.rest_1_) | copy-start | bytes 589828
  33.4 18.8 %copy-start.11 = (bf16[96,1024]{1,0:T(8,128)(2,1)}, bf16[96,1024]{1,0:T(8,128)(2,1)S(1)}, u32[]{:S(2)}) copy-start(bf16[96,1024]{1,0:T(8,128)(2,1)S(1)} %collective-permute-done.4.rest_2_) | copy-start | bytes 589828
  38.6 13.6 %copy-start.12 = (bf16[96,1024]{1,0:T(8,128)(2,1)}, bf16[96,1024]{1,0:T(8,128)(2,1)S(1)}, u32[]{:S(2)}) copy-start(bf16[96,1024]{1,0:T(8,128)(2,1)S(1)} %collective-permute-done.5.rest_3_) | copy-start | bytes 589828
  38.6 24.0 %all-to-all-start.1 = ((bf16[16,24,1024]{2,1,0:T(8,128)(2,1)}), bf16[16,24,1024]{2,1,0:T(8,128)(2,1)S(1)}, u32[]{:S(2)}, u32[]{:S(2)}) async-start(bf16[16,24,1024]{2,1,0:T(8,128)(2,1)} %bitcast.8), calls=%async_computation.1 | async-start | bytes 1572864 | tf_op jit(solution)/shard_map/all_to_all | solution.py:463
  43.5 2.0 %collective-permute-start.6 = (bf16[254,1024]{1,0:T(8,128)(2,1)S(1)}, bf16[254,1024]{1,0:T(8,128)(2,1)S(1)}, u32[]{:S(2)}, u32[]{:S(2)}) collective-permute-start(bf16[254,1024]{1,0:T(8,128)(2,1)S(1)} %collective-permute-done.2.rows_a), channel_id=1, source_target_pairs={{0,1},{1,0},{2,3},{3,2},{4,5},{5,4},{6,7},{7,6},{8,9},{9,8},{10,11... | collective-permute-start | bytes 1560584 | tf_op jit(solution)/shard_map/ppermute | solution.py:467
  45.5 0.8 copy-start.3
  48.8 27.0 %collective-permute-start.7 = (bf16[96,1024]{1,0:T(8,128)(2,1)}, bf16[96,1024]{1,0:T(8,128)(2,1)S(1)}, u32[]{:S(2)}, u32[]{:S(2)}) collective-permute-start(bf16[96,1024]{1,0:T(8,128)(2,1)} %get-tuple-element.57), channel_id=1, source_target_pairs={{0,2},{1,3},{2,0},{3,1},{4,6},{5,7},{6,4},{7,5},{8,10},{9,11},{10,... | collective-permute-start | bytes 589832 | tf_op jit(solution)/shard_map/ppermute | solution.py:444
  50.6 25.1 %collective-permute-start.8 = (bf16[96,1024]{1,0:T(8,128)(2,1)}, bf16[96,1024]{1,0:T(8,128)(2,1)S(1)}, u32[]{:S(2)}, u32[]{:S(2)}) collective-permute-start(bf16[96,1024]{1,0:T(8,128)(2,1)} %get-tuple-element.58), channel_id=1, source_target_pairs={{0,4},{1,5},{2,6},{3,7},{4,0},{5,1},{6,2},{7,3},{8,12},{9,13},{10,... | collective-permute-start | bytes 589832 | tf_op jit(solution)/shard_map/ppermute | solution.py:444
  52.1 23.7 %collective-permute-start.9 = (bf16[96,1024]{1,0:T(8,128)(2,1)}, bf16[96,1024]{1,0:T(8,128)(2,1)S(1)}, u32[]{:S(2)}, u32[]{:S(2)}) collective-permute-start(bf16[96,1024]{1,0:T(8,128)(2,1)} %get-tuple-element.59), channel_id=1, source_target_pairs={{0,6},{1,7},{2,4},{3,5},{4,2},{5,3},{6,0},{7,1},{8,14},{9,15},{10,... | collective-permute-start | bytes 589832 | tf_op jit(solution)/shard_map/ppermute | solution.py:444
  62.7 0.9 %copy-start.1 = (bf16[16,24,1024]{2,1,0:T(8,128)(2,1)}, bf16[16,24,1024]{2,1,0:T(8,128)(2,1)S(1)}, u32[]{:S(2)}) copy-start(bf16[16,24,1024]{2,1,0:T(8,128)(2,1)S(1)} %all-to-all-done.1) | copy-start | bytes 2359300
  63.5 11.0 %copy-start.13 = (s32[1,768]{1,0:T(1,128)S(1)}, s32[1,768]{1,0:T(1,128)}, u32[]{:S(2)}) copy-start(s32[1,768]{1,0:T(1,128)} %reshape.41.places) | copy-start | bytes 9220
  69.2 12.1 %all-to-all-start.2 = ((bf16[16,2,1024]{2,1,0:T(2,128)(2,1)}), bf16[16,2,1024]{2,1,0:T(2,128)(2,1)S(1)}, u32[]{:S(2)}, u32[]{:S(2)}) async-start(bf16[16,2,1024]{2,1,0:T(2,128)(2,1)} %get-tuple-element.52), calls=%async_computation.2 | async-start | bytes 131072 | tf_op jit(solution)/shard_map/all_to_all | solution.py:493
  75.8 5.6 %copy-start.7 = (bf16[96,1024]{1,0:T(8,128)(2,1)}, bf16[96,1024]{1,0:T(8,128)(2,1)S(1)}, u32[]{:S(2)}) copy-start(bf16[96,1024]{1,0:T(8,128)(2,1)S(1)} %collective-permute-done.7.rest_1_) | copy-start | bytes 589828
  75.8 5.6 %copy-start.8 = (bf16[96,1024]{1,0:T(8,128)(2,1)}, bf16[96,1024]{1,0:T(8,128)(2,1)S(1)}, u32[]{:S(2)}) copy-start(bf16[96,1024]{1,0:T(8,128)(2,1)S(1)} %collective-permute-done.8.rest_2_) | copy-start | bytes 589828
  75.8 5.6 %copy-start.9 = (bf16[96,1024]{1,0:T(8,128)(2,1)}, bf16[96,1024]{1,0:T(8,128)(2,1)S(1)}, u32[]{:S(2)}) copy-start(bf16[96,1024]{1,0:T(8,128)(2,1)S(1)} %collective-permute-done.9.rest_3_) | copy-start | bytes 589828
  81.3 0.6 copy-start.6

commit v8 on v7

--- a/solution.py
+++ b/solution.py
@@ -29,55 +29,42 @@
     return jnp.concatenate(sums, axis=1)
 
 
-def encode_kernel(
-    lengths,
-    slots,
-    emb_gain,
-    emb_bias,
-    out_bias,
-    norm_gain,
-    norm_bias,
-    fetched_far,
-    pos_far,
-    w_qkv_far,
-    w_out_far,
-    out,
-    spread,
-    fetched,
-    pos,
-    w_qkv,
-    w_out,
-    arrived,
-):
-    inner = HEADS * HD
+def encode_kernel(*refs):
+    count = (len(refs) - 3) // 2
+    far, (out, spread), near, arrived = refs[:count], refs[count : count + 2], refs[-count - 1 : -1], refs[-1]
+    w_qkv_far, inner = far[-2], HEADS * HD
     copies = [
-        pltpu.make_async_copy(fetched_far, fetched, arrived.at[0]),
-        pltpu.make_async_copy(pos_far, pos, arrived.at[1]),
-        pltpu.make_async_copy(w_out_far, w_out, arrived.at[2]),
+        pltpu.make_async_copy(source, target, arrived.at[at])
+        for at, (source, target) in enumerate(zip(far, near))
+        if source is not w_qkv_far
     ]
+    lengths, slots, fetched, pos, emb_gain, emb_bias, out_bias, norm_gain, norm_bias, w_qkv, w_out = near
+    out_copy = copies.pop()
+    thirds = []
     for third in range(3):
         columns = pl.ds(third * inner, inner)
-        copies.append(
+        thirds.append(
             pltpu.make_async_copy(
-                w_qkv_far.at[:, columns], w_qkv.at[:, columns], arrived.at[3 + third]
+                w_qkv_far.at[:, columns], w_qkv.at[:, columns], arrived.at[count + third]
             )
         )
-    for at in (0, 1, 3, 4, 5, 2):
-        copies[at].start()
+    for copy in copies + thirds + [out_copy]:
+        copy.start()
+    for copy in copies:
+        copy.wait()
+    passes = out.shape[0]
+    size = [lengths[:, p : p + 1] for p in range(passes)]
     tokens, slot_count = slots.shape[0], fetched.shape[0]
-    passes = out.shape[0]
     seq = tokens // passes
     spot = lax.broadcasted_iota(jnp.int32, (tokens, slot_count), 1)
     picker = jnp.where(slots[...] == spot, 1.0, 0.0).astype(jnp.bfloat16)
-    copies[0].wait()
-    copies[1].wait()
     tok = jnp.dot(picker, fetched[...], preferred_element_type=jnp.float32)
     where_at = pos[...].astype(jnp.float32)
     summed = tok + jnp.concatenate([where_at] * passes, axis=0)
     embedded = normed(summed, emb_gain[...], emb_bias[...]).astype(jnp.bfloat16)
     parts = []
     for third in range(3):
-        copies[3 + third].wait()
+        thirds[third].wait()
         weights = w_qkv[:, third * inner : (third + 1) * inner]
         part = jnp.dot(embedded, weights, preferred_element_type=jnp.float32)
         parts.append(part.astype(jnp.bfloat16))
@@ -95,17 +82,17 @@
         scores = lax.dot_general(
             query, keys, (((1,), (1,)), ((), ())), preferred_element_type=jnp.float32
         ) * HD ** (-0.5)
-        weights = jnp.where(lane < lengths[p], jnp.exp(scores), 0.0)
+        weights = jnp.where(lane < size[p], jnp.exp(scores), 0.0)
         probs = (weights / head_sums(weights, seq)).astype(jnp.bfloat16)
         contexts.append(jnp.dot(probs, vals, preferred_element_type=jnp.float32))
     context = jnp.concatenate(contexts, axis=0).astype(jnp.bfloat16)
-    copies[2].wait()
+    out_copy.wait()
     attended = jnp.dot(context, w_out[...], preferred_element_type=jnp.float32) + out_bias[...]
     hidden = normed(embedded.astype(jnp.float32) + attended, norm_gain[...], norm_bias[...])
     row = lax.broadcasted_iota(jnp.int32, (seq, 1), 0)
     for p in range(passes):
-        kept = jnp.where(row < lengths[p], hidden[p * seq : (p + 1) * seq], 0.0)
-        pooled = jnp.sum(kept, axis=0, keepdims=True) / lengths[p].astype(jnp.float32)
+        kept = jnp.where(row < size[p], hidden[p * seq : (p + 1) * seq], 0.0)
+        pooled = jnp.sum(kept, axis=0, keepdims=True) / size[p].astype(jnp.float32)
         scale = lax.rsqrt(jnp.mean(pooled * pooled, axis=-1, keepdims=True) + 1e-06)
         out[p : p + 1, :] = (pooled * scale).astype(jnp.bfloat16)
     spread[...] = jnp.broadcast_to(out[...][None], spread.shape)
@@ -118,41 +105,35 @@
     tokens = slots.shape[0]
     passes = lengths.shape[0]
     macs = tokens * width * (fetched.shape[0] + 4 * HEADS * HD)
+    operands = (
+        lengths[None],
+        slots,
+        fetched,
+        pos_table,
+        emb_gain[None],
+        emb_bias[None],
+        out_bias[None],
+        norm_gain[None],
+        norm_bias[None],
+        w_qkv,
+        w_out,
+    )
     return pl.pallas_call(
         encode_kernel,
         out_shape=[
             jax.ShapeDtypeStruct((passes, width), jnp.bfloat16),
             jax.ShapeDtypeStruct((peers, passes, width), jnp.bfloat16),
         ],
-        in_specs=[pl.BlockSpec(memory_space=pltpu.SMEM)]
-        + [pl.BlockSpec(memory_space=pltpu.VMEM)] * 6
-        + [pl.BlockSpec(memory_space=pltpu.HBM)] * 4,
+        in_specs=[pl.BlockSpec(memory_space=pltpu.HBM)] * len(operands),
         out_specs=[pl.BlockSpec(memory_space=pltpu.VMEM)] * 2,
-        scratch_shapes=[
-            pltpu.VMEM(fetched.shape, fetched.dtype),
-            pltpu.VMEM(pos_table.shape, pos_table.dtype),
-            pltpu.VMEM(w_qkv.shape, w_qkv.dtype),
-            pltpu.VMEM(w_out.shape, w_out.dtype),
-            pltpu.SemaphoreType.DMA((6,)),
-        ],
+        scratch_shapes=[pltpu.VMEM(operand.shape, operand.dtype) for operand in operands]
+        + [pltpu.SemaphoreType.DMA((len(operands) + 3,))],
         compiler_params=pltpu.CompilerParams(vmem_limit_bytes=60 * 1024 * 1024),
         cost_estimate=pl.CostEstimate(
             flops=2 * macs, bytes_accessed=6 * 1024 * 1024, transcendentals=0
         ),
         name="encode",
-    )(
-        lengths,
-        slots,
-        emb_gain[None],
-        emb_bias[None],
-        out_bias[None],
-        norm_gain[None],
-        norm_bias[None],
-        fetched,
-        pos_table,
-        w_qkv,
-        w_out,
-    )
+    )(*operands)
 
 
 def padded(rows):
@@ -164,9 +145,20 @@
 
 
 def route_kernel(
-    sizes, token_ids, owners, row_slot, plan, token_slot, code
+    sizes, token_ids_far, owners_far, row_slot_far, plan, token_slot_far, code, *near
 ):
     peers, vocab_rows, token_cap, row_cap, pooled = sizes
+    token_ids, owners, row_slot, token_slot, arrived = near
+    copies = [
+        pltpu.make_async_copy(source, target, arrived.at[at])
+        for at, (source, target) in enumerate(
+            ((token_ids_far, token_ids), (owners_far, owners), (row_slot_far, row_slot))
+        )
+    ]
+    for copy in copies:
+        copy.start()
+    for copy in copies:
+        copy.wait()
     ids = jnp.concatenate([token_ids[p : p + 1, :] for p in range(token_ids.shape[0])], axis=1)
     tokens, rows = ids.shape[1], owners.shape[1]
     count = tokens + rows
@@ -202,6 +194,9 @@
         plan[p, :, :rows] = code[...]
         plan[p, :, rows:] = filled[p : p + 1]
     token_slot[...] = down[:tokens] * token_cap + rank_col[:tokens]
+    send = pltpu.make_async_copy(token_slot, token_slot_far, arrived.at[3])
+    send.start()
+    send.wait()
 
 
 def route(token_ids, owners, row_slot, sizes):
@@ -216,16 +211,41 @@
             ints(passes * seq_len, 1),
             ints(1, rows),
         ],
-        in_specs=[pl.BlockSpec(memory_space=pltpu.VMEM)] * 3,
-        out_specs=[pl.BlockSpec(memory_space=pltpu.VMEM)] * 3,
+        in_specs=[pl.BlockSpec(memory_space=pltpu.HBM)] * 3,
+        out_specs=[
+            pl.BlockSpec(memory_space=pltpu.VMEM),
+            pl.BlockSpec(memory_space=pltpu.HBM),
+            pl.BlockSpec(memory_space=pltpu.VMEM),
+        ],
+        scratch_shapes=[
+            pltpu.VMEM(token_ids.shape, jnp.int32),
+            pltpu.VMEM(owners.shape, jnp.int32),
+            pltpu.VMEM(row_slot.shape, jnp.int32),
+            pltpu.VMEM((passes * seq_len, 1), jnp.int32),
+            pltpu.SemaphoreType.DMA((4,)),
+        ],
         name="route",
     )(token_ids, owners, row_slot)
 
 
-def pack_kernel(half, row_cap, count, picks, codes_a, codes_b, rows_a, rows_b, *outs):
+def pack_kernel(half, row_cap, count, picks, pieces, *refs):
     me = lax.axis_index("dp")
+    far, refs = refs[: 2 + 2 * pieces], refs[2 + 2 * pieces :]
+    near, arrived = refs[-3 - 2 * pieces : -1], refs[-1]
+    outs, codes_a, codes_b = refs[: -3 - 2 * pieces], near[0], near[1]
     slot_count = len(outs) * row_cap
-    for source, (codes, rows) in enumerate(((codes_a, rows_a), (codes_b, rows_b))):
+    code_copies = [
+        pltpu.make_async_copy(far[0], codes_a, arrived.at[0]),
+        pltpu.make_async_copy(far[1], codes_b, arrived.at[1]),
+    ]
+    row_copies = [
+        pltpu.make_async_copy(far[at], near[at], arrived.at[at]) for at in range(2, len(far))
+    ]
+    for copy in code_copies + row_copies:
+        copy.start()
+    for copy in code_copies:
+        copy.wait()
+    for source, codes in enumerate((codes_a, codes_b)):
         if picks is None:
             code = codes[...]
         else:
@@ -234,10 +254,17 @@
         owner, rank = code >> bits, code & (2**bits - 1)
         fits = ((owner ^ me) & (1 | half)) == 0
         chip = ((owner ^ me) & (half - 1)) >> 1
-        slot = jnp.where(fits, chip * row_cap + rank, -1)[:, : rows.shape[0]]
-        spot = lax.broadcasted_iota(jnp.int32, (slot_count, rows.shape[0]), 0)
-        table = jnp.where(slot == spot, 1.0, 0.0).astype(jnp.bfloat16)
-        packed = jnp.dot(table, rows[...], preferred_element_type=jnp.float32)
+        slot = jnp.where(fits, chip * row_cap + rank, -1)
+        packed, at = 0.0, 0
+        for piece in range(source * pieces, (source + 1) * pieces):
+            rows = near[2 + piece]
+            spot = lax.broadcasted_iota(jnp.int32, (slot_count, rows.shape[0]), 0)
+            table = jnp.where(slot[:, at : at + rows.shape[0]] == spot, 1.0, 0.0)
+            row_copies[piece].wait()
+            packed += jnp.dot(
+                table.astype(jnp.bfloat16), rows[...], preferred_element_type=jnp.float32
+            )
+            at += rows.shape[0]
         packed = packed.astype(jnp.bfloat16)
         for step, out in enumerate(outs):
             if source == 0 and out.shape[0] > 2 * row_cap:
@@ -248,21 +275,28 @@
 
 
 def pack_rows(codes_a, codes_b, rows_a, rows_b, half, row_cap, count, picks=None):
-    width = rows_a.shape[1]
+    width = rows_a[0].shape[1]
+    total = sum(piece.shape[0] for piece in rows_a)
+    pieces = len(rows_a)
     steps = half // 2
+    operands = (codes_a, codes_b, *rows_a, *rows_b)
     return pl.pallas_call(
-        functools.partial(pack_kernel, half, row_cap, count, picks),
+        functools.partial(pack_kernel, half, row_cap, count, picks, pieces),
         out_shape=[jax.ShapeDtypeStruct((padded(2 * row_cap), width), jnp.bfloat16)] * steps,
-        in_specs=[pl.BlockSpec(memory_space=pltpu.VMEM)] * 4,
+        in_specs=[pl.BlockSpec(memory_space=pl.ANY)] * len(operands),
         out_specs=[pl.BlockSpec(memory_space=pltpu.VMEM)] * steps,
-        compiler_params=pltpu.CompilerParams(vmem_limit_bytes=60 * 1024 * 1024),
+        scratch_shapes=[
+            *(pltpu.VMEM(operand.shape, operand.dtype) for operand in operands),
+            pltpu.SemaphoreType.DMA((len(operands),)),
+        ],
+        compiler_params=pltpu.CompilerParams(vmem_limit_bytes=20 * 1024 * 1024),
         cost_estimate=pl.CostEstimate(
-            flops=4 * steps * row_cap * width * rows_a.shape[0],
-            bytes_accessed=4 * width * (rows_a.shape[0] + steps * row_cap),
+            flops=4 * steps * row_cap * width * total,
+            bytes_accessed=4 * width * (total + steps * row_cap),
             transcendentals=0,
         ),
         name="pack",
-    )(codes_a, codes_b, rows_a, rows_b)
+    )(*operands)
 
 
 def onehot(where_to, first, count):
@@ -273,22 +307,29 @@
 BLOCK = 128
 
 
-def early_kernel(places, centroids_far, *rest):
-    pieces, (out_far, share, rows, centroids, out, arrived, left) = rest[:-7], rest[-7:]
+def early_kernel(places_far, centroids_far, *rest):
+    pieces, (out_far, share_far, places, rows, centroids, out, share, arrived, left) = rest[:-9], rest[-9:]
     size = pieces[0].shape[0]
-    count = centroids.shape[0]
-    copies = []
+    steps = centroids.shape[0] // BLOCK
+    copies = [pltpu.make_async_copy(places_far, places, arrived.at[0])]
     for at, piece in enumerate(pieces):
         copies.append(
-            pltpu.make_async_copy(piece, rows.at[pl.ds(at * size, size)], arrived.at[at])
-        )
-    copies.append(pltpu.make_async_copy(centroids_far, centroids, arrived.at[len(pieces)]))
-    for copy in copies:
+            pltpu.make_async_copy(piece, rows.at[pl.ds(at * size, size)], arrived.at[1 + at])
+        )
+    loads = []
+    for step in range(steps):
+        block = pl.ds(step * BLOCK, BLOCK)
+        loads.append(
+            pltpu.make_async_copy(
+                centroids_far.at[block], centroids.at[block], arrived.at[1 + len(pieces) + step]
+            )
+        )
+    for copy in copies + loads:
         copy.start()
     for copy in copies:
         copy.wait()
     sends = []
-    for step in range(count // BLOCK):
+    for step in range(steps):
         block = pl.ds(step * BLOCK, BLOCK)
         hot = onehot(places[...], step * BLOCK, BLOCK)
         counts = jnp.sum(hot, axis=1, keepdims=True)
@@ -298,40 +339,48 @@
             rows[...],
             preferred_element_type=jnp.float32,
         )
+        loads[step].wait()
         out[block, :] = jnp.where(counts > 0, sums * scale, centroids[block, :])
         share[block, :] = jnp.broadcast_to(scale, (BLOCK, share.shape[1]))
         sends.append(pltpu.make_async_copy(out.at[block], out_far.at[block], left.at[step]))
         sends[-1].start()
+    sends.append(pltpu.make_async_copy(share, share_far, left.at[steps]))
+    sends[-1].start()
     for send in sends:
         send.wait()
 
 
-def late_kernel(places, late, spread, share, early_far, *rest):
-    pieces, (out_far, rows, early, out, arrived, left) = rest[:-6], rest[-6:]
+def late_kernel(places_far, late_far, spread_far, share_far, early_far, *rest):
+    pieces, rest = rest[:-10], rest[-10:]
+    out_far, places, late, spread, share, rows, early, out, arrived, left = rest
     size, passes = pieces[0].shape[0], spread.shape[1]
-    count = early.shape[0]
-    steps = count // BLOCK
-    loads = []
+    steps = early.shape[0] // BLOCK
+    loads = [
+        pltpu.make_async_copy(source, target, arrived.at[at])
+        for at, (source, target) in enumerate(
+            ((places_far, places), (late_far, late), (spread_far, spread), (share_far, share))
+        )
+    ]
     for at, piece in enumerate(pieces):
         loads.append(
-            pltpu.make_async_copy(piece, rows.at[pl.ds(at * size, size)], arrived.at[at])
+            pltpu.make_async_copy(piece, rows.at[pl.ds(at * size, size)], arrived.at[4 + at])
         )
     starts = []
     for step in range(steps):
         block = pl.ds(step * BLOCK, BLOCK)
         starts.append(
             pltpu.make_async_copy(
-                early_far.at[block], early.at[block], arrived.at[len(pieces) + step]
+                early_far.at[block], early.at[block], arrived.at[len(loads) + step]
             )
         )
     for copy in loads + starts:
         copy.start()
+    for copy in loads:
+        copy.wait()
     top = len(pieces) * size
     for peer in range(spread.shape[0]):
         rows[top + peer * passes : top + (peer + 1) * passes, :] = spread[peer]
-    for copy in loads:
-        copy.wait()
-    where_to = jnp.concatenate([places[...], late[...]], axis=1)
+    where_to = jnp.concatenate([places[:, places.shape[1] - top :], late[...]], axis=1)
     sends = []
     for step in range(steps):
         block = pl.ds(step * BLOCK, BLOCK)
@@ -349,26 +398,26 @@
     centre_count, width = centroids.shape
     row_total = sum(piece.shape[0] for piece in pieces)
     wide = pltpu.VMEM(centroids.shape, jnp.float32)
+    thin = (centre_count, 128)
+    steps = centre_count // BLOCK
     return pl.pallas_call(
         early_kernel,
         out_shape=[
             jax.ShapeDtypeStruct(centroids.shape, jnp.float32),
-            jax.ShapeDtypeStruct((centre_count, 128), jnp.float32),
-        ],
-        in_specs=[pl.BlockSpec(memory_space=pltpu.VMEM)]
-        + [pl.BlockSpec(memory_space=pltpu.HBM)] * (1 + len(pieces)),
-        out_specs=[
-            pl.BlockSpec(memory_space=pltpu.HBM),
-            pl.BlockSpec(memory_space=pltpu.VMEM),
-        ],
+            jax.ShapeDtypeStruct(thin, jnp.float32),
+        ],
+        in_specs=[pl.BlockSpec(memory_space=pl.ANY)] * (2 + len(pieces)),
+        out_specs=[pl.BlockSpec(memory_space=pltpu.HBM)] * 2,
         scratch_shapes=[
+            pltpu.VMEM(places.shape, jnp.int32),
             pltpu.VMEM((row_total, width), jnp.bfloat16),
             wide,
             wide,
-            pltpu.SemaphoreType.DMA((len(pieces) + 1,)),
-            pltpu.SemaphoreType.DMA((centre_count // BLOCK,)),
-        ],
-        compiler_params=pltpu.CompilerParams(vmem_limit_bytes=60 * 1024 * 1024),
+            pltpu.VMEM(thin, jnp.float32),
+            pltpu.SemaphoreType.DMA((1 + len(pieces) + steps,)),
+            pltpu.SemaphoreType.DMA((steps + 1,)),
+        ],
+        compiler_params=pltpu.CompilerParams(vmem_limit_bytes=20 * 1024 * 1024),
         cost_estimate=pl.CostEstimate(
             flops=2 * centre_count * width * row_total,
             bytes_accessed=8 * centre_count * width,
@@ -380,20 +429,23 @@
 
 def late_update(places, late, spread, share, early, pieces):
     centre_count, width = early.shape
-    row_total = places.shape[1] + late.shape[1]
+    row_total = places.shape[1] // 2 + late.shape[1]
     wide = pltpu.VMEM(early.shape, jnp.float32)
     steps = centre_count // BLOCK
     return pl.pallas_call(
         late_kernel,
         out_shape=jax.ShapeDtypeStruct(early.shape, jnp.float32),
-        in_specs=[pl.BlockSpec(memory_space=pltpu.VMEM)] * 4
-        + [pl.BlockSpec(memory_space=pltpu.HBM)] * (1 + len(pieces)),
+        in_specs=[pl.BlockSpec(memory_space=pltpu.HBM)] * (5 + len(pieces)),
         out_specs=pl.BlockSpec(memory_space=pltpu.HBM),
         scratch_shapes=[
+            pltpu.VMEM(places.shape, jnp.int32),
+            pltpu.VMEM(late.shape, jnp.int32),
+            pltpu.VMEM(spread.shape, jnp.bfloat16),
+            pltpu.VMEM(share.shape, jnp.float32),
             pltpu.VMEM((row_total, width), jnp.bfloat16),
             wide,
             wide,
-            pltpu.SemaphoreType.DMA((len(pieces) + steps,)),
+            pltpu.SemaphoreType.DMA((4 + len(pieces) + steps,)),
             pltpu.SemaphoreType.DMA((steps,)),
         ],
         compiler_params=pltpu.CompilerParams(vmem_limit_bytes=60 * 1024 * 1024),
@@ -444,27 +496,33 @@
             got.append(lax.ppermute(blocks[step], "dp", moves))
         return got
 
-    partner_rows = lax.ppermute(stored_rows, "dp", across)
+    ahead = store_count * 3 // 4 // 16 * 16
+    first_rows = lax.ppermute(stored_rows[:ahead], "dp", across)
     sibling_rows = lax.ppermute(stored_rows, "dp", beside)
     sizes = (peer_count, vocab_rows, token_cap, row_cap, row_count - store_count)
     plan, token_slot, code = route(token_ids, row_owner.reshape(1, row_count), row_slot[None], sizes)
     sibling_code = lax.ppermute(code, "dp", beside)
-    blocks = pack_rows(code, sibling_code, stored_rows, sibling_rows, half, row_cap, row_count)
+    blocks = pack_rows(code, sibling_code, [stored_rows], [sibling_rows], half, row_cap, row_count)
     plan, *blocks = lax.optimization_barrier((plan, *blocks))
     own_half = hand_on(blocks)
     codes = lax.all_to_all(plan, "dp", split_axis=0, concat_axis=0, tiled=True)
     plan = codes[:, 0, row_count:]
+    rest, plan = lax.optimization_barrier((stored_rows[ahead:], plan))
+    last_rows = lax.ppermute(rest, "dp", across)
     wanted = plan[:, :token_cap].reshape(peer_count * token_cap)
     chosen = wanted[:, None] == jnp.arange(vocab_rows, dtype=jnp.int32)[None, :]
     found = jnp.dot(
         chosen.astype(jnp.bfloat16), word_table, preferred_element_type=jnp.float32
     ).astype(jnp.bfloat16)
-    found, partner_rows, own_half = lax.optimization_barrier((found, partner_rows, own_half))
+    found, first_rows, own_half[:3] = lax.optimization_barrier(
+        (found, first_rows, own_half[:3])
+    )
     fetched = lax.all_to_all(
         found.reshape(peer_count, token_cap, width), "dp", split_axis=0, concat_axis=0, tiled=True
     ).reshape(peer_count * token_cap, width)
 
-    far_rows = lax.ppermute(partner_rows, "dp", beside)
+    partner_rows = [first_rows, last_rows]
+    far_rows = [lax.ppermute(rows, "dp", beside) for rows in partner_rows]
     picks = (half, half ^ 1)
     blocks = pack_rows(codes, codes, partner_rows, far_rows, half, row_cap, row_count, picks)
     other_half = hand_on(blocks)
@@ -473,8 +531,10 @@
     spare = padded(2 * row_cap) - 2 * row_cap
     got_places = jnp.pad(got_places, ((0, 0), (0, spare)), constant_values=-1).reshape(1, -1)
     means, share = early_update(got_places, centroids, own_half)
-    fetched, means, share = lax.optimization_barrier((fetched, means, share))
     late_places = plan[:, token_cap + row_cap :].reshape(1, -1)
+    fetched, means, share, got_places, late_places = lax.optimization_barrier(
+        (fetched, means, share, got_places, late_places)
+    )
 
     passage_embed, spread = encode(
         peer_count,
@@ -493,8 +553,7 @@
     all_embeds = lax.all_to_all(
         spread, "dp", split_axis=0, concat_axis=0, tiled=True
     )
-    other_places = got_places[:, got_places.shape[1] // 2 :]
-    new_centroids = late_update(other_places, late_places, all_embeds, share, means, other_half)
+    new_centroids = late_update(got_places, late_places, all_embeds, share, means, other_half)
     return (passage_embed, new_centroids)
 
 

time: 87 us -> 98.5 us (1.13)
  local copies, waits for them, and re-layouts: 6.41 us -> 14.1 us
  waiting for transfers between devices: 30.1 us -> 35 us
  Pallas kernels: 22 us -> 17.6 us
  starting transfers between devices: 25.8 us -> 29.2 us
    ppermute x2 -> x4, waiting for transfers between devices: 0.24 us -> 22.8 us  [the longest x1 22.8 us: shards(): last_rows = lax.ppermute(rest, 'dp', across)]
    all_to_all x1, waiting for transfers between devices: 11 us -> 1.59 us  [shards(): codes = lax.all_to_all(plan, 'dp', split_axis=0, concat_axis=0, tiled=True)]
    all_to_all x1, waiting for transfers between devices: 5.26 us -> 0.01 us  [shards(): lax.all_to_all(found.reshape(peer_count, token_cap, width), 'dp', split_a...]
    ppermute x6, waiting for transfers between devices: 6.92 us -> 2.54 us  [hand_on(): got.append(lax.ppermute(blocks[step], 'dp', moves))]
    unnamed x30, local copies, waits for them, and re-layouts: 3.69 us -> 8.01 us
    slice x1 -> x2, local copies, waits for them, and re-layouts: 0.59 us -> 3.33 us  [the longest x1 1.74 us: shards(): first_rows = lax.ppermute(stored_rows[:ahead], 'dp', across)]
    ppermute x2 -> x4, starting transfers between devices: 4.07 us -> 6.5 us  [the longest x1 3.65 us: shards(): first_rows = lax.ppermute(stored_rows[:ahead], 'dp', across)]
    ppermute x6, starting transfers between devices: 7.04 us -> 9.24 us  [hand_on(): got.append(lax.ppermute(blocks[step], 'dp', moves))]
  transfers between devices with their start and end apart: 13 -> 15, of which waited for: 7 -> 6; matrix products, arithmetic and copies ran while one was open for 5% -> 8% of each run, Pallas kernels for 20% -> 14%
where the time goes in v8:
time: 98.5 us; the launch traced here: 98 us
  waiting for transfers between devices  35 us (36%)
  starting transfers between devices  29.2 us (30%)
  Pallas kernels  17.6 us (18%)
  local copies, waits for them, and re-layouts  14.1 us (14%)
  matrix products  1.29 us (1%)
    ppermute x1, waiting for transfers between devices, shards(): last_rows = lax.ppermute(rest, 'dp', across)  22.8 us
    ppermute x6, starting transfers between devices, hand_on(): got.append(lax.ppermute(blocks[step], 'dp', moves))  9.24 us
    unnamed x30, local copies, waits for them, and re-layouts  8.01 us
    all_to_all x1, waiting for transfers between devices, shards(): lax.all_to_all(spread, 'dp', split_axis=0, concat_axis=0, tiled=True)  6.85 us
    all_to_all x1, starting transfers between devices, shards(): lax.all_to_all(found.reshape(peer_count, token_cap, width), 'dp', split_a...  4.99 us
    pallas_call x1, Pallas kernels, encode(): pl.pallas_call(encode_kernel, out_shape=[jax.ShapeDtypeStruct((passes, wi...  4.99 us
    all_to_all x1, starting transfers between devices, shards(): codes = lax.all_to_all(plan, 'dp', split_axis=0, concat_axis=0, tiled=True)  3.91 us
    all_to_all x1, starting transfers between devices, shards(): lax.all_to_all(spread, 'dp', split_axis=0, concat_axis=0, tiled=True)  3.8 us
  transfers between devices with their start and end apart: 15, of which 6 were waited for; matrix products, arithmetic and copies ran while one was open for 8% of the time, Pallas kernels for 14%

profile of v8, /device:TPU:0, one launch (start us, length us, event | category | flops | bytes accessed | tf_op | source)
XLA Modules:
  0.0 98.0 jit_solution(7662866960132769200)
XLA Ops:
  0.6 0.0 copy-start
  0.6 0.5 collective-permute-start.1
  1.2 1.7 %slice.21 = bf16[176,1024]{1,0:T(8,128)(2,1)} slice(bf16[254,1024]{1,0:T(8,128)(2,1)} %refs_2_.1), slice={[0:176], [0:1024]} | slice | bytes 720896 | tf_op jit(solution)/shard_map/slice | solution.py:500
  2.9 3.7 %collective-permute-start.2 = (bf16[176,1024]{1,0:T(8,128)(2,1)}, bf16[176,1024]{1,0:T(8,128)(2,1)S(1)}, u32[]{:S(2)}, u32[]{:S(2)}) collective-permute-start(bf16[176,1024]{1,0:T(8,128)(2,1)} %slice.21), channel_id=1, source_target_pairs={{0,8},{1,9},{2,10},{3,11},{4,12},{5,13},{6,14},{7,15},{8,0},{9,1},... | collective-permute-start | bytes 1081352 | tf_op jit(solution)/shard_map/ppermute | solution.py:500
  6.6 2.3 %route.1 = (s32[16,1,330]{2,1,0:T(1,128)}, s32[128,1]{1,0:T(8,128)}, s32[1,256]{1,0:T(1,128)}) custom-call(s32[2,64]{1,0:T(2,128)} %token_ids_far.1, s32[1,256]{1,0:T(1,128)} %bitcast.24, s32[1,256]{1,0:T(1,128)} %bitcast.25), custom_call_target="tpu_custom_call" | custom-call | tf_op jit(solution)/shard_map/route/pallas_call | solution.py:207
  8.8 0.2 collective-permute-start
  9.1 1.2 %collective-permute-done.refs_1_ = s32[1,256]{1,0:T(1,128)S(1)} collective-permute-done((s32[1,256]{1,0:T(1,128)}, s32[1,256]{1,0:T(1,128)S(1)}, u32[]{:S(2)}, u32[]{:S(2)}) %collective-permute-start) | collective-permute-done | bytes 1056 | tf_op jit(solution)/shard_map/ppermute | solution.py:504
  10.3 0.0 collective-permute-done.1.refs_3_
  10.3 1.0 %copy-done.3 = bf16[254,1024]{1,0:T(8,128)(2,1)S(1)} copy-done((bf16[254,1024]{1,0:T(8,128)(2,1)S(1)}, bf16[254,1024]{1,0:T(8,128)(2,1)}, u32[]{:S(2)}) %copy-start.3) | copy-done | bytes 520216
  11.3 0.7 copy-done.9
  12.0 0.7 pack.2
  12.7 0.0 copy-start.10
  12.7 0.7 copy-done.10
  13.4 0.7 copy-done.11
  14.1 0.7 copy-done.12
  14.7 3.9 %all-to-all-start = ((s32[16,1,330]{2,1,0:T(1,128)}), s32[16,1,330]{2,1,0:T(1,128)S(1)}, u32[]{:S(2)}, u32[]{:S(2)}) async-start(s32[16,1,330]{2,1,0:T(1,128)} %get-tuple-element.41), calls=%async_computation | async-start | bytes 49152 | tf_op jit(solution)/shard_map/all_to_all | solution.py:508
  18.7 1.6 %slice.18 = bf16[78,1024]{1,0:T(8,128)(2,1)} slice(bf16[254,1024]{1,0:T(8,128)(2,1)} %refs_2_.1), slice={[176:254], [0:1024]} | slice | bytes 319488 | tf_op jit(solution)/shard_map/slice | solution.py:510
  20.2 1.9 %collective-permute-start.3 = (bf16[96,1024]{1,0:T(8,128)(2,1)}, bf16[96,1024]{1,0:T(8,128)(2,1)S(1)}, u32[]{:S(2)}, u32[]{:S(2)}) collective-permute-start(bf16[96,1024]{1,0:T(8,128)(2,1)} %copy-done.12), channel_id=1, source_target_pairs={{0,2},{1,3},{2,0},{3,1},{4,6},{5,7},{6,4},{7,5},{8,10},{9,11},{10,... | collective-permute-start | bytes 589832 | tf_op jit(solution)/shard_map/ppermute | solution.py:496
  22.2 1.5 %collective-permute-start.4 = (bf16[96,1024]{1,0:T(8,128)(2,1)}, bf16[96,1024]{1,0:T(8,128)(2,1)}, u32[]{:S(2)}, u32[]{:S(2)}) collective-permute-start(bf16[96,1024]{1,0:T(8,128)(2,1)} %copy-done.11), channel_id=1, source_target_pairs={{0,4},{1,5},{2,6},{3,7},{4,0},{5,1},{6,2},{7,3},{8,12},{9,13},{10,... | collective-permute-start | bytes 589832 | tf_op jit(solution)/shard_map/ppermute | solution.py:496
  23.6 1.6 %all-to-all-done.refs_0_.refs_1_ = s32[16,1,330]{2,1,0:T(1,128)S(1)} async-done(((s32[16,1,330]{2,1,0:T(1,128)}), s32[16,1,330]{2,1,0:T(1,128)S(1)}, u32[]{:S(2)}, u32[]{:S(2)}) %all-to-all-start) | async-done | bytes 21152 | tf_op jit(solution)/shard_map/all_to_all | solution.py:508
  25.2 0.1 eq.15
  25.3 0.0 copy-done
  25.3 1.3 %convolution_convert_fusion = bf16[384,1024]{1,0:T(8,128)(2,1)} fusion(bf16[240,1024]{1,0:T(8,128)(2,1)S(1)} %copy-done, s32[384]{0:T(512)S(1)} %eq.15), kind=kOutput, calls=%fused_computation.1 | convolution fusion | flops 189229056 | bytes 1279488 | tf_op jit(solution)/shard_map/dot_general | solution.py:514
  26.6 0.0 collective-permute-done.2.refs_2_
  26.6 1.2 %collective-permute-done.3.rest_1_ = bf16[96,1024]{1,0:T(8,128)(2,1)S(1)} collective-permute-done((bf16[96,1024]{1,0:T(8,128)(2,1)}, bf16[96,1024]{1,0:T(8,128)(2,1)S(1)}, u32[]{:S(2)}, u32[]{:S(2)}) %collective-permute-start.3) | collective-permute-done | bytes 196640 | tf_op jit(solution)/shard_map/ppermute | solution.py:496
  27.8 1.3 %collective-permute-done.4.rest_2_ = bf16[96,1024]{1,0:T(8,128)(2,1)} collective-permute-done((bf16[96,1024]{1,0:T(8,128)(2,1)}, bf16[96,1024]{1,0:T(8,128)(2,1)}, u32[]{:S(2)}, u32[]{:S(2)}) %collective-permute-start.4) | collective-permute-done | bytes 196640 | tf_op jit(solution)/shard_map/ppermute | solution.py:496
  29.2 5.0 %all-to-all-start.1 = ((bf16[16,24,1024]{2,1,0:T(8,128)(2,1)}), bf16[16,24,1024]{2,1,0:T(8,128)(2,1)}, u32[]{:S(2)}, u32[]{:S(2)}) async-start(bf16[16,24,1024]{2,1,0:T(8,128)(2,1)} %bitcast.15), calls=%async_computation.1 | async-start | bytes 1572864 | tf_op jit(solution)/shard_map/all_to_all | solution.py:520
  34.2 0.0 copy-done.6
  34.2 2.8 %collective-permute-start.6 = (bf16[78,1024]{1,0:T(8,128)(2,1)}, bf16[78,1024]{1,0:T(8,128)(2,1)}, u32[]{:S(2)}, u32[]{:S(2)}) collective-permute-start(bf16[78,1024]{1,0:T(8,128)(2,1)} %slice.18), channel_id=1, source_target_pairs={{0,8},{1,9},{2,10},{3,11},{4,12},{5,13},{6,14},{7,15},{8,0},{9,1},... | collective-permute-start | bytes 479240 | tf_op jit(solution)/shard_map/ppermute | solution.py:511
  37.0 0.0 collective-permute-start.7
  37.0 2.4 %collective-permute-start.5 = (bf16[96,1024]{1,0:T(8,128)(2,1)}, bf16[96,1024]{1,0:T(8,128)(2,1)}, u32[]{:S(2)}, u32[]{:S(2)}) collective-permute-start(bf16[96,1024]{1,0:T(8,128)(2,1)} %copy-done.10), channel_id=1, source_target_pairs={{0,6},{1,7},{2,4},{3,5},{4,2},{5,3},{6,0},{7,1},{8,14},{9,15},{10,... | collective-permute-start | bytes 589832 | tf_op jit(solution)/shard_map/ppermute | solution.py:496
  39.4 22.8 %collective-permute-done.6.refs_3_ = bf16[78,1024]{1,0:T(8,128)(2,1)} collective-permute-done((bf16[78,1024]{1,0:T(8,128)(2,1)}, bf16[78,1024]{1,0:T(8,128)(2,1)}, u32[]{:S(2)}, u32[]{:S(2)}) %collective-permute-start.6) | collective-permute-done | bytes 159776 | tf_op jit(solution)/shard_map/ppermute | solution.py:511
  62.2 0.0 collective-permute-start.8
  62.2 0.7 slice.23
  62.9 0.1 slice.22
  62.9 1.3 %reshape.42.late_far = s32[1,32]{1,0:T(1,128)} reshape(s32[16,2]{1,0:T(8,128)} %slice.23) | data formatting | bytes 256 | tf_op jit(solution)/shard_map/reshape | solution.py:534
  64.2 0.6 gather_fusion
  64.8 0.1 reshape.41.places_far
  64.9 0.0 copy-start.8
  64.9 0.0 collective-permute-done.8.refs_5_
  64.9 0.0 collective-permute-done.7.refs_4_
  64.9 2.8 %pack.3 = (bf16[96,1024]{1,0:T(8,128)(2,1)S(1)}, bf16[96,1024]{1,0:T(8,128)(2,1)}, bf16[96,1024]{1,0:T(8,128)(2,1)}, bf16[96,1024]{1,0:T(8,128)(2,1)}) custom-call(s32[16,1,330]{2,1,0:T(1,128)S(1)} %all-to-all-done.refs_0_.refs_1_, s32[16,1,330]{2,1,0:T(1,128)S(1)} %all-to-all-done.refs_0_.refs_1_, bf16[176,1024]{1,0:T(8,128)(2,1)S(1)} %collective-permute-done.2.refs_2_, ...), custom_call_target="tpu_custom_call" | custom-call | flops 199753728 | bytes 1826816 | tf_op jit(solution)/shard_map/pack/pallas_call | solution.py:283
  67.7 0.0 copy-start.5
  67.7 0.7 copy-done.5
  68.4 1.5 %collective-permute-start.9 = (bf16[96,1024]{1,0:T(8,128)(2,1)}, bf16[96,1024]{1,0:T(8,128)(2,1)S(1)}, u32[]{:S(2)}, u32[]{:S(2)}) collective-permute-start(bf16[96,1024]{1,0:T(8,128)(2,1)} %get-tuple-element.63), channel_id=1, source_target_pairs={{0,2},{1,3},{2,0},{3,1},{4,6},{5,7},{6,4},{7,5},{8,10},{9,11},{10,... | collective-permute-start | bytes 589832 | tf_op jit(solution)/shard_map/ppermute | solution.py:496
  69.9 0.0 collective-permute-start.10
  69.9 2.0 %collective-permute-start.11 = (bf16[96,1024]{1,0:T(8,128)(2,1)}, bf16[96,1024]{1,0:T(8,128)(2,1)}, u32[]{:S(2)}, u32[]{:S(2)}) collective-permute-start(bf16[96,1024]{1,0:T(8,128)(2,1)} %get-tuple-element.65), channel_id=1, source_target_pairs={{0,6},{1,7},{2,4},{3,5},{4,2},{5,3},{6,0},{7,1},{8,14},{9,15},{10,... | collective-permute-start | bytes 589832 | tf_op jit(solution)/shard_map/ppermute | solution.py:496
  71.8 0.0 collective-permute-done.5.rest_3_
  71.8 0.0 copy-done.1
  71.8 0.9 copy-done.7
  72.8 3.3 %early.1 = (f32[512,1024]{1,0:T(8,128)S(1)}, f32[512,128]{1,0:T(8,128)S(1)}) custom-call(s32[1,768]{1,0:T(1,128)S(1)} %reshape.41.places_far, f32[512,1024]{1,0:T(8,128)S(1)} %copy-done.1, bf16[96,1024]{1,0:T(8,128)(2,1)S(1)} %get-tuple-element.47.rest_0_, bf16[96,1024]{1,0:T(8,128)(2,1)S(1)} %copy-done.7, bf16[96,1024]{1,0:T(8,128)(2,1)} %collective-permute-done.4.rest_2_, ...), custom_call_target="tpu_custom_call" | custom-call | flops 402653184 | bytes 4194304 | tf_op jit(solution)/shard_map/early/pallas_call | solution.py:403
  76.0 0.0 copy-start.2
  76.1 1.3 %copy-done.2 = f32[512,1024]{1,0:T(8,128)} copy-done((f32[512,1024]{1,0:T(8,128)}, f32[512,1024]{1,0:T(8,128)S(1)}, u32[]{:S(2)}) %copy-start.2) | copy-done | bytes 2097176
  77.4 0.7 copy-done.4
  78.1 0.0 all-to-all-done.1
  78.1 5.0 %encode.1 = (bf16[2,1024]{1,0:T(2,128)(2,1)}, bf16[16,2,1024]{2,1,0:T(2,128)(2,1)}) custom-call(s32[1,2]{1,0:T(1,128)} %bitcast.26, s32[128,1]{1,0:T(8,128)} %get-tuple-element.34.refs_1_, bf16[384,1024]{1,0:T(8,128)(2,1)} %bitcast.5.refs_2_, bf16[64,1024]{1,0:T(8,128)(2,1)} %refs_3_.1, f32[1,1024]{1,0:T(1,128)} %bitcast.19, f32[1,1024]{1,0:T(1,128)} %bitcast.20, ...), custom_call_target="tpu_custom_call" | custom-call | flops 637534208 | bytes 6291456 | tf_op jit(solution)/shard_map/encode/pallas_call | solution.py:121
  83.1 0.0 copy-done.8
  83.1 3.8 %all-to-all-start.2 = ((bf16[16,2,1024]{2,1,0:T(2,128)(2,1)}), bf16[16,2,1024]{2,1,0:T(2,128)(2,1)S(1)}, u32[]{:S(2)}, u32[]{:S(2)}) async-start(bf16[16,2,1024]{2,1,0:T(2,128)(2,1)} %get-tuple-element.57), calls=%async_computation.2 | async-start | bytes 131072 | tf_op jit(solution)/shard_map/all_to_all | solution.py:553
  86.9 0.0 collective-permute-done.9.rest_1_
  86.9 0.0 collective-permute-done.10.rest_2_
  86.9 0.0 collective-permute-done.11.rest_3_
  87.0 6.9 %all-to-all-done.2.spread_far = bf16[16,2,1024]{2,1,0:T(2,128)(2,1)S(1)} async-done(((bf16[16,2,1024]{2,1,0:T(2,128)(2,1)}), bf16[16,2,1024]{2,1,0:T(2,128)(2,1)S(1)}, u32[]{:S(2)}, u32[]{:S(2)}) %all-to-all-start.2) | async-done | bytes 65568 | tf_op jit(solution)/shard_map/all_to_all | solution.py:553
  93.8 0.6 copy-done.13
  94.4 3.5 %late.1 = f32[512,1024]{1,0:T(8,128)} custom-call(s32[1,768]{1,0:T(1,128)} %copy-done.8, s32[1,32]{1,0:T(1,128)} %reshape.42.late_far, bf16[16,2,1024]{2,1,0:T(2,128)(2,1)} %copy-done.13, f32[512,128]{1,0:T(8,128)} %copy-done.4, f32[512,1024]{1,0:T(8,128)} %copy-done.2, bf16[96,1024]{1,0:T(8,128)(2,1)} %copy-done.5, bf16[96,1024]{1,0:T(8,128)(2,1)} %copy-done.14, ...), custom_call_target="tpu_custom_call" | custom-call | flops 436207616 | bytes 4194304 | tf_op jit(solution)/shard_map/late/pallas_call | solution.py:435
  (14 shorter events, 0.0 us)
Async XLA Ops:
  0.6 24.7 %copy-start = (bf16[240,1024]{1,0:T(8,128)(2,1)S(1)}, bf16[240,1024]{1,0:T(8,128)(2,1)}, u32[]{:S(2)}) copy-start(bf16[240,1024]{1,0:T(8,128)(2,1)} %param.17) | copy-start | bytes 1474564
  0.6 9.6 %collective-permute-start.1 = (bf16[254,1024]{1,0:T(8,128)(2,1)}, bf16[254,1024]{1,0:T(8,128)(2,1)S(1)}, u32[]{:S(2)}, u32[]{:S(2)}) collective-permute-start(bf16[254,1024]{1,0:T(8,128)(2,1)} %refs_2_.1), channel_id=1, source_target_pairs={{0,1},{1,0},{2,3},{3,2},{4,5},{5,4},{6,7},{7,6},{8,9},{9,8},{10,11... | collective-permute-start | bytes 1560584 | tf_op jit(solution)/shard_map/ppermute | solution.py:501
  2.9 23.7 %collective-permute-start.2 = (bf16[176,1024]{1,0:T(8,128)(2,1)}, bf16[176,1024]{1,0:T(8,128)(2,1)S(1)}, u32[]{:S(2)}, u32[]{:S(2)}) collective-permute-start(bf16[176,1024]{1,0:T(8,128)(2,1)} %slice.21), channel_id=1, source_target_pairs={{0,8},{1,9},{2,10},{3,11},{4,12},{5,13},{6,14},{7,15},{8,0},{9,1},... | collective-permute-start | bytes 1081352 | tf_op jit(solution)/shard_map/ppermute | solution.py:500
  8.8 1.4 %collective-permute-start = (s32[1,256]{1,0:T(1,128)}, s32[1,256]{1,0:T(1,128)S(1)}, u32[]{:S(2)}, u32[]{:S(2)}) collective-permute-start(s32[1,256]{1,0:T(1,128)} %get-tuple-element.36.refs_0_), channel_id=1, source_target_pairs={{0,1},{1,0},{2,3},{3,2},{4,5},{5,4},{6,7},{7,6},{8,9},{9,8},{10,11... | collective-permute-start | bytes 3080 | tf_op jit(solution)/shard_map/ppermute | solution.py:504
  10.3 1.0 %copy-start.3 = (bf16[254,1024]{1,0:T(8,128)(2,1)S(1)}, bf16[254,1024]{1,0:T(8,128)(2,1)}, u32[]{:S(2)}) copy-start(bf16[254,1024]{1,0:T(8,128)(2,1)} %refs_2_.1) | copy-start | bytes 1560580
  11.3 0.7 copy-start.9
  12.7 0.7 copy-start.10
  13.4 0.7 copy-start.11
  14.1 0.7 copy-start.12
  14.7 10.5 %all-to-all-start = ((s32[16,1,330]{2,1,0:T(1,128)}), s32[16,1,330]{2,1,0:T(1,128)S(1)}, u32[]{:S(2)}, u32[]{:S(2)}) async-start(s32[16,1,330]{2,1,0:T(1,128)} %get-tuple-element.41), calls=%async_computation | async-start | bytes 49152 | tf_op jit(solution)/shard_map/all_to_all | solution.py:508
  20.2 51.6 %copy-start.1 = (f32[512,1024]{1,0:T(8,128)S(1)}, f32[512,1024]{1,0:T(8,128)}, u32[]{:S(2)}) copy-start(f32[512,1024]{1,0:T(8,128)} %centroids_far.1) | copy-start | bytes 6291460
  20.2 7.6 %collective-permute-start.3 = (bf16[96,1024]{1,0:T(8,128)(2,1)}, bf16[96,1024]{1,0:T(8,128)(2,1)S(1)}, u32[]{:S(2)}, u32[]{:S(2)}) collective-permute-start(bf16[96,1024]{1,0:T(8,128)(2,1)} %copy-done.12), channel_id=1, source_target_pairs={{0,2},{1,3},{2,0},{3,1},{4,6},{5,7},{6,4},{7,5},{8,10},{9,11},{10,... | collective-permute-start | bytes 589832 | tf_op jit(solution)/shard_map/ppermute | solution.py:496
  22.2 7.0 %collective-permute-start.4 = (bf16[96,1024]{1,0:T(8,128)(2,1)}, bf16[96,1024]{1,0:T(8,128)(2,1)}, u32[]{:S(2)}, u32[]{:S(2)}) collective-permute-start(bf16[96,1024]{1,0:T(8,128)(2,1)} %copy-done.11), channel_id=1, source_target_pairs={{0,4},{1,5},{2,6},{3,7},{4,0},{5,1},{6,2},{7,3},{8,12},{9,13},{10,... | collective-permute-start | bytes 589832 | tf_op jit(solution)/shard_map/ppermute | solution.py:496
  27.8 6.3 %copy-start.6 = (bf16[96,1024]{1,0:T(8,128)(2,1)}, bf16[96,1024]{1,0:T(8,128)(2,1)S(1)}, u32[]{:S(2)}) copy-start(bf16[96,1024]{1,0:T(8,128)(2,1)S(1)} %collective-permute-done.3.rest_1_) | copy-start | bytes 589828
  29.2 48.9 %all-to-all-start.1 = ((bf16[16,24,1024]{2,1,0:T(8,128)(2,1)}), bf16[16,24,1024]{2,1,0:T(8,128)(2,1)}, u32[]{:S(2)}, u32[]{:S(2)}) async-start(bf16[16,24,1024]{2,1,0:T(8,128)(2,1)} %bitcast.15), calls=%async_computation.1 | async-start | bytes 1572864 | tf_op jit(solution)/shard_map/all_to_all | solution.py:520
  34.2 28.0 %collective-permute-start.6 = (bf16[78,1024]{1,0:T(8,128)(2,1)}, bf16[78,1024]{1,0:T(8,128)(2,1)}, u32[]{:S(2)}, u32[]{:S(2)}) collective-permute-start(bf16[78,1024]{1,0:T(8,128)(2,1)} %slice.18), channel_id=1, source_target_pairs={{0,8},{1,9},{2,10},{3,11},{4,12},{5,13},{6,14},{7,15},{8,0},{9,1},... | collective-permute-start | bytes 479240 | tf_op jit(solution)/shard_map/ppermute | solution.py:511
  37.0 27.9 %collective-permute-start.7 = (bf16[176,1024]{1,0:T(8,128)(2,1)S(1)}, bf16[176,1024]{1,0:T(8,128)(2,1)S(1)}, u32[]{:S(2)}, u32[]{:S(2)}) collective-permute-start(bf16[176,1024]{1,0:T(8,128)(2,1)S(1)} %collective-permute-done.2.refs_2_), channel_id=1, source_target_pairs={{0,1},{1,0},{2,3},{3,2},{4,5},{5,4},{6,7},{7,6},{8,9},{9,8},{10,11... | collective-permute-start | bytes 1081352 | tf_op jit(solution)/shard_map/ppermute | solution.py:525
  37.0 34.8 %collective-permute-start.5 = (bf16[96,1024]{1,0:T(8,128)(2,1)}, bf16[96,1024]{1,0:T(8,128)(2,1)}, u32[]{:S(2)}, u32[]{:S(2)}) collective-permute-start(bf16[96,1024]{1,0:T(8,128)(2,1)} %copy-done.10), channel_id=1, source_target_pairs={{0,6},{1,7},{2,4},{3,5},{4,2},{5,3},{6,0},{7,1},{8,14},{9,15},{10,... | collective-permute-start | bytes 589832 | tf_op jit(solution)/shard_map/ppermute | solution.py:496
  62.2 2.7 %collective-permute-start.8 = (bf16[78,1024]{1,0:T(8,128)(2,1)}, bf16[78,1024]{1,0:T(8,128)(2,1)}, u32[]{:S(2)}, u32[]{:S(2)}) collective-permute-start(bf16[78,1024]{1,0:T(8,128)(2,1)} %collective-permute-done.6.refs_3_), channel_id=1, source_target_pairs={{0,1},{1,0},{2,3},{3,2},{4,5},{5,4},{6,7},{7,6},{8,9},{9,8},{10,11... | collective-permute-start | bytes 479240 | tf_op jit(solution)/shard_map/ppermute | solution.py:525
  64.9 18.2 %copy-start.8 = (s32[1,768]{1,0:T(1,128)}, s32[1,768]{1,0:T(1,128)S(1)}, u32[]{:S(2)}) copy-start(s32[1,768]{1,0:T(1,128)S(1)} %reshape.41.places_far) | copy-start | bytes 9220
  67.7 0.7 copy-start.5
  68.4 18.6 %collective-permute-start.9 = (bf16[96,1024]{1,0:T(8,128)(2,1)}, bf16[96,1024]{1,0:T(8,128)(2,1)S(1)}, u32[]{:S(2)}, u32[]{:S(2)}) collective-permute-start(bf16[96,1024]{1,0:T(8,128)(2,1)} %get-tuple-element.63), channel_id=1, source_target_pairs={{0,2},{1,3},{2,0},{3,1},{4,6},{5,7},{6,4},{7,5},{8,10},{9,11},{10,... | collective-permute-start | bytes 589832 | tf_op jit(solution)/shard_map/ppermute | solution.py:496
  69.9 17.1 %collective-permute-start.10 = (bf16[96,1024]{1,0:T(8,128)(2,1)}, bf16[96,1024]{1,0:T(8,128)(2,1)}, u32[]{:S(2)}, u32[]{:S(2)}) collective-permute-start(bf16[96,1024]{1,0:T(8,128)(2,1)} %get-tuple-element.64), channel_id=1, source_target_pairs={{0,4},{1,5},{2,6},{3,7},{4,0},{5,1},{6,2},{7,3},{8,12},{9,13},{10,... | collective-permute-start | bytes 589832 | tf_op jit(solution)/shard_map/ppermute | solution.py:496
  69.9 17.1 %collective-permute-start.11 = (bf16[96,1024]{1,0:T(8,128)(2,1)}, bf16[96,1024]{1,0:T(8,128)(2,1)}, u32[]{:S(2)}, u32[]{:S(2)}) collective-permute-start(bf16[96,1024]{1,0:T(8,128)(2,1)} %get-tuple-element.65), channel_id=1, source_target_pairs={{0,6},{1,7},{2,4},{3,5},{4,2},{5,3},{6,0},{7,1},{8,14},{9,15},{10,... | collective-permute-start | bytes 589832 | tf_op jit(solution)/shard_map/ppermute | solution.py:496
  71.8 0.9 copy-start.7
  76.0 1.4 %copy-start.2 = (f32[512,1024]{1,0:T(8,128)}, f32[512,1024]{1,0:T(8,128)S(1)}, u32[]{:S(2)}) copy-start(f32[512,1024]{1,0:T(8,128)S(1)} %get-tuple-element.59.early_far) | copy-start | bytes 6291460
  77.4 0.7 copy-start.4
  83.1 10.7 %all-to-all-start.2 = ((bf16[16,2,1024]{2,1,0:T(2,128)(2,1)}), bf16[16,2,1024]{2,1,0:T(2,128)(2,1)S(1)}, u32[]{:S(2)}, u32[]{:S(2)}) async-start(bf16[16,2,1024]{2,1,0:T(2,128)(2,1)} %get-tuple-element.57), calls=%async_computation.2 | async-start | bytes 131072 | tf_op jit(solution)/shard_map/all_to_all | solution.py:553
  86.9 6.9 %copy-start.14 = (bf16[96,1024]{1,0:T(8,128)(2,1)}, bf16[96,1024]{1,0:T(8,128)(2,1)S(1)}, u32[]{:S(2)}) copy-start(bf16[96,1024]{1,0:T(8,128)(2,1)S(1)} %collective-permute-done.9.rest_1_) | copy-start | bytes 589828
  93.8 0.6 copy-start.13

commit v9 on v8

--- a/solution.py
+++ b/solution.py
@@ -145,7 +145,16 @@
 
 
 def route_kernel(
-    sizes, token_ids_far, owners_far, row_slot_far, plan, token_slot_far, code, *near
+    sizes,
+    token_ids_far,
+    owners_far,
+    row_slot_far,
+    stored,
+    plan,
+    token_slot_far,
+    code,
+    first_rows,
+    *near,
 ):
     peers, vocab_rows, token_cap, row_cap, pooled = sizes
     token_ids, owners, row_slot, token_slot, arrived = near
@@ -155,7 +164,10 @@
             ((token_ids_far, token_ids), (owners_far, owners), (row_slot_far, row_slot))
         )
     ]
-    for copy in copies:
+    cut = pltpu.make_async_copy(
+        stored.at[pl.ds(0, first_rows.shape[0])], first_rows, arrived.at[4]
+    )
+    for copy in copies + [cut]:
         copy.start()
     for copy in copies:
         copy.wait()
@@ -196,10 +208,11 @@
     token_slot[...] = down[:tokens] * token_cap + rank_col[:tokens]
     send = pltpu.make_async_copy(token_slot, token_slot_far, arrived.at[3])
     send.start()
+    cut.wait()
     send.wait()
 
 
-def route(token_ids, owners, row_slot, sizes):
+def route(token_ids, owners, row_slot, stored_rows, ahead, sizes):
     peers, _, token_cap, row_cap, pooled = sizes
     passes, seq_len = token_ids.shape
     rows = owners.shape[1]
@@ -210,86 +223,103 @@
             ints(peers, 1, rows + token_cap + row_cap + pooled),
             ints(passes * seq_len, 1),
             ints(1, rows),
-        ],
-        in_specs=[pl.BlockSpec(memory_space=pltpu.HBM)] * 3,
+            jax.ShapeDtypeStruct((ahead, stored_rows.shape[1]), stored_rows.dtype),
+        ],
+        in_specs=[pl.BlockSpec(memory_space=pltpu.HBM)] * 4,
         out_specs=[
             pl.BlockSpec(memory_space=pltpu.VMEM),
             pl.BlockSpec(memory_space=pltpu.HBM),
             pl.BlockSpec(memory_space=pltpu.VMEM),
+            pl.BlockSpec(memory_space=pltpu.HBM),
         ],
         scratch_shapes=[
             pltpu.VMEM(token_ids.shape, jnp.int32),
             pltpu.VMEM(owners.shape, jnp.int32),
             pltpu.VMEM(row_slot.shape, jnp.int32),
             pltpu.VMEM((passes * seq_len, 1), jnp.int32),
-            pltpu.SemaphoreType.DMA((4,)),
-        ],
+            pltpu.SemaphoreType.DMA((5,)),
+        ],
+        compiler_params=pltpu.CompilerParams(vmem_limit_bytes=60 * 1024 * 1024),
         name="route",
-    )(token_ids, owners, row_slot)
-
-
-def pack_kernel(half, row_cap, count, picks, pieces, *refs):
+    )(token_ids, owners, row_slot, stored_rows)
+
+
+def pack_kernel(half, row_cap, count, picks, pieces, rest, *refs):
     me = lax.axis_index("dp")
-    far, refs = refs[: 2 + 2 * pieces], refs[2 + 2 * pieces :]
-    near, arrived = refs[-3 - 2 * pieces : -1], refs[-1]
-    outs, codes_a, codes_b = refs[: -3 - 2 * pieces], near[0], near[1]
-    slot_count = len(outs) * row_cap
-    code_copies = [
-        pltpu.make_async_copy(far[0], codes_a, arrived.at[0]),
-        pltpu.make_async_copy(far[1], codes_b, arrived.at[1]),
+    operands = 2 + 2 * pieces
+    far, refs = refs[:operands], refs[operands:]
+    steps = half // 2
+    outs, refs = refs[: steps + bool(rest)], refs[steps + bool(rest) :]
+    near, (blocks, tail, arrived, left) = refs[:operands], refs[operands:]
+    size = blocks.shape[0] // steps
+    copies = [
+        pltpu.make_async_copy(far[at], near[at], arrived.at[at]) for at in range(operands)
     ]
-    row_copies = [
-        pltpu.make_async_copy(far[at], near[at], arrived.at[at]) for at in range(2, len(far))
-    ]
-    for copy in code_copies + row_copies:
+    for copy in copies:
         copy.start()
-    for copy in code_copies:
+    for copy in copies[:2]:
         copy.wait()
-    for source, codes in enumerate((codes_a, codes_b)):
+    if size > 2 * row_cap:
+        blocks[...] = jnp.zeros(blocks.shape, blocks.dtype)
+    for source in range(2):
         if picks is None:
-            code = codes[...]
+            code = near[source][...]
         else:
-            code = codes[me ^ picks[source], :, :count]
+            code = near[source][me ^ picks[source], :, :count]
         bits = rank_bits(count)
         owner, rank = code >> bits, code & (2**bits - 1)
         fits = ((owner ^ me) & (1 | half)) == 0
         chip = ((owner ^ me) & (half - 1)) >> 1
         slot = jnp.where(fits, chip * row_cap + rank, -1)
         packed, at = 0.0, 0
-        for piece in range(source * pieces, (source + 1) * pieces):
-            rows = near[2 + piece]
-            spot = lax.broadcasted_iota(jnp.int32, (slot_count, rows.shape[0]), 0)
+        for piece in range(2 + source * pieces, 2 + (source + 1) * pieces):
+            rows = near[piece]
+            spot = lax.broadcasted_iota(jnp.int32, (steps * row_cap, rows.shape[0]), 0)
             table = jnp.where(slot[:, at : at + rows.shape[0]] == spot, 1.0, 0.0)
-            row_copies[piece].wait()
+            copies[piece].wait()
             packed += jnp.dot(
                 table.astype(jnp.bfloat16), rows[...], preferred_element_type=jnp.float32
             )
             at += rows.shape[0]
         packed = packed.astype(jnp.bfloat16)
-        for step, out in enumerate(outs):
-            if source == 0 and out.shape[0] > 2 * row_cap:
-                out[...] = jnp.zeros(out.shape, out.dtype)
-            out[source * row_cap : (source + 1) * row_cap, :] = packed[
-                step * row_cap : (step + 1) * row_cap
-            ]
-
-
-def pack_rows(codes_a, codes_b, rows_a, rows_b, half, row_cap, count, picks=None):
+        for step in range(steps):
+            first = step * size + source * row_cap
+            blocks[first : first + row_cap, :] = packed[step * row_cap : (step + 1) * row_cap]
+    sends = [
+        pltpu.make_async_copy(
+            blocks.at[pl.ds(step * size, size)], outs[step], left.at[step]
+        )
+        for step in range(steps)
+    ]
+    if rest:
+        tail[...] = near[2][near[2].shape[0] - rest :, :]
+        sends.append(pltpu.make_async_copy(tail, outs[steps], left.at[steps]))
+    for send in sends:
+        send.start()
+    for send in sends:
+        send.wait()
+
+
+def pack_rows(codes_a, codes_b, rows_a, rows_b, half, row_cap, count, picks=None, rest=0):
     width = rows_a[0].shape[1]
     total = sum(piece.shape[0] for piece in rows_a)
-    pieces = len(rows_a)
     steps = half // 2
+    size = padded(2 * row_cap)
     operands = (codes_a, codes_b, *rows_a, *rows_b)
+    shapes = [(size, width)] * steps + [(rest, width)] * bool(rest)
     return pl.pallas_call(
-        functools.partial(pack_kernel, half, row_cap, count, picks, pieces),
-        out_shape=[jax.ShapeDtypeStruct((padded(2 * row_cap), width), jnp.bfloat16)] * steps,
-        in_specs=[pl.BlockSpec(memory_space=pl.ANY)] * len(operands),
-        out_specs=[pl.BlockSpec(memory_space=pltpu.VMEM)] * steps,
+        functools.partial(pack_kernel, half, row_cap, count, picks, len(rows_a), rest),
+        out_shape=[jax.ShapeDtypeStruct(shape, jnp.bfloat16) for shape in shapes],
+        in_specs=[pl.BlockSpec(memory_space=pltpu.HBM)] * len(operands),
+        out_specs=[pl.BlockSpec(memory_space=pltpu.HBM)] * len(shapes),
         scratch_shapes=[
             *(pltpu.VMEM(operand.shape, operand.dtype) for operand in operands),
+            pltpu.VMEM((steps * size, width), jnp.bfloat16),
+            pltpu.VMEM((max(rest, 16), width), jnp.bfloat16),
             pltpu.SemaphoreType.DMA((len(operands),)),
-        ],
-        compiler_params=pltpu.CompilerParams(vmem_limit_bytes=20 * 1024 * 1024),
+            pltpu.SemaphoreType.DMA((len(shapes),)),
+        ],
+        compiler_params=pltpu.CompilerParams(vmem_limit_bytes=60 * 1024 * 1024),
         cost_estimate=pl.CostEstimate(
             flops=4 * steps * row_cap * width * total,
             bytes_accessed=4 * width * (total + steps * row_cap),
@@ -417,10 +447,10 @@
             pltpu.SemaphoreType.DMA((1 + len(pieces) + steps,)),
             pltpu.SemaphoreType.DMA((steps + 1,)),
         ],
-        compiler_params=pltpu.CompilerParams(vmem_limit_bytes=20 * 1024 * 1024),
+        compiler_params=pltpu.CompilerParams(vmem_limit_bytes=60 * 1024 * 1024),
         cost_estimate=pl.CostEstimate(
-            flops=2 * centre_count * width * row_total,
-            bytes_accessed=8 * centre_count * width,
+            flops=100 * centre_count * width * row_total,
+            bytes_accessed=200 * centre_count * width,
             transcendentals=0,
         ),
         name="early",
@@ -496,19 +526,29 @@
             got.append(lax.ppermute(blocks[step], "dp", moves))
         return got
 
-    ahead = store_count * 3 // 4 // 16 * 16
-    first_rows = lax.ppermute(stored_rows[:ahead], "dp", across)
+    ahead = store_count * 7 // 16 // 16 * 16
     sibling_rows = lax.ppermute(stored_rows, "dp", beside)
     sizes = (peer_count, vocab_rows, token_cap, row_cap, row_count - store_count)
-    plan, token_slot, code = route(token_ids, row_owner.reshape(1, row_count), row_slot[None], sizes)
+    plan, token_slot, code, first_rows = route(
+        token_ids, row_owner.reshape(1, row_count), row_slot[None], stored_rows, ahead, sizes
+    )
+    first_rows = lax.ppermute(first_rows, "dp", across)
     sibling_code = lax.ppermute(code, "dp", beside)
-    blocks = pack_rows(code, sibling_code, [stored_rows], [sibling_rows], half, row_cap, row_count)
-    plan, *blocks = lax.optimization_barrier((plan, *blocks))
+    *blocks, last_rows = pack_rows(
+        code,
+        sibling_code,
+        [stored_rows],
+        [sibling_rows],
+        half,
+        row_cap,
+        row_count,
+        rest=store_count - ahead,
+    )
+    plan, last_rows, *blocks = lax.optimization_barrier((plan, last_rows, *blocks))
+    codes = lax.all_to_all(plan, "dp", split_axis=0, concat_axis=0, tiled=True)
+    last_rows = lax.ppermute(last_rows, "dp", across)
     own_half = hand_on(blocks)
-    codes = lax.all_to_all(plan, "dp", split_axis=0, concat_axis=0, tiled=True)
     plan = codes[:, 0, row_count:]
-    rest, plan = lax.optimization_barrier((stored_rows[ahead:], plan))
-    last_rows = lax.ppermute(rest, "dp", across)
     wanted = plan[:, :token_cap].reshape(peer_count * token_cap)
     chosen = wanted[:, None] == jnp.arange(vocab_rows, dtype=jnp.int32)[None, :]
     found = jnp.dot(

time: 98.5 us -> 92.6 us (0.940)
  Pallas kernels: 17.6 us -> 25.7 us
  local copies, waits for them, and re-layouts: 14.1 us -> 7.06 us
  waiting for transfers between devices: 35 us -> 29.4 us
  starting transfers between devices: 29.2 us -> 27.8 us
    ppermute x2, waiting for transfers between devices: 22.8 us -> 1.25 us  [the longest x1 1.25 us: shards(): first_rows = lax.ppermute(first_rows, 'dp', across)]
    all_to_all x1, waiting for transfers between devices: 1.59 us -> 11.3 us  [shards(): codes = lax.all_to_all(plan, 'dp', split_axis=0, concat_axis=0, tiled=True)]
    all_to_all x1, waiting for transfers between devices: 0.01 us -> 6.76 us  [shards(): lax.all_to_all(found.reshape(peer_count, token_cap, width), 'dp', split_a...]
    pallas_call x1, Pallas kernels: 2.28 us -> 7.71 us  [route(): pl.pallas_call(functools.partial(route_kernel, sizes), out_shape=[ints(pe...]
    slice x2 -> x0, local copies, waits for them, and re-layouts: 3.33 us -> none  [the longest x1 1.74 us: shards(): first_rows = lax.ppermute(stored_rows[:ahead], 'dp', across)]
    unnamed x30 -> x32, local copies, waits for them, and re-layouts: 8.01 us -> 4.93 us
    pallas_call x2, Pallas kernels: 3.48 us -> 5.7 us  [pack_rows(): pl.pallas_call(functools.partial(pack_kernel, half, row_cap, count, picks...]
    ppermute x6, starting transfers between devices: 9.24 us -> 7.04 us  [hand_on(): got.append(lax.ppermute(blocks[step], 'dp', moves))]
  transfers between devices with their start and end apart: 15 -> 15, of which waited for: 6 -> 6; matrix products, arithmetic and copies ran while one was open for 8% -> 4% of each run, Pallas kernels for 14% -> 21%
where the time goes in v9:
time: 92.6 us; the launch traced here: 92.2 us
  waiting for transfers between devices  29.4 us (32%)
  starting transfers between devices  27.8 us (30%)
  Pallas kernels  25.7 us (28%)
  local copies, waits for them, and re-layouts  7.06 us (8%)
  matrix products  1.29 us (1%)
    all_to_all x1, waiting for transfers between devices, shards(): codes = lax.all_to_all(plan, 'dp', split_axis=0, concat_axis=0, tiled=True)  11.3 us
    pallas_call x1, Pallas kernels, route(): pl.pallas_call(functools.partial(route_kernel, sizes), out_shape=[ints(pe...  7.71 us
    ppermute x6, starting transfers between devices, hand_on(): got.append(lax.ppermute(blocks[step], 'dp', moves))  7.04 us
    all_to_all x1, waiting for transfers between devices, shards(): lax.all_to_all(spread, 'dp', split_axis=0, concat_axis=0, tiled=True)  6.83 us
    all_to_all x1, waiting for transfers between devices, shards(): lax.all_to_all(found.reshape(peer_count, token_cap, width), 'dp', split_a...  6.76 us
    pallas_call x2, Pallas kernels, pack_rows(): pl.pallas_call(functools.partial(pack_kernel, half, row_cap, count, picks...  5.7 us
    all_to_all x1, starting transfers between devices, shards(): lax.all_to_all(spread, 'dp', split_axis=0, concat_axis=0, tiled=True)  5.19 us
    pallas_call x1, Pallas kernels, encode(): pl.pallas_call(encode_kernel, out_shape=[jax.ShapeDtypeStruct((passes, wi...  4.99 us
  transfers between devices with their start and end apart: 15, of which 6 were waited for; matrix products, arithmetic and copies ran while one was open for 4% of the time, Pallas kernels for 21%

profile of v9, /device:TPU:0, one launch (start us, length us, event | category | flops | bytes accessed | tf_op | source)
XLA Modules:
  0.0 92.2 jit_solution(7105803070680433633)
XLA Ops:
  0.6 0.0 copy-start
  0.6 0.5 collective-permute-start.1
  1.2 7.7 %route.1 = (s32[16,1,330]{2,1,0:T(1,128)}, s32[128,1]{1,0:T(8,128)}, s32[1,256]{1,0:T(1,128)}, bf16[96,1024]{1,0:T(8,128)(2,1)}) custom-call(s32[2,64]{1,0:T(2,128)} %token_ids_far.1, s32[1,256]{1,0:T(1,128)} %bitcast.24, s32[1,256]{1,0:T(1,128)} %bitcast.25, bf16[254,1024]{1,0:T(8,128)(2,1)} %refs_2_.1), custom_call_target="tpu_custom_call" | custom-call | tf_op jit(solution)/shard_map/route/pallas_call | solution.py:220
  8.9 0.1 collective-permute-start
  9.0 1.3 %collective-permute-done.refs_1_ = s32[1,256]{1,0:T(1,128)S(1)} collective-permute-done((s32[1,256]{1,0:T(1,128)}, s32[1,256]{1,0:T(1,128)S(1)}, u32[]{:S(2)}, u32[]{:S(2)}) %collective-permute-start) | collective-permute-done | bytes 1056 | tf_op jit(solution)/shard_map/ppermute | solution.py:536
  10.3 0.0 collective-permute-done.1.refs_3_
  10.3 0.6 copy-done.12
  10.9 0.8 copy-done.2
  11.7 2.8 %pack.2 = (bf16[96,1024]{1,0:T(8,128)(2,1)}, bf16[96,1024]{1,0:T(8,128)(2,1)}, bf16[96,1024]{1,0:T(8,128)(2,1)}, bf16[96,1024]{1,0:T(8,128)(2,1)}, bf16[158,1024]{1,0:T(8,128)(2,1)}) custom-call(s32[1,256]{1,0:T(1,128)} %get-tuple-element.37.refs_0_, s32[1,256]{1,0:T(1,128)} %copy-done.12, bf16[254,1024]{1,0:T(8,128)(2,1)} %refs_2_.1, ...), custom_call_target="tpu_custom_call" | custom-call | flops 199753728 | bytes 1826816 | tf_op jit(solution)/shard_map/pack/pallas_call | solution.py:310
  14.4 3.8 %collective-permute-start.6 = (bf16[158,1024]{1,0:T(8,128)(2,1)}, bf16[158,1024]{1,0:T(8,128)(2,1)S(1)}, u32[]{:S(2)}, u32[]{:S(2)}) collective-permute-start(bf16[158,1024]{1,0:T(8,128)(2,1)} %get-tuple-element.63), channel_id=1, source_target_pairs={{0,8},{1,9},{2,10},{3,11},{4,12},{5,13},{6,14},{7,15},{8,0},{9,1},... | collective-permute-start | bytes 970760 | tf_op jit(solution)/shard_map/ppermute | solution.py:549
  18.3 3.9 %all-to-all-start = ((s32[16,1,330]{2,1,0:T(1,128)}), s32[16,1,330]{2,1,0:T(1,128)S(1)}, u32[]{:S(2)}, u32[]{:S(2)}) async-start(s32[16,1,330]{2,1,0:T(1,128)} %get-tuple-element.43), calls=%async_computation | async-start | bytes 49152 | tf_op jit(solution)/shard_map/all_to_all | solution.py:548
  22.2 2.8 %collective-permute-start.2 = (bf16[96,1024]{1,0:T(8,128)(2,1)}, bf16[96,1024]{1,0:T(8,128)(2,1)S(1)}, u32[]{:S(2)}, u32[]{:S(2)}) collective-permute-start(bf16[96,1024]{1,0:T(8,128)(2,1)} %get-tuple-element.44), channel_id=1, source_target_pairs={{0,8},{1,9},{2,10},{3,11},{4,12},{5,13},{6,14},{7,15},{8,0},{9,1},... | collective-permute-start | bytes 589832 | tf_op jit(solution)/shard_map/ppermute | solution.py:535
  25.0 1.5 %collective-permute-start.3 = (bf16[96,1024]{1,0:T(8,128)(2,1)}, bf16[96,1024]{1,0:T(8,128)(2,1)S(1)}, u32[]{:S(2)}, u32[]{:S(2)}) collective-permute-start(bf16[96,1024]{1,0:T(8,128)(2,1)} %get-tuple-element.46), channel_id=1, source_target_pairs={{0,2},{1,3},{2,0},{3,1},{4,6},{5,7},{6,4},{7,5},{8,10},{9,11},{10,... | collective-permute-start | bytes 589832 | tf_op jit(solution)/shard_map/ppermute | solution.py:526
  26.5 1.5 %collective-permute-start.4 = (bf16[96,1024]{1,0:T(8,128)(2,1)}, bf16[96,1024]{1,0:T(8,128)(2,1)S(1)}, u32[]{:S(2)}, u32[]{:S(2)}) collective-permute-start(bf16[96,1024]{1,0:T(8,128)(2,1)} %get-tuple-element.47), channel_id=1, source_target_pairs={{0,4},{1,5},{2,6},{3,7},{4,0},{5,1},{6,2},{7,3},{8,12},{9,13},{10,... | collective-permute-start | bytes 589832 | tf_op jit(solution)/shard_map/ppermute | solution.py:526
  28.0 0.6 collective-permute-start.5
  28.5 11.3 %all-to-all-done.refs_0_.refs_1_ = s32[16,1,330]{2,1,0:T(1,128)S(1)} async-done(((s32[16,1,330]{2,1,0:T(1,128)}), s32[16,1,330]{2,1,0:T(1,128)S(1)}, u32[]{:S(2)}, u32[]{:S(2)}) %all-to-all-start) | async-done | bytes 21152 | tf_op jit(solution)/shard_map/all_to_all | solution.py:548
  39.9 0.1 eq.15
  40.0 0.0 collective-permute-done.6.refs_3_
  40.0 0.0 copy-start.3
  40.0 0.2 collective-permute-start.8
  40.2 0.0 copy-done
  40.2 1.3 %convolution_convert_fusion = bf16[384,1024]{1,0:T(8,128)(2,1)} fusion(bf16[240,1024]{1,0:T(8,128)(2,1)S(1)} %copy-done, s32[384]{0:T(512)S(1)} %eq.15), kind=kOutput, calls=%fused_computation.1 | convolution fusion | flops 189229056 | bytes 1279488 | tf_op jit(solution)/shard_map/dot_general | solution.py:554
  41.5 1.2 %collective-permute-done.2.refs_2_ = bf16[96,1024]{1,0:T(8,128)(2,1)S(1)} collective-permute-done((bf16[96,1024]{1,0:T(8,128)(2,1)}, bf16[96,1024]{1,0:T(8,128)(2,1)S(1)}, u32[]{:S(2)}, u32[]{:S(2)}) %collective-permute-start.2) | collective-permute-done | bytes 196640 | tf_op jit(solution)/shard_map/ppermute | solution.py:535
  42.7 0.0 collective-permute-done.3.rest_1_
  42.7 1.9 %collective-permute-done.4.rest_2_ = bf16[96,1024]{1,0:T(8,128)(2,1)S(1)} collective-permute-done((bf16[96,1024]{1,0:T(8,128)(2,1)}, bf16[96,1024]{1,0:T(8,128)(2,1)S(1)}, u32[]{:S(2)}, u32[]{:S(2)}) %collective-permute-start.4) | collective-permute-done | bytes 196640 | tf_op jit(solution)/shard_map/ppermute | solution.py:526
  44.7 0.0 collective-permute-start.7
  44.7 0.1 slice.21
  44.8 0.1 slice.20
  44.8 0.7 reshape.42.late_far
  45.5 0.6 gather_fusion
  46.1 0.7 reshape.41.places_far
  46.7 4.1 %all-to-all-start.1 = ((bf16[16,24,1024]{2,1,0:T(8,128)(2,1)}), bf16[16,24,1024]{2,1,0:T(8,128)(2,1)S(1)}, u32[]{:S(2)}, u32[]{:S(2)}) async-start(bf16[16,24,1024]{2,1,0:T(8,128)(2,1)} %bitcast.4), calls=%async_computation.1 | async-start | bytes 1572864 | tf_op jit(solution)/shard_map/all_to_all | solution.py:560
  50.9 0.0 collective-permute-done.7.refs_4_
  50.9 0.0 copy-start.11
  50.9 0.0 collective-permute-done.8.refs_5_
  50.9 0.0 copy-done.5
  50.9 0.0 copy-done.3
  50.9 0.0 copy-done.10
  50.9 0.6 copy-done.11
  51.6 0.7 copy-done.4
  52.3 2.9 %pack.3 = (bf16[96,1024]{1,0:T(8,128)(2,1)}, bf16[96,1024]{1,0:T(8,128)(2,1)}, bf16[96,1024]{1,0:T(8,128)(2,1)}, bf16[96,1024]{1,0:T(8,128)(2,1)}) custom-call(s32[16,1,330]{2,1,0:T(1,128)} %copy-done.5, s32[16,1,330]{2,1,0:T(1,128)} %copy-done.5, bf16[96,1024]{1,0:T(8,128)(2,1)} %copy-done.10, bf16[158,1024]{1,0:T(8,128)(2,1)} %copy-done.3, ...), custom_call_target="tpu_custom_call" | custom-call | flops 199753728 | bytes 1826816 | tf_op jit(solution)/shard_map/pack/pallas_call | solution.py:310
  55.2 2.0 %collective-permute-start.9 = (bf16[96,1024]{1,0:T(8,128)(2,1)}, bf16[96,1024]{1,0:T(8,128)(2,1)S(1)}, u32[]{:S(2)}, u32[]{:S(2)}) collective-permute-start(bf16[96,1024]{1,0:T(8,128)(2,1)} %get-tuple-element.65), channel_id=1, source_target_pairs={{0,2},{1,3},{2,0},{3,1},{4,6},{5,7},{6,4},{7,5},{8,10},{9,11},{10,... | collective-permute-start | bytes 589832 | tf_op jit(solution)/shard_map/ppermute | solution.py:526
  57.2 1.4 %collective-permute-start.10 = (bf16[96,1024]{1,0:T(8,128)(2,1)}, bf16[96,1024]{1,0:T(8,128)(2,1)S(1)}, u32[]{:S(2)}, u32[]{:S(2)}) collective-permute-start(bf16[96,1024]{1,0:T(8,128)(2,1)} %get-tuple-element.66), channel_id=1, source_target_pairs={{0,4},{1,5},{2,6},{3,7},{4,0},{5,1},{6,2},{7,3},{8,12},{9,13},{10,... | collective-permute-start | bytes 589832 | tf_op jit(solution)/shard_map/ppermute | solution.py:526
  58.7 0.1 collective-permute-start.11
  58.8 0.0 collective-permute-done.5.rest_3_
  58.8 0.0 copy-done.13
  58.8 0.0 copy-done.14
  58.8 0.0 copy-start.15
  58.8 0.7 copy-done.15
  59.5 3.8 %early.1 = (f32[512,1024]{1,0:T(8,128)}, f32[512,128]{1,0:T(8,128)}) custom-call(s32[1,768]{1,0:T(1,128)} %reshape.41.places_far, f32[512,1024]{1,0:T(8,128)} %centroids_far.1, bf16[96,1024]{1,0:T(8,128)(2,1)} %get-tuple-element.49.rest_0_, bf16[96,1024]{1,0:T(8,128)(2,1)} %copy-done.13, bf16[96,1024]{1,0:T(8,128)(2,1)} %copy-done.14, ...), custom_call_target="tpu_custom_call" | custom-call | flops 20132659200 | bytes 104857600 | tf_op jit(solution)/shard_map/early/pallas_call | solution.py:433
  63.2 6.8 %all-to-all-done.1 = bf16[16,24,1024]{2,1,0:T(8,128)(2,1)S(1)} async-done(((bf16[16,24,1024]{2,1,0:T(8,128)(2,1)}), bf16[16,24,1024]{2,1,0:T(8,128)(2,1)S(1)}, u32[]{:S(2)}, u32[]{:S(2)}) %all-to-all-start.1) | async-done | bytes 786464 | tf_op jit(solution)/shard_map/all_to_all | solution.py:560
  70.0 0.9 copy-done.1
  70.9 5.0 %encode.1 = (bf16[2,1024]{1,0:T(2,128)(2,1)}, bf16[16,2,1024]{2,1,0:T(2,128)(2,1)}) custom-call(s32[1,2]{1,0:T(1,128)} %bitcast.26, s32[128,1]{1,0:T(8,128)} %get-tuple-element.35.refs_1_, bf16[384,1024]{1,0:T(8,128)(2,1)} %bitcast.15, bf16[64,1024]{1,0:T(8,128)(2,1)} %refs_3_.1, f32[1,1024]{1,0:T(1,128)} %bitcast.19, f32[1,1024]{1,0:T(1,128)} %bitcast.20, ...), custom_call_target="tpu_custom_call" | custom-call | flops 637534208 | bytes 6291456 | tf_op jit(solution)/shard_map/encode/pallas_call | solution.py:121
  75.9 5.2 %all-to-all-start.2 = ((bf16[16,2,1024]{2,1,0:T(2,128)(2,1)}), bf16[16,2,1024]{2,1,0:T(2,128)(2,1)S(1)}, u32[]{:S(2)}, u32[]{:S(2)}) async-start(bf16[16,2,1024]{2,1,0:T(2,128)(2,1)} %get-tuple-element.59), calls=%async_computation.2 | async-start | bytes 131072 | tf_op jit(solution)/shard_map/all_to_all | solution.py:593
  81.1 0.0 collective-permute-done.9.rest_1_
  81.1 0.0 copy-start.7
  81.1 0.0 collective-permute-done.10.rest_2_
  81.1 0.0 copy-start.8
  81.1 0.0 collective-permute-done.11.rest_3_
  81.1 6.8 %all-to-all-done.2.spread_far = bf16[16,2,1024]{2,1,0:T(2,128)(2,1)S(1)} async-done(((bf16[16,2,1024]{2,1,0:T(2,128)(2,1)}), bf16[16,2,1024]{2,1,0:T(2,128)(2,1)S(1)}, u32[]{:S(2)}, u32[]{:S(2)}) %all-to-all-start.2) | async-done | bytes 65568 | tf_op jit(solution)/shard_map/all_to_all | solution.py:593
  88.0 0.0 copy-done.7
  88.0 0.0 copy-done.9
  88.0 0.6 copy-done.6
  88.6 3.6 %late.1 = f32[512,1024]{1,0:T(8,128)} custom-call(s32[1,768]{1,0:T(1,128)} %reshape.41.places_far, s32[1,32]{1,0:T(1,128)} %reshape.42.late_far, bf16[16,2,1024]{2,1,0:T(2,128)(2,1)} %copy-done.6, f32[512,128]{1,0:T(8,128)} %get-tuple-element.60.share_far, f32[512,1024]{1,0:T(8,128)} %get-tuple-element.61.early_far, ...), custom_call_target="tpu_custom_call" | custom-call | flops 436207616 | bytes 4194304 | tf_op jit(solution)/shard_map/late/pallas_call | solution.py:465
  (14 shorter events, 0.0 us)
Async XLA Ops:
  0.6 39.5 %copy-start = (bf16[240,1024]{1,0:T(8,128)(2,1)S(1)}, bf16[240,1024]{1,0:T(8,128)(2,1)}, u32[]{:S(2)}) copy-start(bf16[240,1024]{1,0:T(8,128)(2,1)} %param.17) | copy-start | bytes 1474564
  0.6 9.7 %collective-permute-start.1 = (bf16[254,1024]{1,0:T(8,128)(2,1)}, bf16[254,1024]{1,0:T(8,128)(2,1)S(1)}, u32[]{:S(2)}, u32[]{:S(2)}) collective-permute-start(bf16[254,1024]{1,0:T(8,128)(2,1)} %refs_2_.1), channel_id=1, source_target_pairs={{0,1},{1,0},{2,3},{3,2},{4,5},{5,4},{6,7},{7,6},{8,9},{9,8},{10,11... | collective-permute-start | bytes 1560584 | tf_op jit(solution)/shard_map/ppermute | solution.py:530
  8.9 1.4 %collective-permute-start = (s32[1,256]{1,0:T(1,128)}, s32[1,256]{1,0:T(1,128)S(1)}, u32[]{:S(2)}, u32[]{:S(2)}) collective-permute-start(s32[1,256]{1,0:T(1,128)} %get-tuple-element.37.refs_0_), channel_id=1, source_target_pairs={{0,1},{1,0},{2,3},{3,2},{4,5},{5,4},{6,7},{7,6},{8,9},{9,8},{10,11... | collective-permute-start | bytes 3080 | tf_op jit(solution)/shard_map/ppermute | solution.py:536
  10.3 0.6 copy-start.12
  10.9 0.8 copy-start.2
  14.4 25.5 %collective-permute-start.6 = (bf16[158,1024]{1,0:T(8,128)(2,1)}, bf16[158,1024]{1,0:T(8,128)(2,1)S(1)}, u32[]{:S(2)}, u32[]{:S(2)}) collective-permute-start(bf16[158,1024]{1,0:T(8,128)(2,1)} %get-tuple-element.63), channel_id=1, source_target_pairs={{0,8},{1,9},{2,10},{3,11},{4,12},{5,13},{6,14},{7,15},{8,0},{9,1},... | collective-permute-start | bytes 970760 | tf_op jit(solution)/shard_map/ppermute | solution.py:549
  18.3 21.6 %all-to-all-start = ((s32[16,1,330]{2,1,0:T(1,128)}), s32[16,1,330]{2,1,0:T(1,128)S(1)}, u32[]{:S(2)}, u32[]{:S(2)}) async-start(s32[16,1,330]{2,1,0:T(1,128)} %get-tuple-element.43), calls=%async_computation | async-start | bytes 49152 | tf_op jit(solution)/shard_map/all_to_all | solution.py:548
  22.2 20.5 %collective-permute-start.2 = (bf16[96,1024]{1,0:T(8,128)(2,1)}, bf16[96,1024]{1,0:T(8,128)(2,1)S(1)}, u32[]{:S(2)}, u32[]{:S(2)}) collective-permute-start(bf16[96,1024]{1,0:T(8,128)(2,1)} %get-tuple-element.44), channel_id=1, source_target_pairs={{0,8},{1,9},{2,10},{3,11},{4,12},{5,13},{6,14},{7,15},{8,0},{9,1},... | collective-permute-start | bytes 589832 | tf_op jit(solution)/shard_map/ppermute | solution.py:535
  25.0 17.7 %collective-permute-start.3 = (bf16[96,1024]{1,0:T(8,128)(2,1)}, bf16[96,1024]{1,0:T(8,128)(2,1)S(1)}, u32[]{:S(2)}, u32[]{:S(2)}) collective-permute-start(bf16[96,1024]{1,0:T(8,128)(2,1)} %get-tuple-element.46), channel_id=1, source_target_pairs={{0,2},{1,3},{2,0},{3,1},{4,6},{5,7},{6,4},{7,5},{8,10},{9,11},{10,... | collective-permute-start | bytes 589832 | tf_op jit(solution)/shard_map/ppermute | solution.py:526
  26.5 18.2 %collective-permute-start.4 = (bf16[96,1024]{1,0:T(8,128)(2,1)}, bf16[96,1024]{1,0:T(8,128)(2,1)S(1)}, u32[]{:S(2)}, u32[]{:S(2)}) collective-permute-start(bf16[96,1024]{1,0:T(8,128)(2,1)} %get-tuple-element.47), channel_id=1, source_target_pairs={{0,4},{1,5},{2,6},{3,7},{4,0},{5,1},{6,2},{7,3},{8,12},{9,13},{10,... | collective-permute-start | bytes 589832 | tf_op jit(solution)/shard_map/ppermute | solution.py:526
  28.0 30.8 %collective-permute-start.5 = (bf16[96,1024]{1,0:T(8,128)(2,1)}, bf16[96,1024]{1,0:T(8,128)(2,1)S(1)}, u32[]{:S(2)}, u32[]{:S(2)}) collective-permute-start(bf16[96,1024]{1,0:T(8,128)(2,1)} %get-tuple-element.52), channel_id=1, source_target_pairs={{0,6},{1,7},{2,4},{3,5},{4,2},{5,3},{6,0},{7,1},{8,14},{9,15},{10,... | collective-permute-start | bytes 589832 | tf_op jit(solution)/shard_map/ppermute | solution.py:526
  39.9 11.0 %copy-start.5 = (s32[16,1,330]{2,1,0:T(1,128)}, s32[16,1,330]{2,1,0:T(1,128)S(1)}, u32[]{:S(2)}) copy-start(s32[16,1,330]{2,1,0:T(1,128)S(1)} %all-to-all-done.refs_0_.refs_1_) | copy-start | bytes 63364
  40.0 10.9 %copy-start.3 = (bf16[158,1024]{1,0:T(8,128)(2,1)}, bf16[158,1024]{1,0:T(8,128)(2,1)S(1)}, u32[]{:S(2)}) copy-start(bf16[158,1024]{1,0:T(8,128)(2,1)S(1)} %collective-permute-done.6.refs_3_) | copy-start | bytes 970756
  40.0 10.9 %collective-permute-start.8 = (bf16[158,1024]{1,0:T(8,128)(2,1)S(1)}, bf16[158,1024]{1,0:T(8,128)(2,1)S(1)}, u32[]{:S(2)}, u32[]{:S(2)}) collective-permute-start(bf16[158,1024]{1,0:T(8,128)(2,1)S(1)} %collective-permute-done.6.refs_3_), channel_id=1, source_target_pairs={{0,1},{1,0},{2,3},{3,2},{4,5},{5,4},{6,7},{7,6},{8,9},{9,8},{10,11... | collective-permute-start | bytes 970760 | tf_op jit(solution)/shard_map/ppermute | solution.py:565
  42.7 8.2 %copy-start.10 = (bf16[96,1024]{1,0:T(8,128)(2,1)}, bf16[96,1024]{1,0:T(8,128)(2,1)S(1)}, u32[]{:S(2)}) copy-start(bf16[96,1024]{1,0:T(8,128)(2,1)S(1)} %collective-permute-done.2.refs_2_) | copy-start | bytes 589828
  42.7 16.1 %copy-start.13 = (bf16[96,1024]{1,0:T(8,128)(2,1)}, bf16[96,1024]{1,0:T(8,128)(2,1)S(1)}, u32[]{:S(2)}) copy-start(bf16[96,1024]{1,0:T(8,128)(2,1)S(1)} %collective-permute-done.3.rest_1_) | copy-start | bytes 589828
  44.7 14.1 %copy-start.14 = (bf16[96,1024]{1,0:T(8,128)(2,1)}, bf16[96,1024]{1,0:T(8,128)(2,1)S(1)}, u32[]{:S(2)}) copy-start(bf16[96,1024]{1,0:T(8,128)(2,1)S(1)} %collective-permute-done.4.rest_2_) | copy-start | bytes 589828
  44.7 6.2 %collective-permute-start.7 = (bf16[96,1024]{1,0:T(8,128)(2,1)S(1)}, bf16[96,1024]{1,0:T(8,128)(2,1)S(1)}, u32[]{:S(2)}, u32[]{:S(2)}) collective-permute-start(bf16[96,1024]{1,0:T(8,128)(2,1)S(1)} %collective-permute-done.2.refs_2_), channel_id=1, source_target_pairs={{0,1},{1,0},{2,3},{3,2},{4,5},{5,4},{6,7},{7,6},{8,9},{9,8},{10,11... | collective-permute-start | bytes 589832 | tf_op jit(solution)/shard_map/ppermute | solution.py:565
  46.7 23.3 %all-to-all-start.1 = ((bf16[16,24,1024]{2,1,0:T(8,128)(2,1)}), bf16[16,24,1024]{2,1,0:T(8,128)(2,1)S(1)}, u32[]{:S(2)}, u32[]{:S(2)}) async-start(bf16[16,24,1024]{2,1,0:T(8,128)(2,1)} %bitcast.4), calls=%async_computation.1 | async-start | bytes 1572864 | tf_op jit(solution)/shard_map/all_to_all | solution.py:560
  50.9 0.7 copy-start.11
  51.6 0.7 copy-start.4
  55.2 25.8 %collective-permute-start.9 = (bf16[96,1024]{1,0:T(8,128)(2,1)}, bf16[96,1024]{1,0:T(8,128)(2,1)S(1)}, u32[]{:S(2)}, u32[]{:S(2)}) collective-permute-start(bf16[96,1024]{1,0:T(8,128)(2,1)} %get-tuple-element.65), channel_id=1, source_target_pairs={{0,2},{1,3},{2,0},{3,1},{4,6},{5,7},{6,4},{7,5},{8,10},{9,11},{10,... | collective-permute-start | bytes 589832 | tf_op jit(solution)/shard_map/ppermute | solution.py:526
  57.2 23.9 %collective-permute-start.10 = (bf16[96,1024]{1,0:T(8,128)(2,1)}, bf16[96,1024]{1,0:T(8,128)(2,1)S(1)}, u32[]{:S(2)}, u32[]{:S(2)}) collective-permute-start(bf16[96,1024]{1,0:T(8,128)(2,1)} %get-tuple-element.66), channel_id=1, source_target_pairs={{0,4},{1,5},{2,6},{3,7},{4,0},{5,1},{6,2},{7,3},{8,12},{9,13},{10,... | collective-permute-start | bytes 589832 | tf_op jit(solution)/shard_map/ppermute | solution.py:526
  58.7 22.4 %collective-permute-start.11 = (bf16[96,1024]{1,0:T(8,128)(2,1)}, bf16[96,1024]{1,0:T(8,128)(2,1)S(1)}, u32[]{:S(2)}, u32[]{:S(2)}) collective-permute-start(bf16[96,1024]{1,0:T(8,128)(2,1)} %get-tuple-element.67), channel_id=1, source_target_pairs={{0,6},{1,7},{2,4},{3,5},{4,2},{5,3},{6,0},{7,1},{8,14},{9,15},{10,... | collective-permute-start | bytes 589832 | tf_op jit(solution)/shard_map/ppermute | solution.py:526
  58.8 0.7 copy-start.15
  70.0 0.9 copy-start.1
  75.9 12.1 %all-to-all-start.2 = ((bf16[16,2,1024]{2,1,0:T(2,128)(2,1)}), bf16[16,2,1024]{2,1,0:T(2,128)(2,1)S(1)}, u32[]{:S(2)}, u32[]{:S(2)}) async-start(bf16[16,2,1024]{2,1,0:T(2,128)(2,1)} %get-tuple-element.59), calls=%async_computation.2 | async-start | bytes 131072 | tf_op jit(solution)/shard_map/all_to_all | solution.py:593
  81.1 6.9 %copy-start.7 = (bf16[96,1024]{1,0:T(8,128)(2,1)}, bf16[96,1024]{1,0:T(8,128)(2,1)S(1)}, u32[]{:S(2)}) copy-start(bf16[96,1024]{1,0:T(8,128)(2,1)S(1)} %collective-permute-done.9.rest_1_) | copy-start | bytes 589828
  81.1 6.9 %copy-start.8 = (bf16[96,1024]{1,0:T(8,128)(2,1)}, bf16[96,1024]{1,0:T(8,128)(2,1)S(1)}, u32[]{:S(2)}) copy-start(bf16[96,1024]{1,0:T(8,128)(2,1)S(1)} %collective-permute-done.10.rest_2_) | copy-start | bytes 589828
  81.1 6.9 %copy-start.9 = (bf16[96,1024]{1,0:T(8,128)(2,1)}, bf16[96,1024]{1,0:T(8,128)(2,1)S(1)}, u32[]{:S(2)}) copy-start(bf16[96,1024]{1,0:T(8,128)(2,1)S(1)} %collective-permute-done.11.rest_3_) | copy-start | bytes 589828
  88.0 0.6 copy-start.6

commit v10 on v9

--- a/solution.py
+++ b/solution.py
@@ -149,11 +149,9 @@
     token_ids_far,
     owners_far,
     row_slot_far,
-    stored,
     plan,
     token_slot_far,
     code,
-    first_rows,
     *near,
 ):
     peers, vocab_rows, token_cap, row_cap, pooled = sizes
@@ -164,10 +162,7 @@
             ((token_ids_far, token_ids), (owners_far, owners), (row_slot_far, row_slot))
         )
     ]
-    cut = pltpu.make_async_copy(
-        stored.at[pl.ds(0, first_rows.shape[0])], first_rows, arrived.at[4]
-    )
-    for copy in copies + [cut]:
+    for copy in copies:
         copy.start()
     for copy in copies:
         copy.wait()
@@ -208,11 +203,32 @@
     token_slot[...] = down[:tokens] * token_cap + rank_col[:tokens]
     send = pltpu.make_async_copy(token_slot, token_slot_far, arrived.at[3])
     send.start()
-    cut.wait()
     send.wait()
 
 
-def route(token_ids, owners, row_slot, stored_rows, ahead, sizes):
+def cut_kernel(far, out_far, near, done):
+    load = pltpu.make_async_copy(far.at[pl.ds(0, near.shape[0])], near, done.at[0])
+    load.start()
+    load.wait()
+    send = pltpu.make_async_copy(near, out_far, done.at[1])
+    send.start()
+    send.wait()
+
+
+def cut(rows, count):
+    shape = (count, rows.shape[1])
+    return pl.pallas_call(
+        cut_kernel,
+        out_shape=jax.ShapeDtypeStruct(shape, rows.dtype),
+        in_specs=[pl.BlockSpec(memory_space=pltpu.HBM)],
+        out_specs=pl.BlockSpec(memory_space=pltpu.HBM),
+        scratch_shapes=[pltpu.VMEM(shape, rows.dtype), pltpu.SemaphoreType.DMA((2,))],
+        compiler_params=pltpu.CompilerParams(vmem_limit_bytes=60 * 1024 * 1024),
+        name="cut",
+    )(rows)
+
+
+def route(token_ids, owners, row_slot, sizes):
     peers, _, token_cap, row_cap, pooled = sizes
     passes, seq_len = token_ids.shape
     rows = owners.shape[1]
@@ -223,25 +239,23 @@
             ints(peers, 1, rows + token_cap + row_cap + pooled),
             ints(passes * seq_len, 1),
             ints(1, rows),
-            jax.ShapeDtypeStruct((ahead, stored_rows.shape[1]), stored_rows.dtype),
-        ],
-        in_specs=[pl.BlockSpec(memory_space=pltpu.HBM)] * 4,
+        ],
+        in_specs=[pl.BlockSpec(memory_space=pltpu.HBM)] * 3,
         out_specs=[
             pl.BlockSpec(memory_space=pltpu.VMEM),
             pl.BlockSpec(memory_space=pltpu.HBM),
             pl.BlockSpec(memory_space=pltpu.VMEM),
-            pl.BlockSpec(memory_space=pltpu.HBM),
         ],
         scratch_shapes=[
             pltpu.VMEM(token_ids.shape, jnp.int32),
             pltpu.VMEM(owners.shape, jnp.int32),
             pltpu.VMEM(row_slot.shape, jnp.int32),
             pltpu.VMEM((passes * seq_len, 1), jnp.int32),
-            pltpu.SemaphoreType.DMA((5,)),
+            pltpu.SemaphoreType.DMA((4,)),
         ],
         compiler_params=pltpu.CompilerParams(vmem_limit_bytes=60 * 1024 * 1024),
         name="route",
-    )(token_ids, owners, row_slot, stored_rows)
+    )(token_ids, owners, row_slot)
 
 
 def pack_kernel(half, row_cap, count, picks, pieces, rest, *refs):
@@ -526,13 +540,11 @@
             got.append(lax.ppermute(blocks[step], "dp", moves))
         return got
 
-    ahead = store_count * 7 // 16 // 16 * 16
+    ahead = store_count * 5 // 8 // 16 * 16
     sibling_rows = lax.ppermute(stored_rows, "dp", beside)
+    first_rows = lax.ppermute(cut(stored_rows, ahead), "dp", across)
     sizes = (peer_count, vocab_rows, token_cap, row_cap, row_count - store_count)
-    plan, token_slot, code, first_rows = route(
-        token_ids, row_owner.reshape(1, row_count), row_slot[None], stored_rows, ahead, sizes
-    )
-    first_rows = lax.ppermute(first_rows, "dp", across)
+    plan, token_slot, code = route(token_ids, row_owner.reshape(1, row_count), row_slot[None], sizes)
     sibling_code = lax.ppermute(code, "dp", beside)
     *blocks, last_rows = pack_rows(
         code,
@@ -544,10 +556,11 @@
         row_count,
         rest=store_count - ahead,
     )
-    plan, last_rows, *blocks = lax.optimization_barrier((plan, last_rows, *blocks))
+    plan, *blocks = lax.optimization_barrier((plan, *blocks))
     codes = lax.all_to_all(plan, "dp", split_axis=0, concat_axis=0, tiled=True)
+    own_half = hand_on(blocks)
+    codes, last_rows = lax.optimization_barrier((codes, last_rows))
     last_rows = lax.ppermute(last_rows, "dp", across)
-    own_half = hand_on(blocks)
     plan = codes[:, 0, row_count:]
     wanted = plan[:, :token_cap].reshape(peer_count * token_cap)
     chosen = wanted[:, None] == jnp.arange(vocab_rows, dtype=jnp.int32)[None, :]

time: 92.6 us -> 94.6 us (1.022)
  waiting for transfers between devices: 29.4 us -> 33.7 us
  Pallas kernels: 25.7 us -> 21.7 us
  starting transfers between devices: 27.8 us -> 29.6 us
    ppermute x1, waiting for transfers between devices: 1.25 us -> 14.4 us  [shards(): first_rows = lax.ppermute(cut(stored_rows, ahead), 'dp', across)]
    all_to_all x1, waiting for transfers between devices: 11.3 us -> 0.01 us  [shards(): codes = lax.all_to_all(plan, 'dp', split_axis=0, concat_axis=0, tiled=True)]
    pallas_call x1, Pallas kernels: 7.71 us -> 2.27 us  [route(): pl.pallas_call(functools.partial(route_kernel, sizes), out_shape=[ints(pe...]
    ppermute x1, waiting for transfers between devices: 0.01 us -> 4.34 us  [shards(): last_rows = lax.ppermute(last_rows, 'dp', across)]
    all_to_all x1, starting transfers between devices: 3.91 us -> 7.27 us  [shards(): codes = lax.all_to_all(plan, 'dp', split_axis=0, concat_axis=0, tiled=True)]
    ppermute x1, starting transfers between devices: 3.84 us -> 0.62 us  [shards(): last_rows = lax.ppermute(last_rows, 'dp', across)]
    ppermute x6, waiting for transfers between devices: 1.95 us -> 0.02 us  [hand_on(): got.append(lax.ppermute(blocks[step], 'dp', moves))]
    pallas_call x0 -> x1, Pallas kernels: none -> 1.69 us  [cut(): pl.pallas_call(cut_kernel, out_shape=jax.ShapeDtypeStruct(shape, rows.dty...]
  transfers between devices with their start and end apart: 15 -> 15, of which waited for: 6 -> 5; matrix products, arithmetic and copies ran while one was open for 4% -> 4% of each run, Pallas kernels for 21% -> 16%
where the time goes in v10:
time: 94.6 us; the launch traced here: 94.2 us
  waiting for transfers between devices  33.7 us (36%)
  starting transfers between devices  29.6 us (31%)
  Pallas kernels  21.7 us (23%)
  local copies, waits for them, and re-layouts  6.96 us (7%)
  matrix products  1.29 us (1%)
    ppermute x1, waiting for transfers between devices, shards(): first_rows = lax.ppermute(cut(stored_rows, ahead), 'dp', across)  14.4 us
    ppermute x6, starting transfers between devices, hand_on(): got.append(lax.ppermute(blocks[step], 'dp', moves))  8.15 us
    all_to_all x1, starting transfers between devices, shards(): codes = lax.all_to_all(plan, 'dp', split_axis=0, concat_axis=0, tiled=True)  7.27 us
    all_to_all x1, waiting for transfers between devices, shards(): lax.all_to_all(found.reshape(peer_count, token_cap, width), 'dp', split_a...  6.88 us
    all_to_all x1, waiting for transfers between devices, shards(): lax.all_to_all(spread, 'dp', split_axis=0, concat_axis=0, tiled=True)  6.83 us
    pallas_call x2, Pallas kernels, pack_rows(): pl.pallas_call(functools.partial(pack_kernel, half, row_cap, count, picks...  5.51 us
    all_to_all x1, starting transfers between devices, shards(): lax.all_to_all(spread, 'dp', split_axis=0, concat_axis=0, tiled=True)  5.19 us
    pallas_call x1, Pallas kernels, encode(): pl.pallas_call(encode_kernel, out_shape=[jax.ShapeDtypeStruct((passes, wi...  4.97 us
  transfers between devices with their start and end apart: 15, of which 5 were waited for; matrix products, arithmetic and copies ran while one was open for 4% of the time, Pallas kernels for 16%

profile of v10, /device:TPU:0, one launch (start us, length us, event | category | flops | bytes accessed | tf_op | source)
XLA Modules:
  0.0 94.2 jit_solution(17585026775977543498)
XLA Ops:
  0.6 0.0 copy-start
  0.6 0.5 collective-permute-start.1
  1.2 2.3 %route.1 = (s32[16,1,330]{2,1,0:T(1,128)}, s32[128,1]{1,0:T(8,128)}, s32[1,256]{1,0:T(1,128)}) custom-call(s32[2,64]{1,0:T(2,128)} %token_ids_far.1, s32[1,256]{1,0:T(1,128)} %bitcast.24, s32[1,256]{1,0:T(1,128)} %bitcast.25), custom_call_target="tpu_custom_call" | custom-call | tf_op jit(solution)/shard_map/route/pallas_call | solution.py:236
  3.4 0.2 collective-permute-start
  3.6 1.3 %collective-permute-done.refs_1_ = s32[1,256]{1,0:T(1,128)S(1)} collective-permute-done((s32[1,256]{1,0:T(1,128)}, s32[1,256]{1,0:T(1,128)S(1)}, u32[]{:S(2)}, u32[]{:S(2)}) %collective-permute-start) | collective-permute-done | bytes 1056 | tf_op jit(solution)/shard_map/ppermute | solution.py:548
  4.9 0.0 collective-permute-done.1.refs_3_
  4.9 0.5 copy-done.12
  5.4 0.8 copy-done.2
  6.2 2.7 %pack.2 = (bf16[96,1024]{1,0:T(8,128)(2,1)}, bf16[96,1024]{1,0:T(8,128)(2,1)}, bf16[96,1024]{1,0:T(8,128)(2,1)}, bf16[96,1024]{1,0:T(8,128)(2,1)}, bf16[110,1024]{1,0:T(8,128)(2,1)}) custom-call(s32[1,256]{1,0:T(1,128)} %get-tuple-element.37.refs_0_, s32[1,256]{1,0:T(1,128)} %copy-done.12, bf16[254,1024]{1,0:T(8,128)(2,1)} %far.1, bf16[254,1024]{1,0:T(8,128)(2,1)} %copy-done.2), custom_call_target="tpu_custom_call" | custom-call | flops 199753728 | bytes 1826816 | tf_op jit(solution)/shard_map/pack/pallas_call | solution.py:324
  8.8 0.0 copy-start.13
  8.9 7.3 %all-to-all-start = ((s32[16,1,330]{2,1,0:T(1,128)}), s32[16,1,330]{2,1,0:T(1,128)S(1)}, u32[]{:S(2)}, u32[]{:S(2)}) async-start(s32[16,1,330]{2,1,0:T(1,128)} %get-tuple-element.42), calls=%async_computation | async-start | bytes 49152 | tf_op jit(solution)/shard_map/all_to_all | solution.py:560
  16.1 1.7 %cut.1 = bf16[144,1024]{1,0:T(8,128)(2,1)} custom-call(bf16[254,1024]{1,0:T(8,128)(2,1)} %far.1), custom_call_target="tpu_custom_call" | custom-call | tf_op jit(solution)/shard_map/cut/pallas_call | solution.py:220
  17.8 2.9 %collective-permute-start.2 = (bf16[144,1024]{1,0:T(8,128)(2,1)}, bf16[144,1024]{1,0:T(8,128)(2,1)S(1)}, u32[]{:S(2)}, u32[]{:S(2)}) collective-permute-start(bf16[144,1024]{1,0:T(8,128)(2,1)} %cut.1), channel_id=1, source_target_pairs={{0,8},{1,9},{2,10},{3,11},{4,12},{5,13},{6,14},{7,15},{8,0},{9,1},... | collective-permute-start | bytes 884744 | tf_op jit(solution)/shard_map/ppermute | solution.py:545
  20.7 1.5 %collective-permute-start.3 = (bf16[96,1024]{1,0:T(8,128)(2,1)}, bf16[96,1024]{1,0:T(8,128)(2,1)S(1)}, u32[]{:S(2)}, u32[]{:S(2)}) collective-permute-start(bf16[96,1024]{1,0:T(8,128)(2,1)} %get-tuple-element.46), channel_id=1, source_target_pairs={{0,2},{1,3},{2,0},{3,1},{4,6},{5,7},{6,4},{7,5},{8,10},{9,11},{10,... | collective-permute-start | bytes 589832 | tf_op jit(solution)/shard_map/ppermute | solution.py:540
  22.2 1.5 %collective-permute-start.4 = (bf16[96,1024]{1,0:T(8,128)(2,1)}, bf16[96,1024]{1,0:T(8,128)(2,1)S(1)}, u32[]{:S(2)}, u32[]{:S(2)}) collective-permute-start(bf16[96,1024]{1,0:T(8,128)(2,1)} %get-tuple-element.47), channel_id=1, source_target_pairs={{0,4},{1,5},{2,6},{3,7},{4,0},{5,1},{6,2},{7,3},{8,12},{9,13},{10,... | collective-permute-start | bytes 589832 | tf_op jit(solution)/shard_map/ppermute | solution.py:540
  23.6 0.0 all-to-all-done.refs_0_.refs_1_
  23.7 0.1 eq.15
  23.8 0.6 collective-permute-start.6
  24.4 0.0 copy-done
  24.4 1.3 %convolution_convert_fusion = bf16[384,1024]{1,0:T(8,128)(2,1)} fusion(bf16[240,1024]{1,0:T(8,128)(2,1)S(1)} %copy-done, s32[384]{0:T(512)S(1)} %eq.15), kind=kOutput, calls=%fused_computation.1 | convolution fusion | flops 189229056 | bytes 1279488 | tf_op jit(solution)/shard_map/dot_general | solution.py:567
  25.7 14.4 %collective-permute-done.2.refs_2_ = bf16[144,1024]{1,0:T(8,128)(2,1)S(1)} collective-permute-done((bf16[144,1024]{1,0:T(8,128)(2,1)}, bf16[144,1024]{1,0:T(8,128)(2,1)S(1)}, u32[]{:S(2)}, u32[]{:S(2)}) %collective-permute-start.2) | collective-permute-done | bytes 294944 | tf_op jit(solution)/shard_map/ppermute | solution.py:545
  40.1 0.0 collective-permute-done.3.rest_1_
  40.1 0.0 collective-permute-done.4.rest_2_
  40.1 0.0 copy-start.15
  40.1 0.1 collective-permute-start.7
  40.2 4.3 %collective-permute-done.6.refs_3_ = bf16[110,1024]{1,0:T(8,128)(2,1)S(1)} collective-permute-done((bf16[110,1024]{1,0:T(8,128)(2,1)}, bf16[110,1024]{1,0:T(8,128)(2,1)S(1)}, u32[]{:S(2)}, u32[]{:S(2)}) %collective-permute-start.6) | collective-permute-done | bytes 225312 | tf_op jit(solution)/shard_map/ppermute | solution.py:563
  44.5 0.0 collective-permute-start.8
  44.5 0.0 copy-done.13
  44.5 1.7 %collective-permute-start.5 = (bf16[96,1024]{1,0:T(8,128)(2,1)S(1)}, bf16[96,1024]{1,0:T(8,128)(2,1)S(1)}, u32[]{:S(2)}, u32[]{:S(2)}) collective-permute-start(bf16[96,1024]{1,0:T(8,128)(2,1)S(1)} %copy-done.13), channel_id=1, source_target_pairs={{0,6},{1,7},{2,4},{3,5},{4,2},{5,3},{6,0},{7,1},{8,14},{9,15},{10,... | collective-permute-start | bytes 589832 | tf_op jit(solution)/shard_map/ppermute | solution.py:540
  46.2 0.1 slice.20
  46.3 0.1 slice.19
  46.3 0.6 reshape.42.late_far
  47.0 0.6 gather_fusion
  47.5 0.7 reshape.41.places_far
  48.2 4.7 %all-to-all-start.1 = ((bf16[16,24,1024]{2,1,0:T(8,128)(2,1)}), bf16[16,24,1024]{2,1,0:T(8,128)(2,1)S(1)}, u32[]{:S(2)}, u32[]{:S(2)}) async-start(bf16[16,24,1024]{2,1,0:T(8,128)(2,1)} %bitcast.4), calls=%async_computation.1 | async-start | bytes 1572864 | tf_op jit(solution)/shard_map/all_to_all | solution.py:573
  52.9 0.0 collective-permute-done.8.refs_5_
  52.9 0.0 copy-start.8
  52.9 0.0 collective-permute-done.7.refs_4_
  52.9 0.0 copy-done.5
  52.9 0.0 copy-done.3
  52.9 0.0 copy-done.7
  53.0 0.6 copy-done.8
  53.6 0.7 copy-done.4
  54.3 2.9 %pack.3 = (bf16[96,1024]{1,0:T(8,128)(2,1)}, bf16[96,1024]{1,0:T(8,128)(2,1)}, bf16[96,1024]{1,0:T(8,128)(2,1)}, bf16[96,1024]{1,0:T(8,128)(2,1)}) custom-call(s32[16,1,330]{2,1,0:T(1,128)} %copy-done.5, s32[16,1,330]{2,1,0:T(1,128)} %copy-done.5, bf16[144,1024]{1,0:T(8,128)(2,1)} %copy-done.3, bf16[110,1024]{1,0:T(8,128)(2,1)} %copy-done.7, ...), custom_call_target="tpu_custom_call" | custom-call | flops 199753728 | bytes 1826816 | tf_op jit(solution)/shard_map/pack/pallas_call | solution.py:324
  57.1 2.0 %collective-permute-start.9 = (bf16[96,1024]{1,0:T(8,128)(2,1)}, bf16[96,1024]{1,0:T(8,128)(2,1)S(1)}, u32[]{:S(2)}, u32[]{:S(2)}) collective-permute-start(bf16[96,1024]{1,0:T(8,128)(2,1)} %get-tuple-element.65), channel_id=1, source_target_pairs={{0,2},{1,3},{2,0},{3,1},{4,6},{5,7},{6,4},{7,5},{8,10},{9,11},{10,... | collective-permute-start | bytes 589832 | tf_op jit(solution)/shard_map/ppermute | solution.py:540
  59.1 1.5 %collective-permute-start.10 = (bf16[96,1024]{1,0:T(8,128)(2,1)}, bf16[96,1024]{1,0:T(8,128)(2,1)S(1)}, u32[]{:S(2)}, u32[]{:S(2)}) collective-permute-start(bf16[96,1024]{1,0:T(8,128)(2,1)} %get-tuple-element.66), channel_id=1, source_target_pairs={{0,4},{1,5},{2,6},{3,7},{4,0},{5,1},{6,2},{7,3},{8,12},{9,13},{10,... | collective-permute-start | bytes 589832 | tf_op jit(solution)/shard_map/ppermute | solution.py:540
  60.6 0.1 collective-permute-start.11
  60.7 0.0 collective-permute-done.5.rest_3_
  60.7 0.0 copy-done.14
  60.7 0.0 copy-done.15
  60.7 0.7 copy-done.16
  61.4 3.8 %early.1 = (f32[512,1024]{1,0:T(8,128)}, f32[512,128]{1,0:T(8,128)}) custom-call(s32[1,768]{1,0:T(1,128)} %reshape.41.places_far, f32[512,1024]{1,0:T(8,128)} %centroids_far.1, bf16[96,1024]{1,0:T(8,128)(2,1)} %get-tuple-element.49.rest_0_, bf16[96,1024]{1,0:T(8,128)(2,1)} %copy-done.14, bf16[96,1024]{1,0:T(8,128)(2,1)} %copy-done.15, ...), custom_call_target="tpu_custom_call" | custom-call | flops 20132659200 | bytes 104857600 | tf_op jit(solution)/shard_map/early/pallas_call | solution.py:447
  65.1 6.9 %all-to-all-done.1 = bf16[16,24,1024]{2,1,0:T(8,128)(2,1)S(1)} async-done(((bf16[16,24,1024]{2,1,0:T(8,128)(2,1)}), bf16[16,24,1024]{2,1,0:T(8,128)(2,1)S(1)}, u32[]{:S(2)}, u32[]{:S(2)}) %all-to-all-start.1) | async-done | bytes 786464 | tf_op jit(solution)/shard_map/all_to_all | solution.py:573
  72.0 0.9 copy-done.1
  72.9 5.0 %encode.1 = (bf16[2,1024]{1,0:T(2,128)(2,1)}, bf16[16,2,1024]{2,1,0:T(2,128)(2,1)}) custom-call(s32[1,2]{1,0:T(1,128)} %bitcast.26, s32[128,1]{1,0:T(8,128)} %get-tuple-element.35.refs_1_, bf16[384,1024]{1,0:T(8,128)(2,1)} %bitcast.15, bf16[64,1024]{1,0:T(8,128)(2,1)} %refs_3_.1, f32[1,1024]{1,0:T(1,128)} %bitcast.19, f32[1,1024]{1,0:T(1,128)} %bitcast.20, ...), custom_call_target="tpu_custom_call" | custom-call | flops 637534208 | bytes 6291456 | tf_op jit(solution)/shard_map/encode/pallas_call | solution.py:121
  77.9 5.2 %all-to-all-start.2 = ((bf16[16,2,1024]{2,1,0:T(2,128)(2,1)}), bf16[16,2,1024]{2,1,0:T(2,128)(2,1)S(1)}, u32[]{:S(2)}, u32[]{:S(2)}) async-start(bf16[16,2,1024]{2,1,0:T(2,128)(2,1)} %get-tuple-element.59), calls=%async_computation.2 | async-start | bytes 131072 | tf_op jit(solution)/shard_map/all_to_all | solution.py:606
  83.1 0.0 collective-permute-done.9.rest_1_
  83.1 0.0 collective-permute-done.10.rest_2_
  83.1 0.0 collective-permute-done.11.rest_3_
  83.1 0.0 copy-start.11
  83.1 6.8 %all-to-all-done.2.spread_far = bf16[16,2,1024]{2,1,0:T(2,128)(2,1)S(1)} async-done(((bf16[16,2,1024]{2,1,0:T(2,128)(2,1)}), bf16[16,2,1024]{2,1,0:T(2,128)(2,1)S(1)}, u32[]{:S(2)}, u32[]{:S(2)}) %all-to-all-start.2) | async-done | bytes 65568 | tf_op jit(solution)/shard_map/all_to_all | solution.py:606
  90.0 0.0 copy-done.10
  90.0 0.6 copy-done.6
  90.6 3.6 %late.1 = f32[512,1024]{1,0:T(8,128)} custom-call(s32[1,768]{1,0:T(1,128)} %reshape.41.places_far, s32[1,32]{1,0:T(1,128)} %reshape.42.late_far, bf16[16,2,1024]{2,1,0:T(2,128)(2,1)} %copy-done.6, f32[512,128]{1,0:T(8,128)} %get-tuple-element.60.share_far, f32[512,1024]{1,0:T(8,128)} %get-tuple-element.61.early_far, ...), custom_call_target="tpu_custom_call" | custom-call | flops 436207616 | bytes 4194304 | tf_op jit(solution)/shard_map/late/pallas_call | solution.py:479
  (17 shorter events, 0.0 us)
Async XLA Ops:
  0.6 23.7 %copy-start = (bf16[240,1024]{1,0:T(8,128)(2,1)S(1)}, bf16[240,1024]{1,0:T(8,128)(2,1)}, u32[]{:S(2)}) copy-start(bf16[240,1024]{1,0:T(8,128)(2,1)} %param.17) | copy-start | bytes 1474564
  0.6 4.2 %collective-permute-start.1 = (bf16[254,1024]{1,0:T(8,128)(2,1)}, bf16[254,1024]{1,0:T(8,128)(2,1)S(1)}, u32[]{:S(2)}, u32[]{:S(2)}) collective-permute-start(bf16[254,1024]{1,0:T(8,128)(2,1)} %far.1), channel_id=1, source_target_pairs={{0,1},{1,0},{2,3},{3,2},{4,5},{5,4},{6,7},{7,6},{8,9},{9,8},{10,11... | collective-permute-start | bytes 1560584 | tf_op jit(solution)/shard_map/ppermute | solution.py:544
  3.4 1.4 %collective-permute-start = (s32[1,256]{1,0:T(1,128)}, s32[1,256]{1,0:T(1,128)S(1)}, u32[]{:S(2)}, u32[]{:S(2)}) collective-permute-start(s32[1,256]{1,0:T(1,128)} %get-tuple-element.37.refs_0_), channel_id=1, source_target_pairs={{0,1},{1,0},{2,3},{3,2},{4,5},{5,4},{6,7},{7,6},{8,9},{9,8},{10,11... | collective-permute-start | bytes 3080 | tf_op jit(solution)/shard_map/ppermute | solution.py:548
  4.9 0.5 copy-start.12
  5.4 0.8 copy-start.2
  8.8 35.7 %copy-start.13 = (bf16[96,1024]{1,0:T(8,128)(2,1)S(1)}, bf16[96,1024]{1,0:T(8,128)(2,1)}, u32[]{:S(2)}) copy-start(bf16[96,1024]{1,0:T(8,128)(2,1)} %get-tuple-element.52) | copy-start | bytes 589828
  8.9 14.8 %all-to-all-start = ((s32[16,1,330]{2,1,0:T(1,128)}), s32[16,1,330]{2,1,0:T(1,128)S(1)}, u32[]{:S(2)}, u32[]{:S(2)}) async-start(s32[16,1,330]{2,1,0:T(1,128)} %get-tuple-element.42), calls=%async_computation | async-start | bytes 49152 | tf_op jit(solution)/shard_map/all_to_all | solution.py:560
  17.8 22.2 %collective-permute-start.2 = (bf16[144,1024]{1,0:T(8,128)(2,1)}, bf16[144,1024]{1,0:T(8,128)(2,1)S(1)}, u32[]{:S(2)}, u32[]{:S(2)}) collective-permute-start(bf16[144,1024]{1,0:T(8,128)(2,1)} %cut.1), channel_id=1, source_target_pairs={{0,8},{1,9},{2,10},{3,11},{4,12},{5,13},{6,14},{7,15},{8,0},{9,1},... | collective-permute-start | bytes 884744 | tf_op jit(solution)/shard_map/ppermute | solution.py:545
  20.7 19.3 %collective-permute-start.3 = (bf16[96,1024]{1,0:T(8,128)(2,1)}, bf16[96,1024]{1,0:T(8,128)(2,1)S(1)}, u32[]{:S(2)}, u32[]{:S(2)}) collective-permute-start(bf16[96,1024]{1,0:T(8,128)(2,1)} %get-tuple-element.46), channel_id=1, source_target_pairs={{0,2},{1,3},{2,0},{3,1},{4,6},{5,7},{6,4},{7,5},{8,10},{9,11},{10,... | collective-permute-start | bytes 589832 | tf_op jit(solution)/shard_map/ppermute | solution.py:540
  22.2 17.9 %collective-permute-start.4 = (bf16[96,1024]{1,0:T(8,128)(2,1)}, bf16[96,1024]{1,0:T(8,128)(2,1)S(1)}, u32[]{:S(2)}, u32[]{:S(2)}) collective-permute-start(bf16[96,1024]{1,0:T(8,128)(2,1)} %get-tuple-element.47), channel_id=1, source_target_pairs={{0,4},{1,5},{2,6},{3,7},{4,0},{5,1},{6,2},{7,3},{8,12},{9,13},{10,... | collective-permute-start | bytes 589832 | tf_op jit(solution)/shard_map/ppermute | solution.py:540
  23.7 29.3 %copy-start.5 = (s32[16,1,330]{2,1,0:T(1,128)}, s32[16,1,330]{2,1,0:T(1,128)S(1)}, u32[]{:S(2)}) copy-start(s32[16,1,330]{2,1,0:T(1,128)S(1)} %all-to-all-done.refs_0_.refs_1_) | copy-start | bytes 63364
  23.8 20.7 %collective-permute-start.6 = (bf16[110,1024]{1,0:T(8,128)(2,1)}, bf16[110,1024]{1,0:T(8,128)(2,1)S(1)}, u32[]{:S(2)}, u32[]{:S(2)}) collective-permute-start(bf16[110,1024]{1,0:T(8,128)(2,1)} %get-tuple-element.63), channel_id=1, source_target_pairs={{0,8},{1,9},{2,10},{3,11},{4,12},{5,13},{6,14},{7,15},{8,0},{9,1},... | collective-permute-start | bytes 675848 | tf_op jit(solution)/shard_map/ppermute | solution.py:563
  40.1 12.9 %copy-start.3 = (bf16[144,1024]{1,0:T(8,128)(2,1)}, bf16[144,1024]{1,0:T(8,128)(2,1)S(1)}, u32[]{:S(2)}) copy-start(bf16[144,1024]{1,0:T(8,128)(2,1)S(1)} %collective-permute-done.2.refs_2_) | copy-start | bytes 884740
  40.1 20.6 %copy-start.14 = (bf16[96,1024]{1,0:T(8,128)(2,1)}, bf16[96,1024]{1,0:T(8,128)(2,1)S(1)}, u32[]{:S(2)}) copy-start(bf16[96,1024]{1,0:T(8,128)(2,1)S(1)} %collective-permute-done.3.rest_1_) | copy-start | bytes 589828
  40.1 20.6 %copy-start.15 = (bf16[96,1024]{1,0:T(8,128)(2,1)}, bf16[96,1024]{1,0:T(8,128)(2,1)S(1)}, u32[]{:S(2)}) copy-start(bf16[96,1024]{1,0:T(8,128)(2,1)S(1)} %collective-permute-done.4.rest_2_) | copy-start | bytes 589828
  40.1 12.8 %collective-permute-start.7 = (bf16[144,1024]{1,0:T(8,128)(2,1)S(1)}, bf16[144,1024]{1,0:T(8,128)(2,1)S(1)}, u32[]{:S(2)}, u32[]{:S(2)}) collective-permute-start(bf16[144,1024]{1,0:T(8,128)(2,1)S(1)} %collective-permute-done.2.refs_2_), channel_id=1, source_target_pairs={{0,1},{1,0},{2,3},{3,2},{4,5},{5,4},{6,7},{7,6},{8,9},{9,8},{10,11... | collective-permute-start | bytes 884744 | tf_op jit(solution)/shard_map/ppermute | solution.py:578
  44.5 8.4 %copy-start.7 = (bf16[110,1024]{1,0:T(8,128)(2,1)}, bf16[110,1024]{1,0:T(8,128)(2,1)S(1)}, u32[]{:S(2)}) copy-start(bf16[110,1024]{1,0:T(8,128)(2,1)S(1)} %collective-permute-done.6.refs_3_) | copy-start | bytes 675844
  44.5 8.4 %collective-permute-start.8 = (bf16[110,1024]{1,0:T(8,128)(2,1)S(1)}, bf16[110,1024]{1,0:T(8,128)(2,1)S(1)}, u32[]{:S(2)}, u32[]{:S(2)}) collective-permute-start(bf16[110,1024]{1,0:T(8,128)(2,1)S(1)} %collective-permute-done.6.refs_3_), channel_id=1, source_target_pairs={{0,1},{1,0},{2,3},{3,2},{4,5},{5,4},{6,7},{7,6},{8,9},{9,8},{10,11... | collective-permute-start | bytes 675848 | tf_op jit(solution)/shard_map/ppermute | solution.py:578
  44.5 16.2 %collective-permute-start.5 = (bf16[96,1024]{1,0:T(8,128)(2,1)S(1)}, bf16[96,1024]{1,0:T(8,128)(2,1)S(1)}, u32[]{:S(2)}, u32[]{:S(2)}) collective-permute-start(bf16[96,1024]{1,0:T(8,128)(2,1)S(1)} %copy-done.13), channel_id=1, source_target_pairs={{0,6},{1,7},{2,4},{3,5},{4,2},{5,3},{6,0},{7,1},{8,14},{9,15},{10,... | collective-permute-start | bytes 589832 | tf_op jit(solution)/shard_map/ppermute | solution.py:540
  48.2 23.8 %all-to-all-start.1 = ((bf16[16,24,1024]{2,1,0:T(8,128)(2,1)}), bf16[16,24,1024]{2,1,0:T(8,128)(2,1)S(1)}, u32[]{:S(2)}, u32[]{:S(2)}) async-start(bf16[16,24,1024]{2,1,0:T(8,128)(2,1)} %bitcast.4), calls=%async_computation.1 | async-start | bytes 1572864 | tf_op jit(solution)/shard_map/all_to_all | solution.py:573
  52.9 0.7 copy-start.8
  53.6 0.7 copy-start.4
  57.1 25.9 %collective-permute-start.9 = (bf16[96,1024]{1,0:T(8,128)(2,1)}, bf16[96,1024]{1,0:T(8,128)(2,1)S(1)}, u32[]{:S(2)}, u32[]{:S(2)}) collective-permute-start(bf16[96,1024]{1,0:T(8,128)(2,1)} %get-tuple-element.65), channel_id=1, source_target_pairs={{0,2},{1,3},{2,0},{3,1},{4,6},{5,7},{6,4},{7,5},{8,10},{9,11},{10,... | collective-permute-start | bytes 589832 | tf_op jit(solution)/shard_map/ppermute | solution.py:540
  59.1 24.0 %collective-permute-start.10 = (bf16[96,1024]{1,0:T(8,128)(2,1)}, bf16[96,1024]{1,0:T(8,128)(2,1)S(1)}, u32[]{:S(2)}, u32[]{:S(2)}) collective-permute-start(bf16[96,1024]{1,0:T(8,128)(2,1)} %get-tuple-element.66), channel_id=1, source_target_pairs={{0,4},{1,5},{2,6},{3,7},{4,0},{5,1},{6,2},{7,3},{8,12},{9,13},{10,... | collective-permute-start | bytes 589832 | tf_op jit(solution)/shard_map/ppermute | solution.py:540
  60.6 22.5 %collective-permute-start.11 = (bf16[96,1024]{1,0:T(8,128)(2,1)}, bf16[96,1024]{1,0:T(8,128)(2,1)S(1)}, u32[]{:S(2)}, u32[]{:S(2)}) collective-permute-start(bf16[96,1024]{1,0:T(8,128)(2,1)} %get-tuple-element.67), channel_id=1, source_target_pairs={{0,6},{1,7},{2,4},{3,5},{4,2},{5,3},{6,0},{7,1},{8,14},{9,15},{10,... | collective-permute-start | bytes 589832 | tf_op jit(solution)/shard_map/ppermute | solution.py:540
  60.7 0.7 copy-start.16
  72.0 0.9 copy-start.1
  77.9 12.1 %all-to-all-start.2 = ((bf16[16,2,1024]{2,1,0:T(2,128)(2,1)}), bf16[16,2,1024]{2,1,0:T(2,128)(2,1)S(1)}, u32[]{:S(2)}, u32[]{:S(2)}) async-start(bf16[16,2,1024]{2,1,0:T(2,128)(2,1)} %get-tuple-element.59), calls=%async_computation.2 | async-start | bytes 131072 | tf_op jit(solution)/shard_map/all_to_all | solution.py:606
  83.1 6.9 %copy-start.9 = (bf16[96,1024]{1,0:T(8,128)(2,1)}, bf16[96,1024]{1,0:T(8,128)(2,1)S(1)}, u32[]{:S(2)}) copy-start(bf16[96,1024]{1,0:T(8,128)(2,1)S(1)} %collective-permute-done.9.rest_1_) | copy-start | bytes 589828
  83.1 6.9 %copy-start.10 = (bf16[96,1024]{1,0:T(8,128)(2,1)}, bf16[96,1024]{1,0:T(8,128)(2,1)S(1)}, u32[]{:S(2)}) copy-start(bf16[96,1024]{1,0:T(8,128)(2,1)S(1)} %collective-permute-done.10.rest_2_) | copy-start | bytes 589828
  83.1 6.9 %copy-start.11 = (bf16[96,1024]{1,0:T(8,128)(2,1)}, bf16[96,1024]{1,0:T(8,128)(2,1)S(1)}, u32[]{:S(2)}) copy-start(bf16[96,1024]{1,0:T(8,128)(2,1)S(1)} %collective-permute-done.11.rest_3_) | copy-start | bytes 589828
  90.0 0.6 copy-start.6

commit v11 on v10

--- a/solution.py
+++ b/solution.py
@@ -206,28 +206,6 @@
     send.wait()
 
 
-def cut_kernel(far, out_far, near, done):
-    load = pltpu.make_async_copy(far.at[pl.ds(0, near.shape[0])], near, done.at[0])
-    load.start()
-    load.wait()
-    send = pltpu.make_async_copy(near, out_far, done.at[1])
-    send.start()
-    send.wait()
-
-
-def cut(rows, count):
-    shape = (count, rows.shape[1])
-    return pl.pallas_call(
-        cut_kernel,
-        out_shape=jax.ShapeDtypeStruct(shape, rows.dtype),
-        in_specs=[pl.BlockSpec(memory_space=pltpu.HBM)],
-        out_specs=pl.BlockSpec(memory_space=pltpu.HBM),
-        scratch_shapes=[pltpu.VMEM(shape, rows.dtype), pltpu.SemaphoreType.DMA((2,))],
-        compiler_params=pltpu.CompilerParams(vmem_limit_bytes=60 * 1024 * 1024),
-        name="cut",
-    )(rows)
-
-
 def route(token_ids, owners, row_slot, sizes):
     peers, _, token_cap, row_cap, pooled = sizes
     passes, seq_len = token_ids.shape
@@ -258,17 +236,12 @@
     )(token_ids, owners, row_slot)
 
 
-def pack_kernel(half, row_cap, count, picks, pieces, rest, *refs):
+def pack_kernel(half, row_cap, count, picks, *refs):
     me = lax.axis_index("dp")
-    operands = 2 + 2 * pieces
-    far, refs = refs[:operands], refs[operands:]
     steps = half // 2
-    outs, refs = refs[: steps + bool(rest)], refs[steps + bool(rest) :]
-    near, (blocks, tail, arrived, left) = refs[:operands], refs[operands:]
+    far, outs, near, (blocks, arrived, left) = refs[:4], refs[4:-7], refs[-7:-3], refs[-3:]
     size = blocks.shape[0] // steps
-    copies = [
-        pltpu.make_async_copy(far[at], near[at], arrived.at[at]) for at in range(operands)
-    ]
+    copies = [pltpu.make_async_copy(far[at], near[at], arrived.at[at]) for at in range(4)]
     for copy in copies:
         copy.start()
     for copy in copies[:2]:
@@ -276,62 +249,46 @@
     if size > 2 * row_cap:
         blocks[...] = jnp.zeros(blocks.shape, blocks.dtype)
     for source in range(2):
-        if picks is None:
-            code = near[source][...]
-        else:
-            code = near[source][me ^ picks[source], :, :count]
+        codes, rows = near[source], near[2 + source]
+        code = codes[...] if picks is None else codes[me ^ picks[source], :, :count]
         bits = rank_bits(count)
         owner, rank = code >> bits, code & (2**bits - 1)
         fits = ((owner ^ me) & (1 | half)) == 0
         chip = ((owner ^ me) & (half - 1)) >> 1
-        slot = jnp.where(fits, chip * row_cap + rank, -1)
-        packed, at = 0.0, 0
-        for piece in range(2 + source * pieces, 2 + (source + 1) * pieces):
-            rows = near[piece]
-            spot = lax.broadcasted_iota(jnp.int32, (steps * row_cap, rows.shape[0]), 0)
-            table = jnp.where(slot[:, at : at + rows.shape[0]] == spot, 1.0, 0.0)
-            copies[piece].wait()
-            packed += jnp.dot(
-                table.astype(jnp.bfloat16), rows[...], preferred_element_type=jnp.float32
-            )
-            at += rows.shape[0]
+        slot = jnp.where(fits, chip * row_cap + rank, -1)[:, : rows.shape[0]]
+        spot = lax.broadcasted_iota(jnp.int32, (steps * row_cap, rows.shape[0]), 0)
+        table = jnp.where(slot == spot, 1.0, 0.0).astype(jnp.bfloat16)
+        copies[2 + source].wait()
+        packed = jnp.dot(table, rows[...], preferred_element_type=jnp.float32)
         packed = packed.astype(jnp.bfloat16)
         for step in range(steps):
             first = step * size + source * row_cap
             blocks[first : first + row_cap, :] = packed[step * row_cap : (step + 1) * row_cap]
     sends = [
-        pltpu.make_async_copy(
-            blocks.at[pl.ds(step * size, size)], outs[step], left.at[step]
-        )
+        pltpu.make_async_copy(blocks.at[pl.ds(step * size, size)], outs[step], left.at[step])
         for step in range(steps)
     ]
-    if rest:
-        tail[...] = near[2][near[2].shape[0] - rest :, :]
-        sends.append(pltpu.make_async_copy(tail, outs[steps], left.at[steps]))
     for send in sends:
         send.start()
     for send in sends:
         send.wait()
 
 
-def pack_rows(codes_a, codes_b, rows_a, rows_b, half, row_cap, count, picks=None, rest=0):
-    width = rows_a[0].shape[1]
-    total = sum(piece.shape[0] for piece in rows_a)
+def pack_rows(codes_a, codes_b, rows_a, rows_b, half, row_cap, count, picks=None):
+    total, width = rows_a.shape
     steps = half // 2
     size = padded(2 * row_cap)
-    operands = (codes_a, codes_b, *rows_a, *rows_b)
-    shapes = [(size, width)] * steps + [(rest, width)] * bool(rest)
+    operands = (codes_a, codes_b, rows_a, rows_b)
     return pl.pallas_call(
-        functools.partial(pack_kernel, half, row_cap, count, picks, len(rows_a), rest),
-        out_shape=[jax.ShapeDtypeStruct(shape, jnp.bfloat16) for shape in shapes],
-        in_specs=[pl.BlockSpec(memory_space=pltpu.HBM)] * len(operands),
-        out_specs=[pl.BlockSpec(memory_space=pltpu.HBM)] * len(shapes),
+        functools.partial(pack_kernel, half, row_cap, count, picks),
+        out_shape=[jax.ShapeDtypeStruct((size, width), jnp.bfloat16)] * steps,
+        in_specs=[pl.BlockSpec(memory_space=pltpu.HBM)] * 4,
+        out_specs=[pl.BlockSpec(memory_space=pltpu.HBM)] * steps,
         scratch_shapes=[
             *(pltpu.VMEM(operand.shape, operand.dtype) for operand in operands),
             pltpu.VMEM((steps * size, width), jnp.bfloat16),
-            pltpu.VMEM((max(rest, 16), width), jnp.bfloat16),
-            pltpu.SemaphoreType.DMA((len(operands),)),
-            pltpu.SemaphoreType.DMA((len(shapes),)),
+            pltpu.SemaphoreType.DMA((4,)),
+            pltpu.SemaphoreType.DMA((steps,)),
         ],
         compiler_params=pltpu.CompilerParams(vmem_limit_bytes=60 * 1024 * 1024),
         cost_estimate=pl.CostEstimate(
@@ -463,8 +420,8 @@
         ],
         compiler_params=pltpu.CompilerParams(vmem_limit_bytes=60 * 1024 * 1024),
         cost_estimate=pl.CostEstimate(
-            flops=100 * centre_count * width * row_total,
-            bytes_accessed=200 * centre_count * width,
+            flops=2 * centre_count * width * row_total,
+            bytes_accessed=8 * centre_count * width,
             transcendentals=0,
         ),
         name="early",
@@ -540,42 +497,29 @@
             got.append(lax.ppermute(blocks[step], "dp", moves))
         return got
 
-    ahead = store_count * 5 // 8 // 16 * 16
+    partner_rows = lax.ppermute(stored_rows, "dp", across)
     sibling_rows = lax.ppermute(stored_rows, "dp", beside)
-    first_rows = lax.ppermute(cut(stored_rows, ahead), "dp", across)
     sizes = (peer_count, vocab_rows, token_cap, row_cap, row_count - store_count)
     plan, token_slot, code = route(token_ids, row_owner.reshape(1, row_count), row_slot[None], sizes)
     sibling_code = lax.ppermute(code, "dp", beside)
-    *blocks, last_rows = pack_rows(
-        code,
-        sibling_code,
-        [stored_rows],
-        [sibling_rows],
-        half,
-        row_cap,
-        row_count,
-        rest=store_count - ahead,
-    )
+    blocks = pack_rows(code, sibling_code, stored_rows, sibling_rows, half, row_cap, row_count)
     plan, *blocks = lax.optimization_barrier((plan, *blocks))
     codes = lax.all_to_all(plan, "dp", split_axis=0, concat_axis=0, tiled=True)
     own_half = hand_on(blocks)
-    codes, last_rows = lax.optimization_barrier((codes, last_rows))
-    last_rows = lax.ppermute(last_rows, "dp", across)
     plan = codes[:, 0, row_count:]
     wanted = plan[:, :token_cap].reshape(peer_count * token_cap)
     chosen = wanted[:, None] == jnp.arange(vocab_rows, dtype=jnp.int32)[None, :]
     found = jnp.dot(
         chosen.astype(jnp.bfloat16), word_table, preferred_element_type=jnp.float32
     ).astype(jnp.bfloat16)
-    found, first_rows, own_half[:3] = lax.optimization_barrier(
-        (found, first_rows, own_half[:3])
+    found, partner_rows, own_half[:3] = lax.optimization_barrier(
+        (found, partner_rows, own_half[:3])
     )
     fetched = lax.all_to_all(
         found.reshape(peer_count, token_cap, width), "dp", split_axis=0, concat_axis=0, tiled=True
     ).reshape(peer_count * token_cap, width)
 
-    partner_rows = [first_rows, last_rows]
-    far_rows = [lax.ppermute(rows, "dp", beside) for rows in partner_rows]
+    far_rows = lax.ppermute(partner_rows, "dp", beside)
     picks = (half, half ^ 1)
     blocks = pack_rows(codes, codes, partner_rows, far_rows, half, row_cap, row_count, picks)
     other_half = hand_on(blocks)

time: 94.6 us -> 87.5 us (0.925)
  waiting for transfers between devices: 33.7 us -> 29.4 us
  Pallas kernels: 21.7 us -> 19.8 us
    ppermute x4 -> x2, waiting for transfers between devices: 18.7 us -> 0.01 us  [the longest x1 0.01 us: shards(): far_rows = lax.ppermute(partner_rows, 'dp', beside)]
    ppermute x6, waiting for transfers between devices: 0.02 us -> 11 us  [hand_on(): got.append(lax.ppermute(blocks[step], 'dp', moves))]
    all_to_all x1, waiting for transfers between devices: 0.01 us -> 10.4 us  [shards(): codes = lax.all_to_all(plan, 'dp', split_axis=0, concat_axis=0, tiled=True)]
    all_to_all x1, waiting for transfers between devices: 6.88 us -> 0.01 us  [shards(): lax.all_to_all(found.reshape(peer_count, token_cap, width), 'dp', split_a...]
    all_to_all x1, starting transfers between devices: 7.27 us -> 4.06 us  [shards(): codes = lax.all_to_all(plan, 'dp', split_axis=0, concat_axis=0, tiled=True)]
    pallas_call x1 -> x0, Pallas kernels: 1.69 us -> none  [cut(): pl.pallas_call(cut_kernel, out_shape=jax.ShapeDtypeStruct(shape, rows.dty...]
    ppermute x6, starting transfers between devices: 8.15 us -> 9.52 us  [hand_on(): got.append(lax.ppermute(blocks[step], 'dp', moves))]
    all_to_all x1, starting transfers between devices: 4.69 us -> 5.89 us  [shards(): lax.all_to_all(found.reshape(peer_count, token_cap, width), 'dp', split_a...]
  transfers between devices with their start and end apart: 15 -> 13, of which waited for: 5 -> 5; matrix products, arithmetic and copies ran while one was open for 4% -> 4% of each run, Pallas kernels for 16% -> 19%
where the time goes in v11:
time: 87.5 us; the launch traced here: 87.1 us
  waiting for transfers between devices  29.4 us (34%)
  starting transfers between devices  29.3 us (33%)
  Pallas kernels  19.8 us (23%)
  local copies, waits for them, and re-layouts  6.49 us (7%)
  matrix products  1.29 us (1%)
    ppermute x6, waiting for transfers between devices, hand_on(): got.append(lax.ppermute(blocks[step], 'dp', moves))  11 us
    all_to_all x1, waiting for transfers between devices, shards(): codes = lax.all_to_all(plan, 'dp', split_axis=0, concat_axis=0, tiled=True)  10.4 us
    ppermute x6, starting transfers between devices, hand_on(): got.append(lax.ppermute(blocks[step], 'dp', moves))  9.52 us
    all_to_all x1, waiting for transfers between devices, shards(): lax.all_to_all(spread, 'dp', split_axis=0, concat_axis=0, tiled=True)  6.83 us
    all_to_all x1, starting transfers between devices, shards(): lax.all_to_all(found.reshape(peer_count, token_cap, width), 'dp', split_a...  5.89 us
    pallas_call x2, Pallas kernels, pack_rows(): pl.pallas_call(functools.partial(pack_kernel, half, row_cap, count, picks...  5.21 us
    all_to_all x1, starting transfers between devices, shards(): lax.all_to_all(spread, 'dp', split_axis=0, concat_axis=0, tiled=True)  5 us
    pallas_call x1, Pallas kernels, encode(): pl.pallas_call(encode_kernel, out_shape=[jax.ShapeDtypeStruct((passes, wi...  4.96 us
  transfers between devices with their start and end apart: 13, of which 5 were waited for; matrix products, arithmetic and copies ran while one was open for 4% of the time, Pallas kernels for 19%

profile of v11, /device:TPU:0, one launch (start us, length us, event | category | flops | bytes accessed | tf_op | source)
XLA Modules:
  0.0 87.1 jit_solution(14989417456806950502)
XLA Ops:
  0.6 0.0 copy-start
  0.6 0.5 collective-permute-start.1
  1.2 3.7 %collective-permute-start.2 = (bf16[254,1024]{1,0:T(8,128)(2,1)}, bf16[254,1024]{1,0:T(8,128)(2,1)S(1)}, u32[]{:S(2)}, u32[]{:S(2)}) collective-permute-start(bf16[254,1024]{1,0:T(8,128)(2,1)} %refs_2_.1), channel_id=1, source_target_pairs={{0,8},{1,9},{2,10},{3,11},{4,12},{5,13},{6,14},{7,15},{8,0},{9,1},... | collective-permute-start | bytes 1560584 | tf_op jit(solution)/shard_map/ppermute | solution.py:500
  4.8 2.3 %route.1 = (s32[16,1,330]{2,1,0:T(1,128)}, s32[128,1]{1,0:T(8,128)}, s32[1,256]{1,0:T(1,128)}) custom-call(s32[2,64]{1,0:T(2,128)} %token_ids_far.1, s32[1,256]{1,0:T(1,128)} %bitcast.24, s32[1,256]{1,0:T(1,128)} %bitcast.25), custom_call_target="tpu_custom_call" | custom-call | tf_op jit(solution)/shard_map/route/pallas_call | solution.py:214
  7.1 0.2 collective-permute-start
  7.3 1.2 %collective-permute-done.refs_1_ = s32[1,256]{1,0:T(1,128)S(1)} collective-permute-done((s32[1,256]{1,0:T(1,128)}, s32[1,256]{1,0:T(1,128)S(1)}, u32[]{:S(2)}, u32[]{:S(2)}) %collective-permute-start) | collective-permute-done | bytes 1056 | tf_op jit(solution)/shard_map/ppermute | solution.py:504
  8.5 0.0 copy-start.13
  8.5 0.0 collective-permute-done.1.refs_3_
  8.5 0.6 copy-done.13
  9.1 0.0 copy-start.4
  9.1 0.8 copy-done.4
  9.9 2.6 %pack.2 = (bf16[96,1024]{1,0:T(8,128)(2,1)}, bf16[96,1024]{1,0:T(8,128)(2,1)}, bf16[96,1024]{1,0:T(8,128)(2,1)}, bf16[96,1024]{1,0:T(8,128)(2,1)}) custom-call(s32[1,256]{1,0:T(1,128)} %get-tuple-element.34.refs_0_, s32[1,256]{1,0:T(1,128)} %copy-done.13, bf16[254,1024]{1,0:T(8,128)(2,1)} %refs_2_.1, bf16[254,1024]{1,0:T(8,128)(2,1)} %copy-done.4), custom_call_target="tpu_custom_call" | custom-call | flops 199753728 | bytes 1826816 | tf_op jit(solution)/shard_map/pack/pallas_call | solution.py:282
  12.5 0.0 copy-start.14
  12.5 4.1 %all-to-all-start = ((s32[16,1,330]{2,1,0:T(1,128)}), s32[16,1,330]{2,1,0:T(1,128)S(1)}, u32[]{:S(2)}, u32[]{:S(2)}) async-start(s32[16,1,330]{2,1,0:T(1,128)} %get-tuple-element.39), calls=%async_computation | async-start | bytes 49152 | tf_op jit(solution)/shard_map/all_to_all | solution.py:507
  16.6 1.9 %collective-permute-start.3 = (bf16[96,1024]{1,0:T(8,128)(2,1)}, bf16[96,1024]{1,0:T(8,128)(2,1)S(1)}, u32[]{:S(2)}, u32[]{:S(2)}) collective-permute-start(bf16[96,1024]{1,0:T(8,128)(2,1)} %get-tuple-element.41), channel_id=1, source_target_pairs={{0,2},{1,3},{2,0},{3,1},{4,6},{5,7},{6,4},{7,5},{8,10},{9,11},{10,... | collective-permute-start | bytes 589832 | tf_op jit(solution)/shard_map/ppermute | solution.py:497
  18.5 1.5 %collective-permute-start.4 = (bf16[96,1024]{1,0:T(8,128)(2,1)}, bf16[96,1024]{1,0:T(8,128)(2,1)S(1)}, u32[]{:S(2)}, u32[]{:S(2)}) collective-permute-start(bf16[96,1024]{1,0:T(8,128)(2,1)} %get-tuple-element.42), channel_id=1, source_target_pairs={{0,4},{1,5},{2,6},{3,7},{4,0},{5,1},{6,2},{7,3},{8,12},{9,13},{10,... | collective-permute-start | bytes 589832 | tf_op jit(solution)/shard_map/ppermute | solution.py:497
  20.0 10.4 %all-to-all-done.refs_0_.refs_1_ = s32[16,1,330]{2,1,0:T(1,128)S(1)} async-done(((s32[16,1,330]{2,1,0:T(1,128)}), s32[16,1,330]{2,1,0:T(1,128)S(1)}, u32[]{:S(2)}, u32[]{:S(2)}) %all-to-all-start) | async-done | bytes 21152 | tf_op jit(solution)/shard_map/all_to_all | solution.py:507
  30.3 0.1 eq.15
  30.4 0.0 copy-done
  30.4 1.3 %convolution_convert_fusion = bf16[384,1024]{1,0:T(8,128)(2,1)} fusion(bf16[240,1024]{1,0:T(8,128)(2,1)S(1)} %copy-done, s32[384]{0:T(512)S(1)} %eq.15), kind=kOutput, calls=%fused_computation.1 | convolution fusion | flops 189229056 | bytes 1279488 | tf_op jit(solution)/shard_map/dot_general | solution.py:512
  31.7 0.0 collective-permute-done.2.refs_2_
  31.7 0.0 collective-permute-done.3.rest_1_
  31.7 0.0 copy-start.10
  31.7 1.7 %collective-permute-done.4.rest_2_ = bf16[96,1024]{1,0:T(8,128)(2,1)S(1)} collective-permute-done((bf16[96,1024]{1,0:T(8,128)(2,1)}, bf16[96,1024]{1,0:T(8,128)(2,1)S(1)}, u32[]{:S(2)}, u32[]{:S(2)}) %collective-permute-start.4) | collective-permute-done | bytes 196640 | tf_op jit(solution)/shard_map/ppermute | solution.py:497
  33.4 5.9 %all-to-all-start.1 = ((bf16[16,24,1024]{2,1,0:T(8,128)(2,1)}), bf16[16,24,1024]{2,1,0:T(8,128)(2,1)S(1)}, u32[]{:S(2)}, u32[]{:S(2)}) async-start(bf16[16,24,1024]{2,1,0:T(8,128)(2,1)} %bitcast.4), calls=%async_computation.1 | async-start | bytes 1572864 | tf_op jit(solution)/shard_map/all_to_all | solution.py:518
  39.3 0.4 collective-permute-start.6
  39.7 0.0 copy-done.14
  39.7 2.6 %collective-permute-start.5 = (bf16[96,1024]{1,0:T(8,128)(2,1)S(1)}, bf16[96,1024]{1,0:T(8,128)(2,1)S(1)}, u32[]{:S(2)}, u32[]{:S(2)}) collective-permute-start(bf16[96,1024]{1,0:T(8,128)(2,1)S(1)} %copy-done.14), channel_id=1, source_target_pairs={{0,6},{1,7},{2,4},{3,5},{4,2},{5,3},{6,0},{7,1},{8,14},{9,15},{10,... | collective-permute-start | bytes 589832 | tf_op jit(solution)/shard_map/ppermute | solution.py:497
  42.3 0.1 slice.21
  42.4 0.1 slice.20
  42.5 0.7 reshape.42.late_far
  43.1 0.6 gather_fusion
  43.7 0.7 reshape.41.places_far
  44.4 0.0 collective-permute-done.6.refs_3_
  44.4 0.0 copy-done.5
  44.4 0.0 copy-done.2
  44.4 0.0 copy-start.3
  44.4 0.8 copy-done.3
  45.2 2.6 %pack.3 = (bf16[96,1024]{1,0:T(8,128)(2,1)}, bf16[96,1024]{1,0:T(8,128)(2,1)}, bf16[96,1024]{1,0:T(8,128)(2,1)}, bf16[96,1024]{1,0:T(8,128)(2,1)}) custom-call(s32[16,1,330]{2,1,0:T(1,128)} %copy-done.5, s32[16,1,330]{2,1,0:T(1,128)} %copy-done.5, bf16[254,1024]{1,0:T(8,128)(2,1)} %copy-done.2, bf16[254,1024]{1,0:T(8,128)(2,1)} %copy-done.3), custom_call_target="tpu_custom_call" | custom-call | flops 199753728 | bytes 1826816 | tf_op jit(solution)/shard_map/pack/pallas_call | solution.py:282
  47.8 0.6 collective-permute-start.7
  48.4 0.3 collective-permute-start.8
  48.8 2.6 %collective-permute-start.9 = (bf16[96,1024]{1,0:T(8,128)(2,1)}, bf16[96,1024]{1,0:T(8,128)(2,1)S(1)}, u32[]{:S(2)}, u32[]{:S(2)}) collective-permute-start(bf16[96,1024]{1,0:T(8,128)(2,1)} %get-tuple-element.61), channel_id=1, source_target_pairs={{0,6},{1,7},{2,4},{3,5},{4,2},{5,3},{6,0},{7,1},{8,14},{9,15},{10,... | collective-permute-start | bytes 589832 | tf_op jit(solution)/shard_map/ppermute | solution.py:497
  51.4 9.3 %collective-permute-done.5.rest_3_ = bf16[96,1024]{1,0:T(8,128)(2,1)S(1)} collective-permute-done((bf16[96,1024]{1,0:T(8,128)(2,1)S(1)}, bf16[96,1024]{1,0:T(8,128)(2,1)S(1)}, u32[]{:S(2)}, u32[]{:S(2)}) %collective-permute-start.5) | collective-permute-done | bytes 196640 | tf_op jit(solution)/shard_map/ppermute | solution.py:497
  60.7 0.0 copy-done.10
  60.7 0.0 copy-done.11
  60.7 0.7 copy-done.12
  61.3 3.8 %early.1 = (f32[512,1024]{1,0:T(8,128)}, f32[512,128]{1,0:T(8,128)}) custom-call(s32[1,768]{1,0:T(1,128)} %reshape.41.places_far, f32[512,1024]{1,0:T(8,128)} %centroids_far.1, bf16[96,1024]{1,0:T(8,128)(2,1)} %get-tuple-element.44.rest_0_, bf16[96,1024]{1,0:T(8,128)(2,1)} %copy-done.10, bf16[96,1024]{1,0:T(8,128)(2,1)} %copy-done.11, ...), custom_call_target="tpu_custom_call" | custom-call | flops 402653184 | bytes 4194304 | tf_op jit(solution)/shard_map/early/pallas_call | solution.py:404
  65.1 0.0 all-to-all-done.1
  65.1 0.0 copy-start.1
  65.1 0.9 copy-done.1
  66.0 5.0 %encode.1 = (bf16[2,1024]{1,0:T(2,128)(2,1)}, bf16[16,2,1024]{2,1,0:T(2,128)(2,1)}) custom-call(s32[1,2]{1,0:T(1,128)} %bitcast.26, s32[128,1]{1,0:T(8,128)} %get-tuple-element.32.refs_1_, bf16[384,1024]{1,0:T(8,128)(2,1)} %bitcast.15, bf16[64,1024]{1,0:T(8,128)(2,1)} %refs_3_.1, f32[1,1024]{1,0:T(1,128)} %bitcast.19, f32[1,1024]{1,0:T(1,128)} %bitcast.20, ...), custom_call_target="tpu_custom_call" | custom-call | flops 637534208 | bytes 6291456 | tf_op jit(solution)/shard_map/encode/pallas_call | solution.py:121
  71.0 5.0 %all-to-all-start.2 = ((bf16[16,2,1024]{2,1,0:T(2,128)(2,1)}), bf16[16,2,1024]{2,1,0:T(2,128)(2,1)S(1)}, u32[]{:S(2)}, u32[]{:S(2)}) async-start(bf16[16,2,1024]{2,1,0:T(2,128)(2,1)} %get-tuple-element.54), calls=%async_computation.2 | async-start | bytes 131072 | tf_op jit(solution)/shard_map/all_to_all | solution.py:550
  76.0 0.0 collective-permute-done.7.rest_1_
  76.0 0.0 copy-start.7
  76.0 0.0 collective-permute-done.8.rest_2_
  76.0 0.0 copy-start.8
  76.0 0.0 collective-permute-done.9.rest_3_
  76.0 0.0 copy-start.9
  76.0 6.8 %all-to-all-done.2.spread_far = bf16[16,2,1024]{2,1,0:T(2,128)(2,1)S(1)} async-done(((bf16[16,2,1024]{2,1,0:T(2,128)(2,1)}), bf16[16,2,1024]{2,1,0:T(2,128)(2,1)S(1)}, u32[]{:S(2)}, u32[]{:S(2)}) %all-to-all-start.2) | async-done | bytes 65568 | tf_op jit(solution)/shard_map/all_to_all | solution.py:550
  82.9 0.0 copy-done.7
  82.9 0.0 copy-done.8
  82.9 0.0 copy-done.9
  82.9 0.6 copy-done.6
  83.5 3.6 %late.1 = f32[512,1024]{1,0:T(8,128)} custom-call(s32[1,768]{1,0:T(1,128)} %reshape.41.places_far, s32[1,32]{1,0:T(1,128)} %reshape.42.late_far, bf16[16,2,1024]{2,1,0:T(2,128)(2,1)} %copy-done.6, f32[512,128]{1,0:T(8,128)} %get-tuple-element.55.share_far, f32[512,1024]{1,0:T(8,128)} %get-tuple-element.56.early_far, ...), custom_call_target="tpu_custom_call" | custom-call | flops 436207616 | bytes 4194304 | tf_op jit(solution)/shard_map/late/pallas_call | solution.py:436
  (8 shorter events, 0.0 us)
Async XLA Ops:
  0.6 29.8 %copy-start = (bf16[240,1024]{1,0:T(8,128)(2,1)S(1)}, bf16[240,1024]{1,0:T(8,128)(2,1)}, u32[]{:S(2)}) copy-start(bf16[240,1024]{1,0:T(8,128)(2,1)} %param.17) | copy-start | bytes 1474564
  0.6 7.9 %collective-permute-start.1 = (bf16[254,1024]{1,0:T(8,128)(2,1)}, bf16[254,1024]{1,0:T(8,128)(2,1)S(1)}, u32[]{:S(2)}, u32[]{:S(2)}) collective-permute-start(bf16[254,1024]{1,0:T(8,128)(2,1)} %refs_2_.1), channel_id=1, source_target_pairs={{0,1},{1,0},{2,3},{3,2},{4,5},{5,4},{6,7},{7,6},{8,9},{9,8},{10,11... | collective-permute-start | bytes 1560584 | tf_op jit(solution)/shard_map/ppermute | solution.py:501
  1.2 30.5 %collective-permute-start.2 = (bf16[254,1024]{1,0:T(8,128)(2,1)}, bf16[254,1024]{1,0:T(8,128)(2,1)S(1)}, u32[]{:S(2)}, u32[]{:S(2)}) collective-permute-start(bf16[254,1024]{1,0:T(8,128)(2,1)} %refs_2_.1), channel_id=1, source_target_pairs={{0,8},{1,9},{2,10},{3,11},{4,12},{5,13},{6,14},{7,15},{8,0},{9,1},... | collective-permute-start | bytes 1560584 | tf_op jit(solution)/shard_map/ppermute | solution.py:500
  7.1 1.4 %collective-permute-start = (s32[1,256]{1,0:T(1,128)}, s32[1,256]{1,0:T(1,128)S(1)}, u32[]{:S(2)}, u32[]{:S(2)}) collective-permute-start(s32[1,256]{1,0:T(1,128)} %get-tuple-element.34.refs_0_), channel_id=1, source_target_pairs={{0,1},{1,0},{2,3},{3,2},{4,5},{5,4},{6,7},{7,6},{8,9},{9,8},{10,11... | collective-permute-start | bytes 3080 | tf_op jit(solution)/shard_map/ppermute | solution.py:504
  8.5 0.6 copy-start.13
  9.1 0.8 copy-start.4
  12.5 27.2 %copy-start.14 = (bf16[96,1024]{1,0:T(8,128)(2,1)S(1)}, bf16[96,1024]{1,0:T(8,128)(2,1)}, u32[]{:S(2)}) copy-start(bf16[96,1024]{1,0:T(8,128)(2,1)} %get-tuple-element.47) | copy-start | bytes 589828
  12.5 17.8 %all-to-all-start = ((s32[16,1,330]{2,1,0:T(1,128)}), s32[16,1,330]{2,1,0:T(1,128)S(1)}, u32[]{:S(2)}, u32[]{:S(2)}) async-start(s32[16,1,330]{2,1,0:T(1,128)} %get-tuple-element.39), calls=%async_computation | async-start | bytes 49152 | tf_op jit(solution)/shard_map/all_to_all | solution.py:507
  16.6 15.1 %collective-permute-start.3 = (bf16[96,1024]{1,0:T(8,128)(2,1)}, bf16[96,1024]{1,0:T(8,128)(2,1)S(1)}, u32[]{:S(2)}, u32[]{:S(2)}) collective-permute-start(bf16[96,1024]{1,0:T(8,128)(2,1)} %get-tuple-element.41), channel_id=1, source_target_pairs={{0,2},{1,3},{2,0},{3,1},{4,6},{5,7},{6,4},{7,5},{8,10},{9,11},{10,... | collective-permute-start | bytes 589832 | tf_op jit(solution)/shard_map/ppermute | solution.py:497
  18.5 14.9 %collective-permute-start.4 = (bf16[96,1024]{1,0:T(8,128)(2,1)}, bf16[96,1024]{1,0:T(8,128)(2,1)S(1)}, u32[]{:S(2)}, u32[]{:S(2)}) collective-permute-start(bf16[96,1024]{1,0:T(8,128)(2,1)} %get-tuple-element.42), channel_id=1, source_target_pairs={{0,4},{1,5},{2,6},{3,7},{4,0},{5,1},{6,2},{7,3},{8,12},{9,13},{10,... | collective-permute-start | bytes 589832 | tf_op jit(solution)/shard_map/ppermute | solution.py:497
  30.3 14.1 %copy-start.5 = (s32[16,1,330]{2,1,0:T(1,128)}, s32[16,1,330]{2,1,0:T(1,128)S(1)}, u32[]{:S(2)}) copy-start(s32[16,1,330]{2,1,0:T(1,128)S(1)} %all-to-all-done.refs_0_.refs_1_) | copy-start | bytes 63364
  31.7 12.7 %copy-start.2 = (bf16[254,1024]{1,0:T(8,128)(2,1)}, bf16[254,1024]{1,0:T(8,128)(2,1)S(1)}, u32[]{:S(2)}) copy-start(bf16[254,1024]{1,0:T(8,128)(2,1)S(1)} %collective-permute-done.2.refs_2_) | copy-start | bytes 1560580
  31.7 28.9 %copy-start.10 = (bf16[96,1024]{1,0:T(8,128)(2,1)}, bf16[96,1024]{1,0:T(8,128)(2,1)S(1)}, u32[]{:S(2)}) copy-start(bf16[96,1024]{1,0:T(8,128)(2,1)S(1)} %collective-permute-done.3.rest_1_) | copy-start | bytes 589828
  33.4 27.3 %copy-start.11 = (bf16[96,1024]{1,0:T(8,128)(2,1)}, bf16[96,1024]{1,0:T(8,128)(2,1)S(1)}, u32[]{:S(2)}) copy-start(bf16[96,1024]{1,0:T(8,128)(2,1)S(1)} %collective-permute-done.4.rest_2_) | copy-start | bytes 589828
  33.4 31.7 %all-to-all-start.1 = ((bf16[16,24,1024]{2,1,0:T(8,128)(2,1)}), bf16[16,24,1024]{2,1,0:T(8,128)(2,1)S(1)}, u32[]{:S(2)}, u32[]{:S(2)}) async-start(bf16[16,24,1024]{2,1,0:T(8,128)(2,1)} %bitcast.4), calls=%async_computation.1 | async-start | bytes 1572864 | tf_op jit(solution)/shard_map/all_to_all | solution.py:518
  39.3 5.1 %collective-permute-start.6 = (bf16[254,1024]{1,0:T(8,128)(2,1)S(1)}, bf16[254,1024]{1,0:T(8,128)(2,1)S(1)}, u32[]{:S(2)}, u32[]{:S(2)}) collective-permute-start(bf16[254,1024]{1,0:T(8,128)(2,1)S(1)} %collective-permute-done.2.refs_2_), channel_id=1, source_target_pairs={{0,1},{1,0},{2,3},{3,2},{4,5},{5,4},{6,7},{7,6},{8,9},{9,8},{10,11... | collective-permute-start | bytes 1560584 | tf_op jit(solution)/shard_map/ppermute | solution.py:522
  39.7 20.9 %collective-permute-start.5 = (bf16[96,1024]{1,0:T(8,128)(2,1)S(1)}, bf16[96,1024]{1,0:T(8,128)(2,1)S(1)}, u32[]{:S(2)}, u32[]{:S(2)}) collective-permute-start(bf16[96,1024]{1,0:T(8,128)(2,1)S(1)} %copy-done.14), channel_id=1, source_target_pairs={{0,6},{1,7},{2,4},{3,5},{4,2},{5,3},{6,0},{7,1},{8,14},{9,15},{10,... | collective-permute-start | bytes 589832 | tf_op jit(solution)/shard_map/ppermute | solution.py:497
  44.4 0.8 copy-start.3
  47.8 28.2 %collective-permute-start.7 = (bf16[96,1024]{1,0:T(8,128)(2,1)}, bf16[96,1024]{1,0:T(8,128)(2,1)S(1)}, u32[]{:S(2)}, u32[]{:S(2)}) collective-permute-start(bf16[96,1024]{1,0:T(8,128)(2,1)} %get-tuple-element.59), channel_id=1, source_target_pairs={{0,2},{1,3},{2,0},{3,1},{4,6},{5,7},{6,4},{7,5},{8,10},{9,11},{10,... | collective-permute-start | bytes 589832 | tf_op jit(solution)/shard_map/ppermute | solution.py:497
  48.4 27.6 %collective-permute-start.8 = (bf16[96,1024]{1,0:T(8,128)(2,1)}, bf16[96,1024]{1,0:T(8,128)(2,1)S(1)}, u32[]{:S(2)}, u32[]{:S(2)}) collective-permute-start(bf16[96,1024]{1,0:T(8,128)(2,1)} %get-tuple-element.60), channel_id=1, source_target_pairs={{0,4},{1,5},{2,6},{3,7},{4,0},{5,1},{6,2},{7,3},{8,12},{9,13},{10,... | collective-permute-start | bytes 589832 | tf_op jit(solution)/shard_map/ppermute | solution.py:497
  48.8 27.2 %collective-permute-start.9 = (bf16[96,1024]{1,0:T(8,128)(2,1)}, bf16[96,1024]{1,0:T(8,128)(2,1)S(1)}, u32[]{:S(2)}, u32[]{:S(2)}) collective-permute-start(bf16[96,1024]{1,0:T(8,128)(2,1)} %get-tuple-element.61), channel_id=1, source_target_pairs={{0,6},{1,7},{2,4},{3,5},{4,2},{5,3},{6,0},{7,1},{8,14},{9,15},{10,... | collective-permute-start | bytes 589832 | tf_op jit(solution)/shard_map/ppermute | solution.py:497
  60.7 0.7 copy-start.12
  65.1 0.9 %copy-start.1 = (bf16[16,24,1024]{2,1,0:T(8,128)(2,1)}, bf16[16,24,1024]{2,1,0:T(8,128)(2,1)S(1)}, u32[]{:S(2)}) copy-start(bf16[16,24,1024]{2,1,0:T(8,128)(2,1)S(1)} %all-to-all-done.1) | copy-start | bytes 2359300
  71.0 11.9 %all-to-all-start.2 = ((bf16[16,2,1024]{2,1,0:T(2,128)(2,1)}), bf16[16,2,1024]{2,1,0:T(2,128)(2,1)S(1)}, u32[]{:S(2)}, u32[]{:S(2)}) async-start(bf16[16,2,1024]{2,1,0:T(2,128)(2,1)} %get-tuple-element.54), calls=%async_computation.2 | async-start | bytes 131072 | tf_op jit(solution)/shard_map/all_to_all | solution.py:550
  76.0 6.9 %copy-start.7 = (bf16[96,1024]{1,0:T(8,128)(2,1)}, bf16[96,1024]{1,0:T(8,128)(2,1)S(1)}, u32[]{:S(2)}) copy-start(bf16[96,1024]{1,0:T(8,128)(2,1)S(1)} %collective-permute-done.7.rest_1_) | copy-start | bytes 589828
  76.0 6.9 %copy-start.8 = (bf16[96,1024]{1,0:T(8,128)(2,1)}, bf16[96,1024]{1,0:T(8,128)(2,1)S(1)}, u32[]{:S(2)}) copy-start(bf16[96,1024]{1,0:T(8,128)(2,1)S(1)} %collective-permute-done.8.rest_2_) | copy-start | bytes 589828
  76.0 6.9 %copy-start.9 = (bf16[96,1024]{1,0:T(8,128)(2,1)}, bf16[96,1024]{1,0:T(8,128)(2,1)S(1)}, u32[]{:S(2)}) copy-start(bf16[96,1024]{1,0:T(8,128)(2,1)S(1)} %collective-permute-done.9.rest_3_) | copy-start | bytes 589828
  82.9 0.6 copy-start.6

commit v12 on v11

--- a/solution.py
+++ b/solution.py
@@ -198,8 +198,7 @@
     )
     filled = filled.astype(jnp.int32) - 1
     for p in range(peers):
-        plan[p, :, :rows] = code[...]
-        plan[p, :, rows:] = filled[p : p + 1]
+        plan[p] = filled[p : p + 1]
     token_slot[...] = down[:tokens] * token_cap + rank_col[:tokens]
     send = pltpu.make_async_copy(token_slot, token_slot_far, arrived.at[3])
     send.start()
@@ -214,7 +213,7 @@
     return pl.pallas_call(
         functools.partial(route_kernel, sizes),
         out_shape=[
-            ints(peers, 1, rows + token_cap + row_cap + pooled),
+            ints(peers, 1, token_cap + row_cap + pooled),
             ints(passes * seq_len, 1),
             ints(1, rows),
         ],
@@ -236,11 +235,11 @@
     )(token_ids, owners, row_slot)
 
 
-def pack_kernel(half, row_cap, count, picks, *refs):
+def pack_kernel(row_cap, *refs):
     me = lax.axis_index("dp")
-    steps = half // 2
     far, outs, near, (blocks, arrived, left) = refs[:4], refs[4:-7], refs[-7:-3], refs[-3:]
-    size = blocks.shape[0] // steps
+    chips = len(outs)
+    size = blocks.shape[0] // chips
     copies = [pltpu.make_async_copy(far[at], near[at], arrived.at[at]) for at in range(4)]
     for copy in copies:
         copy.start()
@@ -249,24 +248,22 @@
     if size > 2 * row_cap:
         blocks[...] = jnp.zeros(blocks.shape, blocks.dtype)
     for source in range(2):
-        codes, rows = near[source], near[2 + source]
-        code = codes[...] if picks is None else codes[me ^ picks[source], :, :count]
-        bits = rank_bits(count)
+        code, rows = near[source][...], near[2 + source]
+        bits = rank_bits(code.shape[1])
         owner, rank = code >> bits, code & (2**bits - 1)
-        fits = ((owner ^ me) & (1 | half)) == 0
-        chip = ((owner ^ me) & (half - 1)) >> 1
-        slot = jnp.where(fits, chip * row_cap + rank, -1)[:, : rows.shape[0]]
-        spot = lax.broadcasted_iota(jnp.int32, (steps * row_cap, rows.shape[0]), 0)
+        fits = ((owner ^ me) & 1) == 0
+        slot = jnp.where(fits, ((owner ^ me) >> 1) * row_cap + rank, -1)[:, : rows.shape[0]]
+        spot = lax.broadcasted_iota(jnp.int32, (chips * row_cap, rows.shape[0]), 0)
         table = jnp.where(slot == spot, 1.0, 0.0).astype(jnp.bfloat16)
         copies[2 + source].wait()
         packed = jnp.dot(table, rows[...], preferred_element_type=jnp.float32)
         packed = packed.astype(jnp.bfloat16)
-        for step in range(steps):
-            first = step * size + source * row_cap
-            blocks[first : first + row_cap, :] = packed[step * row_cap : (step + 1) * row_cap]
+        for chip in range(chips):
+            first = chip * size + source * row_cap
+            blocks[first : first + row_cap, :] = packed[chip * row_cap : (chip + 1) * row_cap]
     sends = [
-        pltpu.make_async_copy(blocks.at[pl.ds(step * size, size)], outs[step], left.at[step])
-        for step in range(steps)
+        pltpu.make_async_copy(blocks.at[pl.ds(chip * size, size)], outs[chip], left.at[chip])
+        for chip in range(chips)
     ]
     for send in sends:
         send.start()
@@ -274,26 +271,25 @@
         send.wait()
 
 
-def pack_rows(codes_a, codes_b, rows_a, rows_b, half, row_cap, count, picks=None):
+def pack_rows(codes_a, codes_b, rows_a, rows_b, chips, row_cap):
     total, width = rows_a.shape
-    steps = half // 2
     size = padded(2 * row_cap)
     operands = (codes_a, codes_b, rows_a, rows_b)
     return pl.pallas_call(
-        functools.partial(pack_kernel, half, row_cap, count, picks),
-        out_shape=[jax.ShapeDtypeStruct((size, width), jnp.bfloat16)] * steps,
+        functools.partial(pack_kernel, row_cap),
+        out_shape=[jax.ShapeDtypeStruct((size, width), jnp.bfloat16)] * chips,
         in_specs=[pl.BlockSpec(memory_space=pltpu.HBM)] * 4,
-        out_specs=[pl.BlockSpec(memory_space=pltpu.HBM)] * steps,
+        out_specs=[pl.BlockSpec(memory_space=pltpu.HBM)] * chips,
         scratch_shapes=[
             *(pltpu.VMEM(operand.shape, operand.dtype) for operand in operands),
-            pltpu.VMEM((steps * size, width), jnp.bfloat16),
+            pltpu.VMEM((chips * size, width), jnp.bfloat16),
             pltpu.SemaphoreType.DMA((4,)),
-            pltpu.SemaphoreType.DMA((steps,)),
+            pltpu.SemaphoreType.DMA((chips,)),
         ],
         compiler_params=pltpu.CompilerParams(vmem_limit_bytes=60 * 1024 * 1024),
         cost_estimate=pl.CostEstimate(
-            flops=4 * steps * row_cap * width * total,
-            bytes_accessed=4 * width * (total + steps * row_cap),
+            flops=4 * chips * row_cap * width * total,
+            bytes_accessed=4 * width * (total + chips * row_cap),
             transcendentals=0,
         ),
         name="pack",
@@ -430,7 +426,7 @@
 
 def late_update(places, late, spread, share, early, pieces):
     centre_count, width = early.shape
-    row_total = places.shape[1] // 2 + late.shape[1]
+    row_total = sum(piece.shape[0] for piece in pieces) + late.shape[1]
     wide = pltpu.VMEM(early.shape, jnp.float32)
     steps = centre_count // BLOCK
     return pl.pallas_call(
@@ -477,7 +473,6 @@
     centroids,
 ):
     peer_count = lax.axis_size("dp")
-    half = peer_count // 2
     width = word_table.shape[1]
     vocab_rows = word_table.shape[0]
     passes, seq_len = token_ids.shape
@@ -487,47 +482,37 @@
     token_cap = max(2, 3 * token_count // peer_count)
     row_cap = max(2, 3 * row_count // peer_count)
 
-    across = [(i, i ^ half) for i in range(peer_count)]
     beside = [(i, i ^ 1) for i in range(peer_count)]
-
-    def hand_on(blocks):
-        got = [blocks[0]]
-        for step in range(1, len(blocks)):
-            moves = [(i, i ^ (2 * step)) for i in range(peer_count)]
-            got.append(lax.ppermute(blocks[step], "dp", moves))
-        return got
-
-    partner_rows = lax.ppermute(stored_rows, "dp", across)
     sibling_rows = lax.ppermute(stored_rows, "dp", beside)
     sizes = (peer_count, vocab_rows, token_cap, row_cap, row_count - store_count)
     plan, token_slot, code = route(token_ids, row_owner.reshape(1, row_count), row_slot[None], sizes)
     sibling_code = lax.ppermute(code, "dp", beside)
-    blocks = pack_rows(code, sibling_code, stored_rows, sibling_rows, half, row_cap, row_count)
-    plan, *blocks = lax.optimization_barrier((plan, *blocks))
-    codes = lax.all_to_all(plan, "dp", split_axis=0, concat_axis=0, tiled=True)
-    own_half = hand_on(blocks)
-    plan = codes[:, 0, row_count:]
+    plan, sibling_rows = lax.optimization_barrier((plan, sibling_rows))
+    plan = lax.all_to_all(plan, "dp", split_axis=0, concat_axis=0, tiled=True)[:, 0]
+    chips = peer_count // 2
+    got_rows = [*pack_rows(code, sibling_code, stored_rows, sibling_rows, chips, row_cap)]
+    for chip in range(1, chips):
+        moves = [(i, i ^ (2 * chip)) for i in range(peer_count)]
+        got_rows[chip] = lax.ppermute(got_rows[chip], "dp", moves)
+    ahead = [0, 1, chips // 2]
+    behind = [chip for chip in range(chips) if chip not in ahead]
     wanted = plan[:, :token_cap].reshape(peer_count * token_cap)
     chosen = wanted[:, None] == jnp.arange(vocab_rows, dtype=jnp.int32)[None, :]
     found = jnp.dot(
         chosen.astype(jnp.bfloat16), word_table, preferred_element_type=jnp.float32
     ).astype(jnp.bfloat16)
-    found, partner_rows, own_half[:3] = lax.optimization_barrier(
-        (found, partner_rows, own_half[:3])
-    )
+    first_rows = [got_rows[chip] for chip in ahead]
+    found, first_rows = lax.optimization_barrier((found, first_rows))
     fetched = lax.all_to_all(
         found.reshape(peer_count, token_cap, width), "dp", split_axis=0, concat_axis=0, tiled=True
     ).reshape(peer_count * token_cap, width)
 
-    far_rows = lax.ppermute(partner_rows, "dp", beside)
-    picks = (half, half ^ 1)
-    blocks = pack_rows(codes, codes, partner_rows, far_rows, half, row_cap, row_count, picks)
-    other_half = hand_on(blocks)
     sources = lax.axis_index("dp") ^ jnp.arange(peer_count, dtype=jnp.int32)
-    got_places = plan[:, token_cap : token_cap + row_cap][sources].reshape(half, 2 * row_cap)
+    got_places = plan[:, token_cap : token_cap + row_cap][sources].reshape(chips, 2 * row_cap)
     spare = padded(2 * row_cap) - 2 * row_cap
-    got_places = jnp.pad(got_places, ((0, 0), (0, spare)), constant_values=-1).reshape(1, -1)
-    means, share = early_update(got_places, centroids, own_half)
+    got_places = jnp.pad(got_places, ((0, 0), (0, spare)), constant_values=-1)
+    got_places = jnp.concatenate([got_places[chip] for chip in ahead + behind])[None]
+    means, share = early_update(got_places, centroids, first_rows)
     late_places = plan[:, token_cap + row_cap :].reshape(1, -1)
     fetched, means, share, got_places, late_places = lax.optimization_barrier(
         (fetched, means, share, got_places, late_places)
@@ -550,7 +535,8 @@
     all_embeds = lax.all_to_all(
         spread, "dp", split_axis=0, concat_axis=0, tiled=True
     )
-    new_centroids = late_update(got_places, late_places, all_embeds, share, means, other_half)
+    last_rows = [got_rows[chip] for chip in behind]
+    new_centroids = late_update(got_places, late_places, all_embeds, share, means, last_rows)
     return (passage_embed, new_centroids)
 
 

time: 87.5 us -> 86.3 us (0.986)
  starting transfers between devices: 29.3 us -> 33.1 us
  Pallas kernels: 19.8 us -> 17.7 us
  local copies, waits for them, and re-layouts: 6.49 us -> 4.85 us
  waiting for transfers between devices: 29.4 us -> 28.1 us
    all_to_all x1, waiting for transfers between devices: 10.4 us -> 0.01 us  [shards(): lax.all_to_all(plan, 'dp', split_axis=0, concat_axis=0, tiled=True)[:, 0]]
    ppermute x8 -> x7, waiting for transfers between devices: 11 us -> 17.8 us  [shards(): got_rows[chip] = lax.ppermute(got_rows[chip], 'dp', moves)]
    all_to_all x1, starting transfers between devices: 4.06 us -> 7.35 us  [shards(): lax.all_to_all(plan, 'dp', split_axis=0, concat_axis=0, tiled=True)[:, 0]]
    unnamed x30 -> x32, local copies, waits for them, and re-layouts: 4.35 us -> 2.08 us
    all_to_all x1, waiting for transfers between devices: 0.01 us -> 2.17 us  [shards(): lax.all_to_all(found.reshape(peer_count, token_cap, width), 'dp', split_a...]
    pallas_call x2 -> x1, Pallas kernels: 5.21 us -> 3.09 us  [pack_rows(): pl.pallas_call(functools.partial(pack_kernel, row_cap), out_shape=[jax.Sh...]
    ppermute x8 -> x7, starting transfers between devices: 13.6 us -> 14.9 us  [shards(): got_rows[chip] = lax.ppermute(got_rows[chip], 'dp', moves)]
    all_to_all x1, starting transfers between devices: 5.89 us -> 4.65 us  [shards(): lax.all_to_all(found.reshape(peer_count, token_cap, width), 'dp', split_a...]
  transfers between devices with their start and end apart: 13 -> 12, of which waited for: 5 -> 6; matrix products, arithmetic and copies ran while one was open for 4% -> 5% of each run, Pallas kernels for 19% -> 16%
where the time goes in v12:
time: 86.3 us; the launch traced here: 85.9 us
  starting transfers between devices  33.1 us (38%)
  waiting for transfers between devices  28.1 us (33%)
  Pallas kernels  17.7 us (21%)
  local copies, waits for them, and re-layouts  4.85 us (6%)
  matrix products  1.29 us (1%)
  between operations  0.89 us (1%)
    ppermute x7, waiting for transfers between devices, shards(): got_rows[chip] = lax.ppermute(got_rows[chip], 'dp', moves)  17.8 us
    ppermute x7, starting transfers between devices, shards(): got_rows[chip] = lax.ppermute(got_rows[chip], 'dp', moves)  14.9 us
    all_to_all x1, waiting for transfers between devices, shards(): lax.all_to_all(spread, 'dp', split_axis=0, concat_axis=0, tiled=True)  8.06 us
    all_to_all x1, starting transfers between devices, shards(): lax.all_to_all(plan, 'dp', split_axis=0, concat_axis=0, tiled=True)[:, 0]  7.35 us
    all_to_all x1, starting transfers between devices, shards(): lax.all_to_all(spread, 'dp', split_axis=0, concat_axis=0, tiled=True)  5.57 us
    pallas_call x1, Pallas kernels, encode(): pl.pallas_call(encode_kernel, out_shape=[jax.ShapeDtypeStruct((passes, wi...  4.98 us
    all_to_all x1, starting transfers between devices, shards(): lax.all_to_all(found.reshape(peer_count, token_cap, width), 'dp', split_a...  4.65 us
    pallas_call x1, Pallas kernels, late_update(): pl.pallas_call(late_kernel, out_shape=jax.ShapeDtypeStruct(early.shape, j...  3.69 us
  transfers between devices with their start and end apart: 12, of which 6 were waited for; matrix products, arithmetic and copies ran while one was open for 5% of the time, Pallas kernels for 16%

profile of v12, /device:TPU:0, one launch (start us, length us, event | category | flops | bytes accessed | tf_op | source)
XLA Modules:
  0.0 85.9 jit_solution(11935578016651196412)
XLA Ops:
  0.6 0.0 copy-start
  0.6 0.5 collective-permute-start
  1.2 2.3 %route.1 = (s32[16,1,74]{2,1,0:T(1,128)}, s32[128,1]{1,0:T(8,128)}, s32[1,256]{1,0:T(1,128)}) custom-call(s32[2,64]{1,0:T(2,128)} %token_ids_far.1, s32[1,256]{1,0:T(1,128)} %bitcast.24, s32[1,256]{1,0:T(1,128)} %bitcast.25), custom_call_target="tpu_custom_call" | custom-call | tf_op jit(solution)/shard_map/route/pallas_call | solution.py:213
  3.4 0.2 collective-permute-start.1
  3.6 0.0 collective-permute-done.refs_3_
  3.6 7.4 %all-to-all-start = ((s32[16,1,74]{2,1,0:T(1,128)}), s32[16,1,74]{2,1,0:T(1,128)S(1)}, u32[]{:S(2)}, u32[]{:S(2)}) async-start(s32[16,1,74]{2,1,0:T(1,128)} %get-tuple-element.30), calls=%async_computation | async-start | bytes 16384 | tf_op jit(solution)/shard_map/all_to_all | solution.py:491
  10.9 0.0 collective-permute-done.1.refs_1_
  11.0 0.0 copy-done.10
  11.0 0.0 copy-start.15
  11.0 0.5 copy-done.15
  11.5 3.1 %pack.1 = (bf16[96,1024]{1,0:T(8,128)(2,1)}, bf16[96,1024]{1,0:T(8,128)(2,1)}, bf16[96,1024]{1,0:T(8,128)(2,1)}, bf16[96,1024]{1,0:T(8,128)(2,1)}, bf16[96,1024]...) custom-call(s32[1,256]{1,0:T(1,128)} %get-tuple-element.31.refs_0_, ...), custom_call_target="tpu_custom_call" | custom-call | flops 399507456 | bytes 2613248 | tf_op jit(solution)/shard_map/pack/pallas_call | solution.py:278
  14.6 0.0 copy-start.14
  14.6 0.0 copy-start.13
  14.6 0.0 copy-start.12
  14.6 0.0 copy-start.11
  14.7 2.0 %collective-permute-start.2 = (bf16[96,1024]{1,0:T(8,128)(2,1)}, bf16[96,1024]{1,0:T(8,128)(2,1)S(1)}, u32[]{:S(2)}, u32[]{:S(2)}) collective-permute-start(bf16[96,1024]{1,0:T(8,128)(2,1)} %get-tuple-element.34), channel_id=1, source_target_pairs={{0,2},{1,3},{2,0},{3,1},{4,6},{5,7},{6,4},{7,5},{8,10},{9,11},{10,... | collective-permute-start | bytes 589832 | tf_op jit(solution)/shard_map/ppermute | solution.py:496
  16.6 2.4 %collective-permute-start.3 = (bf16[96,1024]{1,0:T(8,128)(2,1)}, bf16[96,1024]{1,0:T(8,128)(2,1)S(1)}, u32[]{:S(2)}, u32[]{:S(2)}) collective-permute-start(bf16[96,1024]{1,0:T(8,128)(2,1)} %get-tuple-element.35), channel_id=1, source_target_pairs={{0,8},{1,9},{2,10},{3,11},{4,12},{5,13},{6,14},{7,15},{8,0},{9,1},... | collective-permute-start | bytes 589832 | tf_op jit(solution)/shard_map/ppermute | solution.py:496
  19.0 0.0 all-to-all-done
  19.0 0.1 eq.15
  19.1 0.0 copy-done
  19.1 1.3 %convolution_convert_fusion = bf16[384,1024]{1,0:T(8,128)(2,1)} fusion(bf16[240,1024]{1,0:T(8,128)(2,1)S(1)} %copy-done, s32[384]{0:T(512)S(1)} %eq.15), kind=kOutput, calls=%fused_computation.1 | convolution fusion | flops 189229056 | bytes 1279488 | tf_op jit(solution)/shard_map/dot_general | solution.py:501
  20.4 1.8 %collective-permute-done.2.rest_1_ = bf16[96,1024]{1,0:T(8,128)(2,1)S(1)} collective-permute-done((bf16[96,1024]{1,0:T(8,128)(2,1)}, bf16[96,1024]{1,0:T(8,128)(2,1)S(1)}, u32[]{:S(2)}, u32[]{:S(2)}) %collective-permute-start.2) | collective-permute-done | bytes 196640 | tf_op jit(solution)/shard_map/ppermute | solution.py:496
  22.2 6.5 %collective-permute-done.3.rest_2_ = bf16[96,1024]{1,0:T(8,128)(2,1)S(1)} collective-permute-done((bf16[96,1024]{1,0:T(8,128)(2,1)}, bf16[96,1024]{1,0:T(8,128)(2,1)S(1)}, u32[]{:S(2)}, u32[]{:S(2)}) %collective-permute-start.3) | collective-permute-done | bytes 196640 | tf_op jit(solution)/shard_map/ppermute | solution.py:496
  28.6 4.6 %all-to-all-start.1 = ((bf16[16,24,1024]{2,1,0:T(8,128)(2,1)}), bf16[16,24,1024]{2,1,0:T(8,128)(2,1)S(1)}, u32[]{:S(2)}, u32[]{:S(2)}) async-start(bf16[16,24,1024]{2,1,0:T(8,128)(2,1)} %bitcast.4), calls=%async_computation.1 | async-start | bytes 1572864 | tf_op jit(solution)/shard_map/all_to_all | solution.py:506
  33.3 2.0 %collective-permute-start.4 = (bf16[96,1024]{1,0:T(8,128)(2,1)}, bf16[96,1024]{1,0:T(8,128)(2,1)S(1)}, u32[]{:S(2)}, u32[]{:S(2)}) collective-permute-start(bf16[96,1024]{1,0:T(8,128)(2,1)} %get-tuple-element.49), channel_id=1, source_target_pairs={{0,4},{1,5},{2,6},{3,7},{4,0},{5,1},{6,2},{7,3},{8,12},{9,13},{10,... | collective-permute-start | bytes 589832 | tf_op jit(solution)/shard_map/ppermute | solution.py:496
  35.3 0.0 copy-done.14
  35.3 1.5 %collective-permute-start.5 = (bf16[96,1024]{1,0:T(8,128)(2,1)S(1)}, bf16[96,1024]{1,0:T(8,128)(2,1)S(1)}, u32[]{:S(2)}, u32[]{:S(2)}) collective-permute-start(bf16[96,1024]{1,0:T(8,128)(2,1)S(1)} %copy-done.14), channel_id=1, source_target_pairs={{0,6},{1,7},{2,4},{3,5},{4,2},{5,3},{6,0},{7,1},{8,14},{9,15},{10,... | collective-permute-start | bytes 589832 | tf_op jit(solution)/shard_map/ppermute | solution.py:496
  36.8 0.0 copy-done.13
  36.8 2.4 %collective-permute-start.6 = (bf16[96,1024]{1,0:T(8,128)(2,1)S(1)}, bf16[96,1024]{1,0:T(8,128)(2,1)S(1)}, u32[]{:S(2)}, u32[]{:S(2)}) collective-permute-start(bf16[96,1024]{1,0:T(8,128)(2,1)S(1)} %copy-done.13), channel_id=1, source_target_pairs={{0,10},{1,11},{2,8},{3,9},{4,14},{5,15},{6,12},{7,13},{8,2},{9,3},... | collective-permute-start | bytes 589832 | tf_op jit(solution)/shard_map/ppermute | solution.py:496
  39.1 0.0 copy-done.12
  39.1 1.5 %collective-permute-start.7 = (bf16[96,1024]{1,0:T(8,128)(2,1)S(1)}, bf16[96,1024]{1,0:T(8,128)(2,1)S(1)}, u32[]{:S(2)}, u32[]{:S(2)}) collective-permute-start(bf16[96,1024]{1,0:T(8,128)(2,1)S(1)} %copy-done.12), channel_id=1, source_target_pairs={{0,12},{1,13},{2,14},{3,15},{4,8},{5,9},{6,10},{7,11},{8,4},{9,5},... | collective-permute-start | bytes 589832 | tf_op jit(solution)/shard_map/ppermute | solution.py:496
  40.6 0.0 copy-done.11
  40.6 3.3 %collective-permute-start.8 = (bf16[96,1024]{1,0:T(8,128)(2,1)S(1)}, bf16[96,1024]{1,0:T(8,128)(2,1)S(1)}, u32[]{:S(2)}, u32[]{:S(2)}) collective-permute-start(bf16[96,1024]{1,0:T(8,128)(2,1)S(1)} %copy-done.11), channel_id=1, source_target_pairs={{0,14},{1,15},{2,12},{3,13},{4,10},{5,11},{6,8},{7,9},{8,6},{9,7},... | collective-permute-start | bytes 589832 | tf_op jit(solution)/shard_map/ppermute | solution.py:496
  43.9 0.1 slice.64
  43.9 0.1 slice.55
  44.0 0.7 reshape.53.late_far
  44.7 0.6 gather_fusion
  45.2 0.1 squeeze.35
  45.3 0.1 squeeze.34
  45.4 0.1 squeeze.33
  45.5 0.1 squeeze.32
  45.6 0.1 squeeze.31
  45.7 0.1 squeeze.30
  45.7 0.1 squeeze.29
  45.8 0.1 squeeze.28
  45.9 0.1 concatenate.3
  46.0 0.6 broadcast_in_dim.28.places_far
  46.6 0.0 copy-done.8
  46.6 0.0 copy-done.9
  46.6 3.7 %early.1 = (f32[512,1024]{1,0:T(8,128)}, f32[512,128]{1,0:T(8,128)}) custom-call(s32[1,768]{1,0:T(1,128)} %broadcast_in_dim.28.places_far, f32[512,1024]{1,0:T(8,128)} %centroids_far.1, bf16[96,1024]{1,0:T(8,128)(2,1)} %get-tuple-element.37.rest_0_, bf16[96,1024]{1,0:T(8,128)(2,1)} %copy-done.8, bf16[96,1024]{1,0:T(8,128)(2,1)} %copy-done.9), custom_call_target="tpu_custom_call" | custom-call | flops 301989888 | bytes 4194304 | tf_op jit(solution)/shard_map/early/pallas_call | solution.py:400
  50.3 2.2 %all-to-all-done.1 = bf16[16,24,1024]{2,1,0:T(8,128)(2,1)S(1)} async-done(((bf16[16,24,1024]{2,1,0:T(8,128)(2,1)}), bf16[16,24,1024]{2,1,0:T(8,128)(2,1)S(1)}, u32[]{:S(2)}, u32[]{:S(2)}) %all-to-all-start.1) | async-done | bytes 786464 | tf_op jit(solution)/shard_map/all_to_all | solution.py:506
  52.4 0.9 %copy-done.1 = bf16[16,24,1024]{2,1,0:T(8,128)(2,1)} copy-done((bf16[16,24,1024]{2,1,0:T(8,128)(2,1)}, bf16[16,24,1024]{2,1,0:T(8,128)(2,1)S(1)}, u32[]{:S(2)}) %copy-start.1) | copy-done | bytes 786456
  53.3 5.0 %encode.1 = (bf16[2,1024]{1,0:T(2,128)(2,1)}, bf16[16,2,1024]{2,1,0:T(2,128)(2,1)}) custom-call(s32[1,2]{1,0:T(1,128)} %bitcast.26, s32[128,1]{1,0:T(8,128)} %get-tuple-element.28.refs_1_, bf16[384,1024]{1,0:T(8,128)(2,1)} %bitcast.15, bf16[64,1024]{1,0:T(8,128)(2,1)} %refs_3_.1, f32[1,1024]{1,0:T(1,128)} %bitcast.19, f32[1,1024]{1,0:T(1,128)} %bitcast.20, ...), custom_call_target="tpu_custom_call" | custom-call | flops 637534208 | bytes 6291456 | tf_op jit(solution)/shard_map/encode/pallas_call | solution.py:121
  58.3 5.6 %all-to-all-start.2 = ((bf16[16,2,1024]{2,1,0:T(2,128)(2,1)}), bf16[16,2,1024]{2,1,0:T(2,128)(2,1)S(1)}, u32[]{:S(2)}, u32[]{:S(2)}) async-start(bf16[16,2,1024]{2,1,0:T(2,128)(2,1)} %get-tuple-element.46), calls=%async_computation.2 | async-start | bytes 131072 | tf_op jit(solution)/shard_map/all_to_all | solution.py:535
  63.9 0.0 collective-permute-done.4.rest_0_
  63.9 0.0 copy-start.3
  63.9 0.0 collective-permute-done.5.rest_1_
  63.9 0.0 collective-permute-done.6.rest_2_
  63.9 4.6 %collective-permute-done.7.rest_3_ = bf16[96,1024]{1,0:T(8,128)(2,1)S(1)} collective-permute-done((bf16[96,1024]{1,0:T(8,128)(2,1)S(1)}, bf16[96,1024]{1,0:T(8,128)(2,1)S(1)}, u32[]{:S(2)}, u32[]{:S(2)}) %collective-permute-start.7) | collective-permute-done | bytes 196640 | tf_op jit(solution)/shard_map/ppermute | solution.py:496
  68.5 5.0 %collective-permute-done.8.rest_4_ = bf16[96,1024]{1,0:T(8,128)(2,1)S(1)} collective-permute-done((bf16[96,1024]{1,0:T(8,128)(2,1)S(1)}, bf16[96,1024]{1,0:T(8,128)(2,1)S(1)}, u32[]{:S(2)}, u32[]{:S(2)}) %collective-permute-start.8) | collective-permute-done | bytes 196640 | tf_op jit(solution)/shard_map/ppermute | solution.py:496
  73.5 8.1 %all-to-all-done.2.spread_far = bf16[16,2,1024]{2,1,0:T(2,128)(2,1)S(1)} async-done(((bf16[16,2,1024]{2,1,0:T(2,128)(2,1)}), bf16[16,2,1024]{2,1,0:T(2,128)(2,1)S(1)}, u32[]{:S(2)}, u32[]{:S(2)}) %all-to-all-start.2) | async-done | bytes 65568 | tf_op jit(solution)/shard_map/all_to_all | solution.py:535
  81.6 0.0 copy-done.4
  81.6 0.6 copy-done.2
  82.2 3.7 %late.1 = f32[512,1024]{1,0:T(8,128)} custom-call(s32[1,768]{1,0:T(1,128)} %broadcast_in_dim.28.places_far, s32[1,32]{1,0:T(1,128)} %reshape.53.late_far, bf16[16,2,1024]{2,1,0:T(2,128)(2,1)} %copy-done.2, f32[512,128]{1,0:T(8,128)} %get-tuple-element.47.share_far, f32[512,1024]{1,0:T(8,128)} %get-tuple-element.48.early_far, bf16[96,1024]{1,0:T(8,128)(2,1)} %copy-done.3, ...), custom_call_target="tpu_custom_call" | custom-call | flops 536870912 | bytes 4194304 | tf_op jit(solution)/shard_map/late/pallas_call | solution.py:432
  (16 shorter events, 0.0 us)
Async XLA Ops:
  0.6 18.5 %copy-start = (bf16[240,1024]{1,0:T(8,128)(2,1)S(1)}, bf16[240,1024]{1,0:T(8,128)(2,1)}, u32[]{:S(2)}) copy-start(bf16[240,1024]{1,0:T(8,128)(2,1)} %param.17) | copy-start | bytes 1474564
  0.6 2.9 %collective-permute-start = (bf16[254,1024]{1,0:T(8,128)(2,1)}, bf16[254,1024]{1,0:T(8,128)(2,1)S(1)}, u32[]{:S(2)}, u32[]{:S(2)}) collective-permute-start(bf16[254,1024]{1,0:T(8,128)(2,1)} %refs_2_.1), channel_id=1, source_target_pairs={{0,1},{1,0},{2,3},{3,2},{4,5},{5,4},{6,7},{7,6},{8,9},{9,8},{10,11... | collective-permute-start | bytes 1560584 | tf_op jit(solution)/shard_map/ppermute | solution.py:486
  3.4 7.5 %collective-permute-start.1 = (s32[1,256]{1,0:T(1,128)}, s32[1,256]{1,0:T(1,128)S(1)}, u32[]{:S(2)}, u32[]{:S(2)}) collective-permute-start(s32[1,256]{1,0:T(1,128)} %get-tuple-element.31.refs_0_), channel_id=1, source_target_pairs={{0,1},{1,0},{2,3},{3,2},{4,5},{5,4},{6,7},{7,6},{8,9},{9,8},{10,11... | collective-permute-start | bytes 3080 | tf_op jit(solution)/shard_map/ppermute | solution.py:489
  3.6 7.4 %copy-start.10 = (bf16[254,1024]{1,0:T(8,128)(2,1)}, bf16[254,1024]{1,0:T(8,128)(2,1)S(1)}, u32[]{:S(2)}) copy-start(bf16[254,1024]{1,0:T(8,128)(2,1)S(1)} %collective-permute-done.refs_3_) | copy-start | bytes 1560580
  3.6 15.4 %all-to-all-start = ((s32[16,1,74]{2,1,0:T(1,128)}), s32[16,1,74]{2,1,0:T(1,128)S(1)}, u32[]{:S(2)}, u32[]{:S(2)}) async-start(s32[16,1,74]{2,1,0:T(1,128)} %get-tuple-element.30), calls=%async_computation | async-start | bytes 16384 | tf_op jit(solution)/shard_map/all_to_all | solution.py:491
  11.0 0.5 copy-start.15
  14.6 20.7 %copy-start.14 = (bf16[96,1024]{1,0:T(8,128)(2,1)S(1)}, bf16[96,1024]{1,0:T(8,128)(2,1)}, u32[]{:S(2)}) copy-start(bf16[96,1024]{1,0:T(8,128)(2,1)} %get-tuple-element.50) | copy-start | bytes 589828
  14.6 22.2 %copy-start.13 = (bf16[96,1024]{1,0:T(8,128)(2,1)S(1)}, bf16[96,1024]{1,0:T(8,128)(2,1)}, u32[]{:S(2)}) copy-start(bf16[96,1024]{1,0:T(8,128)(2,1)} %get-tuple-element.51) | copy-start | bytes 589828
  14.6 24.5 %copy-start.12 = (bf16[96,1024]{1,0:T(8,128)(2,1)S(1)}, bf16[96,1024]{1,0:T(8,128)(2,1)}, u32[]{:S(2)}) copy-start(bf16[96,1024]{1,0:T(8,128)(2,1)} %get-tuple-element.52) | copy-start | bytes 589828
  14.6 26.0 %copy-start.11 = (bf16[96,1024]{1,0:T(8,128)(2,1)S(1)}, bf16[96,1024]{1,0:T(8,128)(2,1)}, u32[]{:S(2)}) copy-start(bf16[96,1024]{1,0:T(8,128)(2,1)} %get-tuple-element.53) | copy-start | bytes 589828
  14.7 7.5 %collective-permute-start.2 = (bf16[96,1024]{1,0:T(8,128)(2,1)}, bf16[96,1024]{1,0:T(8,128)(2,1)S(1)}, u32[]{:S(2)}, u32[]{:S(2)}) collective-permute-start(bf16[96,1024]{1,0:T(8,128)(2,1)} %get-tuple-element.34), channel_id=1, source_target_pairs={{0,2},{1,3},{2,0},{3,1},{4,6},{5,7},{6,4},{7,5},{8,10},{9,11},{10,... | collective-permute-start | bytes 589832 | tf_op jit(solution)/shard_map/ppermute | solution.py:496
  16.6 12.0 %collective-permute-start.3 = (bf16[96,1024]{1,0:T(8,128)(2,1)}, bf16[96,1024]{1,0:T(8,128)(2,1)S(1)}, u32[]{:S(2)}, u32[]{:S(2)}) collective-permute-start(bf16[96,1024]{1,0:T(8,128)(2,1)} %get-tuple-element.35), channel_id=1, source_target_pairs={{0,8},{1,9},{2,10},{3,11},{4,12},{5,13},{6,14},{7,15},{8,0},{9,1},... | collective-permute-start | bytes 589832 | tf_op jit(solution)/shard_map/ppermute | solution.py:496
  22.2 24.4 %copy-start.8 = (bf16[96,1024]{1,0:T(8,128)(2,1)}, bf16[96,1024]{1,0:T(8,128)(2,1)S(1)}, u32[]{:S(2)}) copy-start(bf16[96,1024]{1,0:T(8,128)(2,1)S(1)} %collective-permute-done.2.rest_1_) | copy-start | bytes 589828
  28.6 17.9 %copy-start.9 = (bf16[96,1024]{1,0:T(8,128)(2,1)}, bf16[96,1024]{1,0:T(8,128)(2,1)S(1)}, u32[]{:S(2)}) copy-start(bf16[96,1024]{1,0:T(8,128)(2,1)S(1)} %collective-permute-done.3.rest_2_) | copy-start | bytes 589828
  28.6 23.8 %all-to-all-start.1 = ((bf16[16,24,1024]{2,1,0:T(8,128)(2,1)}), bf16[16,24,1024]{2,1,0:T(8,128)(2,1)S(1)}, u32[]{:S(2)}, u32[]{:S(2)}) async-start(bf16[16,24,1024]{2,1,0:T(8,128)(2,1)} %bitcast.4), calls=%async_computation.1 | async-start | bytes 1572864 | tf_op jit(solution)/shard_map/all_to_all | solution.py:506
  33.3 30.6 %collective-permute-start.4 = (bf16[96,1024]{1,0:T(8,128)(2,1)}, bf16[96,1024]{1,0:T(8,128)(2,1)S(1)}, u32[]{:S(2)}, u32[]{:S(2)}) collective-permute-start(bf16[96,1024]{1,0:T(8,128)(2,1)} %get-tuple-element.49), channel_id=1, source_target_pairs={{0,4},{1,5},{2,6},{3,7},{4,0},{5,1},{6,2},{7,3},{8,12},{9,13},{10,... | collective-permute-start | bytes 589832 | tf_op jit(solution)/shard_map/ppermute | solution.py:496
  35.3 28.6 %collective-permute-start.5 = (bf16[96,1024]{1,0:T(8,128)(2,1)S(1)}, bf16[96,1024]{1,0:T(8,128)(2,1)S(1)}, u32[]{:S(2)}, u32[]{:S(2)}) collective-permute-start(bf16[96,1024]{1,0:T(8,128)(2,1)S(1)} %copy-done.14), channel_id=1, source_target_pairs={{0,6},{1,7},{2,4},{3,5},{4,2},{5,3},{6,0},{7,1},{8,14},{9,15},{10,... | collective-permute-start | bytes 589832 | tf_op jit(solution)/shard_map/ppermute | solution.py:496
  36.8 27.1 %collective-permute-start.6 = (bf16[96,1024]{1,0:T(8,128)(2,1)S(1)}, bf16[96,1024]{1,0:T(8,128)(2,1)S(1)}, u32[]{:S(2)}, u32[]{:S(2)}) collective-permute-start(bf16[96,1024]{1,0:T(8,128)(2,1)S(1)} %copy-done.13), channel_id=1, source_target_pairs={{0,10},{1,11},{2,8},{3,9},{4,14},{5,15},{6,12},{7,13},{8,2},{9,3},... | collective-permute-start | bytes 589832 | tf_op jit(solution)/shard_map/ppermute | solution.py:496
  39.1 29.4 %collective-permute-start.7 = (bf16[96,1024]{1,0:T(8,128)(2,1)S(1)}, bf16[96,1024]{1,0:T(8,128)(2,1)S(1)}, u32[]{:S(2)}, u32[]{:S(2)}) collective-permute-start(bf16[96,1024]{1,0:T(8,128)(2,1)S(1)} %copy-done.12), channel_id=1, source_target_pairs={{0,12},{1,13},{2,14},{3,15},{4,8},{5,9},{6,10},{7,11},{8,4},{9,5},... | collective-permute-start | bytes 589832 | tf_op jit(solution)/shard_map/ppermute | solution.py:496
  40.6 32.9 %collective-permute-start.8 = (bf16[96,1024]{1,0:T(8,128)(2,1)S(1)}, bf16[96,1024]{1,0:T(8,128)(2,1)S(1)}, u32[]{:S(2)}, u32[]{:S(2)}) collective-permute-start(bf16[96,1024]{1,0:T(8,128)(2,1)S(1)} %copy-done.11), channel_id=1, source_target_pairs={{0,14},{1,15},{2,12},{3,13},{4,10},{5,11},{6,8},{7,9},{8,6},{9,7},... | collective-permute-start | bytes 589832 | tf_op jit(solution)/shard_map/ppermute | solution.py:496
  52.4 0.9 %copy-start.1 = (bf16[16,24,1024]{2,1,0:T(8,128)(2,1)}, bf16[16,24,1024]{2,1,0:T(8,128)(2,1)S(1)}, u32[]{:S(2)}) copy-start(bf16[16,24,1024]{2,1,0:T(8,128)(2,1)S(1)} %all-to-all-done.1) | copy-start | bytes 2359300
  58.3 23.3 %all-to-all-start.2 = ((bf16[16,2,1024]{2,1,0:T(2,128)(2,1)}), bf16[16,2,1024]{2,1,0:T(2,128)(2,1)S(1)}, u32[]{:S(2)}, u32[]{:S(2)}) async-start(bf16[16,2,1024]{2,1,0:T(2,128)(2,1)} %get-tuple-element.46), calls=%async_computation.2 | async-start | bytes 131072 | tf_op jit(solution)/shard_map/all_to_all | solution.py:535
  63.9 17.7 %copy-start.3 = (bf16[96,1024]{1,0:T(8,128)(2,1)}, bf16[96,1024]{1,0:T(8,128)(2,1)S(1)}, u32[]{:S(2)}) copy-start(bf16[96,1024]{1,0:T(8,128)(2,1)S(1)} %collective-permute-done.4.rest_0_) | copy-start | bytes 589828
  63.9 17.7 %copy-start.4 = (bf16[96,1024]{1,0:T(8,128)(2,1)}, bf16[96,1024]{1,0:T(8,128)(2,1)S(1)}, u32[]{:S(2)}) copy-start(bf16[96,1024]{1,0:T(8,128)(2,1)S(1)} %collective-permute-done.5.rest_1_) | copy-start | bytes 589828
  63.9 17.7 %copy-start.5 = (bf16[96,1024]{1,0:T(8,128)(2,1)}, bf16[96,1024]{1,0:T(8,128)(2,1)S(1)}, u32[]{:S(2)}) copy-start(bf16[96,1024]{1,0:T(8,128)(2,1)S(1)} %collective-permute-done.6.rest_2_) | copy-start | bytes 589828
  68.5 13.1 %copy-start.6 = (bf16[96,1024]{1,0:T(8,128)(2,1)}, bf16[96,1024]{1,0:T(8,128)(2,1)S(1)}, u32[]{:S(2)}) copy-start(bf16[96,1024]{1,0:T(8,128)(2,1)S(1)} %collective-permute-done.7.rest_3_) | copy-start | bytes 589828
  73.5 8.1 %copy-start.7 = (bf16[96,1024]{1,0:T(8,128)(2,1)}, bf16[96,1024]{1,0:T(8,128)(2,1)S(1)}, u32[]{:S(2)}) copy-start(bf16[96,1024]{1,0:T(8,128)(2,1)S(1)} %collective-permute-done.8.rest_4_) | copy-start | bytes 589828
  81.6 0.6 copy-start.2

commit v13 on v10

--- a/solution.py
+++ b/solution.py
@@ -204,28 +204,6 @@
     send = pltpu.make_async_copy(token_slot, token_slot_far, arrived.at[3])
     send.start()
     send.wait()
-
-
-def cut_kernel(far, out_far, near, done):
-    load = pltpu.make_async_copy(far.at[pl.ds(0, near.shape[0])], near, done.at[0])
-    load.start()
-    load.wait()
-    send = pltpu.make_async_copy(near, out_far, done.at[1])
-    send.start()
-    send.wait()
-
-
-def cut(rows, count):
-    shape = (count, rows.shape[1])
-    return pl.pallas_call(
-        cut_kernel,
-        out_shape=jax.ShapeDtypeStruct(shape, rows.dtype),
-        in_specs=[pl.BlockSpec(memory_space=pltpu.HBM)],
-        out_specs=pl.BlockSpec(memory_space=pltpu.HBM),
-        scratch_shapes=[pltpu.VMEM(shape, rows.dtype), pltpu.SemaphoreType.DMA((2,))],
-        compiler_params=pltpu.CompilerParams(vmem_limit_bytes=60 * 1024 * 1024),
-        name="cut",
-    )(rows)
 
 
 def route(token_ids, owners, row_slot, sizes):
@@ -463,8 +441,8 @@
         ],
         compiler_params=pltpu.CompilerParams(vmem_limit_bytes=60 * 1024 * 1024),
         cost_estimate=pl.CostEstimate(
-            flops=100 * centre_count * width * row_total,
-            bytes_accessed=200 * centre_count * width,
+            flops=2 * centre_count * width * row_total,
+            bytes_accessed=8 * centre_count * width,
             transcendentals=0,
         ),
         name="early",
@@ -473,7 +451,7 @@
 
 def late_update(places, late, spread, share, early, pieces):
     centre_count, width = early.shape
-    row_total = places.shape[1] // 2 + late.shape[1]
+    row_total = sum(piece.shape[0] for piece in pieces) + late.shape[1]
     wide = pltpu.VMEM(early.shape, jnp.float32)
     steps = centre_count // BLOCK
     return pl.pallas_call(
@@ -540,12 +518,14 @@
             got.append(lax.ppermute(blocks[step], "dp", moves))
         return got
 
-    ahead = store_count * 5 // 8 // 16 * 16
+    ahead = store_count * 3 // 4 // 16 * 16
     sibling_rows = lax.ppermute(stored_rows, "dp", beside)
-    first_rows = lax.ppermute(cut(stored_rows, ahead), "dp", across)
+    first_rows = lax.ppermute(stored_rows[:ahead], "dp", across)
     sizes = (peer_count, vocab_rows, token_cap, row_cap, row_count - store_count)
     plan, token_slot, code = route(token_ids, row_owner.reshape(1, row_count), row_slot[None], sizes)
     sibling_code = lax.ppermute(code, "dp", beside)
+    plan, sibling_rows = lax.optimization_barrier((plan, sibling_rows))
+    codes = lax.all_to_all(plan, "dp", split_axis=0, concat_axis=0, tiled=True)
     *blocks, last_rows = pack_rows(
         code,
         sibling_code,
@@ -556,19 +536,16 @@
         row_count,
         rest=store_count - ahead,
     )
-    plan, *blocks = lax.optimization_barrier((plan, *blocks))
-    codes = lax.all_to_all(plan, "dp", split_axis=0, concat_axis=0, tiled=True)
+    last_rows = lax.ppermute(last_rows, "dp", across)
     own_half = hand_on(blocks)
-    codes, last_rows = lax.optimization_barrier((codes, last_rows))
-    last_rows = lax.ppermute(last_rows, "dp", across)
     plan = codes[:, 0, row_count:]
     wanted = plan[:, :token_cap].reshape(peer_count * token_cap)
     chosen = wanted[:, None] == jnp.arange(vocab_rows, dtype=jnp.int32)[None, :]
     found = jnp.dot(
         chosen.astype(jnp.bfloat16), word_table, preferred_element_type=jnp.float32
     ).astype(jnp.bfloat16)
-    found, first_rows, own_half[:3] = lax.optimization_barrier(
-        (found, first_rows, own_half[:3])
+    found, first_rows, last_rows, own_half[:3] = lax.optimization_barrier(
+        (found, first_rows, last_rows, own_half[:3])
     )
     fetched = lax.all_to_all(
         found.reshape(peer_count, token_cap, width), "dp", split_axis=0, concat_axis=0, tiled=True
@@ -583,7 +560,7 @@
     got_places = plan[:, token_cap : token_cap + row_cap][sources].reshape(half, 2 * row_cap)
     spare = padded(2 * row_cap) - 2 * row_cap
     got_places = jnp.pad(got_places, ((0, 0), (0, spare)), constant_values=-1).reshape(1, -1)
-    means, share = early_update(got_places, centroids, own_half)
+    means, share = early_update(got_places, centroids, own_half[:3])
     late_places = plan[:, token_cap + row_cap :].reshape(1, -1)
     fetched, means, share, got_places, late_places = lax.optimization_barrier(
         (fetched, means, share, got_places, late_places)
@@ -606,7 +583,8 @@
     all_embeds = lax.all_to_all(
         spread, "dp", split_axis=0, concat_axis=0, tiled=True
     )
-    new_centroids = late_update(got_places, late_places, all_embeds, share, means, other_half)
+    pieces = own_half[3:] + other_half
+    new_centroids = late_update(got_places, late_places, all_embeds, share, means, pieces)
     return (passage_embed, new_centroids)
 
 

time: 94.6 us -> 78.9 us (0.83)
  waiting for transfers between devices: 33.7 us -> 18.3 us
  starting transfers between devices: 29.6 us -> 31.4 us
  Pallas kernels: 21.7 us -> 20.1 us
    ppermute x1, waiting for transfers between devices: 14.4 us -> 0.01 us  [shards(): first_rows = lax.ppermute(stored_rows[:ahead], 'dp', across)]
    all_to_all x1, waiting for transfers between devices: 0.01 us -> 5.5 us  [shards(): codes = lax.all_to_all(plan, 'dp', split_axis=0, concat_axis=0, tiled=True)]
    all_to_all x1, waiting for transfers between devices: 6.88 us -> 2.2 us  [shards(): lax.all_to_all(found.reshape(peer_count, token_cap, width), 'dp', split_a...]
    ppermute x1, waiting for transfers between devices: 4.34 us -> 0.83 us  [shards(): last_rows = lax.ppermute(last_rows, 'dp', across)]
    all_to_all x1, starting transfers between devices: 7.27 us -> 3.92 us  [shards(): codes = lax.all_to_all(plan, 'dp', split_axis=0, concat_axis=0, tiled=True)]
    ppermute x1, starting transfers between devices: 0.62 us -> 2.8 us  [shards(): last_rows = lax.ppermute(last_rows, 'dp', across)]
    ppermute x6, waiting for transfers between devices: 0.02 us -> 1.88 us  [hand_on(): got.append(lax.ppermute(blocks[step], 'dp', moves))]
    pallas_call x1 -> x0, Pallas kernels: 1.69 us -> none  [cut(): pl.pallas_call(cut_kernel, out_shape=jax.ShapeDtypeStruct(shape, rows.dty...]
  transfers between devices with their start and end apart: 15 -> 15, of which waited for: 5 -> 6; matrix products, arithmetic and copies ran while one was open for 4% -> 6% of each run, Pallas kernels for 16% -> 21%
where the time goes in v13:
time: 78.9 us; the launch traced here: 78.5 us
  starting transfers between devices  31.4 us (40%)
  Pallas kernels  20.1 us (25%)
  waiting for transfers between devices  18.3 us (23%)
  local copies, waits for them, and re-layouts  6.57 us (8%)
  matrix products  1.29 us (2%)
  between operations  0.88 us (1%)
    ppermute x6, starting transfers between devices, hand_on(): got.append(lax.ppermute(blocks[step], 'dp', moves))  9.31 us
    all_to_all x1, waiting for transfers between devices, shards(): lax.all_to_all(spread, 'dp', split_axis=0, concat_axis=0, tiled=True)  6.81 us
    all_to_all x1, starting transfers between devices, shards(): lax.all_to_all(spread, 'dp', split_axis=0, concat_axis=0, tiled=True)  5.64 us
    all_to_all x1, waiting for transfers between devices, shards(): codes = lax.all_to_all(plan, 'dp', split_axis=0, concat_axis=0, tiled=True)  5.5 us
    pallas_call x2, Pallas kernels, pack_rows(): pl.pallas_call(functools.partial(pack_kernel, half, row_cap, count, picks...  5.5 us
    pallas_call x1, Pallas kernels, encode(): pl.pallas_call(encode_kernel, out_shape=[jax.ShapeDtypeStruct((passes, wi...  4.97 us
    all_to_all x1, starting transfers between devices, shards(): lax.all_to_all(found.reshape(peer_count, token_cap, width), 'dp', split_a...  4.51 us
    all_to_all x1, starting transfers between devices, shards(): codes = lax.all_to_all(plan, 'dp', split_axis=0, concat_axis=0, tiled=True)  3.92 us
  transfers between devices with their start and end apart: 15, of which 6 were waited for; matrix products, arithmetic and copies ran while one was open for 6% of the time, Pallas kernels for 21%

profile of v13, /device:TPU:0, one launch (start us, length us, event | category | flops | bytes accessed | tf_op | source)
XLA Modules:
  0.0 78.5 jit_solution(17809123909257964289)
XLA Ops:
  0.6 0.0 copy-start
  0.6 0.5 collective-permute-start
  1.2 1.0 %slice.17 = bf16[176,1024]{1,0:T(8,128)(2,1)S(1)} slice(bf16[254,1024]{1,0:T(8,128)(2,1)} %refs_2_.1), slice={[0:176], [0:1024]} | slice | bytes 720896 | tf_op jit(solution)/shard_map/slice | solution.py:523
  2.2 3.7 %collective-permute-start.1 = (bf16[176,1024]{1,0:T(8,128)(2,1)S(1)}, bf16[176,1024]{1,0:T(8,128)(2,1)S(1)}, u32[]{:S(2)}, u32[]{:S(2)}) collective-permute-start(bf16[176,1024]{1,0:T(8,128)(2,1)S(1)} %slice.17), channel_id=1, source_target_pairs={{0,8},{1,9},{2,10},{3,11},{4,12},{5,13},{6,14},{7,15},{8,0},{9,1},... | collective-permute-start | bytes 1081352 | tf_op jit(solution)/shard_map/ppermute | solution.py:523
  5.9 2.3 %route.1 = (s32[16,1,330]{2,1,0:T(1,128)}, s32[128,1]{1,0:T(8,128)}, s32[1,256]{1,0:T(1,128)}) custom-call(s32[2,64]{1,0:T(2,128)} %token_ids_far.1, s32[1,256]{1,0:T(1,128)} %bitcast.24, s32[1,256]{1,0:T(1,128)} %bitcast.25), custom_call_target="tpu_custom_call" | custom-call | tf_op jit(solution)/shard_map/route/pallas_call | solution.py:214
  8.2 0.0 collective-permute-done.refs_3_
  8.2 0.0 copy-start.2
  8.2 3.9 %all-to-all-start = ((s32[16,1,330]{2,1,0:T(1,128)}), s32[16,1,330]{2,1,0:T(1,128)S(1)}, u32[]{:S(2)}, u32[]{:S(2)}) async-start(s32[16,1,330]{2,1,0:T(1,128)} %get-tuple-element.33), calls=%async_computation | async-start | bytes 49152 | tf_op jit(solution)/shard_map/all_to_all | solution.py:528
  12.1 0.4 collective-permute-start.2
  12.5 1.0 %collective-permute-done.2.refs_1_ = s32[1,256]{1,0:T(1,128)S(1)} collective-permute-done((s32[1,256]{1,0:T(1,128)}, s32[1,256]{1,0:T(1,128)S(1)}, u32[]{:S(2)}, u32[]{:S(2)}) %collective-permute-start.2) | collective-permute-done | bytes 1056 | tf_op jit(solution)/shard_map/ppermute | solution.py:526
  13.6 0.0 copy-done.2
  13.6 0.5 copy-done.15
  14.1 2.7 %pack.2 = (bf16[96,1024]{1,0:T(8,128)(2,1)}, bf16[96,1024]{1,0:T(8,128)(2,1)}, bf16[96,1024]{1,0:T(8,128)(2,1)}, bf16[96,1024]{1,0:T(8,128)(2,1)}, bf16[78,1024]{1,0:T(8,128)(2,1)}) custom-call(s32[1,256]{1,0:T(1,128)} %get-tuple-element.34.refs_0_, s32[1,256]{1,0:T(1,128)} %copy-done.15, bf16[254,1024]{1,0:T(8,128)(2,1)} %refs_2_.1, bf16[254,1024]{1,0:T(8,128)(2,1)} %copy-done.2), custom_call_target="tpu_custom_call" | custom-call | flops 199753728 | bytes 1826816 | tf_op jit(solution)/shard_map/pack/pallas_call | solution.py:302
  16.8 0.0 copy-start.16
  16.8 2.8 %collective-permute-start.3 = (bf16[78,1024]{1,0:T(8,128)(2,1)}, bf16[78,1024]{1,0:T(8,128)(2,1)S(1)}, u32[]{:S(2)}, u32[]{:S(2)}) collective-permute-start(bf16[78,1024]{1,0:T(8,128)(2,1)} %get-tuple-element.36), channel_id=1, source_target_pairs={{0,8},{1,9},{2,10},{3,11},{4,12},{5,13},{6,14},{7,15},{8,0},{9,1},... | collective-permute-start | bytes 479240 | tf_op jit(solution)/shard_map/ppermute | solution.py:539
  19.6 1.5 %collective-permute-start.4 = (bf16[96,1024]{1,0:T(8,128)(2,1)}, bf16[96,1024]{1,0:T(8,128)(2,1)S(1)}, u32[]{:S(2)}, u32[]{:S(2)}) collective-permute-start(bf16[96,1024]{1,0:T(8,128)(2,1)} %get-tuple-element.38), channel_id=1, source_target_pairs={{0,2},{1,3},{2,0},{3,1},{4,6},{5,7},{6,4},{7,5},{8,10},{9,11},{10,... | collective-permute-start | bytes 589832 | tf_op jit(solution)/shard_map/ppermute | solution.py:518
  21.0 1.5 %collective-permute-start.5 = (bf16[96,1024]{1,0:T(8,128)(2,1)}, bf16[96,1024]{1,0:T(8,128)(2,1)S(1)}, u32[]{:S(2)}, u32[]{:S(2)}) collective-permute-start(bf16[96,1024]{1,0:T(8,128)(2,1)} %get-tuple-element.39), channel_id=1, source_target_pairs={{0,4},{1,5},{2,6},{3,7},{4,0},{5,1},{6,2},{7,3},{8,12},{9,13},{10,... | collective-permute-start | bytes 589832 | tf_op jit(solution)/shard_map/ppermute | solution.py:518
  22.5 5.5 %all-to-all-done.refs_0_.refs_1_ = s32[16,1,330]{2,1,0:T(1,128)S(1)} async-done(((s32[16,1,330]{2,1,0:T(1,128)}), s32[16,1,330]{2,1,0:T(1,128)S(1)}, u32[]{:S(2)}, u32[]{:S(2)}) %all-to-all-start) | async-done | bytes 21152 | tf_op jit(solution)/shard_map/all_to_all | solution.py:528
  28.0 0.1 eq.15
  28.1 0.0 copy-done
  28.1 1.3 %convolution_convert_fusion = bf16[384,1024]{1,0:T(8,128)(2,1)} fusion(bf16[240,1024]{1,0:T(8,128)(2,1)S(1)} %copy-done, s32[384]{0:T(512)S(1)} %eq.15), kind=kOutput, calls=%fused_computation.1 | convolution fusion | flops 189229056 | bytes 1279488 | tf_op jit(solution)/shard_map/dot_general | solution.py:544
  29.4 0.0 collective-permute-done.1.refs_2_
  29.4 0.8 %collective-permute-done.3.refs_3_ = bf16[78,1024]{1,0:T(8,128)(2,1)S(1)} collective-permute-done((bf16[78,1024]{1,0:T(8,128)(2,1)}, bf16[78,1024]{1,0:T(8,128)(2,1)S(1)}, u32[]{:S(2)}, u32[]{:S(2)}) %collective-permute-start.3) | collective-permute-done | bytes 159776 | tf_op jit(solution)/shard_map/ppermute | solution.py:539
  30.2 0.0 collective-permute-done.4.rest_1_
  30.3 1.9 %collective-permute-done.5.rest_2_ = bf16[96,1024]{1,0:T(8,128)(2,1)S(1)} collective-permute-done((bf16[96,1024]{1,0:T(8,128)(2,1)}, bf16[96,1024]{1,0:T(8,128)(2,1)S(1)}, u32[]{:S(2)}, u32[]{:S(2)}) %collective-permute-start.5) | collective-permute-done | bytes 196640 | tf_op jit(solution)/shard_map/ppermute | solution.py:518
  32.1 4.5 %all-to-all-start.1 = ((bf16[16,24,1024]{2,1,0:T(8,128)(2,1)}), bf16[16,24,1024]{2,1,0:T(8,128)(2,1)S(1)}, u32[]{:S(2)}, u32[]{:S(2)}) async-start(bf16[16,24,1024]{2,1,0:T(8,128)(2,1)} %bitcast.4), calls=%async_computation.1 | async-start | bytes 1572864 | tf_op jit(solution)/shard_map/all_to_all | solution.py:550
  36.6 0.4 collective-permute-start.7
  37.0 0.2 collective-permute-start.8
  37.2 0.0 copy-done.16
  37.2 2.8 %collective-permute-start.6 = (bf16[96,1024]{1,0:T(8,128)(2,1)S(1)}, bf16[96,1024]{1,0:T(8,128)(2,1)S(1)}, u32[]{:S(2)}, u32[]{:S(2)}) collective-permute-start(bf16[96,1024]{1,0:T(8,128)(2,1)S(1)} %copy-done.16), channel_id=1, source_target_pairs={{0,6},{1,7},{2,4},{3,5},{4,2},{5,3},{6,0},{7,1},{8,14},{9,15},{10,... | collective-permute-start | bytes 589832 | tf_op jit(solution)/shard_map/ppermute | solution.py:518
  40.1 0.1 slice.25
  40.1 0.1 slice.24
  40.2 0.7 reshape.42.late_far
  40.9 0.6 gather_fusion
  41.4 0.7 reshape.41.places_far
  42.1 0.0 collective-permute-done.8.refs_5_
  42.1 0.0 collective-permute-done.7.refs_4_
  42.1 0.0 copy-done.5
  42.1 0.0 copy-done.3
  42.1 0.0 copy-done.13
  42.1 0.6 copy-done.14
  42.8 0.7 copy-done.4
  43.5 2.9 %pack.3 = (bf16[96,1024]{1,0:T(8,128)(2,1)}, bf16[96,1024]{1,0:T(8,128)(2,1)}, bf16[96,1024]{1,0:T(8,128)(2,1)}, bf16[96,1024]{1,0:T(8,128)(2,1)}) custom-call(s32[16,1,330]{2,1,0:T(1,128)} %copy-done.5, s32[16,1,330]{2,1,0:T(1,128)} %copy-done.5, bf16[176,1024]{1,0:T(8,128)(2,1)} %copy-done.3, bf16[78,1024]{1,0:T(8,128)(2,1)} %copy-done.13, ...), custom_call_target="tpu_custom_call" | custom-call | flops 199753728 | bytes 1826816 | tf_op jit(solution)/shard_map/pack/pallas_call | solution.py:302
  46.4 0.6 collective-permute-start.9
  47.0 0.2 collective-permute-start.10
  47.2 2.8 %collective-permute-start.11 = (bf16[96,1024]{1,0:T(8,128)(2,1)}, bf16[96,1024]{1,0:T(8,128)(2,1)S(1)}, u32[]{:S(2)}, u32[]{:S(2)}) collective-permute-start(bf16[96,1024]{1,0:T(8,128)(2,1)} %get-tuple-element.59), channel_id=1, source_target_pairs={{0,6},{1,7},{2,4},{3,5},{4,2},{5,3},{6,0},{7,1},{8,14},{9,15},{10,... | collective-permute-start | bytes 589832 | tf_op jit(solution)/shard_map/ppermute | solution.py:518
  49.9 0.0 copy-done.11
  49.9 0.0 copy-done.12
  49.9 3.6 %early.1 = (f32[512,1024]{1,0:T(8,128)}, f32[512,128]{1,0:T(8,128)}) custom-call(s32[1,768]{1,0:T(1,128)} %reshape.41.places_far, f32[512,1024]{1,0:T(8,128)} %centroids_far.1, bf16[96,1024]{1,0:T(8,128)(2,1)} %get-tuple-element.41.rest_0_, bf16[96,1024]{1,0:T(8,128)(2,1)} %copy-done.11, bf16[96,1024]{1,0:T(8,128)(2,1)} %copy-done.12), custom_call_target="tpu_custom_call" | custom-call | flops 301989888 | bytes 4194304 | tf_op jit(solution)/shard_map/early/pallas_call | solution.py:425
  53.6 2.2 %all-to-all-done.1 = bf16[16,24,1024]{2,1,0:T(8,128)(2,1)S(1)} async-done(((bf16[16,24,1024]{2,1,0:T(8,128)(2,1)}), bf16[16,24,1024]{2,1,0:T(8,128)(2,1)S(1)}, u32[]{:S(2)}, u32[]{:S(2)}) %all-to-all-start.1) | async-done | bytes 786464 | tf_op jit(solution)/shard_map/all_to_all | solution.py:550
  55.8 0.9 %copy-done.1 = bf16[16,24,1024]{2,1,0:T(8,128)(2,1)} copy-done((bf16[16,24,1024]{2,1,0:T(8,128)(2,1)}, bf16[16,24,1024]{2,1,0:T(8,128)(2,1)S(1)}, u32[]{:S(2)}) %copy-start.1) | copy-done | bytes 786456
  56.7 5.0 %encode.1 = (bf16[2,1024]{1,0:T(2,128)(2,1)}, bf16[16,2,1024]{2,1,0:T(2,128)(2,1)}) custom-call(s32[1,2]{1,0:T(1,128)} %bitcast.26, s32[128,1]{1,0:T(8,128)} %get-tuple-element.31.refs_1_, bf16[384,1024]{1,0:T(8,128)(2,1)} %bitcast.15, bf16[64,1024]{1,0:T(8,128)(2,1)} %refs_3_.1, f32[1,1024]{1,0:T(1,128)} %bitcast.19, f32[1,1024]{1,0:T(1,128)} %bitcast.20, ...), custom_call_target="tpu_custom_call" | custom-call | flops 637534208 | bytes 6291456 | tf_op jit(solution)/shard_map/encode/pallas_call | solution.py:121
  61.6 5.6 %all-to-all-start.2 = ((bf16[16,2,1024]{2,1,0:T(2,128)(2,1)}), bf16[16,2,1024]{2,1,0:T(2,128)(2,1)S(1)}, u32[]{:S(2)}, u32[]{:S(2)}) async-start(bf16[16,2,1024]{2,1,0:T(2,128)(2,1)} %get-tuple-element.50), calls=%async_computation.2 | async-start | bytes 131072 | tf_op jit(solution)/shard_map/all_to_all | solution.py:583
  67.3 0.0 collective-permute-done.6.rest_0_
  67.3 0.0 copy-start.7
  67.3 0.0 collective-permute-done.9.rest_2_
  67.3 0.0 copy-start.8
  67.3 0.0 collective-permute-done.10.rest_3_
  67.3 0.0 copy-start.9
  67.3 0.0 collective-permute-done.11.rest_4_
  67.4 6.8 %all-to-all-done.2.spread_far = bf16[16,2,1024]{2,1,0:T(2,128)(2,1)S(1)} async-done(((bf16[16,2,1024]{2,1,0:T(2,128)(2,1)}), bf16[16,2,1024]{2,1,0:T(2,128)(2,1)S(1)}, u32[]{:S(2)}, u32[]{:S(2)}) %all-to-all-start.2) | async-done | bytes 65568 | tf_op jit(solution)/shard_map/all_to_all | solution.py:583
  74.2 0.0 copy-done.9
  74.2 0.6 copy-done.6
  74.8 3.7 %late.1 = f32[512,1024]{1,0:T(8,128)} custom-call(s32[1,768]{1,0:T(1,128)} %reshape.41.places_far, s32[1,32]{1,0:T(1,128)} %reshape.42.late_far, bf16[16,2,1024]{2,1,0:T(2,128)(2,1)} %copy-done.6, f32[512,128]{1,0:T(8,128)} %get-tuple-element.51.share_far, f32[512,1024]{1,0:T(8,128)} %get-tuple-element.52.early_far, bf16[96,1024]{1,0:T(8,128)(2,1)} %copy-done.7, ...), custom_call_target="tpu_custom_call" | custom-call | flops 536870912 | bytes 4194304 | tf_op jit(solution)/shard_map/late/pallas_call | solution.py:457
  (17 shorter events, 0.0 us)
Async XLA Ops:
  0.6 27.5 %copy-start = (bf16[240,1024]{1,0:T(8,128)(2,1)S(1)}, bf16[240,1024]{1,0:T(8,128)(2,1)}, u32[]{:S(2)}) copy-start(bf16[240,1024]{1,0:T(8,128)(2,1)} %param.17) | copy-start | bytes 1474564
  0.6 7.5 %collective-permute-start = (bf16[254,1024]{1,0:T(8,128)(2,1)}, bf16[254,1024]{1,0:T(8,128)(2,1)S(1)}, u32[]{:S(2)}, u32[]{:S(2)}) collective-permute-start(bf16[254,1024]{1,0:T(8,128)(2,1)} %refs_2_.1), channel_id=1, source_target_pairs={{0,1},{1,0},{2,3},{3,2},{4,5},{5,4},{6,7},{7,6},{8,9},{9,8},{10,11... | collective-permute-start | bytes 1560584 | tf_op jit(solution)/shard_map/ppermute | solution.py:522
  2.2 27.2 %collective-permute-start.1 = (bf16[176,1024]{1,0:T(8,128)(2,1)S(1)}, bf16[176,1024]{1,0:T(8,128)(2,1)S(1)}, u32[]{:S(2)}, u32[]{:S(2)}) collective-permute-start(bf16[176,1024]{1,0:T(8,128)(2,1)S(1)} %slice.17), channel_id=1, source_target_pairs={{0,8},{1,9},{2,10},{3,11},{4,12},{5,13},{6,14},{7,15},{8,0},{9,1},... | collective-permute-start | bytes 1081352 | tf_op jit(solution)/shard_map/ppermute | solution.py:523
  8.2 5.4 %copy-start.2 = (bf16[254,1024]{1,0:T(8,128)(2,1)}, bf16[254,1024]{1,0:T(8,128)(2,1)S(1)}, u32[]{:S(2)}) copy-start(bf16[254,1024]{1,0:T(8,128)(2,1)S(1)} %collective-permute-done.refs_3_) | copy-start | bytes 1560580
  8.2 19.8 %all-to-all-start = ((s32[16,1,330]{2,1,0:T(1,128)}), s32[16,1,330]{2,1,0:T(1,128)S(1)}, u32[]{:S(2)}, u32[]{:S(2)}) async-start(s32[16,1,330]{2,1,0:T(1,128)} %get-tuple-element.33), calls=%async_computation | async-start | bytes 49152 | tf_op jit(solution)/shard_map/all_to_all | solution.py:528
  12.1 1.4 %collective-permute-start.2 = (s32[1,256]{1,0:T(1,128)}, s32[1,256]{1,0:T(1,128)S(1)}, u32[]{:S(2)}, u32[]{:S(2)}) collective-permute-start(s32[1,256]{1,0:T(1,128)} %get-tuple-element.34.refs_0_), channel_id=1, source_target_pairs={{0,1},{1,0},{2,3},{3,2},{4,5},{5,4},{6,7},{7,6},{8,9},{9,8},{10,11... | collective-permute-start | bytes 3080 | tf_op jit(solution)/shard_map/ppermute | solution.py:526
  13.6 0.5 copy-start.15
  16.8 20.5 %copy-start.16 = (bf16[96,1024]{1,0:T(8,128)(2,1)S(1)}, bf16[96,1024]{1,0:T(8,128)(2,1)}, u32[]{:S(2)}) copy-start(bf16[96,1024]{1,0:T(8,128)(2,1)} %get-tuple-element.53) | copy-start | bytes 589828
  16.8 13.5 %collective-permute-start.3 = (bf16[78,1024]{1,0:T(8,128)(2,1)}, bf16[78,1024]{1,0:T(8,128)(2,1)S(1)}, u32[]{:S(2)}, u32[]{:S(2)}) collective-permute-start(bf16[78,1024]{1,0:T(8,128)(2,1)} %get-tuple-element.36), channel_id=1, source_target_pairs={{0,8},{1,9},{2,10},{3,11},{4,12},{5,13},{6,14},{7,15},{8,0},{9,1},... | collective-permute-start | bytes 479240 | tf_op jit(solution)/shard_map/ppermute | solution.py:539
  19.6 10.7 %collective-permute-start.4 = (bf16[96,1024]{1,0:T(8,128)(2,1)}, bf16[96,1024]{1,0:T(8,128)(2,1)S(1)}, u32[]{:S(2)}, u32[]{:S(2)}) collective-permute-start(bf16[96,1024]{1,0:T(8,128)(2,1)} %get-tuple-element.38), channel_id=1, source_target_pairs={{0,2},{1,3},{2,0},{3,1},{4,6},{5,7},{6,4},{7,5},{8,10},{9,11},{10,... | collective-permute-start | bytes 589832 | tf_op jit(solution)/shard_map/ppermute | solution.py:518
  21.0 11.1 %collective-permute-start.5 = (bf16[96,1024]{1,0:T(8,128)(2,1)}, bf16[96,1024]{1,0:T(8,128)(2,1)S(1)}, u32[]{:S(2)}, u32[]{:S(2)}) collective-permute-start(bf16[96,1024]{1,0:T(8,128)(2,1)} %get-tuple-element.39), channel_id=1, source_target_pairs={{0,4},{1,5},{2,6},{3,7},{4,0},{5,1},{6,2},{7,3},{8,12},{9,13},{10,... | collective-permute-start | bytes 589832 | tf_op jit(solution)/shard_map/ppermute | solution.py:518
  28.0 14.1 %copy-start.5 = (s32[16,1,330]{2,1,0:T(1,128)}, s32[16,1,330]{2,1,0:T(1,128)S(1)}, u32[]{:S(2)}) copy-start(s32[16,1,330]{2,1,0:T(1,128)S(1)} %all-to-all-done.refs_0_.refs_1_) | copy-start | bytes 63364
  29.4 12.7 %copy-start.3 = (bf16[176,1024]{1,0:T(8,128)(2,1)}, bf16[176,1024]{1,0:T(8,128)(2,1)S(1)}, u32[]{:S(2)}) copy-start(bf16[176,1024]{1,0:T(8,128)(2,1)S(1)} %collective-permute-done.1.refs_2_) | copy-start | bytes 1081348
  30.2 11.9 %copy-start.13 = (bf16[78,1024]{1,0:T(8,128)(2,1)}, bf16[78,1024]{1,0:T(8,128)(2,1)S(1)}, u32[]{:S(2)}) copy-start(bf16[78,1024]{1,0:T(8,128)(2,1)S(1)} %collective-permute-done.3.refs_3_) | copy-start | bytes 479236
  30.2 19.7 %copy-start.11 = (bf16[96,1024]{1,0:T(8,128)(2,1)}, bf16[96,1024]{1,0:T(8,128)(2,1)S(1)}, u32[]{:S(2)}) copy-start(bf16[96,1024]{1,0:T(8,128)(2,1)S(1)} %collective-permute-done.4.rest_1_) | copy-start | bytes 589828
  32.1 17.8 %copy-start.12 = (bf16[96,1024]{1,0:T(8,128)(2,1)}, bf16[96,1024]{1,0:T(8,128)(2,1)S(1)}, u32[]{:S(2)}) copy-start(bf16[96,1024]{1,0:T(8,128)(2,1)S(1)} %collective-permute-done.5.rest_2_) | copy-start | bytes 589828
  32.1 23.7 %all-to-all-start.1 = ((bf16[16,24,1024]{2,1,0:T(8,128)(2,1)}), bf16[16,24,1024]{2,1,0:T(8,128)(2,1)S(1)}, u32[]{:S(2)}, u32[]{:S(2)}) async-start(bf16[16,24,1024]{2,1,0:T(8,128)(2,1)} %bitcast.4), calls=%async_computation.1 | async-start | bytes 1572864 | tf_op jit(solution)/shard_map/all_to_all | solution.py:550
  36.6 5.5 %collective-permute-start.7 = (bf16[176,1024]{1,0:T(8,128)(2,1)S(1)}, bf16[176,1024]{1,0:T(8,128)(2,1)S(1)}, u32[]{:S(2)}, u32[]{:S(2)}) collective-permute-start(bf16[176,1024]{1,0:T(8,128)(2,1)S(1)} %collective-permute-done.1.refs_2_), channel_id=1, source_target_pairs={{0,1},{1,0},{2,3},{3,2},{4,5},{5,4},{6,7},{7,6},{8,9},{9,8},{10,11... | collective-permute-start | bytes 1081352 | tf_op jit(solution)/shard_map/ppermute | solution.py:555
  37.0 5.1 %collective-permute-start.8 = (bf16[78,1024]{1,0:T(8,128)(2,1)S(1)}, bf16[78,1024]{1,0:T(8,128)(2,1)S(1)}, u32[]{:S(2)}, u32[]{:S(2)}) collective-permute-start(bf16[78,1024]{1,0:T(8,128)(2,1)S(1)} %collective-permute-done.3.refs_3_), channel_id=1, source_target_pairs={{0,1},{1,0},{2,3},{3,2},{4,5},{5,4},{6,7},{7,6},{8,9},{9,8},{10,11... | collective-permute-start | bytes 479240 | tf_op jit(solution)/shard_map/ppermute | solution.py:555
  37.2 30.0 %collective-permute-start.6 = (bf16[96,1024]{1,0:T(8,128)(2,1)S(1)}, bf16[96,1024]{1,0:T(8,128)(2,1)S(1)}, u32[]{:S(2)}, u32[]{:S(2)}) collective-permute-start(bf16[96,1024]{1,0:T(8,128)(2,1)S(1)} %copy-done.16), channel_id=1, source_target_pairs={{0,6},{1,7},{2,4},{3,5},{4,2},{5,3},{6,0},{7,1},{8,14},{9,15},{10,... | collective-permute-start | bytes 589832 | tf_op jit(solution)/shard_map/ppermute | solution.py:518
  42.1 0.7 copy-start.14
  42.8 0.7 copy-start.4
  46.4 20.9 %collective-permute-start.9 = (bf16[96,1024]{1,0:T(8,128)(2,1)}, bf16[96,1024]{1,0:T(8,128)(2,1)S(1)}, u32[]{:S(2)}, u32[]{:S(2)}) collective-permute-start(bf16[96,1024]{1,0:T(8,128)(2,1)} %get-tuple-element.57), channel_id=1, source_target_pairs={{0,2},{1,3},{2,0},{3,1},{4,6},{5,7},{6,4},{7,5},{8,10},{9,11},{10,... | collective-permute-start | bytes 589832 | tf_op jit(solution)/shard_map/ppermute | solution.py:518
  47.0 20.3 %collective-permute-start.10 = (bf16[96,1024]{1,0:T(8,128)(2,1)}, bf16[96,1024]{1,0:T(8,128)(2,1)S(1)}, u32[]{:S(2)}, u32[]{:S(2)}) collective-permute-start(bf16[96,1024]{1,0:T(8,128)(2,1)} %get-tuple-element.58), channel_id=1, source_target_pairs={{0,4},{1,5},{2,6},{3,7},{4,0},{5,1},{6,2},{7,3},{8,12},{9,13},{10,... | collective-permute-start | bytes 589832 | tf_op jit(solution)/shard_map/ppermute | solution.py:518
  47.2 20.2 %collective-permute-start.11 = (bf16[96,1024]{1,0:T(8,128)(2,1)}, bf16[96,1024]{1,0:T(8,128)(2,1)S(1)}, u32[]{:S(2)}, u32[]{:S(2)}) collective-permute-start(bf16[96,1024]{1,0:T(8,128)(2,1)} %get-tuple-element.59), channel_id=1, source_target_pairs={{0,6},{1,7},{2,4},{3,5},{4,2},{5,3},{6,0},{7,1},{8,14},{9,15},{10,... | collective-permute-start | bytes 589832 | tf_op jit(solution)/shard_map/ppermute | solution.py:518
  55.8 0.9 %copy-start.1 = (bf16[16,24,1024]{2,1,0:T(8,128)(2,1)}, bf16[16,24,1024]{2,1,0:T(8,128)(2,1)S(1)}, u32[]{:S(2)}) copy-start(bf16[16,24,1024]{2,1,0:T(8,128)(2,1)S(1)} %all-to-all-done.1) | copy-start | bytes 2359300
  61.6 12.5 %all-to-all-start.2 = ((bf16[16,2,1024]{2,1,0:T(2,128)(2,1)}), bf16[16,2,1024]{2,1,0:T(2,128)(2,1)S(1)}, u32[]{:S(2)}, u32[]{:S(2)}) async-start(bf16[16,2,1024]{2,1,0:T(2,128)(2,1)} %get-tuple-element.50), calls=%async_computation.2 | async-start | bytes 131072 | tf_op jit(solution)/shard_map/all_to_all | solution.py:583
  67.3 6.9 %copy-start.7 = (bf16[96,1024]{1,0:T(8,128)(2,1)}, bf16[96,1024]{1,0:T(8,128)(2,1)S(1)}, u32[]{:S(2)}) copy-start(bf16[96,1024]{1,0:T(8,128)(2,1)S(1)} %collective-permute-done.6.rest_0_) | copy-start | bytes 589828
  67.3 6.9 %copy-start.8 = (bf16[96,1024]{1,0:T(8,128)(2,1)}, bf16[96,1024]{1,0:T(8,128)(2,1)S(1)}, u32[]{:S(2)}) copy-start(bf16[96,1024]{1,0:T(8,128)(2,1)S(1)} %collective-permute-done.9.rest_2_) | copy-start | bytes 589828
  67.3 6.9 %copy-start.9 = (bf16[96,1024]{1,0:T(8,128)(2,1)}, bf16[96,1024]{1,0:T(8,128)(2,1)S(1)}, u32[]{:S(2)}) copy-start(bf16[96,1024]{1,0:T(8,128)(2,1)S(1)} %collective-permute-done.10.rest_3_) | copy-start | bytes 589828
  67.4 6.8 %copy-start.10 = (bf16[96,1024]{1,0:T(8,128)(2,1)}, bf16[96,1024]{1,0:T(8,128)(2,1)S(1)}, u32[]{:S(2)}) copy-start(bf16[96,1024]{1,0:T(8,128)(2,1)S(1)} %collective-permute-done.11.rest_4_) | copy-start | bytes 589828
  74.2 0.6 copy-start.6

commit v14 on v13

--- a/solution.py
+++ b/solution.py
@@ -518,25 +518,16 @@
             got.append(lax.ppermute(blocks[step], "dp", moves))
         return got
 
-    ahead = store_count * 3 // 4 // 16 * 16
+    ahead = store_count * 2 // 5 // 16 * 16
     sibling_rows = lax.ppermute(stored_rows, "dp", beside)
     first_rows = lax.ppermute(stored_rows[:ahead], "dp", across)
     sizes = (peer_count, vocab_rows, token_cap, row_cap, row_count - store_count)
     plan, token_slot, code = route(token_ids, row_owner.reshape(1, row_count), row_slot[None], sizes)
     sibling_code = lax.ppermute(code, "dp", beside)
-    plan, sibling_rows = lax.optimization_barrier((plan, sibling_rows))
+    plan, sibling_rows, rest = lax.optimization_barrier((plan, sibling_rows, stored_rows))
+    last_rows = lax.ppermute(rest[ahead:], "dp", across)
     codes = lax.all_to_all(plan, "dp", split_axis=0, concat_axis=0, tiled=True)
-    *blocks, last_rows = pack_rows(
-        code,
-        sibling_code,
-        [stored_rows],
-        [sibling_rows],
-        half,
-        row_cap,
-        row_count,
-        rest=store_count - ahead,
-    )
-    last_rows = lax.ppermute(last_rows, "dp", across)
+    blocks = pack_rows(code, sibling_code, [stored_rows], [sibling_rows], half, row_cap, row_count)
     own_half = hand_on(blocks)
     plan = codes[:, 0, row_count:]
     wanted = plan[:, :token_cap].reshape(peer_count * token_cap)

time: 78.9 us -> 83.9 us (1.063)
  waiting for transfers between devices: 18.3 us -> 21.8 us
  local copies, waits for them, and re-layouts: 6.57 us -> 7.74 us
    ppermute x6, waiting for transfers between devices: 1.88 us -> 3.99 us  [hand_on(): got.append(lax.ppermute(blocks[step], 'dp', moves))]
    all_to_all x1, waiting for transfers between devices: 5.5 us -> 7.3 us  [shards(): codes = lax.all_to_all(plan, 'dp', split_axis=0, concat_axis=0, tiled=True)]
    ppermute x1, waiting for transfers between devices: 0.01 us -> 1.58 us  [shards(): first_rows = lax.ppermute(stored_rows[:ahead], 'dp', across)]
    slice x0 -> x1, local copies, waits for them, and re-layouts: none -> 1.19 us  [shards(): last_rows = lax.ppermute(rest[ahead:], 'dp', across)]
    ppermute x1, starting transfers between devices: 3.72 us -> 2.65 us  [shards(): first_rows = lax.ppermute(stored_rows[:ahead], 'dp', across)]
    ppermute x1, waiting for transfers between devices: 1.03 us -> 0.01 us  [shards(): sibling_code = lax.ppermute(code, 'dp', beside)]
    ppermute x1, starting transfers between devices: 2.8 us -> 3.72 us  [shards(): last_rows = lax.ppermute(rest[ahead:], 'dp', across)]
  transfers between devices with their start and end apart: 15 -> 15, of which waited for: 6 -> 5; matrix products, arithmetic and copies ran while one was open for 6% -> 5% of each run, Pallas kernels for 21% -> 20%
where the time goes in v14:
time: 83.9 us; the launch traced here: 83.4 us
  starting transfers between devices  31.6 us (38%)
  waiting for transfers between devices  21.8 us (26%)
  Pallas kernels  20.1 us (24%)
  local copies, waits for them, and re-layouts  7.74 us (9%)
  matrix products  1.29 us (2%)
  between operations  0.88 us (1%)
    ppermute x6, starting transfers between devices, hand_on(): got.append(lax.ppermute(blocks[step], 'dp', moves))  9.38 us
    all_to_all x1, waiting for transfers between devices, shards(): codes = lax.all_to_all(plan, 'dp', split_axis=0, concat_axis=0, tiled=True)  7.3 us
    all_to_all x1, waiting for transfers between devices, shards(): lax.all_to_all(spread, 'dp', split_axis=0, concat_axis=0, tiled=True)  6.81 us
    all_to_all x1, starting transfers between devices, shards(): lax.all_to_all(spread, 'dp', split_axis=0, concat_axis=0, tiled=True)  5.64 us
    pallas_call x2, Pallas kernels, pack_rows(): pl.pallas_call(functools.partial(pack_kernel, half, row_cap, count, picks...  5.49 us
    pallas_call x1, Pallas kernels, encode(): pl.pallas_call(encode_kernel, out_shape=[jax.ShapeDtypeStruct((passes, wi...  4.97 us
    all_to_all x1, starting transfers between devices, shards(): lax.all_to_all(found.reshape(peer_count, token_cap, width), 'dp', split_a...  4.8 us
    ppermute x6, waiting for transfers between devices, hand_on(): got.append(lax.ppermute(blocks[step], 'dp', moves))  3.99 us
  transfers between devices with their start and end apart: 15, of which 5 were waited for; matrix products, arithmetic and copies ran while one was open for 5% of the time, Pallas kernels for 20%

profile of v14, /device:TPU:0, one launch (start us, length us, event | category | flops | bytes accessed | tf_op | source)
XLA Modules:
  0.0 83.4 jit_solution(11170026700132813216)
XLA Ops:
  0.6 0.0 copy-start
  0.6 0.5 collective-permute-start
  1.2 2.3 %route.1 = (s32[16,1,330]{2,1,0:T(1,128)}, s32[128,1]{1,0:T(8,128)}, s32[1,256]{1,0:T(1,128)}) custom-call(s32[2,64]{1,0:T(2,128)} %token_ids_far.1, s32[1,256]{1,0:T(1,128)} %bitcast.24, s32[1,256]{1,0:T(1,128)} %bitcast.25), custom_call_target="tpu_custom_call" | custom-call | tf_op jit(solution)/shard_map/route/pallas_call | solution.py:214
  3.4 0.0 collective-permute-done.refs_3_
  3.4 0.0 copy-start.2
  3.5 1.2 %slice.21 = bf16[158,1024]{1,0:T(8,128)(2,1)S(1)} slice(bf16[254,1024]{1,0:T(8,128)(2,1)} %refs_2_.1), slice={[96:254], [0:1024]} | slice | bytes 647168 | tf_op jit(solution)/shard_map/slice | solution.py:528
  4.7 3.7 %collective-permute-start.2 = (bf16[158,1024]{1,0:T(8,128)(2,1)S(1)}, bf16[158,1024]{1,0:T(8,128)(2,1)S(1)}, u32[]{:S(2)}, u32[]{:S(2)}) collective-permute-start(bf16[158,1024]{1,0:T(8,128)(2,1)S(1)} %slice.21), channel_id=1, source_target_pairs={{0,8},{1,9},{2,10},{3,11},{4,12},{5,13},{6,14},{7,15},{8,0},{9,1},... | collective-permute-start | bytes 970760 | tf_op jit(solution)/shard_map/ppermute | solution.py:528
  8.4 3.9 %all-to-all-start = ((s32[16,1,330]{2,1,0:T(1,128)}), s32[16,1,330]{2,1,0:T(1,128)S(1)}, u32[]{:S(2)}, u32[]{:S(2)}) async-start(s32[16,1,330]{2,1,0:T(1,128)} %get-tuple-element.33), calls=%async_computation | async-start | bytes 49152 | tf_op jit(solution)/shard_map/all_to_all | solution.py:529
  12.3 0.4 collective-permute-start.3
  12.7 0.9 %slice.20 = bf16[96,1024]{1,0:T(8,128)(2,1)S(1)} slice(bf16[254,1024]{1,0:T(8,128)(2,1)} %refs_2_.1), slice={[0:96], [0:1024]} | slice | bytes 393216 | tf_op jit(solution)/shard_map/slice | solution.py:523
  13.6 2.6 %collective-permute-start.1 = (bf16[96,1024]{1,0:T(8,128)(2,1)S(1)}, bf16[96,1024]{1,0:T(8,128)(2,1)S(1)}, u32[]{:S(2)}, u32[]{:S(2)}) collective-permute-start(bf16[96,1024]{1,0:T(8,128)(2,1)S(1)} %slice.20), channel_id=1, source_target_pairs={{0,8},{1,9},{2,10},{3,11},{4,12},{5,13},{6,14},{7,15},{8,0},{9,1},... | collective-permute-start | bytes 589832 | tf_op jit(solution)/shard_map/ppermute | solution.py:523
  16.3 0.0 collective-permute-done.3.refs_1_
  16.3 0.0 copy-done.2
  16.3 0.6 copy-done.15
  16.9 2.6 %pack.2 = (bf16[96,1024]{1,0:T(8,128)(2,1)}, bf16[96,1024]{1,0:T(8,128)(2,1)}, bf16[96,1024]{1,0:T(8,128)(2,1)}, bf16[96,1024]{1,0:T(8,128)(2,1)}) custom-call(s32[1,256]{1,0:T(1,128)} %get-tuple-element.35.refs_0_, s32[1,256]{1,0:T(1,128)} %copy-done.15, bf16[254,1024]{1,0:T(8,128)(2,1)} %refs_2_.1, bf16[254,1024]{1,0:T(8,128)(2,1)} %copy-done.2), custom_call_target="tpu_custom_call" | custom-call | flops 199753728 | bytes 1826816 | tf_op jit(solution)/shard_map/pack/pallas_call | solution.py:302
  19.5 0.0 copy-start.16
  19.5 1.5 %collective-permute-start.4 = (bf16[96,1024]{1,0:T(8,128)(2,1)}, bf16[96,1024]{1,0:T(8,128)(2,1)S(1)}, u32[]{:S(2)}, u32[]{:S(2)}) collective-permute-start(bf16[96,1024]{1,0:T(8,128)(2,1)} %get-tuple-element.38), channel_id=1, source_target_pairs={{0,2},{1,3},{2,0},{3,1},{4,6},{5,7},{6,4},{7,5},{8,10},{9,11},{10,... | collective-permute-start | bytes 589832 | tf_op jit(solution)/shard_map/ppermute | solution.py:518
  21.0 1.5 %collective-permute-start.5 = (bf16[96,1024]{1,0:T(8,128)(2,1)}, bf16[96,1024]{1,0:T(8,128)(2,1)S(1)}, u32[]{:S(2)}, u32[]{:S(2)}) collective-permute-start(bf16[96,1024]{1,0:T(8,128)(2,1)} %get-tuple-element.39), channel_id=1, source_target_pairs={{0,4},{1,5},{2,6},{3,7},{4,0},{5,1},{6,2},{7,3},{8,12},{9,13},{10,... | collective-permute-start | bytes 589832 | tf_op jit(solution)/shard_map/ppermute | solution.py:518
  22.5 7.3 %all-to-all-done.refs_0_.refs_1_ = s32[16,1,330]{2,1,0:T(1,128)S(1)} async-done(((s32[16,1,330]{2,1,0:T(1,128)}), s32[16,1,330]{2,1,0:T(1,128)S(1)}, u32[]{:S(2)}, u32[]{:S(2)}) %all-to-all-start) | async-done | bytes 21152 | tf_op jit(solution)/shard_map/all_to_all | solution.py:529
  29.8 0.1 eq.15
  29.9 0.0 copy-done
  29.9 1.3 %convolution_convert_fusion = bf16[384,1024]{1,0:T(8,128)(2,1)} fusion(bf16[240,1024]{1,0:T(8,128)(2,1)S(1)} %copy-done, s32[384]{0:T(512)S(1)} %eq.15), kind=kOutput, calls=%fused_computation.1 | convolution fusion | flops 189229056 | bytes 1279488 | tf_op jit(solution)/shard_map/dot_general | solution.py:535
  31.2 1.6 %collective-permute-done.1.refs_2_ = bf16[96,1024]{1,0:T(8,128)(2,1)S(1)} collective-permute-done((bf16[96,1024]{1,0:T(8,128)(2,1)S(1)}, bf16[96,1024]{1,0:T(8,128)(2,1)S(1)}, u32[]{:S(2)}, u32[]{:S(2)}) %collective-permute-start.1) | collective-permute-done | bytes 196640 | tf_op jit(solution)/shard_map/ppermute | solution.py:523
  32.8 0.0 collective-permute-done.4.rest_1_
  32.8 4.0 %collective-permute-done.5.rest_2_ = bf16[96,1024]{1,0:T(8,128)(2,1)S(1)} collective-permute-done((bf16[96,1024]{1,0:T(8,128)(2,1)}, bf16[96,1024]{1,0:T(8,128)(2,1)S(1)}, u32[]{:S(2)}, u32[]{:S(2)}) %collective-permute-start.5) | collective-permute-done | bytes 196640 | tf_op jit(solution)/shard_map/ppermute | solution.py:518
  36.7 0.0 collective-permute-done.2.refs_3_
  36.8 4.8 %all-to-all-start.1 = ((bf16[16,24,1024]{2,1,0:T(8,128)(2,1)}), bf16[16,24,1024]{2,1,0:T(8,128)(2,1)S(1)}, u32[]{:S(2)}, u32[]{:S(2)}) async-start(bf16[16,24,1024]{2,1,0:T(8,128)(2,1)} %bitcast.4), calls=%async_computation.1 | async-start | bytes 1572864 | tf_op jit(solution)/shard_map/all_to_all | solution.py:541
  41.6 0.4 collective-permute-start.8
  42.0 0.2 collective-permute-start.7
  42.2 0.0 copy-done.16
  42.2 2.8 %collective-permute-start.6 = (bf16[96,1024]{1,0:T(8,128)(2,1)S(1)}, bf16[96,1024]{1,0:T(8,128)(2,1)S(1)}, u32[]{:S(2)}, u32[]{:S(2)}) collective-permute-start(bf16[96,1024]{1,0:T(8,128)(2,1)S(1)} %copy-done.16), channel_id=1, source_target_pairs={{0,6},{1,7},{2,4},{3,5},{4,2},{5,3},{6,0},{7,1},{8,14},{9,15},{10,... | collective-permute-start | bytes 589832 | tf_op jit(solution)/shard_map/ppermute | solution.py:518
  45.0 0.1 slice.29
  45.1 0.1 slice.28
  45.1 0.7 reshape.42.late_far
  45.8 0.6 gather_fusion
  46.4 0.7 reshape.41.places_far
  47.0 0.0 collective-permute-done.7.refs_4_
  47.0 0.0 collective-permute-done.8.refs_5_
  47.0 0.0 copy-done.5
  47.0 0.0 copy-done.13
  47.1 0.0 copy-done.3
  47.1 0.6 copy-done.14
  47.7 0.7 copy-done.4
  48.4 2.9 %pack.3 = (bf16[96,1024]{1,0:T(8,128)(2,1)}, bf16[96,1024]{1,0:T(8,128)(2,1)}, bf16[96,1024]{1,0:T(8,128)(2,1)}, bf16[96,1024]{1,0:T(8,128)(2,1)}) custom-call(s32[16,1,330]{2,1,0:T(1,128)} %copy-done.5, s32[16,1,330]{2,1,0:T(1,128)} %copy-done.5, bf16[96,1024]{1,0:T(8,128)(2,1)} %copy-done.13, bf16[158,1024]{1,0:T(8,128)(2,1)} %copy-done.3, ...), custom_call_target="tpu_custom_call" | custom-call | flops 199753728 | bytes 1826816 | tf_op jit(solution)/shard_map/pack/pallas_call | solution.py:302
  51.4 0.6 collective-permute-start.9
  52.0 0.2 collective-permute-start.10
  52.1 2.8 %collective-permute-start.11 = (bf16[96,1024]{1,0:T(8,128)(2,1)}, bf16[96,1024]{1,0:T(8,128)(2,1)S(1)}, u32[]{:S(2)}, u32[]{:S(2)}) collective-permute-start(bf16[96,1024]{1,0:T(8,128)(2,1)} %get-tuple-element.59), channel_id=1, source_target_pairs={{0,6},{1,7},{2,4},{3,5},{4,2},{5,3},{6,0},{7,1},{8,14},{9,15},{10,... | collective-permute-start | bytes 589832 | tf_op jit(solution)/shard_map/ppermute | solution.py:518
  54.9 0.0 copy-done.11
  54.9 0.0 copy-done.12
  54.9 3.7 %early.1 = (f32[512,1024]{1,0:T(8,128)}, f32[512,128]{1,0:T(8,128)}) custom-call(s32[1,768]{1,0:T(1,128)} %reshape.41.places_far, f32[512,1024]{1,0:T(8,128)} %centroids_far.1, bf16[96,1024]{1,0:T(8,128)(2,1)} %get-tuple-element.41.rest_0_, bf16[96,1024]{1,0:T(8,128)(2,1)} %copy-done.11, bf16[96,1024]{1,0:T(8,128)(2,1)} %copy-done.12), custom_call_target="tpu_custom_call" | custom-call | flops 301989888 | bytes 4194304 | tf_op jit(solution)/shard_map/early/pallas_call | solution.py:425
  58.6 2.1 %all-to-all-done.1 = bf16[16,24,1024]{2,1,0:T(8,128)(2,1)S(1)} async-done(((bf16[16,24,1024]{2,1,0:T(8,128)(2,1)}), bf16[16,24,1024]{2,1,0:T(8,128)(2,1)S(1)}, u32[]{:S(2)}, u32[]{:S(2)}) %all-to-all-start.1) | async-done | bytes 786464 | tf_op jit(solution)/shard_map/all_to_all | solution.py:541
  60.7 0.9 %copy-done.1 = bf16[16,24,1024]{2,1,0:T(8,128)(2,1)} copy-done((bf16[16,24,1024]{2,1,0:T(8,128)(2,1)}, bf16[16,24,1024]{2,1,0:T(8,128)(2,1)S(1)}, u32[]{:S(2)}) %copy-start.1) | copy-done | bytes 786456
  61.6 5.0 %encode.1 = (bf16[2,1024]{1,0:T(2,128)(2,1)}, bf16[16,2,1024]{2,1,0:T(2,128)(2,1)}) custom-call(s32[1,2]{1,0:T(1,128)} %bitcast.26, s32[128,1]{1,0:T(8,128)} %get-tuple-element.31.refs_1_, bf16[384,1024]{1,0:T(8,128)(2,1)} %bitcast.15, bf16[64,1024]{1,0:T(8,128)(2,1)} %refs_3_.1, f32[1,1024]{1,0:T(1,128)} %bitcast.19, f32[1,1024]{1,0:T(1,128)} %bitcast.20, ...), custom_call_target="tpu_custom_call" | custom-call | flops 637534208 | bytes 6291456 | tf_op jit(solution)/shard_map/encode/pallas_call | solution.py:121
  66.6 5.6 %all-to-all-start.2 = ((bf16[16,2,1024]{2,1,0:T(2,128)(2,1)}), bf16[16,2,1024]{2,1,0:T(2,128)(2,1)S(1)}, u32[]{:S(2)}, u32[]{:S(2)}) async-start(bf16[16,2,1024]{2,1,0:T(2,128)(2,1)} %get-tuple-element.50), calls=%async_computation.2 | async-start | bytes 131072 | tf_op jit(solution)/shard_map/all_to_all | solution.py:574
  72.2 0.0 collective-permute-done.6.rest_0_
  72.2 0.0 copy-start.7
  72.2 0.0 collective-permute-done.9.rest_2_
  72.2 0.0 copy-start.8
  72.2 0.0 collective-permute-done.10.rest_3_
  72.3 0.0 collective-permute-done.11.rest_4_
  72.3 0.0 copy-start.10
  72.3 6.8 %all-to-all-done.2.spread_far = bf16[16,2,1024]{2,1,0:T(2,128)(2,1)S(1)} async-done(((bf16[16,2,1024]{2,1,0:T(2,128)(2,1)}), bf16[16,2,1024]{2,1,0:T(2,128)(2,1)S(1)}, u32[]{:S(2)}, u32[]{:S(2)}) %all-to-all-start.2) | async-done | bytes 65568 | tf_op jit(solution)/shard_map/all_to_all | solution.py:574
  79.1 0.6 copy-done.6
  79.7 3.7 %late.1 = f32[512,1024]{1,0:T(8,128)} custom-call(s32[1,768]{1,0:T(1,128)} %reshape.41.places_far, s32[1,32]{1,0:T(1,128)} %reshape.42.late_far, bf16[16,2,1024]{2,1,0:T(2,128)(2,1)} %copy-done.6, f32[512,128]{1,0:T(8,128)} %get-tuple-element.51.share_far, f32[512,1024]{1,0:T(8,128)} %get-tuple-element.52.early_far, bf16[96,1024]{1,0:T(8,128)(2,1)} %copy-done.7, ...), custom_call_target="tpu_custom_call" | custom-call | flops 536870912 | bytes 4194304 | tf_op jit(solution)/shard_map/late/pallas_call | solution.py:457
  (18 shorter events, 0.0 us)
Async XLA Ops:
  0.6 29.2 %copy-start = (bf16[240,1024]{1,0:T(8,128)(2,1)S(1)}, bf16[240,1024]{1,0:T(8,128)(2,1)}, u32[]{:S(2)}) copy-start(bf16[240,1024]{1,0:T(8,128)(2,1)} %param.17) | copy-start | bytes 1474564
  0.6 2.8 %collective-permute-start = (bf16[254,1024]{1,0:T(8,128)(2,1)}, bf16[254,1024]{1,0:T(8,128)(2,1)S(1)}, u32[]{:S(2)}, u32[]{:S(2)}) collective-permute-start(bf16[254,1024]{1,0:T(8,128)(2,1)} %refs_2_.1), channel_id=1, source_target_pairs={{0,1},{1,0},{2,3},{3,2},{4,5},{5,4},{6,7},{7,6},{8,9},{9,8},{10,11... | collective-permute-start | bytes 1560584 | tf_op jit(solution)/shard_map/ppermute | solution.py:522
  3.4 12.8 %copy-start.2 = (bf16[254,1024]{1,0:T(8,128)(2,1)}, bf16[254,1024]{1,0:T(8,128)(2,1)S(1)}, u32[]{:S(2)}) copy-start(bf16[254,1024]{1,0:T(8,128)(2,1)S(1)} %collective-permute-done.refs_3_) | copy-start | bytes 1560580
  4.7 32.1 %collective-permute-start.2 = (bf16[158,1024]{1,0:T(8,128)(2,1)S(1)}, bf16[158,1024]{1,0:T(8,128)(2,1)S(1)}, u32[]{:S(2)}, u32[]{:S(2)}) collective-permute-start(bf16[158,1024]{1,0:T(8,128)(2,1)S(1)} %slice.21), channel_id=1, source_target_pairs={{0,8},{1,9},{2,10},{3,11},{4,12},{5,13},{6,14},{7,15},{8,0},{9,1},... | collective-permute-start | bytes 970760 | tf_op jit(solution)/shard_map/ppermute | solution.py:528
  8.4 21.4 %all-to-all-start = ((s32[16,1,330]{2,1,0:T(1,128)}), s32[16,1,330]{2,1,0:T(1,128)S(1)}, u32[]{:S(2)}, u32[]{:S(2)}) async-start(s32[16,1,330]{2,1,0:T(1,128)} %get-tuple-element.33), calls=%async_computation | async-start | bytes 49152 | tf_op jit(solution)/shard_map/all_to_all | solution.py:529
  12.3 4.0 %collective-permute-start.3 = (s32[1,256]{1,0:T(1,128)}, s32[1,256]{1,0:T(1,128)S(1)}, u32[]{:S(2)}, u32[]{:S(2)}) collective-permute-start(s32[1,256]{1,0:T(1,128)} %get-tuple-element.35.refs_0_), channel_id=1, source_target_pairs={{0,1},{1,0},{2,3},{3,2},{4,5},{5,4},{6,7},{7,6},{8,9},{9,8},{10,11... | collective-permute-start | bytes 3080 | tf_op jit(solution)/shard_map/ppermute | solution.py:526
  13.6 19.1 %collective-permute-start.1 = (bf16[96,1024]{1,0:T(8,128)(2,1)S(1)}, bf16[96,1024]{1,0:T(8,128)(2,1)S(1)}, u32[]{:S(2)}, u32[]{:S(2)}) collective-permute-start(bf16[96,1024]{1,0:T(8,128)(2,1)S(1)} %slice.20), channel_id=1, source_target_pairs={{0,8},{1,9},{2,10},{3,11},{4,12},{5,13},{6,14},{7,15},{8,0},{9,1},... | collective-permute-start | bytes 589832 | tf_op jit(solution)/shard_map/ppermute | solution.py:523
  16.3 0.6 copy-start.15
  19.5 22.7 %copy-start.16 = (bf16[96,1024]{1,0:T(8,128)(2,1)S(1)}, bf16[96,1024]{1,0:T(8,128)(2,1)}, u32[]{:S(2)}) copy-start(bf16[96,1024]{1,0:T(8,128)(2,1)} %get-tuple-element.53) | copy-start | bytes 589828
  19.5 13.3 %collective-permute-start.4 = (bf16[96,1024]{1,0:T(8,128)(2,1)}, bf16[96,1024]{1,0:T(8,128)(2,1)S(1)}, u32[]{:S(2)}, u32[]{:S(2)}) collective-permute-start(bf16[96,1024]{1,0:T(8,128)(2,1)} %get-tuple-element.38), channel_id=1, source_target_pairs={{0,2},{1,3},{2,0},{3,1},{4,6},{5,7},{6,4},{7,5},{8,10},{9,11},{10,... | collective-permute-start | bytes 589832 | tf_op jit(solution)/shard_map/ppermute | solution.py:518
  21.0 15.7 %collective-permute-start.5 = (bf16[96,1024]{1,0:T(8,128)(2,1)}, bf16[96,1024]{1,0:T(8,128)(2,1)S(1)}, u32[]{:S(2)}, u32[]{:S(2)}) collective-permute-start(bf16[96,1024]{1,0:T(8,128)(2,1)} %get-tuple-element.39), channel_id=1, source_target_pairs={{0,4},{1,5},{2,6},{3,7},{4,0},{5,1},{6,2},{7,3},{8,12},{9,13},{10,... | collective-permute-start | bytes 589832 | tf_op jit(solution)/shard_map/ppermute | solution.py:518
  29.8 17.3 %copy-start.5 = (s32[16,1,330]{2,1,0:T(1,128)}, s32[16,1,330]{2,1,0:T(1,128)S(1)}, u32[]{:S(2)}) copy-start(s32[16,1,330]{2,1,0:T(1,128)S(1)} %all-to-all-done.refs_0_.refs_1_) | copy-start | bytes 63364
  32.8 14.3 %copy-start.13 = (bf16[96,1024]{1,0:T(8,128)(2,1)}, bf16[96,1024]{1,0:T(8,128)(2,1)S(1)}, u32[]{:S(2)}) copy-start(bf16[96,1024]{1,0:T(8,128)(2,1)S(1)} %collective-permute-done.1.refs_2_) | copy-start | bytes 589828
  32.8 22.1 %copy-start.11 = (bf16[96,1024]{1,0:T(8,128)(2,1)}, bf16[96,1024]{1,0:T(8,128)(2,1)S(1)}, u32[]{:S(2)}) copy-start(bf16[96,1024]{1,0:T(8,128)(2,1)S(1)} %collective-permute-done.4.rest_1_) | copy-start | bytes 589828
  36.7 18.2 %copy-start.12 = (bf16[96,1024]{1,0:T(8,128)(2,1)}, bf16[96,1024]{1,0:T(8,128)(2,1)S(1)}, u32[]{:S(2)}) copy-start(bf16[96,1024]{1,0:T(8,128)(2,1)S(1)} %collective-permute-done.5.rest_2_) | copy-start | bytes 589828
  36.7 10.3 %copy-start.3 = (bf16[158,1024]{1,0:T(8,128)(2,1)}, bf16[158,1024]{1,0:T(8,128)(2,1)S(1)}, u32[]{:S(2)}) copy-start(bf16[158,1024]{1,0:T(8,128)(2,1)S(1)} %collective-permute-done.2.refs_3_) | copy-start | bytes 970756
  36.8 23.9 %all-to-all-start.1 = ((bf16[16,24,1024]{2,1,0:T(8,128)(2,1)}), bf16[16,24,1024]{2,1,0:T(8,128)(2,1)S(1)}, u32[]{:S(2)}, u32[]{:S(2)}) async-start(bf16[16,24,1024]{2,1,0:T(8,128)(2,1)} %bitcast.4), calls=%async_computation.1 | async-start | bytes 1572864 | tf_op jit(solution)/shard_map/all_to_all | solution.py:541
  41.6 5.5 %collective-permute-start.8 = (bf16[158,1024]{1,0:T(8,128)(2,1)S(1)}, bf16[158,1024]{1,0:T(8,128)(2,1)S(1)}, u32[]{:S(2)}, u32[]{:S(2)}) collective-permute-start(bf16[158,1024]{1,0:T(8,128)(2,1)S(1)} %collective-permute-done.2.refs_3_), channel_id=1, source_target_pairs={{0,1},{1,0},{2,3},{3,2},{4,5},{5,4},{6,7},{7,6},{8,9},{9,8},{10,11... | collective-permute-start | bytes 970760 | tf_op jit(solution)/shard_map/ppermute | solution.py:546
  42.0 5.1 %collective-permute-start.7 = (bf16[96,1024]{1,0:T(8,128)(2,1)S(1)}, bf16[96,1024]{1,0:T(8,128)(2,1)S(1)}, u32[]{:S(2)}, u32[]{:S(2)}) collective-permute-start(bf16[96,1024]{1,0:T(8,128)(2,1)S(1)} %collective-permute-done.1.refs_2_), channel_id=1, source_target_pairs={{0,1},{1,0},{2,3},{3,2},{4,5},{5,4},{6,7},{7,6},{8,9},{9,8},{10,11... | collective-permute-start | bytes 589832 | tf_op jit(solution)/shard_map/ppermute | solution.py:546
  42.2 30.0 %collective-permute-start.6 = (bf16[96,1024]{1,0:T(8,128)(2,1)S(1)}, bf16[96,1024]{1,0:T(8,128)(2,1)S(1)}, u32[]{:S(2)}, u32[]{:S(2)}) collective-permute-start(bf16[96,1024]{1,0:T(8,128)(2,1)S(1)} %copy-done.16), channel_id=1, source_target_pairs={{0,6},{1,7},{2,4},{3,5},{4,2},{5,3},{6,0},{7,1},{8,14},{9,15},{10,... | collective-permute-start | bytes 589832 | tf_op jit(solution)/shard_map/ppermute | solution.py:518
  47.0 0.7 copy-start.14
  47.7 0.7 copy-start.4
  51.4 20.9 %collective-permute-start.9 = (bf16[96,1024]{1,0:T(8,128)(2,1)}, bf16[96,1024]{1,0:T(8,128)(2,1)S(1)}, u32[]{:S(2)}, u32[]{:S(2)}) collective-permute-start(bf16[96,1024]{1,0:T(8,128)(2,1)} %get-tuple-element.57), channel_id=1, source_target_pairs={{0,2},{1,3},{2,0},{3,1},{4,6},{5,7},{6,4},{7,5},{8,10},{9,11},{10,... | collective-permute-start | bytes 589832 | tf_op jit(solution)/shard_map/ppermute | solution.py:518
  52.0 20.3 %collective-permute-start.10 = (bf16[96,1024]{1,0:T(8,128)(2,1)}, bf16[96,1024]{1,0:T(8,128)(2,1)S(1)}, u32[]{:S(2)}, u32[]{:S(2)}) collective-permute-start(bf16[96,1024]{1,0:T(8,128)(2,1)} %get-tuple-element.58), channel_id=1, source_target_pairs={{0,4},{1,5},{2,6},{3,7},{4,0},{5,1},{6,2},{7,3},{8,12},{9,13},{10,... | collective-permute-start | bytes 589832 | tf_op jit(solution)/shard_map/ppermute | solution.py:518
  52.1 20.1 %collective-permute-start.11 = (bf16[96,1024]{1,0:T(8,128)(2,1)}, bf16[96,1024]{1,0:T(8,128)(2,1)S(1)}, u32[]{:S(2)}, u32[]{:S(2)}) collective-permute-start(bf16[96,1024]{1,0:T(8,128)(2,1)} %get-tuple-element.59), channel_id=1, source_target_pairs={{0,6},{1,7},{2,4},{3,5},{4,2},{5,3},{6,0},{7,1},{8,14},{9,15},{10,... | collective-permute-start | bytes 589832 | tf_op jit(solution)/shard_map/ppermute | solution.py:518
  60.7 0.9 %copy-start.1 = (bf16[16,24,1024]{2,1,0:T(8,128)(2,1)}, bf16[16,24,1024]{2,1,0:T(8,128)(2,1)S(1)}, u32[]{:S(2)}) copy-start(bf16[16,24,1024]{2,1,0:T(8,128)(2,1)S(1)} %all-to-all-done.1) | copy-start | bytes 2359300
  66.6 12.5 %all-to-all-start.2 = ((bf16[16,2,1024]{2,1,0:T(2,128)(2,1)}), bf16[16,2,1024]{2,1,0:T(2,128)(2,1)S(1)}, u32[]{:S(2)}, u32[]{:S(2)}) async-start(bf16[16,2,1024]{2,1,0:T(2,128)(2,1)} %get-tuple-element.50), calls=%async_computation.2 | async-start | bytes 131072 | tf_op jit(solution)/shard_map/all_to_all | solution.py:574
  72.2 6.9 %copy-start.7 = (bf16[96,1024]{1,0:T(8,128)(2,1)}, bf16[96,1024]{1,0:T(8,128)(2,1)S(1)}, u32[]{:S(2)}) copy-start(bf16[96,1024]{1,0:T(8,128)(2,1)S(1)} %collective-permute-done.6.rest_0_) | copy-start | bytes 589828
  72.2 6.9 %copy-start.8 = (bf16[96,1024]{1,0:T(8,128)(2,1)}, bf16[96,1024]{1,0:T(8,128)(2,1)S(1)}, u32[]{:S(2)}) copy-start(bf16[96,1024]{1,0:T(8,128)(2,1)S(1)} %collective-permute-done.9.rest_2_) | copy-start | bytes 589828
  72.3 6.9 %copy-start.9 = (bf16[96,1024]{1,0:T(8,128)(2,1)}, bf16[96,1024]{1,0:T(8,128)(2,1)S(1)}, u32[]{:S(2)}) copy-start(bf16[96,1024]{1,0:T(8,128)(2,1)S(1)} %collective-permute-done.10.rest_3_) | copy-start | bytes 589828
  72.3 6.8 %copy-start.10 = (bf16[96,1024]{1,0:T(8,128)(2,1)}, bf16[96,1024]{1,0:T(8,128)(2,1)S(1)}, u32[]{:S(2)}) copy-start(bf16[96,1024]{1,0:T(8,128)(2,1)S(1)} %collective-permute-done.11.rest_4_) | copy-start | bytes 589828
  79.1 0.6 copy-start.6

commit v15 on v13

--- a/solution.py
+++ b/solution.py
@@ -518,7 +518,7 @@
             got.append(lax.ppermute(blocks[step], "dp", moves))
         return got
 
-    ahead = store_count * 3 // 4 // 16 * 16
+    ahead = store_count * 5 // 8 // 16 * 16
     sibling_rows = lax.ppermute(stored_rows, "dp", beside)
     first_rows = lax.ppermute(stored_rows[:ahead], "dp", across)
     sizes = (peer_count, vocab_rows, token_cap, row_cap, row_count - store_count)

time: 78.9 us -> 86.1 us (1.091)
  waiting for transfers between devices: 18.3 us -> 24.7 us
    ppermute x1, waiting for transfers between devices: 0.01 us -> 9.73 us  [shards(): first_rows = lax.ppermute(stored_rows[:ahead], 'dp', across)]
    all_to_all x1, waiting for transfers between devices: 5.5 us -> 0.01 us  [shards(): codes = lax.all_to_all(plan, 'dp', split_axis=0, concat_axis=0, tiled=True)]
    ppermute x1, waiting for transfers between devices: 0.83 us -> 4.55 us  [shards(): last_rows = lax.ppermute(last_rows, 'dp', across)]
    all_to_all x1, starting transfers between devices: 3.92 us -> 7.06 us  [shards(): codes = lax.all_to_all(plan, 'dp', split_axis=0, concat_axis=0, tiled=True)]
    ppermute x1, starting transfers between devices: 2.8 us -> 0.56 us  [shards(): last_rows = lax.ppermute(last_rows, 'dp', across)]
    ppermute x6, waiting for transfers between devices: 1.88 us -> 0.02 us  [hand_on(): got.append(lax.ppermute(blocks[step], 'dp', moves))]
    all_to_all x1, starting transfers between devices: 4.51 us -> 5.51 us  [shards(): lax.all_to_all(found.reshape(peer_count, token_cap, width), 'dp', split_a...]
  transfers between devices with their start and end apart: 15 -> 15, of which waited for: 6 -> 5; matrix products, arithmetic and copies ran while one was open for 6% -> 5% of each run, Pallas kernels for 21% -> 19%
where the time goes in v15:
time: 86.1 us; the launch traced here: 85.6 us
  starting transfers between devices  32.1 us (37%)
  waiting for transfers between devices  24.7 us (29%)
  Pallas kernels  20.1 us (23%)
  local copies, waits for them, and re-layouts  6.53 us (8%)
  matrix products  1.29 us (1%)
  between operations  0.89 us (1%)
    ppermute x1, waiting for transfers between devices, shards(): first_rows = lax.ppermute(stored_rows[:ahead], 'dp', across)  9.73 us
    ppermute x6, starting transfers between devices, hand_on(): got.append(lax.ppermute(blocks[step], 'dp', moves))  9.37 us
    all_to_all x1, starting transfers between devices, shards(): codes = lax.all_to_all(plan, 'dp', split_axis=0, concat_axis=0, tiled=True)  7.06 us
    all_to_all x1, waiting for transfers between devices, shards(): lax.all_to_all(spread, 'dp', split_axis=0, concat_axis=0, tiled=True)  6.81 us
    all_to_all x1, starting transfers between devices, shards(): lax.all_to_all(spread, 'dp', split_axis=0, concat_axis=0, tiled=True)  5.65 us
    all_to_all x1, starting transfers between devices, shards(): lax.all_to_all(found.reshape(peer_count, token_cap, width), 'dp', split_a...  5.51 us
    pallas_call x2, Pallas kernels, pack_rows(): pl.pallas_call(functools.partial(pack_kernel, half, row_cap, count, picks...  5.51 us
    pallas_call x1, Pallas kernels, encode(): pl.pallas_call(encode_kernel, out_shape=[jax.ShapeDtypeStruct((passes, wi...  4.97 us
  transfers between devices with their start and end apart: 15, of which 5 were waited for; matrix products, arithmetic and copies ran while one was open for 5% of the time, Pallas kernels for 19%

profile of v15, /device:TPU:0, one launch (start us, length us, event | category | flops | bytes accessed | tf_op | source)
XLA Modules:
  0.0 85.6 jit_solution(11418508946332218987)
XLA Ops:
  0.6 0.0 copy-start
  0.6 0.5 collective-permute-start
  1.2 2.3 %route.1 = (s32[16,1,330]{2,1,0:T(1,128)}, s32[128,1]{1,0:T(8,128)}, s32[1,256]{1,0:T(1,128)}) custom-call(s32[2,64]{1,0:T(2,128)} %token_ids_far.1, s32[1,256]{1,0:T(1,128)} %bitcast.24, s32[1,256]{1,0:T(1,128)} %bitcast.25), custom_call_target="tpu_custom_call" | custom-call | tf_op jit(solution)/shard_map/route/pallas_call | solution.py:214
  3.4 0.0 collective-permute-done.refs_3_
  3.5 0.0 copy-start.2
  3.5 7.1 %all-to-all-start = ((s32[16,1,330]{2,1,0:T(1,128)}), s32[16,1,330]{2,1,0:T(1,128)S(1)}, u32[]{:S(2)}, u32[]{:S(2)}) async-start(s32[16,1,330]{2,1,0:T(1,128)} %get-tuple-element.33), calls=%async_computation | async-start | bytes 49152 | tf_op jit(solution)/shard_map/all_to_all | solution.py:528
  10.5 1.0 %slice.17 = bf16[144,1024]{1,0:T(8,128)(2,1)S(1)} slice(bf16[254,1024]{1,0:T(8,128)(2,1)} %refs_2_.1), slice={[0:144], [0:1024]} | slice | bytes 589824 | tf_op jit(solution)/shard_map/slice | solution.py:523
  11.5 2.9 %collective-permute-start.1 = (bf16[144,1024]{1,0:T(8,128)(2,1)S(1)}, bf16[144,1024]{1,0:T(8,128)(2,1)S(1)}, u32[]{:S(2)}, u32[]{:S(2)}) collective-permute-start(bf16[144,1024]{1,0:T(8,128)(2,1)S(1)} %slice.17), channel_id=1, source_target_pairs={{0,8},{1,9},{2,10},{3,11},{4,12},{5,13},{6,14},{7,15},{8,0},{9,1},... | collective-permute-start | bytes 884744 | tf_op jit(solution)/shard_map/ppermute | solution.py:523
  14.4 0.0 collective-permute-start.2
  14.4 1.3 %collective-permute-done.2.refs_1_ = s32[1,256]{1,0:T(1,128)S(1)} collective-permute-done((s32[1,256]{1,0:T(1,128)}, s32[1,256]{1,0:T(1,128)S(1)}, u32[]{:S(2)}, u32[]{:S(2)}) %collective-permute-start.2) | collective-permute-done | bytes 1056 | tf_op jit(solution)/shard_map/ppermute | solution.py:526
  15.8 0.0 copy-done.2
  15.8 0.5 copy-done.15
  16.3 2.7 %pack.2 = (bf16[96,1024]{1,0:T(8,128)(2,1)}, bf16[96,1024]{1,0:T(8,128)(2,1)}, bf16[96,1024]{1,0:T(8,128)(2,1)}, bf16[96,1024]{1,0:T(8,128)(2,1)}, bf16[110,1024]{1,0:T(8,128)(2,1)}) custom-call(s32[1,256]{1,0:T(1,128)} %get-tuple-element.34.refs_0_, s32[1,256]{1,0:T(1,128)} %copy-done.15, bf16[254,1024]{1,0:T(8,128)(2,1)} %refs_2_.1, ...), custom_call_target="tpu_custom_call" | custom-call | flops 199753728 | bytes 1826816 | tf_op jit(solution)/shard_map/pack/pallas_call | solution.py:302
  19.0 0.0 copy-start.16
  19.0 1.5 %collective-permute-start.4 = (bf16[96,1024]{1,0:T(8,128)(2,1)}, bf16[96,1024]{1,0:T(8,128)(2,1)S(1)}, u32[]{:S(2)}, u32[]{:S(2)}) collective-permute-start(bf16[96,1024]{1,0:T(8,128)(2,1)} %get-tuple-element.38), channel_id=1, source_target_pairs={{0,2},{1,3},{2,0},{3,1},{4,6},{5,7},{6,4},{7,5},{8,10},{9,11},{10,... | collective-permute-start | bytes 589832 | tf_op jit(solution)/shard_map/ppermute | solution.py:518
  20.5 1.5 %collective-permute-start.5 = (bf16[96,1024]{1,0:T(8,128)(2,1)}, bf16[96,1024]{1,0:T(8,128)(2,1)S(1)}, u32[]{:S(2)}, u32[]{:S(2)}) collective-permute-start(bf16[96,1024]{1,0:T(8,128)(2,1)} %get-tuple-element.39), channel_id=1, source_target_pairs={{0,4},{1,5},{2,6},{3,7},{4,0},{5,1},{6,2},{7,3},{8,12},{9,13},{10,... | collective-permute-start | bytes 589832 | tf_op jit(solution)/shard_map/ppermute | solution.py:518
  22.0 0.6 collective-permute-start.3
  22.5 0.0 all-to-all-done.refs_0_.refs_1_
  22.5 0.1 eq.15
  22.6 0.0 copy-done
  22.6 1.3 %convolution_convert_fusion = bf16[384,1024]{1,0:T(8,128)(2,1)} fusion(bf16[240,1024]{1,0:T(8,128)(2,1)S(1)} %copy-done, s32[384]{0:T(512)S(1)} %eq.15), kind=kOutput, calls=%fused_computation.1 | convolution fusion | flops 189229056 | bytes 1279488 | tf_op jit(solution)/shard_map/dot_general | solution.py:544
  23.9 9.7 %collective-permute-done.1.refs_2_ = bf16[144,1024]{1,0:T(8,128)(2,1)S(1)} collective-permute-done((bf16[144,1024]{1,0:T(8,128)(2,1)S(1)}, bf16[144,1024]{1,0:T(8,128)(2,1)S(1)}, u32[]{:S(2)}, u32[]{:S(2)}) %collective-permute-start.1) | collective-permute-done | bytes 294944 | tf_op jit(solution)/shard_map/ppermute | solution.py:523
  33.7 0.0 collective-permute-done.4.rest_1_
  33.7 0.0 collective-permute-done.5.rest_2_
  33.7 0.0 copy-start.14
  33.7 4.6 %collective-permute-done.3.refs_3_ = bf16[110,1024]{1,0:T(8,128)(2,1)S(1)} collective-permute-done((bf16[110,1024]{1,0:T(8,128)(2,1)}, bf16[110,1024]{1,0:T(8,128)(2,1)S(1)}, u32[]{:S(2)}, u32[]{:S(2)}) %collective-permute-start.3) | collective-permute-done | bytes 225312 | tf_op jit(solution)/shard_map/ppermute | solution.py:539
  38.2 5.5 %all-to-all-start.1 = ((bf16[16,24,1024]{2,1,0:T(8,128)(2,1)}), bf16[16,24,1024]{2,1,0:T(8,128)(2,1)S(1)}, u32[]{:S(2)}, u32[]{:S(2)}) async-start(bf16[16,24,1024]{2,1,0:T(8,128)(2,1)} %bitcast.4), calls=%async_computation.1 | async-start | bytes 1572864 | tf_op jit(solution)/shard_map/all_to_all | solution.py:550
  43.8 0.4 collective-permute-start.7
  44.2 0.2 collective-permute-start.8
  44.3 0.0 copy-done.16
  44.4 2.8 %collective-permute-start.6 = (bf16[96,1024]{1,0:T(8,128)(2,1)S(1)}, bf16[96,1024]{1,0:T(8,128)(2,1)S(1)}, u32[]{:S(2)}, u32[]{:S(2)}) collective-permute-start(bf16[96,1024]{1,0:T(8,128)(2,1)S(1)} %copy-done.16), channel_id=1, source_target_pairs={{0,6},{1,7},{2,4},{3,5},{4,2},{5,3},{6,0},{7,1},{8,14},{9,15},{10,... | collective-permute-start | bytes 589832 | tf_op jit(solution)/shard_map/ppermute | solution.py:518
  47.2 0.1 slice.25
  47.3 0.1 slice.24
  47.3 0.7 reshape.42.late_far
  48.0 0.6 gather_fusion
  48.6 0.7 reshape.41.places_far
  49.2 0.0 collective-permute-done.8.refs_5_
  49.2 0.0 collective-permute-done.7.refs_4_
  49.2 0.0 copy-done.5
  49.2 0.0 copy-done.3
  49.2 0.0 copy-done.7
  49.3 0.6 copy-done.8
  49.9 0.7 copy-done.4
  50.6 2.9 %pack.3 = (bf16[96,1024]{1,0:T(8,128)(2,1)}, bf16[96,1024]{1,0:T(8,128)(2,1)}, bf16[96,1024]{1,0:T(8,128)(2,1)}, bf16[96,1024]{1,0:T(8,128)(2,1)}) custom-call(s32[16,1,330]{2,1,0:T(1,128)} %copy-done.5, s32[16,1,330]{2,1,0:T(1,128)} %copy-done.5, bf16[144,1024]{1,0:T(8,128)(2,1)} %copy-done.3, bf16[110,1024]{1,0:T(8,128)(2,1)} %copy-done.7, ...), custom_call_target="tpu_custom_call" | custom-call | flops 199753728 | bytes 1826816 | tf_op jit(solution)/shard_map/pack/pallas_call | solution.py:302
  53.5 0.6 collective-permute-start.9
  54.1 0.2 collective-permute-start.10
  54.3 2.8 %collective-permute-start.11 = (bf16[96,1024]{1,0:T(8,128)(2,1)}, bf16[96,1024]{1,0:T(8,128)(2,1)S(1)}, u32[]{:S(2)}, u32[]{:S(2)}) collective-permute-start(bf16[96,1024]{1,0:T(8,128)(2,1)} %get-tuple-element.59), channel_id=1, source_target_pairs={{0,6},{1,7},{2,4},{3,5},{4,2},{5,3},{6,0},{7,1},{8,14},{9,15},{10,... | collective-permute-start | bytes 589832 | tf_op jit(solution)/shard_map/ppermute | solution.py:518
  57.0 0.0 copy-done.13
  57.0 0.0 copy-done.14
  57.0 3.6 %early.1 = (f32[512,1024]{1,0:T(8,128)}, f32[512,128]{1,0:T(8,128)}) custom-call(s32[1,768]{1,0:T(1,128)} %reshape.41.places_far, f32[512,1024]{1,0:T(8,128)} %centroids_far.1, bf16[96,1024]{1,0:T(8,128)(2,1)} %get-tuple-element.41.rest_0_, bf16[96,1024]{1,0:T(8,128)(2,1)} %copy-done.13, bf16[96,1024]{1,0:T(8,128)(2,1)} %copy-done.14), custom_call_target="tpu_custom_call" | custom-call | flops 301989888 | bytes 4194304 | tf_op jit(solution)/shard_map/early/pallas_call | solution.py:425
  60.7 2.2 %all-to-all-done.1 = bf16[16,24,1024]{2,1,0:T(8,128)(2,1)S(1)} async-done(((bf16[16,24,1024]{2,1,0:T(8,128)(2,1)}), bf16[16,24,1024]{2,1,0:T(8,128)(2,1)S(1)}, u32[]{:S(2)}, u32[]{:S(2)}) %all-to-all-start.1) | async-done | bytes 786464 | tf_op jit(solution)/shard_map/all_to_all | solution.py:550
  62.9 0.9 %copy-done.1 = bf16[16,24,1024]{2,1,0:T(8,128)(2,1)} copy-done((bf16[16,24,1024]{2,1,0:T(8,128)(2,1)}, bf16[16,24,1024]{2,1,0:T(8,128)(2,1)S(1)}, u32[]{:S(2)}) %copy-start.1) | copy-done | bytes 786456
  63.8 5.0 %encode.1 = (bf16[2,1024]{1,0:T(2,128)(2,1)}, bf16[16,2,1024]{2,1,0:T(2,128)(2,1)}) custom-call(s32[1,2]{1,0:T(1,128)} %bitcast.26, s32[128,1]{1,0:T(8,128)} %get-tuple-element.31.refs_1_, bf16[384,1024]{1,0:T(8,128)(2,1)} %bitcast.15, bf16[64,1024]{1,0:T(8,128)(2,1)} %refs_3_.1, f32[1,1024]{1,0:T(1,128)} %bitcast.19, f32[1,1024]{1,0:T(1,128)} %bitcast.20, ...), custom_call_target="tpu_custom_call" | custom-call | flops 637534208 | bytes 6291456 | tf_op jit(solution)/shard_map/encode/pallas_call | solution.py:121
  68.7 5.6 %all-to-all-start.2 = ((bf16[16,2,1024]{2,1,0:T(2,128)(2,1)}), bf16[16,2,1024]{2,1,0:T(2,128)(2,1)S(1)}, u32[]{:S(2)}, u32[]{:S(2)}) async-start(bf16[16,2,1024]{2,1,0:T(2,128)(2,1)} %get-tuple-element.50), calls=%async_computation.2 | async-start | bytes 131072 | tf_op jit(solution)/shard_map/all_to_all | solution.py:583
  74.4 0.0 collective-permute-done.6.rest_0_
  74.4 0.0 collective-permute-done.9.rest_2_
  74.4 0.0 collective-permute-done.10.rest_3_
  74.5 0.0 copy-start.11
  74.5 0.0 collective-permute-done.11.rest_4_
  74.5 6.8 %all-to-all-done.2.spread_far = bf16[16,2,1024]{2,1,0:T(2,128)(2,1)S(1)} async-done(((bf16[16,2,1024]{2,1,0:T(2,128)(2,1)}), bf16[16,2,1024]{2,1,0:T(2,128)(2,1)S(1)}, u32[]{:S(2)}, u32[]{:S(2)}) %all-to-all-start.2) | async-done | bytes 65568 | tf_op jit(solution)/shard_map/all_to_all | solution.py:583
  81.3 0.0 copy-done.10
  81.3 0.0 copy-done.12
  81.3 0.6 copy-done.6
  81.9 3.7 %late.1 = f32[512,1024]{1,0:T(8,128)} custom-call(s32[1,768]{1,0:T(1,128)} %reshape.41.places_far, s32[1,32]{1,0:T(1,128)} %reshape.42.late_far, bf16[16,2,1024]{2,1,0:T(2,128)(2,1)} %copy-done.6, f32[512,128]{1,0:T(8,128)} %get-tuple-element.51.share_far, f32[512,1024]{1,0:T(8,128)} %get-tuple-element.52.early_far, bf16[96,1024]{1,0:T(8,128)(2,1)} %copy-done.9, ...), custom_call_target="tpu_custom_call" | custom-call | flops 536870912 | bytes 4194304 | tf_op jit(solution)/shard_map/late/pallas_call | solution.py:457
  (17 shorter events, 0.0 us)
Async XLA Ops:
  0.6 22.0 %copy-start = (bf16[240,1024]{1,0:T(8,128)(2,1)S(1)}, bf16[240,1024]{1,0:T(8,128)(2,1)}, u32[]{:S(2)}) copy-start(bf16[240,1024]{1,0:T(8,128)(2,1)} %param.17) | copy-start | bytes 1474564
  0.6 2.8 %collective-permute-start = (bf16[254,1024]{1,0:T(8,128)(2,1)}, bf16[254,1024]{1,0:T(8,128)(2,1)S(1)}, u32[]{:S(2)}, u32[]{:S(2)}) collective-permute-start(bf16[254,1024]{1,0:T(8,128)(2,1)} %refs_2_.1), channel_id=1, source_target_pairs={{0,1},{1,0},{2,3},{3,2},{4,5},{5,4},{6,7},{7,6},{8,9},{9,8},{10,11... | collective-permute-start | bytes 1560584 | tf_op jit(solution)/shard_map/ppermute | solution.py:522
  3.5 12.3 %copy-start.2 = (bf16[254,1024]{1,0:T(8,128)(2,1)}, bf16[254,1024]{1,0:T(8,128)(2,1)S(1)}, u32[]{:S(2)}) copy-start(bf16[254,1024]{1,0:T(8,128)(2,1)S(1)} %collective-permute-done.refs_3_) | copy-start | bytes 1560580
  3.5 19.1 %all-to-all-start = ((s32[16,1,330]{2,1,0:T(1,128)}), s32[16,1,330]{2,1,0:T(1,128)S(1)}, u32[]{:S(2)}, u32[]{:S(2)}) async-start(s32[16,1,330]{2,1,0:T(1,128)} %get-tuple-element.33), calls=%async_computation | async-start | bytes 49152 | tf_op jit(solution)/shard_map/all_to_all | solution.py:528
  11.5 22.1 %collective-permute-start.1 = (bf16[144,1024]{1,0:T(8,128)(2,1)S(1)}, bf16[144,1024]{1,0:T(8,128)(2,1)S(1)}, u32[]{:S(2)}, u32[]{:S(2)}) collective-permute-start(bf16[144,1024]{1,0:T(8,128)(2,1)S(1)} %slice.17), channel_id=1, source_target_pairs={{0,8},{1,9},{2,10},{3,11},{4,12},{5,13},{6,14},{7,15},{8,0},{9,1},... | collective-permute-start | bytes 884744 | tf_op jit(solution)/shard_map/ppermute | solution.py:523
  14.4 1.4 %collective-permute-start.2 = (s32[1,256]{1,0:T(1,128)}, s32[1,256]{1,0:T(1,128)S(1)}, u32[]{:S(2)}, u32[]{:S(2)}) collective-permute-start(s32[1,256]{1,0:T(1,128)} %get-tuple-element.34.refs_0_), channel_id=1, source_target_pairs={{0,1},{1,0},{2,3},{3,2},{4,5},{5,4},{6,7},{7,6},{8,9},{9,8},{10,11... | collective-permute-start | bytes 3080 | tf_op jit(solution)/shard_map/ppermute | solution.py:526
  15.8 0.5 copy-start.15
  19.0 25.4 %copy-start.16 = (bf16[96,1024]{1,0:T(8,128)(2,1)S(1)}, bf16[96,1024]{1,0:T(8,128)(2,1)}, u32[]{:S(2)}) copy-start(bf16[96,1024]{1,0:T(8,128)(2,1)} %get-tuple-element.53) | copy-start | bytes 589828
  19.0 14.7 %collective-permute-start.4 = (bf16[96,1024]{1,0:T(8,128)(2,1)}, bf16[96,1024]{1,0:T(8,128)(2,1)S(1)}, u32[]{:S(2)}, u32[]{:S(2)}) collective-permute-start(bf16[96,1024]{1,0:T(8,128)(2,1)} %get-tuple-element.38), channel_id=1, source_target_pairs={{0,2},{1,3},{2,0},{3,1},{4,6},{5,7},{6,4},{7,5},{8,10},{9,11},{10,... | collective-permute-start | bytes 589832 | tf_op jit(solution)/shard_map/ppermute | solution.py:518
  20.5 13.2 %collective-permute-start.5 = (bf16[96,1024]{1,0:T(8,128)(2,1)}, bf16[96,1024]{1,0:T(8,128)(2,1)S(1)}, u32[]{:S(2)}, u32[]{:S(2)}) collective-permute-start(bf16[96,1024]{1,0:T(8,128)(2,1)} %get-tuple-element.39), channel_id=1, source_target_pairs={{0,4},{1,5},{2,6},{3,7},{4,0},{5,1},{6,2},{7,3},{8,12},{9,13},{10,... | collective-permute-start | bytes 589832 | tf_op jit(solution)/shard_map/ppermute | solution.py:518
  22.0 16.3 %collective-permute-start.3 = (bf16[110,1024]{1,0:T(8,128)(2,1)}, bf16[110,1024]{1,0:T(8,128)(2,1)S(1)}, u32[]{:S(2)}, u32[]{:S(2)}) collective-permute-start(bf16[110,1024]{1,0:T(8,128)(2,1)} %get-tuple-element.36), channel_id=1, source_target_pairs={{0,8},{1,9},{2,10},{3,11},{4,12},{5,13},{6,14},{7,15},{8,0},{9,1},... | collective-permute-start | bytes 675848 | tf_op jit(solution)/shard_map/ppermute | solution.py:539
  22.5 26.7 %copy-start.5 = (s32[16,1,330]{2,1,0:T(1,128)}, s32[16,1,330]{2,1,0:T(1,128)S(1)}, u32[]{:S(2)}) copy-start(s32[16,1,330]{2,1,0:T(1,128)S(1)} %all-to-all-done.refs_0_.refs_1_) | copy-start | bytes 63364
  33.7 15.6 %copy-start.3 = (bf16[144,1024]{1,0:T(8,128)(2,1)}, bf16[144,1024]{1,0:T(8,128)(2,1)S(1)}, u32[]{:S(2)}) copy-start(bf16[144,1024]{1,0:T(8,128)(2,1)S(1)} %collective-permute-done.1.refs_2_) | copy-start | bytes 884740
  33.7 23.4 %copy-start.13 = (bf16[96,1024]{1,0:T(8,128)(2,1)}, bf16[96,1024]{1,0:T(8,128)(2,1)S(1)}, u32[]{:S(2)}) copy-start(bf16[96,1024]{1,0:T(8,128)(2,1)S(1)} %collective-permute-done.4.rest_1_) | copy-start | bytes 589828
  33.7 23.4 %copy-start.14 = (bf16[96,1024]{1,0:T(8,128)(2,1)}, bf16[96,1024]{1,0:T(8,128)(2,1)S(1)}, u32[]{:S(2)}) copy-start(bf16[96,1024]{1,0:T(8,128)(2,1)S(1)} %collective-permute-done.5.rest_2_) | copy-start | bytes 589828
  38.2 11.0 %copy-start.7 = (bf16[110,1024]{1,0:T(8,128)(2,1)}, bf16[110,1024]{1,0:T(8,128)(2,1)S(1)}, u32[]{:S(2)}) copy-start(bf16[110,1024]{1,0:T(8,128)(2,1)S(1)} %collective-permute-done.3.refs_3_) | copy-start | bytes 675844
  38.2 24.7 %all-to-all-start.1 = ((bf16[16,24,1024]{2,1,0:T(8,128)(2,1)}), bf16[16,24,1024]{2,1,0:T(8,128)(2,1)S(1)}, u32[]{:S(2)}, u32[]{:S(2)}) async-start(bf16[16,24,1024]{2,1,0:T(8,128)(2,1)} %bitcast.4), calls=%async_computation.1 | async-start | bytes 1572864 | tf_op jit(solution)/shard_map/all_to_all | solution.py:550
  43.8 5.5 %collective-permute-start.7 = (bf16[144,1024]{1,0:T(8,128)(2,1)S(1)}, bf16[144,1024]{1,0:T(8,128)(2,1)S(1)}, u32[]{:S(2)}, u32[]{:S(2)}) collective-permute-start(bf16[144,1024]{1,0:T(8,128)(2,1)S(1)} %collective-permute-done.1.refs_2_), channel_id=1, source_target_pairs={{0,1},{1,0},{2,3},{3,2},{4,5},{5,4},{6,7},{7,6},{8,9},{9,8},{10,11... | collective-permute-start | bytes 884744 | tf_op jit(solution)/shard_map/ppermute | solution.py:555
  44.2 5.1 %collective-permute-start.8 = (bf16[110,1024]{1,0:T(8,128)(2,1)S(1)}, bf16[110,1024]{1,0:T(8,128)(2,1)S(1)}, u32[]{:S(2)}, u32[]{:S(2)}) collective-permute-start(bf16[110,1024]{1,0:T(8,128)(2,1)S(1)} %collective-permute-done.3.refs_3_), channel_id=1, source_target_pairs={{0,1},{1,0},{2,3},{3,2},{4,5},{5,4},{6,7},{7,6},{8,9},{9,8},{10,11... | collective-permute-start | bytes 675848 | tf_op jit(solution)/shard_map/ppermute | solution.py:555
  44.4 30.1 %collective-permute-start.6 = (bf16[96,1024]{1,0:T(8,128)(2,1)S(1)}, bf16[96,1024]{1,0:T(8,128)(2,1)S(1)}, u32[]{:S(2)}, u32[]{:S(2)}) collective-permute-start(bf16[96,1024]{1,0:T(8,128)(2,1)S(1)} %copy-done.16), channel_id=1, source_target_pairs={{0,6},{1,7},{2,4},{3,5},{4,2},{5,3},{6,0},{7,1},{8,14},{9,15},{10,... | collective-permute-start | bytes 589832 | tf_op jit(solution)/shard_map/ppermute | solution.py:518
  49.2 0.7 copy-start.8
  49.9 0.7 copy-start.4
  53.5 21.0 %collective-permute-start.9 = (bf16[96,1024]{1,0:T(8,128)(2,1)}, bf16[96,1024]{1,0:T(8,128)(2,1)S(1)}, u32[]{:S(2)}, u32[]{:S(2)}) collective-permute-start(bf16[96,1024]{1,0:T(8,128)(2,1)} %get-tuple-element.57), channel_id=1, source_target_pairs={{0,2},{1,3},{2,0},{3,1},{4,6},{5,7},{6,4},{7,5},{8,10},{9,11},{10,... | collective-permute-start | bytes 589832 | tf_op jit(solution)/shard_map/ppermute | solution.py:518
  54.1 20.3 %collective-permute-start.10 = (bf16[96,1024]{1,0:T(8,128)(2,1)}, bf16[96,1024]{1,0:T(8,128)(2,1)S(1)}, u32[]{:S(2)}, u32[]{:S(2)}) collective-permute-start(bf16[96,1024]{1,0:T(8,128)(2,1)} %get-tuple-element.58), channel_id=1, source_target_pairs={{0,4},{1,5},{2,6},{3,7},{4,0},{5,1},{6,2},{7,3},{8,12},{9,13},{10,... | collective-permute-start | bytes 589832 | tf_op jit(solution)/shard_map/ppermute | solution.py:518
  54.3 20.2 %collective-permute-start.11 = (bf16[96,1024]{1,0:T(8,128)(2,1)}, bf16[96,1024]{1,0:T(8,128)(2,1)S(1)}, u32[]{:S(2)}, u32[]{:S(2)}) collective-permute-start(bf16[96,1024]{1,0:T(8,128)(2,1)} %get-tuple-element.59), channel_id=1, source_target_pairs={{0,6},{1,7},{2,4},{3,5},{4,2},{5,3},{6,0},{7,1},{8,14},{9,15},{10,... | collective-permute-start | bytes 589832 | tf_op jit(solution)/shard_map/ppermute | solution.py:518
  62.9 0.9 %copy-start.1 = (bf16[16,24,1024]{2,1,0:T(8,128)(2,1)}, bf16[16,24,1024]{2,1,0:T(8,128)(2,1)S(1)}, u32[]{:S(2)}) copy-start(bf16[16,24,1024]{2,1,0:T(8,128)(2,1)S(1)} %all-to-all-done.1) | copy-start | bytes 2359300
  68.7 12.5 %all-to-all-start.2 = ((bf16[16,2,1024]{2,1,0:T(2,128)(2,1)}), bf16[16,2,1024]{2,1,0:T(2,128)(2,1)S(1)}, u32[]{:S(2)}, u32[]{:S(2)}) async-start(bf16[16,2,1024]{2,1,0:T(2,128)(2,1)} %get-tuple-element.50), calls=%async_computation.2 | async-start | bytes 131072 | tf_op jit(solution)/shard_map/all_to_all | solution.py:583
  74.4 6.9 %copy-start.9 = (bf16[96,1024]{1,0:T(8,128)(2,1)}, bf16[96,1024]{1,0:T(8,128)(2,1)S(1)}, u32[]{:S(2)}) copy-start(bf16[96,1024]{1,0:T(8,128)(2,1)S(1)} %collective-permute-done.6.rest_0_) | copy-start | bytes 589828
  74.4 6.9 %copy-start.10 = (bf16[96,1024]{1,0:T(8,128)(2,1)}, bf16[96,1024]{1,0:T(8,128)(2,1)S(1)}, u32[]{:S(2)}) copy-start(bf16[96,1024]{1,0:T(8,128)(2,1)S(1)} %collective-permute-done.9.rest_2_) | copy-start | bytes 589828
  74.5 6.9 %copy-start.11 = (bf16[96,1024]{1,0:T(8,128)(2,1)}, bf16[96,1024]{1,0:T(8,128)(2,1)S(1)}, u32[]{:S(2)}) copy-start(bf16[96,1024]{1,0:T(8,128)(2,1)S(1)} %collective-permute-done.10.rest_3_) | copy-start | bytes 589828
  74.5 6.8 %copy-start.12 = (bf16[96,1024]{1,0:T(8,128)(2,1)}, bf16[96,1024]{1,0:T(8,128)(2,1)S(1)}, u32[]{:S(2)}) copy-start(bf16[96,1024]{1,0:T(8,128)(2,1)S(1)} %collective-permute-done.11.rest_4_) | copy-start | bytes 589828
  81.3 0.6 copy-start.6

commit v16 on v15

--- a/solution.py
+++ b/solution.py
@@ -144,22 +144,41 @@
     return max(1, (count - 1).bit_length())
 
 
+def ranks(kind):
+    count = kind.shape[1]
+    at = lax.broadcasted_iota(jnp.int32, (count, count), 0)
+    by = lax.broadcasted_iota(jnp.int32, (count, count), 1)
+    across = jnp.broadcast_to(kind, (count, count))
+    down = jnp.sum(jnp.where(at == by, across, 0), axis=1, keepdims=True)
+    same = down == across
+    rank_row = jnp.sum(jnp.where(same & (at < by), 1, 0), axis=0, keepdims=True)
+    rank_col = jnp.sum(jnp.where(same & (by < at), 1, 0), axis=1, keepdims=True)
+    return down, rank_row, rank_col
+
+
 def route_kernel(
     sizes,
     token_ids_far,
     owners_far,
     row_slot_far,
+    sibling_far,
     plan,
     token_slot_far,
     code,
+    sibling_code,
     *near,
 ):
     peers, vocab_rows, token_cap, row_cap, pooled = sizes
-    token_ids, owners, row_slot, token_slot, arrived = near
+    token_ids, owners, row_slot, sibling, token_slot, arrived = near
     copies = [
         pltpu.make_async_copy(source, target, arrived.at[at])
         for at, (source, target) in enumerate(
-            ((token_ids_far, token_ids), (owners_far, owners), (row_slot_far, row_slot))
+            (
+                (token_ids_far, token_ids),
+                (owners_far, owners),
+                (row_slot_far, row_slot),
+                (sibling_far, sibling),
+            )
         )
     ]
     for copy in copies:
@@ -174,15 +193,10 @@
     values = jnp.concatenate([ids - holder * vocab_rows, row_slot[...]], axis=1)
 
     kind = jnp.concatenate([holder, owners[...] + peers], axis=1)
-    at = lax.broadcasted_iota(jnp.int32, (count, count), 0)
-    by = lax.broadcasted_iota(jnp.int32, (count, count), 1)
-    across = jnp.broadcast_to(kind, (count, count))
-    down = jnp.sum(jnp.where(at == by, across, 0), axis=1, keepdims=True)
-    same = down == across
-    rank_row = jnp.sum(jnp.where(same & (at < by), 1, 0), axis=0, keepdims=True)
-    rank_col = jnp.sum(jnp.where(same & (by < at), 1, 0), axis=1, keepdims=True)
+    down, rank_row, rank_col = ranks(kind)
 
     code[...] = owners[...] * 2 ** rank_bits(rows) + rank_row[:, tokens:]
+    sibling_code[...] = sibling[...] * 2 ** rank_bits(rows) + ranks(sibling[...])[1]
     goal = jnp.concatenate([holder, owners[...]], axis=1)
     peer = lax.broadcasted_iota(jnp.int32, (peers, count), 0)
     left = jnp.where(peer == goal, values + 1, 0).astype(jnp.float32)
@@ -201,12 +215,12 @@
         plan[p, :, :rows] = code[...]
         plan[p, :, rows:] = filled[p : p + 1]
     token_slot[...] = down[:tokens] * token_cap + rank_col[:tokens]
-    send = pltpu.make_async_copy(token_slot, token_slot_far, arrived.at[3])
+    send = pltpu.make_async_copy(token_slot, token_slot_far, arrived.at[4])
     send.start()
     send.wait()
 
 
-def route(token_ids, owners, row_slot, sizes):
+def route(token_ids, owners, row_slot, sibling_owners, sizes):
     peers, _, token_cap, row_cap, pooled = sizes
     passes, seq_len = token_ids.shape
     rows = owners.shape[1]
@@ -217,23 +231,26 @@
             ints(peers, 1, rows + token_cap + row_cap + pooled),
             ints(passes * seq_len, 1),
             ints(1, rows),
-        ],
-        in_specs=[pl.BlockSpec(memory_space=pltpu.HBM)] * 3,
+            ints(1, rows),
+        ],
+        in_specs=[pl.BlockSpec(memory_space=pltpu.HBM)] * 4,
         out_specs=[
             pl.BlockSpec(memory_space=pltpu.VMEM),
             pl.BlockSpec(memory_space=pltpu.HBM),
             pl.BlockSpec(memory_space=pltpu.VMEM),
+            pl.BlockSpec(memory_space=pltpu.VMEM),
         ],
         scratch_shapes=[
             pltpu.VMEM(token_ids.shape, jnp.int32),
             pltpu.VMEM(owners.shape, jnp.int32),
             pltpu.VMEM(row_slot.shape, jnp.int32),
+            pltpu.VMEM(owners.shape, jnp.int32),
             pltpu.VMEM((passes * seq_len, 1), jnp.int32),
-            pltpu.SemaphoreType.DMA((4,)),
+            pltpu.SemaphoreType.DMA((5,)),
         ],
         compiler_params=pltpu.CompilerParams(vmem_limit_bytes=60 * 1024 * 1024),
         name="route",
-    )(token_ids, owners, row_slot)
+    )(token_ids, owners, row_slot, sibling_owners)
 
 
 def pack_kernel(half, row_cap, count, picks, pieces, rest, *refs):
@@ -518,12 +535,15 @@
             got.append(lax.ppermute(blocks[step], "dp", moves))
         return got
 
-    ahead = store_count * 5 // 8 // 16 * 16
+    ahead = store_count * 2 // 3 // 16 * 16
     sibling_rows = lax.ppermute(stored_rows, "dp", beside)
     first_rows = lax.ppermute(stored_rows[:ahead], "dp", across)
     sizes = (peer_count, vocab_rows, token_cap, row_cap, row_count - store_count)
-    plan, token_slot, code = route(token_ids, row_owner.reshape(1, row_count), row_slot[None], sizes)
-    sibling_code = lax.ppermute(code, "dp", beside)
+    owners = row_owner.reshape(1, row_count)
+    sibling_owners = lax.ppermute(owners, "dp", beside)
+    plan, token_slot, code, sibling_code = route(
+        token_ids, owners, row_slot[None], sibling_owners, sizes
+    )
     plan, sibling_rows = lax.optimization_barrier((plan, sibling_rows))
     codes = lax.all_to_all(plan, "dp", split_axis=0, concat_axis=0, tiled=True)
     *blocks, last_rows = pack_rows(
@@ -544,8 +564,8 @@
     found = jnp.dot(
         chosen.astype(jnp.bfloat16), word_table, preferred_element_type=jnp.float32
     ).astype(jnp.bfloat16)
-    found, first_rows, last_rows, own_half[:3] = lax.optimization_barrier(
-        (found, first_rows, last_rows, own_half[:3])
+    found, first_rows, last_rows, own_half[:2] = lax.optimization_barrier(
+        (found, first_rows, last_rows, own_half[:2])
     )
     fetched = lax.all_to_all(
         found.reshape(peer_count, token_cap, width), "dp", split_axis=0, concat_axis=0, tiled=True
@@ -560,7 +580,7 @@
     got_places = plan[:, token_cap : token_cap + row_cap][sources].reshape(half, 2 * row_cap)
     spare = padded(2 * row_cap) - 2 * row_cap
     got_places = jnp.pad(got_places, ((0, 0), (0, spare)), constant_values=-1).reshape(1, -1)
-    means, share = early_update(got_places, centroids, own_half[:3])
+    means, share = early_update(got_places, centroids, own_half[:2])
     late_places = plan[:, token_cap + row_cap :].reshape(1, -1)
     fetched, means, share, got_places, late_places = lax.optimization_barrier(
         (fetched, means, share, got_places, late_places)
@@ -583,7 +603,7 @@
     all_embeds = lax.all_to_all(
         spread, "dp", split_axis=0, concat_axis=0, tiled=True
     )
-    pieces = own_half[3:] + other_half
+    pieces = own_half[2:] + other_half
     new_centroids = late_update(got_places, late_places, all_embeds, share, means, pieces)
     return (passage_embed, new_centroids)
 

time: 86.1 us -> 78.3 us (0.909)
  waiting for transfers between devices: 24.7 us -> 17.7 us
  starting transfers between devices: 32.1 us -> 31.2 us
    ppermute x1, waiting for transfers between devices: 9.73 us -> 0.01 us  [shards(): first_rows = lax.ppermute(stored_rows[:ahead], 'dp', across)]
    all_to_all x1, waiting for transfers between devices: 6.81 us -> 3.56 us  [shards(): lax.all_to_all(spread, 'dp', split_axis=0, concat_axis=0, tiled=True)]
    ppermute x6, waiting for transfers between devices: 0.02 us -> 3.26 us  [hand_on(): got.append(lax.ppermute(blocks[step], 'dp', moves))]
    all_to_all x1, starting transfers between devices: 7.06 us -> 3.92 us  [shards(): codes = lax.all_to_all(plan, 'dp', split_axis=0, concat_axis=0, tiled=True)]
    ppermute x1, starting transfers between devices: 0.56 us -> 2.89 us  [shards(): last_rows = lax.ppermute(last_rows, 'dp', across)]
    all_to_all x1, waiting for transfers between devices: 0.01 us -> 1.9 us  [shards(): codes = lax.all_to_all(plan, 'dp', split_axis=0, concat_axis=0, tiled=True)]
    ppermute x1, waiting for transfers between devices: 4.55 us -> 5.77 us  [shards(): last_rows = lax.ppermute(last_rows, 'dp', across)]
    ppermute x6, starting transfers between devices: 9.37 us -> 8.4 us  [hand_on(): got.append(lax.ppermute(blocks[step], 'dp', moves))]
  transfers between devices with their start and end apart: 15 -> 15, of which waited for: 5 -> 6; matrix products, arithmetic and copies ran while one was open for 5% -> 6% of each run, Pallas kernels for 19% -> 21%
where the time goes in v16:
time: 78.3 us; the launch traced here: 77.8 us
  starting transfers between devices  31.2 us (40%)
  Pallas kernels  20.1 us (26%)
  waiting for transfers between devices  17.7 us (23%)
  local copies, waits for them, and re-layouts  6.52 us (8%)
  matrix products  1.29 us (2%)
  between operations  0.9 us (1%)
    ppermute x6, starting transfers between devices, hand_on(): got.append(lax.ppermute(blocks[step], 'dp', moves))  8.4 us
    all_to_all x1, starting transfers between devices, shards(): lax.all_to_all(found.reshape(peer_count, token_cap, width), 'dp', split_a...  5.84 us
    ppermute x1, waiting for transfers between devices, shards(): last_rows = lax.ppermute(last_rows, 'dp', across)  5.77 us
    pallas_call x2, Pallas kernels, pack_rows(): pl.pallas_call(functools.partial(pack_kernel, half, row_cap, count, picks...  5.51 us
    all_to_all x1, starting transfers between devices, shards(): lax.all_to_all(spread, 'dp', split_axis=0, concat_axis=0, tiled=True)  5.2 us
    pallas_call x1, Pallas kernels, encode(): pl.pallas_call(encode_kernel, out_shape=[jax.ShapeDtypeStruct((passes, wi...  4.97 us
    pallas_call x1, Pallas kernels, late_update(): pl.pallas_call(late_kernel, out_shape=jax.ShapeDtypeStruct(early.shape, j...  4.01 us
    all_to_all x1, starting transfers between devices, shards(): codes = lax.all_to_all(plan, 'dp', split_axis=0, concat_axis=0, tiled=True)  3.92 us
  transfers between devices with their start and end apart: 15, of which 6 were waited for; matrix products, arithmetic and copies ran while one was open for 6% of the time, Pallas kernels for 21%

profile of v16, /device:TPU:0, one launch (start us, length us, event | category | flops | bytes accessed | tf_op | source)
XLA Modules:
  0.0 77.8 jit_solution(17240717609683404303)
XLA Ops:
  0.6 0.0 copy-start
  0.6 0.5 collective-permute-start.1
  1.2 1.0 %slice.17 = bf16[160,1024]{1,0:T(8,128)(2,1)S(1)} slice(bf16[254,1024]{1,0:T(8,128)(2,1)} %refs_2_.1), slice={[0:160], [0:1024]} | slice | bytes 655360 | tf_op jit(solution)/shard_map/slice | solution.py:540
  2.2 3.7 %collective-permute-start.2 = (bf16[160,1024]{1,0:T(8,128)(2,1)S(1)}, bf16[160,1024]{1,0:T(8,128)(2,1)S(1)}, u32[]{:S(2)}, u32[]{:S(2)}) collective-permute-start(bf16[160,1024]{1,0:T(8,128)(2,1)S(1)} %slice.17), channel_id=1, source_target_pairs={{0,8},{1,9},{2,10},{3,11},{4,12},{5,13},{6,14},{7,15},{8,0},{9,1},... | collective-permute-start | bytes 983048 | tf_op jit(solution)/shard_map/ppermute | solution.py:540
  5.9 0.2 collective-permute-start
  6.0 1.2 %collective-permute-done.sibling_far = s32[1,256]{1,0:T(1,128)S(1)} collective-permute-done((s32[1,256]{1,0:T(1,128)}, s32[1,256]{1,0:T(1,128)S(1)}, u32[]{:S(2)}, u32[]{:S(2)}) %collective-permute-start) | collective-permute-done | bytes 1056 | tf_op jit(solution)/shard_map/ppermute | solution.py:543
  7.2 0.6 copy-done.15
  7.8 2.3 %route.1 = (s32[16,1,330]{2,1,0:T(1,128)}, s32[128,1]{1,0:T(8,128)}, s32[1,256]{1,0:T(1,128)}, s32[1,256]{1,0:T(1,128)}) custom-call(s32[2,64]{1,0:T(2,128)} %token_ids_far.1, s32[1,256]{1,0:T(1,128)} %bitcast.25, s32[1,256]{1,0:T(1,128)} %bitcast.26, s32[1,256]{1,0:T(1,128)} %copy-done.15), custom_call_target="tpu_custom_call" | custom-call | tf_op jit(solution)/shard_map/route/pallas_call | solution.py:228
  10.1 0.0 collective-permute-done.1.refs_3_
  10.1 0.0 copy-start.2
  10.1 3.9 %all-to-all-start = ((s32[16,1,330]{2,1,0:T(1,128)}), s32[16,1,330]{2,1,0:T(1,128)S(1)}, u32[]{:S(2)}, u32[]{:S(2)}) async-start(s32[16,1,330]{2,1,0:T(1,128)} %get-tuple-element.33), calls=%async_computation | async-start | bytes 49152 | tf_op jit(solution)/shard_map/all_to_all | solution.py:548
  14.1 0.0 copy-done.2
  14.1 2.7 %pack.2 = (bf16[96,1024]{1,0:T(8,128)(2,1)}, bf16[96,1024]{1,0:T(8,128)(2,1)}, bf16[96,1024]{1,0:T(8,128)(2,1)}, bf16[96,1024]{1,0:T(8,128)(2,1)}, bf16[94,1024]{1,0:T(8,128)(2,1)}) custom-call(s32[1,256]{1,0:T(1,128)} %get-tuple-element.34.refs_0_, s32[1,256]{1,0:T(1,128)} %get-tuple-element.35.refs_1_, bf16[254,1024]{1,0:T(8,128)(2,1)} %refs_2_.1, ...), custom_call_target="tpu_custom_call" | custom-call | flops 199753728 | bytes 1826816 | tf_op jit(solution)/shard_map/pack/pallas_call | solution.py:319
  16.8 0.0 copy-start.17
  16.8 0.0 copy-start.16
  16.8 2.9 %collective-permute-start.3 = (bf16[94,1024]{1,0:T(8,128)(2,1)}, bf16[94,1024]{1,0:T(8,128)(2,1)S(1)}, u32[]{:S(2)}, u32[]{:S(2)}) collective-permute-start(bf16[94,1024]{1,0:T(8,128)(2,1)} %get-tuple-element.37), channel_id=1, source_target_pairs={{0,8},{1,9},{2,10},{3,11},{4,12},{5,13},{6,14},{7,15},{8,0},{9,1},... | collective-permute-start | bytes 577544 | tf_op jit(solution)/shard_map/ppermute | solution.py:559
  19.7 1.5 %collective-permute-start.4 = (bf16[96,1024]{1,0:T(8,128)(2,1)}, bf16[96,1024]{1,0:T(8,128)(2,1)S(1)}, u32[]{:S(2)}, u32[]{:S(2)}) collective-permute-start(bf16[96,1024]{1,0:T(8,128)(2,1)} %get-tuple-element.39), channel_id=1, source_target_pairs={{0,2},{1,3},{2,0},{3,1},{4,6},{5,7},{6,4},{7,5},{8,10},{9,11},{10,... | collective-permute-start | bytes 589832 | tf_op jit(solution)/shard_map/ppermute | solution.py:535
  21.1 1.9 %all-to-all-done.refs_0_.refs_1_ = s32[16,1,330]{2,1,0:T(1,128)S(1)} async-done(((s32[16,1,330]{2,1,0:T(1,128)}), s32[16,1,330]{2,1,0:T(1,128)S(1)}, u32[]{:S(2)}, u32[]{:S(2)}) %all-to-all-start) | async-done | bytes 21152 | tf_op jit(solution)/shard_map/all_to_all | solution.py:548
  23.0 0.1 eq.15
  23.1 0.0 copy-done
  23.1 1.3 %convolution_convert_fusion = bf16[384,1024]{1,0:T(8,128)(2,1)} fusion(bf16[240,1024]{1,0:T(8,128)(2,1)S(1)} %copy-done, s32[384]{0:T(512)S(1)} %eq.15), kind=kOutput, calls=%fused_computation.1 | convolution fusion | flops 189229056 | bytes 1279488 | tf_op jit(solution)/shard_map/dot_general | solution.py:564
  24.4 0.0 collective-permute-done.2.refs_2_
  24.4 5.8 %collective-permute-done.3.refs_3_ = bf16[94,1024]{1,0:T(8,128)(2,1)S(1)} collective-permute-done((bf16[94,1024]{1,0:T(8,128)(2,1)}, bf16[94,1024]{1,0:T(8,128)(2,1)S(1)}, u32[]{:S(2)}, u32[]{:S(2)}) %collective-permute-start.3) | collective-permute-done | bytes 192544 | tf_op jit(solution)/shard_map/ppermute | solution.py:559
  30.2 0.0 collective-permute-done.4.rest_1_
  30.2 5.8 %all-to-all-start.1 = ((bf16[16,24,1024]{2,1,0:T(8,128)(2,1)}), bf16[16,24,1024]{2,1,0:T(8,128)(2,1)S(1)}, u32[]{:S(2)}, u32[]{:S(2)}) async-start(bf16[16,24,1024]{2,1,0:T(8,128)(2,1)} %bitcast.4), calls=%async_computation.1 | async-start | bytes 1572864 | tf_op jit(solution)/shard_map/all_to_all | solution.py:570
  36.1 0.4 collective-permute-start.7
  36.5 0.2 collective-permute-start.8
  36.7 0.0 copy-done.17
  36.7 1.9 %collective-permute-start.5 = (bf16[96,1024]{1,0:T(8,128)(2,1)S(1)}, bf16[96,1024]{1,0:T(8,128)(2,1)S(1)}, u32[]{:S(2)}, u32[]{:S(2)}) collective-permute-start(bf16[96,1024]{1,0:T(8,128)(2,1)S(1)} %copy-done.17), channel_id=1, source_target_pairs={{0,4},{1,5},{2,6},{3,7},{4,0},{5,1},{6,2},{7,3},{8,12},{9,13},{10,... | collective-permute-start | bytes 589832 | tf_op jit(solution)/shard_map/ppermute | solution.py:535
  38.6 0.0 copy-done.16
  38.6 1.5 %collective-permute-start.6 = (bf16[96,1024]{1,0:T(8,128)(2,1)S(1)}, bf16[96,1024]{1,0:T(8,128)(2,1)S(1)}, u32[]{:S(2)}, u32[]{:S(2)}) collective-permute-start(bf16[96,1024]{1,0:T(8,128)(2,1)S(1)} %copy-done.16), channel_id=1, source_target_pairs={{0,6},{1,7},{2,4},{3,5},{4,2},{5,3},{6,0},{7,1},{8,14},{9,15},{10,... | collective-permute-start | bytes 589832 | tf_op jit(solution)/shard_map/ppermute | solution.py:535
  40.1 0.1 slice.25
  40.1 0.1 slice.24
  40.2 0.6 reshape.42.late_far
  40.8 0.6 gather_fusion
  41.4 0.7 reshape.41.places_far
  42.0 0.0 collective-permute-done.8.refs_5_
  42.0 0.0 collective-permute-done.7.refs_4_
  42.0 0.0 copy-done.5
  42.1 0.0 copy-done.3
  42.1 0.0 copy-done.12
  42.1 0.6 copy-done.13
  42.7 0.7 copy-done.4
  43.4 2.8 %pack.3 = (bf16[96,1024]{1,0:T(8,128)(2,1)}, bf16[96,1024]{1,0:T(8,128)(2,1)}, bf16[96,1024]{1,0:T(8,128)(2,1)}, bf16[96,1024]{1,0:T(8,128)(2,1)}) custom-call(s32[16,1,330]{2,1,0:T(1,128)} %copy-done.5, s32[16,1,330]{2,1,0:T(1,128)} %copy-done.5, bf16[160,1024]{1,0:T(8,128)(2,1)} %copy-done.3, bf16[94,1024]{1,0:T(8,128)(2,1)} %copy-done.12, ...), custom_call_target="tpu_custom_call" | custom-call | flops 199753728 | bytes 1826816 | tf_op jit(solution)/shard_map/pack/pallas_call | solution.py:319
  46.3 0.2 collective-permute-start.9
  46.5 1.9 %collective-permute-start.10 = (bf16[96,1024]{1,0:T(8,128)(2,1)}, bf16[96,1024]{1,0:T(8,128)(2,1)S(1)}, u32[]{:S(2)}, u32[]{:S(2)}) collective-permute-start(bf16[96,1024]{1,0:T(8,128)(2,1)} %get-tuple-element.58), channel_id=1, source_target_pairs={{0,4},{1,5},{2,6},{3,7},{4,0},{5,1},{6,2},{7,3},{8,12},{9,13},{10,... | collective-permute-start | bytes 589832 | tf_op jit(solution)/shard_map/ppermute | solution.py:535
  48.4 1.5 %collective-permute-start.11 = (bf16[96,1024]{1,0:T(8,128)(2,1)}, bf16[96,1024]{1,0:T(8,128)(2,1)S(1)}, u32[]{:S(2)}, u32[]{:S(2)}) collective-permute-start(bf16[96,1024]{1,0:T(8,128)(2,1)} %get-tuple-element.59), channel_id=1, source_target_pairs={{0,6},{1,7},{2,4},{3,5},{4,2},{5,3},{6,0},{7,1},{8,14},{9,15},{10,... | collective-permute-start | bytes 589832 | tf_op jit(solution)/shard_map/ppermute | solution.py:535
  49.9 3.3 %early.1 = (f32[512,1024]{1,0:T(8,128)}, f32[512,128]{1,0:T(8,128)}) custom-call(s32[1,768]{1,0:T(1,128)} %reshape.41.places_far, f32[512,1024]{1,0:T(8,128)} %centroids_far.1, bf16[96,1024]{1,0:T(8,128)(2,1)} %get-tuple-element.41.rest_0_, bf16[96,1024]{1,0:T(8,128)(2,1)} %copy-done.14), custom_call_target="tpu_custom_call" | custom-call | flops 201326592 | bytes 4194304 | tf_op jit(solution)/shard_map/early/pallas_call | solution.py:442
  53.2 2.1 %all-to-all-done.1 = bf16[16,24,1024]{2,1,0:T(8,128)(2,1)S(1)} async-done(((bf16[16,24,1024]{2,1,0:T(8,128)(2,1)}), bf16[16,24,1024]{2,1,0:T(8,128)(2,1)S(1)}, u32[]{:S(2)}, u32[]{:S(2)}) %all-to-all-start.1) | async-done | bytes 786464 | tf_op jit(solution)/shard_map/all_to_all | solution.py:570
  55.2 0.9 %copy-done.1 = bf16[16,24,1024]{2,1,0:T(8,128)(2,1)} copy-done((bf16[16,24,1024]{2,1,0:T(8,128)(2,1)}, bf16[16,24,1024]{2,1,0:T(8,128)(2,1)S(1)}, u32[]{:S(2)}) %copy-start.1) | copy-done | bytes 786456
  56.1 5.0 %encode.1 = (bf16[2,1024]{1,0:T(2,128)(2,1)}, bf16[16,2,1024]{2,1,0:T(2,128)(2,1)}) custom-call(s32[1,2]{1,0:T(1,128)} %bitcast.27, s32[128,1]{1,0:T(8,128)} %get-tuple-element.31.refs_1_, bf16[384,1024]{1,0:T(8,128)(2,1)} %bitcast.15, bf16[64,1024]{1,0:T(8,128)(2,1)} %refs_3_.1, f32[1,1024]{1,0:T(1,128)} %bitcast.19, f32[1,1024]{1,0:T(1,128)} %bitcast.20, ...), custom_call_target="tpu_custom_call" | custom-call | flops 637534208 | bytes 6291456 | tf_op jit(solution)/shard_map/encode/pallas_call | solution.py:121
  61.1 5.2 %all-to-all-start.2 = ((bf16[16,2,1024]{2,1,0:T(2,128)(2,1)}), bf16[16,2,1024]{2,1,0:T(2,128)(2,1)S(1)}, u32[]{:S(2)}, u32[]{:S(2)}) async-start(bf16[16,2,1024]{2,1,0:T(2,128)(2,1)} %get-tuple-element.49), calls=%async_computation.2 | async-start | bytes 131072 | tf_op jit(solution)/shard_map/all_to_all | solution.py:603
  66.3 0.0 collective-permute-done.5.rest_0_
  66.3 0.0 collective-permute-done.6.rest_1_
  66.3 0.0 collective-permute-done.9.rest_3_
  66.3 0.0 copy-start.9
  66.3 0.0 collective-permute-done.10.rest_4_
  66.4 3.2 %collective-permute-done.11.rest_5_ = bf16[96,1024]{1,0:T(8,128)(2,1)S(1)} collective-permute-done((bf16[96,1024]{1,0:T(8,128)(2,1)}, bf16[96,1024]{1,0:T(8,128)(2,1)S(1)}, u32[]{:S(2)}, u32[]{:S(2)}) %collective-permute-start.11) | collective-permute-done | bytes 196640 | tf_op jit(solution)/shard_map/ppermute | solution.py:535
  69.6 3.6 %all-to-all-done.2.spread_far = bf16[16,2,1024]{2,1,0:T(2,128)(2,1)S(1)} async-done(((bf16[16,2,1024]{2,1,0:T(2,128)(2,1)}), bf16[16,2,1024]{2,1,0:T(2,128)(2,1)S(1)}, u32[]{:S(2)}, u32[]{:S(2)}) %all-to-all-start.2) | async-done | bytes 65568 | tf_op jit(solution)/shard_map/all_to_all | solution.py:603
  73.2 0.0 copy-done.8
  73.2 0.0 copy-done.10
  73.2 0.0 copy-done.11
  73.2 0.6 copy-done.6
  73.8 4.0 %late.1 = f32[512,1024]{1,0:T(8,128)} custom-call(s32[1,768]{1,0:T(1,128)} %reshape.41.places_far, s32[1,32]{1,0:T(1,128)} %reshape.42.late_far, bf16[16,2,1024]{2,1,0:T(2,128)(2,1)} %copy-done.6, f32[512,128]{1,0:T(8,128)} %get-tuple-element.50.share_far, f32[512,1024]{1,0:T(8,128)} %get-tuple-element.51.early_far, bf16[96,1024]{1,0:T(8,128)(2,1)} %copy-done.7, ...), custom_call_target="tpu_custom_call" | custom-call | flops 637534208 | bytes 4194304 | tf_op jit(solution)/shard_map/late/pallas_call | solution.py:474
  (19 shorter events, 0.0 us)
Async XLA Ops:
  0.6 22.5 %copy-start = (bf16[240,1024]{1,0:T(8,128)(2,1)S(1)}, bf16[240,1024]{1,0:T(8,128)(2,1)}, u32[]{:S(2)}) copy-start(bf16[240,1024]{1,0:T(8,128)(2,1)} %param.17) | copy-start | bytes 1474564
  0.6 9.5 %collective-permute-start.1 = (bf16[254,1024]{1,0:T(8,128)(2,1)}, bf16[254,1024]{1,0:T(8,128)(2,1)S(1)}, u32[]{:S(2)}, u32[]{:S(2)}) collective-permute-start(bf16[254,1024]{1,0:T(8,128)(2,1)} %refs_2_.1), channel_id=1, source_target_pairs={{0,1},{1,0},{2,3},{3,2},{4,5},{5,4},{6,7},{7,6},{8,9},{9,8},{10,11... | collective-permute-start | bytes 1560584 | tf_op jit(solution)/shard_map/ppermute | solution.py:539
  2.2 22.3 %collective-permute-start.2 = (bf16[160,1024]{1,0:T(8,128)(2,1)S(1)}, bf16[160,1024]{1,0:T(8,128)(2,1)S(1)}, u32[]{:S(2)}, u32[]{:S(2)}) collective-permute-start(bf16[160,1024]{1,0:T(8,128)(2,1)S(1)} %slice.17), channel_id=1, source_target_pairs={{0,8},{1,9},{2,10},{3,11},{4,12},{5,13},{6,14},{7,15},{8,0},{9,1},... | collective-permute-start | bytes 983048 | tf_op jit(solution)/shard_map/ppermute | solution.py:540
  5.9 1.4 %collective-permute-start = (s32[1,256]{1,0:T(1,128)}, s32[1,256]{1,0:T(1,128)S(1)}, u32[]{:S(2)}, u32[]{:S(2)}) collective-permute-start(s32[1,256]{1,0:T(1,128)} %bitcast.24), channel_id=1, source_target_pairs={{0,1},{1,0},{2,3},{3,2},{4,5},{5,4},{6,7},{7,6},{8,9},{9,8},{10,11... | collective-permute-start | bytes 3080 | tf_op jit(solution)/shard_map/ppermute | solution.py:543
  7.2 0.6 copy-start.15
  10.1 3.9 %copy-start.2 = (bf16[254,1024]{1,0:T(8,128)(2,1)}, bf16[254,1024]{1,0:T(8,128)(2,1)S(1)}, u32[]{:S(2)}) copy-start(bf16[254,1024]{1,0:T(8,128)(2,1)S(1)} %collective-permute-done.1.refs_3_) | copy-start | bytes 1560580
  10.1 12.9 %all-to-all-start = ((s32[16,1,330]{2,1,0:T(1,128)}), s32[16,1,330]{2,1,0:T(1,128)S(1)}, u32[]{:S(2)}, u32[]{:S(2)}) async-start(s32[16,1,330]{2,1,0:T(1,128)} %get-tuple-element.33), calls=%async_computation | async-start | bytes 49152 | tf_op jit(solution)/shard_map/all_to_all | solution.py:548
  16.8 19.9 %copy-start.17 = (bf16[96,1024]{1,0:T(8,128)(2,1)S(1)}, bf16[96,1024]{1,0:T(8,128)(2,1)}, u32[]{:S(2)}) copy-start(bf16[96,1024]{1,0:T(8,128)(2,1)} %get-tuple-element.52) | copy-start | bytes 589828
  16.8 21.8 %copy-start.16 = (bf16[96,1024]{1,0:T(8,128)(2,1)S(1)}, bf16[96,1024]{1,0:T(8,128)(2,1)}, u32[]{:S(2)}) copy-start(bf16[96,1024]{1,0:T(8,128)(2,1)} %get-tuple-element.53) | copy-start | bytes 589828
  16.8 13.4 %collective-permute-start.3 = (bf16[94,1024]{1,0:T(8,128)(2,1)}, bf16[94,1024]{1,0:T(8,128)(2,1)S(1)}, u32[]{:S(2)}, u32[]{:S(2)}) collective-permute-start(bf16[94,1024]{1,0:T(8,128)(2,1)} %get-tuple-element.37), channel_id=1, source_target_pairs={{0,8},{1,9},{2,10},{3,11},{4,12},{5,13},{6,14},{7,15},{8,0},{9,1},... | collective-permute-start | bytes 577544 | tf_op jit(solution)/shard_map/ppermute | solution.py:559
  19.7 10.5 %collective-permute-start.4 = (bf16[96,1024]{1,0:T(8,128)(2,1)}, bf16[96,1024]{1,0:T(8,128)(2,1)S(1)}, u32[]{:S(2)}, u32[]{:S(2)}) collective-permute-start(bf16[96,1024]{1,0:T(8,128)(2,1)} %get-tuple-element.39), channel_id=1, source_target_pairs={{0,2},{1,3},{2,0},{3,1},{4,6},{5,7},{6,4},{7,5},{8,10},{9,11},{10,... | collective-permute-start | bytes 589832 | tf_op jit(solution)/shard_map/ppermute | solution.py:535
  23.0 19.0 %copy-start.5 = (s32[16,1,330]{2,1,0:T(1,128)}, s32[16,1,330]{2,1,0:T(1,128)S(1)}, u32[]{:S(2)}) copy-start(s32[16,1,330]{2,1,0:T(1,128)S(1)} %all-to-all-done.refs_0_.refs_1_) | copy-start | bytes 63364
  24.4 17.6 %copy-start.3 = (bf16[160,1024]{1,0:T(8,128)(2,1)}, bf16[160,1024]{1,0:T(8,128)(2,1)S(1)}, u32[]{:S(2)}) copy-start(bf16[160,1024]{1,0:T(8,128)(2,1)S(1)} %collective-permute-done.2.refs_2_) | copy-start | bytes 983044
  30.2 11.9 %copy-start.12 = (bf16[94,1024]{1,0:T(8,128)(2,1)}, bf16[94,1024]{1,0:T(8,128)(2,1)S(1)}, u32[]{:S(2)}) copy-start(bf16[94,1024]{1,0:T(8,128)(2,1)S(1)} %collective-permute-done.3.refs_3_) | copy-start | bytes 577540
  30.2 19.6 %copy-start.14 = (bf16[96,1024]{1,0:T(8,128)(2,1)}, bf16[96,1024]{1,0:T(8,128)(2,1)S(1)}, u32[]{:S(2)}) copy-start(bf16[96,1024]{1,0:T(8,128)(2,1)S(1)} %collective-permute-done.4.rest_1_) | copy-start | bytes 589828
  30.2 25.0 %all-to-all-start.1 = ((bf16[16,24,1024]{2,1,0:T(8,128)(2,1)}), bf16[16,24,1024]{2,1,0:T(8,128)(2,1)S(1)}, u32[]{:S(2)}, u32[]{:S(2)}) async-start(bf16[16,24,1024]{2,1,0:T(8,128)(2,1)} %bitcast.4), calls=%async_computation.1 | async-start | bytes 1572864 | tf_op jit(solution)/shard_map/all_to_all | solution.py:570
  36.1 6.0 %collective-permute-start.7 = (bf16[160,1024]{1,0:T(8,128)(2,1)S(1)}, bf16[160,1024]{1,0:T(8,128)(2,1)S(1)}, u32[]{:S(2)}, u32[]{:S(2)}) collective-permute-start(bf16[160,1024]{1,0:T(8,128)(2,1)S(1)} %collective-permute-done.2.refs_2_), channel_id=1, source_target_pairs={{0,1},{1,0},{2,3},{3,2},{4,5},{5,4},{6,7},{7,6},{8,9},{9,8},{10,11... | collective-permute-start | bytes 983048 | tf_op jit(solution)/shard_map/ppermute | solution.py:575
  36.5 5.6 %collective-permute-start.8 = (bf16[94,1024]{1,0:T(8,128)(2,1)S(1)}, bf16[94,1024]{1,0:T(8,128)(2,1)S(1)}, u32[]{:S(2)}, u32[]{:S(2)}) collective-permute-start(bf16[94,1024]{1,0:T(8,128)(2,1)S(1)} %collective-permute-done.3.refs_3_), channel_id=1, source_target_pairs={{0,1},{1,0},{2,3},{3,2},{4,5},{5,4},{6,7},{7,6},{8,9},{9,8},{10,11... | collective-permute-start | bytes 577544 | tf_op jit(solution)/shard_map/ppermute | solution.py:575
  36.7 29.6 %collective-permute-start.5 = (bf16[96,1024]{1,0:T(8,128)(2,1)S(1)}, bf16[96,1024]{1,0:T(8,128)(2,1)S(1)}, u32[]{:S(2)}, u32[]{:S(2)}) collective-permute-start(bf16[96,1024]{1,0:T(8,128)(2,1)S(1)} %copy-done.17), channel_id=1, source_target_pairs={{0,4},{1,5},{2,6},{3,7},{4,0},{5,1},{6,2},{7,3},{8,12},{9,13},{10,... | collective-permute-start | bytes 589832 | tf_op jit(solution)/shard_map/ppermute | solution.py:535
  38.6 27.7 %collective-permute-start.6 = (bf16[96,1024]{1,0:T(8,128)(2,1)S(1)}, bf16[96,1024]{1,0:T(8,128)(2,1)S(1)}, u32[]{:S(2)}, u32[]{:S(2)}) collective-permute-start(bf16[96,1024]{1,0:T(8,128)(2,1)S(1)} %copy-done.16), channel_id=1, source_target_pairs={{0,6},{1,7},{2,4},{3,5},{4,2},{5,3},{6,0},{7,1},{8,14},{9,15},{10,... | collective-permute-start | bytes 589832 | tf_op jit(solution)/shard_map/ppermute | solution.py:535
  42.0 0.7 copy-start.13
  42.7 0.7 copy-start.4
  46.3 20.0 %collective-permute-start.9 = (bf16[96,1024]{1,0:T(8,128)(2,1)}, bf16[96,1024]{1,0:T(8,128)(2,1)S(1)}, u32[]{:S(2)}, u32[]{:S(2)}) collective-permute-start(bf16[96,1024]{1,0:T(8,128)(2,1)} %get-tuple-element.57), channel_id=1, source_target_pairs={{0,2},{1,3},{2,0},{3,1},{4,6},{5,7},{6,4},{7,5},{8,10},{9,11},{10,... | collective-permute-start | bytes 589832 | tf_op jit(solution)/shard_map/ppermute | solution.py:535
  46.5 19.8 %collective-permute-start.10 = (bf16[96,1024]{1,0:T(8,128)(2,1)}, bf16[96,1024]{1,0:T(8,128)(2,1)S(1)}, u32[]{:S(2)}, u32[]{:S(2)}) collective-permute-start(bf16[96,1024]{1,0:T(8,128)(2,1)} %get-tuple-element.58), channel_id=1, source_target_pairs={{0,4},{1,5},{2,6},{3,7},{4,0},{5,1},{6,2},{7,3},{8,12},{9,13},{10,... | collective-permute-start | bytes 589832 | tf_op jit(solution)/shard_map/ppermute | solution.py:535
  48.4 21.2 %collective-permute-start.11 = (bf16[96,1024]{1,0:T(8,128)(2,1)}, bf16[96,1024]{1,0:T(8,128)(2,1)S(1)}, u32[]{:S(2)}, u32[]{:S(2)}) collective-permute-start(bf16[96,1024]{1,0:T(8,128)(2,1)} %get-tuple-element.59), channel_id=1, source_target_pairs={{0,6},{1,7},{2,4},{3,5},{4,2},{5,3},{6,0},{7,1},{8,14},{9,15},{10,... | collective-permute-start | bytes 589832 | tf_op jit(solution)/shard_map/ppermute | solution.py:535
  55.2 0.9 %copy-start.1 = (bf16[16,24,1024]{2,1,0:T(8,128)(2,1)}, bf16[16,24,1024]{2,1,0:T(8,128)(2,1)S(1)}, u32[]{:S(2)}) copy-start(bf16[16,24,1024]{2,1,0:T(8,128)(2,1)S(1)} %all-to-all-done.1) | copy-start | bytes 2359300
  61.1 12.1 %all-to-all-start.2 = ((bf16[16,2,1024]{2,1,0:T(2,128)(2,1)}), bf16[16,2,1024]{2,1,0:T(2,128)(2,1)S(1)}, u32[]{:S(2)}, u32[]{:S(2)}) async-start(bf16[16,2,1024]{2,1,0:T(2,128)(2,1)} %get-tuple-element.49), calls=%async_computation.2 | async-start | bytes 131072 | tf_op jit(solution)/shard_map/all_to_all | solution.py:603
  66.3 6.9 %copy-start.7 = (bf16[96,1024]{1,0:T(8,128)(2,1)}, bf16[96,1024]{1,0:T(8,128)(2,1)S(1)}, u32[]{:S(2)}) copy-start(bf16[96,1024]{1,0:T(8,128)(2,1)S(1)} %collective-permute-done.5.rest_0_) | copy-start | bytes 589828
  66.3 6.9 %copy-start.8 = (bf16[96,1024]{1,0:T(8,128)(2,1)}, bf16[96,1024]{1,0:T(8,128)(2,1)S(1)}, u32[]{:S(2)}) copy-start(bf16[96,1024]{1,0:T(8,128)(2,1)S(1)} %collective-permute-done.6.rest_1_) | copy-start | bytes 589828
  66.3 6.9 %copy-start.9 = (bf16[96,1024]{1,0:T(8,128)(2,1)}, bf16[96,1024]{1,0:T(8,128)(2,1)S(1)}, u32[]{:S(2)}) copy-start(bf16[96,1024]{1,0:T(8,128)(2,1)S(1)} %collective-permute-done.9.rest_3_) | copy-start | bytes 589828
  66.3 6.8 %copy-start.10 = (bf16[96,1024]{1,0:T(8,128)(2,1)}, bf16[96,1024]{1,0:T(8,128)(2,1)S(1)}, u32[]{:S(2)}) copy-start(bf16[96,1024]{1,0:T(8,128)(2,1)S(1)} %collective-permute-done.10.rest_4_) | copy-start | bytes 589828
  69.6 3.6 %copy-start.11 = (bf16[96,1024]{1,0:T(8,128)(2,1)}, bf16[96,1024]{1,0:T(8,128)(2,1)S(1)}, u32[]{:S(2)}) copy-start(bf16[96,1024]{1,0:T(8,128)(2,1)S(1)} %collective-permute-done.11.rest_5_) | copy-start | bytes 589828
  73.2 0.6 copy-start.6

commit v17 on v16

--- a/solution.py
+++ b/solution.py
@@ -459,7 +459,7 @@
         compiler_params=pltpu.CompilerParams(vmem_limit_bytes=60 * 1024 * 1024),
         cost_estimate=pl.CostEstimate(
             flops=2 * centre_count * width * row_total,
-            bytes_accessed=8 * centre_count * width,
+            bytes_accessed=18 * centre_count * width,
             transcendentals=0,
         ),
         name="early",
@@ -564,8 +564,8 @@
     found = jnp.dot(
         chosen.astype(jnp.bfloat16), word_table, preferred_element_type=jnp.float32
     ).astype(jnp.bfloat16)
-    found, first_rows, last_rows, own_half[:2] = lax.optimization_barrier(
-        (found, first_rows, last_rows, own_half[:2])
+    found, first_rows, own_half[:2] = lax.optimization_barrier(
+        (found, first_rows, own_half[:2])
     )
     fetched = lax.all_to_all(
         found.reshape(peer_count, token_cap, width), "dp", split_axis=0, concat_axis=0, tiled=True

time: 78.3 us -> 97 us (1.24)
  waiting for transfers between devices: 17.7 us -> 38.7 us
  starting transfers between devices: 31.2 us -> 28.9 us
    ppermute x1, waiting for transfers between devices: 5.77 us -> 26.5 us  [shards(): last_rows = lax.ppermute(last_rows, 'dp', across)]
    all_to_all x1, waiting for transfers between devices: 3.56 us -> 6.76 us  [shards(): lax.all_to_all(spread, 'dp', split_axis=0, concat_axis=0, tiled=True)]
    ppermute x6, waiting for transfers between devices: 3.26 us -> 0.25 us  [hand_on(): got.append(lax.ppermute(blocks[step], 'dp', moves))]
    all_to_all x1, waiting for transfers between devices: 1.9 us -> 4.03 us  [shards(): codes = lax.all_to_all(plan, 'dp', split_axis=0, concat_axis=0, tiled=True)]
    all_to_all x1, waiting for transfers between devices: 2.05 us -> 0.01 us  [shards(): lax.all_to_all(found.reshape(peer_count, token_cap, width), 'dp', split_a...]
    all_to_all x1, starting transfers between devices: 5.2 us -> 3.5 us  [shards(): lax.all_to_all(spread, 'dp', split_axis=0, concat_axis=0, tiled=True)]
    unnamed x36 -> x38, local copies, waits for them, and re-layouts: 3.46 us -> 3.48 us
  transfers between devices with their start and end apart: 15 -> 15, of which waited for: 6 -> 5; matrix products, arithmetic and copies ran while one was open for 6% -> 5% of each run, Pallas kernels for 21% -> 17%
where the time goes in v17:
time: 97 us; the launch traced here: 96.5 us
  waiting for transfers between devices  38.7 us (40%)
  starting transfers between devices  28.9 us (30%)
  Pallas kernels  20.1 us (21%)
  local copies, waits for them, and re-layouts  6.61 us (7%)
  matrix products  1.29 us (1%)
  between operations  0.97 us (1%)
    ppermute x1, waiting for transfers between devices, shards(): last_rows = lax.ppermute(last_rows, 'dp', across)  26.5 us
    ppermute x6, starting transfers between devices, hand_on(): got.append(lax.ppermute(blocks[step], 'dp', moves))  8.52 us
    all_to_all x1, waiting for transfers between devices, shards(): lax.all_to_all(spread, 'dp', split_axis=0, concat_axis=0, tiled=True)  6.76 us
    all_to_all x1, starting transfers between devices, shards(): lax.all_to_all(found.reshape(peer_count, token_cap, width), 'dp', split_a...  5.64 us
    pallas_call x2, Pallas kernels, pack_rows(): pl.pallas_call(functools.partial(pack_kernel, half, row_cap, count, picks...  5.48 us
    pallas_call x1, Pallas kernels, encode(): pl.pallas_call(encode_kernel, out_shape=[jax.ShapeDtypeStruct((passes, wi...  4.97 us
    all_to_all x1, waiting for transfers between devices, shards(): codes = lax.all_to_all(plan, 'dp', split_axis=0, concat_axis=0, tiled=True)  4.03 us
    pallas_call x1, Pallas kernels, late_update(): pl.pallas_call(late_kernel, out_shape=jax.ShapeDtypeStruct(early.shape, j...  4.02 us
  transfers between devices with their start and end apart: 15, of which 5 were waited for; matrix products, arithmetic and copies ran while one was open for 5% of the time, Pallas kernels for 17%

profile of v17, /device:TPU:0, one launch (start us, length us, event | category | flops | bytes accessed | tf_op | source)
XLA Modules:
  0.0 96.5 jit_solution(11268712916246420043)
XLA Ops:
  0.6 0.0 copy-start
  0.6 0.5 collective-permute-start.1
  1.2 1.0 %slice.17 = bf16[160,1024]{1,0:T(8,128)(2,1)S(1)} slice(bf16[254,1024]{1,0:T(8,128)(2,1)} %refs_2_.1), slice={[0:160], [0:1024]} | slice | bytes 655360 | tf_op jit(solution)/shard_map/slice | solution.py:540
  2.2 3.7 %collective-permute-start.2 = (bf16[160,1024]{1,0:T(8,128)(2,1)S(1)}, bf16[160,1024]{1,0:T(8,128)(2,1)S(1)}, u32[]{:S(2)}, u32[]{:S(2)}) collective-permute-start(bf16[160,1024]{1,0:T(8,128)(2,1)S(1)} %slice.17), channel_id=1, source_target_pairs={{0,8},{1,9},{2,10},{3,11},{4,12},{5,13},{6,14},{7,15},{8,0},{9,1},... | collective-permute-start | bytes 983048 | tf_op jit(solution)/shard_map/ppermute | solution.py:540
  5.9 0.2 collective-permute-start
  6.0 1.2 %collective-permute-done.sibling_far = s32[1,256]{1,0:T(1,128)S(1)} collective-permute-done((s32[1,256]{1,0:T(1,128)}, s32[1,256]{1,0:T(1,128)S(1)}, u32[]{:S(2)}, u32[]{:S(2)}) %collective-permute-start) | collective-permute-done | bytes 1056 | tf_op jit(solution)/shard_map/ppermute | solution.py:543
  7.2 0.6 copy-done.15
  7.8 2.3 %route.1 = (s32[16,1,330]{2,1,0:T(1,128)}, s32[128,1]{1,0:T(8,128)}, s32[1,256]{1,0:T(1,128)}, s32[1,256]{1,0:T(1,128)}) custom-call(s32[2,64]{1,0:T(2,128)} %token_ids_far.1, s32[1,256]{1,0:T(1,128)} %bitcast.25, s32[1,256]{1,0:T(1,128)} %bitcast.26, s32[1,256]{1,0:T(1,128)} %copy-done.15), custom_call_target="tpu_custom_call" | custom-call | tf_op jit(solution)/shard_map/route/pallas_call | solution.py:228
  10.1 0.0 collective-permute-done.1.refs_3_
  10.1 0.0 copy-start.2
  10.1 3.9 %all-to-all-start = ((s32[16,1,330]{2,1,0:T(1,128)}), s32[16,1,330]{2,1,0:T(1,128)S(1)}, u32[]{:S(2)}, u32[]{:S(2)}) async-start(s32[16,1,330]{2,1,0:T(1,128)} %get-tuple-element.32), calls=%async_computation | async-start | bytes 49152 | tf_op jit(solution)/shard_map/all_to_all | solution.py:548
  14.1 0.0 copy-done.2
  14.1 2.6 %pack.2 = (bf16[96,1024]{1,0:T(8,128)(2,1)}, bf16[96,1024]{1,0:T(8,128)(2,1)}, bf16[96,1024]{1,0:T(8,128)(2,1)}, bf16[96,1024]{1,0:T(8,128)(2,1)}, bf16[94,1024]{1,0:T(8,128)(2,1)}) custom-call(s32[1,256]{1,0:T(1,128)} %get-tuple-element.33.refs_0_, s32[1,256]{1,0:T(1,128)} %get-tuple-element.34.refs_1_, bf16[254,1024]{1,0:T(8,128)(2,1)} %refs_2_.1, ...), custom_call_target="tpu_custom_call" | custom-call | flops 199753728 | bytes 1826816 | tf_op jit(solution)/shard_map/pack/pallas_call | solution.py:319
  16.7 0.0 copy-start.18
  16.7 0.0 copy-start.17
  16.8 0.0 copy-start.16
  16.8 2.0 %collective-permute-start.3 = (bf16[96,1024]{1,0:T(8,128)(2,1)}, bf16[96,1024]{1,0:T(8,128)(2,1)S(1)}, u32[]{:S(2)}, u32[]{:S(2)}) collective-permute-start(bf16[96,1024]{1,0:T(8,128)(2,1)} %get-tuple-element.37), channel_id=1, source_target_pairs={{0,2},{1,3},{2,0},{3,1},{4,6},{5,7},{6,4},{7,5},{8,10},{9,11},{10,... | collective-permute-start | bytes 589832 | tf_op jit(solution)/shard_map/ppermute | solution.py:535
  18.7 4.0 %all-to-all-done.refs_0_.refs_1_ = s32[16,1,330]{2,1,0:T(1,128)S(1)} async-done(((s32[16,1,330]{2,1,0:T(1,128)}), s32[16,1,330]{2,1,0:T(1,128)S(1)}, u32[]{:S(2)}, u32[]{:S(2)}) %all-to-all-start) | async-done | bytes 21152 | tf_op jit(solution)/shard_map/all_to_all | solution.py:548
  22.8 0.1 eq.15
  22.9 0.0 copy-done
  22.9 1.3 %convolution_convert_fusion = bf16[384,1024]{1,0:T(8,128)(2,1)} fusion(bf16[240,1024]{1,0:T(8,128)(2,1)S(1)} %copy-done, s32[384]{0:T(512)S(1)} %eq.15), kind=kOutput, calls=%fused_computation.1 | convolution fusion | flops 189229056 | bytes 1279488 | tf_op jit(solution)/shard_map/dot_general | solution.py:564
  24.2 0.0 collective-permute-done.2.refs_2_
  24.2 0.2 collective-permute-done.3.rest_1_
  24.4 5.6 %all-to-all-start.1 = ((bf16[16,24,1024]{2,1,0:T(8,128)(2,1)}), bf16[16,24,1024]{2,1,0:T(8,128)(2,1)S(1)}, u32[]{:S(2)}, u32[]{:S(2)}) async-start(bf16[16,24,1024]{2,1,0:T(8,128)(2,1)} %bitcast.4), calls=%async_computation.1 | async-start | bytes 1572864 | tf_op jit(solution)/shard_map/all_to_all | solution.py:570
  30.1 0.0 copy-done.18
  30.1 2.9 %collective-permute-start.6 = (bf16[94,1024]{1,0:T(8,128)(2,1)S(1)}, bf16[94,1024]{1,0:T(8,128)(2,1)S(1)}, u32[]{:S(2)}, u32[]{:S(2)}) collective-permute-start(bf16[94,1024]{1,0:T(8,128)(2,1)S(1)} %copy-done.18), channel_id=1, source_target_pairs={{0,8},{1,9},{2,10},{3,11},{4,12},{5,13},{6,14},{7,15},{8,0},{9,1},... | collective-permute-start | bytes 577544 | tf_op jit(solution)/shard_map/ppermute | solution.py:559
  33.0 0.0 collective-permute-start.7
  33.0 26.5 %collective-permute-done.6.refs_3_ = bf16[94,1024]{1,0:T(8,128)(2,1)S(1)} collective-permute-done((bf16[94,1024]{1,0:T(8,128)(2,1)S(1)}, bf16[94,1024]{1,0:T(8,128)(2,1)S(1)}, u32[]{:S(2)}, u32[]{:S(2)}) %collective-permute-start.6) | collective-permute-done | bytes 192544 | tf_op jit(solution)/shard_map/ppermute | solution.py:559
  59.4 0.0 collective-permute-start.8
  59.5 0.0 copy-done.17
  59.5 0.1 collective-permute-start.4
  59.5 0.0 copy-done.16
  59.6 2.9 %collective-permute-start.5 = (bf16[96,1024]{1,0:T(8,128)(2,1)S(1)}, bf16[96,1024]{1,0:T(8,128)(2,1)S(1)}, u32[]{:S(2)}, u32[]{:S(2)}) collective-permute-start(bf16[96,1024]{1,0:T(8,128)(2,1)S(1)} %copy-done.16), channel_id=1, source_target_pairs={{0,6},{1,7},{2,4},{3,5},{4,2},{5,3},{6,0},{7,1},{8,14},{9,15},{10,... | collective-permute-start | bytes 589832 | tf_op jit(solution)/shard_map/ppermute | solution.py:535
  62.5 0.1 slice.25
  62.5 0.1 slice.24
  62.6 0.7 reshape.42.late_far
  63.3 0.6 gather_fusion
  63.8 0.7 reshape.41.places_far
  64.5 0.0 collective-permute-done.8.refs_5_
  64.5 0.0 collective-permute-done.7.refs_4_
  64.6 0.6 copy-done.13
  65.2 0.7 copy-done.4
  65.9 2.8 %pack.3 = (bf16[96,1024]{1,0:T(8,128)(2,1)}, bf16[96,1024]{1,0:T(8,128)(2,1)}, bf16[96,1024]{1,0:T(8,128)(2,1)}, bf16[96,1024]{1,0:T(8,128)(2,1)}) custom-call(s32[16,1,330]{2,1,0:T(1,128)} %copy-done.5, s32[16,1,330]{2,1,0:T(1,128)} %copy-done.5, bf16[160,1024]{1,0:T(8,128)(2,1)} %copy-done.3, bf16[94,1024]{1,0:T(8,128)(2,1)} %copy-done.12, ...), custom_call_target="tpu_custom_call" | custom-call | flops 199753728 | bytes 1826816 | tf_op jit(solution)/shard_map/pack/pallas_call | solution.py:319
  68.8 0.6 collective-permute-start.9
  69.4 0.1 collective-permute-start.10
  69.5 2.8 %collective-permute-start.11 = (bf16[96,1024]{1,0:T(8,128)(2,1)}, bf16[96,1024]{1,0:T(8,128)(2,1)S(1)}, u32[]{:S(2)}, u32[]{:S(2)}) collective-permute-start(bf16[96,1024]{1,0:T(8,128)(2,1)} %get-tuple-element.57), channel_id=1, source_target_pairs={{0,6},{1,7},{2,4},{3,5},{4,2},{5,3},{6,0},{7,1},{8,14},{9,15},{10,... | collective-permute-start | bytes 589832 | tf_op jit(solution)/shard_map/ppermute | solution.py:535
  72.3 3.3 %early.1 = (f32[512,1024]{1,0:T(8,128)}, f32[512,128]{1,0:T(8,128)}) custom-call(s32[1,768]{1,0:T(1,128)} %reshape.41.places_far, f32[512,1024]{1,0:T(8,128)} %centroids_far.1, bf16[96,1024]{1,0:T(8,128)(2,1)} %get-tuple-element.39.rest_0_, bf16[96,1024]{1,0:T(8,128)(2,1)} %copy-done.14), custom_call_target="tpu_custom_call" | custom-call | flops 201326592 | bytes 9437184 | tf_op jit(solution)/shard_map/early/pallas_call | solution.py:442
  75.6 0.0 all-to-all-done.1
  75.6 0.0 copy-start.1
  75.7 0.9 copy-done.1
  76.5 5.0 %encode.1 = (bf16[2,1024]{1,0:T(2,128)(2,1)}, bf16[16,2,1024]{2,1,0:T(2,128)(2,1)}) custom-call(s32[1,2]{1,0:T(1,128)} %bitcast.27, s32[128,1]{1,0:T(8,128)} %get-tuple-element.30.refs_1_, bf16[384,1024]{1,0:T(8,128)(2,1)} %bitcast.15, bf16[64,1024]{1,0:T(8,128)(2,1)} %refs_3_.1, f32[1,1024]{1,0:T(1,128)} %bitcast.19, f32[1,1024]{1,0:T(1,128)} %bitcast.20, ...), custom_call_target="tpu_custom_call" | custom-call | flops 637534208 | bytes 6291456 | tf_op jit(solution)/shard_map/encode/pallas_call | solution.py:121
  81.5 3.5 %all-to-all-start.2 = ((bf16[16,2,1024]{2,1,0:T(2,128)(2,1)}), bf16[16,2,1024]{2,1,0:T(2,128)(2,1)S(1)}, u32[]{:S(2)}, u32[]{:S(2)}) async-start(bf16[16,2,1024]{2,1,0:T(2,128)(2,1)} %get-tuple-element.47), calls=%async_computation.2 | async-start | bytes 131072 | tf_op jit(solution)/shard_map/all_to_all | solution.py:603
  85.0 0.0 collective-permute-done.4.rest_0_
  85.0 0.0 collective-permute-done.5.rest_1_
  85.0 0.0 copy-start.8
  85.1 0.0 collective-permute-done.9.rest_3_
  85.1 0.0 collective-permute-done.10.rest_4_
  85.1 0.0 collective-permute-done.11.rest_5_
  85.1 0.0 copy-start.11
  85.1 6.8 %all-to-all-done.2.spread_far = bf16[16,2,1024]{2,1,0:T(2,128)(2,1)S(1)} async-done(((bf16[16,2,1024]{2,1,0:T(2,128)(2,1)}), bf16[16,2,1024]{2,1,0:T(2,128)(2,1)S(1)}, u32[]{:S(2)}, u32[]{:S(2)}) %all-to-all-start.2) | async-done | bytes 65568 | tf_op jit(solution)/shard_map/all_to_all | solution.py:603
  91.9 0.0 copy-done.10
  91.9 0.0 copy-done.11
  91.9 0.6 copy-done.6
  92.5 4.0 %late.1 = f32[512,1024]{1,0:T(8,128)} custom-call(s32[1,768]{1,0:T(1,128)} %reshape.41.places_far, s32[1,32]{1,0:T(1,128)} %reshape.42.late_far, bf16[16,2,1024]{2,1,0:T(2,128)(2,1)} %copy-done.6, f32[512,128]{1,0:T(8,128)} %get-tuple-element.48.share_far, f32[512,1024]{1,0:T(8,128)} %get-tuple-element.49.early_far, bf16[96,1024]{1,0:T(8,128)(2,1)} %copy-done.7, ...), custom_call_target="tpu_custom_call" | custom-call | flops 637534208 | bytes 4194304 | tf_op jit(solution)/shard_map/late/pallas_call | solution.py:474
  (21 shorter events, 0.1 us)
Async XLA Ops:
  0.6 22.3 %copy-start = (bf16[240,1024]{1,0:T(8,128)(2,1)S(1)}, bf16[240,1024]{1,0:T(8,128)(2,1)}, u32[]{:S(2)}) copy-start(bf16[240,1024]{1,0:T(8,128)(2,1)} %param.17) | copy-start | bytes 1474564
  0.6 9.5 %collective-permute-start.1 = (bf16[254,1024]{1,0:T(8,128)(2,1)}, bf16[254,1024]{1,0:T(8,128)(2,1)S(1)}, u32[]{:S(2)}, u32[]{:S(2)}) collective-permute-start(bf16[254,1024]{1,0:T(8,128)(2,1)} %refs_2_.1), channel_id=1, source_target_pairs={{0,1},{1,0},{2,3},{3,2},{4,5},{5,4},{6,7},{7,6},{8,9},{9,8},{10,11... | collective-permute-start | bytes 1560584 | tf_op jit(solution)/shard_map/ppermute | solution.py:539
  2.2 22.0 %collective-permute-start.2 = (bf16[160,1024]{1,0:T(8,128)(2,1)S(1)}, bf16[160,1024]{1,0:T(8,128)(2,1)S(1)}, u32[]{:S(2)}, u32[]{:S(2)}) collective-permute-start(bf16[160,1024]{1,0:T(8,128)(2,1)S(1)} %slice.17), channel_id=1, source_target_pairs={{0,8},{1,9},{2,10},{3,11},{4,12},{5,13},{6,14},{7,15},{8,0},{9,1},... | collective-permute-start | bytes 983048 | tf_op jit(solution)/shard_map/ppermute | solution.py:540
  5.9 1.4 %collective-permute-start = (s32[1,256]{1,0:T(1,128)}, s32[1,256]{1,0:T(1,128)S(1)}, u32[]{:S(2)}, u32[]{:S(2)}) collective-permute-start(s32[1,256]{1,0:T(1,128)} %bitcast.24), channel_id=1, source_target_pairs={{0,1},{1,0},{2,3},{3,2},{4,5},{5,4},{6,7},{7,6},{8,9},{9,8},{10,11... | collective-permute-start | bytes 3080 | tf_op jit(solution)/shard_map/ppermute | solution.py:543
  7.2 0.6 copy-start.15
  10.1 3.9 %copy-start.2 = (bf16[254,1024]{1,0:T(8,128)(2,1)}, bf16[254,1024]{1,0:T(8,128)(2,1)S(1)}, u32[]{:S(2)}) copy-start(bf16[254,1024]{1,0:T(8,128)(2,1)S(1)} %collective-permute-done.1.refs_3_) | copy-start | bytes 1560580
  10.1 12.6 %all-to-all-start = ((s32[16,1,330]{2,1,0:T(1,128)}), s32[16,1,330]{2,1,0:T(1,128)S(1)}, u32[]{:S(2)}, u32[]{:S(2)}) async-start(s32[16,1,330]{2,1,0:T(1,128)} %get-tuple-element.32), calls=%async_computation | async-start | bytes 49152 | tf_op jit(solution)/shard_map/all_to_all | solution.py:548
  16.7 13.3 %copy-start.18 = (bf16[94,1024]{1,0:T(8,128)(2,1)S(1)}, bf16[94,1024]{1,0:T(8,128)(2,1)}, u32[]{:S(2)}) copy-start(bf16[94,1024]{1,0:T(8,128)(2,1)} %get-tuple-element.53) | copy-start | bytes 577540
  16.7 42.7 %copy-start.17 = (bf16[96,1024]{1,0:T(8,128)(2,1)S(1)}, bf16[96,1024]{1,0:T(8,128)(2,1)}, u32[]{:S(2)}) copy-start(bf16[96,1024]{1,0:T(8,128)(2,1)} %get-tuple-element.50) | copy-start | bytes 589828
  16.8 42.8 %copy-start.16 = (bf16[96,1024]{1,0:T(8,128)(2,1)S(1)}, bf16[96,1024]{1,0:T(8,128)(2,1)}, u32[]{:S(2)}) copy-start(bf16[96,1024]{1,0:T(8,128)(2,1)} %get-tuple-element.51) | copy-start | bytes 589828
  16.8 7.7 %collective-permute-start.3 = (bf16[96,1024]{1,0:T(8,128)(2,1)}, bf16[96,1024]{1,0:T(8,128)(2,1)S(1)}, u32[]{:S(2)}, u32[]{:S(2)}) collective-permute-start(bf16[96,1024]{1,0:T(8,128)(2,1)} %get-tuple-element.37), channel_id=1, source_target_pairs={{0,2},{1,3},{2,0},{3,1},{4,6},{5,7},{6,4},{7,5},{8,10},{9,11},{10,... | collective-permute-start | bytes 589832 | tf_op jit(solution)/shard_map/ppermute | solution.py:535
  22.8 41.7 %copy-start.5 = (s32[16,1,330]{2,1,0:T(1,128)}, s32[16,1,330]{2,1,0:T(1,128)S(1)}, u32[]{:S(2)}) copy-start(s32[16,1,330]{2,1,0:T(1,128)S(1)} %all-to-all-done.refs_0_.refs_1_) | copy-start | bytes 63364
  24.2 40.4 %copy-start.3 = (bf16[160,1024]{1,0:T(8,128)(2,1)}, bf16[160,1024]{1,0:T(8,128)(2,1)S(1)}, u32[]{:S(2)}) copy-start(bf16[160,1024]{1,0:T(8,128)(2,1)S(1)} %collective-permute-done.2.refs_2_) | copy-start | bytes 983044
  24.4 47.9 %copy-start.14 = (bf16[96,1024]{1,0:T(8,128)(2,1)}, bf16[96,1024]{1,0:T(8,128)(2,1)S(1)}, u32[]{:S(2)}) copy-start(bf16[96,1024]{1,0:T(8,128)(2,1)S(1)} %collective-permute-done.3.rest_1_) | copy-start | bytes 589828
  24.4 51.2 %all-to-all-start.1 = ((bf16[16,24,1024]{2,1,0:T(8,128)(2,1)}), bf16[16,24,1024]{2,1,0:T(8,128)(2,1)S(1)}, u32[]{:S(2)}, u32[]{:S(2)}) async-start(bf16[16,24,1024]{2,1,0:T(8,128)(2,1)} %bitcast.4), calls=%async_computation.1 | async-start | bytes 1572864 | tf_op jit(solution)/shard_map/all_to_all | solution.py:570
  30.1 29.3 %collective-permute-start.6 = (bf16[94,1024]{1,0:T(8,128)(2,1)S(1)}, bf16[94,1024]{1,0:T(8,128)(2,1)S(1)}, u32[]{:S(2)}, u32[]{:S(2)}) collective-permute-start(bf16[94,1024]{1,0:T(8,128)(2,1)S(1)} %copy-done.18), channel_id=1, source_target_pairs={{0,8},{1,9},{2,10},{3,11},{4,12},{5,13},{6,14},{7,15},{8,0},{9,1},... | collective-permute-start | bytes 577544 | tf_op jit(solution)/shard_map/ppermute | solution.py:559
  33.0 31.5 %collective-permute-start.7 = (bf16[160,1024]{1,0:T(8,128)(2,1)S(1)}, bf16[160,1024]{1,0:T(8,128)(2,1)S(1)}, u32[]{:S(2)}, u32[]{:S(2)}) collective-permute-start(bf16[160,1024]{1,0:T(8,128)(2,1)S(1)} %collective-permute-done.2.refs_2_), channel_id=1, source_target_pairs={{0,1},{1,0},{2,3},{3,2},{4,5},{5,4},{6,7},{7,6},{8,9},{9,8},{10,11... | collective-permute-start | bytes 983048 | tf_op jit(solution)/shard_map/ppermute | solution.py:575
  59.4 5.1 %copy-start.12 = (bf16[94,1024]{1,0:T(8,128)(2,1)}, bf16[94,1024]{1,0:T(8,128)(2,1)S(1)}, u32[]{:S(2)}) copy-start(bf16[94,1024]{1,0:T(8,128)(2,1)S(1)} %collective-permute-done.6.refs_3_) | copy-start | bytes 577540
  59.4 5.1 %collective-permute-start.8 = (bf16[94,1024]{1,0:T(8,128)(2,1)S(1)}, bf16[94,1024]{1,0:T(8,128)(2,1)S(1)}, u32[]{:S(2)}, u32[]{:S(2)}) collective-permute-start(bf16[94,1024]{1,0:T(8,128)(2,1)S(1)} %collective-permute-done.6.refs_3_), channel_id=1, source_target_pairs={{0,1},{1,0},{2,3},{3,2},{4,5},{5,4},{6,7},{7,6},{8,9},{9,8},{10,11... | collective-permute-start | bytes 577544 | tf_op jit(solution)/shard_map/ppermute | solution.py:575
  59.5 25.6 %collective-permute-start.4 = (bf16[96,1024]{1,0:T(8,128)(2,1)S(1)}, bf16[96,1024]{1,0:T(8,128)(2,1)S(1)}, u32[]{:S(2)}, u32[]{:S(2)}) collective-permute-start(bf16[96,1024]{1,0:T(8,128)(2,1)S(1)} %copy-done.17), channel_id=1, source_target_pairs={{0,4},{1,5},{2,6},{3,7},{4,0},{5,1},{6,2},{7,3},{8,12},{9,13},{10,... | collective-permute-start | bytes 589832 | tf_op jit(solution)/shard_map/ppermute | solution.py:535
  59.6 25.5 %collective-permute-start.5 = (bf16[96,1024]{1,0:T(8,128)(2,1)S(1)}, bf16[96,1024]{1,0:T(8,128)(2,1)S(1)}, u32[]{:S(2)}, u32[]{:S(2)}) collective-permute-start(bf16[96,1024]{1,0:T(8,128)(2,1)S(1)} %copy-done.16), channel_id=1, source_target_pairs={{0,6},{1,7},{2,4},{3,5},{4,2},{5,3},{6,0},{7,1},{8,14},{9,15},{10,... | collective-permute-start | bytes 589832 | tf_op jit(solution)/shard_map/ppermute | solution.py:535
  64.5 0.7 copy-start.13
  65.2 0.7 copy-start.4
  68.8 16.3 %collective-permute-start.9 = (bf16[96,1024]{1,0:T(8,128)(2,1)}, bf16[96,1024]{1,0:T(8,128)(2,1)S(1)}, u32[]{:S(2)}, u32[]{:S(2)}) collective-permute-start(bf16[96,1024]{1,0:T(8,128)(2,1)} %get-tuple-element.55), channel_id=1, source_target_pairs={{0,2},{1,3},{2,0},{3,1},{4,6},{5,7},{6,4},{7,5},{8,10},{9,11},{10,... | collective-permute-start | bytes 589832 | tf_op jit(solution)/shard_map/ppermute | solution.py:535
  69.4 15.7 %collective-permute-start.10 = (bf16[96,1024]{1,0:T(8,128)(2,1)}, bf16[96,1024]{1,0:T(8,128)(2,1)S(1)}, u32[]{:S(2)}, u32[]{:S(2)}) collective-permute-start(bf16[96,1024]{1,0:T(8,128)(2,1)} %get-tuple-element.56), channel_id=1, source_target_pairs={{0,4},{1,5},{2,6},{3,7},{4,0},{5,1},{6,2},{7,3},{8,12},{9,13},{10,... | collective-permute-start | bytes 589832 | tf_op jit(solution)/shard_map/ppermute | solution.py:535
  69.5 15.6 %collective-permute-start.11 = (bf16[96,1024]{1,0:T(8,128)(2,1)}, bf16[96,1024]{1,0:T(8,128)(2,1)S(1)}, u32[]{:S(2)}, u32[]{:S(2)}) collective-permute-start(bf16[96,1024]{1,0:T(8,128)(2,1)} %get-tuple-element.57), channel_id=1, source_target_pairs={{0,6},{1,7},{2,4},{3,5},{4,2},{5,3},{6,0},{7,1},{8,14},{9,15},{10,... | collective-permute-start | bytes 589832 | tf_op jit(solution)/shard_map/ppermute | solution.py:535
  75.6 0.9 copy-start.1
  81.5 10.4 %all-to-all-start.2 = ((bf16[16,2,1024]{2,1,0:T(2,128)(2,1)}), bf16[16,2,1024]{2,1,0:T(2,128)(2,1)S(1)}, u32[]{:S(2)}, u32[]{:S(2)}) async-start(bf16[16,2,1024]{2,1,0:T(2,128)(2,1)} %get-tuple-element.47), calls=%async_computation.2 | async-start | bytes 131072 | tf_op jit(solution)/shard_map/all_to_all | solution.py:603
  85.0 6.9 %copy-start.7 = (bf16[96,1024]{1,0:T(8,128)(2,1)}, bf16[96,1024]{1,0:T(8,128)(2,1)S(1)}, u32[]{:S(2)}) copy-start(bf16[96,1024]{1,0:T(8,128)(2,1)S(1)} %collective-permute-done.4.rest_0_) | copy-start | bytes 589828
  85.0 6.8 %copy-start.8 = (bf16[96,1024]{1,0:T(8,128)(2,1)}, bf16[96,1024]{1,0:T(8,128)(2,1)S(1)}, u32[]{:S(2)}) copy-start(bf16[96,1024]{1,0:T(8,128)(2,1)S(1)} %collective-permute-done.5.rest_1_) | copy-start | bytes 589828
  85.1 6.8 %copy-start.9 = (bf16[96,1024]{1,0:T(8,128)(2,1)}, bf16[96,1024]{1,0:T(8,128)(2,1)S(1)}, u32[]{:S(2)}) copy-start(bf16[96,1024]{1,0:T(8,128)(2,1)S(1)} %collective-permute-done.9.rest_3_) | copy-start | bytes 589828
  85.1 6.8 %copy-start.10 = (bf16[96,1024]{1,0:T(8,128)(2,1)}, bf16[96,1024]{1,0:T(8,128)(2,1)S(1)}, u32[]{:S(2)}) copy-start(bf16[96,1024]{1,0:T(8,128)(2,1)S(1)} %collective-permute-done.10.rest_4_) | copy-start | bytes 589828
  85.1 6.8 %copy-start.11 = (bf16[96,1024]{1,0:T(8,128)(2,1)}, bf16[96,1024]{1,0:T(8,128)(2,1)S(1)}, u32[]{:S(2)}) copy-start(bf16[96,1024]{1,0:T(8,128)(2,1)S(1)} %collective-permute-done.11.rest_5_) | copy-start | bytes 589828
  91.9 0.6 copy-start.6

commit v18 on v17

--- a/solution.py
+++ b/solution.py
@@ -459,7 +459,7 @@
         compiler_params=pltpu.CompilerParams(vmem_limit_bytes=60 * 1024 * 1024),
         cost_estimate=pl.CostEstimate(
             flops=2 * centre_count * width * row_total,
-            bytes_accessed=18 * centre_count * width,
+            bytes_accessed=60 * centre_count * width,
             transcendentals=0,
         ),
         name="early",

time: 97 us -> 97 us (level)
  no operation moved by 1% of the time
where the time goes in v18:
time: 97 us; the launch traced here: 96.5 us
  waiting for transfers between devices  38.7 us (40%)
  starting transfers between devices  28.9 us (30%)
  Pallas kernels  20.1 us (21%)
  local copies, waits for them, and re-layouts  6.61 us (7%)
  matrix products  1.29 us (1%)
  between operations  0.97 us (1%)
    ppermute x1, waiting for transfers between devices, shards(): last_rows = lax.ppermute(last_rows, 'dp', across)  26.5 us
    ppermute x6, starting transfers between devices, hand_on(): got.append(lax.ppermute(blocks[step], 'dp', moves))  8.52 us
    all_to_all x1, waiting for transfers between devices, shards(): lax.all_to_all(spread, 'dp', split_axis=0, concat_axis=0, tiled=True)  6.76 us
    all_to_all x1, starting transfers between devices, shards(): lax.all_to_all(found.reshape(peer_count, token_cap, width), 'dp', split_a...  5.64 us
    pallas_call x2, Pallas kernels, pack_rows(): pl.pallas_call(functools.partial(pack_kernel, half, row_cap, count, picks...  5.48 us
    pallas_call x1, Pallas kernels, encode(): pl.pallas_call(encode_kernel, out_shape=[jax.ShapeDtypeStruct((passes, wi...  4.97 us
    all_to_all x1, waiting for transfers between devices, shards(): codes = lax.all_to_all(plan, 'dp', split_axis=0, concat_axis=0, tiled=True)  4.03 us
    pallas_call x1, Pallas kernels, late_update(): pl.pallas_call(late_kernel, out_shape=jax.ShapeDtypeStruct(early.shape, j...  4.02 us
  transfers between devices with their start and end apart: 15, of which 5 were waited for; matrix products, arithmetic and copies ran while one was open for 5% of the time, Pallas kernels for 17%

profile of v18, /device:TPU:0, one launch (start us, length us, event | category | flops | bytes accessed | tf_op | source)
XLA Modules:
  0.0 96.5 jit_solution(11268712916246420043)
XLA Ops:
  0.6 0.0 copy-start
  0.6 0.5 collective-permute-start.1
  1.2 1.0 %slice.17 = bf16[160,1024]{1,0:T(8,128)(2,1)S(1)} slice(bf16[254,1024]{1,0:T(8,128)(2,1)} %refs_2_.1), slice={[0:160], [0:1024]} | slice | bytes 655360 | tf_op jit(solution)/shard_map/slice | solution.py:540
  2.2 3.7 %collective-permute-start.2 = (bf16[160,1024]{1,0:T(8,128)(2,1)S(1)}, bf16[160,1024]{1,0:T(8,128)(2,1)S(1)}, u32[]{:S(2)}, u32[]{:S(2)}) collective-permute-start(bf16[160,1024]{1,0:T(8,128)(2,1)S(1)} %slice.17), channel_id=1, source_target_pairs={{0,8},{1,9},{2,10},{3,11},{4,12},{5,13},{6,14},{7,15},{8,0},{9,1},... | collective-permute-start | bytes 983048 | tf_op jit(solution)/shard_map/ppermute | solution.py:540
  5.9 0.2 collective-permute-start
  6.0 1.2 %collective-permute-done.sibling_far = s32[1,256]{1,0:T(1,128)S(1)} collective-permute-done((s32[1,256]{1,0:T(1,128)}, s32[1,256]{1,0:T(1,128)S(1)}, u32[]{:S(2)}, u32[]{:S(2)}) %collective-permute-start) | collective-permute-done | bytes 1056 | tf_op jit(solution)/shard_map/ppermute | solution.py:543
  7.2 0.6 copy-done.15
  7.8 2.3 %route.1 = (s32[16,1,330]{2,1,0:T(1,128)}, s32[128,1]{1,0:T(8,128)}, s32[1,256]{1,0:T(1,128)}, s32[1,256]{1,0:T(1,128)}) custom-call(s32[2,64]{1,0:T(2,128)} %token_ids_far.1, s32[1,256]{1,0:T(1,128)} %bitcast.25, s32[1,256]{1,0:T(1,128)} %bitcast.26, s32[1,256]{1,0:T(1,128)} %copy-done.15), custom_call_target="tpu_custom_call" | custom-call | tf_op jit(solution)/shard_map/route/pallas_call | solution.py:228
  10.1 0.0 collective-permute-done.1.refs_3_
  10.1 0.0 copy-start.2
  10.1 3.9 %all-to-all-start = ((s32[16,1,330]{2,1,0:T(1,128)}), s32[16,1,330]{2,1,0:T(1,128)S(1)}, u32[]{:S(2)}, u32[]{:S(2)}) async-start(s32[16,1,330]{2,1,0:T(1,128)} %get-tuple-element.32), calls=%async_computation | async-start | bytes 49152 | tf_op jit(solution)/shard_map/all_to_all | solution.py:548
  14.1 0.0 copy-done.2
  14.1 2.6 %pack.2 = (bf16[96,1024]{1,0:T(8,128)(2,1)}, bf16[96,1024]{1,0:T(8,128)(2,1)}, bf16[96,1024]{1,0:T(8,128)(2,1)}, bf16[96,1024]{1,0:T(8,128)(2,1)}, bf16[94,1024]{1,0:T(8,128)(2,1)}) custom-call(s32[1,256]{1,0:T(1,128)} %get-tuple-element.33.refs_0_, s32[1,256]{1,0:T(1,128)} %get-tuple-element.34.refs_1_, bf16[254,1024]{1,0:T(8,128)(2,1)} %refs_2_.1, ...), custom_call_target="tpu_custom_call" | custom-call | flops 199753728 | bytes 1826816 | tf_op jit(solution)/shard_map/pack/pallas_call | solution.py:319
  16.7 0.0 copy-start.18
  16.7 0.0 copy-start.17
  16.8 0.0 copy-start.16
  16.8 2.0 %collective-permute-start.3 = (bf16[96,1024]{1,0:T(8,128)(2,1)}, bf16[96,1024]{1,0:T(8,128)(2,1)S(1)}, u32[]{:S(2)}, u32[]{:S(2)}) collective-permute-start(bf16[96,1024]{1,0:T(8,128)(2,1)} %get-tuple-element.37), channel_id=1, source_target_pairs={{0,2},{1,3},{2,0},{3,1},{4,6},{5,7},{6,4},{7,5},{8,10},{9,11},{10,... | collective-permute-start | bytes 589832 | tf_op jit(solution)/shard_map/ppermute | solution.py:535
  18.7 4.0 %all-to-all-done.refs_0_.refs_1_ = s32[16,1,330]{2,1,0:T(1,128)S(1)} async-done(((s32[16,1,330]{2,1,0:T(1,128)}), s32[16,1,330]{2,1,0:T(1,128)S(1)}, u32[]{:S(2)}, u32[]{:S(2)}) %all-to-all-start) | async-done | bytes 21152 | tf_op jit(solution)/shard_map/all_to_all | solution.py:548
  22.8 0.1 eq.15
  22.9 0.0 copy-done
  22.9 1.3 %convolution_convert_fusion = bf16[384,1024]{1,0:T(8,128)(2,1)} fusion(bf16[240,1024]{1,0:T(8,128)(2,1)S(1)} %copy-done, s32[384]{0:T(512)S(1)} %eq.15), kind=kOutput, calls=%fused_computation.1 | convolution fusion | flops 189229056 | bytes 1279488 | tf_op jit(solution)/shard_map/dot_general | solution.py:564
  24.2 0.0 collective-permute-done.2.refs_2_
  24.2 0.2 collective-permute-done.3.rest_1_
  24.4 5.6 %all-to-all-start.1 = ((bf16[16,24,1024]{2,1,0:T(8,128)(2,1)}), bf16[16,24,1024]{2,1,0:T(8,128)(2,1)S(1)}, u32[]{:S(2)}, u32[]{:S(2)}) async-start(bf16[16,24,1024]{2,1,0:T(8,128)(2,1)} %bitcast.4), calls=%async_computation.1 | async-start | bytes 1572864 | tf_op jit(solution)/shard_map/all_to_all | solution.py:570
  30.1 0.0 copy-done.18
  30.1 2.9 %collective-permute-start.6 = (bf16[94,1024]{1,0:T(8,128)(2,1)S(1)}, bf16[94,1024]{1,0:T(8,128)(2,1)S(1)}, u32[]{:S(2)}, u32[]{:S(2)}) collective-permute-start(bf16[94,1024]{1,0:T(8,128)(2,1)S(1)} %copy-done.18), channel_id=1, source_target_pairs={{0,8},{1,9},{2,10},{3,11},{4,12},{5,13},{6,14},{7,15},{8,0},{9,1},... | collective-permute-start | bytes 577544 | tf_op jit(solution)/shard_map/ppermute | solution.py:559
  33.0 0.0 collective-permute-start.7
  33.0 26.5 %collective-permute-done.6.refs_3_ = bf16[94,1024]{1,0:T(8,128)(2,1)S(1)} collective-permute-done((bf16[94,1024]{1,0:T(8,128)(2,1)S(1)}, bf16[94,1024]{1,0:T(8,128)(2,1)S(1)}, u32[]{:S(2)}, u32[]{:S(2)}) %collective-permute-start.6) | collective-permute-done | bytes 192544 | tf_op jit(solution)/shard_map/ppermute | solution.py:559
  59.4 0.0 collective-permute-start.8
  59.5 0.0 copy-done.17
  59.5 0.1 collective-permute-start.4
  59.5 0.0 copy-done.16
  59.6 2.9 %collective-permute-start.5 = (bf16[96,1024]{1,0:T(8,128)(2,1)S(1)}, bf16[96,1024]{1,0:T(8,128)(2,1)S(1)}, u32[]{:S(2)}, u32[]{:S(2)}) collective-permute-start(bf16[96,1024]{1,0:T(8,128)(2,1)S(1)} %copy-done.16), channel_id=1, source_target_pairs={{0,6},{1,7},{2,4},{3,5},{4,2},{5,3},{6,0},{7,1},{8,14},{9,15},{10,... | collective-permute-start | bytes 589832 | tf_op jit(solution)/shard_map/ppermute | solution.py:535
  62.5 0.1 slice.25
  62.5 0.1 slice.24
  62.6 0.7 reshape.42.late_far
  63.3 0.6 gather_fusion
  63.8 0.7 reshape.41.places_far
  64.5 0.0 collective-permute-done.8.refs_5_
  64.5 0.0 collective-permute-done.7.refs_4_
  64.6 0.6 copy-done.13
  65.2 0.7 copy-done.4
  65.9 2.8 %pack.3 = (bf16[96,1024]{1,0:T(8,128)(2,1)}, bf16[96,1024]{1,0:T(8,128)(2,1)}, bf16[96,1024]{1,0:T(8,128)(2,1)}, bf16[96,1024]{1,0:T(8,128)(2,1)}) custom-call(s32[16,1,330]{2,1,0:T(1,128)} %copy-done.5, s32[16,1,330]{2,1,0:T(1,128)} %copy-done.5, bf16[160,1024]{1,0:T(8,128)(2,1)} %copy-done.3, bf16[94,1024]{1,0:T(8,128)(2,1)} %copy-done.12, ...), custom_call_target="tpu_custom_call" | custom-call | flops 199753728 | bytes 1826816 | tf_op jit(solution)/shard_map/pack/pallas_call | solution.py:319
  68.8 0.6 collective-permute-start.9
  69.4 0.1 collective-permute-start.10
  69.5 2.8 %collective-permute-start.11 = (bf16[96,1024]{1,0:T(8,128)(2,1)}, bf16[96,1024]{1,0:T(8,128)(2,1)S(1)}, u32[]{:S(2)}, u32[]{:S(2)}) collective-permute-start(bf16[96,1024]{1,0:T(8,128)(2,1)} %get-tuple-element.57), channel_id=1, source_target_pairs={{0,6},{1,7},{2,4},{3,5},{4,2},{5,3},{6,0},{7,1},{8,14},{9,15},{10,... | collective-permute-start | bytes 589832 | tf_op jit(solution)/shard_map/ppermute | solution.py:535
  72.3 3.3 %early.1 = (f32[512,1024]{1,0:T(8,128)}, f32[512,128]{1,0:T(8,128)}) custom-call(s32[1,768]{1,0:T(1,128)} %reshape.41.places_far, f32[512,1024]{1,0:T(8,128)} %centroids_far.1, bf16[96,1024]{1,0:T(8,128)(2,1)} %get-tuple-element.39.rest_0_, bf16[96,1024]{1,0:T(8,128)(2,1)} %copy-done.14), custom_call_target="tpu_custom_call" | custom-call | flops 201326592 | bytes 31457280 | tf_op jit(solution)/shard_map/early/pallas_call | solution.py:442
  75.6 0.0 all-to-all-done.1
  75.6 0.0 copy-start.1
  75.7 0.9 copy-done.1
  76.5 5.0 %encode.1 = (bf16[2,1024]{1,0:T(2,128)(2,1)}, bf16[16,2,1024]{2,1,0:T(2,128)(2,1)}) custom-call(s32[1,2]{1,0:T(1,128)} %bitcast.27, s32[128,1]{1,0:T(8,128)} %get-tuple-element.30.refs_1_, bf16[384,1024]{1,0:T(8,128)(2,1)} %bitcast.15, bf16[64,1024]{1,0:T(8,128)(2,1)} %refs_3_.1, f32[1,1024]{1,0:T(1,128)} %bitcast.19, f32[1,1024]{1,0:T(1,128)} %bitcast.20, ...), custom_call_target="tpu_custom_call" | custom-call | flops 637534208 | bytes 6291456 | tf_op jit(solution)/shard_map/encode/pallas_call | solution.py:121
  81.5 3.5 %all-to-all-start.2 = ((bf16[16,2,1024]{2,1,0:T(2,128)(2,1)}), bf16[16,2,1024]{2,1,0:T(2,128)(2,1)S(1)}, u32[]{:S(2)}, u32[]{:S(2)}) async-start(bf16[16,2,1024]{2,1,0:T(2,128)(2,1)} %get-tuple-element.47), calls=%async_computation.2 | async-start | bytes 131072 | tf_op jit(solution)/shard_map/all_to_all | solution.py:603
  85.0 0.0 collective-permute-done.4.rest_0_
  85.0 0.0 collective-permute-done.5.rest_1_
  85.0 0.0 copy-start.8
  85.1 0.0 collective-permute-done.9.rest_3_
  85.1 0.0 collective-permute-done.10.rest_4_
  85.1 0.0 collective-permute-done.11.rest_5_
  85.1 0.0 copy-start.11
  85.1 6.8 %all-to-all-done.2.spread_far = bf16[16,2,1024]{2,1,0:T(2,128)(2,1)S(1)} async-done(((bf16[16,2,1024]{2,1,0:T(2,128)(2,1)}), bf16[16,2,1024]{2,1,0:T(2,128)(2,1)S(1)}, u32[]{:S(2)}, u32[]{:S(2)}) %all-to-all-start.2) | async-done | bytes 65568 | tf_op jit(solution)/shard_map/all_to_all | solution.py:603
  91.9 0.0 copy-done.10
  91.9 0.0 copy-done.11
  91.9 0.6 copy-done.6
  92.5 4.0 %late.1 = f32[512,1024]{1,0:T(8,128)} custom-call(s32[1,768]{1,0:T(1,128)} %reshape.41.places_far, s32[1,32]{1,0:T(1,128)} %reshape.42.late_far, bf16[16,2,1024]{2,1,0:T(2,128)(2,1)} %copy-done.6, f32[512,128]{1,0:T(8,128)} %get-tuple-element.48.share_far, f32[512,1024]{1,0:T(8,128)} %get-tuple-element.49.early_far, bf16[96,1024]{1,0:T(8,128)(2,1)} %copy-done.7, ...), custom_call_target="tpu_custom_call" | custom-call | flops 637534208 | bytes 4194304 | tf_op jit(solution)/shard_map/late/pallas_call | solution.py:474
  (21 shorter events, 0.1 us)
Async XLA Ops:
  0.6 22.3 %copy-start = (bf16[240,1024]{1,0:T(8,128)(2,1)S(1)}, bf16[240,1024]{1,0:T(8,128)(2,1)}, u32[]{:S(2)}) copy-start(bf16[240,1024]{1,0:T(8,128)(2,1)} %param.17) | copy-start | bytes 1474564
  0.6 9.5 %collective-permute-start.1 = (bf16[254,1024]{1,0:T(8,128)(2,1)}, bf16[254,1024]{1,0:T(8,128)(2,1)S(1)}, u32[]{:S(2)}, u32[]{:S(2)}) collective-permute-start(bf16[254,1024]{1,0:T(8,128)(2,1)} %refs_2_.1), channel_id=1, source_target_pairs={{0,1},{1,0},{2,3},{3,2},{4,5},{5,4},{6,7},{7,6},{8,9},{9,8},{10,11... | collective-permute-start | bytes 1560584 | tf_op jit(solution)/shard_map/ppermute | solution.py:539
  2.2 22.0 %collective-permute-start.2 = (bf16[160,1024]{1,0:T(8,128)(2,1)S(1)}, bf16[160,1024]{1,0:T(8,128)(2,1)S(1)}, u32[]{:S(2)}, u32[]{:S(2)}) collective-permute-start(bf16[160,1024]{1,0:T(8,128)(2,1)S(1)} %slice.17), channel_id=1, source_target_pairs={{0,8},{1,9},{2,10},{3,11},{4,12},{5,13},{6,14},{7,15},{8,0},{9,1},... | collective-permute-start | bytes 983048 | tf_op jit(solution)/shard_map/ppermute | solution.py:540
  5.9 1.4 %collective-permute-start = (s32[1,256]{1,0:T(1,128)}, s32[1,256]{1,0:T(1,128)S(1)}, u32[]{:S(2)}, u32[]{:S(2)}) collective-permute-start(s32[1,256]{1,0:T(1,128)} %bitcast.24), channel_id=1, source_target_pairs={{0,1},{1,0},{2,3},{3,2},{4,5},{5,4},{6,7},{7,6},{8,9},{9,8},{10,11... | collective-permute-start | bytes 3080 | tf_op jit(solution)/shard_map/ppermute | solution.py:543
  7.2 0.6 copy-start.15
  10.1 3.9 %copy-start.2 = (bf16[254,1024]{1,0:T(8,128)(2,1)}, bf16[254,1024]{1,0:T(8,128)(2,1)S(1)}, u32[]{:S(2)}) copy-start(bf16[254,1024]{1,0:T(8,128)(2,1)S(1)} %collective-permute-done.1.refs_3_) | copy-start | bytes 1560580
  10.1 12.6 %all-to-all-start = ((s32[16,1,330]{2,1,0:T(1,128)}), s32[16,1,330]{2,1,0:T(1,128)S(1)}, u32[]{:S(2)}, u32[]{:S(2)}) async-start(s32[16,1,330]{2,1,0:T(1,128)} %get-tuple-element.32), calls=%async_computation | async-start | bytes 49152 | tf_op jit(solution)/shard_map/all_to_all | solution.py:548
  16.7 13.3 %copy-start.18 = (bf16[94,1024]{1,0:T(8,128)(2,1)S(1)}, bf16[94,1024]{1,0:T(8,128)(2,1)}, u32[]{:S(2)}) copy-start(bf16[94,1024]{1,0:T(8,128)(2,1)} %get-tuple-element.53) | copy-start | bytes 577540
  16.7 42.7 %copy-start.17 = (bf16[96,1024]{1,0:T(8,128)(2,1)S(1)}, bf16[96,1024]{1,0:T(8,128)(2,1)}, u32[]{:S(2)}) copy-start(bf16[96,1024]{1,0:T(8,128)(2,1)} %get-tuple-element.50) | copy-start | bytes 589828
  16.8 42.8 %copy-start.16 = (bf16[96,1024]{1,0:T(8,128)(2,1)S(1)}, bf16[96,1024]{1,0:T(8,128)(2,1)}, u32[]{:S(2)}) copy-start(bf16[96,1024]{1,0:T(8,128)(2,1)} %get-tuple-element.51) | copy-start | bytes 589828
  16.8 7.7 %collective-permute-start.3 = (bf16[96,1024]{1,0:T(8,128)(2,1)}, bf16[96,1024]{1,0:T(8,128)(2,1)S(1)}, u32[]{:S(2)}, u32[]{:S(2)}) collective-permute-start(bf16[96,1024]{1,0:T(8,128)(2,1)} %get-tuple-element.37), channel_id=1, source_target_pairs={{0,2},{1,3},{2,0},{3,1},{4,6},{5,7},{6,4},{7,5},{8,10},{9,11},{10,... | collective-permute-start | bytes 589832 | tf_op jit(solution)/shard_map/ppermute | solution.py:535
  22.8 41.7 %copy-start.5 = (s32[16,1,330]{2,1,0:T(1,128)}, s32[16,1,330]{2,1,0:T(1,128)S(1)}, u32[]{:S(2)}) copy-start(s32[16,1,330]{2,1,0:T(1,128)S(1)} %all-to-all-done.refs_0_.refs_1_) | copy-start | bytes 63364
  24.2 40.4 %copy-start.3 = (bf16[160,1024]{1,0:T(8,128)(2,1)}, bf16[160,1024]{1,0:T(8,128)(2,1)S(1)}, u32[]{:S(2)}) copy-start(bf16[160,1024]{1,0:T(8,128)(2,1)S(1)} %collective-permute-done.2.refs_2_) | copy-start | bytes 983044
  24.4 47.9 %copy-start.14 = (bf16[96,1024]{1,0:T(8,128)(2,1)}, bf16[96,1024]{1,0:T(8,128)(2,1)S(1)}, u32[]{:S(2)}) copy-start(bf16[96,1024]{1,0:T(8,128)(2,1)S(1)} %collective-permute-done.3.rest_1_) | copy-start | bytes 589828
  24.4 51.2 %all-to-all-start.1 = ((bf16[16,24,1024]{2,1,0:T(8,128)(2,1)}), bf16[16,24,1024]{2,1,0:T(8,128)(2,1)S(1)}, u32[]{:S(2)}, u32[]{:S(2)}) async-start(bf16[16,24,1024]{2,1,0:T(8,128)(2,1)} %bitcast.4), calls=%async_computation.1 | async-start | bytes 1572864 | tf_op jit(solution)/shard_map/all_to_all | solution.py:570
  30.1 29.3 %collective-permute-start.6 = (bf16[94,1024]{1,0:T(8,128)(2,1)S(1)}, bf16[94,1024]{1,0:T(8,128)(2,1)S(1)}, u32[]{:S(2)}, u32[]{:S(2)}) collective-permute-start(bf16[94,1024]{1,0:T(8,128)(2,1)S(1)} %copy-done.18), channel_id=1, source_target_pairs={{0,8},{1,9},{2,10},{3,11},{4,12},{5,13},{6,14},{7,15},{8,0},{9,1},... | collective-permute-start | bytes 577544 | tf_op jit(solution)/shard_map/ppermute | solution.py:559
  33.0 31.5 %collective-permute-start.7 = (bf16[160,1024]{1,0:T(8,128)(2,1)S(1)}, bf16[160,1024]{1,0:T(8,128)(2,1)S(1)}, u32[]{:S(2)}, u32[]{:S(2)}) collective-permute-start(bf16[160,1024]{1,0:T(8,128)(2,1)S(1)} %collective-permute-done.2.refs_2_), channel_id=1, source_target_pairs={{0,1},{1,0},{2,3},{3,2},{4,5},{5,4},{6,7},{7,6},{8,9},{9,8},{10,11... | collective-permute-start | bytes 983048 | tf_op jit(solution)/shard_map/ppermute | solution.py:575
  59.4 5.1 %copy-start.12 = (bf16[94,1024]{1,0:T(8,128)(2,1)}, bf16[94,1024]{1,0:T(8,128)(2,1)S(1)}, u32[]{:S(2)}) copy-start(bf16[94,1024]{1,0:T(8,128)(2,1)S(1)} %collective-permute-done.6.refs_3_) | copy-start | bytes 577540
  59.4 5.1 %collective-permute-start.8 = (bf16[94,1024]{1,0:T(8,128)(2,1)S(1)}, bf16[94,1024]{1,0:T(8,128)(2,1)S(1)}, u32[]{:S(2)}, u32[]{:S(2)}) collective-permute-start(bf16[94,1024]{1,0:T(8,128)(2,1)S(1)} %collective-permute-done.6.refs_3_), channel_id=1, source_target_pairs={{0,1},{1,0},{2,3},{3,2},{4,5},{5,4},{6,7},{7,6},{8,9},{9,8},{10,11... | collective-permute-start | bytes 577544 | tf_op jit(solution)/shard_map/ppermute | solution.py:575
  59.5 25.6 %collective-permute-start.4 = (bf16[96,1024]{1,0:T(8,128)(2,1)S(1)}, bf16[96,1024]{1,0:T(8,128)(2,1)S(1)}, u32[]{:S(2)}, u32[]{:S(2)}) collective-permute-start(bf16[96,1024]{1,0:T(8,128)(2,1)S(1)} %copy-done.17), channel_id=1, source_target_pairs={{0,4},{1,5},{2,6},{3,7},{4,0},{5,1},{6,2},{7,3},{8,12},{9,13},{10,... | collective-permute-start | bytes 589832 | tf_op jit(solution)/shard_map/ppermute | solution.py:535
  59.6 25.5 %collective-permute-start.5 = (bf16[96,1024]{1,0:T(8,128)(2,1)S(1)}, bf16[96,1024]{1,0:T(8,128)(2,1)S(1)}, u32[]{:S(2)}, u32[]{:S(2)}) collective-permute-start(bf16[96,1024]{1,0:T(8,128)(2,1)S(1)} %copy-done.16), channel_id=1, source_target_pairs={{0,6},{1,7},{2,4},{3,5},{4,2},{5,3},{6,0},{7,1},{8,14},{9,15},{10,... | collective-permute-start | bytes 589832 | tf_op jit(solution)/shard_map/ppermute | solution.py:535
  64.5 0.7 copy-start.13
  65.2 0.7 copy-start.4
  68.8 16.3 %collective-permute-start.9 = (bf16[96,1024]{1,0:T(8,128)(2,1)}, bf16[96,1024]{1,0:T(8,128)(2,1)S(1)}, u32[]{:S(2)}, u32[]{:S(2)}) collective-permute-start(bf16[96,1024]{1,0:T(8,128)(2,1)} %get-tuple-element.55), channel_id=1, source_target_pairs={{0,2},{1,3},{2,0},{3,1},{4,6},{5,7},{6,4},{7,5},{8,10},{9,11},{10,... | collective-permute-start | bytes 589832 | tf_op jit(solution)/shard_map/ppermute | solution.py:535
  69.4 15.7 %collective-permute-start.10 = (bf16[96,1024]{1,0:T(8,128)(2,1)}, bf16[96,1024]{1,0:T(8,128)(2,1)S(1)}, u32[]{:S(2)}, u32[]{:S(2)}) collective-permute-start(bf16[96,1024]{1,0:T(8,128)(2,1)} %get-tuple-element.56), channel_id=1, source_target_pairs={{0,4},{1,5},{2,6},{3,7},{4,0},{5,1},{6,2},{7,3},{8,12},{9,13},{10,... | collective-permute-start | bytes 589832 | tf_op jit(solution)/shard_map/ppermute | solution.py:535
  69.5 15.6 %collective-permute-start.11 = (bf16[96,1024]{1,0:T(8,128)(2,1)}, bf16[96,1024]{1,0:T(8,128)(2,1)S(1)}, u32[]{:S(2)}, u32[]{:S(2)}) collective-permute-start(bf16[96,1024]{1,0:T(8,128)(2,1)} %get-tuple-element.57), channel_id=1, source_target_pairs={{0,6},{1,7},{2,4},{3,5},{4,2},{5,3},{6,0},{7,1},{8,14},{9,15},{10,... | collective-permute-start | bytes 589832 | tf_op jit(solution)/shard_map/ppermute | solution.py:535
  75.6 0.9 copy-start.1
  81.5 10.4 %all-to-all-start.2 = ((bf16[16,2,1024]{2,1,0:T(2,128)(2,1)}), bf16[16,2,1024]{2,1,0:T(2,128)(2,1)S(1)}, u32[]{:S(2)}, u32[]{:S(2)}) async-start(bf16[16,2,1024]{2,1,0:T(2,128)(2,1)} %get-tuple-element.47), calls=%async_computation.2 | async-start | bytes 131072 | tf_op jit(solution)/shard_map/all_to_all | solution.py:603
  85.0 6.9 %copy-start.7 = (bf16[96,1024]{1,0:T(8,128)(2,1)}, bf16[96,1024]{1,0:T(8,128)(2,1)S(1)}, u32[]{:S(2)}) copy-start(bf16[96,1024]{1,0:T(8,128)(2,1)S(1)} %collective-permute-done.4.rest_0_) | copy-start | bytes 589828
  85.0 6.8 %copy-start.8 = (bf16[96,1024]{1,0:T(8,128)(2,1)}, bf16[96,1024]{1,0:T(8,128)(2,1)S(1)}, u32[]{:S(2)}) copy-start(bf16[96,1024]{1,0:T(8,128)(2,1)S(1)} %collective-permute-done.5.rest_1_) | copy-start | bytes 589828
  85.1 6.8 %copy-start.9 = (bf16[96,1024]{1,0:T(8,128)(2,1)}, bf16[96,1024]{1,0:T(8,128)(2,1)S(1)}, u32[]{:S(2)}) copy-start(bf16[96,1024]{1,0:T(8,128)(2,1)S(1)} %collective-permute-done.9.rest_3_) | copy-start | bytes 589828
  85.1 6.8 %copy-start.10 = (bf16[96,1024]{1,0:T(8,128)(2,1)}, bf16[96,1024]{1,0:T(8,128)(2,1)S(1)}, u32[]{:S(2)}) copy-start(bf16[96,1024]{1,0:T(8,128)(2,1)S(1)} %collective-permute-done.10.rest_4_) | copy-start | bytes 589828
  85.1 6.8 %copy-start.11 = (bf16[96,1024]{1,0:T(8,128)(2,1)}, bf16[96,1024]{1,0:T(8,128)(2,1)S(1)}, u32[]{:S(2)}) copy-start(bf16[96,1024]{1,0:T(8,128)(2,1)S(1)} %collective-permute-done.11.rest_5_) | copy-start | bytes 589828
  91.9 0.6 copy-start.6

commit v19 on v18

--- a/solution.py
+++ b/solution.py
@@ -459,7 +459,7 @@
         compiler_params=pltpu.CompilerParams(vmem_limit_bytes=60 * 1024 * 1024),
         cost_estimate=pl.CostEstimate(
             flops=2 * centre_count * width * row_total,
-            bytes_accessed=60 * centre_count * width,
+            bytes_accessed=200 * centre_count * width,
             transcendentals=0,
         ),
         name="early",
@@ -571,16 +571,18 @@
         found.reshape(peer_count, token_cap, width), "dp", split_axis=0, concat_axis=0, tiled=True
     ).reshape(peer_count * token_cap, width)
 
+    sources = lax.axis_index("dp") ^ jnp.arange(peer_count, dtype=jnp.int32)
+    got_places = plan[:, token_cap : token_cap + row_cap][sources].reshape(half, 2 * row_cap)
+    spare = padded(2 * row_cap) - 2 * row_cap
+    got_places = jnp.pad(got_places, ((0, 0), (0, spare)), constant_values=-1).reshape(1, -1)
+    near_rows, last_rows = lax.optimization_barrier((own_half[:2], last_rows))
+    means, share = early_update(got_places, centroids, near_rows)
+    first_rows, last_rows, means = lax.optimization_barrier((first_rows, last_rows, means))
     partner_rows = [first_rows, last_rows]
     far_rows = [lax.ppermute(rows, "dp", beside) for rows in partner_rows]
     picks = (half, half ^ 1)
     blocks = pack_rows(codes, codes, partner_rows, far_rows, half, row_cap, row_count, picks)
     other_half = hand_on(blocks)
-    sources = lax.axis_index("dp") ^ jnp.arange(peer_count, dtype=jnp.int32)
-    got_places = plan[:, token_cap : token_cap + row_cap][sources].reshape(half, 2 * row_cap)
-    spare = padded(2 * row_cap) - 2 * row_cap
-    got_places = jnp.pad(got_places, ((0, 0), (0, spare)), constant_values=-1).reshape(1, -1)
-    means, share = early_update(got_places, centroids, own_half[:2])
     late_places = plan[:, token_cap + row_cap :].reshape(1, -1)
     fetched, means, share, got_places, late_places = lax.optimization_barrier(
         (fetched, means, share, got_places, late_places)

time: 97 us -> 96.2 us (level)
  waiting for transfers between devices: 38.7 us -> 37.4 us
    ppermute x1, waiting for transfers between devices: 26.5 us -> 25.1 us  [shards(): last_rows = lax.ppermute(last_rows, 'dp', across)]
where the time goes in v19:
time: 96.2 us; the launch traced here: 95.7 us
  waiting for transfers between devices  37.4 us (39%)
  starting transfers between devices  29.4 us (31%)
  Pallas kernels  20.1 us (21%)
  local copies, waits for them, and re-layouts  6.58 us (7%)
  matrix products  1.29 us (1%)
    ppermute x1, waiting for transfers between devices, shards(): last_rows = lax.ppermute(last_rows, 'dp', across)  25.1 us
    ppermute x6, starting transfers between devices, hand_on(): got.append(lax.ppermute(blocks[step], 'dp', moves))  8.46 us
    all_to_all x1, waiting for transfers between devices, shards(): lax.all_to_all(spread, 'dp', split_axis=0, concat_axis=0, tiled=True)  6.76 us
    all_to_all x1, starting transfers between devices, shards(): lax.all_to_all(found.reshape(peer_count, token_cap, width), 'dp', split_a...  5.66 us
    pallas_call x2, Pallas kernels, pack_rows(): pl.pallas_call(functools.partial(pack_kernel, half, row_cap, count, picks...  5.49 us
    pallas_call x1, Pallas kernels, encode(): pl.pallas_call(encode_kernel, out_shape=[jax.ShapeDtypeStruct((passes, wi...  4.98 us
    all_to_all x1, waiting for transfers between devices, shards(): codes = lax.all_to_all(plan, 'dp', split_axis=0, concat_axis=0, tiled=True)  4.05 us
    pallas_call x1, Pallas kernels, late_update(): pl.pallas_call(late_kernel, out_shape=jax.ShapeDtypeStruct(early.shape, j...  4 us
  transfers between devices with their start and end apart: 15, of which 5 were waited for; matrix products, arithmetic and copies ran while one was open for 5% of the time, Pallas kernels for 17%

profile of v19, /device:TPU:0, one launch (start us, length us, event | category | flops | bytes accessed | tf_op | source)
XLA Modules:
  0.0 95.7 jit_solution(15501412330934756129)
XLA Ops:
  0.6 0.0 copy-start
  0.6 0.5 collective-permute-start.1
  1.2 1.0 %slice.17 = bf16[160,1024]{1,0:T(8,128)(2,1)S(1)} slice(bf16[254,1024]{1,0:T(8,128)(2,1)} %refs_2_.1), slice={[0:160], [0:1024]} | slice | bytes 655360 | tf_op jit(solution)/shard_map/slice | solution.py:540
  2.2 3.7 %collective-permute-start.2 = (bf16[160,1024]{1,0:T(8,128)(2,1)S(1)}, bf16[160,1024]{1,0:T(8,128)(2,1)S(1)}, u32[]{:S(2)}, u32[]{:S(2)}) collective-permute-start(bf16[160,1024]{1,0:T(8,128)(2,1)S(1)} %slice.17), channel_id=1, source_target_pairs={{0,8},{1,9},{2,10},{3,11},{4,12},{5,13},{6,14},{7,15},{8,0},{9,1},... | collective-permute-start | bytes 983048 | tf_op jit(solution)/shard_map/ppermute | solution.py:540
  5.9 0.2 collective-permute-start
  6.0 1.2 %collective-permute-done.sibling_far = s32[1,256]{1,0:T(1,128)S(1)} collective-permute-done((s32[1,256]{1,0:T(1,128)}, s32[1,256]{1,0:T(1,128)S(1)}, u32[]{:S(2)}, u32[]{:S(2)}) %collective-permute-start) | collective-permute-done | bytes 1056 | tf_op jit(solution)/shard_map/ppermute | solution.py:543
  7.2 0.6 copy-done.15
  7.8 2.3 %route.1 = (s32[16,1,330]{2,1,0:T(1,128)}, s32[128,1]{1,0:T(8,128)}, s32[1,256]{1,0:T(1,128)}, s32[1,256]{1,0:T(1,128)}) custom-call(s32[2,64]{1,0:T(2,128)} %token_ids_far.1, s32[1,256]{1,0:T(1,128)} %bitcast.25, s32[1,256]{1,0:T(1,128)} %bitcast.26, s32[1,256]{1,0:T(1,128)} %copy-done.15), custom_call_target="tpu_custom_call" | custom-call | tf_op jit(solution)/shard_map/route/pallas_call | solution.py:228
  10.1 0.0 collective-permute-done.1.refs_3_
  10.1 0.0 copy-start.2
  10.1 3.9 %all-to-all-start = ((s32[16,1,330]{2,1,0:T(1,128)}), s32[16,1,330]{2,1,0:T(1,128)S(1)}, u32[]{:S(2)}, u32[]{:S(2)}) async-start(s32[16,1,330]{2,1,0:T(1,128)} %get-tuple-element.38), calls=%async_computation | async-start | bytes 49152 | tf_op jit(solution)/shard_map/all_to_all | solution.py:548
  14.1 0.0 copy-done.2
  14.1 2.7 %pack.2 = (bf16[96,1024]{1,0:T(8,128)(2,1)}, bf16[96,1024]{1,0:T(8,128)(2,1)}, bf16[96,1024]{1,0:T(8,128)(2,1)}, bf16[96,1024]{1,0:T(8,128)(2,1)}, bf16[94,1024]{1,0:T(8,128)(2,1)}) custom-call(s32[1,256]{1,0:T(1,128)} %get-tuple-element.39.refs_0_, s32[1,256]{1,0:T(1,128)} %get-tuple-element.40.refs_1_, bf16[254,1024]{1,0:T(8,128)(2,1)} %refs_2_.1, ...), custom_call_target="tpu_custom_call" | custom-call | flops 199753728 | bytes 1826816 | tf_op jit(solution)/shard_map/pack/pallas_call | solution.py:319
  16.7 0.0 copy-start.18
  16.7 2.0 %collective-permute-start.3 = (bf16[96,1024]{1,0:T(8,128)(2,1)}, bf16[96,1024]{1,0:T(8,128)(2,1)S(1)}, u32[]{:S(2)}, u32[]{:S(2)}) collective-permute-start(bf16[96,1024]{1,0:T(8,128)(2,1)} %get-tuple-element.43), channel_id=1, source_target_pairs={{0,2},{1,3},{2,0},{3,1},{4,6},{5,7},{6,4},{7,5},{8,10},{9,11},{10,... | collective-permute-start | bytes 589832 | tf_op jit(solution)/shard_map/ppermute | solution.py:535
  18.7 4.1 %all-to-all-done.refs_0_.refs_1_ = s32[16,1,330]{2,1,0:T(1,128)S(1)} async-done(((s32[16,1,330]{2,1,0:T(1,128)}), s32[16,1,330]{2,1,0:T(1,128)S(1)}, u32[]{:S(2)}, u32[]{:S(2)}) %all-to-all-start) | async-done | bytes 21152 | tf_op jit(solution)/shard_map/all_to_all | solution.py:548
  22.8 0.1 eq.15
  22.9 0.0 copy-done
  22.9 1.3 %convolution_convert_fusion = bf16[384,1024]{1,0:T(8,128)(2,1)} fusion(bf16[240,1024]{1,0:T(8,128)(2,1)S(1)} %copy-done, s32[384]{0:T(512)S(1)} %eq.15), kind=kOutput, calls=%fused_computation.1 | convolution fusion | flops 189229056 | bytes 1279488 | tf_op jit(solution)/shard_map/dot_general | solution.py:564
  24.2 0.0 collective-permute-done.2.refs_2_
  24.2 0.2 collective-permute-done.3.rest_1_
  24.4 5.7 %all-to-all-start.1 = ((bf16[16,24,1024]{2,1,0:T(8,128)(2,1)}), bf16[16,24,1024]{2,1,0:T(8,128)(2,1)S(1)}, u32[]{:S(2)}, u32[]{:S(2)}) async-start(bf16[16,24,1024]{2,1,0:T(8,128)(2,1)} %bitcast.4), calls=%async_computation.1 | async-start | bytes 1572864 | tf_op jit(solution)/shard_map/all_to_all | solution.py:570
  30.1 0.0 copy-done.18
  30.1 2.9 %collective-permute-start.4 = (bf16[94,1024]{1,0:T(8,128)(2,1)S(1)}, bf16[94,1024]{1,0:T(8,128)(2,1)S(1)}, u32[]{:S(2)}, u32[]{:S(2)}) collective-permute-start(bf16[94,1024]{1,0:T(8,128)(2,1)S(1)} %copy-done.18), channel_id=1, source_target_pairs={{0,8},{1,9},{2,10},{3,11},{4,12},{5,13},{6,14},{7,15},{8,0},{9,1},... | collective-permute-start | bytes 577544 | tf_op jit(solution)/shard_map/ppermute | solution.py:559
  33.0 0.1 slice.24
  33.1 0.6 gather_fusion
  33.6 0.7 reshape.41.places_far
  34.3 25.1 %collective-permute-done.4.refs_3_ = bf16[94,1024]{1,0:T(8,128)(2,1)S(1)} collective-permute-done((bf16[94,1024]{1,0:T(8,128)(2,1)S(1)}, bf16[94,1024]{1,0:T(8,128)(2,1)S(1)}, u32[]{:S(2)}, u32[]{:S(2)}) %collective-permute-start.4) | collective-permute-done | bytes 192544 | tf_op jit(solution)/shard_map/ppermute | solution.py:559
  59.4 0.0 copy-done.14
  59.4 3.4 %early.1 = (f32[512,1024]{1,0:T(8,128)}, f32[512,128]{1,0:T(8,128)}) custom-call(s32[1,768]{1,0:T(1,128)} %reshape.41.places_far, f32[512,1024]{1,0:T(8,128)} %centroids_far.1, bf16[96,1024]{1,0:T(8,128)(2,1)} %get-tuple-element.50.rest_0_, bf16[96,1024]{1,0:T(8,128)(2,1)} %copy-done.14), custom_call_target="tpu_custom_call" | custom-call | flops 201326592 | bytes 104857600 | tf_op jit(solution)/shard_map/early/pallas_call | solution.py:442
  62.8 0.0 copy-done.5
  62.8 0.1 collective-permute-start.7
  62.9 0.5 collective-permute-start.8
  63.4 0.0 copy-done.17
  63.4 0.0 collective-permute-start.5
  63.4 0.0 copy-done.16
  63.4 2.9 %collective-permute-start.6 = (bf16[96,1024]{1,0:T(8,128)(2,1)S(1)}, bf16[96,1024]{1,0:T(8,128)(2,1)S(1)}, u32[]{:S(2)}, u32[]{:S(2)}) collective-permute-start(bf16[96,1024]{1,0:T(8,128)(2,1)S(1)} %copy-done.16), channel_id=1, source_target_pairs={{0,6},{1,7},{2,4},{3,5},{4,2},{5,3},{6,0},{7,1},{8,14},{9,15},{10,... | collective-permute-start | bytes 589832 | tf_op jit(solution)/shard_map/ppermute | solution.py:535
  66.3 0.0 collective-permute-done.8.refs_5_
  66.3 0.0 collective-permute-done.7.refs_4_
  66.3 0.0 copy-done.3
  66.3 0.0 copy-done.12
  66.3 0.7 copy-done.13
  67.0 0.7 copy-done.4
  67.7 2.8 %pack.3 = (bf16[96,1024]{1,0:T(8,128)(2,1)}, bf16[96,1024]{1,0:T(8,128)(2,1)}, bf16[96,1024]{1,0:T(8,128)(2,1)}, bf16[96,1024]{1,0:T(8,128)(2,1)}) custom-call(s32[16,1,330]{2,1,0:T(1,128)} %copy-done.5, s32[16,1,330]{2,1,0:T(1,128)} %copy-done.5, bf16[160,1024]{1,0:T(8,128)(2,1)} %copy-done.3, bf16[94,1024]{1,0:T(8,128)(2,1)} %copy-done.12, ...), custom_call_target="tpu_custom_call" | custom-call | flops 199753728 | bytes 1826816 | tf_op jit(solution)/shard_map/pack/pallas_call | solution.py:319
  70.6 0.6 collective-permute-start.9
  71.2 0.1 collective-permute-start.10
  71.3 2.9 %collective-permute-start.11 = (bf16[96,1024]{1,0:T(8,128)(2,1)}, bf16[96,1024]{1,0:T(8,128)(2,1)S(1)}, u32[]{:S(2)}, u32[]{:S(2)}) collective-permute-start(bf16[96,1024]{1,0:T(8,128)(2,1)} %get-tuple-element.69), channel_id=1, source_target_pairs={{0,6},{1,7},{2,4},{3,5},{4,2},{5,3},{6,0},{7,1},{8,14},{9,15},{10,... | collective-permute-start | bytes 589832 | tf_op jit(solution)/shard_map/ppermute | solution.py:535
  74.1 0.1 slice.25
  74.2 0.6 reshape.42.late_far
  74.8 0.0 all-to-all-done.1
  74.8 0.9 copy-done.1
  75.7 5.0 %encode.1 = (bf16[2,1024]{1,0:T(2,128)(2,1)}, bf16[16,2,1024]{2,1,0:T(2,128)(2,1)}) custom-call(s32[1,2]{1,0:T(1,128)} %bitcast.27, s32[128,1]{1,0:T(8,128)} %get-tuple-element.36.refs_1_, bf16[384,1024]{1,0:T(8,128)(2,1)} %bitcast.15, bf16[64,1024]{1,0:T(8,128)(2,1)} %refs_3_.1, f32[1,1024]{1,0:T(1,128)} %bitcast.19, f32[1,1024]{1,0:T(1,128)} %bitcast.20, ...), custom_call_target="tpu_custom_call" | custom-call | flops 637534208 | bytes 6291456 | tf_op jit(solution)/shard_map/encode/pallas_call | solution.py:121
  80.7 3.5 %all-to-all-start.2 = ((bf16[16,2,1024]{2,1,0:T(2,128)(2,1)}), bf16[16,2,1024]{2,1,0:T(2,128)(2,1)S(1)}, u32[]{:S(2)}, u32[]{:S(2)}) async-start(bf16[16,2,1024]{2,1,0:T(2,128)(2,1)} %get-tuple-element.59), calls=%async_computation.2 | async-start | bytes 131072 | tf_op jit(solution)/shard_map/all_to_all | solution.py:605
  84.2 0.0 collective-permute-done.5.rest_0_
  84.2 0.0 copy-start.7
  84.2 0.0 collective-permute-done.6.rest_1_
  84.2 0.0 copy-start.8
  84.3 0.0 collective-permute-done.9.rest_3_
  84.3 0.0 collective-permute-done.10.rest_4_
  84.3 0.0 collective-permute-done.11.rest_5_
  84.3 6.8 %all-to-all-done.2.spread_far = bf16[16,2,1024]{2,1,0:T(2,128)(2,1)S(1)} async-done(((bf16[16,2,1024]{2,1,0:T(2,128)(2,1)}), bf16[16,2,1024]{2,1,0:T(2,128)(2,1)S(1)}, u32[]{:S(2)}, u32[]{:S(2)}) %all-to-all-start.2) | async-done | bytes 65568 | tf_op jit(solution)/shard_map/all_to_all | solution.py:605
  91.1 0.0 copy-done.8
  91.1 0.6 copy-done.6
  91.7 4.0 %late.1 = f32[512,1024]{1,0:T(8,128)} custom-call(s32[1,768]{1,0:T(1,128)} %reshape.41.places_far, s32[1,32]{1,0:T(1,128)} %reshape.42.late_far, bf16[16,2,1024]{2,1,0:T(2,128)(2,1)} %copy-done.6, f32[512,128]{1,0:T(8,128)} %get-tuple-element.60.share_far, f32[512,1024]{1,0:T(8,128)} %get-tuple-element.61.early_far, bf16[96,1024]{1,0:T(8,128)(2,1)} %copy-done.7, ...), custom_call_target="tpu_custom_call" | custom-call | flops 637534208 | bytes 4194304 | tf_op jit(solution)/shard_map/late/pallas_call | solution.py:474
  (21 shorter events, 0.1 us)
Async XLA Ops:
  0.6 22.3 %copy-start = (bf16[240,1024]{1,0:T(8,128)(2,1)S(1)}, bf16[240,1024]{1,0:T(8,128)(2,1)}, u32[]{:S(2)}) copy-start(bf16[240,1024]{1,0:T(8,128)(2,1)} %param.17) | copy-start | bytes 1474564
  0.6 9.5 %collective-permute-start.1 = (bf16[254,1024]{1,0:T(8,128)(2,1)}, bf16[254,1024]{1,0:T(8,128)(2,1)S(1)}, u32[]{:S(2)}, u32[]{:S(2)}) collective-permute-start(bf16[254,1024]{1,0:T(8,128)(2,1)} %refs_2_.1), channel_id=1, source_target_pairs={{0,1},{1,0},{2,3},{3,2},{4,5},{5,4},{6,7},{7,6},{8,9},{9,8},{10,11... | collective-permute-start | bytes 1560584 | tf_op jit(solution)/shard_map/ppermute | solution.py:539
  2.2 22.0 %collective-permute-start.2 = (bf16[160,1024]{1,0:T(8,128)(2,1)S(1)}, bf16[160,1024]{1,0:T(8,128)(2,1)S(1)}, u32[]{:S(2)}, u32[]{:S(2)}) collective-permute-start(bf16[160,1024]{1,0:T(8,128)(2,1)S(1)} %slice.17), channel_id=1, source_target_pairs={{0,8},{1,9},{2,10},{3,11},{4,12},{5,13},{6,14},{7,15},{8,0},{9,1},... | collective-permute-start | bytes 983048 | tf_op jit(solution)/shard_map/ppermute | solution.py:540
  5.9 1.4 %collective-permute-start = (s32[1,256]{1,0:T(1,128)}, s32[1,256]{1,0:T(1,128)S(1)}, u32[]{:S(2)}, u32[]{:S(2)}) collective-permute-start(s32[1,256]{1,0:T(1,128)} %bitcast.24), channel_id=1, source_target_pairs={{0,1},{1,0},{2,3},{3,2},{4,5},{5,4},{6,7},{7,6},{8,9},{9,8},{10,11... | collective-permute-start | bytes 3080 | tf_op jit(solution)/shard_map/ppermute | solution.py:543
  7.2 0.6 copy-start.15
  10.1 3.9 %copy-start.2 = (bf16[254,1024]{1,0:T(8,128)(2,1)}, bf16[254,1024]{1,0:T(8,128)(2,1)S(1)}, u32[]{:S(2)}) copy-start(bf16[254,1024]{1,0:T(8,128)(2,1)S(1)} %collective-permute-done.1.refs_3_) | copy-start | bytes 1560580
  10.1 12.7 %all-to-all-start = ((s32[16,1,330]{2,1,0:T(1,128)}), s32[16,1,330]{2,1,0:T(1,128)S(1)}, u32[]{:S(2)}, u32[]{:S(2)}) async-start(s32[16,1,330]{2,1,0:T(1,128)} %get-tuple-element.38), calls=%async_computation | async-start | bytes 49152 | tf_op jit(solution)/shard_map/all_to_all | solution.py:548
  16.7 13.3 %copy-start.18 = (bf16[94,1024]{1,0:T(8,128)(2,1)S(1)}, bf16[94,1024]{1,0:T(8,128)(2,1)}, u32[]{:S(2)}) copy-start(bf16[94,1024]{1,0:T(8,128)(2,1)} %get-tuple-element.48) | copy-start | bytes 577540
  16.7 7.7 %collective-permute-start.3 = (bf16[96,1024]{1,0:T(8,128)(2,1)}, bf16[96,1024]{1,0:T(8,128)(2,1)S(1)}, u32[]{:S(2)}, u32[]{:S(2)}) collective-permute-start(bf16[96,1024]{1,0:T(8,128)(2,1)} %get-tuple-element.43), channel_id=1, source_target_pairs={{0,2},{1,3},{2,0},{3,1},{4,6},{5,7},{6,4},{7,5},{8,10},{9,11},{10,... | collective-permute-start | bytes 589832 | tf_op jit(solution)/shard_map/ppermute | solution.py:535
  22.8 40.0 %copy-start.5 = (s32[16,1,330]{2,1,0:T(1,128)}, s32[16,1,330]{2,1,0:T(1,128)S(1)}, u32[]{:S(2)}) copy-start(s32[16,1,330]{2,1,0:T(1,128)S(1)} %all-to-all-done.refs_0_.refs_1_) | copy-start | bytes 63364
  24.2 39.2 %copy-start.17 = (bf16[96,1024]{1,0:T(8,128)(2,1)S(1)}, bf16[96,1024]{1,0:T(8,128)(2,1)}, u32[]{:S(2)}) copy-start(bf16[96,1024]{1,0:T(8,128)(2,1)} %get-tuple-element.62) | copy-start | bytes 589828
  24.2 39.2 %copy-start.16 = (bf16[96,1024]{1,0:T(8,128)(2,1)S(1)}, bf16[96,1024]{1,0:T(8,128)(2,1)}, u32[]{:S(2)}) copy-start(bf16[96,1024]{1,0:T(8,128)(2,1)} %get-tuple-element.63) | copy-start | bytes 589828
  24.2 42.1 %copy-start.3 = (bf16[160,1024]{1,0:T(8,128)(2,1)}, bf16[160,1024]{1,0:T(8,128)(2,1)S(1)}, u32[]{:S(2)}) copy-start(bf16[160,1024]{1,0:T(8,128)(2,1)S(1)} %collective-permute-done.2.refs_2_) | copy-start | bytes 983044
  24.4 35.0 %copy-start.14 = (bf16[96,1024]{1,0:T(8,128)(2,1)}, bf16[96,1024]{1,0:T(8,128)(2,1)S(1)}, u32[]{:S(2)}) copy-start(bf16[96,1024]{1,0:T(8,128)(2,1)S(1)} %collective-permute-done.3.rest_1_) | copy-start | bytes 589828
  24.4 50.4 %all-to-all-start.1 = ((bf16[16,24,1024]{2,1,0:T(8,128)(2,1)}), bf16[16,24,1024]{2,1,0:T(8,128)(2,1)S(1)}, u32[]{:S(2)}, u32[]{:S(2)}) async-start(bf16[16,24,1024]{2,1,0:T(8,128)(2,1)} %bitcast.4), calls=%async_computation.1 | async-start | bytes 1572864 | tf_op jit(solution)/shard_map/all_to_all | solution.py:570
  30.1 29.3 %collective-permute-start.4 = (bf16[94,1024]{1,0:T(8,128)(2,1)S(1)}, bf16[94,1024]{1,0:T(8,128)(2,1)S(1)}, u32[]{:S(2)}, u32[]{:S(2)}) collective-permute-start(bf16[94,1024]{1,0:T(8,128)(2,1)S(1)} %copy-done.18), channel_id=1, source_target_pairs={{0,8},{1,9},{2,10},{3,11},{4,12},{5,13},{6,14},{7,15},{8,0},{9,1},... | collective-permute-start | bytes 577544 | tf_op jit(solution)/shard_map/ppermute | solution.py:559
  59.4 6.9 %copy-start.12 = (bf16[94,1024]{1,0:T(8,128)(2,1)}, bf16[94,1024]{1,0:T(8,128)(2,1)S(1)}, u32[]{:S(2)}) copy-start(bf16[94,1024]{1,0:T(8,128)(2,1)S(1)} %collective-permute-done.4.refs_3_) | copy-start | bytes 577540
  62.8 3.5 %collective-permute-start.7 = (bf16[160,1024]{1,0:T(8,128)(2,1)S(1)}, bf16[160,1024]{1,0:T(8,128)(2,1)S(1)}, u32[]{:S(2)}, u32[]{:S(2)}) collective-permute-start(bf16[160,1024]{1,0:T(8,128)(2,1)S(1)} %collective-permute-done.2.refs_2_), channel_id=1, source_target_pairs={{0,1},{1,0},{2,3},{3,2},{4,5},{5,4},{6,7},{7,6},{8,9},{9,8},{10,11... | collective-permute-start | bytes 983048 | tf_op jit(solution)/shard_map/ppermute | solution.py:582
  62.9 3.4 %collective-permute-start.8 = (bf16[94,1024]{1,0:T(8,128)(2,1)S(1)}, bf16[94,1024]{1,0:T(8,128)(2,1)S(1)}, u32[]{:S(2)}, u32[]{:S(2)}) collective-permute-start(bf16[94,1024]{1,0:T(8,128)(2,1)S(1)} %collective-permute-done.4.refs_3_), channel_id=1, source_target_pairs={{0,1},{1,0},{2,3},{3,2},{4,5},{5,4},{6,7},{7,6},{8,9},{9,8},{10,11... | collective-permute-start | bytes 577544 | tf_op jit(solution)/shard_map/ppermute | solution.py:582
  63.4 20.8 %collective-permute-start.5 = (bf16[96,1024]{1,0:T(8,128)(2,1)S(1)}, bf16[96,1024]{1,0:T(8,128)(2,1)S(1)}, u32[]{:S(2)}, u32[]{:S(2)}) collective-permute-start(bf16[96,1024]{1,0:T(8,128)(2,1)S(1)} %copy-done.17), channel_id=1, source_target_pairs={{0,4},{1,5},{2,6},{3,7},{4,0},{5,1},{6,2},{7,3},{8,12},{9,13},{10,... | collective-permute-start | bytes 589832 | tf_op jit(solution)/shard_map/ppermute | solution.py:535
  63.4 20.8 %collective-permute-start.6 = (bf16[96,1024]{1,0:T(8,128)(2,1)S(1)}, bf16[96,1024]{1,0:T(8,128)(2,1)S(1)}, u32[]{:S(2)}, u32[]{:S(2)}) collective-permute-start(bf16[96,1024]{1,0:T(8,128)(2,1)S(1)} %copy-done.16), channel_id=1, source_target_pairs={{0,6},{1,7},{2,4},{3,5},{4,2},{5,3},{6,0},{7,1},{8,14},{9,15},{10,... | collective-permute-start | bytes 589832 | tf_op jit(solution)/shard_map/ppermute | solution.py:535
  66.3 0.7 copy-start.13
  67.0 0.7 copy-start.4
  70.6 13.7 %collective-permute-start.9 = (bf16[96,1024]{1,0:T(8,128)(2,1)}, bf16[96,1024]{1,0:T(8,128)(2,1)S(1)}, u32[]{:S(2)}, u32[]{:S(2)}) collective-permute-start(bf16[96,1024]{1,0:T(8,128)(2,1)} %get-tuple-element.67), channel_id=1, source_target_pairs={{0,2},{1,3},{2,0},{3,1},{4,6},{5,7},{6,4},{7,5},{8,10},{9,11},{10,... | collective-permute-start | bytes 589832 | tf_op jit(solution)/shard_map/ppermute | solution.py:535
  71.2 13.1 %collective-permute-start.10 = (bf16[96,1024]{1,0:T(8,128)(2,1)}, bf16[96,1024]{1,0:T(8,128)(2,1)S(1)}, u32[]{:S(2)}, u32[]{:S(2)}) collective-permute-start(bf16[96,1024]{1,0:T(8,128)(2,1)} %get-tuple-element.68), channel_id=1, source_target_pairs={{0,4},{1,5},{2,6},{3,7},{4,0},{5,1},{6,2},{7,3},{8,12},{9,13},{10,... | collective-permute-start | bytes 589832 | tf_op jit(solution)/shard_map/ppermute | solution.py:535
  71.3 13.0 %collective-permute-start.11 = (bf16[96,1024]{1,0:T(8,128)(2,1)}, bf16[96,1024]{1,0:T(8,128)(2,1)S(1)}, u32[]{:S(2)}, u32[]{:S(2)}) collective-permute-start(bf16[96,1024]{1,0:T(8,128)(2,1)} %get-tuple-element.69), channel_id=1, source_target_pairs={{0,6},{1,7},{2,4},{3,5},{4,2},{5,3},{6,0},{7,1},{8,14},{9,15},{10,... | collective-permute-start | bytes 589832 | tf_op jit(solution)/shard_map/ppermute | solution.py:535
  74.8 0.9 copy-start.1
  80.7 10.4 %all-to-all-start.2 = ((bf16[16,2,1024]{2,1,0:T(2,128)(2,1)}), bf16[16,2,1024]{2,1,0:T(2,128)(2,1)S(1)}, u32[]{:S(2)}, u32[]{:S(2)}) async-start(bf16[16,2,1024]{2,1,0:T(2,128)(2,1)} %get-tuple-element.59), calls=%async_computation.2 | async-start | bytes 131072 | tf_op jit(solution)/shard_map/all_to_all | solution.py:605
  84.2 6.9 %copy-start.7 = (bf16[96,1024]{1,0:T(8,128)(2,1)}, bf16[96,1024]{1,0:T(8,128)(2,1)S(1)}, u32[]{:S(2)}) copy-start(bf16[96,1024]{1,0:T(8,128)(2,1)S(1)} %collective-permute-done.5.rest_0_) | copy-start | bytes 589828
  84.2 6.8 %copy-start.8 = (bf16[96,1024]{1,0:T(8,128)(2,1)}, bf16[96,1024]{1,0:T(8,128)(2,1)S(1)}, u32[]{:S(2)}) copy-start(bf16[96,1024]{1,0:T(8,128)(2,1)S(1)} %collective-permute-done.6.rest_1_) | copy-start | bytes 589828
  84.3 6.8 %copy-start.9 = (bf16[96,1024]{1,0:T(8,128)(2,1)}, bf16[96,1024]{1,0:T(8,128)(2,1)S(1)}, u32[]{:S(2)}) copy-start(bf16[96,1024]{1,0:T(8,128)(2,1)S(1)} %collective-permute-done.9.rest_3_) | copy-start | bytes 589828
  84.3 6.8 %copy-start.10 = (bf16[96,1024]{1,0:T(8,128)(2,1)}, bf16[96,1024]{1,0:T(8,128)(2,1)S(1)}, u32[]{:S(2)}) copy-start(bf16[96,1024]{1,0:T(8,128)(2,1)S(1)} %collective-permute-done.10.rest_4_) | copy-start | bytes 589828
  84.3 6.8 %copy-start.11 = (bf16[96,1024]{1,0:T(8,128)(2,1)}, bf16[96,1024]{1,0:T(8,128)(2,1)S(1)}, u32[]{:S(2)}) copy-start(bf16[96,1024]{1,0:T(8,128)(2,1)S(1)} %collective-permute-done.11.rest_5_) | copy-start | bytes 589828
  91.1 0.6 copy-start.6

commit v20 on v19

--- a/solution.py
+++ b/solution.py
@@ -458,7 +458,7 @@
         ],
         compiler_params=pltpu.CompilerParams(vmem_limit_bytes=60 * 1024 * 1024),
         cost_estimate=pl.CostEstimate(
-            flops=2 * centre_count * width * row_total,
+            flops=100 * centre_count * width * row_total,
             bytes_accessed=200 * centre_count * width,
             transcendentals=0,
         ),

time: 96.2 us -> 75.4 us (0.78)
  waiting for transfers between devices: 37.4 us -> 11.7 us
  starting transfers between devices: 29.4 us -> 34.1 us
    ppermute x1, waiting for transfers between devices: 25.1 us -> 0.01 us  [shards(): last_rows = lax.ppermute(last_rows, 'dp', across)]
    all_to_all x1, waiting for transfers between devices: 6.76 us -> 3.53 us  [shards(): lax.all_to_all(spread, 'dp', split_axis=0, concat_axis=0, tiled=True)]
    ppermute x6, waiting for transfers between devices: 0.22 us -> 3.31 us  [hand_on(): got.append(lax.ppermute(blocks[step], 'dp', moves))]
    all_to_all x1, starting transfers between devices: 5.66 us -> 8.73 us  [shards(): lax.all_to_all(found.reshape(peer_count, token_cap, width), 'dp', split_a...]
    all_to_all x1, waiting for transfers between devices: 4.05 us -> 1.89 us  [shards(): codes = lax.all_to_all(plan, 'dp', split_axis=0, concat_axis=0, tiled=True)]
    all_to_all x1, waiting for transfers between devices: 0.01 us -> 1.77 us  [shards(): lax.all_to_all(found.reshape(peer_count, token_cap, width), 'dp', split_a...]
    all_to_all x1, starting transfers between devices: 3.49 us -> 5.2 us  [shards(): lax.all_to_all(spread, 'dp', split_axis=0, concat_axis=0, tiled=True)]
    unnamed x38 -> x36, local copies, waits for them, and re-layouts: 3.49 us -> 3.55 us
  transfers between devices with their start and end apart: 15 -> 15, of which waited for: 5 -> 5; matrix products, arithmetic and copies ran while one was open for 5% -> 6% of each run, Pallas kernels for 17% -> 22%
where the time goes in v20:
time: 75.4 us; the launch traced here: 74.9 us
  starting transfers between devices  34.1 us (45%)
  Pallas kernels  20.2 us (27%)
  waiting for transfers between devices  11.7 us (16%)
  local copies, waits for them, and re-layouts  6.7 us (9%)
  matrix products  1.29 us (2%)
  between operations  0.9 us (1%)
    ppermute x6, starting transfers between devices, hand_on(): got.append(lax.ppermute(blocks[step], 'dp', moves))  8.92 us
    all_to_all x1, starting transfers between devices, shards(): lax.all_to_all(found.reshape(peer_count, token_cap, width), 'dp', split_a...  8.73 us
    pallas_call x2, Pallas kernels, pack_rows(): pl.pallas_call(functools.partial(pack_kernel, half, row_cap, count, picks...  5.51 us
    all_to_all x1, starting transfers between devices, shards(): lax.all_to_all(spread, 'dp', split_axis=0, concat_axis=0, tiled=True)  5.2 us
    pallas_call x1, Pallas kernels, encode(): pl.pallas_call(encode_kernel, out_shape=[jax.ShapeDtypeStruct((passes, wi...  4.99 us
    pallas_call x1, Pallas kernels, late_update(): pl.pallas_call(late_kernel, out_shape=jax.ShapeDtypeStruct(early.shape, j...  4 us
    all_to_all x1, starting transfers between devices, shards(): codes = lax.all_to_all(plan, 'dp', split_axis=0, concat_axis=0, tiled=True)  3.92 us
    ppermute x1, starting transfers between devices, shards(): first_rows = lax.ppermute(stored_rows[:ahead], 'dp', across)  3.72 us
  transfers between devices with their start and end apart: 15, of which 5 were waited for; matrix products, arithmetic and copies ran while one was open for 6% of the time, Pallas kernels for 22%

profile of v20, /device:TPU:0, one launch (start us, length us, event | category | flops | bytes accessed | tf_op | source)
XLA Modules:
  0.0 74.9 jit_solution(4759794794876532457)
XLA Ops:
  0.6 0.0 copy-start
  0.6 0.5 collective-permute-start.1
  1.2 1.0 %slice.17 = bf16[160,1024]{1,0:T(8,128)(2,1)S(1)} slice(bf16[254,1024]{1,0:T(8,128)(2,1)} %refs_2_.1), slice={[0:160], [0:1024]} | slice | bytes 655360 | tf_op jit(solution)/shard_map/slice | solution.py:540
  2.2 3.7 %collective-permute-start.2 = (bf16[160,1024]{1,0:T(8,128)(2,1)S(1)}, bf16[160,1024]{1,0:T(8,128)(2,1)S(1)}, u32[]{:S(2)}, u32[]{:S(2)}) collective-permute-start(bf16[160,1024]{1,0:T(8,128)(2,1)S(1)} %slice.17), channel_id=1, source_target_pairs={{0,8},{1,9},{2,10},{3,11},{4,12},{5,13},{6,14},{7,15},{8,0},{9,1},... | collective-permute-start | bytes 983048 | tf_op jit(solution)/shard_map/ppermute | solution.py:540
  5.9 0.2 collective-permute-start
  6.0 1.2 %collective-permute-done.sibling_far = s32[1,256]{1,0:T(1,128)S(1)} collective-permute-done((s32[1,256]{1,0:T(1,128)}, s32[1,256]{1,0:T(1,128)S(1)}, u32[]{:S(2)}, u32[]{:S(2)}) %collective-permute-start) | collective-permute-done | bytes 1056 | tf_op jit(solution)/shard_map/ppermute | solution.py:543
  7.2 0.6 copy-done.14
  7.8 2.3 %route.1 = (s32[16,1,330]{2,1,0:T(1,128)}, s32[128,1]{1,0:T(8,128)}, s32[1,256]{1,0:T(1,128)}, s32[1,256]{1,0:T(1,128)}) custom-call(s32[2,64]{1,0:T(2,128)} %token_ids_far.1, s32[1,256]{1,0:T(1,128)} %bitcast.25, s32[1,256]{1,0:T(1,128)} %bitcast.26, s32[1,256]{1,0:T(1,128)} %copy-done.14), custom_call_target="tpu_custom_call" | custom-call | tf_op jit(solution)/shard_map/route/pallas_call | solution.py:228
  10.1 0.0 collective-permute-done.1.refs_3_
  10.1 0.0 copy-start.2
  10.1 3.9 %all-to-all-start = ((s32[16,1,330]{2,1,0:T(1,128)}), s32[16,1,330]{2,1,0:T(1,128)S(1)}, u32[]{:S(2)}, u32[]{:S(2)}) async-start(s32[16,1,330]{2,1,0:T(1,128)} %get-tuple-element.38), calls=%async_computation | async-start | bytes 49152 | tf_op jit(solution)/shard_map/all_to_all | solution.py:548
  14.1 0.0 copy-done.2
  14.1 2.7 %pack.2 = (bf16[96,1024]{1,0:T(8,128)(2,1)}, bf16[96,1024]{1,0:T(8,128)(2,1)}, bf16[96,1024]{1,0:T(8,128)(2,1)}, bf16[96,1024]{1,0:T(8,128)(2,1)}, bf16[94,1024]{1,0:T(8,128)(2,1)}) custom-call(s32[1,256]{1,0:T(1,128)} %get-tuple-element.39.refs_0_, s32[1,256]{1,0:T(1,128)} %get-tuple-element.40.refs_1_, bf16[254,1024]{1,0:T(8,128)(2,1)} %refs_2_.1, ...), custom_call_target="tpu_custom_call" | custom-call | flops 199753728 | bytes 1826816 | tf_op jit(solution)/shard_map/pack/pallas_call | solution.py:319
  16.8 2.0 %collective-permute-start.3 = (bf16[96,1024]{1,0:T(8,128)(2,1)}, bf16[96,1024]{1,0:T(8,128)(2,1)S(1)}, u32[]{:S(2)}, u32[]{:S(2)}) collective-permute-start(bf16[96,1024]{1,0:T(8,128)(2,1)} %get-tuple-element.43), channel_id=1, source_target_pairs={{0,2},{1,3},{2,0},{3,1},{4,6},{5,7},{6,4},{7,5},{8,10},{9,11},{10,... | collective-permute-start | bytes 589832 | tf_op jit(solution)/shard_map/ppermute | solution.py:535
  18.8 2.4 %collective-permute-start.4 = (bf16[94,1024]{1,0:T(8,128)(2,1)}, bf16[94,1024]{1,0:T(8,128)(2,1)S(1)}, u32[]{:S(2)}, u32[]{:S(2)}) collective-permute-start(bf16[94,1024]{1,0:T(8,128)(2,1)} %get-tuple-element.48), channel_id=1, source_target_pairs={{0,8},{1,9},{2,10},{3,11},{4,12},{5,13},{6,14},{7,15},{8,0},{9,1},... | collective-permute-start | bytes 577544 | tf_op jit(solution)/shard_map/ppermute | solution.py:559
  21.1 1.9 %all-to-all-done.refs_0_.refs_1_ = s32[16,1,330]{2,1,0:T(1,128)S(1)} async-done(((s32[16,1,330]{2,1,0:T(1,128)}), s32[16,1,330]{2,1,0:T(1,128)S(1)}, u32[]{:S(2)}, u32[]{:S(2)}) %all-to-all-start) | async-done | bytes 21152 | tf_op jit(solution)/shard_map/all_to_all | solution.py:548
  23.0 0.1 eq.15
  23.1 0.0 copy-done
  23.1 1.3 %convolution_convert_fusion = bf16[384,1024]{1,0:T(8,128)(2,1)} fusion(bf16[240,1024]{1,0:T(8,128)(2,1)S(1)} %copy-done, s32[384]{0:T(512)S(1)} %eq.15), kind=kOutput, calls=%fused_computation.1 | convolution fusion | flops 189229056 | bytes 1279488 | tf_op jit(solution)/shard_map/dot_general | solution.py:564
  24.4 0.0 collective-permute-done.2.refs_2_
  24.4 0.0 collective-permute-done.3.rest_1_
  24.4 8.7 %all-to-all-start.1 = ((bf16[16,24,1024]{2,1,0:T(8,128)(2,1)}), bf16[16,24,1024]{2,1,0:T(8,128)(2,1)S(1)}, u32[]{:S(2)}, u32[]{:S(2)}) async-start(bf16[16,24,1024]{2,1,0:T(8,128)(2,1)} %bitcast.4), calls=%async_computation.1 | async-start | bytes 1572864 | tf_op jit(solution)/shard_map/all_to_all | solution.py:570
  33.2 0.1 slice.24
  33.3 0.6 gather_fusion
  33.9 0.7 reshape.41.places_far
  34.5 0.0 collective-permute-done.4.refs_3_
  34.5 0.0 copy-done.17
  34.5 0.0 copy-start.12
  34.5 3.4 %early.1 = (f32[512,1024]{1,0:T(8,128)}, f32[512,128]{1,0:T(8,128)}) custom-call(s32[1,768]{1,0:T(1,128)} %reshape.41.places_far, f32[512,1024]{1,0:T(8,128)} %centroids_far.1, bf16[96,1024]{1,0:T(8,128)(2,1)} %get-tuple-element.50.rest_0_, bf16[96,1024]{1,0:T(8,128)(2,1)} %copy-done.17), custom_call_target="tpu_custom_call" | custom-call | flops 10066329600 | bytes 104857600 | tf_op jit(solution)/shard_map/early/pallas_call | solution.py:442
  38.0 0.0 copy-done.5
  38.0 0.0 copy-done.3
  38.0 0.5 collective-permute-start.7
  38.4 0.0 copy-done.12
  38.4 0.1 collective-permute-start.8
  38.6 0.0 copy-done.16
  38.6 1.9 %collective-permute-start.5 = (bf16[96,1024]{1,0:T(8,128)(2,1)S(1)}, bf16[96,1024]{1,0:T(8,128)(2,1)S(1)}, u32[]{:S(2)}, u32[]{:S(2)}) collective-permute-start(bf16[96,1024]{1,0:T(8,128)(2,1)S(1)} %copy-done.16), channel_id=1, source_target_pairs={{0,4},{1,5},{2,6},{3,7},{4,0},{5,1},{6,2},{7,3},{8,12},{9,13},{10,... | collective-permute-start | bytes 589832 | tf_op jit(solution)/shard_map/ppermute | solution.py:535
  40.5 0.0 copy-done.15
  40.5 1.5 %collective-permute-start.6 = (bf16[96,1024]{1,0:T(8,128)(2,1)S(1)}, bf16[96,1024]{1,0:T(8,128)(2,1)S(1)}, u32[]{:S(2)}, u32[]{:S(2)}) collective-permute-start(bf16[96,1024]{1,0:T(8,128)(2,1)S(1)} %copy-done.15), channel_id=1, source_target_pairs={{0,6},{1,7},{2,4},{3,5},{4,2},{5,3},{6,0},{7,1},{8,14},{9,15},{10,... | collective-permute-start | bytes 589832 | tf_op jit(solution)/shard_map/ppermute | solution.py:535
  41.9 0.0 collective-permute-done.8.refs_5_
  41.9 0.0 collective-permute-done.7.refs_4_
  42.0 0.7 copy-done.13
  42.7 0.8 %copy-done.4 = bf16[160,1024]{1,0:T(8,128)(2,1)} copy-done((bf16[160,1024]{1,0:T(8,128)(2,1)}, bf16[160,1024]{1,0:T(8,128)(2,1)S(1)}, u32[]{:S(2)}) %copy-start.4) | copy-done | bytes 327704
  43.4 2.8 %pack.3 = (bf16[96,1024]{1,0:T(8,128)(2,1)}, bf16[96,1024]{1,0:T(8,128)(2,1)}, bf16[96,1024]{1,0:T(8,128)(2,1)}, bf16[96,1024]{1,0:T(8,128)(2,1)}) custom-call(s32[16,1,330]{2,1,0:T(1,128)} %copy-done.5, s32[16,1,330]{2,1,0:T(1,128)} %copy-done.5, bf16[160,1024]{1,0:T(8,128)(2,1)} %copy-done.3, bf16[94,1024]{1,0:T(8,128)(2,1)} %copy-done.12, ...), custom_call_target="tpu_custom_call" | custom-call | flops 199753728 | bytes 1826816 | tf_op jit(solution)/shard_map/pack/pallas_call | solution.py:319
  46.2 0.2 collective-permute-start.9
  46.4 1.9 %collective-permute-start.10 = (bf16[96,1024]{1,0:T(8,128)(2,1)}, bf16[96,1024]{1,0:T(8,128)(2,1)S(1)}, u32[]{:S(2)}, u32[]{:S(2)}) collective-permute-start(bf16[96,1024]{1,0:T(8,128)(2,1)} %get-tuple-element.68), channel_id=1, source_target_pairs={{0,4},{1,5},{2,6},{3,7},{4,0},{5,1},{6,2},{7,3},{8,12},{9,13},{10,... | collective-permute-start | bytes 589832 | tf_op jit(solution)/shard_map/ppermute | solution.py:535
  48.3 1.5 %collective-permute-start.11 = (bf16[96,1024]{1,0:T(8,128)(2,1)}, bf16[96,1024]{1,0:T(8,128)(2,1)S(1)}, u32[]{:S(2)}, u32[]{:S(2)}) collective-permute-start(bf16[96,1024]{1,0:T(8,128)(2,1)} %get-tuple-element.69), channel_id=1, source_target_pairs={{0,6},{1,7},{2,4},{3,5},{4,2},{5,3},{6,0},{7,1},{8,14},{9,15},{10,... | collective-permute-start | bytes 589832 | tf_op jit(solution)/shard_map/ppermute | solution.py:535
  49.8 0.1 slice.25
  49.9 0.7 reshape.42.late_far
  50.6 1.8 %all-to-all-done.1 = bf16[16,24,1024]{2,1,0:T(8,128)(2,1)S(1)} async-done(((bf16[16,24,1024]{2,1,0:T(8,128)(2,1)}), bf16[16,24,1024]{2,1,0:T(8,128)(2,1)S(1)}, u32[]{:S(2)}, u32[]{:S(2)}) %all-to-all-start.1) | async-done | bytes 786464 | tf_op jit(solution)/shard_map/all_to_all | solution.py:570
  52.3 0.9 %copy-done.1 = bf16[16,24,1024]{2,1,0:T(8,128)(2,1)} copy-done((bf16[16,24,1024]{2,1,0:T(8,128)(2,1)}, bf16[16,24,1024]{2,1,0:T(8,128)(2,1)S(1)}, u32[]{:S(2)}) %copy-start.1) | copy-done | bytes 786456
  53.2 5.0 %encode.1 = (bf16[2,1024]{1,0:T(2,128)(2,1)}, bf16[16,2,1024]{2,1,0:T(2,128)(2,1)}) custom-call(s32[1,2]{1,0:T(1,128)} %bitcast.27, s32[128,1]{1,0:T(8,128)} %get-tuple-element.36.refs_1_, bf16[384,1024]{1,0:T(8,128)(2,1)} %bitcast.15, bf16[64,1024]{1,0:T(8,128)(2,1)} %refs_3_.1, f32[1,1024]{1,0:T(1,128)} %bitcast.19, f32[1,1024]{1,0:T(1,128)} %bitcast.20, ...), custom_call_target="tpu_custom_call" | custom-call | flops 637534208 | bytes 6291456 | tf_op jit(solution)/shard_map/encode/pallas_call | solution.py:121
  58.2 5.2 %all-to-all-start.2 = ((bf16[16,2,1024]{2,1,0:T(2,128)(2,1)}), bf16[16,2,1024]{2,1,0:T(2,128)(2,1)S(1)}, u32[]{:S(2)}, u32[]{:S(2)}) async-start(bf16[16,2,1024]{2,1,0:T(2,128)(2,1)} %get-tuple-element.59), calls=%async_computation.2 | async-start | bytes 131072 | tf_op jit(solution)/shard_map/all_to_all | solution.py:605
  63.4 0.0 collective-permute-done.5.rest_0_
  63.4 0.0 copy-start.7
  63.4 0.0 collective-permute-done.6.rest_1_
  63.4 0.0 copy-start.8
  63.5 0.0 collective-permute-done.9.rest_3_
  63.5 0.0 collective-permute-done.10.rest_4_
  63.5 0.0 copy-start.10
  63.5 3.3 %collective-permute-done.11.rest_5_ = bf16[96,1024]{1,0:T(8,128)(2,1)S(1)} collective-permute-done((bf16[96,1024]{1,0:T(8,128)(2,1)}, bf16[96,1024]{1,0:T(8,128)(2,1)S(1)}, u32[]{:S(2)}, u32[]{:S(2)}) %collective-permute-start.11) | collective-permute-done | bytes 196640 | tf_op jit(solution)/shard_map/ppermute | solution.py:535
  66.8 3.5 %all-to-all-done.2.spread_far = bf16[16,2,1024]{2,1,0:T(2,128)(2,1)S(1)} async-done(((bf16[16,2,1024]{2,1,0:T(2,128)(2,1)}), bf16[16,2,1024]{2,1,0:T(2,128)(2,1)S(1)}, u32[]{:S(2)}, u32[]{:S(2)}) %all-to-all-start.2) | async-done | bytes 65568 | tf_op jit(solution)/shard_map/all_to_all | solution.py:605
  70.3 0.0 copy-done.7
  70.3 0.6 copy-done.6
  70.9 4.0 %late.1 = f32[512,1024]{1,0:T(8,128)} custom-call(s32[1,768]{1,0:T(1,128)} %reshape.41.places_far, s32[1,32]{1,0:T(1,128)} %reshape.42.late_far, bf16[16,2,1024]{2,1,0:T(2,128)(2,1)} %copy-done.6, f32[512,128]{1,0:T(8,128)} %get-tuple-element.60.share_far, f32[512,1024]{1,0:T(8,128)} %get-tuple-element.61.early_far, bf16[96,1024]{1,0:T(8,128)(2,1)} %copy-done.7, ...), custom_call_target="tpu_custom_call" | custom-call | flops 637534208 | bytes 4194304 | tf_op jit(solution)/shard_map/late/pallas_call | solution.py:474
  (19 shorter events, 0.0 us)
Async XLA Ops:
  0.6 22.5 %copy-start = (bf16[240,1024]{1,0:T(8,128)(2,1)S(1)}, bf16[240,1024]{1,0:T(8,128)(2,1)}, u32[]{:S(2)}) copy-start(bf16[240,1024]{1,0:T(8,128)(2,1)} %param.17) | copy-start | bytes 1474564
  0.6 9.5 %collective-permute-start.1 = (bf16[254,1024]{1,0:T(8,128)(2,1)}, bf16[254,1024]{1,0:T(8,128)(2,1)S(1)}, u32[]{:S(2)}, u32[]{:S(2)}) collective-permute-start(bf16[254,1024]{1,0:T(8,128)(2,1)} %refs_2_.1), channel_id=1, source_target_pairs={{0,1},{1,0},{2,3},{3,2},{4,5},{5,4},{6,7},{7,6},{8,9},{9,8},{10,11... | collective-permute-start | bytes 1560584 | tf_op jit(solution)/shard_map/ppermute | solution.py:539
  2.2 22.3 %collective-permute-start.2 = (bf16[160,1024]{1,0:T(8,128)(2,1)S(1)}, bf16[160,1024]{1,0:T(8,128)(2,1)S(1)}, u32[]{:S(2)}, u32[]{:S(2)}) collective-permute-start(bf16[160,1024]{1,0:T(8,128)(2,1)S(1)} %slice.17), channel_id=1, source_target_pairs={{0,8},{1,9},{2,10},{3,11},{4,12},{5,13},{6,14},{7,15},{8,0},{9,1},... | collective-permute-start | bytes 983048 | tf_op jit(solution)/shard_map/ppermute | solution.py:540
  5.9 1.4 %collective-permute-start = (s32[1,256]{1,0:T(1,128)}, s32[1,256]{1,0:T(1,128)S(1)}, u32[]{:S(2)}, u32[]{:S(2)}) collective-permute-start(s32[1,256]{1,0:T(1,128)} %bitcast.24), channel_id=1, source_target_pairs={{0,1},{1,0},{2,3},{3,2},{4,5},{5,4},{6,7},{7,6},{8,9},{9,8},{10,11... | collective-permute-start | bytes 3080 | tf_op jit(solution)/shard_map/ppermute | solution.py:543
  7.2 0.6 copy-start.14
  10.1 4.0 %copy-start.2 = (bf16[254,1024]{1,0:T(8,128)(2,1)}, bf16[254,1024]{1,0:T(8,128)(2,1)S(1)}, u32[]{:S(2)}) copy-start(bf16[254,1024]{1,0:T(8,128)(2,1)S(1)} %collective-permute-done.1.refs_3_) | copy-start | bytes 1560580
  10.1 12.9 %all-to-all-start = ((s32[16,1,330]{2,1,0:T(1,128)}), s32[16,1,330]{2,1,0:T(1,128)S(1)}, u32[]{:S(2)}, u32[]{:S(2)}) async-start(s32[16,1,330]{2,1,0:T(1,128)} %get-tuple-element.38), calls=%async_computation | async-start | bytes 49152 | tf_op jit(solution)/shard_map/all_to_all | solution.py:548
  16.8 7.7 %collective-permute-start.3 = (bf16[96,1024]{1,0:T(8,128)(2,1)}, bf16[96,1024]{1,0:T(8,128)(2,1)S(1)}, u32[]{:S(2)}, u32[]{:S(2)}) collective-permute-start(bf16[96,1024]{1,0:T(8,128)(2,1)} %get-tuple-element.43), channel_id=1, source_target_pairs={{0,2},{1,3},{2,0},{3,1},{4,6},{5,7},{6,4},{7,5},{8,10},{9,11},{10,... | collective-permute-start | bytes 589832 | tf_op jit(solution)/shard_map/ppermute | solution.py:535
  18.8 15.8 %collective-permute-start.4 = (bf16[94,1024]{1,0:T(8,128)(2,1)}, bf16[94,1024]{1,0:T(8,128)(2,1)S(1)}, u32[]{:S(2)}, u32[]{:S(2)}) collective-permute-start(bf16[94,1024]{1,0:T(8,128)(2,1)} %get-tuple-element.48), channel_id=1, source_target_pairs={{0,8},{1,9},{2,10},{3,11},{4,12},{5,13},{6,14},{7,15},{8,0},{9,1},... | collective-permute-start | bytes 577544 | tf_op jit(solution)/shard_map/ppermute | solution.py:559
  23.0 14.9 %copy-start.5 = (s32[16,1,330]{2,1,0:T(1,128)}, s32[16,1,330]{2,1,0:T(1,128)S(1)}, u32[]{:S(2)}) copy-start(s32[16,1,330]{2,1,0:T(1,128)S(1)} %all-to-all-done.refs_0_.refs_1_) | copy-start | bytes 63364
  24.4 13.5 %copy-start.3 = (bf16[160,1024]{1,0:T(8,128)(2,1)}, bf16[160,1024]{1,0:T(8,128)(2,1)S(1)}, u32[]{:S(2)}) copy-start(bf16[160,1024]{1,0:T(8,128)(2,1)S(1)} %collective-permute-done.2.refs_2_) | copy-start | bytes 983044
  24.4 10.1 %copy-start.17 = (bf16[96,1024]{1,0:T(8,128)(2,1)}, bf16[96,1024]{1,0:T(8,128)(2,1)S(1)}, u32[]{:S(2)}) copy-start(bf16[96,1024]{1,0:T(8,128)(2,1)S(1)} %collective-permute-done.3.rest_1_) | copy-start | bytes 589828
  24.4 27.9 %all-to-all-start.1 = ((bf16[16,24,1024]{2,1,0:T(8,128)(2,1)}), bf16[16,24,1024]{2,1,0:T(8,128)(2,1)S(1)}, u32[]{:S(2)}, u32[]{:S(2)}) async-start(bf16[16,24,1024]{2,1,0:T(8,128)(2,1)} %bitcast.4), calls=%async_computation.1 | async-start | bytes 1572864 | tf_op jit(solution)/shard_map/all_to_all | solution.py:570
  34.5 4.0 %copy-start.16 = (bf16[96,1024]{1,0:T(8,128)(2,1)S(1)}, bf16[96,1024]{1,0:T(8,128)(2,1)}, u32[]{:S(2)}) copy-start(bf16[96,1024]{1,0:T(8,128)(2,1)} %get-tuple-element.62) | copy-start | bytes 589828
  34.5 6.0 %copy-start.15 = (bf16[96,1024]{1,0:T(8,128)(2,1)S(1)}, bf16[96,1024]{1,0:T(8,128)(2,1)}, u32[]{:S(2)}) copy-start(bf16[96,1024]{1,0:T(8,128)(2,1)} %get-tuple-element.63) | copy-start | bytes 589828
  34.5 3.9 %copy-start.12 = (bf16[94,1024]{1,0:T(8,128)(2,1)}, bf16[94,1024]{1,0:T(8,128)(2,1)S(1)}, u32[]{:S(2)}) copy-start(bf16[94,1024]{1,0:T(8,128)(2,1)S(1)} %collective-permute-done.4.refs_3_) | copy-start | bytes 577540
  38.0 4.0 %collective-permute-start.7 = (bf16[160,1024]{1,0:T(8,128)(2,1)S(1)}, bf16[160,1024]{1,0:T(8,128)(2,1)S(1)}, u32[]{:S(2)}, u32[]{:S(2)}) collective-permute-start(bf16[160,1024]{1,0:T(8,128)(2,1)S(1)} %collective-permute-done.2.refs_2_), channel_id=1, source_target_pairs={{0,1},{1,0},{2,3},{3,2},{4,5},{5,4},{6,7},{7,6},{8,9},{9,8},{10,11... | collective-permute-start | bytes 983048 | tf_op jit(solution)/shard_map/ppermute | solution.py:582
  38.4 3.5 %collective-permute-start.8 = (bf16[94,1024]{1,0:T(8,128)(2,1)S(1)}, bf16[94,1024]{1,0:T(8,128)(2,1)S(1)}, u32[]{:S(2)}, u32[]{:S(2)}) collective-permute-start(bf16[94,1024]{1,0:T(8,128)(2,1)S(1)} %collective-permute-done.4.refs_3_), channel_id=1, source_target_pairs={{0,1},{1,0},{2,3},{3,2},{4,5},{5,4},{6,7},{7,6},{8,9},{9,8},{10,11... | collective-permute-start | bytes 577544 | tf_op jit(solution)/shard_map/ppermute | solution.py:582
  38.6 24.9 %collective-permute-start.5 = (bf16[96,1024]{1,0:T(8,128)(2,1)S(1)}, bf16[96,1024]{1,0:T(8,128)(2,1)S(1)}, u32[]{:S(2)}, u32[]{:S(2)}) collective-permute-start(bf16[96,1024]{1,0:T(8,128)(2,1)S(1)} %copy-done.16), channel_id=1, source_target_pairs={{0,4},{1,5},{2,6},{3,7},{4,0},{5,1},{6,2},{7,3},{8,12},{9,13},{10,... | collective-permute-start | bytes 589832 | tf_op jit(solution)/shard_map/ppermute | solution.py:535
  40.5 23.0 %collective-permute-start.6 = (bf16[96,1024]{1,0:T(8,128)(2,1)S(1)}, bf16[96,1024]{1,0:T(8,128)(2,1)S(1)}, u32[]{:S(2)}, u32[]{:S(2)}) collective-permute-start(bf16[96,1024]{1,0:T(8,128)(2,1)S(1)} %copy-done.15), channel_id=1, source_target_pairs={{0,6},{1,7},{2,4},{3,5},{4,2},{5,3},{6,0},{7,1},{8,14},{9,15},{10,... | collective-permute-start | bytes 589832 | tf_op jit(solution)/shard_map/ppermute | solution.py:535
  41.9 0.7 copy-start.13
  42.7 0.8 %copy-start.4 = (bf16[160,1024]{1,0:T(8,128)(2,1)}, bf16[160,1024]{1,0:T(8,128)(2,1)S(1)}, u32[]{:S(2)}) copy-start(bf16[160,1024]{1,0:T(8,128)(2,1)S(1)} %collective-permute-done.7.refs_4_) | copy-start | bytes 983044
  46.2 17.2 %collective-permute-start.9 = (bf16[96,1024]{1,0:T(8,128)(2,1)}, bf16[96,1024]{1,0:T(8,128)(2,1)S(1)}, u32[]{:S(2)}, u32[]{:S(2)}) collective-permute-start(bf16[96,1024]{1,0:T(8,128)(2,1)} %get-tuple-element.67), channel_id=1, source_target_pairs={{0,2},{1,3},{2,0},{3,1},{4,6},{5,7},{6,4},{7,5},{8,10},{9,11},{10,... | collective-permute-start | bytes 589832 | tf_op jit(solution)/shard_map/ppermute | solution.py:535
  46.4 17.1 %collective-permute-start.10 = (bf16[96,1024]{1,0:T(8,128)(2,1)}, bf16[96,1024]{1,0:T(8,128)(2,1)S(1)}, u32[]{:S(2)}, u32[]{:S(2)}) collective-permute-start(bf16[96,1024]{1,0:T(8,128)(2,1)} %get-tuple-element.68), channel_id=1, source_target_pairs={{0,4},{1,5},{2,6},{3,7},{4,0},{5,1},{6,2},{7,3},{8,12},{9,13},{10,... | collective-permute-start | bytes 589832 | tf_op jit(solution)/shard_map/ppermute | solution.py:535
  48.3 18.4 %collective-permute-start.11 = (bf16[96,1024]{1,0:T(8,128)(2,1)}, bf16[96,1024]{1,0:T(8,128)(2,1)S(1)}, u32[]{:S(2)}, u32[]{:S(2)}) collective-permute-start(bf16[96,1024]{1,0:T(8,128)(2,1)} %get-tuple-element.69), channel_id=1, source_target_pairs={{0,6},{1,7},{2,4},{3,5},{4,2},{5,3},{6,0},{7,1},{8,14},{9,15},{10,... | collective-permute-start | bytes 589832 | tf_op jit(solution)/shard_map/ppermute | solution.py:535
  52.3 0.9 %copy-start.1 = (bf16[16,24,1024]{2,1,0:T(8,128)(2,1)}, bf16[16,24,1024]{2,1,0:T(8,128)(2,1)S(1)}, u32[]{:S(2)}) copy-start(bf16[16,24,1024]{2,1,0:T(8,128)(2,1)S(1)} %all-to-all-done.1) | copy-start | bytes 2359300
  58.2 12.1 %all-to-all-start.2 = ((bf16[16,2,1024]{2,1,0:T(2,128)(2,1)}), bf16[16,2,1024]{2,1,0:T(2,128)(2,1)S(1)}, u32[]{:S(2)}, u32[]{:S(2)}) async-start(bf16[16,2,1024]{2,1,0:T(2,128)(2,1)} %get-tuple-element.59), calls=%async_computation.2 | async-start | bytes 131072 | tf_op jit(solution)/shard_map/all_to_all | solution.py:605
  63.4 6.9 %copy-start.7 = (bf16[96,1024]{1,0:T(8,128)(2,1)}, bf16[96,1024]{1,0:T(8,128)(2,1)S(1)}, u32[]{:S(2)}) copy-start(bf16[96,1024]{1,0:T(8,128)(2,1)S(1)} %collective-permute-done.5.rest_0_) | copy-start | bytes 589828
  63.4 6.9 %copy-start.8 = (bf16[96,1024]{1,0:T(8,128)(2,1)}, bf16[96,1024]{1,0:T(8,128)(2,1)S(1)}, u32[]{:S(2)}) copy-start(bf16[96,1024]{1,0:T(8,128)(2,1)S(1)} %collective-permute-done.6.rest_1_) | copy-start | bytes 589828
  63.5 6.9 %copy-start.9 = (bf16[96,1024]{1,0:T(8,128)(2,1)}, bf16[96,1024]{1,0:T(8,128)(2,1)S(1)}, u32[]{:S(2)}) copy-start(bf16[96,1024]{1,0:T(8,128)(2,1)S(1)} %collective-permute-done.9.rest_3_) | copy-start | bytes 589828
  63.5 6.8 %copy-start.10 = (bf16[96,1024]{1,0:T(8,128)(2,1)}, bf16[96,1024]{1,0:T(8,128)(2,1)S(1)}, u32[]{:S(2)}) copy-start(bf16[96,1024]{1,0:T(8,128)(2,1)S(1)} %collective-permute-done.10.rest_4_) | copy-start | bytes 589828
  66.8 3.6 %copy-start.11 = (bf16[96,1024]{1,0:T(8,128)(2,1)}, bf16[96,1024]{1,0:T(8,128)(2,1)S(1)}, u32[]{:S(2)}) copy-start(bf16[96,1024]{1,0:T(8,128)(2,1)S(1)} %collective-permute-done.11.rest_5_) | copy-start | bytes 589828
  70.3 0.6 copy-start.6

commit v21 on v20

--- a/solution.py
+++ b/solution.py
@@ -556,6 +556,7 @@
         row_count,
         rest=store_count - ahead,
     )
+    codes, last_rows = lax.optimization_barrier((codes, last_rows))
     last_rows = lax.ppermute(last_rows, "dp", across)
     own_half = hand_on(blocks)
     plan = codes[:, 0, row_count:]

time: 75.4 us -> 77.6 us (1.029)
  waiting for transfers between devices: 11.7 us -> 20.4 us
  starting transfers between devices: 34.1 us -> 27.6 us
    ppermute x1, waiting for transfers between devices: 0.01 us -> 7.65 us  [shards(): last_rows = lax.ppermute(last_rows, 'dp', across)]
    all_to_all x1, starting transfers between devices: 8.73 us -> 3.63 us  [shards(): lax.all_to_all(found.reshape(peer_count, token_cap, width), 'dp', split_a...]
    ppermute x6, waiting for transfers between devices: 3.31 us -> 0.02 us  [hand_on(): got.append(lax.ppermute(blocks[step], 'dp', moves))]
    all_to_all x1, waiting for transfers between devices: 3.53 us -> 6.79 us  [shards(): lax.all_to_all(spread, 'dp', split_axis=0, concat_axis=0, tiled=True)]
    ppermute x6, starting transfers between devices: 8.92 us -> 6.31 us  [hand_on(): got.append(lax.ppermute(blocks[step], 'dp', moves))]
    all_to_all x1, waiting for transfers between devices: 1.89 us -> 4.01 us  [shards(): codes = lax.all_to_all(plan, 'dp', split_axis=0, concat_axis=0, tiled=True)]
    all_to_all x1, waiting for transfers between devices: 1.77 us -> 0.01 us  [shards(): lax.all_to_all(found.reshape(peer_count, token_cap, width), 'dp', split_a...]
    all_to_all x1, starting transfers between devices: 5.2 us -> 6.04 us  [shards(): lax.all_to_all(spread, 'dp', split_axis=0, concat_axis=0, tiled=True)]
  transfers between devices with their start and end apart: 15 -> 15, of which waited for: 5 -> 5; matrix products, arithmetic and copies ran while one was open for 6% -> 6% of each run, Pallas kernels for 22% -> 21%
where the time goes in v21:
time: 77.6 us; the launch traced here: 77.1 us
  starting transfers between devices  27.6 us (36%)
  waiting for transfers between devices  20.4 us (26%)
  Pallas kernels  20.2 us (26%)
  local copies, waits for them, and re-layouts  6.7 us (9%)
  matrix products  1.29 us (2%)
  between operations  0.92 us (1%)
    ppermute x1, waiting for transfers between devices, shards(): last_rows = lax.ppermute(last_rows, 'dp', across)  7.65 us
    all_to_all x1, waiting for transfers between devices, shards(): lax.all_to_all(spread, 'dp', split_axis=0, concat_axis=0, tiled=True)  6.79 us
    ppermute x6, starting transfers between devices, hand_on(): got.append(lax.ppermute(blocks[step], 'dp', moves))  6.31 us
    all_to_all x1, starting transfers between devices, shards(): lax.all_to_all(spread, 'dp', split_axis=0, concat_axis=0, tiled=True)  6.04 us
    pallas_call x2, Pallas kernels, pack_rows(): pl.pallas_call(functools.partial(pack_kernel, half, row_cap, count, picks...  5.51 us
    pallas_call x1, Pallas kernels, encode(): pl.pallas_call(encode_kernel, out_shape=[jax.ShapeDtypeStruct((passes, wi...  4.98 us
    all_to_all x1, waiting for transfers between devices, shards(): codes = lax.all_to_all(plan, 'dp', split_axis=0, concat_axis=0, tiled=True)  4.01 us
    pallas_call x1, Pallas kernels, late_update(): pl.pallas_call(late_kernel, out_shape=jax.ShapeDtypeStruct(early.shape, j...  4 us
  transfers between devices with their start and end apart: 15, of which 5 were waited for; matrix products, arithmetic and copies ran while one was open for 6% of the time, Pallas kernels for 21%

profile of v21, /device:TPU:0, one launch (start us, length us, event | category | flops | bytes accessed | tf_op | source)
XLA Modules:
  0.0 77.1 jit_solution(11495876567071219766)
XLA Ops:
  0.6 0.0 copy-start
  0.6 0.5 collective-permute-start.1
  1.2 1.0 %slice.17 = bf16[160,1024]{1,0:T(8,128)(2,1)S(1)} slice(bf16[254,1024]{1,0:T(8,128)(2,1)} %refs_2_.1), slice={[0:160], [0:1024]} | slice | bytes 655360 | tf_op jit(solution)/shard_map/slice | solution.py:540
  2.2 3.7 %collective-permute-start.2 = (bf16[160,1024]{1,0:T(8,128)(2,1)S(1)}, bf16[160,1024]{1,0:T(8,128)(2,1)S(1)}, u32[]{:S(2)}, u32[]{:S(2)}) collective-permute-start(bf16[160,1024]{1,0:T(8,128)(2,1)S(1)} %slice.17), channel_id=1, source_target_pairs={{0,8},{1,9},{2,10},{3,11},{4,12},{5,13},{6,14},{7,15},{8,0},{9,1},... | collective-permute-start | bytes 983048 | tf_op jit(solution)/shard_map/ppermute | solution.py:540
  5.9 0.2 collective-permute-start
  6.0 1.2 %collective-permute-done.sibling_far = s32[1,256]{1,0:T(1,128)S(1)} collective-permute-done((s32[1,256]{1,0:T(1,128)}, s32[1,256]{1,0:T(1,128)S(1)}, u32[]{:S(2)}, u32[]{:S(2)}) %collective-permute-start) | collective-permute-done | bytes 1056 | tf_op jit(solution)/shard_map/ppermute | solution.py:543
  7.2 0.6 copy-done.14
  7.8 2.3 %route.1 = (s32[16,1,330]{2,1,0:T(1,128)}, s32[128,1]{1,0:T(8,128)}, s32[1,256]{1,0:T(1,128)}, s32[1,256]{1,0:T(1,128)}) custom-call(s32[2,64]{1,0:T(2,128)} %token_ids_far.1, s32[1,256]{1,0:T(1,128)} %bitcast.25, s32[1,256]{1,0:T(1,128)} %bitcast.26, s32[1,256]{1,0:T(1,128)} %copy-done.14), custom_call_target="tpu_custom_call" | custom-call | tf_op jit(solution)/shard_map/route/pallas_call | solution.py:228
  10.1 0.0 collective-permute-done.1.refs_3_
  10.1 0.0 copy-start.2
  10.1 3.9 %all-to-all-start = ((s32[16,1,330]{2,1,0:T(1,128)}), s32[16,1,330]{2,1,0:T(1,128)S(1)}, u32[]{:S(2)}, u32[]{:S(2)}) async-start(s32[16,1,330]{2,1,0:T(1,128)} %get-tuple-element.40), calls=%async_computation | async-start | bytes 49152 | tf_op jit(solution)/shard_map/all_to_all | solution.py:548
  14.1 0.0 copy-done.2
  14.1 2.7 %pack.2 = (bf16[96,1024]{1,0:T(8,128)(2,1)}, bf16[96,1024]{1,0:T(8,128)(2,1)}, bf16[96,1024]{1,0:T(8,128)(2,1)}, bf16[96,1024]{1,0:T(8,128)(2,1)}, bf16[94,1024]{1,0:T(8,128)(2,1)}) custom-call(s32[1,256]{1,0:T(1,128)} %get-tuple-element.41.refs_0_, s32[1,256]{1,0:T(1,128)} %get-tuple-element.42.refs_1_, bf16[254,1024]{1,0:T(8,128)(2,1)} %refs_2_.1, ...), custom_call_target="tpu_custom_call" | custom-call | flops 199753728 | bytes 1826816 | tf_op jit(solution)/shard_map/pack/pallas_call | solution.py:319
  16.8 2.0 %collective-permute-start.3 = (bf16[96,1024]{1,0:T(8,128)(2,1)}, bf16[96,1024]{1,0:T(8,128)(2,1)S(1)}, u32[]{:S(2)}, u32[]{:S(2)}) collective-permute-start(bf16[96,1024]{1,0:T(8,128)(2,1)} %get-tuple-element.47), channel_id=1, source_target_pairs={{0,2},{1,3},{2,0},{3,1},{4,6},{5,7},{6,4},{7,5},{8,10},{9,11},{10,... | collective-permute-start | bytes 589832 | tf_op jit(solution)/shard_map/ppermute | solution.py:535
  18.8 4.0 %all-to-all-done.refs_0_.refs_1_ = s32[16,1,330]{2,1,0:T(1,128)S(1)} async-done(((s32[16,1,330]{2,1,0:T(1,128)}), s32[16,1,330]{2,1,0:T(1,128)S(1)}, u32[]{:S(2)}, u32[]{:S(2)}) %all-to-all-start) | async-done | bytes 21152 | tf_op jit(solution)/shard_map/all_to_all | solution.py:548
  22.8 0.1 eq.15
  22.9 2.7 %collective-permute-start.4 = (bf16[94,1024]{1,0:T(8,128)(2,1)}, bf16[94,1024]{1,0:T(8,128)(2,1)S(1)}, u32[]{:S(2)}, u32[]{:S(2)}) collective-permute-start(bf16[94,1024]{1,0:T(8,128)(2,1)} %get-tuple-element.52), channel_id=1, source_target_pairs={{0,8},{1,9},{2,10},{3,11},{4,12},{5,13},{6,14},{7,15},{8,0},{9,1},... | collective-permute-start | bytes 577544 | tf_op jit(solution)/shard_map/ppermute | solution.py:560
  25.6 0.0 copy-done
  25.6 1.3 %convolution_convert_fusion = bf16[384,1024]{1,0:T(8,128)(2,1)} fusion(bf16[240,1024]{1,0:T(8,128)(2,1)S(1)} %copy-done, s32[384]{0:T(512)S(1)} %eq.15), kind=kOutput, calls=%fused_computation.1 | convolution fusion | flops 189229056 | bytes 1279488 | tf_op jit(solution)/shard_map/dot_general | solution.py:565
  26.9 0.0 collective-permute-done.2.refs_2_
  26.9 0.0 collective-permute-done.3.rest_1_
  26.9 0.0 copy-start.17
  26.9 3.6 %all-to-all-start.1 = ((bf16[16,24,1024]{2,1,0:T(8,128)(2,1)}), bf16[16,24,1024]{2,1,0:T(8,128)(2,1)S(1)}, u32[]{:S(2)}, u32[]{:S(2)}) async-start(bf16[16,24,1024]{2,1,0:T(8,128)(2,1)} %bitcast.4), calls=%async_computation.1 | async-start | bytes 1572864 | tf_op jit(solution)/shard_map/all_to_all | solution.py:571
  30.6 0.1 slice.23
  30.6 0.6 gather_fusion
  31.2 0.7 reshape.41.places_far
  31.9 7.7 %collective-permute-done.4.refs_3_ = bf16[94,1024]{1,0:T(8,128)(2,1)S(1)} collective-permute-done((bf16[94,1024]{1,0:T(8,128)(2,1)}, bf16[94,1024]{1,0:T(8,128)(2,1)S(1)}, u32[]{:S(2)}, u32[]{:S(2)}) %collective-permute-start.4) | collective-permute-done | bytes 192544 | tf_op jit(solution)/shard_map/ppermute | solution.py:560
  39.5 0.0 copy-done.17
  39.6 3.4 %early.1 = (f32[512,1024]{1,0:T(8,128)}, f32[512,128]{1,0:T(8,128)}) custom-call(s32[1,768]{1,0:T(1,128)} %reshape.41.places_far, f32[512,1024]{1,0:T(8,128)} %centroids_far.1, bf16[96,1024]{1,0:T(8,128)(2,1)} %get-tuple-element.54.rest_0_, bf16[96,1024]{1,0:T(8,128)(2,1)} %copy-done.17), custom_call_target="tpu_custom_call" | custom-call | flops 10066329600 | bytes 104857600 | tf_op jit(solution)/shard_map/early/pallas_call | solution.py:442
  42.9 0.0 copy-done.5
  42.9 0.0 copy-done.3
  42.9 0.1 collective-permute-start.7
  43.0 0.0 copy-done.12
  43.0 0.5 collective-permute-start.8
  43.5 0.0 copy-done.16
  43.5 0.5 collective-permute-start.5
  44.0 0.0 copy-done.15
  44.0 0.1 collective-permute-start.6
  44.1 0.8 collective-permute-done.8.refs_5_
  44.9 0.0 collective-permute-done.7.refs_4_
  44.9 0.7 copy-done.13
  45.6 0.8 copy-done.4
  46.4 2.8 %pack.3 = (bf16[96,1024]{1,0:T(8,128)(2,1)}, bf16[96,1024]{1,0:T(8,128)(2,1)}, bf16[96,1024]{1,0:T(8,128)(2,1)}, bf16[96,1024]{1,0:T(8,128)(2,1)}) custom-call(s32[16,1,330]{2,1,0:T(1,128)} %copy-done.5, s32[16,1,330]{2,1,0:T(1,128)} %copy-done.5, bf16[160,1024]{1,0:T(8,128)(2,1)} %copy-done.3, bf16[94,1024]{1,0:T(8,128)(2,1)} %copy-done.12, ...), custom_call_target="tpu_custom_call" | custom-call | flops 199753728 | bytes 1826816 | tf_op jit(solution)/shard_map/pack/pallas_call | solution.py:319
  49.2 2.2 %collective-permute-start.9 = (bf16[96,1024]{1,0:T(8,128)(2,1)}, bf16[96,1024]{1,0:T(8,128)(2,1)S(1)}, u32[]{:S(2)}, u32[]{:S(2)}) collective-permute-start(bf16[96,1024]{1,0:T(8,128)(2,1)} %get-tuple-element.71), channel_id=1, source_target_pairs={{0,2},{1,3},{2,0},{3,1},{4,6},{5,7},{6,4},{7,5},{8,10},{9,11},{10,... | collective-permute-start | bytes 589832 | tf_op jit(solution)/shard_map/ppermute | solution.py:535
  51.4 0.5 collective-permute-start.10
  51.9 1.0 %collective-permute-start.11 = (bf16[96,1024]{1,0:T(8,128)(2,1)}, bf16[96,1024]{1,0:T(8,128)(2,1)S(1)}, u32[]{:S(2)}, u32[]{:S(2)}) collective-permute-start(bf16[96,1024]{1,0:T(8,128)(2,1)} %get-tuple-element.73), channel_id=1, source_target_pairs={{0,6},{1,7},{2,4},{3,5},{4,2},{5,3},{6,0},{7,1},{8,14},{9,15},{10,... | collective-permute-start | bytes 589832 | tf_op jit(solution)/shard_map/ppermute | solution.py:535
  52.9 0.1 slice.24
  53.0 0.7 reshape.42.late_far
  53.7 0.0 all-to-all-done.1
  53.7 0.9 %copy-done.1 = bf16[16,24,1024]{2,1,0:T(8,128)(2,1)} copy-done((bf16[16,24,1024]{2,1,0:T(8,128)(2,1)}, bf16[16,24,1024]{2,1,0:T(8,128)(2,1)S(1)}, u32[]{:S(2)}) %copy-start.1) | copy-done | bytes 786456
  54.6 5.0 %encode.1 = (bf16[2,1024]{1,0:T(2,128)(2,1)}, bf16[16,2,1024]{2,1,0:T(2,128)(2,1)}) custom-call(s32[1,2]{1,0:T(1,128)} %bitcast.27, s32[128,1]{1,0:T(8,128)} %get-tuple-element.38.refs_1_, bf16[384,1024]{1,0:T(8,128)(2,1)} %bitcast.15, bf16[64,1024]{1,0:T(8,128)(2,1)} %refs_3_.1, f32[1,1024]{1,0:T(1,128)} %bitcast.19, f32[1,1024]{1,0:T(1,128)} %bitcast.20, ...), custom_call_target="tpu_custom_call" | custom-call | flops 637534208 | bytes 6291456 | tf_op jit(solution)/shard_map/encode/pallas_call | solution.py:121
  59.6 6.0 %all-to-all-start.2 = ((bf16[16,2,1024]{2,1,0:T(2,128)(2,1)}), bf16[16,2,1024]{2,1,0:T(2,128)(2,1)S(1)}, u32[]{:S(2)}, u32[]{:S(2)}) async-start(bf16[16,2,1024]{2,1,0:T(2,128)(2,1)} %get-tuple-element.63), calls=%async_computation.2 | async-start | bytes 131072 | tf_op jit(solution)/shard_map/all_to_all | solution.py:606
  65.6 0.0 collective-permute-done.5.rest_0_
  65.6 0.0 copy-start.7
  65.6 0.0 collective-permute-done.6.rest_1_
  65.6 0.0 copy-start.8
  65.6 0.0 collective-permute-done.9.rest_3_
  65.7 0.0 collective-permute-done.10.rest_4_
  65.7 0.0 collective-permute-done.11.rest_5_
  65.7 0.0 copy-start.11
  65.7 6.8 %all-to-all-done.2.spread_far = bf16[16,2,1024]{2,1,0:T(2,128)(2,1)S(1)} async-done(((bf16[16,2,1024]{2,1,0:T(2,128)(2,1)}), bf16[16,2,1024]{2,1,0:T(2,128)(2,1)S(1)}, u32[]{:S(2)}, u32[]{:S(2)}) %all-to-all-start.2) | async-done | bytes 65568 | tf_op jit(solution)/shard_map/all_to_all | solution.py:606
  72.5 0.0 copy-done.9
  72.5 0.6 copy-done.6
  73.1 4.0 %late.1 = f32[512,1024]{1,0:T(8,128)} custom-call(s32[1,768]{1,0:T(1,128)} %reshape.41.places_far, s32[1,32]{1,0:T(1,128)} %reshape.42.late_far, bf16[16,2,1024]{2,1,0:T(2,128)(2,1)} %copy-done.6, f32[512,128]{1,0:T(8,128)} %get-tuple-element.64.share_far, f32[512,1024]{1,0:T(8,128)} %get-tuple-element.65.early_far, bf16[96,1024]{1,0:T(8,128)(2,1)} %copy-done.7, ...), custom_call_target="tpu_custom_call" | custom-call | flops 637534208 | bytes 4194304 | tf_op jit(solution)/shard_map/late/pallas_call | solution.py:474
  (19 shorter events, 0.0 us)
Async XLA Ops:
  0.6 25.0 %copy-start = (bf16[240,1024]{1,0:T(8,128)(2,1)S(1)}, bf16[240,1024]{1,0:T(8,128)(2,1)}, u32[]{:S(2)}) copy-start(bf16[240,1024]{1,0:T(8,128)(2,1)} %param.17) | copy-start | bytes 1474564
  0.6 9.5 %collective-permute-start.1 = (bf16[254,1024]{1,0:T(8,128)(2,1)}, bf16[254,1024]{1,0:T(8,128)(2,1)S(1)}, u32[]{:S(2)}, u32[]{:S(2)}) collective-permute-start(bf16[254,1024]{1,0:T(8,128)(2,1)} %refs_2_.1), channel_id=1, source_target_pairs={{0,1},{1,0},{2,3},{3,2},{4,5},{5,4},{6,7},{7,6},{8,9},{9,8},{10,11... | collective-permute-start | bytes 1560584 | tf_op jit(solution)/shard_map/ppermute | solution.py:539
  2.2 24.7 %collective-permute-start.2 = (bf16[160,1024]{1,0:T(8,128)(2,1)S(1)}, bf16[160,1024]{1,0:T(8,128)(2,1)S(1)}, u32[]{:S(2)}, u32[]{:S(2)}) collective-permute-start(bf16[160,1024]{1,0:T(8,128)(2,1)S(1)} %slice.17), channel_id=1, source_target_pairs={{0,8},{1,9},{2,10},{3,11},{4,12},{5,13},{6,14},{7,15},{8,0},{9,1},... | collective-permute-start | bytes 983048 | tf_op jit(solution)/shard_map/ppermute | solution.py:540
  5.9 1.4 %collective-permute-start = (s32[1,256]{1,0:T(1,128)}, s32[1,256]{1,0:T(1,128)S(1)}, u32[]{:S(2)}, u32[]{:S(2)}) collective-permute-start(s32[1,256]{1,0:T(1,128)} %bitcast.24), channel_id=1, source_target_pairs={{0,1},{1,0},{2,3},{3,2},{4,5},{5,4},{6,7},{7,6},{8,9},{9,8},{10,11... | collective-permute-start | bytes 3080 | tf_op jit(solution)/shard_map/ppermute | solution.py:543
  7.2 0.6 copy-start.14
  10.1 4.0 %copy-start.2 = (bf16[254,1024]{1,0:T(8,128)(2,1)}, bf16[254,1024]{1,0:T(8,128)(2,1)S(1)}, u32[]{:S(2)}) copy-start(bf16[254,1024]{1,0:T(8,128)(2,1)S(1)} %collective-permute-done.1.refs_3_) | copy-start | bytes 1560580
  10.1 12.6 %all-to-all-start = ((s32[16,1,330]{2,1,0:T(1,128)}), s32[16,1,330]{2,1,0:T(1,128)S(1)}, u32[]{:S(2)}, u32[]{:S(2)}) async-start(s32[16,1,330]{2,1,0:T(1,128)} %get-tuple-element.40), calls=%async_computation | async-start | bytes 49152 | tf_op jit(solution)/shard_map/all_to_all | solution.py:548
  16.8 10.1 %collective-permute-start.3 = (bf16[96,1024]{1,0:T(8,128)(2,1)}, bf16[96,1024]{1,0:T(8,128)(2,1)S(1)}, u32[]{:S(2)}, u32[]{:S(2)}) collective-permute-start(bf16[96,1024]{1,0:T(8,128)(2,1)} %get-tuple-element.47), channel_id=1, source_target_pairs={{0,2},{1,3},{2,0},{3,1},{4,6},{5,7},{6,4},{7,5},{8,10},{9,11},{10,... | collective-permute-start | bytes 589832 | tf_op jit(solution)/shard_map/ppermute | solution.py:535
  22.8 20.1 %copy-start.5 = (s32[16,1,330]{2,1,0:T(1,128)}, s32[16,1,330]{2,1,0:T(1,128)S(1)}, u32[]{:S(2)}) copy-start(s32[16,1,330]{2,1,0:T(1,128)S(1)} %all-to-all-done.refs_0_.refs_1_) | copy-start | bytes 63364
  22.9 16.7 %collective-permute-start.4 = (bf16[94,1024]{1,0:T(8,128)(2,1)}, bf16[94,1024]{1,0:T(8,128)(2,1)S(1)}, u32[]{:S(2)}, u32[]{:S(2)}) collective-permute-start(bf16[94,1024]{1,0:T(8,128)(2,1)} %get-tuple-element.52), channel_id=1, source_target_pairs={{0,8},{1,9},{2,10},{3,11},{4,12},{5,13},{6,14},{7,15},{8,0},{9,1},... | collective-permute-start | bytes 577544 | tf_op jit(solution)/shard_map/ppermute | solution.py:560
  26.9 16.0 %copy-start.3 = (bf16[160,1024]{1,0:T(8,128)(2,1)}, bf16[160,1024]{1,0:T(8,128)(2,1)S(1)}, u32[]{:S(2)}) copy-start(bf16[160,1024]{1,0:T(8,128)(2,1)S(1)} %collective-permute-done.2.refs_2_) | copy-start | bytes 983044
  26.9 12.6 %copy-start.17 = (bf16[96,1024]{1,0:T(8,128)(2,1)}, bf16[96,1024]{1,0:T(8,128)(2,1)S(1)}, u32[]{:S(2)}) copy-start(bf16[96,1024]{1,0:T(8,128)(2,1)S(1)} %collective-permute-done.3.rest_1_) | copy-start | bytes 589828
  26.9 26.8 %all-to-all-start.1 = ((bf16[16,24,1024]{2,1,0:T(8,128)(2,1)}), bf16[16,24,1024]{2,1,0:T(8,128)(2,1)S(1)}, u32[]{:S(2)}, u32[]{:S(2)}) async-start(bf16[16,24,1024]{2,1,0:T(8,128)(2,1)} %bitcast.4), calls=%async_computation.1 | async-start | bytes 1572864 | tf_op jit(solution)/shard_map/all_to_all | solution.py:571
  31.9 11.6 %copy-start.16 = (bf16[96,1024]{1,0:T(8,128)(2,1)S(1)}, bf16[96,1024]{1,0:T(8,128)(2,1)}, u32[]{:S(2)}) copy-start(bf16[96,1024]{1,0:T(8,128)(2,1)} %get-tuple-element.66) | copy-start | bytes 589828
  31.9 12.1 %copy-start.15 = (bf16[96,1024]{1,0:T(8,128)(2,1)S(1)}, bf16[96,1024]{1,0:T(8,128)(2,1)}, u32[]{:S(2)}) copy-start(bf16[96,1024]{1,0:T(8,128)(2,1)} %get-tuple-element.67) | copy-start | bytes 589828
  39.5 3.5 %copy-start.12 = (bf16[94,1024]{1,0:T(8,128)(2,1)}, bf16[94,1024]{1,0:T(8,128)(2,1)S(1)}, u32[]{:S(2)}) copy-start(bf16[94,1024]{1,0:T(8,128)(2,1)S(1)} %collective-permute-done.4.refs_3_) | copy-start | bytes 577540
  42.9 2.0 %collective-permute-start.7 = (bf16[160,1024]{1,0:T(8,128)(2,1)S(1)}, bf16[160,1024]{1,0:T(8,128)(2,1)S(1)}, u32[]{:S(2)}, u32[]{:S(2)}) collective-permute-start(bf16[160,1024]{1,0:T(8,128)(2,1)S(1)} %collective-permute-done.2.refs_2_), channel_id=1, source_target_pairs={{0,1},{1,0},{2,3},{3,2},{4,5},{5,4},{6,7},{7,6},{8,9},{9,8},{10,11... | collective-permute-start | bytes 983048 | tf_op jit(solution)/shard_map/ppermute | solution.py:583
  43.0 1.9 %collective-permute-start.8 = (bf16[94,1024]{1,0:T(8,128)(2,1)S(1)}, bf16[94,1024]{1,0:T(8,128)(2,1)S(1)}, u32[]{:S(2)}, u32[]{:S(2)}) collective-permute-start(bf16[94,1024]{1,0:T(8,128)(2,1)S(1)} %collective-permute-done.4.refs_3_), channel_id=1, source_target_pairs={{0,1},{1,0},{2,3},{3,2},{4,5},{5,4},{6,7},{7,6},{8,9},{9,8},{10,11... | collective-permute-start | bytes 577544 | tf_op jit(solution)/shard_map/ppermute | solution.py:583
  43.5 22.1 %collective-permute-start.5 = (bf16[96,1024]{1,0:T(8,128)(2,1)S(1)}, bf16[96,1024]{1,0:T(8,128)(2,1)S(1)}, u32[]{:S(2)}, u32[]{:S(2)}) collective-permute-start(bf16[96,1024]{1,0:T(8,128)(2,1)S(1)} %copy-done.16), channel_id=1, source_target_pairs={{0,4},{1,5},{2,6},{3,7},{4,0},{5,1},{6,2},{7,3},{8,12},{9,13},{10,... | collective-permute-start | bytes 589832 | tf_op jit(solution)/shard_map/ppermute | solution.py:535
  44.0 21.6 %collective-permute-start.6 = (bf16[96,1024]{1,0:T(8,128)(2,1)S(1)}, bf16[96,1024]{1,0:T(8,128)(2,1)S(1)}, u32[]{:S(2)}, u32[]{:S(2)}) collective-permute-start(bf16[96,1024]{1,0:T(8,128)(2,1)S(1)} %copy-done.15), channel_id=1, source_target_pairs={{0,6},{1,7},{2,4},{3,5},{4,2},{5,3},{6,0},{7,1},{8,14},{9,15},{10,... | collective-permute-start | bytes 589832 | tf_op jit(solution)/shard_map/ppermute | solution.py:535
  44.9 0.7 copy-start.13
  45.6 0.8 copy-start.4
  49.2 16.4 %collective-permute-start.9 = (bf16[96,1024]{1,0:T(8,128)(2,1)}, bf16[96,1024]{1,0:T(8,128)(2,1)S(1)}, u32[]{:S(2)}, u32[]{:S(2)}) collective-permute-start(bf16[96,1024]{1,0:T(8,128)(2,1)} %get-tuple-element.71), channel_id=1, source_target_pairs={{0,2},{1,3},{2,0},{3,1},{4,6},{5,7},{6,4},{7,5},{8,10},{9,11},{10,... | collective-permute-start | bytes 589832 | tf_op jit(solution)/shard_map/ppermute | solution.py:535
  51.4 14.3 %collective-permute-start.10 = (bf16[96,1024]{1,0:T(8,128)(2,1)}, bf16[96,1024]{1,0:T(8,128)(2,1)S(1)}, u32[]{:S(2)}, u32[]{:S(2)}) collective-permute-start(bf16[96,1024]{1,0:T(8,128)(2,1)} %get-tuple-element.72), channel_id=1, source_target_pairs={{0,4},{1,5},{2,6},{3,7},{4,0},{5,1},{6,2},{7,3},{8,12},{9,13},{10,... | collective-permute-start | bytes 589832 | tf_op jit(solution)/shard_map/ppermute | solution.py:535
  51.9 13.8 %collective-permute-start.11 = (bf16[96,1024]{1,0:T(8,128)(2,1)}, bf16[96,1024]{1,0:T(8,128)(2,1)S(1)}, u32[]{:S(2)}, u32[]{:S(2)}) collective-permute-start(bf16[96,1024]{1,0:T(8,128)(2,1)} %get-tuple-element.73), channel_id=1, source_target_pairs={{0,6},{1,7},{2,4},{3,5},{4,2},{5,3},{6,0},{7,1},{8,14},{9,15},{10,... | collective-permute-start | bytes 589832 | tf_op jit(solution)/shard_map/ppermute | solution.py:535
  53.7 0.9 %copy-start.1 = (bf16[16,24,1024]{2,1,0:T(8,128)(2,1)}, bf16[16,24,1024]{2,1,0:T(8,128)(2,1)S(1)}, u32[]{:S(2)}) copy-start(bf16[16,24,1024]{2,1,0:T(8,128)(2,1)S(1)} %all-to-all-done.1) | copy-start | bytes 2359300
  59.6 12.9 %all-to-all-start.2 = ((bf16[16,2,1024]{2,1,0:T(2,128)(2,1)}), bf16[16,2,1024]{2,1,0:T(2,128)(2,1)S(1)}, u32[]{:S(2)}, u32[]{:S(2)}) async-start(bf16[16,2,1024]{2,1,0:T(2,128)(2,1)} %get-tuple-element.63), calls=%async_computation.2 | async-start | bytes 131072 | tf_op jit(solution)/shard_map/all_to_all | solution.py:606
  65.6 6.9 %copy-start.7 = (bf16[96,1024]{1,0:T(8,128)(2,1)}, bf16[96,1024]{1,0:T(8,128)(2,1)S(1)}, u32[]{:S(2)}) copy-start(bf16[96,1024]{1,0:T(8,128)(2,1)S(1)} %collective-permute-done.5.rest_0_) | copy-start | bytes 589828
  65.6 6.9 %copy-start.8 = (bf16[96,1024]{1,0:T(8,128)(2,1)}, bf16[96,1024]{1,0:T(8,128)(2,1)S(1)}, u32[]{:S(2)}) copy-start(bf16[96,1024]{1,0:T(8,128)(2,1)S(1)} %collective-permute-done.6.rest_1_) | copy-start | bytes 589828
  65.6 6.9 %copy-start.9 = (bf16[96,1024]{1,0:T(8,128)(2,1)}, bf16[96,1024]{1,0:T(8,128)(2,1)S(1)}, u32[]{:S(2)}) copy-start(bf16[96,1024]{1,0:T(8,128)(2,1)S(1)} %collective-permute-done.9.rest_3_) | copy-start | bytes 589828
  65.7 6.8 %copy-start.10 = (bf16[96,1024]{1,0:T(8,128)(2,1)}, bf16[96,1024]{1,0:T(8,128)(2,1)S(1)}, u32[]{:S(2)}) copy-start(bf16[96,1024]{1,0:T(8,128)(2,1)S(1)} %collective-permute-done.10.rest_4_) | copy-start | bytes 589828
  65.7 6.8 %copy-start.11 = (bf16[96,1024]{1,0:T(8,128)(2,1)}, bf16[96,1024]{1,0:T(8,128)(2,1)S(1)}, u32[]{:S(2)}) copy-start(bf16[96,1024]{1,0:T(8,128)(2,1)S(1)} %collective-permute-done.11.rest_5_) | copy-start | bytes 589828
  72.5 0.6 copy-start.6

commit v22 on v21

--- a/solution.py
+++ b/solution.py
@@ -535,7 +535,7 @@
             got.append(lax.ppermute(blocks[step], "dp", moves))
         return got
 
-    ahead = store_count * 2 // 3 // 16 * 16
+    ahead = store_count * 3 // 4 // 16 * 16
     sibling_rows = lax.ppermute(stored_rows, "dp", beside)
     first_rows = lax.ppermute(stored_rows[:ahead], "dp", across)
     sizes = (peer_count, vocab_rows, token_cap, row_cap, row_count - store_count)

time: 77.6 us -> 75.6 us (0.974)
  waiting for transfers between devices: 20.4 us -> 16.6 us
  starting transfers between devices: 27.6 us -> 29.5 us
    ppermute x1, waiting for transfers between devices: 7.65 us -> 1.79 us  [shards(): last_rows = lax.ppermute(last_rows, 'dp', across)]
    ppermute x6, waiting for transfers between devices: 0.02 us -> 1.72 us  [hand_on(): got.append(lax.ppermute(blocks[step], 'dp', moves))]
    all_to_all x1, waiting for transfers between devices: 6.79 us -> 5.11 us  [shards(): lax.all_to_all(spread, 'dp', split_axis=0, concat_axis=0, tiled=True)]
    all_to_all x1, waiting for transfers between devices: 4.01 us -> 5.46 us  [shards(): codes = lax.all_to_all(plan, 'dp', split_axis=0, concat_axis=0, tiled=True)]
    all_to_all x1, waiting for transfers between devices: 0.01 us -> 1.35 us  [shards(): lax.all_to_all(found.reshape(peer_count, token_cap, width), 'dp', split_a...]
    ppermute x6, starting transfers between devices: 6.31 us -> 7.57 us  [hand_on(): got.append(lax.ppermute(blocks[step], 'dp', moves))]
  transfers between devices with their start and end apart: 15 -> 15, of which waited for: 5 -> 6; matrix products, arithmetic and copies ran while one was open for 6% -> 6% of each run, Pallas kernels for 21% -> 21%
where the time goes in v22:
time: 75.6 us; the launch traced here: 75.2 us
  starting transfers between devices  29.5 us (39%)
  Pallas kernels  20.2 us (27%)
  waiting for transfers between devices  16.6 us (22%)
  local copies, waits for them, and re-layouts  6.67 us (9%)
  matrix products  1.29 us (2%)
  between operations  0.91 us (1%)
    ppermute x6, starting transfers between devices, hand_on(): got.append(lax.ppermute(blocks[step], 'dp', moves))  7.57 us
    all_to_all x1, starting transfers between devices, shards(): lax.all_to_all(spread, 'dp', split_axis=0, concat_axis=0, tiled=True)  6.71 us
    pallas_call x2, Pallas kernels, pack_rows(): pl.pallas_call(functools.partial(pack_kernel, half, row_cap, count, picks...  5.49 us
    all_to_all x1, waiting for transfers between devices, shards(): codes = lax.all_to_all(plan, 'dp', split_axis=0, concat_axis=0, tiled=True)  5.46 us
    all_to_all x1, waiting for transfers between devices, shards(): lax.all_to_all(spread, 'dp', split_axis=0, concat_axis=0, tiled=True)  5.11 us
    pallas_call x1, Pallas kernels, encode(): pl.pallas_call(encode_kernel, out_shape=[jax.ShapeDtypeStruct((passes, wi...  4.99 us
    pallas_call x1, Pallas kernels, late_update(): pl.pallas_call(late_kernel, out_shape=jax.ShapeDtypeStruct(early.shape, j...  4 us
    all_to_all x1, starting transfers between devices, shards(): codes = lax.all_to_all(plan, 'dp', split_axis=0, concat_axis=0, tiled=True)  3.92 us
  transfers between devices with their start and end apart: 15, of which 6 were waited for; matrix products, arithmetic and copies ran while one was open for 6% of the time, Pallas kernels for 21%

profile of v22, /device:TPU:0, one launch (start us, length us, event | category | flops | bytes accessed | tf_op | source)
XLA Modules:
  0.0 75.2 jit_solution(6431905463754687346)
XLA Ops:
  0.6 0.0 copy-start
  0.6 0.5 collective-permute-start.1
  1.2 1.0 %slice.17 = bf16[176,1024]{1,0:T(8,128)(2,1)S(1)} slice(bf16[254,1024]{1,0:T(8,128)(2,1)} %refs_2_.1), slice={[0:176], [0:1024]} | slice | bytes 720896 | tf_op jit(solution)/shard_map/slice | solution.py:540
  2.2 3.7 %collective-permute-start.2 = (bf16[176,1024]{1,0:T(8,128)(2,1)S(1)}, bf16[176,1024]{1,0:T(8,128)(2,1)S(1)}, u32[]{:S(2)}, u32[]{:S(2)}) collective-permute-start(bf16[176,1024]{1,0:T(8,128)(2,1)S(1)} %slice.17), channel_id=1, source_target_pairs={{0,8},{1,9},{2,10},{3,11},{4,12},{5,13},{6,14},{7,15},{8,0},{9,1},... | collective-permute-start | bytes 1081352 | tf_op jit(solution)/shard_map/ppermute | solution.py:540
  5.9 0.2 collective-permute-start
  6.1 1.2 %collective-permute-done.sibling_far = s32[1,256]{1,0:T(1,128)S(1)} collective-permute-done((s32[1,256]{1,0:T(1,128)}, s32[1,256]{1,0:T(1,128)S(1)}, u32[]{:S(2)}, u32[]{:S(2)}) %collective-permute-start) | collective-permute-done | bytes 1056 | tf_op jit(solution)/shard_map/ppermute | solution.py:543
  7.2 0.6 copy-done.14
  7.8 2.3 %route.1 = (s32[16,1,330]{2,1,0:T(1,128)}, s32[128,1]{1,0:T(8,128)}, s32[1,256]{1,0:T(1,128)}, s32[1,256]{1,0:T(1,128)}) custom-call(s32[2,64]{1,0:T(2,128)} %token_ids_far.1, s32[1,256]{1,0:T(1,128)} %bitcast.25, s32[1,256]{1,0:T(1,128)} %bitcast.26, s32[1,256]{1,0:T(1,128)} %copy-done.14), custom_call_target="tpu_custom_call" | custom-call | tf_op jit(solution)/shard_map/route/pallas_call | solution.py:228
  10.1 0.0 collective-permute-done.1.refs_3_
  10.1 0.0 copy-start.2
  10.1 3.9 %all-to-all-start = ((s32[16,1,330]{2,1,0:T(1,128)}), s32[16,1,330]{2,1,0:T(1,128)S(1)}, u32[]{:S(2)}, u32[]{:S(2)}) async-start(s32[16,1,330]{2,1,0:T(1,128)} %get-tuple-element.40), calls=%async_computation | async-start | bytes 49152 | tf_op jit(solution)/shard_map/all_to_all | solution.py:548
  14.1 0.0 copy-done.2
  14.1 2.6 %pack.2 = (bf16[96,1024]{1,0:T(8,128)(2,1)}, bf16[96,1024]{1,0:T(8,128)(2,1)}, bf16[96,1024]{1,0:T(8,128)(2,1)}, bf16[96,1024]{1,0:T(8,128)(2,1)}, bf16[78,1024]{1,0:T(8,128)(2,1)}) custom-call(s32[1,256]{1,0:T(1,128)} %get-tuple-element.41.refs_0_, s32[1,256]{1,0:T(1,128)} %get-tuple-element.42.refs_1_, bf16[254,1024]{1,0:T(8,128)(2,1)} %refs_2_.1, ...), custom_call_target="tpu_custom_call" | custom-call | flops 199753728 | bytes 1826816 | tf_op jit(solution)/shard_map/pack/pallas_call | solution.py:319
  16.7 2.0 %collective-permute-start.3 = (bf16[96,1024]{1,0:T(8,128)(2,1)}, bf16[96,1024]{1,0:T(8,128)(2,1)S(1)}, u32[]{:S(2)}, u32[]{:S(2)}) collective-permute-start(bf16[96,1024]{1,0:T(8,128)(2,1)} %get-tuple-element.47), channel_id=1, source_target_pairs={{0,2},{1,3},{2,0},{3,1},{4,6},{5,7},{6,4},{7,5},{8,10},{9,11},{10,... | collective-permute-start | bytes 589832 | tf_op jit(solution)/shard_map/ppermute | solution.py:535
  18.7 5.5 %all-to-all-done.refs_0_.refs_1_ = s32[16,1,330]{2,1,0:T(1,128)S(1)} async-done(((s32[16,1,330]{2,1,0:T(1,128)}), s32[16,1,330]{2,1,0:T(1,128)S(1)}, u32[]{:S(2)}, u32[]{:S(2)}) %all-to-all-start) | async-done | bytes 21152 | tf_op jit(solution)/shard_map/all_to_all | solution.py:548
  24.2 0.1 eq.15
  24.3 2.7 %collective-permute-start.4 = (bf16[78,1024]{1,0:T(8,128)(2,1)}, bf16[78,1024]{1,0:T(8,128)(2,1)S(1)}, u32[]{:S(2)}, u32[]{:S(2)}) collective-permute-start(bf16[78,1024]{1,0:T(8,128)(2,1)} %get-tuple-element.52), channel_id=1, source_target_pairs={{0,8},{1,9},{2,10},{3,11},{4,12},{5,13},{6,14},{7,15},{8,0},{9,1},... | collective-permute-start | bytes 479240 | tf_op jit(solution)/shard_map/ppermute | solution.py:560
  27.0 0.0 copy-done
  27.0 1.3 %convolution_convert_fusion = bf16[384,1024]{1,0:T(8,128)(2,1)} fusion(bf16[240,1024]{1,0:T(8,128)(2,1)S(1)} %copy-done, s32[384]{0:T(512)S(1)} %eq.15), kind=kOutput, calls=%fused_computation.1 | convolution fusion | flops 189229056 | bytes 1279488 | tf_op jit(solution)/shard_map/dot_general | solution.py:565
  28.3 0.0 collective-permute-done.2.refs_2_
  28.3 0.0 collective-permute-done.3.rest_1_
  28.3 0.0 copy-start.17
  28.3 3.6 %all-to-all-start.1 = ((bf16[16,24,1024]{2,1,0:T(8,128)(2,1)}), bf16[16,24,1024]{2,1,0:T(8,128)(2,1)S(1)}, u32[]{:S(2)}, u32[]{:S(2)}) async-start(bf16[16,24,1024]{2,1,0:T(8,128)(2,1)} %bitcast.4), calls=%async_computation.1 | async-start | bytes 1572864 | tf_op jit(solution)/shard_map/all_to_all | solution.py:571
  32.0 0.1 slice.23
  32.1 0.6 gather_fusion
  32.6 0.7 reshape.41.places_far
  33.3 1.8 %collective-permute-done.4.refs_3_ = bf16[78,1024]{1,0:T(8,128)(2,1)S(1)} collective-permute-done((bf16[78,1024]{1,0:T(8,128)(2,1)}, bf16[78,1024]{1,0:T(8,128)(2,1)S(1)}, u32[]{:S(2)}, u32[]{:S(2)}) %collective-permute-start.4) | collective-permute-done | bytes 159776 | tf_op jit(solution)/shard_map/ppermute | solution.py:560
  35.1 0.0 copy-done.17
  35.1 3.4 %early.1 = (f32[512,1024]{1,0:T(8,128)}, f32[512,128]{1,0:T(8,128)}) custom-call(s32[1,768]{1,0:T(1,128)} %reshape.41.places_far, f32[512,1024]{1,0:T(8,128)} %centroids_far.1, bf16[96,1024]{1,0:T(8,128)(2,1)} %get-tuple-element.54.rest_0_, bf16[96,1024]{1,0:T(8,128)(2,1)} %copy-done.17), custom_call_target="tpu_custom_call" | custom-call | flops 10066329600 | bytes 104857600 | tf_op jit(solution)/shard_map/early/pallas_call | solution.py:442
  38.5 0.0 copy-done.5
  38.5 0.0 copy-done.3
  38.5 0.1 collective-permute-start.7
  38.6 0.0 copy-done.12
  38.6 0.5 collective-permute-start.8
  39.1 0.0 copy-done.16
  39.1 0.7 collective-permute-start.5
  39.8 0.0 copy-done.15
  39.8 1.3 %collective-permute-start.6 = (bf16[96,1024]{1,0:T(8,128)(2,1)S(1)}, bf16[96,1024]{1,0:T(8,128)(2,1)S(1)}, u32[]{:S(2)}, u32[]{:S(2)}) collective-permute-start(bf16[96,1024]{1,0:T(8,128)(2,1)S(1)} %copy-done.15), channel_id=1, source_target_pairs={{0,6},{1,7},{2,4},{3,5},{4,2},{5,3},{6,0},{7,1},{8,14},{9,15},{10,... | collective-permute-start | bytes 589832 | tf_op jit(solution)/shard_map/ppermute | solution.py:535
  41.1 0.0 collective-permute-done.8.refs_5_
  41.1 0.0 collective-permute-done.7.refs_4_
  41.1 0.7 copy-done.13
  41.8 0.7 copy-done.4
  42.5 2.8 %pack.3 = (bf16[96,1024]{1,0:T(8,128)(2,1)}, bf16[96,1024]{1,0:T(8,128)(2,1)}, bf16[96,1024]{1,0:T(8,128)(2,1)}, bf16[96,1024]{1,0:T(8,128)(2,1)}) custom-call(s32[16,1,330]{2,1,0:T(1,128)} %copy-done.5, s32[16,1,330]{2,1,0:T(1,128)} %copy-done.5, bf16[176,1024]{1,0:T(8,128)(2,1)} %copy-done.3, bf16[78,1024]{1,0:T(8,128)(2,1)} %copy-done.12, ...), custom_call_target="tpu_custom_call" | custom-call | flops 199753728 | bytes 1826816 | tf_op jit(solution)/shard_map/pack/pallas_call | solution.py:319
  45.4 1.5 %collective-permute-start.9 = (bf16[96,1024]{1,0:T(8,128)(2,1)}, bf16[96,1024]{1,0:T(8,128)(2,1)S(1)}, u32[]{:S(2)}, u32[]{:S(2)}) collective-permute-start(bf16[96,1024]{1,0:T(8,128)(2,1)} %get-tuple-element.71), channel_id=1, source_target_pairs={{0,2},{1,3},{2,0},{3,1},{4,6},{5,7},{6,4},{7,5},{8,10},{9,11},{10,... | collective-permute-start | bytes 589832 | tf_op jit(solution)/shard_map/ppermute | solution.py:535
  46.9 0.7 collective-permute-start.10
  47.6 1.3 %collective-permute-start.11 = (bf16[96,1024]{1,0:T(8,128)(2,1)}, bf16[96,1024]{1,0:T(8,128)(2,1)S(1)}, u32[]{:S(2)}, u32[]{:S(2)}) collective-permute-start(bf16[96,1024]{1,0:T(8,128)(2,1)} %get-tuple-element.73), channel_id=1, source_target_pairs={{0,6},{1,7},{2,4},{3,5},{4,2},{5,3},{6,0},{7,1},{8,14},{9,15},{10,... | collective-permute-start | bytes 589832 | tf_op jit(solution)/shard_map/ppermute | solution.py:535
  49.0 0.1 slice.24
  49.0 0.7 reshape.42.late_far
  49.7 1.4 %all-to-all-done.1 = bf16[16,24,1024]{2,1,0:T(8,128)(2,1)S(1)} async-done(((bf16[16,24,1024]{2,1,0:T(8,128)(2,1)}), bf16[16,24,1024]{2,1,0:T(8,128)(2,1)S(1)}, u32[]{:S(2)}, u32[]{:S(2)}) %all-to-all-start.1) | async-done | bytes 786464 | tf_op jit(solution)/shard_map/all_to_all | solution.py:571
  51.1 0.9 %copy-done.1 = bf16[16,24,1024]{2,1,0:T(8,128)(2,1)} copy-done((bf16[16,24,1024]{2,1,0:T(8,128)(2,1)}, bf16[16,24,1024]{2,1,0:T(8,128)(2,1)S(1)}, u32[]{:S(2)}) %copy-start.1) | copy-done | bytes 786456
  51.9 5.0 %encode.1 = (bf16[2,1024]{1,0:T(2,128)(2,1)}, bf16[16,2,1024]{2,1,0:T(2,128)(2,1)}) custom-call(s32[1,2]{1,0:T(1,128)} %bitcast.27, s32[128,1]{1,0:T(8,128)} %get-tuple-element.38.refs_1_, bf16[384,1024]{1,0:T(8,128)(2,1)} %bitcast.15, bf16[64,1024]{1,0:T(8,128)(2,1)} %refs_3_.1, f32[1,1024]{1,0:T(1,128)} %bitcast.19, f32[1,1024]{1,0:T(1,128)} %bitcast.20, ...), custom_call_target="tpu_custom_call" | custom-call | flops 637534208 | bytes 6291456 | tf_op jit(solution)/shard_map/encode/pallas_call | solution.py:121
  56.9 6.7 %all-to-all-start.2 = ((bf16[16,2,1024]{2,1,0:T(2,128)(2,1)}), bf16[16,2,1024]{2,1,0:T(2,128)(2,1)S(1)}, u32[]{:S(2)}, u32[]{:S(2)}) async-start(bf16[16,2,1024]{2,1,0:T(2,128)(2,1)} %get-tuple-element.63), calls=%async_computation.2 | async-start | bytes 131072 | tf_op jit(solution)/shard_map/all_to_all | solution.py:606
  63.7 0.0 collective-permute-done.5.rest_0_
  63.7 0.0 copy-start.7
  63.7 0.0 collective-permute-done.6.rest_1_
  63.7 0.0 copy-start.8
  63.7 0.0 collective-permute-done.9.rest_3_
  63.7 0.0 copy-start.9
  63.7 0.0 collective-permute-done.10.rest_4_
  63.7 0.0 copy-start.10
  63.7 1.7 %collective-permute-done.11.rest_5_ = bf16[96,1024]{1,0:T(8,128)(2,1)S(1)} collective-permute-done((bf16[96,1024]{1,0:T(8,128)(2,1)}, bf16[96,1024]{1,0:T(8,128)(2,1)S(1)}, u32[]{:S(2)}, u32[]{:S(2)}) %collective-permute-start.11) | collective-permute-done | bytes 196640 | tf_op jit(solution)/shard_map/ppermute | solution.py:535
  65.4 5.1 %all-to-all-done.2.spread_far = bf16[16,2,1024]{2,1,0:T(2,128)(2,1)S(1)} async-done(((bf16[16,2,1024]{2,1,0:T(2,128)(2,1)}), bf16[16,2,1024]{2,1,0:T(2,128)(2,1)S(1)}, u32[]{:S(2)}, u32[]{:S(2)}) %all-to-all-start.2) | async-done | bytes 65568 | tf_op jit(solution)/shard_map/all_to_all | solution.py:606
  70.6 0.6 copy-done.6
  71.2 4.0 %late.1 = f32[512,1024]{1,0:T(8,128)} custom-call(s32[1,768]{1,0:T(1,128)} %reshape.41.places_far, s32[1,32]{1,0:T(1,128)} %reshape.42.late_far, bf16[16,2,1024]{2,1,0:T(2,128)(2,1)} %copy-done.6, f32[512,128]{1,0:T(8,128)} %get-tuple-element.64.share_far, f32[512,1024]{1,0:T(8,128)} %get-tuple-element.65.early_far, bf16[96,1024]{1,0:T(8,128)(2,1)} %copy-done.7, ...), custom_call_target="tpu_custom_call" | custom-call | flops 637534208 | bytes 4194304 | tf_op jit(solution)/shard_map/late/pallas_call | solution.py:474
  (19 shorter events, 0.0 us)
Async XLA Ops:
  0.6 26.4 %copy-start = (bf16[240,1024]{1,0:T(8,128)(2,1)S(1)}, bf16[240,1024]{1,0:T(8,128)(2,1)}, u32[]{:S(2)}) copy-start(bf16[240,1024]{1,0:T(8,128)(2,1)} %param.17) | copy-start | bytes 1474564
  0.6 9.5 %collective-permute-start.1 = (bf16[254,1024]{1,0:T(8,128)(2,1)}, bf16[254,1024]{1,0:T(8,128)(2,1)S(1)}, u32[]{:S(2)}, u32[]{:S(2)}) collective-permute-start(bf16[254,1024]{1,0:T(8,128)(2,1)} %refs_2_.1), channel_id=1, source_target_pairs={{0,1},{1,0},{2,3},{3,2},{4,5},{5,4},{6,7},{7,6},{8,9},{9,8},{10,11... | collective-permute-start | bytes 1560584 | tf_op jit(solution)/shard_map/ppermute | solution.py:539
  2.2 26.1 %collective-permute-start.2 = (bf16[176,1024]{1,0:T(8,128)(2,1)S(1)}, bf16[176,1024]{1,0:T(8,128)(2,1)S(1)}, u32[]{:S(2)}, u32[]{:S(2)}) collective-permute-start(bf16[176,1024]{1,0:T(8,128)(2,1)S(1)} %slice.17), channel_id=1, source_target_pairs={{0,8},{1,9},{2,10},{3,11},{4,12},{5,13},{6,14},{7,15},{8,0},{9,1},... | collective-permute-start | bytes 1081352 | tf_op jit(solution)/shard_map/ppermute | solution.py:540
  5.9 1.4 %collective-permute-start = (s32[1,256]{1,0:T(1,128)}, s32[1,256]{1,0:T(1,128)S(1)}, u32[]{:S(2)}, u32[]{:S(2)}) collective-permute-start(s32[1,256]{1,0:T(1,128)} %bitcast.24), channel_id=1, source_target_pairs={{0,1},{1,0},{2,3},{3,2},{4,5},{5,4},{6,7},{7,6},{8,9},{9,8},{10,11... | collective-permute-start | bytes 3080 | tf_op jit(solution)/shard_map/ppermute | solution.py:543
  7.2 0.6 copy-start.14
  10.1 4.0 %copy-start.2 = (bf16[254,1024]{1,0:T(8,128)(2,1)}, bf16[254,1024]{1,0:T(8,128)(2,1)S(1)}, u32[]{:S(2)}) copy-start(bf16[254,1024]{1,0:T(8,128)(2,1)S(1)} %collective-permute-done.1.refs_3_) | copy-start | bytes 1560580
  10.1 14.0 %all-to-all-start = ((s32[16,1,330]{2,1,0:T(1,128)}), s32[16,1,330]{2,1,0:T(1,128)S(1)}, u32[]{:S(2)}, u32[]{:S(2)}) async-start(s32[16,1,330]{2,1,0:T(1,128)} %get-tuple-element.40), calls=%async_computation | async-start | bytes 49152 | tf_op jit(solution)/shard_map/all_to_all | solution.py:548
  16.7 11.6 %collective-permute-start.3 = (bf16[96,1024]{1,0:T(8,128)(2,1)}, bf16[96,1024]{1,0:T(8,128)(2,1)S(1)}, u32[]{:S(2)}, u32[]{:S(2)}) collective-permute-start(bf16[96,1024]{1,0:T(8,128)(2,1)} %get-tuple-element.47), channel_id=1, source_target_pairs={{0,2},{1,3},{2,0},{3,1},{4,6},{5,7},{6,4},{7,5},{8,10},{9,11},{10,... | collective-permute-start | bytes 589832 | tf_op jit(solution)/shard_map/ppermute | solution.py:535
  24.2 14.3 %copy-start.5 = (s32[16,1,330]{2,1,0:T(1,128)}, s32[16,1,330]{2,1,0:T(1,128)S(1)}, u32[]{:S(2)}) copy-start(s32[16,1,330]{2,1,0:T(1,128)S(1)} %all-to-all-done.refs_0_.refs_1_) | copy-start | bytes 63364
  24.3 10.8 %collective-permute-start.4 = (bf16[78,1024]{1,0:T(8,128)(2,1)}, bf16[78,1024]{1,0:T(8,128)(2,1)S(1)}, u32[]{:S(2)}, u32[]{:S(2)}) collective-permute-start(bf16[78,1024]{1,0:T(8,128)(2,1)} %get-tuple-element.52), channel_id=1, source_target_pairs={{0,8},{1,9},{2,10},{3,11},{4,12},{5,13},{6,14},{7,15},{8,0},{9,1},... | collective-permute-start | bytes 479240 | tf_op jit(solution)/shard_map/ppermute | solution.py:560
  28.3 10.2 %copy-start.3 = (bf16[176,1024]{1,0:T(8,128)(2,1)}, bf16[176,1024]{1,0:T(8,128)(2,1)S(1)}, u32[]{:S(2)}) copy-start(bf16[176,1024]{1,0:T(8,128)(2,1)S(1)} %collective-permute-done.2.refs_2_) | copy-start | bytes 1081348
  28.3 6.8 %copy-start.17 = (bf16[96,1024]{1,0:T(8,128)(2,1)}, bf16[96,1024]{1,0:T(8,128)(2,1)S(1)}, u32[]{:S(2)}) copy-start(bf16[96,1024]{1,0:T(8,128)(2,1)S(1)} %collective-permute-done.3.rest_1_) | copy-start | bytes 589828
  28.3 22.7 %all-to-all-start.1 = ((bf16[16,24,1024]{2,1,0:T(8,128)(2,1)}), bf16[16,24,1024]{2,1,0:T(8,128)(2,1)S(1)}, u32[]{:S(2)}, u32[]{:S(2)}) async-start(bf16[16,24,1024]{2,1,0:T(8,128)(2,1)} %bitcast.4), calls=%async_computation.1 | async-start | bytes 1572864 | tf_op jit(solution)/shard_map/all_to_all | solution.py:571
  33.3 5.8 %copy-start.16 = (bf16[96,1024]{1,0:T(8,128)(2,1)S(1)}, bf16[96,1024]{1,0:T(8,128)(2,1)}, u32[]{:S(2)}) copy-start(bf16[96,1024]{1,0:T(8,128)(2,1)} %get-tuple-element.66) | copy-start | bytes 589828
  33.3 6.5 %copy-start.15 = (bf16[96,1024]{1,0:T(8,128)(2,1)S(1)}, bf16[96,1024]{1,0:T(8,128)(2,1)}, u32[]{:S(2)}) copy-start(bf16[96,1024]{1,0:T(8,128)(2,1)} %get-tuple-element.67) | copy-start | bytes 589828
  35.1 3.5 %copy-start.12 = (bf16[78,1024]{1,0:T(8,128)(2,1)}, bf16[78,1024]{1,0:T(8,128)(2,1)S(1)}, u32[]{:S(2)}) copy-start(bf16[78,1024]{1,0:T(8,128)(2,1)S(1)} %collective-permute-done.4.refs_3_) | copy-start | bytes 479236
  38.5 2.6 %collective-permute-start.7 = (bf16[176,1024]{1,0:T(8,128)(2,1)S(1)}, bf16[176,1024]{1,0:T(8,128)(2,1)S(1)}, u32[]{:S(2)}, u32[]{:S(2)}) collective-permute-start(bf16[176,1024]{1,0:T(8,128)(2,1)S(1)} %collective-permute-done.2.refs_2_), channel_id=1, source_target_pairs={{0,1},{1,0},{2,3},{3,2},{4,5},{5,4},{6,7},{7,6},{8,9},{9,8},{10,11... | collective-permute-start | bytes 1081352 | tf_op jit(solution)/shard_map/ppermute | solution.py:583
  38.6 2.5 %collective-permute-start.8 = (bf16[78,1024]{1,0:T(8,128)(2,1)S(1)}, bf16[78,1024]{1,0:T(8,128)(2,1)S(1)}, u32[]{:S(2)}, u32[]{:S(2)}) collective-permute-start(bf16[78,1024]{1,0:T(8,128)(2,1)S(1)} %collective-permute-done.4.refs_3_), channel_id=1, source_target_pairs={{0,1},{1,0},{2,3},{3,2},{4,5},{5,4},{6,7},{7,6},{8,9},{9,8},{10,11... | collective-permute-start | bytes 479240 | tf_op jit(solution)/shard_map/ppermute | solution.py:583
  39.1 24.6 %collective-permute-start.5 = (bf16[96,1024]{1,0:T(8,128)(2,1)S(1)}, bf16[96,1024]{1,0:T(8,128)(2,1)S(1)}, u32[]{:S(2)}, u32[]{:S(2)}) collective-permute-start(bf16[96,1024]{1,0:T(8,128)(2,1)S(1)} %copy-done.16), channel_id=1, source_target_pairs={{0,4},{1,5},{2,6},{3,7},{4,0},{5,1},{6,2},{7,3},{8,12},{9,13},{10,... | collective-permute-start | bytes 589832 | tf_op jit(solution)/shard_map/ppermute | solution.py:535
  39.8 23.9 %collective-permute-start.6 = (bf16[96,1024]{1,0:T(8,128)(2,1)S(1)}, bf16[96,1024]{1,0:T(8,128)(2,1)S(1)}, u32[]{:S(2)}, u32[]{:S(2)}) collective-permute-start(bf16[96,1024]{1,0:T(8,128)(2,1)S(1)} %copy-done.15), channel_id=1, source_target_pairs={{0,6},{1,7},{2,4},{3,5},{4,2},{5,3},{6,0},{7,1},{8,14},{9,15},{10,... | collective-permute-start | bytes 589832 | tf_op jit(solution)/shard_map/ppermute | solution.py:535
  41.1 0.7 copy-start.13
  41.8 0.7 copy-start.4
  45.4 18.3 %collective-permute-start.9 = (bf16[96,1024]{1,0:T(8,128)(2,1)}, bf16[96,1024]{1,0:T(8,128)(2,1)S(1)}, u32[]{:S(2)}, u32[]{:S(2)}) collective-permute-start(bf16[96,1024]{1,0:T(8,128)(2,1)} %get-tuple-element.71), channel_id=1, source_target_pairs={{0,2},{1,3},{2,0},{3,1},{4,6},{5,7},{6,4},{7,5},{8,10},{9,11},{10,... | collective-permute-start | bytes 589832 | tf_op jit(solution)/shard_map/ppermute | solution.py:535
  46.9 16.8 %collective-permute-start.10 = (bf16[96,1024]{1,0:T(8,128)(2,1)}, bf16[96,1024]{1,0:T(8,128)(2,1)S(1)}, u32[]{:S(2)}, u32[]{:S(2)}) collective-permute-start(bf16[96,1024]{1,0:T(8,128)(2,1)} %get-tuple-element.72), channel_id=1, source_target_pairs={{0,4},{1,5},{2,6},{3,7},{4,0},{5,1},{6,2},{7,3},{8,12},{9,13},{10,... | collective-permute-start | bytes 589832 | tf_op jit(solution)/shard_map/ppermute | solution.py:535
  47.6 17.8 %collective-permute-start.11 = (bf16[96,1024]{1,0:T(8,128)(2,1)}, bf16[96,1024]{1,0:T(8,128)(2,1)S(1)}, u32[]{:S(2)}, u32[]{:S(2)}) collective-permute-start(bf16[96,1024]{1,0:T(8,128)(2,1)} %get-tuple-element.73), channel_id=1, source_target_pairs={{0,6},{1,7},{2,4},{3,5},{4,2},{5,3},{6,0},{7,1},{8,14},{9,15},{10,... | collective-permute-start | bytes 589832 | tf_op jit(solution)/shard_map/ppermute | solution.py:535
  51.1 0.9 %copy-start.1 = (bf16[16,24,1024]{2,1,0:T(8,128)(2,1)}, bf16[16,24,1024]{2,1,0:T(8,128)(2,1)S(1)}, u32[]{:S(2)}) copy-start(bf16[16,24,1024]{2,1,0:T(8,128)(2,1)S(1)} %all-to-all-done.1) | copy-start | bytes 2359300
  56.9 13.6 %all-to-all-start.2 = ((bf16[16,2,1024]{2,1,0:T(2,128)(2,1)}), bf16[16,2,1024]{2,1,0:T(2,128)(2,1)S(1)}, u32[]{:S(2)}, u32[]{:S(2)}) async-start(bf16[16,2,1024]{2,1,0:T(2,128)(2,1)} %get-tuple-element.63), calls=%async_computation.2 | async-start | bytes 131072 | tf_op jit(solution)/shard_map/all_to_all | solution.py:606
  63.7 6.9 %copy-start.7 = (bf16[96,1024]{1,0:T(8,128)(2,1)}, bf16[96,1024]{1,0:T(8,128)(2,1)S(1)}, u32[]{:S(2)}) copy-start(bf16[96,1024]{1,0:T(8,128)(2,1)S(1)} %collective-permute-done.5.rest_0_) | copy-start | bytes 589828
  63.7 6.9 %copy-start.8 = (bf16[96,1024]{1,0:T(8,128)(2,1)}, bf16[96,1024]{1,0:T(8,128)(2,1)S(1)}, u32[]{:S(2)}) copy-start(bf16[96,1024]{1,0:T(8,128)(2,1)S(1)} %collective-permute-done.6.rest_1_) | copy-start | bytes 589828
  63.7 6.9 %copy-start.9 = (bf16[96,1024]{1,0:T(8,128)(2,1)}, bf16[96,1024]{1,0:T(8,128)(2,1)S(1)}, u32[]{:S(2)}) copy-start(bf16[96,1024]{1,0:T(8,128)(2,1)S(1)} %collective-permute-done.9.rest_3_) | copy-start | bytes 589828
  63.7 6.8 %copy-start.10 = (bf16[96,1024]{1,0:T(8,128)(2,1)}, bf16[96,1024]{1,0:T(8,128)(2,1)S(1)}, u32[]{:S(2)}) copy-start(bf16[96,1024]{1,0:T(8,128)(2,1)S(1)} %collective-permute-done.10.rest_4_) | copy-start | bytes 589828
  65.4 5.1 %copy-start.11 = (bf16[96,1024]{1,0:T(8,128)(2,1)}, bf16[96,1024]{1,0:T(8,128)(2,1)S(1)}, u32[]{:S(2)}) copy-start(bf16[96,1024]{1,0:T(8,128)(2,1)S(1)} %collective-permute-done.11.rest_5_) | copy-start | bytes 589828
  70.6 0.6 copy-start.6

commit v23 on v22

--- a/solution.py
+++ b/solution.py
@@ -576,7 +576,7 @@
     got_places = plan[:, token_cap : token_cap + row_cap][sources].reshape(half, 2 * row_cap)
     spare = padded(2 * row_cap) - 2 * row_cap
     got_places = jnp.pad(got_places, ((0, 0), (0, spare)), constant_values=-1).reshape(1, -1)
-    near_rows, last_rows = lax.optimization_barrier((own_half[:2], last_rows))
+    near_rows, last_rows = lax.optimization_barrier((own_half, last_rows))
     means, share = early_update(got_places, centroids, near_rows)
     first_rows, last_rows, means = lax.optimization_barrier((first_rows, last_rows, means))
     partner_rows = [first_rows, last_rows]
@@ -606,8 +606,7 @@
     all_embeds = lax.all_to_all(
         spread, "dp", split_axis=0, concat_axis=0, tiled=True
     )
-    pieces = own_half[2:] + other_half
-    new_centroids = late_update(got_places, late_places, all_embeds, share, means, pieces)
+    new_centroids = late_update(got_places, late_places, all_embeds, share, means, other_half)
     return (passage_embed, new_centroids)
 
 

time: 75.6 us -> 76.5 us (1.012)
  waiting for transfers between devices: 16.6 us -> 17.4 us
    all_to_all x1, waiting for transfers between devices: 5.11 us -> 6.83 us  [shards(): lax.all_to_all(spread, 'dp', split_axis=0, concat_axis=0, tiled=True)]
    ppermute x2, waiting for transfers between devices: 0.01 us -> 1.4 us  [shards(): far_rows = [lax.ppermute(rows, 'dp', beside) for rows in partner_rows]]
    ppermute x1, waiting for transfers between devices: 1.19 us -> 0.01 us  [shards(): sibling_owners = lax.ppermute(owners, 'dp', beside)]
    ppermute x6, waiting for transfers between devices: 1.72 us -> 0.79 us  [hand_on(): got.append(lax.ppermute(blocks[step], 'dp', moves))]
    unnamed x36 -> x32, local copies, waits for them, and re-layouts: 3.5 us -> 3.51 us
  transfers between devices with their start and end apart: 15 -> 15, of which waited for: 6 -> 6; matrix products, arithmetic and copies ran while one was open for 6% -> 6% of each run, Pallas kernels for 21% -> 22%
where the time goes in v23:
time: 76.5 us; the launch traced here: 76 us
  starting transfers between devices  29.6 us (39%)
  Pallas kernels  20.2 us (26%)
  waiting for transfers between devices  17.4 us (23%)
  local copies, waits for them, and re-layouts  6.66 us (9%)
  matrix products  1.29 us (2%)
  between operations  0.89 us (1%)
    ppermute x6, starting transfers between devices, hand_on(): got.append(lax.ppermute(blocks[step], 'dp', moves))  7.11 us
    all_to_all x1, starting transfers between devices, shards(): lax.all_to_all(spread, 'dp', split_axis=0, concat_axis=0, tiled=True)  7.04 us
    all_to_all x1, waiting for transfers between devices, shards(): lax.all_to_all(spread, 'dp', split_axis=0, concat_axis=0, tiled=True)  6.83 us
    pallas_call x2, Pallas kernels, pack_rows(): pl.pallas_call(functools.partial(pack_kernel, half, row_cap, count, picks...  5.47 us
    pallas_call x1, Pallas kernels, encode(): pl.pallas_call(encode_kernel, out_shape=[jax.ShapeDtypeStruct((passes, wi...  4.98 us
    all_to_all x1, waiting for transfers between devices, shards(): codes = lax.all_to_all(plan, 'dp', split_axis=0, concat_axis=0, tiled=True)  4.82 us
    ppermute x1, starting transfers between devices, shards(): first_rows = lax.ppermute(stored_rows[:ahead], 'dp', across)  4.08 us
    all_to_all x1, starting transfers between devices, shards(): codes = lax.all_to_all(plan, 'dp', split_axis=0, concat_axis=0, tiled=True)  3.92 us
  transfers between devices with their start and end apart: 15, of which 6 were waited for; matrix products, arithmetic and copies ran while one was open for 6% of the time, Pallas kernels for 22%

profile of v23, /device:TPU:0, one launch (start us, length us, event | category | flops | bytes accessed | tf_op | source)
XLA Modules:
  0.0 76.0 jit_solution(6568893201504041338)
XLA Ops:
  0.6 0.0 copy-start
  0.6 0.5 collective-permute-start.1
  1.2 0.1 collective-permute-start
  1.2 1.0 %slice.17 = bf16[176,1024]{1,0:T(8,128)(2,1)S(1)} slice(bf16[254,1024]{1,0:T(8,128)(2,1)} %refs_2_.1), slice={[0:176], [0:1024]} | slice | bytes 720896 | tf_op jit(solution)/shard_map/slice | solution.py:540
  2.3 4.1 %collective-permute-start.2 = (bf16[176,1024]{1,0:T(8,128)(2,1)S(1)}, bf16[176,1024]{1,0:T(8,128)(2,1)S(1)}, u32[]{:S(2)}, u32[]{:S(2)}) collective-permute-start(bf16[176,1024]{1,0:T(8,128)(2,1)S(1)} %slice.17), channel_id=1, source_target_pairs={{0,8},{1,9},{2,10},{3,11},{4,12},{5,13},{6,14},{7,15},{8,0},{9,1},... | collective-permute-start | bytes 1081352 | tf_op jit(solution)/shard_map/ppermute | solution.py:540
  6.3 0.0 collective-permute-done.sibling_far
  6.3 0.6 copy-done.12
  6.9 2.3 %route.1 = (s32[16,1,330]{2,1,0:T(1,128)}, s32[128,1]{1,0:T(8,128)}, s32[1,256]{1,0:T(1,128)}, s32[1,256]{1,0:T(1,128)}) custom-call(s32[2,64]{1,0:T(2,128)} %token_ids_far.1, s32[1,256]{1,0:T(1,128)} %bitcast.25, s32[1,256]{1,0:T(1,128)} %bitcast.26, s32[1,256]{1,0:T(1,128)} %copy-done.12), custom_call_target="tpu_custom_call" | custom-call | tf_op jit(solution)/shard_map/route/pallas_call | solution.py:228
  9.2 0.0 collective-permute-done.1.refs_3_
  9.2 0.0 copy-start.2
  9.3 3.9 %all-to-all-start = ((s32[16,1,330]{2,1,0:T(1,128)}), s32[16,1,330]{2,1,0:T(1,128)S(1)}, u32[]{:S(2)}, u32[]{:S(2)}) async-start(s32[16,1,330]{2,1,0:T(1,128)} %get-tuple-element.42), calls=%async_computation | async-start | bytes 49152 | tf_op jit(solution)/shard_map/all_to_all | solution.py:548
  13.2 0.0 copy-done.2
  13.2 2.6 %pack.2 = (bf16[96,1024]{1,0:T(8,128)(2,1)}, bf16[96,1024]{1,0:T(8,128)(2,1)}, bf16[96,1024]{1,0:T(8,128)(2,1)}, bf16[96,1024]{1,0:T(8,128)(2,1)}, bf16[78,1024]{1,0:T(8,128)(2,1)}) custom-call(s32[1,256]{1,0:T(1,128)} %get-tuple-element.43.refs_0_, s32[1,256]{1,0:T(1,128)} %get-tuple-element.44.refs_1_, bf16[254,1024]{1,0:T(8,128)(2,1)} %refs_2_.1, ...), custom_call_target="tpu_custom_call" | custom-call | flops 199753728 | bytes 1826816 | tf_op jit(solution)/shard_map/pack/pallas_call | solution.py:319
  15.9 2.0 %collective-permute-start.3 = (bf16[96,1024]{1,0:T(8,128)(2,1)}, bf16[96,1024]{1,0:T(8,128)(2,1)S(1)}, u32[]{:S(2)}, u32[]{:S(2)}) collective-permute-start(bf16[96,1024]{1,0:T(8,128)(2,1)} %get-tuple-element.49), channel_id=1, source_target_pairs={{0,2},{1,3},{2,0},{3,1},{4,6},{5,7},{6,4},{7,5},{8,10},{9,11},{10,... | collective-permute-start | bytes 589832 | tf_op jit(solution)/shard_map/ppermute | solution.py:535
  17.8 1.5 %collective-permute-start.4 = (bf16[96,1024]{1,0:T(8,128)(2,1)}, bf16[96,1024]{1,0:T(8,128)(2,1)S(1)}, u32[]{:S(2)}, u32[]{:S(2)}) collective-permute-start(bf16[96,1024]{1,0:T(8,128)(2,1)} %get-tuple-element.54), channel_id=1, source_target_pairs={{0,4},{1,5},{2,6},{3,7},{4,0},{5,1},{6,2},{7,3},{8,12},{9,13},{10,... | collective-permute-start | bytes 589832 | tf_op jit(solution)/shard_map/ppermute | solution.py:535
  19.3 0.1 collective-permute-start.5
  19.4 4.8 %all-to-all-done.refs_0_.refs_1_ = s32[16,1,330]{2,1,0:T(1,128)S(1)} async-done(((s32[16,1,330]{2,1,0:T(1,128)}), s32[16,1,330]{2,1,0:T(1,128)S(1)}, u32[]{:S(2)}, u32[]{:S(2)}) %all-to-all-start) | async-done | bytes 21152 | tf_op jit(solution)/shard_map/all_to_all | solution.py:548
  24.2 0.1 slice.23
  24.3 0.1 eq.15
  24.4 0.6 gather_fusion
  25.0 0.7 reshape.41.places_far
  25.6 2.6 %collective-permute-start.6 = (bf16[78,1024]{1,0:T(8,128)(2,1)}, bf16[78,1024]{1,0:T(8,128)(2,1)S(1)}, u32[]{:S(2)}, u32[]{:S(2)}) collective-permute-start(bf16[78,1024]{1,0:T(8,128)(2,1)} %get-tuple-element.56), channel_id=1, source_target_pairs={{0,8},{1,9},{2,10},{3,11},{4,12},{5,13},{6,14},{7,15},{8,0},{9,1},... | collective-permute-start | bytes 479240 | tf_op jit(solution)/shard_map/ppermute | solution.py:560
  28.3 0.0 copy-done
  28.3 1.3 %convolution_convert_fusion = bf16[384,1024]{1,0:T(8,128)(2,1)} fusion(bf16[240,1024]{1,0:T(8,128)(2,1)S(1)} %copy-done, s32[384]{0:T(512)S(1)} %eq.15), kind=kOutput, calls=%fused_computation.1 | convolution fusion | flops 189229056 | bytes 1279488 | tf_op jit(solution)/shard_map/dot_general | solution.py:565
  29.6 0.0 collective-permute-done.2.refs_2_
  29.6 0.0 collective-permute-done.3.rest_1_
  29.6 0.0 copy-start.13
  29.6 3.6 %all-to-all-start.1 = ((bf16[16,24,1024]{2,1,0:T(8,128)(2,1)}), bf16[16,24,1024]{2,1,0:T(8,128)(2,1)S(1)}, u32[]{:S(2)}, u32[]{:S(2)}) async-start(bf16[16,24,1024]{2,1,0:T(8,128)(2,1)} %bitcast.4), calls=%async_computation.1 | async-start | bytes 1572864 | tf_op jit(solution)/shard_map/all_to_all | solution.py:571
  33.2 0.0 collective-permute-done.4.rest_2_
  33.2 0.0 copy-start.14
  33.2 0.8 %collective-permute-done.5.rest_3_ = bf16[96,1024]{1,0:T(8,128)(2,1)S(1)} collective-permute-done((bf16[96,1024]{1,0:T(8,128)(2,1)}, bf16[96,1024]{1,0:T(8,128)(2,1)S(1)}, u32[]{:S(2)}, u32[]{:S(2)}) %collective-permute-start.5) | collective-permute-done | bytes 196640 | tf_op jit(solution)/shard_map/ppermute | solution.py:535
  34.0 2.4 %collective-permute-done.6.refs_3_ = bf16[78,1024]{1,0:T(8,128)(2,1)S(1)} collective-permute-done((bf16[78,1024]{1,0:T(8,128)(2,1)}, bf16[78,1024]{1,0:T(8,128)(2,1)S(1)}, u32[]{:S(2)}, u32[]{:S(2)}) %collective-permute-start.6) | collective-permute-done | bytes 159776 | tf_op jit(solution)/shard_map/ppermute | solution.py:560
  36.4 0.0 copy-done.13
  36.5 0.0 copy-done.14
  36.5 0.0 copy-done.15
  36.5 0.0 copy-start.10
  36.5 3.8 %early.1 = (f32[512,1024]{1,0:T(8,128)}, f32[512,128]{1,0:T(8,128)}) custom-call(s32[1,768]{1,0:T(1,128)} %reshape.41.places_far, f32[512,1024]{1,0:T(8,128)} %centroids_far.1, bf16[96,1024]{1,0:T(8,128)(2,1)} %get-tuple-element.58.rest_0_, bf16[96,1024]{1,0:T(8,128)(2,1)} %copy-done.13, bf16[96,1024]{1,0:T(8,128)(2,1)} %copy-done.14, ...), custom_call_target="tpu_custom_call" | custom-call | flops 20132659200 | bytes 104857600 | tf_op jit(solution)/shard_map/early/pallas_call | solution.py:442
  40.3 0.0 copy-done.5
  40.3 0.0 copy-done.3
  40.3 0.1 collective-permute-start.7
  40.4 0.0 copy-done.10
  40.4 0.5 collective-permute-start.8
  40.9 1.4 %collective-permute-done.8.refs_5_ = bf16[78,1024]{1,0:T(8,128)(2,1)S(1)} collective-permute-done((bf16[78,1024]{1,0:T(8,128)(2,1)S(1)}, bf16[78,1024]{1,0:T(8,128)(2,1)S(1)}, u32[]{:S(2)}, u32[]{:S(2)}) %collective-permute-start.8) | collective-permute-done | bytes 159776 | tf_op jit(solution)/shard_map/ppermute | solution.py:583
  42.3 0.0 collective-permute-done.7.refs_4_
  42.3 0.7 copy-done.11
  43.0 0.8 copy-done.4
  43.7 2.8 %pack.3 = (bf16[96,1024]{1,0:T(8,128)(2,1)}, bf16[96,1024]{1,0:T(8,128)(2,1)}, bf16[96,1024]{1,0:T(8,128)(2,1)}, bf16[96,1024]{1,0:T(8,128)(2,1)}) custom-call(s32[16,1,330]{2,1,0:T(1,128)} %copy-done.5, s32[16,1,330]{2,1,0:T(1,128)} %copy-done.5, bf16[176,1024]{1,0:T(8,128)(2,1)} %copy-done.3, bf16[78,1024]{1,0:T(8,128)(2,1)} %copy-done.10, ...), custom_call_target="tpu_custom_call" | custom-call | flops 199753728 | bytes 1826816 | tf_op jit(solution)/shard_map/pack/pallas_call | solution.py:319
  46.6 0.6 collective-permute-start.9
  47.2 1.0 %collective-permute-start.10 = (bf16[96,1024]{1,0:T(8,128)(2,1)}, bf16[96,1024]{1,0:T(8,128)(2,1)S(1)}, u32[]{:S(2)}, u32[]{:S(2)}) collective-permute-start(bf16[96,1024]{1,0:T(8,128)(2,1)} %get-tuple-element.76), channel_id=1, source_target_pairs={{0,4},{1,5},{2,6},{3,7},{4,0},{5,1},{6,2},{7,3},{8,12},{9,13},{10,... | collective-permute-start | bytes 589832 | tf_op jit(solution)/shard_map/ppermute | solution.py:535
  48.3 1.9 %collective-permute-start.11 = (bf16[96,1024]{1,0:T(8,128)(2,1)}, bf16[96,1024]{1,0:T(8,128)(2,1)S(1)}, u32[]{:S(2)}, u32[]{:S(2)}) collective-permute-start(bf16[96,1024]{1,0:T(8,128)(2,1)} %get-tuple-element.77), channel_id=1, source_target_pairs={{0,6},{1,7},{2,4},{3,5},{4,2},{5,3},{6,0},{7,1},{8,14},{9,15},{10,... | collective-permute-start | bytes 589832 | tf_op jit(solution)/shard_map/ppermute | solution.py:535
  50.1 0.1 slice.24
  50.2 0.7 reshape.42.late_far
  50.9 1.1 %all-to-all-done.1 = bf16[16,24,1024]{2,1,0:T(8,128)(2,1)S(1)} async-done(((bf16[16,24,1024]{2,1,0:T(8,128)(2,1)}), bf16[16,24,1024]{2,1,0:T(8,128)(2,1)S(1)}, u32[]{:S(2)}, u32[]{:S(2)}) %all-to-all-start.1) | async-done | bytes 786464 | tf_op jit(solution)/shard_map/all_to_all | solution.py:571
  52.0 0.9 %copy-done.1 = bf16[16,24,1024]{2,1,0:T(8,128)(2,1)} copy-done((bf16[16,24,1024]{2,1,0:T(8,128)(2,1)}, bf16[16,24,1024]{2,1,0:T(8,128)(2,1)S(1)}, u32[]{:S(2)}) %copy-start.1) | copy-done | bytes 786456
  52.9 5.0 %encode.1 = (bf16[2,1024]{1,0:T(2,128)(2,1)}, bf16[16,2,1024]{2,1,0:T(2,128)(2,1)}) custom-call(s32[1,2]{1,0:T(1,128)} %bitcast.27, s32[128,1]{1,0:T(8,128)} %get-tuple-element.40.refs_1_, bf16[384,1024]{1,0:T(8,128)(2,1)} %bitcast.15, bf16[64,1024]{1,0:T(8,128)(2,1)} %refs_3_.1, f32[1,1024]{1,0:T(1,128)} %bitcast.19, f32[1,1024]{1,0:T(1,128)} %bitcast.20, ...), custom_call_target="tpu_custom_call" | custom-call | flops 637534208 | bytes 6291456 | tf_op jit(solution)/shard_map/encode/pallas_call | solution.py:121
  57.9 7.0 %all-to-all-start.2 = ((bf16[16,2,1024]{2,1,0:T(2,128)(2,1)}), bf16[16,2,1024]{2,1,0:T(2,128)(2,1)S(1)}, u32[]{:S(2)}, u32[]{:S(2)}) async-start(bf16[16,2,1024]{2,1,0:T(2,128)(2,1)} %get-tuple-element.69), calls=%async_computation.2 | async-start | bytes 131072 | tf_op jit(solution)/shard_map/all_to_all | solution.py:606
  64.9 0.0 collective-permute-done.9.rest_1_
  64.9 0.0 copy-start.7
  64.9 0.0 collective-permute-done.10.rest_2_
  64.9 0.0 copy-start.8
  65.0 0.0 collective-permute-done.11.rest_3_
  65.0 6.8 %all-to-all-done.2.spread_far = bf16[16,2,1024]{2,1,0:T(2,128)(2,1)S(1)} async-done(((bf16[16,2,1024]{2,1,0:T(2,128)(2,1)}), bf16[16,2,1024]{2,1,0:T(2,128)(2,1)S(1)}, u32[]{:S(2)}, u32[]{:S(2)}) %all-to-all-start.2) | async-done | bytes 65568 | tf_op jit(solution)/shard_map/all_to_all | solution.py:606
  71.8 0.6 copy-done.6
  72.4 3.6 %late.1 = f32[512,1024]{1,0:T(8,128)} custom-call(s32[1,768]{1,0:T(1,128)} %reshape.41.places_far, s32[1,32]{1,0:T(1,128)} %reshape.42.late_far, bf16[16,2,1024]{2,1,0:T(2,128)(2,1)} %copy-done.6, f32[512,128]{1,0:T(8,128)} %get-tuple-element.70.share_far, f32[512,1024]{1,0:T(8,128)} %get-tuple-element.71.early_far, ...), custom_call_target="tpu_custom_call" | custom-call | flops 436207616 | bytes 4194304 | tf_op jit(solution)/shard_map/late/pallas_call | solution.py:474
  (15 shorter events, 0.0 us)
Async XLA Ops:
  0.6 27.6 %copy-start = (bf16[240,1024]{1,0:T(8,128)(2,1)S(1)}, bf16[240,1024]{1,0:T(8,128)(2,1)}, u32[]{:S(2)}) copy-start(bf16[240,1024]{1,0:T(8,128)(2,1)} %param.17) | copy-start | bytes 1474564
  0.6 8.6 %collective-permute-start.1 = (bf16[254,1024]{1,0:T(8,128)(2,1)}, bf16[254,1024]{1,0:T(8,128)(2,1)S(1)}, u32[]{:S(2)}, u32[]{:S(2)}) collective-permute-start(bf16[254,1024]{1,0:T(8,128)(2,1)} %refs_2_.1), channel_id=1, source_target_pairs={{0,1},{1,0},{2,3},{3,2},{4,5},{5,4},{6,7},{7,6},{8,9},{9,8},{10,11... | collective-permute-start | bytes 1560584 | tf_op jit(solution)/shard_map/ppermute | solution.py:539
  1.2 5.2 %collective-permute-start = (s32[1,256]{1,0:T(1,128)}, s32[1,256]{1,0:T(1,128)S(1)}, u32[]{:S(2)}, u32[]{:S(2)}) collective-permute-start(s32[1,256]{1,0:T(1,128)} %bitcast.24), channel_id=1, source_target_pairs={{0,1},{1,0},{2,3},{3,2},{4,5},{5,4},{6,7},{7,6},{8,9},{9,8},{10,11... | collective-permute-start | bytes 3080 | tf_op jit(solution)/shard_map/ppermute | solution.py:543
  2.3 27.3 %collective-permute-start.2 = (bf16[176,1024]{1,0:T(8,128)(2,1)S(1)}, bf16[176,1024]{1,0:T(8,128)(2,1)S(1)}, u32[]{:S(2)}, u32[]{:S(2)}) collective-permute-start(bf16[176,1024]{1,0:T(8,128)(2,1)S(1)} %slice.17), channel_id=1, source_target_pairs={{0,8},{1,9},{2,10},{3,11},{4,12},{5,13},{6,14},{7,15},{8,0},{9,1},... | collective-permute-start | bytes 1081352 | tf_op jit(solution)/shard_map/ppermute | solution.py:540
  6.3 0.6 copy-start.12
  9.2 4.0 %copy-start.2 = (bf16[254,1024]{1,0:T(8,128)(2,1)}, bf16[254,1024]{1,0:T(8,128)(2,1)S(1)}, u32[]{:S(2)}) copy-start(bf16[254,1024]{1,0:T(8,128)(2,1)S(1)} %collective-permute-done.1.refs_3_) | copy-start | bytes 1560580
  9.3 15.0 %all-to-all-start = ((s32[16,1,330]{2,1,0:T(1,128)}), s32[16,1,330]{2,1,0:T(1,128)S(1)}, u32[]{:S(2)}, u32[]{:S(2)}) async-start(s32[16,1,330]{2,1,0:T(1,128)} %get-tuple-element.42), calls=%async_computation | async-start | bytes 49152 | tf_op jit(solution)/shard_map/all_to_all | solution.py:548
  15.9 13.7 %collective-permute-start.3 = (bf16[96,1024]{1,0:T(8,128)(2,1)}, bf16[96,1024]{1,0:T(8,128)(2,1)S(1)}, u32[]{:S(2)}, u32[]{:S(2)}) collective-permute-start(bf16[96,1024]{1,0:T(8,128)(2,1)} %get-tuple-element.49), channel_id=1, source_target_pairs={{0,2},{1,3},{2,0},{3,1},{4,6},{5,7},{6,4},{7,5},{8,10},{9,11},{10,... | collective-permute-start | bytes 589832 | tf_op jit(solution)/shard_map/ppermute | solution.py:535
  17.8 15.4 %collective-permute-start.4 = (bf16[96,1024]{1,0:T(8,128)(2,1)}, bf16[96,1024]{1,0:T(8,128)(2,1)S(1)}, u32[]{:S(2)}, u32[]{:S(2)}) collective-permute-start(bf16[96,1024]{1,0:T(8,128)(2,1)} %get-tuple-element.54), channel_id=1, source_target_pairs={{0,4},{1,5},{2,6},{3,7},{4,0},{5,1},{6,2},{7,3},{8,12},{9,13},{10,... | collective-permute-start | bytes 589832 | tf_op jit(solution)/shard_map/ppermute | solution.py:535
  19.3 14.7 %collective-permute-start.5 = (bf16[96,1024]{1,0:T(8,128)(2,1)}, bf16[96,1024]{1,0:T(8,128)(2,1)S(1)}, u32[]{:S(2)}, u32[]{:S(2)}) collective-permute-start(bf16[96,1024]{1,0:T(8,128)(2,1)} %get-tuple-element.55), channel_id=1, source_target_pairs={{0,6},{1,7},{2,4},{3,5},{4,2},{5,3},{6,0},{7,1},{8,14},{9,15},{10,... | collective-permute-start | bytes 589832 | tf_op jit(solution)/shard_map/ppermute | solution.py:535
  24.2 16.1 %copy-start.5 = (s32[16,1,330]{2,1,0:T(1,128)}, s32[16,1,330]{2,1,0:T(1,128)S(1)}, u32[]{:S(2)}) copy-start(s32[16,1,330]{2,1,0:T(1,128)S(1)} %all-to-all-done.refs_0_.refs_1_) | copy-start | bytes 63364
  25.6 10.8 %collective-permute-start.6 = (bf16[78,1024]{1,0:T(8,128)(2,1)}, bf16[78,1024]{1,0:T(8,128)(2,1)S(1)}, u32[]{:S(2)}, u32[]{:S(2)}) collective-permute-start(bf16[78,1024]{1,0:T(8,128)(2,1)} %get-tuple-element.56), channel_id=1, source_target_pairs={{0,8},{1,9},{2,10},{3,11},{4,12},{5,13},{6,14},{7,15},{8,0},{9,1},... | collective-permute-start | bytes 479240 | tf_op jit(solution)/shard_map/ppermute | solution.py:560
  29.6 10.8 %copy-start.3 = (bf16[176,1024]{1,0:T(8,128)(2,1)}, bf16[176,1024]{1,0:T(8,128)(2,1)S(1)}, u32[]{:S(2)}) copy-start(bf16[176,1024]{1,0:T(8,128)(2,1)S(1)} %collective-permute-done.2.refs_2_) | copy-start | bytes 1081348
  29.6 6.9 %copy-start.13 = (bf16[96,1024]{1,0:T(8,128)(2,1)}, bf16[96,1024]{1,0:T(8,128)(2,1)S(1)}, u32[]{:S(2)}) copy-start(bf16[96,1024]{1,0:T(8,128)(2,1)S(1)} %collective-permute-done.3.rest_1_) | copy-start | bytes 589828
  29.6 22.4 %all-to-all-start.1 = ((bf16[16,24,1024]{2,1,0:T(8,128)(2,1)}), bf16[16,24,1024]{2,1,0:T(8,128)(2,1)S(1)}, u32[]{:S(2)}, u32[]{:S(2)}) async-start(bf16[16,24,1024]{2,1,0:T(8,128)(2,1)} %bitcast.4), calls=%async_computation.1 | async-start | bytes 1572864 | tf_op jit(solution)/shard_map/all_to_all | solution.py:571
  33.2 3.2 %copy-start.14 = (bf16[96,1024]{1,0:T(8,128)(2,1)}, bf16[96,1024]{1,0:T(8,128)(2,1)S(1)}, u32[]{:S(2)}) copy-start(bf16[96,1024]{1,0:T(8,128)(2,1)S(1)} %collective-permute-done.4.rest_2_) | copy-start | bytes 589828
  34.0 2.5 %copy-start.15 = (bf16[96,1024]{1,0:T(8,128)(2,1)}, bf16[96,1024]{1,0:T(8,128)(2,1)S(1)}, u32[]{:S(2)}) copy-start(bf16[96,1024]{1,0:T(8,128)(2,1)S(1)} %collective-permute-done.5.rest_3_) | copy-start | bytes 589828
  36.5 4.0 %copy-start.10 = (bf16[78,1024]{1,0:T(8,128)(2,1)}, bf16[78,1024]{1,0:T(8,128)(2,1)S(1)}, u32[]{:S(2)}) copy-start(bf16[78,1024]{1,0:T(8,128)(2,1)S(1)} %collective-permute-done.6.refs_3_) | copy-start | bytes 479236
  40.3 2.0 %collective-permute-start.7 = (bf16[176,1024]{1,0:T(8,128)(2,1)S(1)}, bf16[176,1024]{1,0:T(8,128)(2,1)S(1)}, u32[]{:S(2)}, u32[]{:S(2)}) collective-permute-start(bf16[176,1024]{1,0:T(8,128)(2,1)S(1)} %collective-permute-done.2.refs_2_), channel_id=1, source_target_pairs={{0,1},{1,0},{2,3},{3,2},{4,5},{5,4},{6,7},{7,6},{8,9},{9,8},{10,11... | collective-permute-start | bytes 1081352 | tf_op jit(solution)/shard_map/ppermute | solution.py:583
  40.4 1.9 %collective-permute-start.8 = (bf16[78,1024]{1,0:T(8,128)(2,1)S(1)}, bf16[78,1024]{1,0:T(8,128)(2,1)S(1)}, u32[]{:S(2)}, u32[]{:S(2)}) collective-permute-start(bf16[78,1024]{1,0:T(8,128)(2,1)S(1)} %collective-permute-done.6.refs_3_), channel_id=1, source_target_pairs={{0,1},{1,0},{2,3},{3,2},{4,5},{5,4},{6,7},{7,6},{8,9},{9,8},{10,11... | collective-permute-start | bytes 479240 | tf_op jit(solution)/shard_map/ppermute | solution.py:583
  42.3 0.7 copy-start.11
  43.0 0.8 copy-start.4
  46.6 18.3 %collective-permute-start.9 = (bf16[96,1024]{1,0:T(8,128)(2,1)}, bf16[96,1024]{1,0:T(8,128)(2,1)S(1)}, u32[]{:S(2)}, u32[]{:S(2)}) collective-permute-start(bf16[96,1024]{1,0:T(8,128)(2,1)} %get-tuple-element.75), channel_id=1, source_target_pairs={{0,2},{1,3},{2,0},{3,1},{4,6},{5,7},{6,4},{7,5},{8,10},{9,11},{10,... | collective-permute-start | bytes 589832 | tf_op jit(solution)/shard_map/ppermute | solution.py:535
  47.2 17.7 %collective-permute-start.10 = (bf16[96,1024]{1,0:T(8,128)(2,1)}, bf16[96,1024]{1,0:T(8,128)(2,1)S(1)}, u32[]{:S(2)}, u32[]{:S(2)}) collective-permute-start(bf16[96,1024]{1,0:T(8,128)(2,1)} %get-tuple-element.76), channel_id=1, source_target_pairs={{0,4},{1,5},{2,6},{3,7},{4,0},{5,1},{6,2},{7,3},{8,12},{9,13},{10,... | collective-permute-start | bytes 589832 | tf_op jit(solution)/shard_map/ppermute | solution.py:535
  48.3 16.7 %collective-permute-start.11 = (bf16[96,1024]{1,0:T(8,128)(2,1)}, bf16[96,1024]{1,0:T(8,128)(2,1)S(1)}, u32[]{:S(2)}, u32[]{:S(2)}) collective-permute-start(bf16[96,1024]{1,0:T(8,128)(2,1)} %get-tuple-element.77), channel_id=1, source_target_pairs={{0,6},{1,7},{2,4},{3,5},{4,2},{5,3},{6,0},{7,1},{8,14},{9,15},{10,... | collective-permute-start | bytes 589832 | tf_op jit(solution)/shard_map/ppermute | solution.py:535
  52.0 0.9 %copy-start.1 = (bf16[16,24,1024]{2,1,0:T(8,128)(2,1)}, bf16[16,24,1024]{2,1,0:T(8,128)(2,1)S(1)}, u32[]{:S(2)}) copy-start(bf16[16,24,1024]{2,1,0:T(8,128)(2,1)S(1)} %all-to-all-done.1) | copy-start | bytes 2359300
  57.9 13.9 %all-to-all-start.2 = ((bf16[16,2,1024]{2,1,0:T(2,128)(2,1)}), bf16[16,2,1024]{2,1,0:T(2,128)(2,1)S(1)}, u32[]{:S(2)}, u32[]{:S(2)}) async-start(bf16[16,2,1024]{2,1,0:T(2,128)(2,1)} %get-tuple-element.69), calls=%async_computation.2 | async-start | bytes 131072 | tf_op jit(solution)/shard_map/all_to_all | solution.py:606
  64.9 6.9 %copy-start.7 = (bf16[96,1024]{1,0:T(8,128)(2,1)}, bf16[96,1024]{1,0:T(8,128)(2,1)S(1)}, u32[]{:S(2)}) copy-start(bf16[96,1024]{1,0:T(8,128)(2,1)S(1)} %collective-permute-done.9.rest_1_) | copy-start | bytes 589828
  64.9 6.9 %copy-start.8 = (bf16[96,1024]{1,0:T(8,128)(2,1)}, bf16[96,1024]{1,0:T(8,128)(2,1)S(1)}, u32[]{:S(2)}) copy-start(bf16[96,1024]{1,0:T(8,128)(2,1)S(1)} %collective-permute-done.10.rest_2_) | copy-start | bytes 589828
  65.0 6.9 %copy-start.9 = (bf16[96,1024]{1,0:T(8,128)(2,1)}, bf16[96,1024]{1,0:T(8,128)(2,1)S(1)}, u32[]{:S(2)}) copy-start(bf16[96,1024]{1,0:T(8,128)(2,1)S(1)} %collective-permute-done.11.rest_3_) | copy-start | bytes 589828
  71.8 0.6 copy-start.6

commit v24 on v22

--- a/solution.py
+++ b/solution.py
@@ -124,11 +124,11 @@
             jax.ShapeDtypeStruct((passes, width), jnp.bfloat16),
             jax.ShapeDtypeStruct((peers, passes, width), jnp.bfloat16),
         ],
-        in_specs=[pl.BlockSpec(memory_space=pltpu.HBM)] * len(operands),
+        in_specs=[pl.BlockSpec(memory_space=pl.ANY)] * len(operands),
         out_specs=[pl.BlockSpec(memory_space=pltpu.VMEM)] * 2,
         scratch_shapes=[pltpu.VMEM(operand.shape, operand.dtype) for operand in operands]
         + [pltpu.SemaphoreType.DMA((len(operands) + 3,))],
-        compiler_params=pltpu.CompilerParams(vmem_limit_bytes=60 * 1024 * 1024),
+        compiler_params=pltpu.CompilerParams(vmem_limit_bytes=40 * 1024 * 1024),
         cost_estimate=pl.CostEstimate(
             flops=2 * macs, bytes_accessed=6 * 1024 * 1024, transcendentals=0
         ),

time: 75.6 us -> 76.2 us (level)
  local copies, waits for them, and re-layouts: 6.67 us -> 7.71 us
    unnamed x36 -> x48, local copies, waits for them, and re-layouts: 3.5 us -> 4.56 us
where the time goes in v24:
time: 76.2 us; the launch traced here: 75.7 us
  starting transfers between devices  29.5 us (39%)
  Pallas kernels  19.6 us (26%)
  waiting for transfers between devices  16.6 us (22%)
  local copies, waits for them, and re-layouts  7.71 us (10%)
  matrix products  1.29 us (2%)
  between operations  1 us (1%)
    ppermute x6, starting transfers between devices, hand_on(): got.append(lax.ppermute(blocks[step], 'dp', moves))  7.57 us
    all_to_all x1, starting transfers between devices, shards(): lax.all_to_all(spread, 'dp', split_axis=0, concat_axis=0, tiled=True)  6.72 us
    all_to_all x1, waiting for transfers between devices, shards(): lax.all_to_all(spread, 'dp', split_axis=0, concat_axis=0, tiled=True)  5.49 us
    all_to_all x1, waiting for transfers between devices, shards(): codes = lax.all_to_all(plan, 'dp', split_axis=0, concat_axis=0, tiled=True)  5.47 us
    pallas_call x2, Pallas kernels, pack_rows(): pl.pallas_call(functools.partial(pack_kernel, half, row_cap, count, picks...  5.46 us
    unnamed x48, local copies, waits for them, and re-layouts  4.56 us
    pallas_call x1, Pallas kernels, encode(): pl.pallas_call(encode_kernel, out_shape=[jax.ShapeDtypeStruct((passes, wi...  4.38 us
    pallas_call x1, Pallas kernels, late_update(): pl.pallas_call(late_kernel, out_shape=jax.ShapeDtypeStruct(early.shape, j...  4.02 us
  transfers between devices with their start and end apart: 15, of which 6 were waited for; matrix products, arithmetic and copies ran while one was open for 6% of the time, Pallas kernels for 21%

profile of v24, /device:TPU:0, one launch (start us, length us, event | category | flops | bytes accessed | tf_op | source)
XLA Modules:
  0.0 75.7 jit_solution(2451043964036999519)
XLA Ops:
  0.6 0.0 copy-start
  0.6 0.5 collective-permute-start.1
  1.2 1.0 %slice.17 = bf16[176,1024]{1,0:T(8,128)(2,1)S(1)} slice(bf16[254,1024]{1,0:T(8,128)(2,1)} %refs_2_.1), slice={[0:176], [0:1024]} | slice | bytes 720896 | tf_op jit(solution)/shard_map/slice | solution.py:540
  2.2 3.7 %collective-permute-start.2 = (bf16[176,1024]{1,0:T(8,128)(2,1)S(1)}, bf16[176,1024]{1,0:T(8,128)(2,1)S(1)}, u32[]{:S(2)}, u32[]{:S(2)}) collective-permute-start(bf16[176,1024]{1,0:T(8,128)(2,1)S(1)} %slice.17), channel_id=1, source_target_pairs={{0,8},{1,9},{2,10},{3,11},{4,12},{5,13},{6,14},{7,15},{8,0},{9,1},... | collective-permute-start | bytes 1081352 | tf_op jit(solution)/shard_map/ppermute | solution.py:540
  5.9 0.2 collective-permute-start
  6.1 1.2 %collective-permute-done.sibling_far = s32[1,256]{1,0:T(1,128)S(1)} collective-permute-done((s32[1,256]{1,0:T(1,128)}, s32[1,256]{1,0:T(1,128)S(1)}, u32[]{:S(2)}, u32[]{:S(2)}) %collective-permute-start) | collective-permute-done | bytes 1056 | tf_op jit(solution)/shard_map/ppermute | solution.py:543
  7.2 0.6 copy-done.22
  7.8 2.3 %route.1 = (s32[16,1,330]{2,1,0:T(1,128)}, s32[128,1]{1,0:T(8,128)}, s32[1,256]{1,0:T(1,128)}, s32[1,256]{1,0:T(1,128)}) custom-call(s32[2,64]{1,0:T(2,128)} %token_ids_far.1, s32[1,256]{1,0:T(1,128)} %bitcast.26, s32[1,256]{1,0:T(1,128)} %bitcast.27, s32[1,256]{1,0:T(1,128)} %copy-done.22), custom_call_target="tpu_custom_call" | custom-call | tf_op jit(solution)/shard_map/route/pallas_call | solution.py:228
  10.1 0.0 collective-permute-done.1.refs_3_
  10.2 0.0 copy-start.11
  10.2 3.9 %all-to-all-start = ((s32[16,1,330]{2,1,0:T(1,128)}), s32[16,1,330]{2,1,0:T(1,128)S(1)}, u32[]{:S(2)}, u32[]{:S(2)}) async-start(s32[16,1,330]{2,1,0:T(1,128)} %get-tuple-element.40), calls=%async_computation | async-start | bytes 49152 | tf_op jit(solution)/shard_map/all_to_all | solution.py:548
  14.1 0.0 copy-done.11
  14.1 2.6 %pack.2 = (bf16[96,1024]{1,0:T(8,128)(2,1)}, bf16[96,1024]{1,0:T(8,128)(2,1)}, bf16[96,1024]{1,0:T(8,128)(2,1)}, bf16[96,1024]{1,0:T(8,128)(2,1)}, bf16[78,1024]{1,0:T(8,128)(2,1)}) custom-call(s32[1,256]{1,0:T(1,128)} %get-tuple-element.41.refs_0_, s32[1,256]{1,0:T(1,128)} %get-tuple-element.42.refs_1_, bf16[254,1024]{1,0:T(8,128)(2,1)} %refs_2_.1, ...), custom_call_target="tpu_custom_call" | custom-call | flops 199753728 | bytes 1826816 | tf_op jit(solution)/shard_map/pack/pallas_call | solution.py:319
  16.7 2.0 %collective-permute-start.3 = (bf16[96,1024]{1,0:T(8,128)(2,1)}, bf16[96,1024]{1,0:T(8,128)(2,1)S(1)}, u32[]{:S(2)}, u32[]{:S(2)}) collective-permute-start(bf16[96,1024]{1,0:T(8,128)(2,1)} %get-tuple-element.47), channel_id=1, source_target_pairs={{0,2},{1,3},{2,0},{3,1},{4,6},{5,7},{6,4},{7,5},{8,10},{9,11},{10,... | collective-permute-start | bytes 589832 | tf_op jit(solution)/shard_map/ppermute | solution.py:535
  18.7 5.5 %all-to-all-done.refs_0_.refs_1_ = s32[16,1,330]{2,1,0:T(1,128)S(1)} async-done(((s32[16,1,330]{2,1,0:T(1,128)}), s32[16,1,330]{2,1,0:T(1,128)S(1)}, u32[]{:S(2)}, u32[]{:S(2)}) %all-to-all-start) | async-done | bytes 21152 | tf_op jit(solution)/shard_map/all_to_all | solution.py:548
  24.2 0.1 eq.15
  24.3 2.7 %collective-permute-start.4 = (bf16[78,1024]{1,0:T(8,128)(2,1)}, bf16[78,1024]{1,0:T(8,128)(2,1)S(1)}, u32[]{:S(2)}, u32[]{:S(2)}) collective-permute-start(bf16[78,1024]{1,0:T(8,128)(2,1)} %get-tuple-element.52), channel_id=1, source_target_pairs={{0,8},{1,9},{2,10},{3,11},{4,12},{5,13},{6,14},{7,15},{8,0},{9,1},... | collective-permute-start | bytes 479240 | tf_op jit(solution)/shard_map/ppermute | solution.py:560
  27.0 0.0 copy-done
  27.0 1.3 %convolution_convert_fusion = bf16[384,1024]{1,0:T(8,128)(2,1)} fusion(bf16[240,1024]{1,0:T(8,128)(2,1)S(1)} %copy-done, s32[384]{0:T(512)S(1)} %eq.15), kind=kOutput, calls=%fused_computation.1 | convolution fusion | flops 189229056 | bytes 1279488 | tf_op jit(solution)/shard_map/dot_general | solution.py:565
  28.3 0.0 collective-permute-done.2.refs_2_
  28.3 0.0 collective-permute-done.3.rest_1_
  28.3 0.0 copy-start.23
  28.3 3.6 %all-to-all-start.1 = ((bf16[16,24,1024]{2,1,0:T(8,128)(2,1)}), bf16[16,24,1024]{2,1,0:T(8,128)(2,1)S(1)}, u32[]{:S(2)}, u32[]{:S(2)}) async-start(bf16[16,24,1024]{2,1,0:T(8,128)(2,1)} %bitcast.4), calls=%async_computation.1 | async-start | bytes 1572864 | tf_op jit(solution)/shard_map/all_to_all | solution.py:571
  32.0 0.1 slice.23
  32.1 0.6 gather_fusion
  32.6 0.7 reshape.41.places_far
  33.3 0.0 copy-start.6
  33.3 0.0 copy-start.7
  33.3 0.0 copy-start.8
  33.4 0.0 copy-start.9
  33.4 0.0 copy-start.10
  33.4 1.7 %collective-permute-done.4.refs_3_ = bf16[78,1024]{1,0:T(8,128)(2,1)S(1)} collective-permute-done((bf16[78,1024]{1,0:T(8,128)(2,1)}, bf16[78,1024]{1,0:T(8,128)(2,1)S(1)}, u32[]{:S(2)}, u32[]{:S(2)}) %collective-permute-start.4) | collective-permute-done | bytes 159776 | tf_op jit(solution)/shard_map/ppermute | solution.py:560
  35.1 0.0 copy-done.23
  35.1 3.4 %early.1 = (f32[512,1024]{1,0:T(8,128)}, f32[512,128]{1,0:T(8,128)}) custom-call(s32[1,768]{1,0:T(1,128)} %reshape.41.places_far, f32[512,1024]{1,0:T(8,128)} %centroids_far.1, bf16[96,1024]{1,0:T(8,128)(2,1)} %get-tuple-element.54.rest_0_, bf16[96,1024]{1,0:T(8,128)(2,1)} %copy-done.23), custom_call_target="tpu_custom_call" | custom-call | flops 10066329600 | bytes 104857600 | tf_op jit(solution)/shard_map/early/pallas_call | solution.py:442
  38.5 0.0 copy-done.14
  38.5 0.0 copy-done.12
  38.5 0.1 collective-permute-start.7
  38.6 0.5 collective-permute-start.8
  39.1 0.7 collective-permute-start.5
  39.8 1.3 %collective-permute-start.6 = (bf16[96,1024]{1,0:T(8,128)(2,1)}, bf16[96,1024]{1,0:T(8,128)(2,1)S(1)}, u32[]{:S(2)}, u32[]{:S(2)}) collective-permute-start(bf16[96,1024]{1,0:T(8,128)(2,1)} %get-tuple-element.67), channel_id=1, source_target_pairs={{0,6},{1,7},{2,4},{3,5},{4,2},{5,3},{6,0},{7,1},{8,14},{9,15},{10,... | collective-permute-start | bytes 589832 | tf_op jit(solution)/shard_map/ppermute | solution.py:535
  41.1 0.0 collective-permute-done.8.refs_5_
  41.1 0.0 collective-permute-done.7.refs_4_
  41.1 0.7 copy-done.21
  41.8 0.7 copy-done.13
  42.5 2.8 %pack.3 = (bf16[96,1024]{1,0:T(8,128)(2,1)}, bf16[96,1024]{1,0:T(8,128)(2,1)}, bf16[96,1024]{1,0:T(8,128)(2,1)}, bf16[96,1024]{1,0:T(8,128)(2,1)}) custom-call(s32[16,1,330]{2,1,0:T(1,128)} %copy-done.14, s32[16,1,330]{2,1,0:T(1,128)} %copy-done.14, bf16[176,1024]{1,0:T(8,128)(2,1)} %copy-done.12, bf16[78,1024]{1,0:T(8,128)(2,1)} %copy-done.20, ...), custom_call_target="tpu_custom_call" | custom-call | flops 199753728 | bytes 1826816 | tf_op jit(solution)/shard_map/pack/pallas_call | solution.py:319
  45.4 1.5 %collective-permute-start.9 = (bf16[96,1024]{1,0:T(8,128)(2,1)}, bf16[96,1024]{1,0:T(8,128)(2,1)S(1)}, u32[]{:S(2)}, u32[]{:S(2)}) collective-permute-start(bf16[96,1024]{1,0:T(8,128)(2,1)} %get-tuple-element.71), channel_id=1, source_target_pairs={{0,2},{1,3},{2,0},{3,1},{4,6},{5,7},{6,4},{7,5},{8,10},{9,11},{10,... | collective-permute-start | bytes 589832 | tf_op jit(solution)/shard_map/ppermute | solution.py:535
  46.9 0.7 collective-permute-start.10
  47.6 1.3 %collective-permute-start.11 = (bf16[96,1024]{1,0:T(8,128)(2,1)}, bf16[96,1024]{1,0:T(8,128)(2,1)}, u32[]{:S(2)}, u32[]{:S(2)}) collective-permute-start(bf16[96,1024]{1,0:T(8,128)(2,1)} %get-tuple-element.73), channel_id=1, source_target_pairs={{0,6},{1,7},{2,4},{3,5},{4,2},{5,3},{6,0},{7,1},{8,14},{9,15},{10,... | collective-permute-start | bytes 589832 | tf_op jit(solution)/shard_map/ppermute | solution.py:535
  48.9 0.1 slice.24
  49.0 0.7 reshape.42.late_far
  49.7 1.4 %all-to-all-done.1 = bf16[16,24,1024]{2,1,0:T(8,128)(2,1)S(1)} async-done(((bf16[16,24,1024]{2,1,0:T(8,128)(2,1)}), bf16[16,24,1024]{2,1,0:T(8,128)(2,1)S(1)}, u32[]{:S(2)}, u32[]{:S(2)}) %all-to-all-start.1) | async-done | bytes 786464 | tf_op jit(solution)/shard_map/all_to_all | solution.py:571
  51.1 0.0 copy-start.1
  51.1 1.9 %copy-done.1 = bf16[1024,1536]{1,0:T(8,128)(2,1)S(1)} copy-done((bf16[1024,1536]{1,0:T(8,128)(2,1)S(1)}, bf16[1024,1536]{1,0:T(8,128)(2,1)}, u32[]{:S(2)}) %copy-start.1) | copy-done | bytes 3145752
  53.0 4.4 %encode.1 = (bf16[2,1024]{1,0:T(2,128)(2,1)}, bf16[16,2,1024]{2,1,0:T(2,128)(2,1)}) custom-call(s32[1,2]{1,0:T(1,128)S(1)} %bitcast.21, s32[128,1]{1,0:T(8,128)S(1)} %copy-done.4, bf16[384,1024]{1,0:T(8,128)(2,1)S(1)} %bitcast.15, bf16[64,1024]{1,0:T(8,128)(2,1)S(1)} %copy-done.3, f32[1,1024]{1,0:T(1,128)S(1)} %bitcast.16, f32[1,1024]{1,0:T(1,128)S(1)} %bitcast.17, ...), custom_call_target="tpu_custom_call" | custom-call | flops 637534208 | bytes 6291456 | tf_op jit(solution)/shard_map/encode/pallas_call | solution.py:121
  57.4 6.7 %all-to-all-start.2 = ((bf16[16,2,1024]{2,1,0:T(2,128)(2,1)}), bf16[16,2,1024]{2,1,0:T(2,128)(2,1)S(1)}, u32[]{:S(2)}, u32[]{:S(2)}) async-start(bf16[16,2,1024]{2,1,0:T(2,128)(2,1)} %get-tuple-element.63), calls=%async_computation.2 | async-start | bytes 131072 | tf_op jit(solution)/shard_map/all_to_all | solution.py:606
  64.1 0.0 collective-permute-done.5.rest_0_
  64.2 0.0 collective-permute-done.6.rest_1_
  64.2 0.0 collective-permute-done.9.rest_3_
  64.2 0.0 collective-permute-done.10.rest_4_
  64.2 0.0 copy-start.19
  64.2 1.3 %collective-permute-done.11.rest_5_ = bf16[96,1024]{1,0:T(8,128)(2,1)} collective-permute-done((bf16[96,1024]{1,0:T(8,128)(2,1)}, bf16[96,1024]{1,0:T(8,128)(2,1)}, u32[]{:S(2)}, u32[]{:S(2)}) %collective-permute-start.11) | collective-permute-done | bytes 196640 | tf_op jit(solution)/shard_map/ppermute | solution.py:535
  65.6 5.5 %all-to-all-done.2.spread_far = bf16[16,2,1024]{2,1,0:T(2,128)(2,1)S(1)} async-done(((bf16[16,2,1024]{2,1,0:T(2,128)(2,1)}), bf16[16,2,1024]{2,1,0:T(2,128)(2,1)S(1)}, u32[]{:S(2)}, u32[]{:S(2)}) %all-to-all-start.2) | async-done | bytes 65568 | tf_op jit(solution)/shard_map/all_to_all | solution.py:606
  71.1 0.6 copy-done.15
  71.7 4.0 %late.1 = f32[512,1024]{1,0:T(8,128)} custom-call(s32[1,768]{1,0:T(1,128)} %reshape.41.places_far, s32[1,32]{1,0:T(1,128)} %reshape.42.late_far, bf16[16,2,1024]{2,1,0:T(2,128)(2,1)} %copy-done.15, f32[512,128]{1,0:T(8,128)} %get-tuple-element.64.share_far, f32[512,1024]{1,0:T(8,128)} %get-tuple-element.65.early_far, bf16[96,1024]{1,0:T(8,128)(2,1)} %copy-done.16, ...), custom_call_target="tpu_custom_call" | custom-call | flops 637534208 | bytes 4194304 | tf_op jit(solution)/shard_map/late/pallas_call | solution.py:474
  (31 shorter events, 0.1 us)
Async XLA Ops:
  0.6 26.4 %copy-start = (bf16[240,1024]{1,0:T(8,128)(2,1)S(1)}, bf16[240,1024]{1,0:T(8,128)(2,1)}, u32[]{:S(2)}) copy-start(bf16[240,1024]{1,0:T(8,128)(2,1)} %param.17) | copy-start | bytes 1474564
  0.6 9.5 %collective-permute-start.1 = (bf16[254,1024]{1,0:T(8,128)(2,1)}, bf16[254,1024]{1,0:T(8,128)(2,1)S(1)}, u32[]{:S(2)}, u32[]{:S(2)}) collective-permute-start(bf16[254,1024]{1,0:T(8,128)(2,1)} %refs_2_.1), channel_id=1, source_target_pairs={{0,1},{1,0},{2,3},{3,2},{4,5},{5,4},{6,7},{7,6},{8,9},{9,8},{10,11... | collective-permute-start | bytes 1560584 | tf_op jit(solution)/shard_map/ppermute | solution.py:539
  2.2 26.1 %collective-permute-start.2 = (bf16[176,1024]{1,0:T(8,128)(2,1)S(1)}, bf16[176,1024]{1,0:T(8,128)(2,1)S(1)}, u32[]{:S(2)}, u32[]{:S(2)}) collective-permute-start(bf16[176,1024]{1,0:T(8,128)(2,1)S(1)} %slice.17), channel_id=1, source_target_pairs={{0,8},{1,9},{2,10},{3,11},{4,12},{5,13},{6,14},{7,15},{8,0},{9,1},... | collective-permute-start | bytes 1081352 | tf_op jit(solution)/shard_map/ppermute | solution.py:540
  5.9 1.4 %collective-permute-start = (s32[1,256]{1,0:T(1,128)}, s32[1,256]{1,0:T(1,128)S(1)}, u32[]{:S(2)}, u32[]{:S(2)}) collective-permute-start(s32[1,256]{1,0:T(1,128)} %bitcast.25), channel_id=1, source_target_pairs={{0,1},{1,0},{2,3},{3,2},{4,5},{5,4},{6,7},{7,6},{8,9},{9,8},{10,11... | collective-permute-start | bytes 3080 | tf_op jit(solution)/shard_map/ppermute | solution.py:543
  7.2 0.6 copy-start.22
  10.2 4.0 %copy-start.11 = (bf16[254,1024]{1,0:T(8,128)(2,1)}, bf16[254,1024]{1,0:T(8,128)(2,1)S(1)}, u32[]{:S(2)}) copy-start(bf16[254,1024]{1,0:T(8,128)(2,1)S(1)} %collective-permute-done.1.refs_3_) | copy-start | bytes 1560580
  10.2 14.0 %all-to-all-start = ((s32[16,1,330]{2,1,0:T(1,128)}), s32[16,1,330]{2,1,0:T(1,128)S(1)}, u32[]{:S(2)}, u32[]{:S(2)}) async-start(s32[16,1,330]{2,1,0:T(1,128)} %get-tuple-element.40), calls=%async_computation | async-start | bytes 49152 | tf_op jit(solution)/shard_map/all_to_all | solution.py:548
  16.7 11.6 %collective-permute-start.3 = (bf16[96,1024]{1,0:T(8,128)(2,1)}, bf16[96,1024]{1,0:T(8,128)(2,1)S(1)}, u32[]{:S(2)}, u32[]{:S(2)}) collective-permute-start(bf16[96,1024]{1,0:T(8,128)(2,1)} %get-tuple-element.47), channel_id=1, source_target_pairs={{0,2},{1,3},{2,0},{3,1},{4,6},{5,7},{6,4},{7,5},{8,10},{9,11},{10,... | collective-permute-start | bytes 589832 | tf_op jit(solution)/shard_map/ppermute | solution.py:535
  24.2 14.3 %copy-start.14 = (s32[16,1,330]{2,1,0:T(1,128)}, s32[16,1,330]{2,1,0:T(1,128)S(1)}, u32[]{:S(2)}) copy-start(s32[16,1,330]{2,1,0:T(1,128)S(1)} %all-to-all-done.refs_0_.refs_1_) | copy-start | bytes 63364
  24.3 10.8 %collective-permute-start.4 = (bf16[78,1024]{1,0:T(8,128)(2,1)}, bf16[78,1024]{1,0:T(8,128)(2,1)S(1)}, u32[]{:S(2)}, u32[]{:S(2)}) collective-permute-start(bf16[78,1024]{1,0:T(8,128)(2,1)} %get-tuple-element.52), channel_id=1, source_target_pairs={{0,8},{1,9},{2,10},{3,11},{4,12},{5,13},{6,14},{7,15},{8,0},{9,1},... | collective-permute-start | bytes 479240 | tf_op jit(solution)/shard_map/ppermute | solution.py:560
  28.3 10.2 %copy-start.12 = (bf16[176,1024]{1,0:T(8,128)(2,1)}, bf16[176,1024]{1,0:T(8,128)(2,1)S(1)}, u32[]{:S(2)}) copy-start(bf16[176,1024]{1,0:T(8,128)(2,1)S(1)} %collective-permute-done.2.refs_2_) | copy-start | bytes 1081348
  28.3 6.8 %copy-start.23 = (bf16[96,1024]{1,0:T(8,128)(2,1)}, bf16[96,1024]{1,0:T(8,128)(2,1)S(1)}, u32[]{:S(2)}) copy-start(bf16[96,1024]{1,0:T(8,128)(2,1)S(1)} %collective-permute-done.3.rest_1_) | copy-start | bytes 589828
  28.3 22.7 %all-to-all-start.1 = ((bf16[16,24,1024]{2,1,0:T(8,128)(2,1)}), bf16[16,24,1024]{2,1,0:T(8,128)(2,1)S(1)}, u32[]{:S(2)}, u32[]{:S(2)}) async-start(bf16[16,24,1024]{2,1,0:T(8,128)(2,1)} %bitcast.4), calls=%async_computation.1 | async-start | bytes 1572864 | tf_op jit(solution)/shard_map/all_to_all | solution.py:571
  33.3 17.8 %copy-start.2 = (bf16[512,1024]{1,0:T(8,128)(2,1)S(1)}, bf16[512,1024]{1,0:T(8,128)(2,1)}, u32[]{:S(2)}) copy-start(bf16[512,1024]{1,0:T(8,128)(2,1)} %refs_10_.1) | copy-start | bytes 3145732
  33.3 17.8 %copy-start.3 = (bf16[64,1024]{1,0:T(8,128)(2,1)S(1)}, bf16[64,1024]{1,0:T(8,128)(2,1)}, u32[]{:S(2)}) copy-start(bf16[64,1024]{1,0:T(8,128)(2,1)} %refs_3_.1) | copy-start | bytes 393220
  33.3 17.8 %copy-start.4 = (s32[128,1]{1,0:T(8,128)S(1)}, s32[128,1]{1,0:T(8,128)}, u32[]{:S(2)}) copy-start(s32[128,1]{1,0:T(8,128)} %get-tuple-element.38.refs_1_) | copy-start | bytes 1540
  33.3 17.8 %copy-start.5 = (f32[1024]{0:T(1024)S(1)}, f32[1024]{0:T(1024)}, u32[]{:S(2)}) copy-start(f32[1024]{0:T(1024)} %param.19) | copy-start | bytes 12292
  33.3 17.8 %copy-start.6 = (f32[1024]{0:T(1024)S(1)}, f32[1024]{0:T(1024)}, u32[]{:S(2)}) copy-start(f32[1024]{0:T(1024)} %param.20) | copy-start | bytes 12292
  33.3 17.8 %copy-start.7 = (f32[1024]{0:T(1024)S(1)}, f32[1024]{0:T(1024)}, u32[]{:S(2)}) copy-start(f32[1024]{0:T(1024)} %param.23) | copy-start | bytes 12292
  33.3 17.8 %copy-start.8 = (f32[1024]{0:T(1024)S(1)}, f32[1024]{0:T(1024)}, u32[]{:S(2)}) copy-start(f32[1024]{0:T(1024)} %param.24) | copy-start | bytes 12292
  33.4 17.8 %copy-start.9 = (f32[1024]{0:T(1024)S(1)}, f32[1024]{0:T(1024)}, u32[]{:S(2)}) copy-start(f32[1024]{0:T(1024)} %param.25) | copy-start | bytes 12292
  33.4 17.8 %copy-start.10 = (s32[2]{0:T(128)S(1)}, s32[2]{0:T(128)}, u32[]{:S(2)}) copy-start(s32[2]{0:T(128)} %param.16) | copy-start | bytes 28
  35.1 3.5 %copy-start.20 = (bf16[78,1024]{1,0:T(8,128)(2,1)}, bf16[78,1024]{1,0:T(8,128)(2,1)S(1)}, u32[]{:S(2)}) copy-start(bf16[78,1024]{1,0:T(8,128)(2,1)S(1)} %collective-permute-done.4.refs_3_) | copy-start | bytes 479236
  38.5 2.6 %collective-permute-start.7 = (bf16[176,1024]{1,0:T(8,128)(2,1)S(1)}, bf16[176,1024]{1,0:T(8,128)(2,1)S(1)}, u32[]{:S(2)}, u32[]{:S(2)}) collective-permute-start(bf16[176,1024]{1,0:T(8,128)(2,1)S(1)} %collective-permute-done.2.refs_2_), channel_id=1, source_target_pairs={{0,1},{1,0},{2,3},{3,2},{4,5},{5,4},{6,7},{7,6},{8,9},{9,8},{10,11... | collective-permute-start | bytes 1081352 | tf_op jit(solution)/shard_map/ppermute | solution.py:583
  38.6 2.5 %collective-permute-start.8 = (bf16[78,1024]{1,0:T(8,128)(2,1)S(1)}, bf16[78,1024]{1,0:T(8,128)(2,1)S(1)}, u32[]{:S(2)}, u32[]{:S(2)}) collective-permute-start(bf16[78,1024]{1,0:T(8,128)(2,1)S(1)} %collective-permute-done.4.refs_3_), channel_id=1, source_target_pairs={{0,1},{1,0},{2,3},{3,2},{4,5},{5,4},{6,7},{7,6},{8,9},{9,8},{10,11... | collective-permute-start | bytes 479240 | tf_op jit(solution)/shard_map/ppermute | solution.py:583
  39.1 25.1 %collective-permute-start.5 = (bf16[96,1024]{1,0:T(8,128)(2,1)}, bf16[96,1024]{1,0:T(8,128)(2,1)S(1)}, u32[]{:S(2)}, u32[]{:S(2)}) collective-permute-start(bf16[96,1024]{1,0:T(8,128)(2,1)} %get-tuple-element.66), channel_id=1, source_target_pairs={{0,4},{1,5},{2,6},{3,7},{4,0},{5,1},{6,2},{7,3},{8,12},{9,13},{10,... | collective-permute-start | bytes 589832 | tf_op jit(solution)/shard_map/ppermute | solution.py:535
  39.8 24.4 %collective-permute-start.6 = (bf16[96,1024]{1,0:T(8,128)(2,1)}, bf16[96,1024]{1,0:T(8,128)(2,1)S(1)}, u32[]{:S(2)}, u32[]{:S(2)}) collective-permute-start(bf16[96,1024]{1,0:T(8,128)(2,1)} %get-tuple-element.67), channel_id=1, source_target_pairs={{0,6},{1,7},{2,4},{3,5},{4,2},{5,3},{6,0},{7,1},{8,14},{9,15},{10,... | collective-permute-start | bytes 589832 | tf_op jit(solution)/shard_map/ppermute | solution.py:535
  41.1 0.7 copy-start.21
  41.8 0.7 copy-start.13
  45.4 18.8 %collective-permute-start.9 = (bf16[96,1024]{1,0:T(8,128)(2,1)}, bf16[96,1024]{1,0:T(8,128)(2,1)S(1)}, u32[]{:S(2)}, u32[]{:S(2)}) collective-permute-start(bf16[96,1024]{1,0:T(8,128)(2,1)} %get-tuple-element.71), channel_id=1, source_target_pairs={{0,2},{1,3},{2,0},{3,1},{4,6},{5,7},{6,4},{7,5},{8,10},{9,11},{10,... | collective-permute-start | bytes 589832 | tf_op jit(solution)/shard_map/ppermute | solution.py:535
  46.9 17.3 %collective-permute-start.10 = (bf16[96,1024]{1,0:T(8,128)(2,1)}, bf16[96,1024]{1,0:T(8,128)(2,1)S(1)}, u32[]{:S(2)}, u32[]{:S(2)}) collective-permute-start(bf16[96,1024]{1,0:T(8,128)(2,1)} %get-tuple-element.72), channel_id=1, source_target_pairs={{0,4},{1,5},{2,6},{3,7},{4,0},{5,1},{6,2},{7,3},{8,12},{9,13},{10,... | collective-permute-start | bytes 589832 | tf_op jit(solution)/shard_map/ppermute | solution.py:535
  47.6 17.9 %collective-permute-start.11 = (bf16[96,1024]{1,0:T(8,128)(2,1)}, bf16[96,1024]{1,0:T(8,128)(2,1)}, u32[]{:S(2)}, u32[]{:S(2)}) collective-permute-start(bf16[96,1024]{1,0:T(8,128)(2,1)} %get-tuple-element.73), channel_id=1, source_target_pairs={{0,6},{1,7},{2,4},{3,5},{4,2},{5,3},{6,0},{7,1},{8,14},{9,15},{10,... | collective-permute-start | bytes 589832 | tf_op jit(solution)/shard_map/ppermute | solution.py:535
  51.1 1.9 %copy-start.1 = (bf16[1024,1536]{1,0:T(8,128)(2,1)S(1)}, bf16[1024,1536]{1,0:T(8,128)(2,1)}, u32[]{:S(2)}) copy-start(bf16[1024,1536]{1,0:T(8,128)(2,1)} %refs_9_.1) | copy-start | bytes 9437188
  57.4 13.6 %all-to-all-start.2 = ((bf16[16,2,1024]{2,1,0:T(2,128)(2,1)}), bf16[16,2,1024]{2,1,0:T(2,128)(2,1)S(1)}, u32[]{:S(2)}, u32[]{:S(2)}) async-start(bf16[16,2,1024]{2,1,0:T(2,128)(2,1)} %get-tuple-element.63), calls=%async_computation.2 | async-start | bytes 131072 | tf_op jit(solution)/shard_map/all_to_all | solution.py:606
  64.2 6.9 %copy-start.16 = (bf16[96,1024]{1,0:T(8,128)(2,1)}, bf16[96,1024]{1,0:T(8,128)(2,1)S(1)}, u32[]{:S(2)}) copy-start(bf16[96,1024]{1,0:T(8,128)(2,1)S(1)} %collective-permute-done.5.rest_0_) | copy-start | bytes 589828
  64.2 6.9 %copy-start.17 = (bf16[96,1024]{1,0:T(8,128)(2,1)}, bf16[96,1024]{1,0:T(8,128)(2,1)S(1)}, u32[]{:S(2)}) copy-start(bf16[96,1024]{1,0:T(8,128)(2,1)S(1)} %collective-permute-done.6.rest_1_) | copy-start | bytes 589828
  64.2 6.9 %copy-start.18 = (bf16[96,1024]{1,0:T(8,128)(2,1)}, bf16[96,1024]{1,0:T(8,128)(2,1)S(1)}, u32[]{:S(2)}) copy-start(bf16[96,1024]{1,0:T(8,128)(2,1)S(1)} %collective-permute-done.9.rest_3_) | copy-start | bytes 589828
  64.2 6.8 %copy-start.19 = (bf16[96,1024]{1,0:T(8,128)(2,1)}, bf16[96,1024]{1,0:T(8,128)(2,1)S(1)}, u32[]{:S(2)}) copy-start(bf16[96,1024]{1,0:T(8,128)(2,1)S(1)} %collective-permute-done.10.rest_4_) | copy-start | bytes 589828
  71.0 0.6 copy-start.15

commit v25 on v22

--- a/solution.py
+++ b/solution.py
@@ -30,8 +30,9 @@
 
 
 def encode_kernel(*refs):
-    count = (len(refs) - 3) // 2
-    far, (out, spread), near, arrived = refs[:count], refs[count : count + 2], refs[-count - 1 : -1], refs[-1]
+    *refs, same, arrived = refs
+    count = (len(refs) - 2) // 2
+    far, (out, spread), near = refs[:count], refs[count : count + 2], refs[-count:]
     w_qkv_far, inner = far[-2], HEADS * HD
     copies = [
         pltpu.make_async_copy(source, target, arrived.at[at])
@@ -50,14 +51,20 @@
         )
     for copy in copies + thirds + [out_copy]:
         copy.start()
-    for copy in copies:
-        copy.wait()
     passes = out.shape[0]
-    size = [lengths[:, p : p + 1] for p in range(passes)]
     tokens, slot_count = slots.shape[0], fetched.shape[0]
     seq = tokens // passes
+    block_row = lax.broadcasted_iota(jnp.int32, (HEADS * seq, inner), 0) // seq
+    block_col = lax.broadcasted_iota(jnp.int32, (HEADS * seq, inner), 1) // HD
+    same[...] = jnp.where(block_row == block_col, 1.0, 0.0).astype(jnp.bfloat16)
     spot = lax.broadcasted_iota(jnp.int32, (tokens, slot_count), 1)
+    lane = lax.broadcasted_iota(jnp.int32, (seq, HEADS * seq), 1) % seq
+    for copy in copies[:2]:
+        copy.wait()
+    size = [lengths[:, p : p + 1] for p in range(passes)]
     picker = jnp.where(slots[...] == spot, 1.0, 0.0).astype(jnp.bfloat16)
+    for copy in copies[2:]:
+        copy.wait()
     tok = jnp.dot(picker, fetched[...], preferred_element_type=jnp.float32)
     where_at = pos[...].astype(jnp.float32)
     summed = tok + jnp.concatenate([where_at] * passes, axis=0)
@@ -69,16 +76,11 @@
         part = jnp.dot(embedded, weights, preferred_element_type=jnp.float32)
         parts.append(part.astype(jnp.bfloat16))
 
-    block_row = lax.broadcasted_iota(jnp.int32, (HEADS * seq, inner), 0) // seq
-    block_col = lax.broadcasted_iota(jnp.int32, (HEADS * seq, inner), 1) // HD
-    same = block_row == block_col
-    lane = lax.broadcasted_iota(jnp.int32, (seq, HEADS * seq), 1) % seq
     contexts = []
     for p in range(passes):
         query, keys, vals = (part[p * seq : (p + 1) * seq] for part in parts)
-        zero = jnp.zeros((), jnp.bfloat16)
-        keys = jnp.where(same, jnp.concatenate([keys] * HEADS, axis=0), zero)
-        vals = jnp.where(same, jnp.concatenate([vals] * HEADS, axis=0), zero)
+        keys = jnp.concatenate([keys] * HEADS, axis=0) * same[...]
+        vals = jnp.concatenate([vals] * HEADS, axis=0) * same[...]
         scores = lax.dot_general(
             query, keys, (((1,), (1,)), ((), ())), preferred_element_type=jnp.float32
         ) * HD ** (-0.5)
@@ -127,7 +129,10 @@
         in_specs=[pl.BlockSpec(memory_space=pltpu.HBM)] * len(operands),
         out_specs=[pl.BlockSpec(memory_space=pltpu.VMEM)] * 2,
         scratch_shapes=[pltpu.VMEM(operand.shape, operand.dtype) for operand in operands]
-        + [pltpu.SemaphoreType.DMA((len(operands) + 3,))],
+        + [
+            pltpu.VMEM((HEADS * tokens // passes, HEADS * HD), jnp.bfloat16),
+            pltpu.SemaphoreType.DMA((len(operands) + 3,)),
+        ],
         compiler_params=pltpu.CompilerParams(vmem_limit_bytes=60 * 1024 * 1024),
         cost_estimate=pl.CostEstimate(
             flops=2 * macs, bytes_accessed=6 * 1024 * 1024, transcendentals=0
@@ -556,8 +561,6 @@
         row_count,
         rest=store_count - ahead,
     )
-    codes, last_rows = lax.optimization_barrier((codes, last_rows))
-    last_rows = lax.ppermute(last_rows, "dp", across)
     own_half = hand_on(blocks)
     plan = codes[:, 0, row_count:]
     wanted = plan[:, :token_cap].reshape(peer_count * token_cap)
@@ -565,6 +568,8 @@
     found = jnp.dot(
         chosen.astype(jnp.bfloat16), word_table, preferred_element_type=jnp.float32
     ).astype(jnp.bfloat16)
+    found, last_rows = lax.optimization_barrier((found, last_rows))
+    last_rows = lax.ppermute(last_rows, "dp", across)
     found, first_rows, own_half[:2] = lax.optimization_barrier(
         (found, first_rows, own_half[:2])
     )

time: 75.6 us -> 78.8 us (1.042)
  starting transfers between devices: 29.5 us -> 32.2 us
    ppermute x6, starting transfers between devices: 7.57 us -> 10 us  [hand_on(): got.append(lax.ppermute(blocks[step], 'dp', moves))]
    ppermute x1, waiting for transfers between devices: 1.79 us -> 3.58 us  [shards(): last_rows = lax.ppermute(last_rows, 'dp', across)]
    ppermute x6, waiting for transfers between devices: 1.72 us -> 0.02 us  [hand_on(): got.append(lax.ppermute(blocks[step], 'dp', moves))]
    all_to_all x1, waiting for transfers between devices: 5.11 us -> 6.79 us  [shards(): lax.all_to_all(spread, 'dp', split_axis=0, concat_axis=0, tiled=True)]
    all_to_all x1, waiting for transfers between devices: 1.35 us -> 0.01 us  [shards(): lax.all_to_all(found.reshape(peer_count, token_cap, width), 'dp', split_a...]
  transfers between devices with their start and end apart: 15 -> 15, of which waited for: 6 -> 4; matrix products, arithmetic and copies ran while one was open for 6% -> 6% of each run, Pallas kernels for 21% -> 21%
where the time goes in v25:
time: 78.8 us; the launch traced here: 78.3 us
  starting transfers between devices  32.2 us (41%)
  Pallas kernels  20.1 us (26%)
  waiting for transfers between devices  17 us (22%)
  local copies, waits for them, and re-layouts  6.67 us (8%)
  matrix products  1.29 us (2%)
  between operations  0.93 us (1%)
    ppermute x6, starting transfers between devices, hand_on(): got.append(lax.ppermute(blocks[step], 'dp', moves))  10 us
    all_to_all x1, starting transfers between devices, shards(): lax.all_to_all(spread, 'dp', split_axis=0, concat_axis=0, tiled=True)  7.05 us
    all_to_all x1, waiting for transfers between devices, shards(): lax.all_to_all(spread, 'dp', split_axis=0, concat_axis=0, tiled=True)  6.79 us
    pallas_call x2, Pallas kernels, pack_rows(): pl.pallas_call(functools.partial(pack_kernel, half, row_cap, count, picks...  5.49 us
    all_to_all x1, waiting for transfers between devices, shards(): codes = lax.all_to_all(plan, 'dp', split_axis=0, concat_axis=0, tiled=True)  5.46 us
    pallas_call x1, Pallas kernels, encode(): pl.pallas_call(encode_kernel, out_shape=[jax.ShapeDtypeStruct((passes, wi...  4.94 us
    pallas_call x1, Pallas kernels, late_update(): pl.pallas_call(late_kernel, out_shape=jax.ShapeDtypeStruct(early.shape, j...  4.02 us
    all_to_all x1, starting transfers between devices, shards(): codes = lax.all_to_all(plan, 'dp', split_axis=0, concat_axis=0, tiled=True)  3.92 us
  transfers between devices with their start and end apart: 15, of which 4 were waited for; matrix products, arithmetic and copies ran while one was open for 6% of the time, Pallas kernels for 21%

profile of v25, /device:TPU:0, one launch (start us, length us, event | category | flops | bytes accessed | tf_op | source)
XLA Modules:
  0.0 78.3 jit_solution(7891906798170178516)
XLA Ops:
  0.6 0.0 copy-start
  0.6 0.5 collective-permute-start.1
  1.2 1.0 %slice.17 = bf16[176,1024]{1,0:T(8,128)(2,1)S(1)} slice(bf16[254,1024]{1,0:T(8,128)(2,1)} %refs_2_.1), slice={[0:176], [0:1024]} | slice | bytes 720896 | tf_op jit(solution)/shard_map/slice | solution.py:545
  2.2 3.7 %collective-permute-start.2 = (bf16[176,1024]{1,0:T(8,128)(2,1)S(1)}, bf16[176,1024]{1,0:T(8,128)(2,1)S(1)}, u32[]{:S(2)}, u32[]{:S(2)}) collective-permute-start(bf16[176,1024]{1,0:T(8,128)(2,1)S(1)} %slice.17), channel_id=1, source_target_pairs={{0,8},{1,9},{2,10},{3,11},{4,12},{5,13},{6,14},{7,15},{8,0},{9,1},... | collective-permute-start | bytes 1081352 | tf_op jit(solution)/shard_map/ppermute | solution.py:545
  5.9 0.2 collective-permute-start
  6.1 1.2 %collective-permute-done.sibling_far = s32[1,256]{1,0:T(1,128)S(1)} collective-permute-done((s32[1,256]{1,0:T(1,128)}, s32[1,256]{1,0:T(1,128)S(1)}, u32[]{:S(2)}, u32[]{:S(2)}) %collective-permute-start) | collective-permute-done | bytes 1056 | tf_op jit(solution)/shard_map/ppermute | solution.py:548
  7.2 0.6 copy-done.14
  7.8 2.3 %route.1 = (s32[16,1,330]{2,1,0:T(1,128)}, s32[128,1]{1,0:T(8,128)}, s32[1,256]{1,0:T(1,128)}, s32[1,256]{1,0:T(1,128)}) custom-call(s32[2,64]{1,0:T(2,128)} %token_ids_far.1, s32[1,256]{1,0:T(1,128)} %bitcast.25, s32[1,256]{1,0:T(1,128)} %bitcast.26, s32[1,256]{1,0:T(1,128)} %copy-done.14), custom_call_target="tpu_custom_call" | custom-call | tf_op jit(solution)/shard_map/route/pallas_call | solution.py:233
  10.1 0.0 collective-permute-done.1.refs_3_
  10.1 0.0 copy-start.2
  10.1 3.9 %all-to-all-start = ((s32[16,1,330]{2,1,0:T(1,128)}), s32[16,1,330]{2,1,0:T(1,128)S(1)}, u32[]{:S(2)}, u32[]{:S(2)}) async-start(s32[16,1,330]{2,1,0:T(1,128)} %get-tuple-element.40), calls=%async_computation | async-start | bytes 49152 | tf_op jit(solution)/shard_map/all_to_all | solution.py:553
  14.1 0.0 copy-done.2
  14.1 2.6 %pack.2 = (bf16[96,1024]{1,0:T(8,128)(2,1)}, bf16[96,1024]{1,0:T(8,128)(2,1)}, bf16[96,1024]{1,0:T(8,128)(2,1)}, bf16[96,1024]{1,0:T(8,128)(2,1)}, bf16[78,1024]{1,0:T(8,128)(2,1)}) custom-call(s32[1,256]{1,0:T(1,128)} %get-tuple-element.41.refs_0_, s32[1,256]{1,0:T(1,128)} %get-tuple-element.42.refs_1_, bf16[254,1024]{1,0:T(8,128)(2,1)} %refs_2_.1, ...), custom_call_target="tpu_custom_call" | custom-call | flops 199753728 | bytes 1826816 | tf_op jit(solution)/shard_map/pack/pallas_call | solution.py:324
  16.7 2.0 %collective-permute-start.3 = (bf16[96,1024]{1,0:T(8,128)(2,1)}, bf16[96,1024]{1,0:T(8,128)(2,1)S(1)}, u32[]{:S(2)}, u32[]{:S(2)}) collective-permute-start(bf16[96,1024]{1,0:T(8,128)(2,1)} %get-tuple-element.47), channel_id=1, source_target_pairs={{0,2},{1,3},{2,0},{3,1},{4,6},{5,7},{6,4},{7,5},{8,10},{9,11},{10,... | collective-permute-start | bytes 589832 | tf_op jit(solution)/shard_map/ppermute | solution.py:540
  18.7 5.5 %all-to-all-done.refs_0_.refs_1_ = s32[16,1,330]{2,1,0:T(1,128)S(1)} async-done(((s32[16,1,330]{2,1,0:T(1,128)}), s32[16,1,330]{2,1,0:T(1,128)S(1)}, u32[]{:S(2)}, u32[]{:S(2)}) %all-to-all-start) | async-done | bytes 21152 | tf_op jit(solution)/shard_map/all_to_all | solution.py:553
  24.2 0.1 eq.15
  24.3 0.0 copy-done
  24.3 1.3 %convolution_convert_fusion = bf16[384,1024]{1,0:T(8,128)(2,1)} fusion(bf16[240,1024]{1,0:T(8,128)(2,1)S(1)} %copy-done, s32[384]{0:T(512)S(1)} %eq.15), kind=kOutput, calls=%fused_computation.1 | convolution fusion | flops 189229056 | bytes 1279488 | tf_op jit(solution)/shard_map/dot_general | solution.py:568
  25.6 2.7 %collective-permute-start.4 = (bf16[78,1024]{1,0:T(8,128)(2,1)}, bf16[78,1024]{1,0:T(8,128)(2,1)S(1)}, u32[]{:S(2)}, u32[]{:S(2)}) collective-permute-start(bf16[78,1024]{1,0:T(8,128)(2,1)} %get-tuple-element.52), channel_id=1, source_target_pairs={{0,8},{1,9},{2,10},{3,11},{4,12},{5,13},{6,14},{7,15},{8,0},{9,1},... | collective-permute-start | bytes 479240 | tf_op jit(solution)/shard_map/ppermute | solution.py:572
  28.3 0.0 collective-permute-done.2.refs_2_
  28.3 0.0 collective-permute-done.3.rest_1_
  28.3 0.0 copy-start.17
  28.3 3.6 %all-to-all-start.1 = ((bf16[16,24,1024]{2,1,0:T(8,128)(2,1)}), bf16[16,24,1024]{2,1,0:T(8,128)(2,1)S(1)}, u32[]{:S(2)}, u32[]{:S(2)}) async-start(bf16[16,24,1024]{2,1,0:T(8,128)(2,1)} %bitcast.4), calls=%async_computation.1 | async-start | bytes 1572864 | tf_op jit(solution)/shard_map/all_to_all | solution.py:576
  31.9 0.1 slice.24
  32.0 0.6 gather_fusion
  32.6 0.7 reshape.41.places_far
  33.3 3.6 %collective-permute-done.4.refs_3_ = bf16[78,1024]{1,0:T(8,128)(2,1)S(1)} collective-permute-done((bf16[78,1024]{1,0:T(8,128)(2,1)}, bf16[78,1024]{1,0:T(8,128)(2,1)S(1)}, u32[]{:S(2)}, u32[]{:S(2)}) %collective-permute-start.4) | collective-permute-done | bytes 159776 | tf_op jit(solution)/shard_map/ppermute | solution.py:572
  36.8 0.0 copy-done.17
  36.8 3.4 %early.1 = (f32[512,1024]{1,0:T(8,128)}, f32[512,128]{1,0:T(8,128)}) custom-call(s32[1,768]{1,0:T(1,128)} %reshape.41.places_far, f32[512,1024]{1,0:T(8,128)} %centroids_far.1, bf16[96,1024]{1,0:T(8,128)(2,1)} %get-tuple-element.54.rest_0_, bf16[96,1024]{1,0:T(8,128)(2,1)} %copy-done.17), custom_call_target="tpu_custom_call" | custom-call | flops 10066329600 | bytes 104857600 | tf_op jit(solution)/shard_map/early/pallas_call | solution.py:447
  40.2 0.0 copy-done.5
  40.2 0.0 copy-done.3
  40.2 0.1 collective-permute-start.7
  40.3 0.0 copy-done.12
  40.3 0.5 collective-permute-start.8
  40.8 0.0 copy-done.16
  40.8 4.5 %collective-permute-start.5 = (bf16[96,1024]{1,0:T(8,128)(2,1)S(1)}, bf16[96,1024]{1,0:T(8,128)(2,1)S(1)}, u32[]{:S(2)}, u32[]{:S(2)}) collective-permute-start(bf16[96,1024]{1,0:T(8,128)(2,1)S(1)} %copy-done.16), channel_id=1, source_target_pairs={{0,4},{1,5},{2,6},{3,7},{4,0},{5,1},{6,2},{7,3},{8,12},{9,13},{10,... | collective-permute-start | bytes 589832 | tf_op jit(solution)/shard_map/ppermute | solution.py:540
  45.3 0.0 copy-done.15
  45.3 0.0 collective-permute-start.6
  45.3 0.0 collective-permute-done.8.refs_5_
  45.3 0.0 collective-permute-done.7.refs_4_
  45.3 0.7 copy-done.13
  46.0 0.7 copy-done.4
  46.7 2.8 %pack.3 = (bf16[96,1024]{1,0:T(8,128)(2,1)}, bf16[96,1024]{1,0:T(8,128)(2,1)}, bf16[96,1024]{1,0:T(8,128)(2,1)}, bf16[96,1024]{1,0:T(8,128)(2,1)}) custom-call(s32[16,1,330]{2,1,0:T(1,128)} %copy-done.5, s32[16,1,330]{2,1,0:T(1,128)} %copy-done.5, bf16[176,1024]{1,0:T(8,128)(2,1)} %copy-done.3, bf16[78,1024]{1,0:T(8,128)(2,1)} %copy-done.12, ...), custom_call_target="tpu_custom_call" | custom-call | flops 199753728 | bytes 1826816 | tf_op jit(solution)/shard_map/pack/pallas_call | solution.py:324
  49.6 1.6 %collective-permute-start.9 = (bf16[96,1024]{1,0:T(8,128)(2,1)}, bf16[96,1024]{1,0:T(8,128)(2,1)S(1)}, u32[]{:S(2)}, u32[]{:S(2)}) collective-permute-start(bf16[96,1024]{1,0:T(8,128)(2,1)} %get-tuple-element.71), channel_id=1, source_target_pairs={{0,2},{1,3},{2,0},{3,1},{4,6},{5,7},{6,4},{7,5},{8,10},{9,11},{10,... | collective-permute-start | bytes 589832 | tf_op jit(solution)/shard_map/ppermute | solution.py:540
  51.1 2.0 %collective-permute-start.10 = (bf16[96,1024]{1,0:T(8,128)(2,1)}, bf16[96,1024]{1,0:T(8,128)(2,1)S(1)}, u32[]{:S(2)}, u32[]{:S(2)}) collective-permute-start(bf16[96,1024]{1,0:T(8,128)(2,1)} %get-tuple-element.72), channel_id=1, source_target_pairs={{0,4},{1,5},{2,6},{3,7},{4,0},{5,1},{6,2},{7,3},{8,12},{9,13},{10,... | collective-permute-start | bytes 589832 | tf_op jit(solution)/shard_map/ppermute | solution.py:540
  53.1 0.0 collective-permute-start.11
  53.1 0.1 slice.25
  53.2 0.7 reshape.42.late_far
  53.9 0.0 all-to-all-done.1
  53.9 0.9 %copy-done.1 = bf16[16,24,1024]{2,1,0:T(8,128)(2,1)} copy-done((bf16[16,24,1024]{2,1,0:T(8,128)(2,1)}, bf16[16,24,1024]{2,1,0:T(8,128)(2,1)S(1)}, u32[]{:S(2)}) %copy-start.1) | copy-done | bytes 786456
  54.8 4.9 %encode.1 = (bf16[2,1024]{1,0:T(2,128)(2,1)}, bf16[16,2,1024]{2,1,0:T(2,128)(2,1)}) custom-call(s32[1,2]{1,0:T(1,128)} %bitcast.27, s32[128,1]{1,0:T(8,128)} %get-tuple-element.38.refs_1_, bf16[384,1024]{1,0:T(8,128)(2,1)} %bitcast.15, bf16[64,1024]{1,0:T(8,128)(2,1)} %refs_3_.1, f32[1,1024]{1,0:T(1,128)} %bitcast.19, f32[1,1024]{1,0:T(1,128)} %bitcast.20, ...), custom_call_target="tpu_custom_call" | custom-call | flops 637534208 | bytes 6291456 | tf_op jit(solution)/shard_map/encode/pallas_call | solution.py:123
  59.7 7.0 %all-to-all-start.2 = ((bf16[16,2,1024]{2,1,0:T(2,128)(2,1)}), bf16[16,2,1024]{2,1,0:T(2,128)(2,1)S(1)}, u32[]{:S(2)}, u32[]{:S(2)}) async-start(bf16[16,2,1024]{2,1,0:T(2,128)(2,1)} %get-tuple-element.63), calls=%async_computation.2 | async-start | bytes 131072 | tf_op jit(solution)/shard_map/all_to_all | solution.py:611
  66.8 0.0 collective-permute-done.5.rest_0_
  66.8 0.0 copy-start.7
  66.8 0.0 collective-permute-done.6.rest_1_
  66.8 0.0 copy-start.8
  66.8 0.0 collective-permute-done.9.rest_3_
  66.8 0.0 copy-start.9
  66.9 0.0 collective-permute-done.10.rest_4_
  66.9 0.0 collective-permute-done.11.rest_5_
  66.9 0.0 copy-start.11
  66.9 6.8 %all-to-all-done.2.spread_far = bf16[16,2,1024]{2,1,0:T(2,128)(2,1)S(1)} async-done(((bf16[16,2,1024]{2,1,0:T(2,128)(2,1)}), bf16[16,2,1024]{2,1,0:T(2,128)(2,1)S(1)}, u32[]{:S(2)}, u32[]{:S(2)}) %all-to-all-start.2) | async-done | bytes 65568 | tf_op jit(solution)/shard_map/all_to_all | solution.py:611
  73.7 0.6 copy-done.6
  74.3 4.0 %late.1 = f32[512,1024]{1,0:T(8,128)} custom-call(s32[1,768]{1,0:T(1,128)} %reshape.41.places_far, s32[1,32]{1,0:T(1,128)} %reshape.42.late_far, bf16[16,2,1024]{2,1,0:T(2,128)(2,1)} %copy-done.6, f32[512,128]{1,0:T(8,128)} %get-tuple-element.64.share_far, f32[512,1024]{1,0:T(8,128)} %get-tuple-element.65.early_far, bf16[96,1024]{1,0:T(8,128)(2,1)} %copy-done.7, ...), custom_call_target="tpu_custom_call" | custom-call | flops 637534208 | bytes 4194304 | tf_op jit(solution)/shard_map/late/pallas_call | solution.py:479
  (19 shorter events, 0.0 us)
Async XLA Ops:
  0.6 23.7 %copy-start = (bf16[240,1024]{1,0:T(8,128)(2,1)S(1)}, bf16[240,1024]{1,0:T(8,128)(2,1)}, u32[]{:S(2)}) copy-start(bf16[240,1024]{1,0:T(8,128)(2,1)} %param.17) | copy-start | bytes 1474564
  0.6 9.5 %collective-permute-start.1 = (bf16[254,1024]{1,0:T(8,128)(2,1)}, bf16[254,1024]{1,0:T(8,128)(2,1)S(1)}, u32[]{:S(2)}, u32[]{:S(2)}) collective-permute-start(bf16[254,1024]{1,0:T(8,128)(2,1)} %refs_2_.1), channel_id=1, source_target_pairs={{0,1},{1,0},{2,3},{3,2},{4,5},{5,4},{6,7},{7,6},{8,9},{9,8},{10,11... | collective-permute-start | bytes 1560584 | tf_op jit(solution)/shard_map/ppermute | solution.py:544
  2.2 26.1 %collective-permute-start.2 = (bf16[176,1024]{1,0:T(8,128)(2,1)S(1)}, bf16[176,1024]{1,0:T(8,128)(2,1)S(1)}, u32[]{:S(2)}, u32[]{:S(2)}) collective-permute-start(bf16[176,1024]{1,0:T(8,128)(2,1)S(1)} %slice.17), channel_id=1, source_target_pairs={{0,8},{1,9},{2,10},{3,11},{4,12},{5,13},{6,14},{7,15},{8,0},{9,1},... | collective-permute-start | bytes 1081352 | tf_op jit(solution)/shard_map/ppermute | solution.py:545
  5.9 1.4 %collective-permute-start = (s32[1,256]{1,0:T(1,128)}, s32[1,256]{1,0:T(1,128)S(1)}, u32[]{:S(2)}, u32[]{:S(2)}) collective-permute-start(s32[1,256]{1,0:T(1,128)} %bitcast.24), channel_id=1, source_target_pairs={{0,1},{1,0},{2,3},{3,2},{4,5},{5,4},{6,7},{7,6},{8,9},{9,8},{10,11... | collective-permute-start | bytes 3080 | tf_op jit(solution)/shard_map/ppermute | solution.py:548
  7.2 0.6 copy-start.14
  10.1 4.0 %copy-start.2 = (bf16[254,1024]{1,0:T(8,128)(2,1)}, bf16[254,1024]{1,0:T(8,128)(2,1)S(1)}, u32[]{:S(2)}) copy-start(bf16[254,1024]{1,0:T(8,128)(2,1)S(1)} %collective-permute-done.1.refs_3_) | copy-start | bytes 1560580
  10.1 14.0 %all-to-all-start = ((s32[16,1,330]{2,1,0:T(1,128)}), s32[16,1,330]{2,1,0:T(1,128)S(1)}, u32[]{:S(2)}, u32[]{:S(2)}) async-start(s32[16,1,330]{2,1,0:T(1,128)} %get-tuple-element.40), calls=%async_computation | async-start | bytes 49152 | tf_op jit(solution)/shard_map/all_to_all | solution.py:553
  16.7 11.5 %collective-permute-start.3 = (bf16[96,1024]{1,0:T(8,128)(2,1)}, bf16[96,1024]{1,0:T(8,128)(2,1)S(1)}, u32[]{:S(2)}, u32[]{:S(2)}) collective-permute-start(bf16[96,1024]{1,0:T(8,128)(2,1)} %get-tuple-element.47), channel_id=1, source_target_pairs={{0,2},{1,3},{2,0},{3,1},{4,6},{5,7},{6,4},{7,5},{8,10},{9,11},{10,... | collective-permute-start | bytes 589832 | tf_op jit(solution)/shard_map/ppermute | solution.py:540
  24.2 16.0 %copy-start.5 = (s32[16,1,330]{2,1,0:T(1,128)}, s32[16,1,330]{2,1,0:T(1,128)S(1)}, u32[]{:S(2)}) copy-start(s32[16,1,330]{2,1,0:T(1,128)S(1)} %all-to-all-done.refs_0_.refs_1_) | copy-start | bytes 63364
  25.6 11.2 %collective-permute-start.4 = (bf16[78,1024]{1,0:T(8,128)(2,1)}, bf16[78,1024]{1,0:T(8,128)(2,1)S(1)}, u32[]{:S(2)}, u32[]{:S(2)}) collective-permute-start(bf16[78,1024]{1,0:T(8,128)(2,1)} %get-tuple-element.52), channel_id=1, source_target_pairs={{0,8},{1,9},{2,10},{3,11},{4,12},{5,13},{6,14},{7,15},{8,0},{9,1},... | collective-permute-start | bytes 479240 | tf_op jit(solution)/shard_map/ppermute | solution.py:572
  28.3 12.0 %copy-start.3 = (bf16[176,1024]{1,0:T(8,128)(2,1)}, bf16[176,1024]{1,0:T(8,128)(2,1)S(1)}, u32[]{:S(2)}) copy-start(bf16[176,1024]{1,0:T(8,128)(2,1)S(1)} %collective-permute-done.2.refs_2_) | copy-start | bytes 1081348
  28.3 8.6 %copy-start.17 = (bf16[96,1024]{1,0:T(8,128)(2,1)}, bf16[96,1024]{1,0:T(8,128)(2,1)S(1)}, u32[]{:S(2)}) copy-start(bf16[96,1024]{1,0:T(8,128)(2,1)S(1)} %collective-permute-done.3.rest_1_) | copy-start | bytes 589828
  28.3 25.6 %all-to-all-start.1 = ((bf16[16,24,1024]{2,1,0:T(8,128)(2,1)}), bf16[16,24,1024]{2,1,0:T(8,128)(2,1)S(1)}, u32[]{:S(2)}, u32[]{:S(2)}) async-start(bf16[16,24,1024]{2,1,0:T(8,128)(2,1)} %bitcast.4), calls=%async_computation.1 | async-start | bytes 1572864 | tf_op jit(solution)/shard_map/all_to_all | solution.py:576
  33.3 7.6 %copy-start.16 = (bf16[96,1024]{1,0:T(8,128)(2,1)S(1)}, bf16[96,1024]{1,0:T(8,128)(2,1)}, u32[]{:S(2)}) copy-start(bf16[96,1024]{1,0:T(8,128)(2,1)} %get-tuple-element.66) | copy-start | bytes 589828
  33.3 12.0 %copy-start.15 = (bf16[96,1024]{1,0:T(8,128)(2,1)S(1)}, bf16[96,1024]{1,0:T(8,128)(2,1)}, u32[]{:S(2)}) copy-start(bf16[96,1024]{1,0:T(8,128)(2,1)} %get-tuple-element.67) | copy-start | bytes 589828
  36.8 3.5 %copy-start.12 = (bf16[78,1024]{1,0:T(8,128)(2,1)}, bf16[78,1024]{1,0:T(8,128)(2,1)S(1)}, u32[]{:S(2)}) copy-start(bf16[78,1024]{1,0:T(8,128)(2,1)S(1)} %collective-permute-done.4.refs_3_) | copy-start | bytes 479236
  40.2 5.1 %collective-permute-start.7 = (bf16[176,1024]{1,0:T(8,128)(2,1)S(1)}, bf16[176,1024]{1,0:T(8,128)(2,1)S(1)}, u32[]{:S(2)}, u32[]{:S(2)}) collective-permute-start(bf16[176,1024]{1,0:T(8,128)(2,1)S(1)} %collective-permute-done.2.refs_2_), channel_id=1, source_target_pairs={{0,1},{1,0},{2,3},{3,2},{4,5},{5,4},{6,7},{7,6},{8,9},{9,8},{10,11... | collective-permute-start | bytes 1081352 | tf_op jit(solution)/shard_map/ppermute | solution.py:588
  40.3 5.0 %collective-permute-start.8 = (bf16[78,1024]{1,0:T(8,128)(2,1)S(1)}, bf16[78,1024]{1,0:T(8,128)(2,1)S(1)}, u32[]{:S(2)}, u32[]{:S(2)}) collective-permute-start(bf16[78,1024]{1,0:T(8,128)(2,1)S(1)} %collective-permute-done.4.refs_3_), channel_id=1, source_target_pairs={{0,1},{1,0},{2,3},{3,2},{4,5},{5,4},{6,7},{7,6},{8,9},{9,8},{10,11... | collective-permute-start | bytes 479240 | tf_op jit(solution)/shard_map/ppermute | solution.py:588
  40.8 26.0 %collective-permute-start.5 = (bf16[96,1024]{1,0:T(8,128)(2,1)S(1)}, bf16[96,1024]{1,0:T(8,128)(2,1)S(1)}, u32[]{:S(2)}, u32[]{:S(2)}) collective-permute-start(bf16[96,1024]{1,0:T(8,128)(2,1)S(1)} %copy-done.16), channel_id=1, source_target_pairs={{0,4},{1,5},{2,6},{3,7},{4,0},{5,1},{6,2},{7,3},{8,12},{9,13},{10,... | collective-permute-start | bytes 589832 | tf_op jit(solution)/shard_map/ppermute | solution.py:540
  45.3 21.5 %collective-permute-start.6 = (bf16[96,1024]{1,0:T(8,128)(2,1)S(1)}, bf16[96,1024]{1,0:T(8,128)(2,1)S(1)}, u32[]{:S(2)}, u32[]{:S(2)}) collective-permute-start(bf16[96,1024]{1,0:T(8,128)(2,1)S(1)} %copy-done.15), channel_id=1, source_target_pairs={{0,6},{1,7},{2,4},{3,5},{4,2},{5,3},{6,0},{7,1},{8,14},{9,15},{10,... | collective-permute-start | bytes 589832 | tf_op jit(solution)/shard_map/ppermute | solution.py:540
  45.3 0.7 copy-start.13
  46.0 0.7 copy-start.4
  49.6 17.2 %collective-permute-start.9 = (bf16[96,1024]{1,0:T(8,128)(2,1)}, bf16[96,1024]{1,0:T(8,128)(2,1)S(1)}, u32[]{:S(2)}, u32[]{:S(2)}) collective-permute-start(bf16[96,1024]{1,0:T(8,128)(2,1)} %get-tuple-element.71), channel_id=1, source_target_pairs={{0,2},{1,3},{2,0},{3,1},{4,6},{5,7},{6,4},{7,5},{8,10},{9,11},{10,... | collective-permute-start | bytes 589832 | tf_op jit(solution)/shard_map/ppermute | solution.py:540
  51.1 15.7 %collective-permute-start.10 = (bf16[96,1024]{1,0:T(8,128)(2,1)}, bf16[96,1024]{1,0:T(8,128)(2,1)S(1)}, u32[]{:S(2)}, u32[]{:S(2)}) collective-permute-start(bf16[96,1024]{1,0:T(8,128)(2,1)} %get-tuple-element.72), channel_id=1, source_target_pairs={{0,4},{1,5},{2,6},{3,7},{4,0},{5,1},{6,2},{7,3},{8,12},{9,13},{10,... | collective-permute-start | bytes 589832 | tf_op jit(solution)/shard_map/ppermute | solution.py:540
  53.1 13.8 %collective-permute-start.11 = (bf16[96,1024]{1,0:T(8,128)(2,1)}, bf16[96,1024]{1,0:T(8,128)(2,1)S(1)}, u32[]{:S(2)}, u32[]{:S(2)}) collective-permute-start(bf16[96,1024]{1,0:T(8,128)(2,1)} %get-tuple-element.73), channel_id=1, source_target_pairs={{0,6},{1,7},{2,4},{3,5},{4,2},{5,3},{6,0},{7,1},{8,14},{9,15},{10,... | collective-permute-start | bytes 589832 | tf_op jit(solution)/shard_map/ppermute | solution.py:540
  53.9 0.9 %copy-start.1 = (bf16[16,24,1024]{2,1,0:T(8,128)(2,1)}, bf16[16,24,1024]{2,1,0:T(8,128)(2,1)S(1)}, u32[]{:S(2)}) copy-start(bf16[16,24,1024]{2,1,0:T(8,128)(2,1)S(1)} %all-to-all-done.1) | copy-start | bytes 2359300
  59.7 14.0 %all-to-all-start.2 = ((bf16[16,2,1024]{2,1,0:T(2,128)(2,1)}), bf16[16,2,1024]{2,1,0:T(2,128)(2,1)S(1)}, u32[]{:S(2)}, u32[]{:S(2)}) async-start(bf16[16,2,1024]{2,1,0:T(2,128)(2,1)} %get-tuple-element.63), calls=%async_computation.2 | async-start | bytes 131072 | tf_op jit(solution)/shard_map/all_to_all | solution.py:611
  66.8 6.9 %copy-start.7 = (bf16[96,1024]{1,0:T(8,128)(2,1)}, bf16[96,1024]{1,0:T(8,128)(2,1)S(1)}, u32[]{:S(2)}) copy-start(bf16[96,1024]{1,0:T(8,128)(2,1)S(1)} %collective-permute-done.5.rest_0_) | copy-start | bytes 589828
  66.8 6.9 %copy-start.8 = (bf16[96,1024]{1,0:T(8,128)(2,1)}, bf16[96,1024]{1,0:T(8,128)(2,1)S(1)}, u32[]{:S(2)}) copy-start(bf16[96,1024]{1,0:T(8,128)(2,1)S(1)} %collective-permute-done.6.rest_1_) | copy-start | bytes 589828
  66.8 6.9 %copy-start.9 = (bf16[96,1024]{1,0:T(8,128)(2,1)}, bf16[96,1024]{1,0:T(8,128)(2,1)S(1)}, u32[]{:S(2)}) copy-start(bf16[96,1024]{1,0:T(8,128)(2,1)S(1)} %collective-permute-done.9.rest_3_) | copy-start | bytes 589828
  66.9 6.8 %copy-start.10 = (bf16[96,1024]{1,0:T(8,128)(2,1)}, bf16[96,1024]{1,0:T(8,128)(2,1)S(1)}, u32[]{:S(2)}) copy-start(bf16[96,1024]{1,0:T(8,128)(2,1)S(1)} %collective-permute-done.10.rest_4_) | copy-start | bytes 589828
  66.9 6.8 %copy-start.11 = (bf16[96,1024]{1,0:T(8,128)(2,1)}, bf16[96,1024]{1,0:T(8,128)(2,1)S(1)}, u32[]{:S(2)}) copy-start(bf16[96,1024]{1,0:T(8,128)(2,1)S(1)} %collective-permute-done.11.rest_5_) | copy-start | bytes 589828
  73.7 0.6 copy-start.6

commit v26 on v23

--- a/solution.py
+++ b/solution.py
@@ -565,8 +565,8 @@
     found = jnp.dot(
         chosen.astype(jnp.bfloat16), word_table, preferred_element_type=jnp.float32
     ).astype(jnp.bfloat16)
-    found, first_rows, own_half[:2] = lax.optimization_barrier(
-        (found, first_rows, own_half[:2])
+    found, plan, first_rows, own_half[:2] = lax.optimization_barrier(
+        (found, plan, first_rows, own_half[:2])
     )
     fetched = lax.all_to_all(
         found.reshape(peer_count, token_cap, width), "dp", split_axis=0, concat_axis=0, tiled=True

time: 76.5 us -> 75 us (0.980)
  starting transfers between devices: 29.6 us -> 28.1 us
    ppermute x1, waiting for transfers between devices: 2.44 us -> 0.01 us  [shards(): last_rows = lax.ppermute(last_rows, 'dp', across)]
    ppermute x6, waiting for transfers between devices: 0.79 us -> 2.83 us  [hand_on(): got.append(lax.ppermute(blocks[step], 'dp', moves))]
    all_to_all x1, starting transfers between devices: 7.04 us -> 5.54 us  [shards(): lax.all_to_all(spread, 'dp', split_axis=0, concat_axis=0, tiled=True)]
  transfers between devices with their start and end apart: 15 -> 15, of which waited for: 6 -> 5; matrix products, arithmetic and copies ran while one was open for 6% -> 6% of each run, Pallas kernels for 22% -> 22%
where the time goes in v26:
time: 75 us; the launch traced here: 74.5 us
  starting transfers between devices  28.1 us (37%)
  Pallas kernels  20.2 us (27%)
  waiting for transfers between devices  16.7 us (22%)
  local copies, waits for them, and re-layouts  7.3 us (10%)
  matrix products  1.29 us (2%)
  between operations  0.88 us (1%)
    ppermute x6, starting transfers between devices, hand_on(): got.append(lax.ppermute(blocks[step], 'dp', moves))  7.1 us
    all_to_all x1, waiting for transfers between devices, shards(): lax.all_to_all(spread, 'dp', split_axis=0, concat_axis=0, tiled=True)  6.83 us
    all_to_all x1, starting transfers between devices, shards(): lax.all_to_all(spread, 'dp', split_axis=0, concat_axis=0, tiled=True)  5.54 us
    pallas_call x2, Pallas kernels, pack_rows(): pl.pallas_call(functools.partial(pack_kernel, half, row_cap, count, picks...  5.47 us
    pallas_call x1, Pallas kernels, encode(): pl.pallas_call(encode_kernel, out_shape=[jax.ShapeDtypeStruct((passes, wi...  4.97 us
    all_to_all x1, waiting for transfers between devices, shards(): codes = lax.all_to_all(plan, 'dp', split_axis=0, concat_axis=0, tiled=True)  4.82 us
    unnamed x32, local copies, waits for them, and re-layouts  4.16 us
    ppermute x1, starting transfers between devices, shards(): first_rows = lax.ppermute(stored_rows[:ahead], 'dp', across)  4.08 us
  transfers between devices with their start and end apart: 15, of which 5 were waited for; matrix products, arithmetic and copies ran while one was open for 6% of the time, Pallas kernels for 22%

profile of v26, /device:TPU:0, one launch (start us, length us, event | category | flops | bytes accessed | tf_op | source)
XLA Modules:
  0.0 74.5 jit_solution(6444290724945156222)
XLA Ops:
  0.6 0.0 copy-start
  0.6 0.5 collective-permute-start.1
  1.2 0.1 collective-permute-start
  1.2 1.0 %slice.17 = bf16[176,1024]{1,0:T(8,128)(2,1)S(1)} slice(bf16[254,1024]{1,0:T(8,128)(2,1)} %refs_2_.1), slice={[0:176], [0:1024]} | slice | bytes 720896 | tf_op jit(solution)/shard_map/slice | solution.py:540
  2.3 4.1 %collective-permute-start.2 = (bf16[176,1024]{1,0:T(8,128)(2,1)S(1)}, bf16[176,1024]{1,0:T(8,128)(2,1)S(1)}, u32[]{:S(2)}, u32[]{:S(2)}) collective-permute-start(bf16[176,1024]{1,0:T(8,128)(2,1)S(1)} %slice.17), channel_id=1, source_target_pairs={{0,8},{1,9},{2,10},{3,11},{4,12},{5,13},{6,14},{7,15},{8,0},{9,1},... | collective-permute-start | bytes 1081352 | tf_op jit(solution)/shard_map/ppermute | solution.py:540
  6.3 0.0 collective-permute-done.sibling_far
  6.3 0.6 copy-done.12
  6.9 2.3 %route.1 = (s32[16,1,330]{2,1,0:T(1,128)}, s32[128,1]{1,0:T(8,128)}, s32[1,256]{1,0:T(1,128)}, s32[1,256]{1,0:T(1,128)}) custom-call(s32[2,64]{1,0:T(2,128)} %token_ids_far.1, s32[1,256]{1,0:T(1,128)} %bitcast.25, s32[1,256]{1,0:T(1,128)} %bitcast.26, s32[1,256]{1,0:T(1,128)} %copy-done.12), custom_call_target="tpu_custom_call" | custom-call | tf_op jit(solution)/shard_map/route/pallas_call | solution.py:228
  9.2 0.0 collective-permute-done.1.refs_3_
  9.2 0.0 copy-start.2
  9.3 3.9 %all-to-all-start = ((s32[16,1,330]{2,1,0:T(1,128)}), s32[16,1,330]{2,1,0:T(1,128)S(1)}, u32[]{:S(2)}, u32[]{:S(2)}) async-start(s32[16,1,330]{2,1,0:T(1,128)} %get-tuple-element.43), calls=%async_computation | async-start | bytes 49152 | tf_op jit(solution)/shard_map/all_to_all | solution.py:548
  13.2 0.0 copy-done.2
  13.2 2.6 %pack.2 = (bf16[96,1024]{1,0:T(8,128)(2,1)}, bf16[96,1024]{1,0:T(8,128)(2,1)}, bf16[96,1024]{1,0:T(8,128)(2,1)}, bf16[96,1024]{1,0:T(8,128)(2,1)}, bf16[78,1024]{1,0:T(8,128)(2,1)}) custom-call(s32[1,256]{1,0:T(1,128)} %get-tuple-element.44.refs_0_, s32[1,256]{1,0:T(1,128)} %get-tuple-element.45.refs_1_, bf16[254,1024]{1,0:T(8,128)(2,1)} %refs_2_.1, ...), custom_call_target="tpu_custom_call" | custom-call | flops 199753728 | bytes 1826816 | tf_op jit(solution)/shard_map/pack/pallas_call | solution.py:319
  15.9 2.0 %collective-permute-start.3 = (bf16[96,1024]{1,0:T(8,128)(2,1)}, bf16[96,1024]{1,0:T(8,128)(2,1)S(1)}, u32[]{:S(2)}, u32[]{:S(2)}) collective-permute-start(bf16[96,1024]{1,0:T(8,128)(2,1)} %get-tuple-element.50), channel_id=1, source_target_pairs={{0,2},{1,3},{2,0},{3,1},{4,6},{5,7},{6,4},{7,5},{8,10},{9,11},{10,... | collective-permute-start | bytes 589832 | tf_op jit(solution)/shard_map/ppermute | solution.py:535
  17.8 1.5 %collective-permute-start.4 = (bf16[96,1024]{1,0:T(8,128)(2,1)}, bf16[96,1024]{1,0:T(8,128)(2,1)S(1)}, u32[]{:S(2)}, u32[]{:S(2)}) collective-permute-start(bf16[96,1024]{1,0:T(8,128)(2,1)} %get-tuple-element.55), channel_id=1, source_target_pairs={{0,4},{1,5},{2,6},{3,7},{4,0},{5,1},{6,2},{7,3},{8,12},{9,13},{10,... | collective-permute-start | bytes 589832 | tf_op jit(solution)/shard_map/ppermute | solution.py:535
  19.3 0.1 collective-permute-start.5
  19.4 4.8 %all-to-all-done.refs_0_.refs_1_ = s32[16,1,330]{2,1,0:T(1,128)S(1)} async-done(((s32[16,1,330]{2,1,0:T(1,128)}), s32[16,1,330]{2,1,0:T(1,128)S(1)}, u32[]{:S(2)}, u32[]{:S(2)}) %all-to-all-start) | async-done | bytes 21152 | tf_op jit(solution)/shard_map/all_to_all | solution.py:548
  24.2 0.1 eq.15
  24.3 2.7 %collective-permute-start.6 = (bf16[78,1024]{1,0:T(8,128)(2,1)}, bf16[78,1024]{1,0:T(8,128)(2,1)S(1)}, u32[]{:S(2)}, u32[]{:S(2)}) collective-permute-start(bf16[78,1024]{1,0:T(8,128)(2,1)} %get-tuple-element.57), channel_id=1, source_target_pairs={{0,8},{1,9},{2,10},{3,11},{4,12},{5,13},{6,14},{7,15},{8,0},{9,1},... | collective-permute-start | bytes 479240 | tf_op jit(solution)/shard_map/ppermute | solution.py:560
  27.0 0.0 copy-done
  27.0 1.3 %convolution_convert_fusion = bf16[384,1024]{1,0:T(8,128)(2,1)} fusion(bf16[240,1024]{1,0:T(8,128)(2,1)S(1)} %copy-done, s32[384]{0:T(512)S(1)} %eq.15), kind=kOutput, calls=%fused_computation.1 | convolution fusion | flops 189229056 | bytes 1279488 | tf_op jit(solution)/shard_map/dot_general | solution.py:565
  28.3 0.0 collective-permute-done.2.refs_2_
  28.3 0.0 collective-permute-done.3.rest_1_
  28.3 0.0 copy-start.13
  28.3 0.1 slice.18
  28.4 0.6 gather_fusion
  29.0 0.7 reshape.41.places_far
  29.6 3.6 %all-to-all-start.1 = ((bf16[16,24,1024]{2,1,0:T(8,128)(2,1)}), bf16[16,24,1024]{2,1,0:T(8,128)(2,1)S(1)}, u32[]{:S(2)}, u32[]{:S(2)}) async-start(bf16[16,24,1024]{2,1,0:T(8,128)(2,1)} %bitcast.4), calls=%async_computation.1 | async-start | bytes 1572864 | tf_op jit(solution)/shard_map/all_to_all | solution.py:571
  33.3 0.0 collective-permute-done.4.rest_2_
  33.3 0.0 copy-start.14
  33.3 2.8 %collective-permute-done.5.rest_3_ = bf16[96,1024]{1,0:T(8,128)(2,1)S(1)} collective-permute-done((bf16[96,1024]{1,0:T(8,128)(2,1)}, bf16[96,1024]{1,0:T(8,128)(2,1)S(1)}, u32[]{:S(2)}, u32[]{:S(2)}) %collective-permute-start.5) | collective-permute-done | bytes 196640 | tf_op jit(solution)/shard_map/ppermute | solution.py:535
  36.1 0.0 collective-permute-done.6.refs_3_
  36.1 0.0 copy-done.13
  36.1 0.0 copy-done.14
  36.1 0.6 copy-done.15
  36.8 3.8 %early.1 = (f32[512,1024]{1,0:T(8,128)}, f32[512,128]{1,0:T(8,128)}) custom-call(s32[1,768]{1,0:T(1,128)} %reshape.41.places_far, f32[512,1024]{1,0:T(8,128)} %centroids_far.1, bf16[96,1024]{1,0:T(8,128)(2,1)} %get-tuple-element.60.rest_0_, bf16[96,1024]{1,0:T(8,128)(2,1)} %copy-done.13, bf16[96,1024]{1,0:T(8,128)(2,1)} %copy-done.14, ...), custom_call_target="tpu_custom_call" | custom-call | flops 20132659200 | bytes 104857600 | tf_op jit(solution)/shard_map/early/pallas_call | solution.py:442
  40.6 0.0 copy-done.5
  40.6 0.0 copy-done.3
  40.6 0.1 collective-permute-start.7
  40.8 0.0 copy-done.10
  40.8 0.4 collective-permute-start.8
  41.2 1.4 %collective-permute-done.8.refs_5_ = bf16[78,1024]{1,0:T(8,128)(2,1)S(1)} collective-permute-done((bf16[78,1024]{1,0:T(8,128)(2,1)S(1)}, bf16[78,1024]{1,0:T(8,128)(2,1)S(1)}, u32[]{:S(2)}, u32[]{:S(2)}) %collective-permute-start.8) | collective-permute-done | bytes 159776 | tf_op jit(solution)/shard_map/ppermute | solution.py:583
  42.6 0.0 collective-permute-done.7.refs_4_
  42.6 0.7 copy-done.11
  43.3 0.8 %copy-done.4 = bf16[176,1024]{1,0:T(8,128)(2,1)} copy-done((bf16[176,1024]{1,0:T(8,128)(2,1)}, bf16[176,1024]{1,0:T(8,128)(2,1)S(1)}, u32[]{:S(2)}) %copy-start.4) | copy-done | bytes 360472
  44.0 2.8 %pack.3 = (bf16[96,1024]{1,0:T(8,128)(2,1)}, bf16[96,1024]{1,0:T(8,128)(2,1)}, bf16[96,1024]{1,0:T(8,128)(2,1)}, bf16[96,1024]{1,0:T(8,128)(2,1)}) custom-call(s32[16,1,330]{2,1,0:T(1,128)} %copy-done.5, s32[16,1,330]{2,1,0:T(1,128)} %copy-done.5, bf16[176,1024]{1,0:T(8,128)(2,1)} %copy-done.3, bf16[78,1024]{1,0:T(8,128)(2,1)} %copy-done.10, ...), custom_call_target="tpu_custom_call" | custom-call | flops 199753728 | bytes 1826816 | tf_op jit(solution)/shard_map/pack/pallas_call | solution.py:319
  46.9 0.1 collective-permute-start.9
  46.9 0.5 collective-permute-start.10
  47.5 2.9 %collective-permute-start.11 = (bf16[96,1024]{1,0:T(8,128)(2,1)}, bf16[96,1024]{1,0:T(8,128)(2,1)S(1)}, u32[]{:S(2)}, u32[]{:S(2)}) collective-permute-start(bf16[96,1024]{1,0:T(8,128)(2,1)} %get-tuple-element.79), channel_id=1, source_target_pairs={{0,6},{1,7},{2,4},{3,5},{4,2},{5,3},{6,0},{7,1},{8,14},{9,15},{10,... | collective-permute-start | bytes 589832 | tf_op jit(solution)/shard_map/ppermute | solution.py:535
  50.4 0.1 slice.19
  50.5 0.7 reshape.42.late_far
  51.2 0.9 %all-to-all-done.1 = bf16[16,24,1024]{2,1,0:T(8,128)(2,1)S(1)} async-done(((bf16[16,24,1024]{2,1,0:T(8,128)(2,1)}), bf16[16,24,1024]{2,1,0:T(8,128)(2,1)S(1)}, u32[]{:S(2)}, u32[]{:S(2)}) %all-to-all-start.1) | async-done | bytes 786464 | tf_op jit(solution)/shard_map/all_to_all | solution.py:571
  52.0 0.9 %copy-done.1 = bf16[16,24,1024]{2,1,0:T(8,128)(2,1)} copy-done((bf16[16,24,1024]{2,1,0:T(8,128)(2,1)}, bf16[16,24,1024]{2,1,0:T(8,128)(2,1)S(1)}, u32[]{:S(2)}) %copy-start.1) | copy-done | bytes 786456
  52.9 5.0 %encode.1 = (bf16[2,1024]{1,0:T(2,128)(2,1)}, bf16[16,2,1024]{2,1,0:T(2,128)(2,1)}) custom-call(s32[1,2]{1,0:T(1,128)} %bitcast.27, s32[128,1]{1,0:T(8,128)} %get-tuple-element.41.refs_1_, bf16[384,1024]{1,0:T(8,128)(2,1)} %bitcast.15, bf16[64,1024]{1,0:T(8,128)(2,1)} %refs_3_.1, f32[1,1024]{1,0:T(1,128)} %bitcast.19, f32[1,1024]{1,0:T(1,128)} %bitcast.20, ...), custom_call_target="tpu_custom_call" | custom-call | flops 637534208 | bytes 6291456 | tf_op jit(solution)/shard_map/encode/pallas_call | solution.py:121
  57.9 5.5 %all-to-all-start.2 = ((bf16[16,2,1024]{2,1,0:T(2,128)(2,1)}), bf16[16,2,1024]{2,1,0:T(2,128)(2,1)S(1)}, u32[]{:S(2)}, u32[]{:S(2)}) async-start(bf16[16,2,1024]{2,1,0:T(2,128)(2,1)} %get-tuple-element.71), calls=%async_computation.2 | async-start | bytes 131072 | tf_op jit(solution)/shard_map/all_to_all | solution.py:606
  63.4 0.0 collective-permute-done.9.rest_1_
  63.4 0.0 copy-start.7
  63.4 0.0 collective-permute-done.10.rest_2_
  63.5 0.0 copy-start.8
  63.5 0.0 collective-permute-done.11.rest_3_
  63.5 0.0 copy-start.9
  63.5 6.8 %all-to-all-done.2.spread_far = bf16[16,2,1024]{2,1,0:T(2,128)(2,1)S(1)} async-done(((bf16[16,2,1024]{2,1,0:T(2,128)(2,1)}), bf16[16,2,1024]{2,1,0:T(2,128)(2,1)S(1)}, u32[]{:S(2)}, u32[]{:S(2)}) %all-to-all-start.2) | async-done | bytes 65568 | tf_op jit(solution)/shard_map/all_to_all | solution.py:606
  70.3 0.6 copy-done.6
  70.9 3.6 %late.1 = f32[512,1024]{1,0:T(8,128)} custom-call(s32[1,768]{1,0:T(1,128)} %reshape.41.places_far, s32[1,32]{1,0:T(1,128)} %reshape.42.late_far, bf16[16,2,1024]{2,1,0:T(2,128)(2,1)} %copy-done.6, f32[512,128]{1,0:T(8,128)} %get-tuple-element.72.share_far, f32[512,1024]{1,0:T(8,128)} %get-tuple-element.73.early_far, ...), custom_call_target="tpu_custom_call" | custom-call | flops 436207616 | bytes 4194304 | tf_op jit(solution)/shard_map/late/pallas_call | solution.py:474
  (15 shorter events, 0.0 us)
Async XLA Ops:
  0.6 26.4 %copy-start = (bf16[240,1024]{1,0:T(8,128)(2,1)S(1)}, bf16[240,1024]{1,0:T(8,128)(2,1)}, u32[]{:S(2)}) copy-start(bf16[240,1024]{1,0:T(8,128)(2,1)} %param.17) | copy-start | bytes 1474564
  0.6 8.6 %collective-permute-start.1 = (bf16[254,1024]{1,0:T(8,128)(2,1)}, bf16[254,1024]{1,0:T(8,128)(2,1)S(1)}, u32[]{:S(2)}, u32[]{:S(2)}) collective-permute-start(bf16[254,1024]{1,0:T(8,128)(2,1)} %refs_2_.1), channel_id=1, source_target_pairs={{0,1},{1,0},{2,3},{3,2},{4,5},{5,4},{6,7},{7,6},{8,9},{9,8},{10,11... | collective-permute-start | bytes 1560584 | tf_op jit(solution)/shard_map/ppermute | solution.py:539
  1.2 5.2 %collective-permute-start = (s32[1,256]{1,0:T(1,128)}, s32[1,256]{1,0:T(1,128)S(1)}, u32[]{:S(2)}, u32[]{:S(2)}) collective-permute-start(s32[1,256]{1,0:T(1,128)} %bitcast.24), channel_id=1, source_target_pairs={{0,1},{1,0},{2,3},{3,2},{4,5},{5,4},{6,7},{7,6},{8,9},{9,8},{10,11... | collective-permute-start | bytes 3080 | tf_op jit(solution)/shard_map/ppermute | solution.py:543
  2.3 26.0 %collective-permute-start.2 = (bf16[176,1024]{1,0:T(8,128)(2,1)S(1)}, bf16[176,1024]{1,0:T(8,128)(2,1)S(1)}, u32[]{:S(2)}, u32[]{:S(2)}) collective-permute-start(bf16[176,1024]{1,0:T(8,128)(2,1)S(1)} %slice.17), channel_id=1, source_target_pairs={{0,8},{1,9},{2,10},{3,11},{4,12},{5,13},{6,14},{7,15},{8,0},{9,1},... | collective-permute-start | bytes 1081352 | tf_op jit(solution)/shard_map/ppermute | solution.py:540
  6.3 0.6 copy-start.12
  9.2 4.0 %copy-start.2 = (bf16[254,1024]{1,0:T(8,128)(2,1)}, bf16[254,1024]{1,0:T(8,128)(2,1)S(1)}, u32[]{:S(2)}) copy-start(bf16[254,1024]{1,0:T(8,128)(2,1)S(1)} %collective-permute-done.1.refs_3_) | copy-start | bytes 1560580
  9.3 15.0 %all-to-all-start = ((s32[16,1,330]{2,1,0:T(1,128)}), s32[16,1,330]{2,1,0:T(1,128)S(1)}, u32[]{:S(2)}, u32[]{:S(2)}) async-start(s32[16,1,330]{2,1,0:T(1,128)} %get-tuple-element.43), calls=%async_computation | async-start | bytes 49152 | tf_op jit(solution)/shard_map/all_to_all | solution.py:548
  15.9 12.5 %collective-permute-start.3 = (bf16[96,1024]{1,0:T(8,128)(2,1)}, bf16[96,1024]{1,0:T(8,128)(2,1)S(1)}, u32[]{:S(2)}, u32[]{:S(2)}) collective-permute-start(bf16[96,1024]{1,0:T(8,128)(2,1)} %get-tuple-element.50), channel_id=1, source_target_pairs={{0,2},{1,3},{2,0},{3,1},{4,6},{5,7},{6,4},{7,5},{8,10},{9,11},{10,... | collective-permute-start | bytes 589832 | tf_op jit(solution)/shard_map/ppermute | solution.py:535
  17.8 15.4 %collective-permute-start.4 = (bf16[96,1024]{1,0:T(8,128)(2,1)}, bf16[96,1024]{1,0:T(8,128)(2,1)S(1)}, u32[]{:S(2)}, u32[]{:S(2)}) collective-permute-start(bf16[96,1024]{1,0:T(8,128)(2,1)} %get-tuple-element.55), channel_id=1, source_target_pairs={{0,4},{1,5},{2,6},{3,7},{4,0},{5,1},{6,2},{7,3},{8,12},{9,13},{10,... | collective-permute-start | bytes 589832 | tf_op jit(solution)/shard_map/ppermute | solution.py:535
  19.3 16.8 %collective-permute-start.5 = (bf16[96,1024]{1,0:T(8,128)(2,1)}, bf16[96,1024]{1,0:T(8,128)(2,1)S(1)}, u32[]{:S(2)}, u32[]{:S(2)}) collective-permute-start(bf16[96,1024]{1,0:T(8,128)(2,1)} %get-tuple-element.56), channel_id=1, source_target_pairs={{0,6},{1,7},{2,4},{3,5},{4,2},{5,3},{6,0},{7,1},{8,14},{9,15},{10,... | collective-permute-start | bytes 589832 | tf_op jit(solution)/shard_map/ppermute | solution.py:535
  24.2 16.4 %copy-start.5 = (s32[16,1,330]{2,1,0:T(1,128)}, s32[16,1,330]{2,1,0:T(1,128)S(1)}, u32[]{:S(2)}) copy-start(s32[16,1,330]{2,1,0:T(1,128)S(1)} %all-to-all-done.refs_0_.refs_1_) | copy-start | bytes 63364
  24.3 11.8 %collective-permute-start.6 = (bf16[78,1024]{1,0:T(8,128)(2,1)}, bf16[78,1024]{1,0:T(8,128)(2,1)S(1)}, u32[]{:S(2)}, u32[]{:S(2)}) collective-permute-start(bf16[78,1024]{1,0:T(8,128)(2,1)} %get-tuple-element.57), channel_id=1, source_target_pairs={{0,8},{1,9},{2,10},{3,11},{4,12},{5,13},{6,14},{7,15},{8,0},{9,1},... | collective-permute-start | bytes 479240 | tf_op jit(solution)/shard_map/ppermute | solution.py:560
  28.3 12.3 %copy-start.3 = (bf16[176,1024]{1,0:T(8,128)(2,1)}, bf16[176,1024]{1,0:T(8,128)(2,1)S(1)}, u32[]{:S(2)}) copy-start(bf16[176,1024]{1,0:T(8,128)(2,1)S(1)} %collective-permute-done.2.refs_2_) | copy-start | bytes 1081348
  28.3 7.8 %copy-start.13 = (bf16[96,1024]{1,0:T(8,128)(2,1)}, bf16[96,1024]{1,0:T(8,128)(2,1)S(1)}, u32[]{:S(2)}) copy-start(bf16[96,1024]{1,0:T(8,128)(2,1)S(1)} %collective-permute-done.3.rest_1_) | copy-start | bytes 589828
  29.6 22.4 %all-to-all-start.1 = ((bf16[16,24,1024]{2,1,0:T(8,128)(2,1)}), bf16[16,24,1024]{2,1,0:T(8,128)(2,1)S(1)}, u32[]{:S(2)}, u32[]{:S(2)}) async-start(bf16[16,24,1024]{2,1,0:T(8,128)(2,1)} %bitcast.4), calls=%async_computation.1 | async-start | bytes 1572864 | tf_op jit(solution)/shard_map/all_to_all | solution.py:571
  33.3 2.8 %copy-start.14 = (bf16[96,1024]{1,0:T(8,128)(2,1)}, bf16[96,1024]{1,0:T(8,128)(2,1)S(1)}, u32[]{:S(2)}) copy-start(bf16[96,1024]{1,0:T(8,128)(2,1)S(1)} %collective-permute-done.4.rest_2_) | copy-start | bytes 589828
  36.1 0.7 copy-start.15
  36.8 4.0 %copy-start.10 = (bf16[78,1024]{1,0:T(8,128)(2,1)}, bf16[78,1024]{1,0:T(8,128)(2,1)S(1)}, u32[]{:S(2)}) copy-start(bf16[78,1024]{1,0:T(8,128)(2,1)S(1)} %collective-permute-done.6.refs_3_) | copy-start | bytes 479236
  40.6 2.0 %collective-permute-start.7 = (bf16[176,1024]{1,0:T(8,128)(2,1)S(1)}, bf16[176,1024]{1,0:T(8,128)(2,1)S(1)}, u32[]{:S(2)}, u32[]{:S(2)}) collective-permute-start(bf16[176,1024]{1,0:T(8,128)(2,1)S(1)} %collective-permute-done.2.refs_2_), channel_id=1, source_target_pairs={{0,1},{1,0},{2,3},{3,2},{4,5},{5,4},{6,7},{7,6},{8,9},{9,8},{10,11... | collective-permute-start | bytes 1081352 | tf_op jit(solution)/shard_map/ppermute | solution.py:583
  40.8 1.8 %collective-permute-start.8 = (bf16[78,1024]{1,0:T(8,128)(2,1)S(1)}, bf16[78,1024]{1,0:T(8,128)(2,1)S(1)}, u32[]{:S(2)}, u32[]{:S(2)}) collective-permute-start(bf16[78,1024]{1,0:T(8,128)(2,1)S(1)} %collective-permute-done.6.refs_3_), channel_id=1, source_target_pairs={{0,1},{1,0},{2,3},{3,2},{4,5},{5,4},{6,7},{7,6},{8,9},{9,8},{10,11... | collective-permute-start | bytes 479240 | tf_op jit(solution)/shard_map/ppermute | solution.py:583
  42.6 0.7 copy-start.11
  43.3 0.8 %copy-start.4 = (bf16[176,1024]{1,0:T(8,128)(2,1)}, bf16[176,1024]{1,0:T(8,128)(2,1)S(1)}, u32[]{:S(2)}) copy-start(bf16[176,1024]{1,0:T(8,128)(2,1)S(1)} %collective-permute-done.7.refs_4_) | copy-start | bytes 1081348
  46.9 16.6 %collective-permute-start.9 = (bf16[96,1024]{1,0:T(8,128)(2,1)}, bf16[96,1024]{1,0:T(8,128)(2,1)S(1)}, u32[]{:S(2)}, u32[]{:S(2)}) collective-permute-start(bf16[96,1024]{1,0:T(8,128)(2,1)} %get-tuple-element.77), channel_id=1, source_target_pairs={{0,2},{1,3},{2,0},{3,1},{4,6},{5,7},{6,4},{7,5},{8,10},{9,11},{10,... | collective-permute-start | bytes 589832 | tf_op jit(solution)/shard_map/ppermute | solution.py:535
  46.9 16.5 %collective-permute-start.10 = (bf16[96,1024]{1,0:T(8,128)(2,1)}, bf16[96,1024]{1,0:T(8,128)(2,1)S(1)}, u32[]{:S(2)}, u32[]{:S(2)}) collective-permute-start(bf16[96,1024]{1,0:T(8,128)(2,1)} %get-tuple-element.78), channel_id=1, source_target_pairs={{0,4},{1,5},{2,6},{3,7},{4,0},{5,1},{6,2},{7,3},{8,12},{9,13},{10,... | collective-permute-start | bytes 589832 | tf_op jit(solution)/shard_map/ppermute | solution.py:535
  47.5 16.0 %collective-permute-start.11 = (bf16[96,1024]{1,0:T(8,128)(2,1)}, bf16[96,1024]{1,0:T(8,128)(2,1)S(1)}, u32[]{:S(2)}, u32[]{:S(2)}) collective-permute-start(bf16[96,1024]{1,0:T(8,128)(2,1)} %get-tuple-element.79), channel_id=1, source_target_pairs={{0,6},{1,7},{2,4},{3,5},{4,2},{5,3},{6,0},{7,1},{8,14},{9,15},{10,... | collective-permute-start | bytes 589832 | tf_op jit(solution)/shard_map/ppermute | solution.py:535
  52.0 0.9 %copy-start.1 = (bf16[16,24,1024]{2,1,0:T(8,128)(2,1)}, bf16[16,24,1024]{2,1,0:T(8,128)(2,1)S(1)}, u32[]{:S(2)}) copy-start(bf16[16,24,1024]{2,1,0:T(8,128)(2,1)S(1)} %all-to-all-done.1) | copy-start | bytes 2359300
  57.9 12.4 %all-to-all-start.2 = ((bf16[16,2,1024]{2,1,0:T(2,128)(2,1)}), bf16[16,2,1024]{2,1,0:T(2,128)(2,1)S(1)}, u32[]{:S(2)}, u32[]{:S(2)}) async-start(bf16[16,2,1024]{2,1,0:T(2,128)(2,1)} %get-tuple-element.71), calls=%async_computation.2 | async-start | bytes 131072 | tf_op jit(solution)/shard_map/all_to_all | solution.py:606
  63.4 6.9 %copy-start.7 = (bf16[96,1024]{1,0:T(8,128)(2,1)}, bf16[96,1024]{1,0:T(8,128)(2,1)S(1)}, u32[]{:S(2)}) copy-start(bf16[96,1024]{1,0:T(8,128)(2,1)S(1)} %collective-permute-done.9.rest_1_) | copy-start | bytes 589828
  63.5 6.9 %copy-start.8 = (bf16[96,1024]{1,0:T(8,128)(2,1)}, bf16[96,1024]{1,0:T(8,128)(2,1)S(1)}, u32[]{:S(2)}) copy-start(bf16[96,1024]{1,0:T(8,128)(2,1)S(1)} %collective-permute-done.10.rest_2_) | copy-start | bytes 589828
  63.5 6.9 %copy-start.9 = (bf16[96,1024]{1,0:T(8,128)(2,1)}, bf16[96,1024]{1,0:T(8,128)(2,1)S(1)}, u32[]{:S(2)}) copy-start(bf16[96,1024]{1,0:T(8,128)(2,1)S(1)} %collective-permute-done.11.rest_3_) | copy-start | bytes 589828
  70.3 0.6 copy-start.6

commit v27 on v23

--- a/solution.py
+++ b/solution.py
@@ -568,12 +568,13 @@
     found, first_rows, own_half[:2] = lax.optimization_barrier(
         (found, first_rows, own_half[:2])
     )
+    plan_behind, last_rows = lax.optimization_barrier((plan, last_rows))
     fetched = lax.all_to_all(
         found.reshape(peer_count, token_cap, width), "dp", split_axis=0, concat_axis=0, tiled=True
     ).reshape(peer_count * token_cap, width)
 
     sources = lax.axis_index("dp") ^ jnp.arange(peer_count, dtype=jnp.int32)
-    got_places = plan[:, token_cap : token_cap + row_cap][sources].reshape(half, 2 * row_cap)
+    got_places = plan_behind[:, token_cap : token_cap + row_cap][sources].reshape(half, 2 * row_cap)
     spare = padded(2 * row_cap) - 2 * row_cap
     got_places = jnp.pad(got_places, ((0, 0), (0, spare)), constant_values=-1).reshape(1, -1)
     near_rows, last_rows = lax.optimization_barrier((own_half, last_rows))
@@ -585,8 +586,8 @@
     blocks = pack_rows(codes, codes, partner_rows, far_rows, half, row_cap, row_count, picks)
     other_half = hand_on(blocks)
     late_places = plan[:, token_cap + row_cap :].reshape(1, -1)
-    fetched, means, share, got_places, late_places = lax.optimization_barrier(
-        (fetched, means, share, got_places, late_places)
+    fetched, means, share, got_places = lax.optimization_barrier(
+        (fetched, means, share, got_places)
     )
 
     passage_embed, spread = encode(

time: 76.5 us -> 74.8 us (0.978)
  waiting for transfers between devices: 17.4 us -> 15.7 us
  local copies, waits for them, and re-layouts: 6.66 us -> 7.99 us
  starting transfers between devices: 29.6 us -> 28.5 us
    unnamed x32, local copies, waits for them, and re-layouts: 3.51 us -> 4.85 us
    all_to_all x1, starting transfers between devices: 7.04 us -> 5.88 us  [shards(): lax.all_to_all(spread, 'dp', split_axis=0, concat_axis=0, tiled=True)]
    all_to_all x1, waiting for transfers between devices: 1.13 us -> 0.01 us  [shards(): lax.all_to_all(found.reshape(peer_count, token_cap, width), 'dp', split_a...]
    ppermute x1, waiting for transfers between devices: 2.44 us -> 3.29 us  [shards(): last_rows = lax.ppermute(last_rows, 'dp', across)]
    ppermute x6, waiting for transfers between devices: 0.79 us -> 0.02 us  [hand_on(): got.append(lax.ppermute(blocks[step], 'dp', moves))]
  transfers between devices with their start and end apart: 15 -> 15, of which waited for: 6 -> 4; matrix products, arithmetic and copies ran while one was open for 6% -> 6% of each run, Pallas kernels for 22% -> 22%
where the time goes in v27:
time: 74.8 us; the launch traced here: 74.4 us
  starting transfers between devices  28.5 us (38%)
  Pallas kernels  20.1 us (27%)
  waiting for transfers between devices  15.7 us (21%)
  local copies, waits for them, and re-layouts  7.99 us (11%)
  matrix products  1.29 us (2%)
  between operations  0.86 us (1%)
    ppermute x6, starting transfers between devices, hand_on(): got.append(lax.ppermute(blocks[step], 'dp', moves))  7.11 us
    all_to_all x1, waiting for transfers between devices, shards(): lax.all_to_all(spread, 'dp', split_axis=0, concat_axis=0, tiled=True)  6.12 us
    all_to_all x1, starting transfers between devices, shards(): lax.all_to_all(spread, 'dp', split_axis=0, concat_axis=0, tiled=True)  5.88 us
    pallas_call x2, Pallas kernels, pack_rows(): pl.pallas_call(functools.partial(pack_kernel, half, row_cap, count, picks...  5.48 us
    pallas_call x1, Pallas kernels, encode(): pl.pallas_call(encode_kernel, out_shape=[jax.ShapeDtypeStruct((passes, wi...  4.97 us
    unnamed x32, local copies, waits for them, and re-layouts  4.85 us
    all_to_all x1, waiting for transfers between devices, shards(): codes = lax.all_to_all(plan, 'dp', split_axis=0, concat_axis=0, tiled=True)  4.82 us
    ppermute x1, starting transfers between devices, shards(): first_rows = lax.ppermute(stored_rows[:ahead], 'dp', across)  4.08 us
  transfers between devices with their start and end apart: 15, of which 4 were waited for; matrix products, arithmetic and copies ran while one was open for 6% of the time, Pallas kernels for 22%

profile of v27, /device:TPU:0, one launch (start us, length us, event | category | flops | bytes accessed | tf_op | source)
XLA Modules:
  0.0 74.4 jit_solution(887098222137967473)
XLA Ops:
  0.6 0.0 copy-start
  0.6 0.5 collective-permute-start.1
  1.2 0.1 collective-permute-start
  1.2 1.0 %slice.17 = bf16[176,1024]{1,0:T(8,128)(2,1)S(1)} slice(bf16[254,1024]{1,0:T(8,128)(2,1)} %refs_2_.1), slice={[0:176], [0:1024]} | slice | bytes 720896 | tf_op jit(solution)/shard_map/slice | solution.py:540
  2.3 4.1 %collective-permute-start.2 = (bf16[176,1024]{1,0:T(8,128)(2,1)S(1)}, bf16[176,1024]{1,0:T(8,128)(2,1)S(1)}, u32[]{:S(2)}, u32[]{:S(2)}) collective-permute-start(bf16[176,1024]{1,0:T(8,128)(2,1)S(1)} %slice.17), channel_id=1, source_target_pairs={{0,8},{1,9},{2,10},{3,11},{4,12},{5,13},{6,14},{7,15},{8,0},{9,1},... | collective-permute-start | bytes 1081352 | tf_op jit(solution)/shard_map/ppermute | solution.py:540
  6.3 0.0 collective-permute-done.sibling_far
  6.3 0.6 copy-done.12
  6.9 2.3 %route.1 = (s32[16,1,330]{2,1,0:T(1,128)}, s32[128,1]{1,0:T(8,128)}, s32[1,256]{1,0:T(1,128)}, s32[1,256]{1,0:T(1,128)}) custom-call(s32[2,64]{1,0:T(2,128)} %token_ids_far.1, s32[1,256]{1,0:T(1,128)} %bitcast.25, s32[1,256]{1,0:T(1,128)} %bitcast.26, s32[1,256]{1,0:T(1,128)} %copy-done.12), custom_call_target="tpu_custom_call" | custom-call | tf_op jit(solution)/shard_map/route/pallas_call | solution.py:228
  9.2 0.0 collective-permute-done.1.refs_3_
  9.2 0.0 copy-start.2
  9.3 3.9 %all-to-all-start = ((s32[16,1,330]{2,1,0:T(1,128)}), s32[16,1,330]{2,1,0:T(1,128)S(1)}, u32[]{:S(2)}, u32[]{:S(2)}) async-start(s32[16,1,330]{2,1,0:T(1,128)} %get-tuple-element.43), calls=%async_computation | async-start | bytes 49152 | tf_op jit(solution)/shard_map/all_to_all | solution.py:548
  13.2 0.0 copy-done.2
  13.2 2.6 %pack.2 = (bf16[96,1024]{1,0:T(8,128)(2,1)}, bf16[96,1024]{1,0:T(8,128)(2,1)}, bf16[96,1024]{1,0:T(8,128)(2,1)}, bf16[96,1024]{1,0:T(8,128)(2,1)}, bf16[78,1024]{1,0:T(8,128)(2,1)}) custom-call(s32[1,256]{1,0:T(1,128)} %get-tuple-element.44.refs_0_, s32[1,256]{1,0:T(1,128)} %get-tuple-element.45.refs_1_, bf16[254,1024]{1,0:T(8,128)(2,1)} %refs_2_.1, ...), custom_call_target="tpu_custom_call" | custom-call | flops 199753728 | bytes 1826816 | tf_op jit(solution)/shard_map/pack/pallas_call | solution.py:319
  15.9 2.0 %collective-permute-start.3 = (bf16[96,1024]{1,0:T(8,128)(2,1)}, bf16[96,1024]{1,0:T(8,128)(2,1)S(1)}, u32[]{:S(2)}, u32[]{:S(2)}) collective-permute-start(bf16[96,1024]{1,0:T(8,128)(2,1)} %get-tuple-element.50), channel_id=1, source_target_pairs={{0,2},{1,3},{2,0},{3,1},{4,6},{5,7},{6,4},{7,5},{8,10},{9,11},{10,... | collective-permute-start | bytes 589832 | tf_op jit(solution)/shard_map/ppermute | solution.py:535
  17.8 1.5 %collective-permute-start.4 = (bf16[96,1024]{1,0:T(8,128)(2,1)}, bf16[96,1024]{1,0:T(8,128)(2,1)S(1)}, u32[]{:S(2)}, u32[]{:S(2)}) collective-permute-start(bf16[96,1024]{1,0:T(8,128)(2,1)} %get-tuple-element.55), channel_id=1, source_target_pairs={{0,4},{1,5},{2,6},{3,7},{4,0},{5,1},{6,2},{7,3},{8,12},{9,13},{10,... | collective-permute-start | bytes 589832 | tf_op jit(solution)/shard_map/ppermute | solution.py:535
  19.3 0.1 collective-permute-start.5
  19.4 4.8 %all-to-all-done.refs_0_.refs_1_ = s32[16,1,330]{2,1,0:T(1,128)S(1)} async-done(((s32[16,1,330]{2,1,0:T(1,128)}), s32[16,1,330]{2,1,0:T(1,128)S(1)}, u32[]{:S(2)}, u32[]{:S(2)}) %all-to-all-start) | async-done | bytes 21152 | tf_op jit(solution)/shard_map/all_to_all | solution.py:548
  24.2 0.1 eq.15
  24.3 2.7 %collective-permute-start.6 = (bf16[78,1024]{1,0:T(8,128)(2,1)}, bf16[78,1024]{1,0:T(8,128)(2,1)S(1)}, u32[]{:S(2)}, u32[]{:S(2)}) collective-permute-start(bf16[78,1024]{1,0:T(8,128)(2,1)} %get-tuple-element.57), channel_id=1, source_target_pairs={{0,8},{1,9},{2,10},{3,11},{4,12},{5,13},{6,14},{7,15},{8,0},{9,1},... | collective-permute-start | bytes 479240 | tf_op jit(solution)/shard_map/ppermute | solution.py:560
  27.0 0.0 copy-done
  27.0 1.3 %convolution_convert_fusion = bf16[384,1024]{1,0:T(8,128)(2,1)} fusion(bf16[240,1024]{1,0:T(8,128)(2,1)S(1)} %copy-done, s32[384]{0:T(512)S(1)} %eq.15), kind=kOutput, calls=%fused_computation.1 | convolution fusion | flops 189229056 | bytes 1279488 | tf_op jit(solution)/shard_map/dot_general | solution.py:565
  28.3 0.0 collective-permute-done.2.refs_2_
  28.3 0.0 collective-permute-done.3.rest_1_
  28.3 0.0 copy-start.13
  28.3 3.6 %all-to-all-start.1 = ((bf16[16,24,1024]{2,1,0:T(8,128)(2,1)}), bf16[16,24,1024]{2,1,0:T(8,128)(2,1)S(1)}, u32[]{:S(2)}, u32[]{:S(2)}) async-start(bf16[16,24,1024]{2,1,0:T(8,128)(2,1)} %bitcast.4), calls=%async_computation.1 | async-start | bytes 1572864 | tf_op jit(solution)/shard_map/all_to_all | solution.py:572
  32.0 3.3 %collective-permute-done.6.refs_3_ = bf16[78,1024]{1,0:T(8,128)(2,1)S(1)} collective-permute-done((bf16[78,1024]{1,0:T(8,128)(2,1)}, bf16[78,1024]{1,0:T(8,128)(2,1)S(1)}, u32[]{:S(2)}, u32[]{:S(2)}) %collective-permute-start.6) | collective-permute-done | bytes 159776 | tf_op jit(solution)/shard_map/ppermute | solution.py:560
  35.3 0.1 slice.18
  35.3 0.6 gather_fusion
  35.9 0.7 reshape.41.places_far
  36.6 0.0 collective-permute-done.4.rest_2_
  36.6 0.0 collective-permute-done.5.rest_3_
  36.6 0.0 copy-done.13
  36.6 0.7 copy-done.14
  37.3 0.7 copy-done.15
  37.9 3.8 %early.1 = (f32[512,1024]{1,0:T(8,128)}, f32[512,128]{1,0:T(8,128)}) custom-call(s32[1,768]{1,0:T(1,128)} %reshape.41.places_far, f32[512,1024]{1,0:T(8,128)} %centroids_far.1, bf16[96,1024]{1,0:T(8,128)(2,1)} %get-tuple-element.61.rest_0_, bf16[96,1024]{1,0:T(8,128)(2,1)} %copy-done.13, bf16[96,1024]{1,0:T(8,128)(2,1)} %copy-done.14, ...), custom_call_target="tpu_custom_call" | custom-call | flops 20132659200 | bytes 104857600 | tf_op jit(solution)/shard_map/early/pallas_call | solution.py:442
  41.7 0.0 copy-done.5
  41.7 0.0 copy-done.3
  41.7 0.1 collective-permute-start.7
  41.8 0.0 copy-done.10
  41.8 0.5 collective-permute-start.8
  42.3 1.4 %collective-permute-done.8.refs_5_ = bf16[78,1024]{1,0:T(8,128)(2,1)S(1)} collective-permute-done((bf16[78,1024]{1,0:T(8,128)(2,1)S(1)}, bf16[78,1024]{1,0:T(8,128)(2,1)S(1)}, u32[]{:S(2)}, u32[]{:S(2)}) %collective-permute-start.8) | collective-permute-done | bytes 159776 | tf_op jit(solution)/shard_map/ppermute | solution.py:584
  43.7 0.0 collective-permute-done.7.refs_4_
  43.7 0.7 copy-done.11
  44.4 0.8 %copy-done.4 = bf16[176,1024]{1,0:T(8,128)(2,1)} copy-done((bf16[176,1024]{1,0:T(8,128)(2,1)}, bf16[176,1024]{1,0:T(8,128)(2,1)S(1)}, u32[]{:S(2)}) %copy-start.4) | copy-done | bytes 360472
  45.1 2.8 %pack.3 = (bf16[96,1024]{1,0:T(8,128)(2,1)}, bf16[96,1024]{1,0:T(8,128)(2,1)}, bf16[96,1024]{1,0:T(8,128)(2,1)}, bf16[96,1024]{1,0:T(8,128)(2,1)}) custom-call(s32[16,1,330]{2,1,0:T(1,128)} %copy-done.5, s32[16,1,330]{2,1,0:T(1,128)} %copy-done.5, bf16[176,1024]{1,0:T(8,128)(2,1)} %copy-done.3, bf16[78,1024]{1,0:T(8,128)(2,1)} %copy-done.10, ...), custom_call_target="tpu_custom_call" | custom-call | flops 199753728 | bytes 1826816 | tf_op jit(solution)/shard_map/pack/pallas_call | solution.py:319
  48.0 0.7 collective-permute-start.9
  48.7 0.9 %collective-permute-start.10 = (bf16[96,1024]{1,0:T(8,128)(2,1)}, bf16[96,1024]{1,0:T(8,128)(2,1)S(1)}, u32[]{:S(2)}, u32[]{:S(2)}) collective-permute-start(bf16[96,1024]{1,0:T(8,128)(2,1)} %get-tuple-element.78), channel_id=1, source_target_pairs={{0,4},{1,5},{2,6},{3,7},{4,0},{5,1},{6,2},{7,3},{8,12},{9,13},{10,... | collective-permute-start | bytes 589832 | tf_op jit(solution)/shard_map/ppermute | solution.py:535
  49.6 1.9 %collective-permute-start.11 = (bf16[96,1024]{1,0:T(8,128)(2,1)}, bf16[96,1024]{1,0:T(8,128)(2,1)S(1)}, u32[]{:S(2)}, u32[]{:S(2)}) collective-permute-start(bf16[96,1024]{1,0:T(8,128)(2,1)} %get-tuple-element.79), channel_id=1, source_target_pairs={{0,6},{1,7},{2,4},{3,5},{4,2},{5,3},{6,0},{7,1},{8,14},{9,15},{10,... | collective-permute-start | bytes 589832 | tf_op jit(solution)/shard_map/ppermute | solution.py:535
  51.5 0.0 all-to-all-done.1
  51.6 0.9 %copy-done.1 = bf16[16,24,1024]{2,1,0:T(8,128)(2,1)} copy-done((bf16[16,24,1024]{2,1,0:T(8,128)(2,1)}, bf16[16,24,1024]{2,1,0:T(8,128)(2,1)S(1)}, u32[]{:S(2)}) %copy-start.1) | copy-done | bytes 786456
  52.4 5.0 %encode.1 = (bf16[2,1024]{1,0:T(2,128)(2,1)}, bf16[16,2,1024]{2,1,0:T(2,128)(2,1)}) custom-call(s32[1,2]{1,0:T(1,128)} %bitcast.27, s32[128,1]{1,0:T(8,128)} %get-tuple-element.41.refs_1_, bf16[384,1024]{1,0:T(8,128)(2,1)} %bitcast.15, bf16[64,1024]{1,0:T(8,128)(2,1)} %refs_3_.1, f32[1,1024]{1,0:T(1,128)} %bitcast.19, f32[1,1024]{1,0:T(1,128)} %bitcast.20, ...), custom_call_target="tpu_custom_call" | custom-call | flops 637534208 | bytes 6291456 | tf_op jit(solution)/shard_map/encode/pallas_call | solution.py:121
  57.4 5.9 %all-to-all-start.2 = ((bf16[16,2,1024]{2,1,0:T(2,128)(2,1)}), bf16[16,2,1024]{2,1,0:T(2,128)(2,1)S(1)}, u32[]{:S(2)}, u32[]{:S(2)}) async-start(bf16[16,2,1024]{2,1,0:T(2,128)(2,1)} %get-tuple-element.71), calls=%async_computation.2 | async-start | bytes 131072 | tf_op jit(solution)/shard_map/all_to_all | solution.py:607
  63.3 0.1 slice.23
  63.4 0.7 reshape.42.late_far
  64.0 0.0 collective-permute-done.9.rest_1_
  64.0 0.0 collective-permute-done.10.rest_2_
  64.0 0.0 copy-start.8
  64.1 0.0 collective-permute-done.11.rest_3_
  64.1 0.0 copy-start.9
  64.1 6.1 %all-to-all-done.2.spread_far = bf16[16,2,1024]{2,1,0:T(2,128)(2,1)S(1)} async-done(((bf16[16,2,1024]{2,1,0:T(2,128)(2,1)}), bf16[16,2,1024]{2,1,0:T(2,128)(2,1)S(1)}, u32[]{:S(2)}, u32[]{:S(2)}) %all-to-all-start.2) | async-done | bytes 65568 | tf_op jit(solution)/shard_map/all_to_all | solution.py:607
  70.2 0.0 copy-done.7
  70.2 0.0 copy-done.8
  70.2 0.6 copy-done.6
  70.8 3.6 %late.1 = f32[512,1024]{1,0:T(8,128)} custom-call(s32[1,768]{1,0:T(1,128)} %reshape.41.places_far, s32[1,32]{1,0:T(1,128)} %reshape.42.late_far, bf16[16,2,1024]{2,1,0:T(2,128)(2,1)} %copy-done.6, f32[512,128]{1,0:T(8,128)} %get-tuple-element.72.share_far, f32[512,1024]{1,0:T(8,128)} %get-tuple-element.73.early_far, ...), custom_call_target="tpu_custom_call" | custom-call | flops 436207616 | bytes 4194304 | tf_op jit(solution)/shard_map/late/pallas_call | solution.py:474
  (15 shorter events, 0.0 us)
Async XLA Ops:
  0.6 26.4 %copy-start = (bf16[240,1024]{1,0:T(8,128)(2,1)S(1)}, bf16[240,1024]{1,0:T(8,128)(2,1)}, u32[]{:S(2)}) copy-start(bf16[240,1024]{1,0:T(8,128)(2,1)} %param.17) | copy-start | bytes 1474564
  0.6 8.6 %collective-permute-start.1 = (bf16[254,1024]{1,0:T(8,128)(2,1)}, bf16[254,1024]{1,0:T(8,128)(2,1)S(1)}, u32[]{:S(2)}, u32[]{:S(2)}) collective-permute-start(bf16[254,1024]{1,0:T(8,128)(2,1)} %refs_2_.1), channel_id=1, source_target_pairs={{0,1},{1,0},{2,3},{3,2},{4,5},{5,4},{6,7},{7,6},{8,9},{9,8},{10,11... | collective-permute-start | bytes 1560584 | tf_op jit(solution)/shard_map/ppermute | solution.py:539
  1.2 5.2 %collective-permute-start = (s32[1,256]{1,0:T(1,128)}, s32[1,256]{1,0:T(1,128)S(1)}, u32[]{:S(2)}, u32[]{:S(2)}) collective-permute-start(s32[1,256]{1,0:T(1,128)} %bitcast.24), channel_id=1, source_target_pairs={{0,1},{1,0},{2,3},{3,2},{4,5},{5,4},{6,7},{7,6},{8,9},{9,8},{10,11... | collective-permute-start | bytes 3080 | tf_op jit(solution)/shard_map/ppermute | solution.py:543
  2.3 26.0 %collective-permute-start.2 = (bf16[176,1024]{1,0:T(8,128)(2,1)S(1)}, bf16[176,1024]{1,0:T(8,128)(2,1)S(1)}, u32[]{:S(2)}, u32[]{:S(2)}) collective-permute-start(bf16[176,1024]{1,0:T(8,128)(2,1)S(1)} %slice.17), channel_id=1, source_target_pairs={{0,8},{1,9},{2,10},{3,11},{4,12},{5,13},{6,14},{7,15},{8,0},{9,1},... | collective-permute-start | bytes 1081352 | tf_op jit(solution)/shard_map/ppermute | solution.py:540
  6.3 0.6 copy-start.12
  9.2 4.0 %copy-start.2 = (bf16[254,1024]{1,0:T(8,128)(2,1)}, bf16[254,1024]{1,0:T(8,128)(2,1)S(1)}, u32[]{:S(2)}) copy-start(bf16[254,1024]{1,0:T(8,128)(2,1)S(1)} %collective-permute-done.1.refs_3_) | copy-start | bytes 1560580
  9.3 15.0 %all-to-all-start = ((s32[16,1,330]{2,1,0:T(1,128)}), s32[16,1,330]{2,1,0:T(1,128)S(1)}, u32[]{:S(2)}, u32[]{:S(2)}) async-start(s32[16,1,330]{2,1,0:T(1,128)} %get-tuple-element.43), calls=%async_computation | async-start | bytes 49152 | tf_op jit(solution)/shard_map/all_to_all | solution.py:548
  15.9 12.5 %collective-permute-start.3 = (bf16[96,1024]{1,0:T(8,128)(2,1)}, bf16[96,1024]{1,0:T(8,128)(2,1)S(1)}, u32[]{:S(2)}, u32[]{:S(2)}) collective-permute-start(bf16[96,1024]{1,0:T(8,128)(2,1)} %get-tuple-element.50), channel_id=1, source_target_pairs={{0,2},{1,3},{2,0},{3,1},{4,6},{5,7},{6,4},{7,5},{8,10},{9,11},{10,... | collective-permute-start | bytes 589832 | tf_op jit(solution)/shard_map/ppermute | solution.py:535
  17.8 18.7 %collective-permute-start.4 = (bf16[96,1024]{1,0:T(8,128)(2,1)}, bf16[96,1024]{1,0:T(8,128)(2,1)S(1)}, u32[]{:S(2)}, u32[]{:S(2)}) collective-permute-start(bf16[96,1024]{1,0:T(8,128)(2,1)} %get-tuple-element.55), channel_id=1, source_target_pairs={{0,4},{1,5},{2,6},{3,7},{4,0},{5,1},{6,2},{7,3},{8,12},{9,13},{10,... | collective-permute-start | bytes 589832 | tf_op jit(solution)/shard_map/ppermute | solution.py:535
  19.3 17.3 %collective-permute-start.5 = (bf16[96,1024]{1,0:T(8,128)(2,1)}, bf16[96,1024]{1,0:T(8,128)(2,1)S(1)}, u32[]{:S(2)}, u32[]{:S(2)}) collective-permute-start(bf16[96,1024]{1,0:T(8,128)(2,1)} %get-tuple-element.56), channel_id=1, source_target_pairs={{0,6},{1,7},{2,4},{3,5},{4,2},{5,3},{6,0},{7,1},{8,14},{9,15},{10,... | collective-permute-start | bytes 589832 | tf_op jit(solution)/shard_map/ppermute | solution.py:535
  24.2 17.5 %copy-start.5 = (s32[16,1,330]{2,1,0:T(1,128)}, s32[16,1,330]{2,1,0:T(1,128)S(1)}, u32[]{:S(2)}) copy-start(s32[16,1,330]{2,1,0:T(1,128)S(1)} %all-to-all-done.refs_0_.refs_1_) | copy-start | bytes 63364
  24.3 10.9 %collective-permute-start.6 = (bf16[78,1024]{1,0:T(8,128)(2,1)}, bf16[78,1024]{1,0:T(8,128)(2,1)S(1)}, u32[]{:S(2)}, u32[]{:S(2)}) collective-permute-start(bf16[78,1024]{1,0:T(8,128)(2,1)} %get-tuple-element.57), channel_id=1, source_target_pairs={{0,8},{1,9},{2,10},{3,11},{4,12},{5,13},{6,14},{7,15},{8,0},{9,1},... | collective-permute-start | bytes 479240 | tf_op jit(solution)/shard_map/ppermute | solution.py:560
  28.3 13.4 %copy-start.3 = (bf16[176,1024]{1,0:T(8,128)(2,1)}, bf16[176,1024]{1,0:T(8,128)(2,1)S(1)}, u32[]{:S(2)}) copy-start(bf16[176,1024]{1,0:T(8,128)(2,1)S(1)} %collective-permute-done.2.refs_2_) | copy-start | bytes 1081348
  28.3 8.3 %copy-start.13 = (bf16[96,1024]{1,0:T(8,128)(2,1)}, bf16[96,1024]{1,0:T(8,128)(2,1)S(1)}, u32[]{:S(2)}) copy-start(bf16[96,1024]{1,0:T(8,128)(2,1)S(1)} %collective-permute-done.3.rest_1_) | copy-start | bytes 589828
  28.3 23.2 %all-to-all-start.1 = ((bf16[16,24,1024]{2,1,0:T(8,128)(2,1)}), bf16[16,24,1024]{2,1,0:T(8,128)(2,1)S(1)}, u32[]{:S(2)}, u32[]{:S(2)}) async-start(bf16[16,24,1024]{2,1,0:T(8,128)(2,1)} %bitcast.4), calls=%async_computation.1 | async-start | bytes 1572864 | tf_op jit(solution)/shard_map/all_to_all | solution.py:572
  35.2 6.6 %copy-start.10 = (bf16[78,1024]{1,0:T(8,128)(2,1)}, bf16[78,1024]{1,0:T(8,128)(2,1)S(1)}, u32[]{:S(2)}) copy-start(bf16[78,1024]{1,0:T(8,128)(2,1)S(1)} %collective-permute-done.6.refs_3_) | copy-start | bytes 479236
  36.6 0.7 copy-start.14
  37.3 0.7 copy-start.15
  41.7 2.0 %collective-permute-start.7 = (bf16[176,1024]{1,0:T(8,128)(2,1)S(1)}, bf16[176,1024]{1,0:T(8,128)(2,1)S(1)}, u32[]{:S(2)}, u32[]{:S(2)}) collective-permute-start(bf16[176,1024]{1,0:T(8,128)(2,1)S(1)} %collective-permute-done.2.refs_2_), channel_id=1, source_target_pairs={{0,1},{1,0},{2,3},{3,2},{4,5},{5,4},{6,7},{7,6},{8,9},{9,8},{10,11... | collective-permute-start | bytes 1081352 | tf_op jit(solution)/shard_map/ppermute | solution.py:584
  41.8 1.9 %collective-permute-start.8 = (bf16[78,1024]{1,0:T(8,128)(2,1)S(1)}, bf16[78,1024]{1,0:T(8,128)(2,1)S(1)}, u32[]{:S(2)}, u32[]{:S(2)}) collective-permute-start(bf16[78,1024]{1,0:T(8,128)(2,1)S(1)} %collective-permute-done.6.refs_3_), channel_id=1, source_target_pairs={{0,1},{1,0},{2,3},{3,2},{4,5},{5,4},{6,7},{7,6},{8,9},{9,8},{10,11... | collective-permute-start | bytes 479240 | tf_op jit(solution)/shard_map/ppermute | solution.py:584
  43.7 0.7 copy-start.11
  44.4 0.8 %copy-start.4 = (bf16[176,1024]{1,0:T(8,128)(2,1)}, bf16[176,1024]{1,0:T(8,128)(2,1)S(1)}, u32[]{:S(2)}) copy-start(bf16[176,1024]{1,0:T(8,128)(2,1)S(1)} %collective-permute-done.7.refs_4_) | copy-start | bytes 1081348
  48.0 16.0 %collective-permute-start.9 = (bf16[96,1024]{1,0:T(8,128)(2,1)}, bf16[96,1024]{1,0:T(8,128)(2,1)S(1)}, u32[]{:S(2)}, u32[]{:S(2)}) collective-permute-start(bf16[96,1024]{1,0:T(8,128)(2,1)} %get-tuple-element.77), channel_id=1, source_target_pairs={{0,2},{1,3},{2,0},{3,1},{4,6},{5,7},{6,4},{7,5},{8,10},{9,11},{10,... | collective-permute-start | bytes 589832 | tf_op jit(solution)/shard_map/ppermute | solution.py:535
  48.7 15.3 %collective-permute-start.10 = (bf16[96,1024]{1,0:T(8,128)(2,1)}, bf16[96,1024]{1,0:T(8,128)(2,1)S(1)}, u32[]{:S(2)}, u32[]{:S(2)}) collective-permute-start(bf16[96,1024]{1,0:T(8,128)(2,1)} %get-tuple-element.78), channel_id=1, source_target_pairs={{0,4},{1,5},{2,6},{3,7},{4,0},{5,1},{6,2},{7,3},{8,12},{9,13},{10,... | collective-permute-start | bytes 589832 | tf_op jit(solution)/shard_map/ppermute | solution.py:535
  49.6 14.4 %collective-permute-start.11 = (bf16[96,1024]{1,0:T(8,128)(2,1)}, bf16[96,1024]{1,0:T(8,128)(2,1)S(1)}, u32[]{:S(2)}, u32[]{:S(2)}) collective-permute-start(bf16[96,1024]{1,0:T(8,128)(2,1)} %get-tuple-element.79), channel_id=1, source_target_pairs={{0,6},{1,7},{2,4},{3,5},{4,2},{5,3},{6,0},{7,1},{8,14},{9,15},{10,... | collective-permute-start | bytes 589832 | tf_op jit(solution)/shard_map/ppermute | solution.py:535
  51.6 0.9 %copy-start.1 = (bf16[16,24,1024]{2,1,0:T(8,128)(2,1)}, bf16[16,24,1024]{2,1,0:T(8,128)(2,1)S(1)}, u32[]{:S(2)}) copy-start(bf16[16,24,1024]{2,1,0:T(8,128)(2,1)S(1)} %all-to-all-done.1) | copy-start | bytes 2359300
  57.4 12.8 %all-to-all-start.2 = ((bf16[16,2,1024]{2,1,0:T(2,128)(2,1)}), bf16[16,2,1024]{2,1,0:T(2,128)(2,1)S(1)}, u32[]{:S(2)}, u32[]{:S(2)}) async-start(bf16[16,2,1024]{2,1,0:T(2,128)(2,1)} %get-tuple-element.71), calls=%async_computation.2 | async-start | bytes 131072 | tf_op jit(solution)/shard_map/all_to_all | solution.py:607
  64.0 6.2 %copy-start.7 = (bf16[96,1024]{1,0:T(8,128)(2,1)}, bf16[96,1024]{1,0:T(8,128)(2,1)S(1)}, u32[]{:S(2)}) copy-start(bf16[96,1024]{1,0:T(8,128)(2,1)S(1)} %collective-permute-done.9.rest_1_) | copy-start | bytes 589828
  64.0 6.2 %copy-start.8 = (bf16[96,1024]{1,0:T(8,128)(2,1)}, bf16[96,1024]{1,0:T(8,128)(2,1)S(1)}, u32[]{:S(2)}) copy-start(bf16[96,1024]{1,0:T(8,128)(2,1)S(1)} %collective-permute-done.10.rest_2_) | copy-start | bytes 589828
  64.1 6.1 %copy-start.9 = (bf16[96,1024]{1,0:T(8,128)(2,1)}, bf16[96,1024]{1,0:T(8,128)(2,1)S(1)}, u32[]{:S(2)}) copy-start(bf16[96,1024]{1,0:T(8,128)(2,1)S(1)} %collective-permute-done.11.rest_3_) | copy-start | bytes 589828
  70.2 0.6 copy-start.6

commit v28 on v27

--- a/solution.py
+++ b/solution.py
@@ -343,7 +343,7 @@
     return jnp.where(centre == where_to, 1.0, 0.0)
 
 
-BLOCK = 128
+BLOCK = 256
 
 
 def early_kernel(places_far, centroids_far, *rest):

time: 74.8 us -> 74.8 us (level)
  no operation moved by 1% of the time
where the time goes in v28:
time: 74.8 us; the launch traced here: 74.3 us
  starting transfers between devices  28.4 us (38%)
  Pallas kernels  20.1 us (27%)
  waiting for transfers between devices  15.7 us (21%)
  local copies, waits for them, and re-layouts  7.99 us (11%)
  matrix products  1.29 us (2%)
  between operations  0.86 us (1%)
    ppermute x6, starting transfers between devices, hand_on(): got.append(lax.ppermute(blocks[step], 'dp', moves))  7.11 us
    all_to_all x1, waiting for transfers between devices, shards(): lax.all_to_all(spread, 'dp', split_axis=0, concat_axis=0, tiled=True)  6.12 us
    all_to_all x1, starting transfers between devices, shards(): lax.all_to_all(spread, 'dp', split_axis=0, concat_axis=0, tiled=True)  5.84 us
    pallas_call x2, Pallas kernels, pack_rows(): pl.pallas_call(functools.partial(pack_kernel, half, row_cap, count, picks...  5.48 us
    pallas_call x1, Pallas kernels, encode(): pl.pallas_call(encode_kernel, out_shape=[jax.ShapeDtypeStruct((passes, wi...  4.97 us
    unnamed x32, local copies, waits for them, and re-layouts  4.85 us
    all_to_all x1, waiting for transfers between devices, shards(): codes = lax.all_to_all(plan, 'dp', split_axis=0, concat_axis=0, tiled=True)  4.82 us
    ppermute x1, starting transfers between devices, shards(): first_rows = lax.ppermute(stored_rows[:ahead], 'dp', across)  4.08 us
  transfers between devices with their start and end apart: 15, of which 4 were waited for; matrix products, arithmetic and copies ran while one was open for 6% of the time, Pallas kernels for 22%

profile of v28, /device:TPU:0, one launch (start us, length us, event | category | flops | bytes accessed | tf_op | source)
XLA Modules:
  0.0 74.3 jit_solution(7456462900646021776)
XLA Ops:
  0.6 0.0 copy-start
  0.6 0.5 collective-permute-start.1
  1.2 0.1 collective-permute-start
  1.2 1.0 %slice.17 = bf16[176,1024]{1,0:T(8,128)(2,1)S(1)} slice(bf16[254,1024]{1,0:T(8,128)(2,1)} %refs_2_.1), slice={[0:176], [0:1024]} | slice | bytes 720896 | tf_op jit(solution)/shard_map/slice | solution.py:540
  2.3 4.1 %collective-permute-start.2 = (bf16[176,1024]{1,0:T(8,128)(2,1)S(1)}, bf16[176,1024]{1,0:T(8,128)(2,1)S(1)}, u32[]{:S(2)}, u32[]{:S(2)}) collective-permute-start(bf16[176,1024]{1,0:T(8,128)(2,1)S(1)} %slice.17), channel_id=1, source_target_pairs={{0,8},{1,9},{2,10},{3,11},{4,12},{5,13},{6,14},{7,15},{8,0},{9,1},... | collective-permute-start | bytes 1081352 | tf_op jit(solution)/shard_map/ppermute | solution.py:540
  6.3 0.0 collective-permute-done.sibling_far
  6.3 0.6 copy-done.12
  6.9 2.3 %route.1 = (s32[16,1,330]{2,1,0:T(1,128)}, s32[128,1]{1,0:T(8,128)}, s32[1,256]{1,0:T(1,128)}, s32[1,256]{1,0:T(1,128)}) custom-call(s32[2,64]{1,0:T(2,128)} %token_ids_far.1, s32[1,256]{1,0:T(1,128)} %bitcast.25, s32[1,256]{1,0:T(1,128)} %bitcast.26, s32[1,256]{1,0:T(1,128)} %copy-done.12), custom_call_target="tpu_custom_call" | custom-call | tf_op jit(solution)/shard_map/route/pallas_call | solution.py:228
  9.2 0.0 collective-permute-done.1.refs_3_
  9.2 0.0 copy-start.2
  9.3 3.9 %all-to-all-start = ((s32[16,1,330]{2,1,0:T(1,128)}), s32[16,1,330]{2,1,0:T(1,128)S(1)}, u32[]{:S(2)}, u32[]{:S(2)}) async-start(s32[16,1,330]{2,1,0:T(1,128)} %get-tuple-element.43), calls=%async_computation | async-start | bytes 49152 | tf_op jit(solution)/shard_map/all_to_all | solution.py:548
  13.2 0.0 copy-done.2
  13.2 2.6 %pack.2 = (bf16[96,1024]{1,0:T(8,128)(2,1)}, bf16[96,1024]{1,0:T(8,128)(2,1)}, bf16[96,1024]{1,0:T(8,128)(2,1)}, bf16[96,1024]{1,0:T(8,128)(2,1)}, bf16[78,1024]{1,0:T(8,128)(2,1)}) custom-call(s32[1,256]{1,0:T(1,128)} %get-tuple-element.44.refs_0_, s32[1,256]{1,0:T(1,128)} %get-tuple-element.45.refs_1_, bf16[254,1024]{1,0:T(8,128)(2,1)} %refs_2_.1, ...), custom_call_target="tpu_custom_call" | custom-call | flops 199753728 | bytes 1826816 | tf_op jit(solution)/shard_map/pack/pallas_call | solution.py:319
  15.9 2.0 %collective-permute-start.3 = (bf16[96,1024]{1,0:T(8,128)(2,1)}, bf16[96,1024]{1,0:T(8,128)(2,1)S(1)}, u32[]{:S(2)}, u32[]{:S(2)}) collective-permute-start(bf16[96,1024]{1,0:T(8,128)(2,1)} %get-tuple-element.50), channel_id=1, source_target_pairs={{0,2},{1,3},{2,0},{3,1},{4,6},{5,7},{6,4},{7,5},{8,10},{9,11},{10,... | collective-permute-start | bytes 589832 | tf_op jit(solution)/shard_map/ppermute | solution.py:535
  17.8 1.5 %collective-permute-start.4 = (bf16[96,1024]{1,0:T(8,128)(2,1)}, bf16[96,1024]{1,0:T(8,128)(2,1)S(1)}, u32[]{:S(2)}, u32[]{:S(2)}) collective-permute-start(bf16[96,1024]{1,0:T(8,128)(2,1)} %get-tuple-element.55), channel_id=1, source_target_pairs={{0,4},{1,5},{2,6},{3,7},{4,0},{5,1},{6,2},{7,3},{8,12},{9,13},{10,... | collective-permute-start | bytes 589832 | tf_op jit(solution)/shard_map/ppermute | solution.py:535
  19.3 0.1 collective-permute-start.5
  19.4 4.8 %all-to-all-done.refs_0_.refs_1_ = s32[16,1,330]{2,1,0:T(1,128)S(1)} async-done(((s32[16,1,330]{2,1,0:T(1,128)}), s32[16,1,330]{2,1,0:T(1,128)S(1)}, u32[]{:S(2)}, u32[]{:S(2)}) %all-to-all-start) | async-done | bytes 21152 | tf_op jit(solution)/shard_map/all_to_all | solution.py:548
  24.2 0.1 eq.15
  24.3 2.7 %collective-permute-start.6 = (bf16[78,1024]{1,0:T(8,128)(2,1)}, bf16[78,1024]{1,0:T(8,128)(2,1)S(1)}, u32[]{:S(2)}, u32[]{:S(2)}) collective-permute-start(bf16[78,1024]{1,0:T(8,128)(2,1)} %get-tuple-element.57), channel_id=1, source_target_pairs={{0,8},{1,9},{2,10},{3,11},{4,12},{5,13},{6,14},{7,15},{8,0},{9,1},... | collective-permute-start | bytes 479240 | tf_op jit(solution)/shard_map/ppermute | solution.py:560
  27.0 0.0 copy-done
  27.0 1.3 %convolution_convert_fusion = bf16[384,1024]{1,0:T(8,128)(2,1)} fusion(bf16[240,1024]{1,0:T(8,128)(2,1)S(1)} %copy-done, s32[384]{0:T(512)S(1)} %eq.15), kind=kOutput, calls=%fused_computation.1 | convolution fusion | flops 189229056 | bytes 1279488 | tf_op jit(solution)/shard_map/dot_general | solution.py:565
  28.3 0.0 collective-permute-done.2.refs_2_
  28.3 0.0 collective-permute-done.3.rest_1_
  28.3 0.0 copy-start.13
  28.3 3.6 %all-to-all-start.1 = ((bf16[16,24,1024]{2,1,0:T(8,128)(2,1)}), bf16[16,24,1024]{2,1,0:T(8,128)(2,1)S(1)}, u32[]{:S(2)}, u32[]{:S(2)}) async-start(bf16[16,24,1024]{2,1,0:T(8,128)(2,1)} %bitcast.4), calls=%async_computation.1 | async-start | bytes 1572864 | tf_op jit(solution)/shard_map/all_to_all | solution.py:572
  32.0 3.3 %collective-permute-done.6.refs_3_ = bf16[78,1024]{1,0:T(8,128)(2,1)S(1)} collective-permute-done((bf16[78,1024]{1,0:T(8,128)(2,1)}, bf16[78,1024]{1,0:T(8,128)(2,1)S(1)}, u32[]{:S(2)}, u32[]{:S(2)}) %collective-permute-start.6) | collective-permute-done | bytes 159776 | tf_op jit(solution)/shard_map/ppermute | solution.py:560
  35.3 0.1 slice.18
  35.3 0.6 gather_fusion
  35.9 0.7 reshape.41.places_far
  36.6 0.0 collective-permute-done.4.rest_2_
  36.6 0.0 collective-permute-done.5.rest_3_
  36.6 0.0 copy-done.13
  36.6 0.7 copy-done.14
  37.3 0.7 copy-done.15
  37.9 3.8 %early.1 = (f32[512,1024]{1,0:T(8,128)}, f32[512,128]{1,0:T(8,128)}) custom-call(s32[1,768]{1,0:T(1,128)} %reshape.41.places_far, f32[512,1024]{1,0:T(8,128)} %centroids_far.1, bf16[96,1024]{1,0:T(8,128)(2,1)} %get-tuple-element.61.rest_0_, bf16[96,1024]{1,0:T(8,128)(2,1)} %copy-done.13, bf16[96,1024]{1,0:T(8,128)(2,1)} %copy-done.14, ...), custom_call_target="tpu_custom_call" | custom-call | flops 20132659200 | bytes 104857600 | tf_op jit(solution)/shard_map/early/pallas_call | solution.py:442
  41.8 0.0 copy-done.5
  41.8 0.0 copy-done.3
  41.8 0.1 collective-permute-start.7
  41.9 0.0 copy-done.10
  41.9 0.5 collective-permute-start.8
  42.4 1.4 %collective-permute-done.8.refs_5_ = bf16[78,1024]{1,0:T(8,128)(2,1)S(1)} collective-permute-done((bf16[78,1024]{1,0:T(8,128)(2,1)S(1)}, bf16[78,1024]{1,0:T(8,128)(2,1)S(1)}, u32[]{:S(2)}, u32[]{:S(2)}) %collective-permute-start.8) | collective-permute-done | bytes 159776 | tf_op jit(solution)/shard_map/ppermute | solution.py:584
  43.8 0.0 collective-permute-done.7.refs_4_
  43.8 0.7 copy-done.11
  44.4 0.8 %copy-done.4 = bf16[176,1024]{1,0:T(8,128)(2,1)} copy-done((bf16[176,1024]{1,0:T(8,128)(2,1)}, bf16[176,1024]{1,0:T(8,128)(2,1)S(1)}, u32[]{:S(2)}) %copy-start.4) | copy-done | bytes 360472
  45.2 2.8 %pack.3 = (bf16[96,1024]{1,0:T(8,128)(2,1)}, bf16[96,1024]{1,0:T(8,128)(2,1)}, bf16[96,1024]{1,0:T(8,128)(2,1)}, bf16[96,1024]{1,0:T(8,128)(2,1)}) custom-call(s32[16,1,330]{2,1,0:T(1,128)} %copy-done.5, s32[16,1,330]{2,1,0:T(1,128)} %copy-done.5, bf16[176,1024]{1,0:T(8,128)(2,1)} %copy-done.3, bf16[78,1024]{1,0:T(8,128)(2,1)} %copy-done.10, ...), custom_call_target="tpu_custom_call" | custom-call | flops 199753728 | bytes 1826816 | tf_op jit(solution)/shard_map/pack/pallas_call | solution.py:319
  48.0 0.7 collective-permute-start.9
  48.7 0.9 %collective-permute-start.10 = (bf16[96,1024]{1,0:T(8,128)(2,1)}, bf16[96,1024]{1,0:T(8,128)(2,1)S(1)}, u32[]{:S(2)}, u32[]{:S(2)}) collective-permute-start(bf16[96,1024]{1,0:T(8,128)(2,1)} %get-tuple-element.78), channel_id=1, source_target_pairs={{0,4},{1,5},{2,6},{3,7},{4,0},{5,1},{6,2},{7,3},{8,12},{9,13},{10,... | collective-permute-start | bytes 589832 | tf_op jit(solution)/shard_map/ppermute | solution.py:535
  49.7 1.9 %collective-permute-start.11 = (bf16[96,1024]{1,0:T(8,128)(2,1)}, bf16[96,1024]{1,0:T(8,128)(2,1)S(1)}, u32[]{:S(2)}, u32[]{:S(2)}) collective-permute-start(bf16[96,1024]{1,0:T(8,128)(2,1)} %get-tuple-element.79), channel_id=1, source_target_pairs={{0,6},{1,7},{2,4},{3,5},{4,2},{5,3},{6,0},{7,1},{8,14},{9,15},{10,... | collective-permute-start | bytes 589832 | tf_op jit(solution)/shard_map/ppermute | solution.py:535
  51.6 0.0 all-to-all-done.1
  51.6 0.9 %copy-done.1 = bf16[16,24,1024]{2,1,0:T(8,128)(2,1)} copy-done((bf16[16,24,1024]{2,1,0:T(8,128)(2,1)}, bf16[16,24,1024]{2,1,0:T(8,128)(2,1)S(1)}, u32[]{:S(2)}) %copy-start.1) | copy-done | bytes 786456
  52.5 5.0 %encode.1 = (bf16[2,1024]{1,0:T(2,128)(2,1)}, bf16[16,2,1024]{2,1,0:T(2,128)(2,1)}) custom-call(s32[1,2]{1,0:T(1,128)} %bitcast.27, s32[128,1]{1,0:T(8,128)} %get-tuple-element.41.refs_1_, bf16[384,1024]{1,0:T(8,128)(2,1)} %bitcast.15, bf16[64,1024]{1,0:T(8,128)(2,1)} %refs_3_.1, f32[1,1024]{1,0:T(1,128)} %bitcast.19, f32[1,1024]{1,0:T(1,128)} %bitcast.20, ...), custom_call_target="tpu_custom_call" | custom-call | flops 637534208 | bytes 6291456 | tf_op jit(solution)/shard_map/encode/pallas_call | solution.py:121
  57.5 5.8 %all-to-all-start.2 = ((bf16[16,2,1024]{2,1,0:T(2,128)(2,1)}), bf16[16,2,1024]{2,1,0:T(2,128)(2,1)S(1)}, u32[]{:S(2)}, u32[]{:S(2)}) async-start(bf16[16,2,1024]{2,1,0:T(2,128)(2,1)} %get-tuple-element.71), calls=%async_computation.2 | async-start | bytes 131072 | tf_op jit(solution)/shard_map/all_to_all | solution.py:607
  63.3 0.1 slice.23
  63.4 0.7 reshape.42.late_far
  64.0 0.0 collective-permute-done.9.rest_1_
  64.0 0.0 collective-permute-done.10.rest_2_
  64.0 0.0 copy-start.8
  64.1 0.0 collective-permute-done.11.rest_3_
  64.1 0.0 copy-start.9
  64.1 6.1 %all-to-all-done.2.spread_far = bf16[16,2,1024]{2,1,0:T(2,128)(2,1)S(1)} async-done(((bf16[16,2,1024]{2,1,0:T(2,128)(2,1)}), bf16[16,2,1024]{2,1,0:T(2,128)(2,1)S(1)}, u32[]{:S(2)}, u32[]{:S(2)}) %all-to-all-start.2) | async-done | bytes 65568 | tf_op jit(solution)/shard_map/all_to_all | solution.py:607
  70.2 0.0 copy-done.7
  70.2 0.0 copy-done.8
  70.2 0.6 copy-done.6
  70.8 3.5 %late.1 = f32[512,1024]{1,0:T(8,128)} custom-call(s32[1,768]{1,0:T(1,128)} %reshape.41.places_far, s32[1,32]{1,0:T(1,128)} %reshape.42.late_far, bf16[16,2,1024]{2,1,0:T(2,128)(2,1)} %copy-done.6, f32[512,128]{1,0:T(8,128)} %get-tuple-element.72.share_far, f32[512,1024]{1,0:T(8,128)} %get-tuple-element.73.early_far, ...), custom_call_target="tpu_custom_call" | custom-call | flops 436207616 | bytes 4194304 | tf_op jit(solution)/shard_map/late/pallas_call | solution.py:474
  (15 shorter events, 0.0 us)
Async XLA Ops:
  0.6 26.4 %copy-start = (bf16[240,1024]{1,0:T(8,128)(2,1)S(1)}, bf16[240,1024]{1,0:T(8,128)(2,1)}, u32[]{:S(2)}) copy-start(bf16[240,1024]{1,0:T(8,128)(2,1)} %param.17) | copy-start | bytes 1474564
  0.6 8.6 %collective-permute-start.1 = (bf16[254,1024]{1,0:T(8,128)(2,1)}, bf16[254,1024]{1,0:T(8,128)(2,1)S(1)}, u32[]{:S(2)}, u32[]{:S(2)}) collective-permute-start(bf16[254,1024]{1,0:T(8,128)(2,1)} %refs_2_.1), channel_id=1, source_target_pairs={{0,1},{1,0},{2,3},{3,2},{4,5},{5,4},{6,7},{7,6},{8,9},{9,8},{10,11... | collective-permute-start | bytes 1560584 | tf_op jit(solution)/shard_map/ppermute | solution.py:539
  1.2 5.2 %collective-permute-start = (s32[1,256]{1,0:T(1,128)}, s32[1,256]{1,0:T(1,128)S(1)}, u32[]{:S(2)}, u32[]{:S(2)}) collective-permute-start(s32[1,256]{1,0:T(1,128)} %bitcast.24), channel_id=1, source_target_pairs={{0,1},{1,0},{2,3},{3,2},{4,5},{5,4},{6,7},{7,6},{8,9},{9,8},{10,11... | collective-permute-start | bytes 3080 | tf_op jit(solution)/shard_map/ppermute | solution.py:543
  2.3 26.0 %collective-permute-start.2 = (bf16[176,1024]{1,0:T(8,128)(2,1)S(1)}, bf16[176,1024]{1,0:T(8,128)(2,1)S(1)}, u32[]{:S(2)}, u32[]{:S(2)}) collective-permute-start(bf16[176,1024]{1,0:T(8,128)(2,1)S(1)} %slice.17), channel_id=1, source_target_pairs={{0,8},{1,9},{2,10},{3,11},{4,12},{5,13},{6,14},{7,15},{8,0},{9,1},... | collective-permute-start | bytes 1081352 | tf_op jit(solution)/shard_map/ppermute | solution.py:540
  6.3 0.6 copy-start.12
  9.2 4.0 %copy-start.2 = (bf16[254,1024]{1,0:T(8,128)(2,1)}, bf16[254,1024]{1,0:T(8,128)(2,1)S(1)}, u32[]{:S(2)}) copy-start(bf16[254,1024]{1,0:T(8,128)(2,1)S(1)} %collective-permute-done.1.refs_3_) | copy-start | bytes 1560580
  9.3 15.0 %all-to-all-start = ((s32[16,1,330]{2,1,0:T(1,128)}), s32[16,1,330]{2,1,0:T(1,128)S(1)}, u32[]{:S(2)}, u32[]{:S(2)}) async-start(s32[16,1,330]{2,1,0:T(1,128)} %get-tuple-element.43), calls=%async_computation | async-start | bytes 49152 | tf_op jit(solution)/shard_map/all_to_all | solution.py:548
  15.9 12.5 %collective-permute-start.3 = (bf16[96,1024]{1,0:T(8,128)(2,1)}, bf16[96,1024]{1,0:T(8,128)(2,1)S(1)}, u32[]{:S(2)}, u32[]{:S(2)}) collective-permute-start(bf16[96,1024]{1,0:T(8,128)(2,1)} %get-tuple-element.50), channel_id=1, source_target_pairs={{0,2},{1,3},{2,0},{3,1},{4,6},{5,7},{6,4},{7,5},{8,10},{9,11},{10,... | collective-permute-start | bytes 589832 | tf_op jit(solution)/shard_map/ppermute | solution.py:535
  17.8 18.7 %collective-permute-start.4 = (bf16[96,1024]{1,0:T(8,128)(2,1)}, bf16[96,1024]{1,0:T(8,128)(2,1)S(1)}, u32[]{:S(2)}, u32[]{:S(2)}) collective-permute-start(bf16[96,1024]{1,0:T(8,128)(2,1)} %get-tuple-element.55), channel_id=1, source_target_pairs={{0,4},{1,5},{2,6},{3,7},{4,0},{5,1},{6,2},{7,3},{8,12},{9,13},{10,... | collective-permute-start | bytes 589832 | tf_op jit(solution)/shard_map/ppermute | solution.py:535
  19.3 17.3 %collective-permute-start.5 = (bf16[96,1024]{1,0:T(8,128)(2,1)}, bf16[96,1024]{1,0:T(8,128)(2,1)S(1)}, u32[]{:S(2)}, u32[]{:S(2)}) collective-permute-start(bf16[96,1024]{1,0:T(8,128)(2,1)} %get-tuple-element.56), channel_id=1, source_target_pairs={{0,6},{1,7},{2,4},{3,5},{4,2},{5,3},{6,0},{7,1},{8,14},{9,15},{10,... | collective-permute-start | bytes 589832 | tf_op jit(solution)/shard_map/ppermute | solution.py:535
  24.2 17.5 %copy-start.5 = (s32[16,1,330]{2,1,0:T(1,128)}, s32[16,1,330]{2,1,0:T(1,128)S(1)}, u32[]{:S(2)}) copy-start(s32[16,1,330]{2,1,0:T(1,128)S(1)} %all-to-all-done.refs_0_.refs_1_) | copy-start | bytes 63364
  24.3 10.9 %collective-permute-start.6 = (bf16[78,1024]{1,0:T(8,128)(2,1)}, bf16[78,1024]{1,0:T(8,128)(2,1)S(1)}, u32[]{:S(2)}, u32[]{:S(2)}) collective-permute-start(bf16[78,1024]{1,0:T(8,128)(2,1)} %get-tuple-element.57), channel_id=1, source_target_pairs={{0,8},{1,9},{2,10},{3,11},{4,12},{5,13},{6,14},{7,15},{8,0},{9,1},... | collective-permute-start | bytes 479240 | tf_op jit(solution)/shard_map/ppermute | solution.py:560
  28.3 13.5 %copy-start.3 = (bf16[176,1024]{1,0:T(8,128)(2,1)}, bf16[176,1024]{1,0:T(8,128)(2,1)S(1)}, u32[]{:S(2)}) copy-start(bf16[176,1024]{1,0:T(8,128)(2,1)S(1)} %collective-permute-done.2.refs_2_) | copy-start | bytes 1081348
  28.3 8.3 %copy-start.13 = (bf16[96,1024]{1,0:T(8,128)(2,1)}, bf16[96,1024]{1,0:T(8,128)(2,1)S(1)}, u32[]{:S(2)}) copy-start(bf16[96,1024]{1,0:T(8,128)(2,1)S(1)} %collective-permute-done.3.rest_1_) | copy-start | bytes 589828
  28.3 23.3 %all-to-all-start.1 = ((bf16[16,24,1024]{2,1,0:T(8,128)(2,1)}), bf16[16,24,1024]{2,1,0:T(8,128)(2,1)S(1)}, u32[]{:S(2)}, u32[]{:S(2)}) async-start(bf16[16,24,1024]{2,1,0:T(8,128)(2,1)} %bitcast.4), calls=%async_computation.1 | async-start | bytes 1572864 | tf_op jit(solution)/shard_map/all_to_all | solution.py:572
  35.2 6.6 %copy-start.10 = (bf16[78,1024]{1,0:T(8,128)(2,1)}, bf16[78,1024]{1,0:T(8,128)(2,1)S(1)}, u32[]{:S(2)}) copy-start(bf16[78,1024]{1,0:T(8,128)(2,1)S(1)} %collective-permute-done.6.refs_3_) | copy-start | bytes 479236
  36.6 0.7 copy-start.14
  37.3 0.7 copy-start.15
  41.8 2.0 %collective-permute-start.7 = (bf16[176,1024]{1,0:T(8,128)(2,1)S(1)}, bf16[176,1024]{1,0:T(8,128)(2,1)S(1)}, u32[]{:S(2)}, u32[]{:S(2)}) collective-permute-start(bf16[176,1024]{1,0:T(8,128)(2,1)S(1)} %collective-permute-done.2.refs_2_), channel_id=1, source_target_pairs={{0,1},{1,0},{2,3},{3,2},{4,5},{5,4},{6,7},{7,6},{8,9},{9,8},{10,11... | collective-permute-start | bytes 1081352 | tf_op jit(solution)/shard_map/ppermute | solution.py:584
  41.9 1.9 %collective-permute-start.8 = (bf16[78,1024]{1,0:T(8,128)(2,1)S(1)}, bf16[78,1024]{1,0:T(8,128)(2,1)S(1)}, u32[]{:S(2)}, u32[]{:S(2)}) collective-permute-start(bf16[78,1024]{1,0:T(8,128)(2,1)S(1)} %collective-permute-done.6.refs_3_), channel_id=1, source_target_pairs={{0,1},{1,0},{2,3},{3,2},{4,5},{5,4},{6,7},{7,6},{8,9},{9,8},{10,11... | collective-permute-start | bytes 479240 | tf_op jit(solution)/shard_map/ppermute | solution.py:584
  43.8 0.7 copy-start.11
  44.4 0.8 %copy-start.4 = (bf16[176,1024]{1,0:T(8,128)(2,1)}, bf16[176,1024]{1,0:T(8,128)(2,1)S(1)}, u32[]{:S(2)}) copy-start(bf16[176,1024]{1,0:T(8,128)(2,1)S(1)} %collective-permute-done.7.refs_4_) | copy-start | bytes 1081348
  48.0 16.0 %collective-permute-start.9 = (bf16[96,1024]{1,0:T(8,128)(2,1)}, bf16[96,1024]{1,0:T(8,128)(2,1)S(1)}, u32[]{:S(2)}, u32[]{:S(2)}) collective-permute-start(bf16[96,1024]{1,0:T(8,128)(2,1)} %get-tuple-element.77), channel_id=1, source_target_pairs={{0,2},{1,3},{2,0},{3,1},{4,6},{5,7},{6,4},{7,5},{8,10},{9,11},{10,... | collective-permute-start | bytes 589832 | tf_op jit(solution)/shard_map/ppermute | solution.py:535
  48.7 15.3 %collective-permute-start.10 = (bf16[96,1024]{1,0:T(8,128)(2,1)}, bf16[96,1024]{1,0:T(8,128)(2,1)S(1)}, u32[]{:S(2)}, u32[]{:S(2)}) collective-permute-start(bf16[96,1024]{1,0:T(8,128)(2,1)} %get-tuple-element.78), channel_id=1, source_target_pairs={{0,4},{1,5},{2,6},{3,7},{4,0},{5,1},{6,2},{7,3},{8,12},{9,13},{10,... | collective-permute-start | bytes 589832 | tf_op jit(solution)/shard_map/ppermute | solution.py:535
  49.7 14.4 %collective-permute-start.11 = (bf16[96,1024]{1,0:T(8,128)(2,1)}, bf16[96,1024]{1,0:T(8,128)(2,1)S(1)}, u32[]{:S(2)}, u32[]{:S(2)}) collective-permute-start(bf16[96,1024]{1,0:T(8,128)(2,1)} %get-tuple-element.79), channel_id=1, source_target_pairs={{0,6},{1,7},{2,4},{3,5},{4,2},{5,3},{6,0},{7,1},{8,14},{9,15},{10,... | collective-permute-start | bytes 589832 | tf_op jit(solution)/shard_map/ppermute | solution.py:535
  51.6 0.9 %copy-start.1 = (bf16[16,24,1024]{2,1,0:T(8,128)(2,1)}, bf16[16,24,1024]{2,1,0:T(8,128)(2,1)S(1)}, u32[]{:S(2)}) copy-start(bf16[16,24,1024]{2,1,0:T(8,128)(2,1)S(1)} %all-to-all-done.1) | copy-start | bytes 2359300
  57.5 12.7 %all-to-all-start.2 = ((bf16[16,2,1024]{2,1,0:T(2,128)(2,1)}), bf16[16,2,1024]{2,1,0:T(2,128)(2,1)S(1)}, u32[]{:S(2)}, u32[]{:S(2)}) async-start(bf16[16,2,1024]{2,1,0:T(2,128)(2,1)} %get-tuple-element.71), calls=%async_computation.2 | async-start | bytes 131072 | tf_op jit(solution)/shard_map/all_to_all | solution.py:607
  64.0 6.2 %copy-start.7 = (bf16[96,1024]{1,0:T(8,128)(2,1)}, bf16[96,1024]{1,0:T(8,128)(2,1)S(1)}, u32[]{:S(2)}) copy-start(bf16[96,1024]{1,0:T(8,128)(2,1)S(1)} %collective-permute-done.9.rest_1_) | copy-start | bytes 589828
  64.0 6.2 %copy-start.8 = (bf16[96,1024]{1,0:T(8,128)(2,1)}, bf16[96,1024]{1,0:T(8,128)(2,1)S(1)}, u32[]{:S(2)}) copy-start(bf16[96,1024]{1,0:T(8,128)(2,1)S(1)} %collective-permute-done.10.rest_2_) | copy-start | bytes 589828
  64.1 6.1 %copy-start.9 = (bf16[96,1024]{1,0:T(8,128)(2,1)}, bf16[96,1024]{1,0:T(8,128)(2,1)S(1)}, u32[]{:S(2)}) copy-start(bf16[96,1024]{1,0:T(8,128)(2,1)S(1)} %collective-permute-done.11.rest_3_) | copy-start | bytes 589828
  70.2 0.6 copy-start.6
